TPU v7x, 32 devices: a whole 2x2x4 slice. The times are simulated.
32 devices in a mesh: dp: 4 (over y, x), section: 2 (over core), tensor: 4 (over z).
Axes of the slice: x: 2, y: 2, z: 4, core: 2. Of those that a mesh axis runs over, the one named last changes fastest.
Arguments:
- source: bfloat16 [4096, 4096], P(('dp', 'section', 'tensor')), parts along dimension 0, may hold values from -6 to 6
- enc_gain: float32 [4096], replicated, may hold values from 0.1 to 1.9
- w_gate: bfloat16 [4096, 8192], P(None, ('section', 'tensor')), may hold values from -0.09375 to 0.09375
- w_up: bfloat16 [4096, 8192], P(None, ('section', 'tensor')), may hold values from -0.09375 to 0.09375
- w_down: bfloat16 [8192, 4096], P(('section', 'tensor')), may hold values from -0.0625 to 0.0625
- enc_keep: int32 [4096, 1024], P(('dp', 'section', 'tensor')), parts along dimension 0, may hold values from 0 to 4095
- final_gain: float32 [4096], replicated, may hold values from 0.1 to 1.9
- target: bfloat16 [512, 4096], P(('dp', 'section', 'tensor')), parts along dimension 0, may hold values from -6 to 6
- self_gain: float32 [4096], replicated, may hold values from 0.1 to 1.9
- self_qkv: bfloat16 [4096, 3, 1024], P('section', None, 'tensor'), as said below
- self_out: bfloat16 [1024, 4096], P('tensor', 'section'), may hold values from -0.1875 to 0.1875
- cross_gain: float32 [4096], replicated, may hold values from 0.1 to 1.9
- cross_q: bfloat16 [4096, 1024], P('section', 'tensor'), as said below
- cross_kv: bfloat16 [4096, 2, 1024], P('section', None, 'tensor'), as said below
- cross_out: bfloat16 [1024, 4096], P('tensor', 'section'), may hold values from -0.1875 to 0.1875
- dec_keep: int32 [512, 1024], P(('dp', 'section', 'tensor')), parts along dimension 0, may hold values from 0 to 4095
Outputs:
- enc_out: bfloat16 [4096, 4096], P(('dp', 'section', 'tensor')), parts along dimension 0
- dec_out: bfloat16 [512, 4096], P(('dp', 'section', 'tensor')), parts along dimension 0
There are 4 independent parts, one for each index of `dp`. A program takes and returns all parts, laid end to end along the dimension named above; an argument that names none is the same for every part. Nothing has to cross between parts.
Inputs may be any that keep to these rules, and one draw needn't show every extreme that they name: `self_qkv`: query weights of self-attention; independent of the keys' weights in the shown draw. `cross_q`: query weights of cross-attention. `cross_kv`: key and value weights of cross-attention.
All inputs are finite; a program needn't handle non-finite values.
Results may differ from a plain program's by a relative error of at most 0.035.
Values may be sent and summed in bfloat16 or wider, within the bound.
No kernel may reach another device: no remote copies, remote signals or barrier semaphores. Data moves between devices by JAX's collectives and lax.ppermute only.
A program may use at most 192 MiB of HBM per device.

v0:
```python
import jax
import jax.numpy as jnp
from jax import lax
from jax.sharding import PartitionSpec as P

HD = 256


def from_behind(value, axis, by):
    devices = lax.axis_size(axis)
    pairs = [(i, i + by) for i in range(devices) if 0 <= i + by < devices]
    return lax.ppermute(value, axis, pairs)


def swapped(value, axis, distance):
    return lax.ppermute(value, axis, [(i, i ^ 1 << distance) for i in range(lax.axis_size(axis))])


def norm_rows(x, gain):
    values = x.astype(jnp.float32)
    power = jnp.mean(values * values, axis=-1, keepdims=True)
    return values * lax.rsqrt(power + 1e-06) * gain


def keep_factor(words):
    shifts = jnp.arange(4, dtype=jnp.int32) * 3
    bits = jnp.right_shift(words[:, None, :], shifts[None, :, None]) & 7
    kept = jnp.where(bits == 7, 0.0, 8.0 / 7.0).astype(jnp.float32)
    return kept.reshape(words.shape[0], 4 * words.shape[1])


def attend(query, keys, values, head_size, allowed):
    rows = query.shape[0]
    count = keys.shape[0]
    heads = query.shape[1] // head_size
    qh = query.reshape(rows, heads, head_size)
    kh = keys.reshape(count, heads, head_size)
    vh = values.reshape(count, heads, head_size)
    scores = jnp.einsum("rhd,khd->hrk", qh, kh, preferred_element_type=jnp.float32) / jnp.sqrt(
        jnp.float32(head_size)
    )
    if allowed is not None:
        scores = jnp.where(allowed[None], scores, jnp.float32(-1e30))
    top = jnp.max(scores, axis=-1, keepdims=True)
    expo = jnp.exp(scores - top)
    probs = (expo / jnp.sum(expo, axis=-1, keepdims=True)).astype(jnp.bfloat16)
    context = jnp.einsum("hrk,khd->rhd", probs, vh, preferred_element_type=jnp.float32)
    return context.reshape(rows, heads * head_size).astype(jnp.bfloat16)


def order_halves(own, other, section_index):
    lower = jnp.where(section_index == 0, own, other)
    upper = jnp.where(section_index == 0, other, own)
    return jnp.concatenate([lower, upper], axis=0)


def per_device(
    source,
    enc_gain,
    w_gate,
    w_up,
    w_down,
    enc_keep,
    final_gain,
    target,
    self_gain,
    self_qkv,
    self_out,
    cross_gain,
    cross_q,
    cross_kv,
    cross_out,
    dec_keep,
):
    normed = norm_rows(
        lax.all_gather(source, ("section", "tensor"), axis=0, tiled=True), enc_gain
    ).astype(jnp.bfloat16)
    gate = jnp.dot(normed, w_gate, preferred_element_type=jnp.float32)
    up = jnp.dot(normed, w_up, preferred_element_type=jnp.float32)
    hidden = (jax.nn.gelu(gate, approximate=True) * up).astype(jnp.bfloat16)
    piece = hidden
    ffn = lax.psum_scatter(
        jnp.dot(piece, w_down, preferred_element_type=jnp.float32).astype(jnp.bfloat16),
        ("section", "tensor"),
        scatter_dimension=0,
        tiled=True,
    ).astype(jnp.float32)
    enc_out = (source.astype(jnp.float32) + keep_factor(enc_keep) * ffn).astype(jnp.bfloat16)
    section_index = lax.axis_index("section")
    width = self_qkv.shape[0] * lax.axis_size("section")
    qkv_full, sout_full, cq_full, ckv_full, cout_full = (
        lax.all_gather(self_qkv, "section", axis=0, tiled=True),
        lax.all_gather(self_out, "section", axis=1, tiled=True),
        lax.all_gather(cross_q, "section", axis=0, tiled=True),
        lax.all_gather(cross_kv, "section", axis=0, tiled=True),
        lax.all_gather(cross_out, "section", axis=1, tiled=True),
    )
    head_width = qkv_full.shape[2]
    memory = norm_rows(enc_out, final_gain).astype(jnp.bfloat16)
    selfin = norm_rows(target, self_gain).astype(jnp.bfloat16)
    memory_half, target_half = (
        lax.all_gather(memory, "tensor", axis=0, tiled=True),
        lax.all_gather(selfin, "tensor", axis=0, tiled=True),
    )
    half_rows = target_half.shape[0]
    qkv = jnp.dot(
        target_half, qkv_full.reshape(width, 3 * head_width), preferred_element_type=jnp.float32
    ).astype(jnp.bfloat16)
    qkv = qkv.reshape(half_rows, 3, head_width)
    own_kv = qkv[:, 1:, :]
    other_kv = from_behind(own_kv, "section", 1)
    all_kv = order_halves(own_kv, other_kv, section_index)
    query_pos = section_index * half_rows + jnp.arange(half_rows, dtype=jnp.int32)
    key_pos = jnp.arange(2 * half_rows, dtype=jnp.int32)
    causal = key_pos[None, :] <= query_pos[:, None]
    selfctx = attend(qkv[:, 0, :], all_kv[:, 0, :], all_kv[:, 1, :], HD, causal)
    piece = selfctx
    selfsum = lax.psum_scatter(
        jnp.dot(piece, sout_full, preferred_element_type=jnp.float32).astype(jnp.bfloat16),
        "tensor",
        scatter_dimension=0,
        tiled=True,
    ).astype(jnp.float32)
    mid = (target.astype(jnp.float32) + selfsum).astype(jnp.bfloat16)
    crossin = norm_rows(mid, cross_gain).astype(jnp.bfloat16)
    query_rows = lax.all_gather(crossin, "tensor", axis=0, tiled=True)
    cq = jnp.dot(query_rows, cq_full, preferred_element_type=jnp.float32).astype(jnp.bfloat16)
    own_ckv = jnp.dot(
        memory_half, ckv_full.reshape(width, 2 * head_width), preferred_element_type=jnp.float32
    ).astype(jnp.bfloat16)
    own_ckv = own_ckv.reshape(memory_half.shape[0], 2, head_width)
    other_ckv = swapped(own_ckv, "section", 0)
    all_ckv = order_halves(own_ckv, other_ckv, section_index)
    crossctx = attend(cq, all_ckv[:, 0, :], all_ckv[:, 1, :], HD, None)
    piece = crossctx
    crosssum = lax.psum_scatter(
        jnp.dot(piece, cout_full, preferred_element_type=jnp.float32).astype(jnp.bfloat16),
        "tensor",
        scatter_dimension=0,
        tiled=True,
    ).astype(jnp.float32)
    dec_out = (mid.astype(jnp.float32) + keep_factor(dec_keep) * crosssum).astype(jnp.bfloat16)
    return (enc_out, dec_out)


def solution(mesh):
    return jax.shard_map(
        per_device,
        mesh=mesh,
        in_specs=(
            P(("dp", "section", "tensor"), None),
            P(),
            P(None, ("section", "tensor")),
            P(None, ("section", "tensor")),
            P(("section", "tensor"), None),
            P(("dp", "section", "tensor"), None),
            P(),
            P(("dp", "section", "tensor"), None),
            P(),
            P("section", None, "tensor"),
            P("tensor", "section"),
            P(),
            P("section", "tensor"),
            P("section", None, "tensor"),
            P("tensor", "section"),
            P(("dp", "section", "tensor"), None),
        ),
        out_specs=(P(("dp", "section", "tensor"), None), P(("dp", "section", "tensor"), None)),
        check_vma=False,
    )
```

profile of v0, /device:TPU:0, one launch (start us, length us, event | category | flops | bytes accessed | tf_op | source)
XLA Modules:
  0.0 496.3 jit_solution(966564743249215351)
XLA Ops:
  7.2 0.0 all-gather.8.cloned.1.call-start
  7.2 0.7 all-gather.8.cloned.1.call-update
  7.9 0.0 all-gather.10.cloned.1.call-start
  7.9 4.8 copy.19
  12.7 0.0 all-gather.10.cloned.1.call-update
  12.7 0.0 all-gather.12.cloned.1.call-start
  12.8 0.7 all-gather.12.cloned.1.call-update
  13.5 0.0 reduce-scatter.4.cloned.1.call-start
  13.5 80.9 %all-gather.8.cloned.1.call-done = bf16[1024,4096]{1,0:T(8,128)(2,1)} async-done(((bf16[128,4096]{1,0:T(8,128)(2,1)}), bf16[1024,4096]{1,0:T(8,128)(2,1)}) %all-gather.8.cloned.1.call-update) | async-done | bytes 8388624 | tf_op jit(solution)/shard_map/all_gather | solution.py:76
  94.4 5.2 %fusion = f32[1024]{0:T(1024)S(1)} fusion(bf16[1024,4096]{1,0:T(8,128)(2,1)} %all-gather.8.cloned.1.call-done), kind=kLoop, calls=%fused_computation.2 | loop fusion | flops 12581888 | bytes 8392704 | tf_op jit(solution)/shard_map/reduce_sum | solution.py:21
  99.6 0.5 copy-done
  100.2 13.3 %fusion.12 = f32[1024,1024]{1,0:T(8,128)} fusion(bf16[4096,1024]{1,0:T(8,128)(2,1)} %param.19, bf16[1024,4096]{1,0:T(8,128)(2,1)S(1)} %copy-done, f32[4096]{0:T(1024)S(1)} %copy-done.9, f32[1024]{0:T(1024)S(1)} %add_rsqrt_fusion), kind=kOutput, calls=%fused_computation.20 | convolution fusion | flops 8606711808 | bytes 20992000 | tf_op jit(solution)/shard_map/dot_general | solution.py:79
  113.5 28.9 %convolution_convert_fusion = bf16[1024,4096]{1,0:T(8,128)(2,1)} fusion(bf16[1024,4096]{1,0:T(8,128)(2,1)} %param.20, f32[1024,1024]{1,0:T(8,128)} %fusion.12, bf16[4096,1024]{1,0:T(8,128)(2,1)} %param.18, bf16[1024,4096]{1,0:T(8,128)(2,1)} %all-gather.8.cloned.1.call-done, f32[4096]{0:T(1024)S(1)} %copy-done.9, f32[1024]{0:T(1024)S(1)} %add_rsqrt_fusion), kind=kOutput, calls=%fused_computation.5 | convolution fusion | flops 17211326464 | bytes 37769216 | tf_op jit(solution)/shard_map/dot_general | solution.py:83
  142.4 0.0 reduce-scatter.4.cloned.1.call-update
  142.4 0.0 all-gather.16.cloned.1.call-start
  142.5 0.5 all-gather.16.cloned.1.call-update
  143.0 0.2 reduce-scatter.6.cloned.1.call-start
  143.2 0.2 copy-done.4
  143.4 0.6 shift_right_arithmetic.40
  144.0 1.6 copy.23
  145.7 0.1 broadcast_bitcast_fusion
  145.7 0.1 fusion.37
  145.9 0.1 fusion.39
  146.0 21.9 %all_gather.28 = bf16[64,4096]{1,0:T(8,128)(2,1)S(1)} all-gather(bf16[16,4096]{1,0:T(8,128)(2,1)S(1)} %fusion.39), channel_id=1, replica_groups=mesh['dp'=4,'section'=2,'tensor'=4] {'tensor'}, dimensions={0}, use_global_device_ids=true | all-gather | bytes 655360 | tf_op jit(solution)/shard_map/all_gather | solution.py:103
  168.0 4.9 convolution_convert_fusion.4
  172.8 0.1 reshape.132
  172.9 0.1 slice.25
  173.0 1.3 collective-permute-start
  174.4 0.8 collective-permute-done
  175.2 0.2 broadcast_select_fusion.3
  175.3 0.2 slice_maximum_fusion
  175.5 0.3 fusion.70
  175.8 0.2 fusion.58
  176.0 0.0 all-gather.12.cloned.1.call-done
  176.0 3.1 convolution_convert_fusion.2
  179.1 0.0 reduce-scatter.6.cloned.1.call-update
  179.1 0.0 all-gather.14.cloned.1.call-start
  179.2 136.5 %reduce-scatter.4.cloned.1.call-done = bf16[128,4096]{1,0:T(8,128)(2,1)} async-done(((bf16[1024,4096]{1,0:T(8,128)(2,1)}), bf16[128,4096]{1,0:T(8,128)(2,1)}) %reduce-scatter.4.cloned.1.call-update) | async-done | bytes 1048592 | tf_op jit(solution)/shard_map/reduce_scatter | solution.py:82
  315.6 2.3 fusion.20
  318.0 1.3 fusion.22
  319.3 0.0 all-gather.18.cloned.1.call-start
  319.4 0.7 all-gather.18.cloned.1.call-update
  320.1 0.0 all-gather.20.cloned.1.call-start
  320.1 0.7 all-gather.20.cloned.1.call-update
  320.8 0.0 reduce-scatter.8.cloned.1.call-start
  320.9 11.0 %all-gather.16.cloned.1.call-done = bf16[4096,2,256]{2,1,0:T(2,128)(2,1)} async-done(((bf16[2048,2,256]{2,1,0:T(2,128)(2,1)}), bf16[4096,2,256]{2,1,0:T(2,128)(2,1)}) %all-gather.16.cloned.1.call-update) | async-done | bytes 4194320 | tf_op jit(solution)/shard_map/all_gather | solution.py:95
  331.9 4.9 copy.26
  336.8 20.1 %reduce-scatter.6.cloned.1.call-done = bf16[16,4096]{1,0:T(8,128)(2,1)} async-done(((bf16[64,4096]{1,0:T(8,128)(2,1)}), bf16[16,4096]{1,0:T(8,128)(2,1)}) %reduce-scatter.6.cloned.1.call-update) | async-done | bytes 131088 | tf_op jit(solution)/shard_map/reduce_scatter | solution.py:118
  356.9 1.1 fusion.41
  357.9 79.6 %all-gather.14.cloned.1.call-done = bf16[512,4096]{1,0:T(8,128)(2,1)} async-done(((bf16[128,4096]{1,0:T(8,128)(2,1)}), bf16[512,4096]{1,0:T(8,128)(2,1)}) %all-gather.14.cloned.1.call-update) | async-done | bytes 4194320 | tf_op jit(solution)/shard_map/all_gather | solution.py:102
  437.5 5.9 %convolution_convert_fusion.3 = bf16[512,512]{0,1:T(8,128)(2,1)S(1)} fusion(bf16[512,4096]{1,0:T(8,128)(2,1)} %all-gather.14.cloned.1.call-done, bf16[4096,512]{1,0:T(8,128)(2,1)} %bitcast.67), kind=kOutput, calls=%fused_computation.31 | convolution fusion | flops 2147745792 | bytes 8912896 | tf_op jit(solution)/shard_map/dot_general | solution.py:128
  443.4 0.1 collective-permute-start.1
  443.5 0.1 fusion.43
  443.6 16.2 %all_gather.33 = bf16[64,4096]{1,0:T(8,128)(2,1)S(1)} all-gather(bf16[16,4096]{1,0:T(8,128)(2,1)S(1)} %fusion.43), channel_id=1, replica_groups=mesh['dp'=4,'section'=2,'tensor'=4] {'tensor'}, dimensions={0}, use_global_device_ids=true | all-gather | bytes 655360 | tf_op jit(solution)/shard_map/all_gather | solution.py:126
  459.8 0.1 broadcast_select_fusion
  459.8 0.0 all-gather.18.cloned.1.call-done
  459.9 2.5 fusion.71
  462.4 0.2 fusion.45
  462.6 0.0 all-gather.20.cloned.1.call-done
  462.6 3.4 convolution_convert_fusion.1
  466.0 0.1 shift_right_arithmetic.46
  466.1 0.2 copy.25
  466.3 21.6 %reduce-scatter.8.cloned.1.call-done = bf16[16,4096]{1,0:T(8,128)(2,1)} async-done(((bf16[64,4096]{1,0:T(8,128)(2,1)}), bf16[16,4096]{1,0:T(8,128)(2,1)}) %reduce-scatter.8.cloned.1.call-update) | async-done | bytes 131088 | tf_op jit(solution)/shard_map/reduce_scatter | solution.py:136
  487.8 1.7 fusion.44
  (30 shorter events, 0.2 us)
Async XLA Ops:
  7.2 87.2 %all-gather.8.cloned.1.call-start = ((), (), s32[]{:S(2)}) async-start(), calls=%async_computation.3 | async-start | bytes 9437184 | tf_op jit(solution)/shard_map/all_gather | solution.py:76
  7.9 160.1 %all-gather.10.cloned.1.call-start = ((), (), s32[]{:S(2)}) async-start(), calls=%async_computation.5 | async-start | bytes 9437184 | tf_op jit(solution)/shard_map/all_gather | solution.py:92
  12.7 163.3 %all-gather.12.cloned.1.call-start = ((), (), s32[]{:S(2)}) async-start(), calls=%async_computation.6 | async-start | bytes 3145728 | tf_op jit(solution)/shard_map/all_gather | solution.py:93
  12.8 86.9 %copy-start.9 = (f32[4096]{0:T(1024)S(1)}, f32[4096]{0:T(1024)}, u32[]{:S(2)}) copy-start(f32[4096]{0:T(1024)} %param.17) | copy-start | bytes 49156
  13.5 302.2 %reduce-scatter.4.cloned.1.call-start = ((), (), s32[]{:S(2)}) async-start(), calls=%async_computation.4 | async-start | bytes 9437184 | tf_op jit(solution)/shard_map/reduce_scatter | solution.py:82
  94.4 5.8 %copy-start = (bf16[1024,4096]{1,0:T(8,128)(2,1)S(1)}, bf16[1024,4096]{1,0:T(8,128)(2,1)}, u32[]{:S(2)}) copy-start(bf16[1024,4096]{1,0:T(8,128)(2,1)} %all-gather.8.cloned.1.call-done) | copy-start | bytes 25165828
  142.4 1.0 copy-start.4
  142.4 3.3 copy-start.2
  142.4 3.5 copy-start.7
  142.4 189.5 %all-gather.16.cloned.1.call-start = ((), (), s32[]{:S(2)}) async-start(), calls=%async_computation.9 | async-start | bytes 6291456 | tf_op jit(solution)/shard_map/all_gather | solution.py:95
  143.0 213.9 %reduce-scatter.6.cloned.1.call-start = ((), (), s32[]{:S(2)}) async-start(), calls=%async_computation.7 | async-start | bytes 655360 | tf_op jit(solution)/shard_map/reduce_scatter | solution.py:118
  173.0 2.2 collective-permute-start
  176.0 142.0 %copy-start.6 = (f32[4096]{0:T(1024)S(1)}, f32[4096]{0:T(1024)}, u32[]{:S(2)}) copy-start(f32[4096]{0:T(1024)} %param.22) | copy-start | bytes 49156
  179.1 258.4 %all-gather.14.cloned.1.call-start = ((), (), s32[]{:S(2)}) async-start(), calls=%async_computation.8 | async-start | bytes 5242880 | tf_op jit(solution)/shard_map/all_gather | solution.py:102
  318.0 18.8 %copy-start.1 = (bf16[128,4096]{1,0:T(8,128)(2,1)}, bf16[128,4096]{1,0:T(8,128)(2,1)S(1)}, u32[]{:S(2)}) copy-start(bf16[128,4096]{1,0:T(8,128)(2,1)S(1)} %get-tuple-element.3) | copy-start | bytes 3145732
  319.3 140.5 %all-gather.18.cloned.1.call-start = ((), (), s32[]{:S(2)}) async-start(), calls=%async_computation.10 | async-start | bytes 3145728 | tf_op jit(solution)/shard_map/all_gather | solution.py:94
  320.1 142.5 %all-gather.20.cloned.1.call-start = ((), (), s32[]{:S(2)}) async-start(), calls=%async_computation.11 | async-start | bytes 3145728 | tf_op jit(solution)/shard_map/all_gather | solution.py:96
  320.8 167.0 %reduce-scatter.8.cloned.1.call-start = ((), (), s32[]{:S(2)}) async-start(), calls=%async_computation.12 | async-start | bytes 655360 | tf_op jit(solution)/shard_map/reduce_scatter | solution.py:136
  437.5 6.0 %copy-start.3 = (bf16[16,4096]{1,0:T(8,128)(2,1)S(1)}, bf16[16,4096]{1,0:T(8,128)(2,1)}, u32[]{:S(2)}) copy-start(bf16[16,4096]{1,0:T(8,128)(2,1)} %reduce-scatter.6.cloned.1.call-done) | copy-start | bytes 393220
  437.5 6.0 %copy-start.8 = (f32[4096]{0:T(1024)S(1)}, f32[4096]{0:T(1024)}, u32[]{:S(2)}) copy-start(f32[4096]{0:T(1024)} %param.27) | copy-start | bytes 49156
  443.4 16.4 %collective-permute-start.1 = (bf16[512,2,256]{0,2,1:T(8,128)(2,1)S(1)}, bf16[512,2,256]{0,2,1:T(8,128)(2,1)S(1)}, u32[]{:S(2)}, u32[]{:S(2)}) collective-permute-start(bf16[512,2,256]{0,2,1:T(8,128)(2,1)S(1)} %bitcast.70), channel_id=1, source_target_pairs={{0,4},{4,0},{1,5},{5,1},{2,6},{6,2},{3,7},{7,3},{8,12},{12,8},{9,1... | collective-permute-start | bytes 1572872 | tf_op jit(solution)/shard_map/ppermute | solution.py:16
  459.9 6.1 %copy-start.5 = (s32[16,1024]{1,0:T(8,128)S(1)}, s32[16,1024]{1,0:T(8,128)}, u32[]{:S(2)}) copy-start(s32[16,1024]{1,0:T(8,128)} %param.31) | copy-start | bytes 196612
Sparse Core Ops, SparseCore 0:
  9.6 84.7 all-gather.7
  95.9 15.2 all-gather.9
  112.8 11.7 all-gather.11
  142.5 173.0 reduce-scatter.3
  317.0 14.8 all-gather.15
  334.0 22.7 reduce-scatter.5
  358.4 79.0 all-gather.13
  439.0 9.0 all-gather.17
  449.7 11.7 all-gather.19
  466.1 21.6 reduce-scatter.7
where the time goes:
time: 497 us; the launch traced here: 496 us
  waiting for transfers between devices  354 us (71%)
  matrix products  62.1 us (12%)
  blocking collectives  38.1 us (8%)
  between operations  14.4 us (3%)
  local copies, waits for them, and re-layouts  13.1 us (3%)
  other arithmetic  12.8 us (3%)
    reduce_scatter x1, waiting for transfers between devices, per_device(): lax.psum_scatter(jnp.dot(piece, w_down, preferred_element_type=jnp.float3...  136 us
    all_gather x1, waiting for transfers between devices, per_device(): lax.all_gather(source, ('section', 'tensor'), axis=0, tiled=True)  80.9 us
    all_gather x1, waiting for transfers between devices, per_device(): lax.all_gather(memory, 'tensor', axis=0, tiled=True)  79.6 us
    dot_general x1, matrix products, per_device(): jnp.dot(piece, w_down, preferred_element_type=jnp.float32)  28.9 us
    all_gather x1, blocking collectives, per_device(): lax.all_gather(selfin, 'tensor', axis=0, tiled=True)  21.9 us
    reduce_scatter x1, waiting for transfers between devices, per_device(): lax.psum_scatter(jnp.dot(piece, cout_full, preferred_element_type=jnp.flo...  21.6 us
    reduce_scatter x1, waiting for transfers between devices, per_device(): lax.psum_scatter(jnp.dot(piece, sout_full, preferred_element_type=jnp.flo...  20.1 us
    all_gather x1, blocking collectives, per_device(): query_rows = lax.all_gather(crossin, 'tensor', axis=0, tiled=True)  16.2 us
  transfers between devices with their start and end apart: 12, of which 7 were waited for; matrix products, arithmetic and copies ran while one was open for 17% of the time, Pallas kernels for 0%

commit v1 on v0

v1 whole, which is shorter than its diff:
```python
import functools

import jax
import jax.numpy as jnp
from jax import lax
from jax.experimental import pallas as pl
from jax.experimental.pallas import tpu as pltpu
from jax.sharding import PartitionSpec as P

HD = 256
F32 = jnp.float32
BF16 = jnp.bfloat16
CHUNKS = 2
STATS = 5


def norm_rows(x, gain):
    values = x.astype(F32)
    power = jnp.mean(values * values, axis=-1, keepdims=True)
    return values * lax.rsqrt(power + 1e-06) * gain


def keep_factor(words):
    shifts = jnp.arange(4, dtype=jnp.int32) * 3
    bits = jnp.right_shift(words[:, None, :], shifts[None, :, None]) & 7
    kept = jnp.where(bits == 7, 0.0, 8.0 / 7.0).astype(F32)
    return kept.reshape(words.shape[0], 4 * words.shape[1])


def swap_section(value):
    return lax.ppermute(value, "section", [(0, 1), (1, 0)])


def from_slots(value, count):
    return [value] + [
        lax.ppermute(value, "tensor", [(i, (i - o) % count) for i in range(count)]) for o in range(1, count)
    ]


def half_columns(value, index):
    return lax.dynamic_slice_in_dim(value, index * (value.shape[1] // 2), value.shape[1] // 2, 1)


def gather_half(rows, section, count):
    own = half_columns(rows, section)
    other = swap_section(half_columns(rows, 1 - section))
    pair = jnp.where(section == 0, jnp.concatenate([own, other], 0), jnp.concatenate([other, own], 0))
    return jnp.concatenate(from_slots(pair, count), 0)


def both_halves(partial):
    return partial + swap_section(partial)


def ffn_part(x, w_gate, w_up, w_down, section, tensor, count):
    gate = jnp.dot(x, w_gate, preferred_element_type=F32)
    up = jnp.dot(x, w_up, preferred_element_type=F32)
    hidden = (jax.nn.gelu(gate, approximate=True) * up).astype(BF16)
    rows = hidden.shape[0] // 2
    block = rows // count
    theirs = lax.dynamic_slice_in_dim(hidden, (1 - section) * rows, rows, 0)
    got = swap_section(jnp.dot(theirs, w_down, preferred_element_type=F32).astype(BF16))
    ours = lax.dynamic_slice_in_dim(hidden, section * rows, rows, 0)
    mine = jnp.dot(ours, w_down, preferred_element_type=F32).astype(BF16)

    def part(slot):
        at = lax.rem(tensor + slot, count) * block
        return lax.dynamic_slice_in_dim(mine, at, block, 0).astype(F32) + lax.dynamic_slice_in_dim(
            got, at, block, 0
        ).astype(F32)

    above, below = None, None
    for step in range(1, count):
        send_up, send_down = part(count - step), part(step)
        if step > 1:
            send_up = send_up + above.astype(F32)
            send_down = send_down + below.astype(F32)
        above = lax.ppermute(send_up.astype(BF16), "tensor", [(i, i + 1) for i in range(step)])
        below = lax.ppermute(
            send_down.astype(BF16), "tensor", [(i, i - 1) for i in range(count - step, count)]
        )
    return part(0) + above.astype(F32) + below.astype(F32)


def attend_kernel(steps, mem_ref, w_ref, cq_ref, out_ref, keys, values):
    head, step = pl.program_id(0), pl.program_id(1)
    depth = w_ref.shape[4]
    total_k = jnp.zeros(keys.shape, F32)
    total_v = jnp.zeros(values.shape, F32)
    for g in range(w_ref.shape[0]):
        x = mem_ref[:, g * depth : (g + 1) * depth]
        total_k += jnp.dot(x, w_ref[g, 0, 0, 0], preferred_element_type=F32)
        total_v += jnp.dot(x, w_ref[g, 0, 0, 1], preferred_element_type=F32)

    @pl.when(step == 0)
    def _():
        keys[...] = total_k
        values[...] = total_v

    @pl.when(step > 0)
    def _():
        keys[...] += total_k
        values[...] += total_v

    @pl.when(step == steps - 1)
    def _():
        k, v = keys[...].astype(BF16), values[...].astype(BF16)
        scores = lax.dot_general(cq_ref[0], k, (((1,), (1,)), ((), ())), preferred_element_type=F32)
        scores = scores * (1.0 / 16.0)
        top = jnp.max(scores, axis=-1, keepdims=True)
        expo = jnp.exp(scores - top)
        total = jnp.sum(expo, axis=-1, keepdims=True)
        context = jnp.dot(expo.astype(BF16), v, preferred_element_type=F32)
        out_ref[:, pl.ds(pl.multiple_of(head * HD, HD), HD)] = context.astype(BF16)
        lanes = lax.broadcasted_iota(jnp.int32, (scores.shape[0], 128), 1) - head * STATS
        base = out_ref.shape[1] - 128
        high = top.astype(BF16).astype(F32)
        rest = top - high
        middle = rest.astype(BF16).astype(F32)
        low = rest - middle
        sum_high = total.astype(BF16).astype(F32)
        sum_low = total - sum_high
        stats = jnp.where(head == 0, jnp.zeros(lanes.shape, F32), out_ref[:, base:].astype(F32))
        for index, piece in enumerate((high, middle, low, sum_high, sum_low)):
            stats = jnp.where(lanes == index, piece, stats)
        out_ref[:, base:] = stats.astype(BF16)


def attend_own_keys(memory, weights, queries):
    dp, sections, heads, two, depth, width = weights.shape
    rows, features = memory.shape
    count = queries.shape[1]
    return pl.pallas_call(
        functools.partial(attend_kernel, sections),
        grid=(heads, sections),
        in_specs=[
            pl.BlockSpec((rows, features // sections), lambda h, s: (0, s)),
            pl.BlockSpec((dp, 1, 1, two, depth, width), lambda h, s: (0, s, h, 0, 0, 0)),
            pl.BlockSpec((1, count, width), lambda h, s: (h, 0, 0)),
        ],
        out_specs=pl.BlockSpec((count, heads * width + 128), lambda h, s: (0, 0)),
        out_shape=jax.ShapeDtypeStruct((count, heads * width + 128), BF16),
        scratch_shapes=[pltpu.VMEM((rows, width), F32), pltpu.VMEM((rows, width), F32)],
        compiler_params=pltpu.CompilerParams(vmem_limit_bytes=32 * 2**20),
        cost_estimate=pl.CostEstimate(
            flops=4 * rows * features * heads * width, bytes_accessed=2 * weights.size, transcendentals=0
        ),
        name="attend_own_keys",
    )(memory, weights, queries)


def finish(parts, weights, mid, words):
    dp, sections, heads, width, tile = weights.shape
    rows, features = mid.shape
    sources = parts.shape[0]
    per_word = words.shape[1] // tile

    def kernel(parts_ref, w_ref, mid_ref, words_ref, out_ref, context):
        finish_body(heads, words.shape[1], parts_ref, w_ref, mid_ref, words_ref, out_ref, context)

    return pl.pallas_call(
        kernel,
        grid=(sections, dp),
        in_specs=[
            pl.BlockSpec(parts.shape, lambda s, g: (0, 0, 0)),
            pl.BlockSpec((1, 1, heads, width, tile), lambda s, g: (g, s, 0, 0, 0)),
            pl.BlockSpec((rows, tile), lambda s, g: (0, s * dp + g)),
            pl.BlockSpec((rows, tile), lambda s, g: (0, lax.rem(s * dp + g, per_word))),
        ],
        out_specs=pl.BlockSpec((rows, tile), lambda s, g: (0, s * dp + g)),
        out_shape=jax.ShapeDtypeStruct((rows, features), BF16),
        scratch_shapes=[pltpu.VMEM((rows, heads * width), BF16)],
        compiler_params=pltpu.CompilerParams(vmem_limit_bytes=32 * 2**20),
        cost_estimate=pl.CostEstimate(
            flops=2 * rows * features * heads * width, bytes_accessed=2 * weights.size, transcendentals=0
        ),
        name="finish",
    )(parts, weights, mid, words)


def finish_body(heads, words_width, parts_ref, w_ref, mid_ref, words_ref, out_ref, context):
    tile = out_ref.shape[1]
    index = pl.program_id(0) * pl.num_programs(1) + pl.program_id(1)

    @pl.when(index == 0)
    def _():
        base = heads * HD
        stat = parts_ref[:, :, base:].astype(F32)
        for head in range(heads):
            at = head * STATS
            top = stat[:, :, at : at + 1] + stat[:, :, at + 1 : at + 2] + stat[:, :, at + 2 : at + 3]
            total = stat[:, :, at + 3 : at + 4] + stat[:, :, at + 4 : at + 5]
            most = jnp.max(top, axis=0, keepdims=True)
            weight = jnp.exp(top - most)
            whole = jnp.sum(weight * total, axis=0)
            part = parts_ref[:, :, head * HD : (head + 1) * HD].astype(F32)
            context[:, head * HD : (head + 1) * HD] = (jnp.sum(part * weight, axis=0) / whole).astype(BF16)

    w = w_ref[0, 0].reshape(heads * HD, tile)
    total = jnp.dot(context[...], w, preferred_element_type=F32)
    shift = 3 * (index // (words_width // tile))
    bits = lax.shift_right_logical(words_ref[...], jnp.broadcast_to(shift, words_ref.shape)) & 7
    kept = jnp.where(bits == 7, 0.0, 8.0 / 7.0).astype(F32)
    out_ref[...] = (mid_ref[...].astype(F32) + kept * total).astype(BF16)


def per_device(
    source,
    enc_gain,
    w_gate,
    w_up,
    w_down,
    enc_keep,
    final_gain,
    target,
    self_gain,
    self_qkv,
    self_out,
    cross_gain,
    cross_q,
    cross_kv,
    cross_out,
    dec_keep,
):
    count, groups = lax.axis_size("tensor"), lax.axis_size("dp")
    section, tensor, group = lax.axis_index("section"), lax.axis_index("tensor"), lax.axis_index("dp")
    devices = 2 * count

    normed = norm_rows(source, enc_gain).astype(BF16)
    block = normed.shape[0] // CHUNKS
    gathered = [
        lax.all_gather(normed[c * block : (c + 1) * block], ("section", "tensor"), axis=0, tiled=True)
        for c in range(CHUNKS)
    ]

    depth = cross_kv.shape[0] // groups
    kv_share = lax.dynamic_slice_in_dim(jnp.transpose(cross_kv, (1, 0, 2)), group * depth, depth, 1)
    kv_all = lax.all_gather(kv_share, ("dp", "section", "tensor"), axis=0, tiled=False)
    kv_all = kv_all.reshape((groups, 2, count) + kv_share.shape)
    tile = cross_out.shape[1] // groups
    out_share = lax.dynamic_slice_in_dim(cross_out, group * tile, tile, 1)
    out_all = lax.all_gather(out_share, ("dp", "section", "tensor"), axis=0, tiled=False)
    out_all = out_all.reshape((groups, 2, count) + out_share.shape)

    rows = target.shape[0]
    selfin = norm_rows(target, self_gain).astype(BF16)
    x = gather_half(selfin, section, count)
    qkv_w = jnp.transpose(self_qkv, (1, 0, 2))
    q, k, v = [jnp.dot(x, qkv_w[i], preferred_element_type=F32) for i in range(3)]
    q, k, v = [y.astype(BF16) for y in both_halves(jnp.stack([q, k, v]))]
    slot_chip = lax.rem(tensor + jnp.arange(count, dtype=jnp.int32), count)
    positions = (
        (jnp.arange(2, dtype=jnp.int32)[None, :] * count + slot_chip[:, None])[:, :, None] * rows
        + jnp.arange(rows, dtype=jnp.int32)
    ).reshape(-1)
    scores = lax.dot_general(q, k, (((1,), (1,)), ((), ())), preferred_element_type=F32) * (1.0 / 16.0)
    scores = jnp.where(positions[None, :] <= positions[:, None], scores, F32(-1e30))
    expo = jnp.exp(scores - jnp.max(scores, axis=-1, keepdims=True))
    probs = (expo / jnp.sum(expo, axis=-1, keepdims=True)).astype(BF16)
    context = jnp.dot(probs, v, preferred_element_type=F32).astype(BF16)
    product = jnp.dot(context, self_out, preferred_element_type=F32).astype(BF16)
    product = product.reshape(count, 2 * rows, product.shape[1])
    total = product[0].astype(F32)
    for o in range(1, count):
        total = total + lax.ppermute(
            product[o], "tensor", [(i, (i + o) % count) for i in range(count)]
        ).astype(F32)
    own = lax.dynamic_slice_in_dim(total, section * rows, rows, 0)
    other = swap_section(lax.dynamic_slice_in_dim(total, (1 - section) * rows, rows, 0))
    selfsum = jnp.where(section == 0, jnp.concatenate([own, other], 1), jnp.concatenate([other, own], 1))
    mid = (target.astype(F32) + selfsum).astype(BF16)

    crossin = norm_rows(mid, cross_gain).astype(BF16)
    x = gather_half(crossin, section, count)
    cq = both_halves(jnp.dot(x, cross_q, preferred_element_type=F32)).astype(BF16)
    cq = jnp.roll(cq.reshape(count, 2, rows, HD), tensor, axis=0)
    cq = jnp.transpose(cq, (1, 0, 2, 3)).reshape(devices * rows, HD)
    queries = jnp.roll(jnp.stack(from_slots(cq, count)), tensor, axis=0)

    ffn = jnp.concatenate(
        [ffn_part(x, w_gate, w_up, w_down, section, tensor, count) for x in gathered], 0
    )
    enc_out = (source.astype(F32) + keep_factor(enc_keep) * ffn).astype(BF16)
    memory = norm_rows(enc_out, final_gain).astype(BF16)

    parts = attend_own_keys(memory, kv_all, queries)
    parts = parts.reshape(devices, rows, parts.shape[1])
    parts = lax.all_to_all(parts, ("section", "tensor"), split_axis=0, concat_axis=0, tiled=True)
    dec_out = finish(parts, out_all, mid, dec_keep)
    return (enc_out, dec_out)


def solution(mesh):
    return jax.shard_map(
        per_device,
        mesh=mesh,
        in_specs=(
            P(("dp", "section", "tensor"), None),
            P(),
            P(None, ("section", "tensor")),
            P(None, ("section", "tensor")),
            P(("section", "tensor"), None),
            P(("dp", "section", "tensor"), None),
            P(),
            P(("dp", "section", "tensor"), None),
            P(),
            P("section", None, "tensor"),
            P("tensor", "section"),
            P(),
            P("section", "tensor"),
            P("section", None, "tensor"),
            P("tensor", "section"),
            P(("dp", "section", "tensor"), None),
        ),
        out_specs=(P(("dp", "section", "tensor"), None), P(("dp", "section", "tensor"), None)),
        check_vma=False,
    )
```

time: 497 us -> 407 us (0.82)
  waiting for transfers between devices: 354 us -> 203 us
  starting transfers between devices: 1.94 us -> 93.5 us
  blocking collectives: 38.1 us -> 0 us
  Pallas kernels: 0 us -> 11.6 us
  matrix products: 62.1 us -> 51 us
  local copies, waits for them, and re-layouts: 13.1 us -> 18.3 us
    reduce_scatter x3 -> x0, waiting for transfers between devices: 178 us -> none  [the longest x1 136 us: per_device(): lax.psum_scatter(jnp.dot(piece, w_down, preferred_element_type=jnp.float3...]
    ppermute x2 -> x31, waiting for transfers between devices: 0.81 us -> 167 us  [the longest x6 70.8 us: ffn_part(): lax.ppermute(send_up.astype(BF16), 'tensor', [(i, i + 1) for i in range(s...]
    all_gather x7 -> x4, waiting for transfers between devices: 172 us -> 35.3 us  [the longest x1 35.2 us: per_device(): lax.all_gather(out_share, ('dp', 'section', 'tensor'), axis=0, tiled=False)]
    ppermute x2 -> x31, starting transfers between devices: 1.36 us -> 67.2 us  [the longest x9 27.8 us: from_slots(): lax.ppermute(value, 'tensor', [(i, (i - o) % count) for i in range(count)])]
    all_gather x2 -> x0, blocking collectives: 38.1 us -> none  [the longest x1 21.9 us: per_device(): lax.all_gather(selfin, 'tensor', axis=0, tiled=True)]
    all_to_all x0 -> x1, starting transfers between devices: none -> 26.2 us  [per_device(): lax.all_to_all(parts, ('section', 'tensor'), split_axis=0, concat_axis=0,...]
    pallas_call x0 -> x2, Pallas kernels: none -> 11.6 us  [the longest x1 7.6 us: attend_own_keys(): pl.pallas_call(functools.partial(attend_kernel, sections), grid=(heads, s...]
    dot_general x8 -> x14, matrix products: 62.1 us -> 51 us  [the longest x2 17.8 us: ffn_part(): gate = jnp.dot(x, w_gate, preferred_element_type=F32)]
  transfers between devices with their start and end apart: 12 -> 36, of which waited for: 7 -> 20; matrix products, arithmetic and copies ran while one was open for 17% -> 17% of each run, Pallas kernels for 0% -> 2%
where the time goes in v1:
time: 407 us; the launch traced here: 406 us
  waiting for transfers between devices  203 us (50%)
  starting transfers between devices  93.5 us (23%)
  matrix products  51 us (13%)
  local copies, waits for them, and re-layouts  18.3 us (4%)
  between operations  14.6 us (4%)
  other arithmetic  13.9 us (3%)
  Pallas kernels  11.6 us (3%)
    ppermute x6, waiting for transfers between devices, ffn_part(): lax.ppermute(send_up.astype(BF16), 'tensor', [(i, i + 1) for i in range(s...  70.8 us
    ppermute x9, waiting for transfers between devices, from_slots(): lax.ppermute(value, 'tensor', [(i, (i - o) % count) for i in range(count)])  45.5 us
    all_gather x1, waiting for transfers between devices, per_device(): lax.all_gather(out_share, ('dp', 'section', 'tensor'), axis=0, tiled=False)  35.2 us
    ppermute x6, waiting for transfers between devices, ffn_part(): lax.ppermute(send_down.astype(BF16), 'tensor', [(i, i - 1) for i in range...  33.4 us
    ppermute x9, starting transfers between devices, from_slots(): lax.ppermute(value, 'tensor', [(i, (i - o) % count) for i in range(count)])  27.8 us
    all_to_all x1, starting transfers between devices, per_device(): lax.all_to_all(parts, ('section', 'tensor'), split_axis=0, concat_axis=0,...  26.2 us
    ppermute x6, starting transfers between devices, ffn_part(): lax.ppermute(send_up.astype(BF16), 'tensor', [(i, i + 1) for i in range(s...  21 us
    dot_general x2, matrix products, ffn_part(): gate = jnp.dot(x, w_gate, preferred_element_type=F32)  17.8 us
  transfers between devices with their start and end apart: 36, of which 20 were waited for; matrix products, arithmetic and copies ran while one was open for 17% of the time, Pallas kernels for 2%

profile of v1, /device:TPU:0, one launch (start us, length us, event | category | flops | bytes accessed | tf_op | source)
XLA Modules:
  0.0 405.9 jit_solution(12754289229171934443)
XLA Ops:
  7.2 1.7 fusion.3
  8.9 1.6 fusion.5
  10.5 1.1 fusion.63
  12.7 0.9 copy.31
  14.5 0.9 collective-permute-done.14
  15.4 5.0 %collective-permute-start.15 = (bf16[32,2048]{1,0:T(8,128)(2,1)S(1)}, bf16[32,2048]{1,0:T(8,128)(2,1)S(1)}, u32[]{:S(2)}, u32[]{:S(2)}) collective-permute-start(bf16[32,2048]{1,0:T(8,128)(2,1)S(1)} %maximum_select_fusion.1), channel_id=1, source_target_pairs={{0,3},{1,0},{2,1},{3,2},{4,7},{5,4},{6,5},{7,6},{8,11},{9,8},{10,9... | collective-permute-start | bytes 393224 | tf_op jit(solution)/shard_map/ppermute | solution.py:36
  20.4 1.0 collective-permute-start.17
  21.5 4.6 %collective-permute-done.15 = bf16[32,2048]{1,0:T(8,128)(2,1)S(1)} collective-permute-done((bf16[32,2048]{1,0:T(8,128)(2,1)S(1)}, bf16[32,2048]{1,0:T(8,128)(2,1)S(1)}, u32[]{:S(2)}, u32[]{:S(2)}) %collective-permute-start.15) | collective-permute-done | bytes 131104 | tf_op jit(solution)/shard_map/ppermute | solution.py:36
  26.1 14.4 %collective-permute-done.16 = bf16[32,2048]{1,0:T(8,128)(2,1)S(1)} collective-permute-done((bf16[32,2048]{1,0:T(8,128)(2,1)S(1)}, bf16[32,2048]{1,0:T(8,128)(2,1)S(1)}, u32[]{:S(2)}, u32[]{:S(2)}) %collective-permute-start.16) | collective-permute-done | bytes 131104 | tf_op jit(solution)/shard_map/ppermute | solution.py:36
  40.5 1.5 convolution_bitcast_fusion
  42.0 1.5 convolution_bitcast_fusion.1
  43.6 1.6 convolution_bitcast_fusion.2
  45.6 1.5 collective-permute-done.18
  47.9 4.6 %collective-permute-start.19 = (bf16[32,2048]{1,0:T(8,128)(2,1)S(1)}, bf16[32,2048]{1,0:T(8,128)(2,1)S(1)}, u32[]{:S(2)}, u32[]{:S(2)}) collective-permute-start(bf16[32,2048]{1,0:T(8,128)(2,1)S(1)} %get-tuple-element.12), channel_id=1, source_target_pairs={{0,1},{1,2},{2,3},{3,0},{4,5},{5,6},{6,7},{7,4},{8,9},{9,10},{10,1... | collective-permute-start | bytes 393224 | tf_op jit(solution)/shard_map/ppermute | solution.py:265
  52.5 3.8 collective-permute-start.20
  56.3 2.8 collective-permute-start.21
  59.2 11.1 %collective-permute-done.20 = bf16[32,2048]{1,0:T(8,128)(2,1)S(1)} collective-permute-done((bf16[32,2048]{1,0:T(8,128)(2,1)S(1)}, bf16[32,2048]{1,0:T(8,128)(2,1)S(1)}, u32[]{:S(2)}, u32[]{:S(2)}) %collective-permute-start.20) | collective-permute-done | bytes 131104 | tf_op jit(solution)/shard_map/ppermute | solution.py:265
  70.5 1.3 collective-permute-done.22
  72.3 1.1 collective-permute-done.23
  73.5 10.4 %collective-permute-start.24 = (bf16[32,2048]{1,0:T(8,128)(2,1)S(1)}, bf16[32,2048]{1,0:T(8,128)(2,1)S(1)}, u32[]{:S(2)}, u32[]{:S(2)}) collective-permute-start(bf16[32,2048]{1,0:T(8,128)(2,1)S(1)} %maximum_select_fusion.2), channel_id=1, source_target_pairs={{0,3},{1,0},{2,1},{3,2},{4,7},{5,4},{6,5},{7,6},{8,11},{9,8},{10,9... | collective-permute-start | bytes 393224 | tf_op jit(solution)/shard_map/ppermute | solution.py:36
  84.5 1.7 constant_dynamic-slice_fusion.8
  86.8 3.0 copy.27
  89.8 14.5 %collective-permute-done.25 = bf16[32,2048]{1,0:T(8,128)(2,1)S(1)} collective-permute-done((bf16[32,2048]{1,0:T(8,128)(2,1)S(1)}, bf16[32,2048]{1,0:T(8,128)(2,1)S(1)}, u32[]{:S(2)}, u32[]{:S(2)}) %collective-permute-start.25) | collective-permute-done | bytes 131104 | tf_op jit(solution)/shard_map/ppermute | solution.py:36
  104.8 1.3 collective-permute-done.27
  106.2 8.7 %collective-permute-start.29 = (bf16[128,256]{1,0:T(8,128)(2,1)S(1)}, bf16[128,256]{1,0:T(8,128)(2,1)S(1)}, u32[]{:S(2)}, u32[]{:S(2)}) collective-permute-start(bf16[128,256]{1,0:T(8,128)(2,1)S(1)} %bitcast.78), channel_id=1, source_target_pairs={{0,2},{1,3},{2,0},{3,1},{4,6},{5,7},{6,4},{7,5},{8,10},{9,11},{10,... | collective-permute-start | bytes 196616 | tf_op jit(solution)/shard_map/ppermute | solution.py:36
  114.9 1.9 collective-permute-start.30
  117.6 11.2 %collective-permute-done.29 = bf16[128,256]{1,0:T(8,128)(2,1)S(1)} collective-permute-done((bf16[128,256]{1,0:T(8,128)(2,1)S(1)}, bf16[128,256]{1,0:T(8,128)(2,1)S(1)}, u32[]{:S(2)}, u32[]{:S(2)}) %collective-permute-start.29) | collective-permute-done | bytes 65568 | tf_op jit(solution)/shard_map/ppermute | solution.py:36
  128.9 9.3 %fusion.66 = f32[512,1024]{1,0:T(8,128)S(1)} fusion(bf16[512,4096]{1,0:T(8,128)(2,1)} %all-gather.7.cloned.1.call-done, bf16[4096,1024]{1,0:T(8,128)(2,1)} %param.18), kind=kOutput, calls=%fused_computation.150 | convolution fusion | flops 4294967296 | bytes 14680064 | tf_op jit(solution)/shard_map/dot_general | solution.py:56
  138.2 8.4 %fusion.15 = bf16[512,1024]{1,0:T(8,128)(2,1)S(1)} fusion(f32[512,1024]{1,0:T(8,128)S(1)} %fusion.66, bf16[512,4096]{1,0:T(8,128)(2,1)S(1)} %copy-done.15, bf16[4096,1024]{1,0:T(8,128)(2,1)} %param.19), kind=kOutput, calls=%fused_computation.27 | convolution fusion | flops 4300210176 | bytes 15728640 | tf_op jit(solution)/shard_map/dot_general | solution.py:57
  146.7 3.7 convolution_convert_fusion.2
  150.4 8.5 %fusion.67 = f32[512,1024]{1,0:T(8,128)S(1)} fusion(bf16[512,4096]{1,0:T(8,128)(2,1)} %all-gather.9.cloned.1.call-done, bf16[4096,1024]{1,0:T(8,128)(2,1)} %param.18), kind=kOutput, calls=%fused_computation.151 | convolution fusion | flops 4294967296 | bytes 14680064 | tf_op jit(solution)/shard_map/dot_general | solution.py:56
  158.9 8.4 %fusion.24 = bf16[512,1024]{1,0:T(8,128)(2,1)S(1)} fusion(f32[512,1024]{1,0:T(8,128)S(1)} %fusion.67, bf16[512,4096]{1,0:T(8,128)(2,1)S(1)} %copy-done.14, bf16[4096,1024]{1,0:T(8,128)(2,1)} %param.19), kind=kOutput, calls=%fused_computation.36 | convolution fusion | flops 4300210176 | bytes 15728640 | tf_op jit(solution)/shard_map/dot_general | solution.py:57
  167.4 2.3 convolution_convert_fusion
  170.3 2.3 convolution_convert_fusion.3
  172.7 1.2 fusion.27
  173.8 2.1 collective-permute-start.1
  175.9 2.3 convolution_convert_fusion.1
  178.4 1.3 collective-permute-start.8
  179.7 19.6 %collective-permute-done.1 = bf16[64,4096]{1,0:T(8,128)(2,1)S(1)} collective-permute-done((bf16[64,4096]{1,0:T(8,128)(2,1)S(1)}, bf16[64,4096]{1,0:T(8,128)(2,1)S(1)}, u32[]{:S(2)}, u32[]{:S(2)}) %collective-permute-start.1) | collective-permute-done | bytes 524320 | tf_op jit(solution)/shard_map/ppermute | solution.py:78
  199.3 1.2 add_convert_fusion.7
  200.6 4.4 %collective-permute-start.2 = (bf16[64,4096]{1,0:T(8,128)(2,1)S(1)}, bf16[64,4096]{1,0:T(8,128)(2,1)S(1)}, u32[]{:S(2)}, u32[]{:S(2)}) collective-permute-start(bf16[64,4096]{1,0:T(8,128)(2,1)S(1)} %add_convert_fusion.7), channel_id=1, source_target_pairs={{0,1},{1,2},{4,5},{5,6},{8,9},{9,10},{12,13},{13,14},{16,17},{17,1... | collective-permute-start | bytes 1572872 | tf_op jit(solution)/shard_map/ppermute | solution.py:78
  205.0 9.8 %collective-permute-done.8 = bf16[64,4096]{1,0:T(8,128)(2,1)S(1)} collective-permute-done((bf16[64,4096]{1,0:T(8,128)(2,1)S(1)}, bf16[64,4096]{1,0:T(8,128)(2,1)S(1)}, u32[]{:S(2)}, u32[]{:S(2)}) %collective-permute-start.8) | collective-permute-done | bytes 524320 | tf_op jit(solution)/shard_map/ppermute | solution.py:78
  215.0 4.4 %collective-permute-start.9 = (bf16[64,4096]{1,0:T(8,128)(2,1)S(1)}, bf16[64,4096]{1,0:T(8,128)(2,1)S(1)}, u32[]{:S(2)}, u32[]{:S(2)}) collective-permute-start(bf16[64,4096]{1,0:T(8,128)(2,1)S(1)} %add_convert_fusion.3), channel_id=1, source_target_pairs={{0,1},{1,2},{4,5},{5,6},{8,9},{9,10},{12,13},{13,14},{16,17},{17,1... | collective-permute-start | bytes 1572872 | tf_op jit(solution)/shard_map/ppermute | solution.py:78
  219.4 15.5 %collective-permute-done.2 = bf16[64,4096]{1,0:T(8,128)(2,1)S(1)} collective-permute-done((bf16[64,4096]{1,0:T(8,128)(2,1)S(1)}, bf16[64,4096]{1,0:T(8,128)(2,1)S(1)}, u32[]{:S(2)}, u32[]{:S(2)}) %collective-permute-start.2) | collective-permute-done | bytes 524320 | tf_op jit(solution)/shard_map/ppermute | solution.py:78
  234.9 1.3 add_convert_fusion.6
  236.8 4.4 %collective-permute-start.3 = (bf16[64,4096]{1,0:T(8,128)(2,1)S(1)}, bf16[64,4096]{1,0:T(8,128)(2,1)S(1)}, u32[]{:S(2)}, u32[]{:S(2)}) collective-permute-start(bf16[64,4096]{1,0:T(8,128)(2,1)S(1)} %get-tuple-element.6), channel_id=1, source_target_pairs={{0,1},{1,2},{2,3},{4,5},{5,6},{6,7},{8,9},{9,10},{10,11},{12,13},{... | collective-permute-start | bytes 1572872 | tf_op jit(solution)/shard_map/ppermute | solution.py:78
  241.2 16.1 %collective-permute-done.9 = bf16[64,4096]{1,0:T(8,128)(2,1)S(1)} collective-permute-done((bf16[64,4096]{1,0:T(8,128)(2,1)S(1)}, bf16[64,4096]{1,0:T(8,128)(2,1)S(1)}, u32[]{:S(2)}, u32[]{:S(2)}) %collective-permute-start.9) | collective-permute-done | bytes 524320 | tf_op jit(solution)/shard_map/ppermute | solution.py:78
  258.3 4.4 %collective-permute-start.10 = (bf16[64,4096]{1,0:T(8,128)(2,1)S(1)}, bf16[64,4096]{1,0:T(8,128)(2,1)S(1)}, u32[]{:S(2)}, u32[]{:S(2)}) collective-permute-start(bf16[64,4096]{1,0:T(8,128)(2,1)S(1)} %get-tuple-element.8), channel_id=1, source_target_pairs={{0,1},{1,2},{2,3},{4,5},{5,6},{6,7},{8,9},{9,10},{10,11},{12,13},{... | collective-permute-start | bytes 1572872 | tf_op jit(solution)/shard_map/ppermute | solution.py:78
  262.7 1.2 add_convert_fusion.5
  263.9 1.0 collective-permute-start.5
  265.8 1.2 add_convert_fusion.4
  267.1 1.3 collective-permute-start.6
  268.6 1.3 collective-permute-start.13
  269.9 9.9 %collective-permute-done.3 = bf16[64,4096]{1,0:T(8,128)(2,1)S(1)} collective-permute-done((bf16[64,4096]{1,0:T(8,128)(2,1)S(1)}, bf16[64,4096]{1,0:T(8,128)(2,1)S(1)}, u32[]{:S(2)}, u32[]{:S(2)}) %collective-permute-start.3) | collective-permute-done | bytes 524320 | tf_op jit(solution)/shard_map/ppermute | solution.py:78
  279.8 21.1 %collective-permute-done.6 = bf16[64,4096]{1,0:T(8,128)(2,1)S(1)} collective-permute-done((bf16[64,4096]{1,0:T(8,128)(2,1)S(1)}, bf16[64,4096]{1,0:T(8,128)(2,1)S(1)}, u32[]{:S(2)}, u32[]{:S(2)}) %collective-permute-start.6) | collective-permute-done | bytes 524320 | tf_op jit(solution)/shard_map/ppermute | solution.py:79
  300.8 1.3 convert_add_fusion.5
  302.2 12.4 %collective-permute-done.13 = bf16[64,4096]{1,0:T(8,128)(2,1)S(1)} collective-permute-done((bf16[64,4096]{1,0:T(8,128)(2,1)S(1)}, bf16[64,4096]{1,0:T(8,128)(2,1)S(1)}, u32[]{:S(2)}, u32[]{:S(2)}) %collective-permute-start.13) | collective-permute-done | bytes 524320 | tf_op jit(solution)/shard_map/ppermute | solution.py:79
  315.6 1.0 copy-done.7
  316.9 6.0 %copy-done.2 = bf16[64,512,256]{2,1,0:T(8,128)(2,1)S(1)} copy-done((bf16[64,512,256]{2,1,0:T(8,128)(2,1)S(1)}, bf16[64,512,256]{2,1,0:T(8,128)(2,1)}, u32[]{:S(2)}) %copy-start.2) | copy-done | bytes 16777240
  323.0 7.6 %attend_own_keys.1 = bf16[128,1152]{1,0:T(8,128)(2,1)} custom-call(bf16[128,4096]{1,0:T(8,128)(2,1)S(1)} %fusion.2.mem_ref, bf16[4,2,4,2,512,256]{5,4,3,2,1,0:T(8,128)(2,1)S(1)} %bitcast.72, bf16[4,128,256]{2,1,0:T(8,128)(2,1)S(1)} %constant_dynamic-slice_fusion.cq_ref), custom_call_target="tpu_custom_call" | custom-call | flops 2147483648 | bytes 16777216 | tf_op jit(solution)/shard_map/attend_own_keys/pallas_call | solution.py:133
  330.6 26.2 %all-to-all-start = ((bf16[8,16,1152]{2,1,0:T(8,128)(2,1)}), bf16[8,16,1152]{2,1,0:T(8,128)(2,1)S(1)}, u32[]{:S(2)}, u32[]{:S(2)}) async-start(bf16[8,16,1152]{2,1,0:T(8,128)(2,1)} %bitcast.20), calls=%async_computation | async-start | bytes 589824 | tf_op jit(solution)/shard_map/all_to_all | solution.py:288
  356.7 35.2 %all-gather.13.cloned.1.call-done = bf16[8192,512]{1,0:T(8,128)(2,1)} async-done(((bf16[256,512]{1,0:T(8,128)(2,1)}), bf16[8192,512]{1,0:T(8,128)(2,1)}) %all-gather.13.cloned.1.call-update) | async-done | bytes 8388624 | tf_op jit(solution)/shard_map/all_gather | solution.py:242
  392.0 3.4 copy-done.3
  395.3 4.0 finish.1
  (132 shorter events, 11.7 us)
Async XLA Ops:
  7.2 5.2 %copy-start = (bf16[2048,2,256]{2,1,0:T(2,128)(2,1)S(1)}, bf16[2048,2,256]{2,1,0:T(2,128)(2,1)}, u32[]{:S(2)}) copy-start(bf16[2048,2,256]{2,1,0:T(2,128)(2,1)} %param.29) | copy-start | bytes 6291460
  7.2 121.7 %all-gather.7.cloned.1.call-start = ((), (), s32[]{:S(2)}) async-start(), calls=%async_computation.1 | async-start | bytes 4718592 | tf_op jit(solution)/shard_map/all_gather | solution.py:232
  11.5 2.2 copy-start.8
  11.5 2.3 copy-start.12
  11.6 138.8 %all-gather.9.cloned.1.call-start = ((), (), s32[]{:S(2)}) async-start(), calls=%async_computation.2 | async-start | bytes 4718592 | tf_op jit(solution)/shard_map/all_gather | solution.py:232
  12.3 304.6 %all-gather.11.cloned.1.call-start = ((), (), s32[]{:S(2)}) async-start(), calls=%async_computation.3 | async-start | bytes 17301504 | tf_op jit(solution)/shard_map/all_gather | solution.py:238
  13.6 378.3 %all-gather.13.cloned.1.call-start = ((), (), s32[]{:S(2)}) async-start(), calls=%async_computation.4 | async-start | bytes 8650752 | tf_op jit(solution)/shard_map/all_gather | solution.py:242
  14.0 1.4 collective-permute-start.14
  15.4 10.6 %collective-permute-start.15 = (bf16[32,2048]{1,0:T(8,128)(2,1)S(1)}, bf16[32,2048]{1,0:T(8,128)(2,1)S(1)}, u32[]{:S(2)}, u32[]{:S(2)}) collective-permute-start(bf16[32,2048]{1,0:T(8,128)(2,1)S(1)} %maximum_select_fusion.1), channel_id=1, source_target_pairs={{0,3},{1,0},{2,1},{3,2},{4,7},{5,4},{6,5},{7,6},{8,11},{9,8},{10,9... | collective-permute-start | bytes 393224 | tf_op jit(solution)/shard_map/ppermute | solution.py:36
  20.4 20.0 %collective-permute-start.16 = (bf16[32,2048]{1,0:T(8,128)(2,1)S(1)}, bf16[32,2048]{1,0:T(8,128)(2,1)S(1)}, u32[]{:S(2)}, u32[]{:S(2)}) collective-permute-start(bf16[32,2048]{1,0:T(8,128)(2,1)S(1)} %maximum_select_fusion.1), channel_id=1, source_target_pairs={{0,2},{1,3},{2,0},{3,1},{4,6},{5,7},{6,4},{7,5},{8,10},{9,11},{10,... | collective-permute-start | bytes 393224 | tf_op jit(solution)/shard_map/ppermute | solution.py:36
  20.4 20.0 %collective-permute-start.17 = (bf16[32,2048]{1,0:T(8,128)(2,1)S(1)}, bf16[32,2048]{1,0:T(8,128)(2,1)S(1)}, u32[]{:S(2)}, u32[]{:S(2)}) collective-permute-start(bf16[32,2048]{1,0:T(8,128)(2,1)S(1)} %maximum_select_fusion.1), channel_id=1, source_target_pairs={{0,1},{1,2},{2,3},{3,0},{4,5},{5,6},{6,7},{7,4},{8,9},{9,10},{10,1... | collective-permute-start | bytes 393224 | tf_op jit(solution)/shard_map/ppermute | solution.py:36
  43.6 3.8 copy-start.9
  45.3 1.8 collective-permute-start.18
  47.3 24.6 %copy-start.13 = (f32[4096]{0:T(1024)S(1)}, f32[4096]{0:T(1024)}, u32[]{:S(2)}) copy-start(f32[4096]{0:T(1024)} %param.27) | copy-start | bytes 49156
  47.8 38.4 %copy-start.10 = (s32[128,1024]{1,0:T(8,128)S(1)}, s32[128,1024]{1,0:T(8,128)}, u32[]{:S(2)}) copy-start(s32[128,1024]{1,0:T(8,128)} %param.21) | copy-start | bytes 1572868
  47.9 11.3 %collective-permute-start.19 = (bf16[32,2048]{1,0:T(8,128)(2,1)S(1)}, bf16[32,2048]{1,0:T(8,128)(2,1)S(1)}, u32[]{:S(2)}, u32[]{:S(2)}) collective-permute-start(bf16[32,2048]{1,0:T(8,128)(2,1)S(1)} %get-tuple-element.12), channel_id=1, source_target_pairs={{0,1},{1,2},{2,3},{3,0},{4,5},{5,6},{6,7},{7,4},{8,9},{9,10},{10,1... | collective-permute-start | bytes 393224 | tf_op jit(solution)/shard_map/ppermute | solution.py:265
  52.5 17.8 %collective-permute-start.20 = (bf16[32,2048]{1,0:T(8,128)(2,1)S(1)}, bf16[32,2048]{1,0:T(8,128)(2,1)S(1)}, u32[]{:S(2)}, u32[]{:S(2)}) collective-permute-start(bf16[32,2048]{1,0:T(8,128)(2,1)S(1)} %get-tuple-element.14), channel_id=1, source_target_pairs={{0,2},{1,3},{2,0},{3,1},{4,6},{5,7},{6,4},{7,5},{8,10},{9,11},{10,... | collective-permute-start | bytes 393224 | tf_op jit(solution)/shard_map/ppermute | solution.py:265
  56.3 14.0 %collective-permute-start.21 = (bf16[32,2048]{1,0:T(8,128)(2,1)S(1)}, bf16[32,2048]{1,0:T(8,128)(2,1)S(1)}, u32[]{:S(2)}, u32[]{:S(2)}) collective-permute-start(bf16[32,2048]{1,0:T(8,128)(2,1)S(1)} %get-tuple-element.13), channel_id=1, source_target_pairs={{0,3},{1,0},{2,1},{3,2},{4,7},{5,4},{6,5},{7,6},{8,11},{9,8},{10,9... | collective-permute-start | bytes 393224 | tf_op jit(solution)/shard_map/ppermute | solution.py:265
  70.4 1.4 collective-permute-start.22
  72.1 1.3 collective-permute-start.23
  73.5 16.3 %collective-permute-start.24 = (bf16[32,2048]{1,0:T(8,128)(2,1)S(1)}, bf16[32,2048]{1,0:T(8,128)(2,1)S(1)}, u32[]{:S(2)}, u32[]{:S(2)}) collective-permute-start(bf16[32,2048]{1,0:T(8,128)(2,1)S(1)} %maximum_select_fusion.2), channel_id=1, source_target_pairs={{0,3},{1,0},{2,1},{3,2},{4,7},{5,4},{6,5},{7,6},{8,11},{9,8},{10,9... | collective-permute-start | bytes 393224 | tf_op jit(solution)/shard_map/ppermute | solution.py:36
  83.8 20.5 %collective-permute-start.25 = (bf16[32,2048]{1,0:T(8,128)(2,1)S(1)}, bf16[32,2048]{1,0:T(8,128)(2,1)S(1)}, u32[]{:S(2)}, u32[]{:S(2)}) collective-permute-start(bf16[32,2048]{1,0:T(8,128)(2,1)S(1)} %maximum_select_fusion.2), channel_id=1, source_target_pairs={{0,2},{1,3},{2,0},{3,1},{4,6},{5,7},{6,4},{7,5},{8,10},{9,11},{10,... | collective-permute-start | bytes 393224 | tf_op jit(solution)/shard_map/ppermute | solution.py:36
  83.8 20.5 %collective-permute-start.26 = (bf16[32,2048]{1,0:T(8,128)(2,1)S(1)}, bf16[32,2048]{1,0:T(8,128)(2,1)S(1)}, u32[]{:S(2)}, u32[]{:S(2)}) collective-permute-start(bf16[32,2048]{1,0:T(8,128)(2,1)S(1)} %maximum_select_fusion.2), channel_id=1, source_target_pairs={{0,1},{1,2},{2,3},{3,0},{4,5},{5,6},{6,7},{7,4},{8,9},{9,10},{10,1... | collective-permute-start | bytes 393224 | tf_op jit(solution)/shard_map/ppermute | solution.py:36
  86.8 17.5 %copy-start.16 = (bf16[2048,256]{1,0:T(8,128)(2,1)S(1)}, bf16[2048,256]{1,0:T(8,128)(2,1)}, u32[]{:S(2)}) copy-start(bf16[2048,256]{1,0:T(8,128)(2,1)} %param.28) | copy-start | bytes 3145732
  104.6 1.4 collective-permute-start.27
  106.1 11.5 %collective-permute-start.28 = (bf16[128,256]{1,0:T(8,128)(2,1)S(1)}, bf16[128,256]{1,0:T(8,128)(2,1)S(1)}, u32[]{:S(2)}, u32[]{:S(2)}) collective-permute-start(bf16[128,256]{1,0:T(8,128)(2,1)S(1)} %bitcast.77), channel_id=1, source_target_pairs={{0,3},{1,0},{2,1},{3,2},{4,7},{5,4},{6,5},{7,6},{8,11},{9,8},{10,9... | collective-permute-start | bytes 196616 | tf_op jit(solution)/shard_map/ppermute | solution.py:36
  106.2 22.6 %collective-permute-start.29 = (bf16[128,256]{1,0:T(8,128)(2,1)S(1)}, bf16[128,256]{1,0:T(8,128)(2,1)S(1)}, u32[]{:S(2)}, u32[]{:S(2)}) collective-permute-start(bf16[128,256]{1,0:T(8,128)(2,1)S(1)} %bitcast.78), channel_id=1, source_target_pairs={{0,2},{1,3},{2,0},{3,1},{4,6},{5,7},{6,4},{7,5},{8,10},{9,11},{10,... | collective-permute-start | bytes 196616 | tf_op jit(solution)/shard_map/ppermute | solution.py:36
  114.9 13.9 %collective-permute-start.30 = (bf16[128,256]{1,0:T(8,128)(2,1)S(1)}, bf16[128,256]{1,0:T(8,128)(2,1)S(1)}, u32[]{:S(2)}, u32[]{:S(2)}) collective-permute-start(bf16[128,256]{1,0:T(8,128)(2,1)S(1)} %bitcast.79), channel_id=1, source_target_pairs={{0,1},{1,2},{2,3},{3,0},{4,5},{5,6},{6,7},{7,4},{8,9},{9,10},{10,1... | collective-permute-start | bytes 196616 | tf_op jit(solution)/shard_map/ppermute | solution.py:36
  128.9 9.3 %copy-start.15 = (bf16[512,4096]{1,0:T(8,128)(2,1)S(1)}, bf16[512,4096]{1,0:T(8,128)(2,1)}, u32[]{:S(2)}) copy-start(bf16[512,4096]{1,0:T(8,128)(2,1)} %all-gather.7.cloned.1.call-done) | copy-start | bytes 12582916
  128.9 17.7 %slice-start = ((s8[8388608]{0:T(1024)(128)(4,1)}), s8[4194304]{0:T(1024)(128)(4,1)S(1)}, s32[]{:S(2)}) async-start(s8[8388608]{0:T(1024)(128)(4,1)} %bitcast.84), calls=%async_computation.5 | async-start | bytes 8388608
  138.2 8.4 %slice-start.1 = ((s8[8388608]{0:T(1024)(128)(4,1)}), s8[4194304]{0:T(1024)(128)(4,1)S(1)}, s32[]{:S(2)}) async-start(s8[8388608]{0:T(1024)(128)(4,1)} %bitcast.84), calls=%async_computation.6 | async-start | bytes 8388608
  150.4 22.3 %collective-permute-start = (bf16[256,4096]{1,0:T(8,128)(2,1)}, bf16[256,4096]{1,0:T(8,128)(2,1)}, u32[]{:S(2)}, u32[]{:S(2)}) collective-permute-start(bf16[256,4096]{1,0:T(8,128)(2,1)} %convolution_convert_fusion.2), channel_id=1, source_target_pairs={{0,4},{4,0},{1,5},{5,1},{2,6},{6,2},{3,7},{7,3},{8,12},{12,8},{9,1... | collective-permute-start | bytes 6291464 | tf_op jit(solution)/shard_map/ppermute | solution.py:31
  150.4 8.5 %copy-start.14 = (bf16[512,4096]{1,0:T(8,128)(2,1)S(1)}, bf16[512,4096]{1,0:T(8,128)(2,1)}, u32[]{:S(2)}) copy-start(bf16[512,4096]{1,0:T(8,128)(2,1)} %all-gather.9.cloned.1.call-done) | copy-start | bytes 12582916
  150.4 16.9 %slice-start.2 = ((s8[8388608]{0:T(1024)(128)(4,1)}), s8[4194304]{0:T(1024)(128)(4,1)S(1)}, s32[]{:S(2)}) async-start(s8[8388608]{0:T(1024)(128)(4,1)} %bitcast.86), calls=%async_computation.7 | async-start | bytes 8388608
  158.9 8.4 %slice-start.3 = ((s8[8388608]{0:T(1024)(128)(4,1)}), s8[4194304]{0:T(1024)(128)(4,1)S(1)}, s32[]{:S(2)}) async-start(s8[8388608]{0:T(1024)(128)(4,1)} %bitcast.86), calls=%async_computation.8 | async-start | bytes 8388608
  169.7 8.5 %collective-permute-start.7 = (bf16[256,4096]{1,0:T(8,128)(2,1)S(1)}, bf16[256,4096]{1,0:T(8,128)(2,1)S(1)}, u32[]{:S(2)}, u32[]{:S(2)}) collective-permute-start(bf16[256,4096]{1,0:T(8,128)(2,1)S(1)} %convolution_convert_fusion), channel_id=1, source_target_pairs={{0,4},{4,0},{1,5},{5,1},{2,6},{6,2},{3,7},{7,3},{8,12},{12,8},{9,1... | collective-permute-start | bytes 6291464 | tf_op jit(solution)/shard_map/ppermute | solution.py:31
  173.8 25.5 %collective-permute-start.1 = (bf16[64,4096]{1,0:T(8,128)(2,1)S(1)}, bf16[64,4096]{1,0:T(8,128)(2,1)S(1)}, u32[]{:S(2)}, u32[]{:S(2)}) collective-permute-start(bf16[64,4096]{1,0:T(8,128)(2,1)S(1)} %fusion.27), channel_id=1, source_target_pairs={{0,1},{4,5},{8,9},{12,13},{16,17},{20,21},{24,25},{28,29}} | collective-permute-start | bytes 1572872 | tf_op jit(solution)/shard_map/ppermute | solution.py:78
  178.4 36.4 %collective-permute-start.8 = (bf16[64,4096]{1,0:T(8,128)(2,1)S(1)}, bf16[64,4096]{1,0:T(8,128)(2,1)S(1)}, u32[]{:S(2)}, u32[]{:S(2)}) collective-permute-start(bf16[64,4096]{1,0:T(8,128)(2,1)S(1)} %fusion.29), channel_id=1, source_target_pairs={{0,1},{4,5},{8,9},{12,13},{16,17},{20,21},{24,25},{28,29}} | collective-permute-start | bytes 1572872 | tf_op jit(solution)/shard_map/ppermute | solution.py:78
  200.6 34.3 %collective-permute-start.2 = (bf16[64,4096]{1,0:T(8,128)(2,1)S(1)}, bf16[64,4096]{1,0:T(8,128)(2,1)S(1)}, u32[]{:S(2)}, u32[]{:S(2)}) collective-permute-start(bf16[64,4096]{1,0:T(8,128)(2,1)S(1)} %add_convert_fusion.7), channel_id=1, source_target_pairs={{0,1},{1,2},{4,5},{5,6},{8,9},{9,10},{12,13},{13,14},{16,17},{17,1... | collective-permute-start | bytes 1572872 | tf_op jit(solution)/shard_map/ppermute | solution.py:78
  215.0 42.4 %collective-permute-start.9 = (bf16[64,4096]{1,0:T(8,128)(2,1)S(1)}, bf16[64,4096]{1,0:T(8,128)(2,1)S(1)}, u32[]{:S(2)}, u32[]{:S(2)}) collective-permute-start(bf16[64,4096]{1,0:T(8,128)(2,1)S(1)} %add_convert_fusion.3), channel_id=1, source_target_pairs={{0,1},{1,2},{4,5},{5,6},{8,9},{9,10},{12,13},{13,14},{16,17},{17,1... | collective-permute-start | bytes 1572872 | tf_op jit(solution)/shard_map/ppermute | solution.py:78
  236.1 26.6 %collective-permute-start.4 = (bf16[64,4096]{1,0:T(8,128)(2,1)S(1)}, bf16[64,4096]{1,0:T(8,128)(2,1)S(1)}, u32[]{:S(2)}, u32[]{:S(2)}) collective-permute-start(bf16[64,4096]{1,0:T(8,128)(2,1)S(1)} %get-tuple-element.7), channel_id=1, source_target_pairs={{3,2},{7,6},{11,10},{15,14},{19,18},{23,22},{27,26},{31,30}} | collective-permute-start | bytes 1572872 | tf_op jit(solution)/shard_map/ppermute | solution.py:79
  236.8 43.0 %collective-permute-start.3 = (bf16[64,4096]{1,0:T(8,128)(2,1)S(1)}, bf16[64,4096]{1,0:T(8,128)(2,1)S(1)}, u32[]{:S(2)}, u32[]{:S(2)}) collective-permute-start(bf16[64,4096]{1,0:T(8,128)(2,1)S(1)} %get-tuple-element.6), channel_id=1, source_target_pairs={{0,1},{1,2},{2,3},{4,5},{5,6},{6,7},{8,9},{9,10},{10,11},{12,13},{... | collective-permute-start | bytes 1572872 | tf_op jit(solution)/shard_map/ppermute | solution.py:78
  257.6 7.3 %collective-permute-start.11 = (bf16[64,4096]{1,0:T(8,128)(2,1)S(1)}, bf16[64,4096]{1,0:T(8,128)(2,1)S(1)}, u32[]{:S(2)}, u32[]{:S(2)}) collective-permute-start(bf16[64,4096]{1,0:T(8,128)(2,1)S(1)} %get-tuple-element.9), channel_id=1, source_target_pairs={{3,2},{7,6},{11,10},{15,14},{19,18},{23,22},{27,26},{31,30}} | collective-permute-start | bytes 1572872 | tf_op jit(solution)/shard_map/ppermute | solution.py:79
  258.3 43.9 %collective-permute-start.10 = (bf16[64,4096]{1,0:T(8,128)(2,1)S(1)}, bf16[64,4096]{1,0:T(8,128)(2,1)S(1)}, u32[]{:S(2)}, u32[]{:S(2)}) collective-permute-start(bf16[64,4096]{1,0:T(8,128)(2,1)S(1)} %get-tuple-element.8), channel_id=1, source_target_pairs={{0,1},{1,2},{2,3},{4,5},{5,6},{6,7},{8,9},{9,10},{10,11},{12,13},{... | collective-permute-start | bytes 1572872 | tf_op jit(solution)/shard_map/ppermute | solution.py:78
  263.9 1.9 collective-permute-start.5
  265.1 3.3 collective-permute-start.12
  267.1 33.8 %collective-permute-start.6 = (bf16[64,4096]{1,0:T(8,128)(2,1)S(1)}, bf16[64,4096]{1,0:T(8,128)(2,1)S(1)}, u32[]{:S(2)}, u32[]{:S(2)}) collective-permute-start(bf16[64,4096]{1,0:T(8,128)(2,1)S(1)} %add_convert_fusion.4), channel_id=1, source_target_pairs={{1,0},{2,1},{3,2},{5,4},{6,5},{7,6},{9,8},{10,9},{11,10},{13,12},{... | collective-permute-start | bytes 1572872 | tf_op jit(solution)/shard_map/ppermute | solution.py:79
  268.6 46.0 %collective-permute-start.13 = (bf16[64,4096]{1,0:T(8,128)(2,1)S(1)}, bf16[64,4096]{1,0:T(8,128)(2,1)S(1)}, u32[]{:S(2)}, u32[]{:S(2)}) collective-permute-start(bf16[64,4096]{1,0:T(8,128)(2,1)S(1)} %add_convert_fusion), channel_id=1, source_target_pairs={{1,0},{2,1},{3,2},{5,4},{6,5},{7,6},{9,8},{10,9},{11,10},{13,12},{... | collective-permute-start | bytes 1572872 | tf_op jit(solution)/shard_map/ppermute | solution.py:79
  302.1 12.7 %copy-start.5 = (bf16[128,4096]{1,0:T(8,128)(2,1)S(1)}, bf16[128,4096]{1,0:T(8,128)(2,1)}, u32[]{:S(2)}) copy-start(bf16[128,4096]{1,0:T(8,128)(2,1)} %param.16) | copy-start | bytes 3145732
  302.1 12.7 %copy-start.6 = (s32[16,8,4,1024]{3,1,2,0:T(8,128)S(1)}, s32[16,8,4,1024]{3,1,2,0:T(8,128)}, u32[]{:S(2)}) copy-start(s32[16,8,4,1024]{3,1,2,0:T(8,128)} %copy.27) | copy-start | bytes 6291460
  314.8 1.7 copy-start.11
  315.6 1.0 copy-start.7
  316.9 6.1 %copy-start.2 = (bf16[64,512,256]{2,1,0:T(8,128)(2,1)S(1)}, bf16[64,512,256]{2,1,0:T(8,128)(2,1)}, u32[]{:S(2)}) copy-start(bf16[64,512,256]{2,1,0:T(8,128)(2,1)} %all-gather.11.cloned.1.call-done) | copy-start | bytes 50331652
  323.0 69.0 %copy-start.4 = (s32[16,1024]{1,0:T(8,128)S(1)}, s32[16,1024]{1,0:T(8,128)}, u32[]{:S(2)}) copy-start(s32[16,1024]{1,0:T(8,128)} %words_ref.1) | copy-start | bytes 196612
  330.6 61.4 %all-to-all-start = ((bf16[8,16,1152]{2,1,0:T(8,128)(2,1)}), bf16[8,16,1152]{2,1,0:T(8,128)(2,1)S(1)}, u32[]{:S(2)}, u32[]{:S(2)}) async-start(bf16[8,16,1152]{2,1,0:T(8,128)(2,1)} %bitcast.20), calls=%async_computation | async-start | bytes 589824 | tf_op jit(solution)/shard_map/all_to_all | solution.py:288
  392.0 3.4 copy-start.3
  395.3 4.0 copy-start.1
Sparse Core Ops, SparseCore 0:
  11.7 67.2 all-gather.6
  80.5 56.3 all-gather.8
  139.9 164.7 all-gather.10
  307.5 84.3 all-gather.12

commit v2 on v1

v2 whole, which is shorter than its diff:
```python
import functools

import jax
import jax.numpy as jnp
from jax import lax
from jax.experimental import pallas as pl
from jax.experimental.pallas import tpu as pltpu
from jax.sharding import PartitionSpec as P

HD = 256
F32 = jnp.float32
BF16 = jnp.bfloat16
CHUNKS = 2
STATS = 5


def norm_rows(x, gain):
    values = x.astype(F32)
    power = jnp.mean(values * values, axis=-1, keepdims=True)
    return values * lax.rsqrt(power + 1e-06) * gain


def keep_factor(words):
    shifts = jnp.arange(4, dtype=jnp.int32) * 3
    bits = jnp.right_shift(words[:, None, :], shifts[None, :, None]) & 7
    kept = jnp.where(bits == 7, 0.0, 8.0 / 7.0).astype(F32)
    return kept.reshape(words.shape[0], 4 * words.shape[1])


def swap(value, axis, distance):
    return lax.ppermute(value, axis, [(i, i ^ distance) for i in range(lax.axis_size(axis))])


def near_bits(axis):
    bits, bit = [], 1
    while bit < lax.axis_size(axis):
        bits.append(bit)
        bit *= 2
    return bits


def slot_order(bits):
    order = [0]
    for bit in bits:
        order = order + [m ^ bit for m in order]
    return order


def gather_swaps(value, axis, bits):
    for bit in bits:
        value = jnp.concatenate([value, swap(value, axis, bit)], 0)
    return value


def sum_swaps(value, axis, bits, sent):
    for bit in bits[::-1]:
        half = value.shape[0] // 2
        value = value[:half] + swap(value[half:].astype(sent), axis, bit).astype(F32)
    return value


def half_columns(value, index):
    return lax.dynamic_slice_in_dim(value, index * (value.shape[1] // 2), value.shape[1] // 2, 1)


def gather_half(rows, section, bits):
    own = half_columns(rows, section)
    other = swap(half_columns(rows, 1 - section), "section", 1)
    pair = jnp.where(section == 0, jnp.concatenate([own, other], 0), jnp.concatenate([other, own], 0))
    return gather_swaps(pair, "tensor", bits)


def both_halves(partial):
    return partial + swap(partial, "section", 1)


def gelu(x):
    return 0.5 * x * (1.0 + jnp.tanh(0.7978845608028654 * (x + 0.044715 * x * x * x)))


def ffn_kernel(hidden_steps, xa_ref, xb_ref, gate_ref, up_ref, down_ref, ya_ref, yb_ref, hidden):
    step = pl.program_id(0)
    rows = xa_ref.shape[0]
    width = gate_ref.shape[1]

    @pl.when(step < hidden_steps)
    def _():
        for i, x_ref in enumerate((xa_ref, xb_ref)):
            gate = jnp.dot(x_ref[...], gate_ref[...], preferred_element_type=F32)
            up = jnp.dot(x_ref[...], up_ref[...], preferred_element_type=F32)
            hidden[step, i * rows : (i + 1) * rows, :] = (gelu(gate) * up).astype(BF16)

    @pl.when(step >= hidden_steps)
    def _():
        total = jnp.zeros((2 * rows, ya_ref.shape[1]), F32)
        for k in range(hidden.shape[0]):
            total += jnp.dot(
                hidden[k], down_ref[k * width : (k + 1) * width, :], preferred_element_type=F32
            )
        ya_ref[...] = total[:rows].astype(BF16)
        yb_ref[...] = total[rows:].astype(BF16)


def ffn(xa, xb, w_gate, w_up, w_down):
    rows, features = xa.shape
    units = w_gate.shape[1]
    width = min(256, units)
    tile = 512
    first, last = units // width, features // tile
    return pl.pallas_call(
        functools.partial(ffn_kernel, first),
        grid=(first + last,),
        in_specs=[
            pl.BlockSpec((rows, features), lambda i: (0, 0)),
            pl.BlockSpec((rows, features), lambda i: (0, 0)),
            pl.BlockSpec((features, width), lambda i: (0, jnp.minimum(i, first - 1))),
            pl.BlockSpec((features, width), lambda i: (0, jnp.minimum(i, first - 1))),
            pl.BlockSpec((units, tile), lambda i: (0, jnp.maximum(i - first, 0))),
        ],
        out_specs=[pl.BlockSpec((rows, tile), lambda i: (0, jnp.maximum(i - first, 0)))] * 2,
        out_shape=[jax.ShapeDtypeStruct((rows, features), BF16)] * 2,
        scratch_shapes=[pltpu.VMEM((first, 2 * rows, width), BF16)],
        compiler_params=pltpu.CompilerParams(vmem_limit_bytes=48 * 2**20),
        cost_estimate=pl.CostEstimate(
            flops=12 * rows * features * units, bytes_accessed=6 * features * units, transcendentals=0
        ),
        name="ffn",
    )(xa, xb, w_gate, w_up, w_down)


def attend_kernel(
    heads, table, ids, mem_ref, a0_ref, a1_ref, b0_ref, b1_ref, cq_ref, out_ref
):
    slot = pl.program_id(0)
    head = ids[slot]
    groups, depth = a0_ref.shape[0], a0_ref.shape[3]

    def attend(own_ref, other_ref, row):
        keys = jnp.zeros((mem_ref.shape[0], HD), F32)
        values = jnp.zeros((mem_ref.shape[0], HD), F32)
        for place, ref in enumerate((own_ref, other_ref)):
            for i in range(groups):
                at = pl.multiple_of(table[row + place, i] * depth, depth)
                x = mem_ref[:, pl.ds(at, depth)]
                keys += jnp.dot(x, ref[i, 0, 0], preferred_element_type=F32)
                values += jnp.dot(x, ref[i, 0, 1], preferred_element_type=F32)
        k, v = keys.astype(BF16), values.astype(BF16)
        scores = lax.dot_general(cq_ref[0], k, (((1,), (1,)), ((), ())), preferred_element_type=F32)
        scores = scores * (1.0 / 16.0)
        top = jnp.max(scores, axis=-1, keepdims=True)
        expo = jnp.exp(scores - top)
        total = jnp.sum(expo, axis=-1, keepdims=True)
        context = jnp.dot(expo.astype(BF16), v, preferred_element_type=F32)
        out_ref[:, pl.ds(pl.multiple_of(head * HD, HD), HD)] = context.astype(BF16)
        lanes = lax.broadcasted_iota(jnp.int32, (scores.shape[0], 128), 1) - head * STATS
        base = heads * HD
        high = top.astype(BF16).astype(F32)
        rest = top - high
        middle = rest.astype(BF16).astype(F32)
        low = rest - middle
        sum_high = total.astype(BF16).astype(F32)
        sum_low = total - sum_high
        stats = jnp.where(slot == 0, jnp.zeros(lanes.shape, F32), out_ref[:, base:].astype(F32))
        for index, piece in enumerate((high, middle, low, sum_high, sum_low)):
            stats = jnp.where(lanes == index, piece, stats)
        out_ref[:, base:] = stats.astype(BF16)

    @pl.when(slot < heads // 2)
    def _():
        attend(a0_ref, a1_ref, 0)

    @pl.when(slot >= heads // 2)
    def _():
        attend(b0_ref, b1_ref, 2)


def attend_own_keys(memory, weights, queries, table, ids):
    rows, features = memory.shape
    heads, count, width = queries.shape
    groups, half, _, depth, _ = weights[0].shape
    block = (groups, 1, 2, depth, width)
    first = pl.BlockSpec(block, lambda h, t, n: (0, jnp.minimum(h, half - 1), 0, 0, 0))
    second = pl.BlockSpec(block, lambda h, t, n: (0, jnp.maximum(h - half, 0), 0, 0, 0))
    return pl.pallas_call(
        functools.partial(attend_kernel, heads),
        grid_spec=pltpu.PrefetchScalarGridSpec(
            num_scalar_prefetch=2,
            grid=(heads,),
            in_specs=[
                pl.BlockSpec((rows, features), lambda h, t, n: (0, 0)),
                first,
                first,
                second,
                second,
                pl.BlockSpec((1, count, width), lambda h, t, n: (h, 0, 0)),
            ],
            out_specs=pl.BlockSpec((count, heads * width + 128), lambda h, t, n: (0, 0)),
        ),
        out_shape=jax.ShapeDtypeStruct((count, heads * width + 128), BF16),
        compiler_params=pltpu.CompilerParams(vmem_limit_bytes=40 * 2**20),
        cost_estimate=pl.CostEstimate(
            flops=4 * rows * features * heads * width,
            bytes_accessed=4 * features * heads * width,
            transcendentals=0,
        ),
        name="attend_own_keys",
    )(table, ids, memory, *weights, queries)


def finish_kernel(
    heads, words_width, table, ids, parts_ref, a0_ref, a1_ref, b0_ref, b1_ref, mid_ref, words_ref, out_ref, context
):
    place, step = pl.program_id(0), pl.program_id(1)
    tile = out_ref.shape[1]
    index = table[place, step]

    @pl.when((place == 0) & (step == 0))
    def _():
        stat = parts_ref[:, :, heads * HD :].astype(F32)
        lanes = lax.broadcasted_iota(jnp.int32, stat.shape, 2)
        for slot in range(heads):
            head = ids[slot]
            pick = [
                jnp.sum(jnp.where(lanes == head * STATS + j, stat, 0.0), axis=-1, keepdims=True)
                for j in range(STATS)
            ]
            top = pick[0] + pick[1] + pick[2]
            weight = jnp.exp(top - jnp.max(top, axis=0, keepdims=True))
            whole = jnp.sum(weight * (pick[3] + pick[4]), axis=0)
            part = parts_ref[:, :, pl.ds(pl.multiple_of(head * HD, HD), HD)].astype(F32)
            context[:, slot * HD : (slot + 1) * HD] = (jnp.sum(part * weight, axis=0) / whole).astype(BF16)

    def columns(a_ref, b_ref):
        half = heads * HD // 2
        for u in range(tile // HD):
            cut = slice(u * HD, (u + 1) * HD)
            wa = a_ref[0, :, 0, cut, :].reshape(half, HD)
            wb = b_ref[0, :, 0, cut, :].reshape(half, HD)
            total = jnp.dot(context[:, :half], wa, preferred_element_type=F32)
            total += jnp.dot(context[:, half:], wb, preferred_element_type=F32)
            words = words_ref[:, cut]
            shift = 3 * (index // (words_width // tile))
            bits = lax.shift_right_logical(words, jnp.broadcast_to(shift, words.shape)) & 7
            kept = jnp.where(bits == 7, 0.0, 8.0 / 7.0).astype(F32)
            out_ref[:, cut] = (mid_ref[:, cut].astype(F32) + kept * total).astype(BF16)

    @pl.when(place == 0)
    def _():
        columns(a0_ref, b0_ref)

    @pl.when(place == 1)
    def _():
        columns(a1_ref, b1_ref)


def finish(parts, weights, mid, words, table, ids):
    groups, half, _, depth, width = weights[0].shape
    heads = 2 * half
    rows, features = mid.shape
    per_word = words.shape[1] // depth
    block = (1, half, 1, depth, width)
    bits = []
    while 1 << len(bits) < groups:
        bits.append(len(bits))
    top = len(bits) - 1

    def reverse(i):
        out = 0
        for b in bits:
            out = out + ((i >> b) & 1) * (1 << (top - b))
        return out

    def a_own(p, i, t, n):
        return (jnp.where(p == 0, i, groups - 1), 0, 2, 0, 0)

    def a_other(p, i, t, n):
        return (jnp.where(p == 0, 0, i), 0, 2, 0, 0)

    def b_own(p, i, t, n):
        return (reverse(jnp.where(p == 0, i, groups - 1)), 0, 2, 0, 0)

    def b_other(p, i, t, n):
        return (reverse(jnp.where(p == 0, 0, i)), 0, 2, 0, 0)

    return pl.pallas_call(
        functools.partial(finish_kernel, heads, words.shape[1]),
        grid_spec=pltpu.PrefetchScalarGridSpec(
            num_scalar_prefetch=2,
            grid=(2, groups),
            in_specs=[
                pl.BlockSpec(parts.shape, lambda p, i, t, n: (0, 0, 0)),
                pl.BlockSpec(block, a_own),
                pl.BlockSpec(block, a_other),
                pl.BlockSpec(block, b_own),
                pl.BlockSpec(block, b_other),
                pl.BlockSpec((rows, depth), lambda p, i, t, n: (0, t[p, i])),
                pl.BlockSpec((rows, depth), lambda p, i, t, n: (0, lax.rem(t[p, i], per_word))),
            ],
            out_specs=pl.BlockSpec((rows, depth), lambda p, i, t, n: (0, t[p, i])),
            scratch_shapes=[pltpu.VMEM((rows, heads * width), BF16)],
        ),
        out_shape=jax.ShapeDtypeStruct((rows, features), BF16),
        compiler_params=pltpu.CompilerParams(vmem_limit_bytes=32 * 2**20),
        cost_estimate=pl.CostEstimate(
            flops=2 * rows * features * heads * width,
            bytes_accessed=2 * features * heads * width,
            transcendentals=0,
        ),
        name="finish",
    )(table, ids, parts, *weights, mid, words)


def per_device(
    source,
    enc_gain,
    w_gate,
    w_up,
    w_down,
    enc_keep,
    final_gain,
    target,
    self_gain,
    self_qkv,
    self_out,
    cross_gain,
    cross_q,
    cross_kv,
    cross_out,
    dec_keep,
):
    count, groups = lax.axis_size("tensor"), lax.axis_size("dp")
    section, tensor, group = lax.axis_index("section"), lax.axis_index("tensor"), lax.axis_index("dp")
    devices = 2 * count
    bits = near_bits("tensor")[::-1]
    order = slot_order(bits)
    rows = target.shape[0]
    after = lax.optimization_barrier

    normed = norm_rows(source, enc_gain).astype(BF16)
    block = normed.shape[0] // CHUNKS
    near = [gather_swaps(normed[c * block : (c + 1) * block], "tensor", bits) for c in range(CHUNKS)]
    far = [swap(x, "section", 1) for x in near]

    selfin = norm_rows(target, self_gain).astype(BF16)
    x = gather_half(selfin, section, bits)
    qkv_w = jnp.transpose(self_qkv, (1, 0, 2))
    q, k, v = [jnp.dot(x, qkv_w[i], preferred_element_type=F32) for i in range(3)]
    q, k, v = [y.astype(BF16) for y in both_halves(jnp.stack([q, k, v]))]
    slot_chip = jnp.stack([tensor ^ m for m in order])
    positions = (
        (jnp.arange(2, dtype=jnp.int32)[None, :] * count + slot_chip[:, None])[:, :, None] * rows
        + jnp.arange(rows, dtype=jnp.int32)
    ).reshape(-1)
    scores = lax.dot_general(q, k, (((1,), (1,)), ((), ())), preferred_element_type=F32) * (1.0 / 16.0)
    scores = jnp.where(positions[None, :] <= positions[:, None], scores, F32(-1e30))
    expo = jnp.exp(scores - jnp.max(scores, axis=-1, keepdims=True))
    probs = (expo / jnp.sum(expo, axis=-1, keepdims=True)).astype(BF16)
    context = jnp.dot(probs, v, preferred_element_type=F32).astype(BF16)
    product = jnp.dot(context, self_out, preferred_element_type=F32).astype(BF16).astype(F32)
    total = sum_swaps(product, "tensor", bits, BF16)
    own = lax.dynamic_slice_in_dim(total, section * rows, rows, 0)
    other = swap(lax.dynamic_slice_in_dim(total, (1 - section) * rows, rows, 0), "section", 1)
    selfsum = jnp.where(section == 0, jnp.concatenate([own, other], 1), jnp.concatenate([other, own], 1))
    mid = (target.astype(F32) + selfsum).astype(BF16)

    shares = [ffn(near[0], far[0], w_gate, w_up, w_down)]

    depth = cross_kv.shape[0] // groups
    kv_share = lax.dynamic_slice_in_dim(jnp.transpose(cross_kv, (1, 0, 2)), group * depth, depth, 1)
    out_share = lax.dynamic_slice_in_dim(cross_out, group * depth, depth, 1)
    out_share = jnp.transpose(out_share.reshape(HD, depth // HD, HD), (1, 0, 2)).reshape(1, depth, HD)
    share = jnp.concatenate([kv_share, out_share], 0)[None]
    share, near[0] = after((share, near[0]))
    share = gather_swaps(share, "tensor", bits)
    dp_bits = near_bits("dp")
    weights, table = [], []
    for piece, way in ((share[: count // 2], dp_bits), (share[count // 2 :], dp_bits[::-1])):
        own = gather_swaps(piece[None], "dp", way)
        weights += [own, swap(own, "section", 1)]
        at = jnp.stack([group ^ m for m in slot_order(way)])
        table += [section * groups + at, (1 - section) * groups + at]
    table = jnp.stack(table).astype(jnp.int32)
    ids = slot_chip.astype(jnp.int32)

    mid, first = after((mid, shares[0][0]))
    shares[0] = (first, shares[0][1])
    crossin = norm_rows(mid, cross_gain).astype(BF16)
    x = gather_half(crossin, section, bits)
    cq = both_halves(jnp.dot(x, cross_q, preferred_element_type=F32)).astype(BF16)
    cq = cq.reshape(count, 2, rows, HD)
    place = [order.index(m) for m in range(count)]
    back = jnp.asarray(place, jnp.int32)
    cq = jnp.stack(
        [lax.dynamic_index_in_dim(cq, back[tensor ^ c], 0, keepdims=False) for c in range(count)]
    )
    cq = jnp.transpose(cq, (1, 0, 2, 3)).reshape(devices * rows, HD)
    queries = gather_swaps(cq[None], "tensor", bits)

    for c in range(1, CHUNKS):
        shares.append(ffn(near[c], far[c], w_gate, w_up, w_down))
    total = [
        sum_swaps(ya.astype(F32) + swap(yb, "section", 1).astype(F32), "tensor", bits, BF16)
        for ya, yb in shares
    ]
    enc_out = (source.astype(F32) + keep_factor(enc_keep) * jnp.concatenate(total, 0)).astype(BF16)
    memory = norm_rows(enc_out, final_gain).astype(BF16)

    parts = attend_own_keys(memory, weights, queries, table, ids)
    parts = parts.reshape(devices, rows, parts.shape[1])
    parts = lax.all_to_all(parts, ("section", "tensor"), split_axis=0, concat_axis=0, tiled=True)
    dec_out = finish(parts, weights, mid, dec_keep, table, ids)
    return (enc_out, dec_out)


def solution(mesh):
    return jax.shard_map(
        per_device,
        mesh=mesh,
        in_specs=(
            P(("dp", "section", "tensor"), None),
            P(),
            P(None, ("section", "tensor")),
            P(None, ("section", "tensor")),
            P(("section", "tensor"), None),
            P(("dp", "section", "tensor"), None),
            P(),
            P(("dp", "section", "tensor"), None),
            P(),
            P("section", None, "tensor"),
            P("tensor", "section"),
            P(),
            P("section", "tensor"),
            P("section", None, "tensor"),
            P("tensor", "section"),
            P(("dp", "section", "tensor"), None),
        ),
        out_specs=(P(("dp", "section", "tensor"), None), P(("dp", "section", "tensor"), None)),
        check_vma=False,
    )
```

time: 407 us -> 439 us (1.079)
  starting transfers between devices: 93.5 us -> 35.3 us
  waiting for transfers between devices: 203 us -> 255 us
  Pallas kernels: 11.6 us -> 63.3 us
  matrix products: 51 us -> 8.1 us
  other arithmetic: 13.9 us -> 33.9 us
  blocking collectives: 0 us -> 12.8 us
  between operations: 14.6 us -> 9.11 us
    ppermute x31 -> x33, waiting for transfers between devices: 167 us -> 255 us  [swap(): lax.ppermute(value, axis, [(i, i ^ distance) for i in range(lax.axis_size...]
    pallas_call x2 -> x4, Pallas kernels: 11.6 us -> 63.3 us  [the longest x2 45.8 us: ffn(): pl.pallas_call(functools.partial(ffn_kernel, first), grid=(first + last,)...]
    dot_general x8 -> x0, matrix products: 45.3 us -> none  [the longest x2 17.8 us: ffn_part(): gate = jnp.dot(x, w_gate, preferred_element_type=F32)]
    all_gather x4 -> x0, waiting for transfers between devices: 35.3 us -> none  [the longest x1 35.2 us: per_device(): lax.all_gather(out_share, ('dp', 'section', 'tensor'), axis=0, tiled=False)]
    ppermute x31 -> x33, starting transfers between devices: 67.2 us -> 35.3 us  [swap(): lax.ppermute(value, axis, [(i, i ^ distance) for i in range(lax.axis_size...]
    all_to_all x1 -> x0, starting transfers between devices: 26.2 us -> none  [per_device(): lax.all_to_all(parts, ('section', 'tensor'), split_axis=0, concat_axis=0,...]
    concatenate x1 -> x12, other arithmetic: 0.05 us -> 18.2 us  [gather_swaps(): value = jnp.concatenate([value, swap(value, axis, bit)], 0)]
    all_to_all x0 -> x1, blocking collectives: none -> 12.8 us  [per_device(): lax.all_to_all(parts, ('section', 'tensor'), split_axis=0, concat_axis=0,...]
  transfers between devices with their start and end apart: 36 -> 33, of which waited for: 20 -> 13; matrix products, arithmetic and copies ran while one was open for 17% -> 11% of each run, Pallas kernels for 2% -> 10%
where the time goes in v2:
time: 439 us; the launch traced here: 437 us
  waiting for transfers between devices  255 us (58%)
  Pallas kernels  63.3 us (14%)
  starting transfers between devices  35.3 us (8%)
  other arithmetic  33.9 us (8%)
  local copies, waits for them, and re-layouts  20.3 us (5%)
  blocking collectives  12.8 us (3%)
  between operations  9.11 us (2%)
  matrix products  8.1 us (2%)
    ppermute x33, waiting for transfers between devices, swap(): lax.ppermute(value, axis, [(i, i ^ distance) for i in range(lax.axis_size...  255 us
    pallas_call x2, Pallas kernels, ffn(): pl.pallas_call(functools.partial(ffn_kernel, first), grid=(first + last,)...  45.8 us
    ppermute x33, starting transfers between devices, swap(): lax.ppermute(value, axis, [(i, i ^ distance) for i in range(lax.axis_size...  35.3 us
    concatenate x12, other arithmetic, gather_swaps(): value = jnp.concatenate([value, swap(value, axis, bit)], 0)  18.2 us
    unnamed x67, local copies, waits for them, and re-layouts  13.9 us
    all_to_all x1, blocking collectives, per_device(): lax.all_to_all(parts, ('section', 'tensor'), split_axis=0, concat_axis=0,...  12.8 us
    pallas_call x1, Pallas kernels, attend_own_keys(): pl.pallas_call(functools.partial(attend_kernel, heads), grid_spec=pltpu.P...  10.1 us
  transfers between devices with their start and end apart: 33, of which 13 were waited for; matrix products, arithmetic and copies ran while one was open for 11% of the time, Pallas kernels for 10%

profile of v2, /device:TPU:0, one launch (start us, length us, event | category | flops | bytes accessed | tf_op | source)
XLA Modules:
  0.0 437.4 jit_solution(10242147320383238307)
XLA Ops:
  0.7 1.2 fusion.17
  1.9 1.0 fusion.19
  3.4 1.5 fusion.3
  5.0 1.0 fusion.5
  6.0 1.1 fusion.28
  7.1 3.6 collective-permute-start.7
  11.0 1.0 constant_dynamic-slice_fusion.2
  12.8 1.1 copy.26
  14.3 1.0 maximum_select_fusion.1
  15.3 3.0 collective-permute-start.1
  18.3 44.5 %collective-permute-done.1 = bf16[32,2048]{1,0:T(8,128)(2,1)S(1)} collective-permute-done((bf16[32,2048]{1,0:T(8,128)(2,1)S(1)}, bf16[32,2048]{1,0:T(8,128)(2,1)S(1)}, u32[]{:S(2)}, u32[]{:S(2)}) %collective-permute-start.1) | collective-permute-done | bytes 131104 | tf_op jit(solution)/shard_map/ppermute | solution.py:31
  64.9 6.1 %collective-permute-done.2 = bf16[64,2048]{1,0:T(8,128)(2,1)S(1)} collective-permute-done((bf16[64,2048]{1,0:T(8,128)(2,1)S(1)}, bf16[64,2048]{1,0:T(8,128)(2,1)S(1)}, u32[]{:S(2)}, u32[]{:S(2)}) %collective-permute-start.2) | collective-permute-done | bytes 262176 | tf_op jit(solution)/shard_map/ppermute | solution.py:31
  71.0 1.5 convolution_bitcast_fusion.1
  72.6 1.5 convolution_bitcast_fusion
  74.1 1.5 convolution_bitcast_fusion.2
  75.8 2.3 pad_maximum_fusion.7
  78.0 0.9 collective-permute-start.14
  79.2 1.7 convolution_convert_fusion
  80.9 1.2 collective-permute-start.4
  82.1 1.3 pad_maximum_fusion.6
  83.4 0.9 collective-permute-start.8
  84.4 25.4 %collective-permute-done.4 = bf16[64,2048]{1,0:T(8,128)(2,1)S(1)} collective-permute-done((bf16[64,2048]{1,0:T(8,128)(2,1)S(1)}, bf16[64,2048]{1,0:T(8,128)(2,1)S(1)}, u32[]{:S(2)}, u32[]{:S(2)}) %collective-permute-start.4) | collective-permute-done | bytes 262176 | tf_op jit(solution)/shard_map/ppermute | solution.py:31
  109.9 2.6 collective-permute-start.5
  112.5 1.7 pad_maximum_fusion.5.xa_ref
  114.3 18.8 %collective-permute-done.5 = bf16[32,2048]{1,0:T(8,128)(2,1)S(1)} collective-permute-done((bf16[32,2048]{1,0:T(8,128)(2,1)S(1)}, bf16[32,2048]{1,0:T(8,128)(2,1)S(1)}, u32[]{:S(2)}, u32[]{:S(2)}) %collective-permute-start.5) | collective-permute-done | bytes 131104 | tf_op jit(solution)/shard_map/ppermute | solution.py:31
  133.2 1.4 collective-permute-done.8
  134.7 1.6 pad_maximum_fusion.4.xa_ref
  136.4 2.4 collective-permute-start.19
  139.0 35.2 %collective-permute-done.19 = bf16[1,3,512,256]{3,2,1,0:T(8,128)(2,1)S(1)} collective-permute-done((bf16[1,3,512,256]{3,2,1,0:T(8,128)(2,1)S(1)}, bf16[1,3,512,256]{3,2,1,0:T(8,128)(2,1)S(1)}, u32[]{:S(2)}, u32[]{:S(2)}) %collective-permute-start.19) | collective-permute-done | bytes 786464 | tf_op jit(solution)/shard_map/ppermute | solution.py:31
  174.4 1.5 collective-permute-start.20
  175.9 1.4 copy-done.28
  177.2 23.4 %ffn.3 = (bf16[256,4096]{1,0:T(8,128)(2,1)S(1)}, bf16[256,4096]{1,0:T(8,128)(2,1)}) custom-call(bf16[256,4096]{1,0:T(8,128)(2,1)} %copy-done.21, bf16[256,4096]{1,0:T(8,128)(2,1)} %copy-done.28, bf16[4096,1024]{1,0:T(8,128)(2,1)} %gate_ref.3, bf16[4096,1024]{1,0:T(8,128)(2,1)} %up_ref.3, bf16[1024,4096]{1,0:T(8,128)(2,1)} %down_ref.3), custom_call_target="tpu_custom_call" | custom-call | flops 12884901888 | bytes 25165824 | tf_op jit(solution)/shard_map/ffn/pallas_call | solution.py:110
  200.8 1.4 copy-done.29
  202.2 22.4 %ffn.2 = (bf16[256,4096]{1,0:T(8,128)(2,1)S(1)}, bf16[256,4096]{1,0:T(8,128)(2,1)S(1)}) custom-call(bf16[256,4096]{1,0:T(8,128)(2,1)} %copy-done.22, bf16[256,4096]{1,0:T(8,128)(2,1)} %copy-done.29, bf16[4096,1024]{1,0:T(8,128)(2,1)} %gate_ref.3, bf16[4096,1024]{1,0:T(8,128)(2,1)} %up_ref.3, bf16[1024,4096]{1,0:T(8,128)(2,1)} %down_ref.3), custom_call_target="tpu_custom_call" | custom-call | flops 12884901888 | bytes 25165824 | tf_op jit(solution)/shard_map/ffn/pallas_call | solution.py:110
  224.8 1.6 collective-permute-start.24
  226.7 2.2 pad_maximum_fusion.2
  229.5 3.4 collective-permute-start.28
  233.0 29.1 %collective-permute-done.24 = bf16[1,2,3,512,256]{4,3,2,1,0:T(8,128)(2,1)S(1)} collective-permute-done((bf16[1,2,3,512,256]{4,3,2,1,0:T(8,128)(2,1)S(1)}, bf16[1,2,3,512,256]{4,3,2,1,0:T(8,128)(2,1)S(1)}, u32[]{:S(2)}, u32[]{:S(2)}) %collective-permute-start.24) | collective-permute-done | bytes 1572896 | tf_op jit(solution)/shard_map/ppermute | solution.py:31
  262.1 2.2 pad_maximum_fusion.3
  265.6 1.9 collective-permute-start.29
  276.4 0.9 broadcast_bitcast_fusion
  277.3 1.6 fusion.8
  280.4 1.6 collective-permute-start.31
  283.3 1.7 copy.37
  284.9 2.0 collective-permute-done.31
  287.1 2.3 convert_add_fusion
  289.4 1.1 slice.113
  290.5 2.0 collective-permute-start.17
  292.5 36.6 %collective-permute-done.21 = bf16[2,2,3,512,256]{4,3,2,1,0:T(8,128)(2,1)} collective-permute-done((bf16[2,2,3,512,256]{4,3,2,1,0:T(8,128)(2,1)}, bf16[2,2,3,512,256]{4,3,2,1,0:T(8,128)(2,1)}, u32[]{:S(2)}, u32[]{:S(2)}) %collective-permute-start.21) | collective-permute-done | bytes 3145760 | tf_op jit(solution)/shard_map/ppermute | solution.py:31
  329.1 2.9 pad_maximum_fusion.a0_ref
  332.1 1.7 collective-permute-done.25
  333.8 3.1 pad_maximum_fusion.1.b0_ref
  337.8 1.9 copy-done.2
  339.8 1.9 collective-permute-start.11
  341.7 1.5 slice_add_fusion
  343.2 1.7 collective-permute-start.18
  345.0 30.0 %collective-permute-done.11 = bf16[128,4096]{1,0:T(8,128)(2,1)S(1)} collective-permute-done((bf16[128,4096]{1,0:T(8,128)(2,1)S(1)}, bf16[128,4096]{1,0:T(8,128)(2,1)S(1)}, u32[]{:S(2)}, u32[]{:S(2)}) %collective-permute-start.11) | collective-permute-done | bytes 1048608 | tf_op jit(solution)/shard_map/ppermute | solution.py:31
  375.3 1.2 collective-permute-start.12
  376.6 23.6 %collective-permute-done.12 = bf16[64,4096]{1,0:T(8,128)(2,1)S(1)} collective-permute-done((bf16[64,4096]{1,0:T(8,128)(2,1)S(1)}, bf16[64,4096]{1,0:T(8,128)(2,1)S(1)}, u32[]{:S(2)}, u32[]{:S(2)}) %collective-permute-start.12) | collective-permute-done | bytes 524320 | tf_op jit(solution)/shard_map/ppermute | solution.py:31
  401.5 10.1 %attend_own_keys.1 = bf16[128,1152]{1,0:T(8,128)(2,1)S(1)} custom-call(s32[4,4]{1,0:T(4,128)S(1)} %pad_add_fusion.table, s32[4]{0:T(128)S(1)} %pad_add_fusion.1.ids, bf16[128,4096]{1,0:T(8,128)(2,1)S(1)} %fusion.2.mem_ref, bf16[4,2,3,512,256]{4,3,2,1,0:T(8,128)(2,1)S(1)} %pad_maximum_fusion.a0_ref, ...), custom_call_target="tpu_custom_call" | custom-call | flops 2147483648 | bytes 16777216 | tf_op jit(solution)/shard_map/attend_own_keys/pallas_call | solution.py:184
  411.7 12.8 %all_to_all.5.parts_ref = bf16[8,16,1152]{2,1,0:T(8,128)(2,1)S(1)} all-to-all(bf16[8,16,1152]{2,1,0:T(8,128)(2,1)S(1)} %bitcast.75), channel_id=1, replica_groups=mesh['dp'=4,'section'=2,'tensor'=4] {'section','tensor'}, dimensions={0} | all-to-all | bytes 589824 | tf_op jit(solution)/shard_map/all_to_all | solution.py:410
  424.4 2.8 copy-done.3
  427.2 2.8 copy-done.5
  430.0 7.4 %finish.1 = bf16[16,4096]{1,0:T(8,128)(2,1)} custom-call(s32[4,4]{1,0:T(4,128)S(1)} %pad_add_fusion.table, s32[4]{0:T(128)S(1)} %pad_add_fusion.1.ids, bf16[8,16,1152]{2,1,0:T(8,128)(2,1)S(1)} %all_to_all.5.parts_ref, bf16[4,2,3,512,256]{4,3,2,1,0:T(8,128)(2,1)S(1)} %pad_maximum_fusion.a0_ref, bf16[4,2,3,512,256]{4,3,2,1,0:T(8,128)(2,1)S(1)} %copy-done.5, ...), custom_call_target="tpu_custom_call" | custom-call | flops 134217728 | bytes 8388608 | tf_op jit(solution)/shard_map/finish/pallas_call | solution.py:285
  (147 shorter events, 14.6 us)
Async XLA Ops:
  0.6 13.2 %copy-start = (bf16[2048,2,256]{2,1,0:T(2,128)(2,1)S(1)}, bf16[2048,2,256]{2,1,0:T(2,128)(2,1)}, u32[]{:S(2)}) copy-start(bf16[2048,2,256]{2,1,0:T(2,128)(2,1)} %param.30) | copy-start | bytes 6291460
  0.6 4.3 copy-start.13
  2.9 11.4 %collective-permute-start = (bf16[16,2048]{1,0:T(8,128)(2,1)S(1)}, bf16[16,2048]{1,0:T(8,128)(2,1)}, u32[]{:S(2)}, u32[]{:S(2)}) collective-permute-start(bf16[16,2048]{1,0:T(8,128)(2,1)S(1)} %get-tuple-element.29), channel_id=1, source_target_pairs={{0,4},{4,0},{1,5},{5,1},{2,6},{6,2},{3,7},{7,3},{8,12},{12,8},{9,1... | collective-permute-start | bytes 196616 | tf_op jit(solution)/shard_map/ppermute | solution.py:31
  7.1 75.1 %collective-permute-start.7 = (bf16[64,4096]{1,0:T(8,128)(2,1)}, bf16[64,4096]{1,0:T(8,128)(2,1)}, u32[]{:S(2)}, u32[]{:S(2)}) collective-permute-start(bf16[64,4096]{1,0:T(8,128)(2,1)} %get-tuple-element.22), channel_id=1, source_target_pairs={{0,2},{1,3},{2,0},{3,1},{4,6},{5,7},{6,4},{7,5},{8,10},{9,11},{10,... | collective-permute-start | bytes 1572872 | tf_op jit(solution)/shard_map/ppermute | solution.py:31
  10.7 65.1 %collective-permute-start.13 = (bf16[64,4096]{1,0:T(8,128)(2,1)}, bf16[64,4096]{1,0:T(8,128)(2,1)}, u32[]{:S(2)}, u32[]{:S(2)}) collective-permute-start(bf16[64,4096]{1,0:T(8,128)(2,1)} %get-tuple-element.23), channel_id=1, source_target_pairs={{0,2},{1,3},{2,0},{3,1},{4,6},{5,7},{6,4},{7,5},{8,10},{9,11},{10,... | collective-permute-start | bytes 1572872 | tf_op jit(solution)/shard_map/ppermute | solution.py:31
  15.3 47.5 %collective-permute-start.1 = (bf16[32,2048]{1,0:T(8,128)(2,1)S(1)}, bf16[32,2048]{1,0:T(8,128)(2,1)S(1)}, u32[]{:S(2)}, u32[]{:S(2)}) collective-permute-start(bf16[32,2048]{1,0:T(8,128)(2,1)S(1)} %maximum_select_fusion.1), channel_id=1, source_target_pairs={{0,2},{1,3},{2,0},{3,1},{4,6},{5,7},{6,4},{7,5},{8,10},{9,11},{10,... | collective-permute-start | bytes 393224 | tf_op jit(solution)/shard_map/ppermute | solution.py:31
  62.8 8.2 %collective-permute-start.2 = (bf16[64,2048]{1,0:T(8,128)(2,1)S(1)}, bf16[64,2048]{1,0:T(8,128)(2,1)S(1)}, u32[]{:S(2)}, u32[]{:S(2)}) collective-permute-start(bf16[64,2048]{1,0:T(8,128)(2,1)S(1)} %pad_maximum_fusion.10), channel_id=1, source_target_pairs={{0,1},{1,0},{2,3},{3,2},{4,5},{5,4},{6,7},{7,6},{8,9},{9,8},{10,11... | collective-permute-start | bytes 786440 | tf_op jit(solution)/shard_map/ppermute | solution.py:31
  75.7 3.2 collective-permute-start.3
  78.0 34.5 %collective-permute-start.14 = (bf16[128,4096]{1,0:T(8,128)(2,1)}, bf16[128,4096]{1,0:T(8,128)(2,1)}, u32[]{:S(2)}, u32[]{:S(2)}) collective-permute-start(bf16[128,4096]{1,0:T(8,128)(2,1)} %pad_maximum_fusion.7), channel_id=1, source_target_pairs={{0,1},{1,0},{2,3},{3,2},{4,5},{5,4},{6,7},{7,6},{8,9},{9,8},{10,11... | collective-permute-start | bytes 3145736 | tf_op jit(solution)/shard_map/ppermute | solution.py:31
  80.9 28.9 %collective-permute-start.4 = (bf16[64,2048]{1,0:T(8,128)(2,1)S(1)}, bf16[64,2048]{1,0:T(8,128)(2,1)S(1)}, u32[]{:S(2)}, u32[]{:S(2)}) collective-permute-start(bf16[64,2048]{1,0:T(8,128)(2,1)S(1)} %slice.82), channel_id=1, source_target_pairs={{0,1},{1,0},{2,3},{3,2},{4,5},{5,4},{6,7},{7,6},{8,9},{9,8},{10,11... | collective-permute-start | bytes 786440 | tf_op jit(solution)/shard_map/ppermute | solution.py:31
  83.4 51.3 %collective-permute-start.8 = (bf16[128,4096]{1,0:T(8,128)(2,1)S(1)}, bf16[128,4096]{1,0:T(8,128)(2,1)S(1)}, u32[]{:S(2)}, u32[]{:S(2)}) collective-permute-start(bf16[128,4096]{1,0:T(8,128)(2,1)S(1)} %pad_maximum_fusion.6), channel_id=1, source_target_pairs={{0,1},{1,0},{2,3},{3,2},{4,5},{5,4},{6,7},{7,6},{8,9},{9,8},{10,11... | collective-permute-start | bytes 3145736 | tf_op jit(solution)/shard_map/ppermute | solution.py:31
  109.9 23.2 %collective-permute-start.5 = (bf16[32,2048]{1,0:T(8,128)(2,1)S(1)}, bf16[32,2048]{1,0:T(8,128)(2,1)S(1)}, u32[]{:S(2)}, u32[]{:S(2)}) collective-permute-start(bf16[32,2048]{1,0:T(8,128)(2,1)S(1)} %slice.117), channel_id=1, source_target_pairs={{0,2},{1,3},{2,0},{3,1},{4,6},{5,7},{6,4},{7,5},{8,10},{9,11},{10,... | collective-permute-start | bytes 393224 | tf_op jit(solution)/shard_map/ppermute | solution.py:31
  114.2 22.1 %copy-start.21 = (bf16[256,4096]{1,0:T(8,128)(2,1)}, bf16[256,4096]{1,0:T(8,128)(2,1)S(1)}, u32[]{:S(2)}) copy-start(bf16[256,4096]{1,0:T(8,128)(2,1)S(1)} %pad_maximum_fusion.5.xa_ref) | copy-start | bytes 6291460
  114.2 61.6 %collective-permute-start.15 = (bf16[256,4096]{1,0:T(8,128)(2,1)S(1)}, bf16[256,4096]{1,0:T(8,128)(2,1)S(1)}, u32[]{:S(2)}, u32[]{:S(2)}) collective-permute-start(bf16[256,4096]{1,0:T(8,128)(2,1)S(1)} %pad_maximum_fusion.5.xa_ref), channel_id=1, source_target_pairs={{0,4},{4,0},{1,5},{5,1},{2,6},{6,2},{3,7},{7,3},{8,12},{12,8},{9,1... | collective-permute-start | bytes 6291464 | tf_op jit(solution)/shard_map/ppermute | solution.py:31
  133.2 5.7 %copy-start.23 = (bf16[16,4096]{1,0:T(8,128)(2,1)S(1)}, bf16[16,4096]{1,0:T(8,128)(2,1)}, u32[]{:S(2)}) copy-start(bf16[16,4096]{1,0:T(8,128)(2,1)} %param.24) | copy-start | bytes 393220
  133.2 5.7 %collective-permute-start.6 = (f32[16,2048]{1,0:T(8,128)S(1)}, f32[16,2048]{1,0:T(8,128)S(1)}, u32[]{:S(2)}, u32[]{:S(2)}) collective-permute-start(f32[16,2048]{1,0:T(8,128)S(1)} %get-tuple-element.25), channel_id=1, source_target_pairs={{0,4},{4,0},{1,5},{5,1},{2,6},{6,2},{3,7},{7,3},{8,12},{12,8},{9,1... | collective-permute-start | bytes 393224 | tf_op jit(solution)/shard_map/ppermute | solution.py:31
  136.3 64.3 %copy-start.22 = (bf16[256,4096]{1,0:T(8,128)(2,1)}, bf16[256,4096]{1,0:T(8,128)(2,1)S(1)}, u32[]{:S(2)}) copy-start(bf16[256,4096]{1,0:T(8,128)(2,1)S(1)} %pad_maximum_fusion.4.xa_ref) | copy-start | bytes 6291460
  136.4 64.4 %collective-permute-start.9 = (bf16[256,4096]{1,0:T(8,128)(2,1)S(1)}, bf16[256,4096]{1,0:T(8,128)(2,1)S(1)}, u32[]{:S(2)}, u32[]{:S(2)}) collective-permute-start(bf16[256,4096]{1,0:T(8,128)(2,1)S(1)} %pad_maximum_fusion.4.xa_ref), channel_id=1, source_target_pairs={{0,4},{4,0},{1,5},{5,1},{2,6},{6,2},{3,7},{7,3},{8,12},{12,8},{9,1... | collective-permute-start | bytes 6291464 | tf_op jit(solution)/shard_map/ppermute | solution.py:31
  136.4 37.7 %collective-permute-start.19 = (bf16[1,3,512,256]{3,2,1,0:T(8,128)(2,1)S(1)}, bf16[1,3,512,256]{3,2,1,0:T(8,128)(2,1)S(1)}, u32[]{:S(2)}, u32[]{:S(2)}) collective-permute-start(bf16[1,3,512,256]{3,2,1,0:T(8,128)(2,1)S(1)} %maximum_bitcast_fusion), channel_id=1, source_target_pairs={{0,2},{1,3},{2,0},{3,1},{4,6},{5,7},{6,4},{7,5},{8,10},{9,11},{10,... | collective-permute-start | bytes 2359304 | tf_op jit(solution)/shard_map/ppermute | solution.py:31
  174.2 52.5 %copy-start.11 = (bf16[2,3,512,256]{3,2,1,0:T(8,128)(2,1)}, bf16[2,3,512,256]{3,2,1,0:T(8,128)(2,1)S(1)}, u32[]{:S(2)}) copy-start(bf16[2,3,512,256]{3,2,1,0:T(8,128)(2,1)S(1)} %constant_dynamic-update-slice_fusion) | copy-start | bytes 4718596
  174.2 50.6 %collective-permute-start.23 = (bf16[2,3,512,256]{3,2,1,0:T(8,128)(2,1)S(1)}, bf16[2,3,512,256]{3,2,1,0:T(8,128)(2,1)S(1)}, u32[]{:S(2)}, u32[]{:S(2)}) collective-permute-start(bf16[2,3,512,256]{3,2,1,0:T(8,128)(2,1)S(1)} %constant_dynamic-update-slice_fusion), channel_id=1, source_target_pairs={{0,1},{1,0},{2,3},{3,2},{4,5},{5,4},{6,7},{7,6},{8,9},{9,8},{10,11... | collective-permute-start | bytes 4718600 | tf_op jit(solution)/shard_map/ppermute | solution.py:31
  174.4 52.4 %collective-permute-start.20 = (bf16[1,2,3,512,256]{4,3,2,1,0:T(8,128)(2,1)S(1)}, bf16[1,2,3,512,256]{4,3,2,1,0:T(8,128)(2,1)S(1)}, u32[]{:S(2)}, u32[]{:S(2)}) collective-permute-start(bf16[1,2,3,512,256]{4,3,2,1,0:T(8,128)(2,1)S(1)} %bitcast.76), channel_id=1, source_target_pairs={{0,8},{8,0},{16,24},{24,16},{1,9},{9,1},{17,25},{25,17},{2,10},{10... | collective-permute-start | bytes 4718600 | tf_op jit(solution)/shard_map/ppermute | solution.py:31
  175.9 1.4 copy-start.28
  200.7 24.0 %copy-start.6 = (bf16[256,4096]{1,0:T(8,128)(2,1)}, bf16[256,4096]{1,0:T(8,128)(2,1)S(1)}, u32[]{:S(2)}) copy-start(bf16[256,4096]{1,0:T(8,128)(2,1)S(1)} %get-tuple-element.12) | copy-start | bytes 6291460
  200.7 25.7 %copy-start.26 = (f32[4096]{0:T(1024)S(1)}, f32[4096]{0:T(1024)}, u32[]{:S(2)}) copy-start(f32[4096]{0:T(1024)} %param.28) | copy-start | bytes 49156
  200.7 86.4 %collective-permute-start.16 = (bf16[256,4096]{1,0:T(8,128)(2,1)}, bf16[256,4096]{1,0:T(8,128)(2,1)}, u32[]{:S(2)}, u32[]{:S(2)}) collective-permute-start(bf16[256,4096]{1,0:T(8,128)(2,1)} %get-tuple-element.13), channel_id=1, source_target_pairs={{0,4},{4,0},{1,5},{5,1},{2,6},{6,2},{3,7},{7,3},{8,12},{12,8},{9,1... | collective-permute-start | bytes 6291464 | tf_op jit(solution)/shard_map/ppermute | solution.py:31
  200.8 1.4 copy-start.29
  224.6 4.3 copy-start.9
  224.8 37.3 %copy-start.14 = (bf16[2,3,512,256]{3,2,1,0:T(8,128)(2,1)}, bf16[2,3,512,256]{3,2,1,0:T(8,128)(2,1)S(1)}, u32[]{:S(2)}) copy-start(bf16[2,3,512,256]{3,2,1,0:T(8,128)(2,1)S(1)} %collective-permute-done.23) | copy-start | bytes 4718596
  224.8 37.3 %collective-permute-start.24 = (bf16[1,2,3,512,256]{4,3,2,1,0:T(8,128)(2,1)S(1)}, bf16[1,2,3,512,256]{4,3,2,1,0:T(8,128)(2,1)S(1)}, u32[]{:S(2)}, u32[]{:S(2)}) collective-permute-start(bf16[1,2,3,512,256]{4,3,2,1,0:T(8,128)(2,1)S(1)} %bitcast.81), channel_id=1, source_target_pairs={{0,16},{8,24},{16,0},{24,8},{1,17},{9,25},{17,1},{25,9},{2,18},{10... | collective-permute-start | bytes 4718600 | tf_op jit(solution)/shard_map/ppermute | solution.py:31
  226.5 3.0 collective-permute-start.27
  226.7 2.2 copy-start.16
  229.0 100.1 %collective-permute-start.21 = (bf16[2,2,3,512,256]{4,3,2,1,0:T(8,128)(2,1)}, bf16[2,2,3,512,256]{4,3,2,1,0:T(8,128)(2,1)}, u32[]{:S(2)}, u32[]{:S(2)}) collective-permute-start(bf16[2,2,3,512,256]{4,3,2,1,0:T(8,128)(2,1)} %pad_maximum_fusion.2), channel_id=1, source_target_pairs={{0,16},{8,24},{16,0},{24,8},{1,17},{9,25},{17,1},{25,9},{2,18},{10... | collective-permute-start | bytes 9437192 | tf_op jit(solution)/shard_map/ppermute | solution.py:31
  229.5 38.5 %copy-start.27 = (s32[4]{0:T(128)S(1)}, s32[4]{0:T(128)}, u32[]{:S(2)}) copy-start(s32[4]{0:T(128)} %constant.69.clone) | copy-start | bytes 52
  229.5 35.3 %collective-permute-start.28 = (bf16[32,2048]{1,0:T(8,128)(2,1)S(1)}, bf16[32,2048]{1,0:T(8,128)(2,1)S(1)}, u32[]{:S(2)}, u32[]{:S(2)}) collective-permute-start(bf16[32,2048]{1,0:T(8,128)(2,1)S(1)} %maximum_select_fusion.2), channel_id=1, source_target_pairs={{0,2},{1,3},{2,0},{3,1},{4,6},{5,7},{6,4},{7,5},{8,10},{9,11},{10,... | collective-permute-start | bytes 393224 | tf_op jit(solution)/shard_map/ppermute | solution.py:31
  262.1 2.3 copy-start.18
  264.3 69.5 %collective-permute-start.25 = (bf16[2,2,3,512,256]{4,3,2,1,0:T(8,128)(2,1)}, bf16[2,2,3,512,256]{4,3,2,1,0:T(8,128)(2,1)}, u32[]{:S(2)}, u32[]{:S(2)}) collective-permute-start(bf16[2,2,3,512,256]{4,3,2,1,0:T(8,128)(2,1)} %pad_maximum_fusion.3), channel_id=1, source_target_pairs={{0,8},{8,0},{16,24},{24,16},{1,9},{9,1},{17,25},{25,17},{2,10},{10... | collective-permute-start | bytes 9437192 | tf_op jit(solution)/shard_map/ppermute | solution.py:31
  265.6 11.7 %collective-permute-start.29 = (bf16[64,2048]{1,0:T(8,128)(2,1)}, bf16[64,2048]{1,0:T(8,128)(2,1)}, u32[]{:S(2)}, u32[]{:S(2)}) collective-permute-start(bf16[64,2048]{1,0:T(8,128)(2,1)} %pad_maximum_fusion.11), channel_id=1, source_target_pairs={{0,1},{1,0},{2,3},{3,2},{4,5},{5,4},{6,7},{7,6},{8,9},{9,8},{10,11... | collective-permute-start | bytes 786440 | tf_op jit(solution)/shard_map/ppermute | solution.py:31
  276.4 3.3 copy-start.10
  276.4 6.2 %copy-start.24 = (s32[128,1024]{1,0:T(8,128)S(1)}, s32[128,1024]{1,0:T(8,128)}, u32[]{:S(2)}) copy-start(s32[128,1024]{1,0:T(8,128)} %param.22) | copy-start | bytes 1572868
  279.0 1.4 collective-permute-start.30
  279.7 57.3 %collective-permute-start.10 = (bf16[256,4096]{1,0:T(8,128)(2,1)S(1)}, bf16[256,4096]{1,0:T(8,128)(2,1)S(1)}, u32[]{:S(2)}, u32[]{:S(2)}) collective-permute-start(bf16[256,4096]{1,0:T(8,128)(2,1)S(1)} %copy-done.10), channel_id=1, source_target_pairs={{0,4},{4,0},{1,5},{5,1},{2,6},{6,2},{3,7},{7,3},{8,12},{12,8},{9,1... | collective-permute-start | bytes 6291464 | tf_op jit(solution)/shard_map/ppermute | solution.py:31
  280.4 6.5 %collective-permute-start.31 = (bf16[1,128,256]{2,1,0:T(8,128)(2,1)S(1)}, bf16[1,128,256]{2,1,0:T(8,128)(2,1)S(1)}, u32[]{:S(2)}, u32[]{:S(2)}) collective-permute-start(bf16[1,128,256]{2,1,0:T(8,128)(2,1)S(1)} %bitcast.87), channel_id=1, source_target_pairs={{0,2},{1,3},{2,0},{3,1},{4,6},{5,7},{6,4},{7,5},{8,10},{9,11},{10,... | collective-permute-start | bytes 196616 | tf_op jit(solution)/shard_map/ppermute | solution.py:31
  283.3 3.8 copy-start.7
  287.0 54.7 %collective-permute-start.32 = (bf16[2,128,256]{2,1,0:T(8,128)(2,1)S(1)}, bf16[2,128,256]{2,1,0:T(8,128)(2,1)S(1)}, u32[]{:S(2)}, u32[]{:S(2)}) collective-permute-start(bf16[2,128,256]{2,1,0:T(8,128)(2,1)S(1)} %pad_maximum_fusion.13), channel_id=1, source_target_pairs={{0,1},{1,0},{2,3},{3,2},{4,5},{5,4},{6,7},{7,6},{8,9},{9,8},{10,11... | collective-permute-start | bytes 393224 | tf_op jit(solution)/shard_map/ppermute | solution.py:31
  287.1 42.0 %copy-start.17 = (bf16[1,2,3,512,256]{4,3,2,1,0:T(8,128)(2,1)S(1)}, bf16[1,2,3,512,256]{4,3,2,1,0:T(8,128)(2,1)}, u32[]{:S(2)}) copy-start(bf16[1,2,3,512,256]{4,3,2,1,0:T(8,128)(2,1)} %copy-done.16) | copy-start | bytes 4718596
  289.4 39.7 %copy-start.12 = (bf16[2,3,512,256]{3,2,1,0:T(8,128)(2,1)S(1)}, bf16[2,3,512,256]{3,2,1,0:T(8,128)(2,1)}, u32[]{:S(2)}) copy-start(bf16[2,3,512,256]{3,2,1,0:T(8,128)(2,1)} %copy-done.11) | copy-start | bytes 4718596
  290.5 43.3 %copy-start.15 = (bf16[2,3,512,256]{3,2,1,0:T(8,128)(2,1)S(1)}, bf16[2,3,512,256]{3,2,1,0:T(8,128)(2,1)}, u32[]{:S(2)}) copy-start(bf16[2,3,512,256]{3,2,1,0:T(8,128)(2,1)} %copy-done.14) | copy-start | bytes 4718596
  290.5 43.3 %copy-start.19 = (bf16[1,2,3,512,256]{4,3,2,1,0:T(8,128)(2,1)S(1)}, bf16[1,2,3,512,256]{4,3,2,1,0:T(8,128)(2,1)}, u32[]{:S(2)}) copy-start(bf16[1,2,3,512,256]{4,3,2,1,0:T(8,128)(2,1)} %copy-done.18) | copy-start | bytes 4718596
  290.5 51.2 %collective-permute-start.17 = (bf16[128,4096]{1,0:T(8,128)(2,1)}, bf16[128,4096]{1,0:T(8,128)(2,1)}, u32[]{:S(2)}, u32[]{:S(2)}) collective-permute-start(bf16[128,4096]{1,0:T(8,128)(2,1)} %slice.113), channel_id=1, source_target_pairs={{0,1},{1,0},{2,3},{3,2},{4,5},{5,4},{6,7},{7,6},{8,9},{9,8},{10,11... | collective-permute-start | bytes 3145736 | tf_op jit(solution)/shard_map/ppermute | solution.py:31
  332.0 69.5 %collective-permute-start.22 = (bf16[4,2,3,512,256]{4,3,2,1,0:T(8,128)(2,1)S(1)}, bf16[4,2,3,512,256]{4,3,2,1,0:T(8,128)(2,1)S(1)}, u32[]{:S(2)}, u32[]{:S(2)}) collective-permute-start(bf16[4,2,3,512,256]{4,3,2,1,0:T(8,128)(2,1)S(1)} %pad_maximum_fusion.a0_ref), channel_id=1, source_target_pairs={{0,4},{4,0},{1,5},{5,1},{2,6},{6,2},{3,7},{7,3},{8,12},{12,8},{9,1... | collective-permute-start | bytes 18874376 | tf_op jit(solution)/shard_map/ppermute | solution.py:31
  337.0 2.7 copy-start.2
  337.0 64.6 %collective-permute-start.26 = (bf16[4,2,3,512,256]{4,3,2,1,0:T(8,128)(2,1)S(1)}, bf16[4,2,3,512,256]{4,3,2,1,0:T(8,128)(2,1)}, u32[]{:S(2)}, u32[]{:S(2)}) collective-permute-start(bf16[4,2,3,512,256]{4,3,2,1,0:T(8,128)(2,1)S(1)} %pad_maximum_fusion.1.b0_ref), channel_id=1, source_target_pairs={{0,4},{4,0},{1,5},{5,1},{2,6},{6,2},{3,7},{7,3},{8,12},{12,8},{9,1... | collective-permute-start | bytes 18874376 | tf_op jit(solution)/shard_map/ppermute | solution.py:31
  339.8 35.2 %collective-permute-start.11 = (bf16[128,4096]{1,0:T(8,128)(2,1)S(1)}, bf16[128,4096]{1,0:T(8,128)(2,1)S(1)}, u32[]{:S(2)}, u32[]{:S(2)}) collective-permute-start(bf16[128,4096]{1,0:T(8,128)(2,1)S(1)} %slice.114), channel_id=1, source_target_pairs={{0,1},{1,0},{2,3},{3,2},{4,5},{5,4},{6,7},{7,6},{8,9},{9,8},{10,11... | collective-permute-start | bytes 3145736 | tf_op jit(solution)/shard_map/ppermute | solution.py:31
  343.2 33.3 %collective-permute-start.18 = (bf16[64,4096]{1,0:T(8,128)(2,1)S(1)}, bf16[64,4096]{1,0:T(8,128)(2,1)S(1)}, u32[]{:S(2)}, u32[]{:S(2)}) collective-permute-start(bf16[64,4096]{1,0:T(8,128)(2,1)S(1)} %slice.115), channel_id=1, source_target_pairs={{0,2},{1,3},{2,0},{3,1},{4,6},{5,7},{6,4},{7,5},{8,10},{9,11},{10,... | collective-permute-start | bytes 1572872 | tf_op jit(solution)/shard_map/ppermute | solution.py:31
  375.3 24.9 %collective-permute-start.12 = (bf16[64,4096]{1,0:T(8,128)(2,1)S(1)}, bf16[64,4096]{1,0:T(8,128)(2,1)S(1)}, u32[]{:S(2)}, u32[]{:S(2)}) collective-permute-start(bf16[64,4096]{1,0:T(8,128)(2,1)S(1)} %slice.116), channel_id=1, source_target_pairs={{0,2},{1,3},{2,0},{3,1},{4,6},{5,7},{6,4},{7,5},{8,10},{9,11},{10,... | collective-permute-start | bytes 1572872 | tf_op jit(solution)/shard_map/ppermute | solution.py:31
  400.3 0.8 copy-start.25
  401.1 10.5 %copy-start.20 = (bf16[128,4096]{1,0:T(8,128)(2,1)}, bf16[128,4096]{1,0:T(8,128)(2,1)S(1)}, u32[]{:S(2)}) copy-start(bf16[128,4096]{1,0:T(8,128)(2,1)S(1)} %get-tuple-element.17) | copy-start | bytes 3145732
  401.5 22.9 %copy-start.8 = (s32[16,1024]{1,0:T(8,128)S(1)}, s32[16,1024]{1,0:T(8,128)}, u32[]{:S(2)}) copy-start(s32[16,1024]{1,0:T(8,128)} %words_ref.1) | copy-start | bytes 196612
  401.5 10.1 %copy-start.4 = (bf16[4,2,3,512,256]{4,3,2,1,0:T(8,128)(2,1)}, bf16[4,2,3,512,256]{4,3,2,1,0:T(8,128)(2,1)S(1)}, u32[]{:S(2)}) copy-start(bf16[4,2,3,512,256]{4,3,2,1,0:T(8,128)(2,1)S(1)} %collective-permute-done.22.a1_ref) | copy-start | bytes 18874372
  424.4 2.8 copy-start.3
  427.2 2.8 copy-start.5
  430.0 7.4 %copy-start.1 = (bf16[2048,2,256]{2,1,0:T(2,128)(2,1)S(1)}, bf16[2048,2,256]{2,1,0:T(2,128)(2,1)}, u32[]{:S(2)}) copy-start(bf16[2048,2,256]{2,1,0:T(2,128)(2,1)} %param.30) | copy-start | bytes 6291460

commit v3 on v0

v3 whole, which is shorter than its diff:
```python
import functools

import jax
import jax.numpy as jnp
from jax import lax
from jax.experimental import pallas as pl
from jax.experimental.pallas import tpu as pltpu
from jax.sharding import PartitionSpec as P

HD = 256
F32 = jnp.float32
BF16 = jnp.bfloat16
CHUNKS = 2


def norm_rows(x, gain):
    values = x.astype(F32)
    power = jnp.mean(values * values, axis=-1, keepdims=True)
    return values * lax.rsqrt(power + 1e-06) * gain


def keep_factor(words):
    shifts = jnp.arange(4, dtype=jnp.int32) * 3
    bits = jnp.right_shift(words[:, None, :], shifts[None, :, None]) & 7
    kept = jnp.where(bits == 7, 0.0, 8.0 / 7.0).astype(F32)
    return kept.reshape(words.shape[0], 4 * words.shape[1])


def swap(value, axis, distance):
    return lax.ppermute(value, axis, [(i, i ^ distance) for i in range(lax.axis_size(axis))])


def from_slots(value):
    count = lax.axis_size("tensor")
    return [value] + [
        lax.ppermute(value, "tensor", [(i, (i - o) % count) for i in range(count)]) for o in range(1, count)
    ]


def line_slots(value):
    count, tensor = lax.axis_size("tensor"), lax.axis_index("tensor")
    above, below = [value], [value]
    for step in range(1, count):
        above.append(lax.ppermute(above[-1], "tensor", [(i, i + 1) for i in range(step - 1, count - 1)]))
        below.append(lax.ppermute(below[-1], "tensor", [(i, i - 1) for i in range(1, count - step + 1)]))
    return [value] + [jnp.where(tensor + o < count, below[o], above[count - o]) for o in range(1, count)]


def line_sum(mine, got):
    count = lax.axis_size("tensor")
    block = mine.shape[0] // count

    def part(slot):
        at = slice(slot * block, (slot + 1) * block)
        return mine[at].astype(F32) + got[at].astype(F32)

    above, below = None, None
    for step in range(1, count):
        send_up, send_down = part(count - step), part(step)
        if step > 1:
            send_up = send_up + above.astype(F32)
            send_down = send_down + below.astype(F32)
        above = lax.ppermute(send_up.astype(BF16), "tensor", [(i, i + 1) for i in range(step)])
        below = lax.ppermute(
            send_down.astype(BF16), "tensor", [(i, i - 1) for i in range(count - step, count)]
        )
    return part(0) + above.astype(F32) + below.astype(F32)


def slots_sum(product):
    count = lax.axis_size("tensor")
    product = product.reshape(count, product.shape[0] // count, product.shape[1])
    total = product[0].astype(F32)
    for o in range(1, count):
        total = total + lax.ppermute(
            product[o], "tensor", [(i, (i + o) % count) for i in range(count)]
        ).astype(F32)
    return total


def half_columns(value, index):
    return lax.dynamic_slice_in_dim(value, index * (value.shape[1] // 2), value.shape[1] // 2, 1)


def in_order(own, other, section, axis):
    return jnp.where(
        section == 0, jnp.concatenate([own, other], axis), jnp.concatenate([other, own], axis)
    )


def gather_half(rows, section):
    own = half_columns(rows, section)
    other = swap(half_columns(rows, 1 - section), "section", 1)
    return jnp.concatenate(from_slots(in_order(own, other, section, 0)), 0)


def whole_rows(total, section):
    rows = total.shape[0] // 2
    own = lax.dynamic_slice_in_dim(total, section * rows, rows, 0)
    other = swap(lax.dynamic_slice_in_dim(total, (1 - section) * rows, rows, 0), "section", 1)
    return in_order(own, other, section, 1)


def both_halves(partial):
    return partial + swap(partial, "section", 1)


def gelu(x):
    return 0.5 * x * (1.0 + jnp.tanh(0.7978845608028654 * (x + 0.044715 * x * x * x)))


def ffn_kernel(hidden_steps, xa_ref, xb_ref, gate_ref, up_ref, down_ref, ya_ref, yb_ref, x, hidden):
    step = pl.program_id(0)
    rows = xa_ref.shape[0]
    width = gate_ref.shape[1]

    @pl.when(step == 0)
    def _():
        x[:rows, :] = xa_ref[...]
        x[rows:, :] = xb_ref[...]

    @pl.when(step < hidden_steps)
    def _():
        gate = jnp.dot(x[...], gate_ref[...], preferred_element_type=F32)
        up = jnp.dot(x[...], up_ref[...], preferred_element_type=F32)
        hidden[step] = (gelu(gate) * up).astype(BF16)

    @pl.when(step >= hidden_steps)
    def _():
        total = jnp.zeros((2 * rows, ya_ref.shape[1]), F32)
        for k in range(hidden.shape[0]):
            total += jnp.dot(
                hidden[k], down_ref[k * width : (k + 1) * width, :], preferred_element_type=F32
            )
        ya_ref[...] = total[:rows].astype(BF16)
        yb_ref[...] = total[rows:].astype(BF16)


def ffn(xa, xb, w_gate, w_up, w_down):
    rows, features = xa.shape
    units = w_gate.shape[1]
    width = min(256, units)
    tile = 512
    first, last = units // width, features // tile
    return pl.pallas_call(
        functools.partial(ffn_kernel, first),
        grid=(first + last,),
        in_specs=[
            pl.BlockSpec((rows, features), lambda i: (0, 0)),
            pl.BlockSpec((rows, features), lambda i: (0, 0)),
            pl.BlockSpec((features, width), lambda i: (0, jnp.minimum(i, first - 1))),
            pl.BlockSpec((features, width), lambda i: (0, jnp.minimum(i, first - 1))),
            pl.BlockSpec((units, tile), lambda i: (0, jnp.maximum(i - first, 0))),
        ],
        out_specs=[pl.BlockSpec((rows, tile), lambda i: (0, jnp.maximum(i - first, 0)))] * 2,
        out_shape=[jax.ShapeDtypeStruct((rows, features), BF16)] * 2,
        scratch_shapes=[
            pltpu.VMEM((2 * rows, features), BF16),
            pltpu.VMEM((first, 2 * rows, width), BF16),
        ],
        compiler_params=pltpu.CompilerParams(vmem_limit_bytes=48 * 2**20),
        cost_estimate=pl.CostEstimate(
            flops=12 * rows * features * units, bytes_accessed=6 * features * units, transcendentals=0
        ),
        name="ffn",
    )(xa, xb, w_gate, w_up, w_down)


def per_device(
    source,
    enc_gain,
    w_gate,
    w_up,
    w_down,
    enc_keep,
    final_gain,
    target,
    self_gain,
    self_qkv,
    self_out,
    cross_gain,
    cross_q,
    cross_kv,
    cross_out,
    dec_keep,
):
    section = lax.axis_index("section")
    count, tensor = lax.axis_size("tensor"), lax.axis_index("tensor")
    rows = target.shape[0]
    after = lax.optimization_barrier

    selfin = norm_rows(target, self_gain).astype(BF16)
    selfin = gather_half(selfin, section)

    normed = norm_rows(source, enc_gain).astype(BF16)
    block = normed.shape[0] // CHUNKS
    near = [
        jnp.concatenate(line_slots(normed[c * block : (c + 1) * block]), 0) for c in range(CHUNKS)
    ]
    far = [swap(x, "section", 1) for x in near]
    kv = jnp.transpose(cross_kv, (1, 0, 2))
    kv = in_order(kv, swap(kv, "section", 1), section, 1)

    qkv_w = jnp.transpose(self_qkv, (1, 0, 2))
    q, k, v = [jnp.dot(selfin, qkv_w[i], preferred_element_type=F32) for i in range(3)]
    q, k, v = [y.astype(BF16) for y in both_halves(jnp.stack([q, k, v]))]
    slot_chip = lax.rem(tensor + jnp.arange(count, dtype=jnp.int32), count)
    positions = (
        (jnp.arange(2, dtype=jnp.int32)[None, :] * count + slot_chip[:, None])[:, :, None] * rows
        + jnp.arange(rows, dtype=jnp.int32)
    ).reshape(-1)
    scores = lax.dot_general(q, k, (((1,), (1,)), ((), ())), preferred_element_type=F32) * (1.0 / 16.0)
    scores = jnp.where(positions[None, :] <= positions[:, None], scores, F32(-1e30))
    expo = jnp.exp(scores - jnp.max(scores, axis=-1, keepdims=True))
    probs = (expo / jnp.sum(expo, axis=-1, keepdims=True)).astype(BF16)
    context = jnp.dot(probs, v, preferred_element_type=F32).astype(BF16)
    product = jnp.dot(context, self_out, preferred_element_type=F32).astype(BF16)
    total = slots_sum(product)

    shares = [ffn(near[0], far[0], w_gate, w_up, w_down)]
    total, first = after((total, shares[0][0]))
    shares[0] = (first, shares[0][1])
    mid = (target.astype(F32) + whole_rows(total, section)).astype(BF16)
    crossin = gather_half(norm_rows(mid, cross_gain).astype(BF16), section)
    for c in range(1, CHUNKS):
        shares.append(ffn(near[c], far[c], w_gate, w_up, w_down))
    crossin, last = after((crossin, shares[-1][0]))
    shares[-1] = (last, shares[-1][1])
    cq = both_halves(jnp.dot(crossin, cross_q, preferred_element_type=F32)).astype(BF16)

    outs, keys, values = [], [], []
    for c, (ya, yb) in enumerate(shares):
        at = slice(c * block, (c + 1) * block)
        total = line_sum(ya, swap(yb, "section", 1))
        out = (source[at].astype(F32) + keep_factor(enc_keep[at]) * total).astype(BF16)
        outs.append(out)
        memory = norm_rows(out, final_gain).astype(BF16)
        memory = jnp.concatenate(line_slots(memory), 0)
        keys.append(jnp.dot(memory, kv[0], preferred_element_type=F32).astype(BF16))
        values.append(jnp.dot(memory, kv[1], preferred_element_type=F32).astype(BF16))
    enc_out = jnp.concatenate(outs, 0)
    keys, values = jnp.concatenate(keys, 0), jnp.concatenate(values, 0)

    scores = lax.dot_general(cq, keys, (((1,), (1,)), ((), ())), preferred_element_type=F32) * (1.0 / 16.0)
    top = jnp.max(scores, axis=-1, keepdims=True)
    expo = jnp.exp(scores - top)
    whole = jnp.sum(expo, axis=-1, keepdims=True)
    context = jnp.dot(expo.astype(BF16), values, preferred_element_type=F32)
    ours = jnp.concatenate(
        [context, jnp.broadcast_to(top, (top.shape[0], 128)), jnp.broadcast_to(whole, (top.shape[0], 128))], 1
    )
    theirs = swap(ours, "section", 1)
    their_top, their_whole = theirs[:, HD : HD + 1], theirs[:, HD + 128 : HD + 129]
    most = jnp.maximum(top, their_top)
    mine, other = jnp.exp(top - most), jnp.exp(their_top - most)
    context = (context * mine + theirs[:, :HD] * other) / (whole * mine + their_whole * other)
    product = jnp.dot(context.astype(BF16), cross_out, preferred_element_type=F32).astype(BF16)
    crosssum = whole_rows(slots_sum(product), section)
    dec_out = (mid.astype(F32) + keep_factor(dec_keep) * crosssum).astype(BF16)
    return (enc_out, dec_out)


def solution(mesh):
    return jax.shard_map(
        per_device,
        mesh=mesh,
        in_specs=(
            P(("dp", "section", "tensor"), None),
            P(),
            P(None, ("section", "tensor")),
            P(None, ("section", "tensor")),
            P(("section", "tensor"), None),
            P(("dp", "section", "tensor"), None),
            P(),
            P(("dp", "section", "tensor"), None),
            P(),
            P("section", None, "tensor"),
            P("tensor", "section"),
            P(),
            P("section", "tensor"),
            P("section", None, "tensor"),
            P("tensor", "section"),
            P(("dp", "section", "tensor"), None),
        ),
        out_specs=(P(("dp", "section", "tensor"), None), P(("dp", "section", "tensor"), None)),
        check_vma=False,
    )
```

time: 497 us -> 377 us (0.76)
  waiting for transfers between devices: 354 us -> 199 us
  starting transfers between devices: 1.94 us -> 93.9 us
  matrix products: 62.1 us -> 9.95 us
  Pallas kernels: 0 us -> 45.3 us
  blocking collectives: 38.1 us -> 0 us
  between operations: 14.4 us -> 1.8 us
  local copies, waits for them, and re-layouts: 13.1 us -> 3.31 us
  other arithmetic: 12.8 us -> 22 us
    ppermute x2 -> x60, waiting for transfers between devices: 0.81 us -> 199 us  [the longest x12 78.1 us: line_slots(): lax.ppermute(below[-1], 'tensor', [(i, i - 1) for i in range(1, count - s...]
    reduce_scatter x3 -> x0, waiting for transfers between devices: 178 us -> none  [the longest x1 136 us: per_device(): lax.psum_scatter(jnp.dot(piece, w_down, preferred_element_type=jnp.float3...]
    all_gather x7 -> x0, waiting for transfers between devices: 172 us -> none  [the longest x1 80.9 us: per_device(): lax.all_gather(source, ('section', 'tensor'), axis=0, tiled=True)]
    ppermute x2 -> x60, starting transfers between devices: 1.36 us -> 93.9 us  [the longest x12 33.2 us: line_slots(): lax.ppermute(above[-1], 'tensor', [(i, i + 1) for i in range(step - 1, co...]
    dot_general x8 -> x13, matrix products: 62.1 us -> 9.95 us  [the longest x3 4.3 us: per_device(): jnp.dot(selfin, qkv_w[i], preferred_element_type=F32)]
    pallas_call x0 -> x2, Pallas kernels: none -> 45.3 us  [ffn(): pl.pallas_call(functools.partial(ffn_kernel, first), grid=(first + last,)...]
    all_gather x2 -> x0, blocking collectives: 38.1 us -> none  [the longest x1 21.9 us: per_device(): lax.all_gather(selfin, 'tensor', axis=0, tiled=True)]
    unnamed x26 -> x46, local copies, waits for them, and re-layouts: 12.2 us -> 2.32 us
  transfers between devices with their start and end apart: 12 -> 60, of which waited for: 7 -> 31; matrix products, arithmetic and copies ran while one was open for 17% -> 8% of each run, Pallas kernels for 0% -> 12%
where the time goes in v3:
time: 377 us; the launch traced here: 376 us
  waiting for transfers between devices  199 us (53%)
  starting transfers between devices  93.9 us (25%)
  Pallas kernels  45.3 us (12%)
  other arithmetic  22 us (6%)
  matrix products  9.95 us (3%)
    ppermute x12, waiting for transfers between devices, line_slots(): lax.ppermute(below[-1], 'tensor', [(i, i - 1) for i in range(1, count - s...  78.1 us
    pallas_call x2, Pallas kernels, ffn(): pl.pallas_call(functools.partial(ffn_kernel, first), grid=(first + last,)...  45.3 us
    ppermute x6, waiting for transfers between devices, line_sum(): lax.ppermute(send_up.astype(BF16), 'tensor', [(i, i + 1) for i in range(s...  38.7 us
    ppermute x12, starting transfers between devices, line_slots(): lax.ppermute(above[-1], 'tensor', [(i, i + 1) for i in range(step - 1, co...  33.2 us
    ppermute x6, waiting for transfers between devices, from_slots(): lax.ppermute(value, 'tensor', [(i, (i - o) % count) for i in range(count)])  28.4 us
    ppermute x6, waiting for transfers between devices, line_sum(): lax.ppermute(send_down.astype(BF16), 'tensor', [(i, i - 1) for i in range...  21.5 us
    ppermute x6, starting transfers between devices, line_sum(): lax.ppermute(send_up.astype(BF16), 'tensor', [(i, i + 1) for i in range(s...  20.5 us
    ppermute x6, waiting for transfers between devices, slots_sum(): lax.ppermute(product[o], 'tensor', [(i, (i + o) % count) for i in range(c...  18.5 us
  transfers between devices with their start and end apart: 60, of which 31 were waited for; matrix products, arithmetic and copies ran while one was open for 8% of the time, Pallas kernels for 12%

profile of v3, /device:TPU:0, one launch (start us, length us, event | category | flops | bytes accessed | tf_op | source)
XLA Modules:
  0.0 375.7 jit_solution(1896532891873195559)
XLA Ops:
  3.4 1.5 fusion
  6.1 5.3 %collective-permute-start.9 = (bf16[64,4096]{1,0:T(8,128)(2,1)S(1)}, bf16[64,4096]{1,0:T(8,128)(2,1)}, u32[]{:S(2)}, u32[]{:S(2)}) collective-permute-start(bf16[64,4096]{1,0:T(8,128)(2,1)S(1)} %get-tuple-element.30), channel_id=1, source_target_pairs={{0,1},{1,2},{2,3},{4,5},{5,6},{6,7},{8,9},{9,10},{10,11},{12,13},{... | collective-permute-start | bytes 1572872 | tf_op jit(solution)/shard_map/ppermute | solution.py:44
  12.8 4.7 %collective-permute-start.1 = (bf16[32,2048]{1,0:T(8,128)(2,1)S(1)}, bf16[32,2048]{1,0:T(8,128)(2,1)S(1)}, u32[]{:S(2)}, u32[]{:S(2)}) collective-permute-start(bf16[32,2048]{1,0:T(8,128)(2,1)S(1)} %maximum_select_fusion.3), channel_id=1, source_target_pairs={{0,3},{1,0},{2,1},{3,2},{4,7},{5,4},{6,5},{7,6},{8,11},{9,8},{10,9... | collective-permute-start | bytes 393224 | tf_op jit(solution)/shard_map/ppermute | solution.py:36
  18.1 12.5 %collective-permute-done.1 = bf16[32,2048]{1,0:T(8,128)(2,1)S(1)} collective-permute-done((bf16[32,2048]{1,0:T(8,128)(2,1)S(1)}, bf16[32,2048]{1,0:T(8,128)(2,1)S(1)}, u32[]{:S(2)}, u32[]{:S(2)}) %collective-permute-start.1) | collective-permute-done | bytes 131104 | tf_op jit(solution)/shard_map/ppermute | solution.py:36
  30.6 4.1 %collective-permute-start.28 = (bf16[64,4096]{1,0:T(8,128)(2,1)S(1)}, bf16[64,4096]{1,0:T(8,128)(2,1)}, u32[]{:S(2)}, u32[]{:S(2)}) collective-permute-start(bf16[64,4096]{1,0:T(8,128)(2,1)S(1)} %get-tuple-element.31), channel_id=1, source_target_pairs={{0,1},{1,2},{2,3},{4,5},{5,6},{6,7},{8,9},{9,10},{10,11},{12,13},{... | collective-permute-start | bytes 1572872 | tf_op jit(solution)/shard_map/ppermute | solution.py:44
  34.8 4.0 %collective-permute-done.2 = bf16[32,2048]{1,0:T(8,128)(2,1)S(1)} collective-permute-done((bf16[32,2048]{1,0:T(8,128)(2,1)S(1)}, bf16[32,2048]{1,0:T(8,128)(2,1)S(1)}, u32[]{:S(2)}, u32[]{:S(2)}) %collective-permute-start.2) | collective-permute-done | bytes 131104 | tf_op jit(solution)/shard_map/ppermute | solution.py:36
  38.8 1.3 collective-permute-start.27
  40.1 1.7 convolution_bitcast_fusion
  41.9 1.3 convolution_bitcast_fusion.1
  43.2 1.3 convolution_bitcast_fusion.2
  45.5 1.5 collective-permute-start.10
  47.0 1.3 collective-permute-start.12
  48.3 1.5 collective-permute-start.29
  49.8 4.3 %collective-permute-done.27 = bf16[64,4096]{1,0:T(8,128)(2,1)} collective-permute-done((bf16[64,4096]{1,0:T(8,128)(2,1)S(1)}, bf16[64,4096]{1,0:T(8,128)(2,1)}, u32[]{:S(2)}, u32[]{:S(2)}) %collective-permute-start.27) | collective-permute-done | bytes 524320 | tf_op jit(solution)/shard_map/ppermute | solution.py:45
  57.2 1.3 convolution_convert_fusion.1
  59.2 6.1 %collective-permute-done.12 = bf16[64,4096]{1,0:T(8,128)(2,1)} collective-permute-done((bf16[64,4096]{1,0:T(8,128)(2,1)}, bf16[64,4096]{1,0:T(8,128)(2,1)}, u32[]{:S(2)}, u32[]{:S(2)}) %collective-permute-start.12) | collective-permute-done | bytes 524320 | tf_op jit(solution)/shard_map/ppermute | solution.py:45
  68.5 8.1 %collective-permute-done.31 = bf16[64,4096]{1,0:T(8,128)(2,1)} collective-permute-done((bf16[64,4096]{1,0:T(8,128)(2,1)}, bf16[64,4096]{1,0:T(8,128)(2,1)}, u32[]{:S(2)}, u32[]{:S(2)}) %collective-permute-start.31) | collective-permute-done | bytes 524320 | tf_op jit(solution)/shard_map/ppermute | solution.py:45
  80.1 7.6 %collective-permute-done.13 = bf16[64,4096]{1,0:T(8,128)(2,1)S(1)} collective-permute-done((bf16[64,4096]{1,0:T(8,128)(2,1)}, bf16[64,4096]{1,0:T(8,128)(2,1)S(1)}, u32[]{:S(2)}, u32[]{:S(2)}) %collective-permute-start.13) | collective-permute-done | bytes 524320 | tf_op jit(solution)/shard_map/ppermute | solution.py:45
  87.8 1.5 pad_maximum_fusion.xa_ref
  90.4 8.4 %collective-permute-done.32 = bf16[64,4096]{1,0:T(8,128)(2,1)S(1)} collective-permute-done((bf16[64,4096]{1,0:T(8,128)(2,1)}, bf16[64,4096]{1,0:T(8,128)(2,1)S(1)}, u32[]{:S(2)}, u32[]{:S(2)}) %collective-permute-start.32) | collective-permute-done | bytes 524320 | tf_op jit(solution)/shard_map/ppermute | solution.py:45
  98.9 1.6 pad_maximum_fusion.1.xa_ref
  101.5 2.9 collective-permute-start.7
  104.4 4.4 %collective-permute-done.5 = bf16[32,2048]{1,0:T(8,128)(2,1)S(1)} collective-permute-done((bf16[32,2048]{1,0:T(8,128)(2,1)S(1)}, bf16[32,2048]{1,0:T(8,128)(2,1)S(1)}, u32[]{:S(2)}, u32[]{:S(2)}) %collective-permute-start.5) | collective-permute-done | bytes 131104 | tf_op jit(solution)/shard_map/ppermute | solution.py:75
  108.8 5.2 %collective-permute-done.6 = bf16[32,2048]{1,0:T(8,128)(2,1)S(1)} collective-permute-done((bf16[32,2048]{1,0:T(8,128)(2,1)S(1)}, bf16[32,2048]{1,0:T(8,128)(2,1)S(1)}, u32[]{:S(2)}, u32[]{:S(2)}) %collective-permute-start.6) | collective-permute-done | bytes 131104 | tf_op jit(solution)/shard_map/ppermute | solution.py:75
  114.1 22.6 %ffn.2 = (bf16[256,4096]{1,0:T(8,128)(2,1)S(1)}, bf16[256,4096]{1,0:T(8,128)(2,1)S(1)}) custom-call(bf16[256,4096]{1,0:T(8,128)(2,1)} %pad_maximum_fusion.xa_ref, bf16[256,4096]{1,0:T(8,128)(2,1)} %collective-permute-done.14.xb_ref, bf16[4096,1024]{1,0:T(8,128)(2,1)} %gate_ref.3, bf16[4096,1024]{1,0:T(8,128)(2,1)} %up_ref.3, bf16[1024,4096]{1,0:T(8,128)(2,1)} %down_ref.3), custom_call_target="tpu_custom_call" | custom-call | flops 12884901888 | bytes 25165824 | tf_op jit(solution)/shard_map/ffn/pallas_call | solution.py:145
  136.8 22.7 %ffn.3 = (bf16[256,4096]{1,0:T(8,128)(2,1)S(1)}, bf16[256,4096]{1,0:T(8,128)(2,1)S(1)}) custom-call(bf16[256,4096]{1,0:T(8,128)(2,1)} %pad_maximum_fusion.1.xa_ref, bf16[256,4096]{1,0:T(8,128)(2,1)} %collective-permute-done.33.xb_ref, bf16[4096,1024]{1,0:T(8,128)(2,1)} %gate_ref.3, bf16[4096,1024]{1,0:T(8,128)(2,1)} %up_ref.3, bf16[1024,4096]{1,0:T(8,128)(2,1)} %down_ref.3), custom_call_target="tpu_custom_call" | custom-call | flops 12884901888 | bytes 25165824 | tf_op jit(solution)/shard_map/ffn/pallas_call | solution.py:145
  161.0 6.0 %collective-permute-done.23 = bf16[16,2048]{1,0:T(8,128)(2,1)S(1)} collective-permute-done((bf16[16,2048]{1,0:T(8,128)(2,1)S(1)}, bf16[16,2048]{1,0:T(8,128)(2,1)S(1)}, u32[]{:S(2)}, u32[]{:S(2)}) %collective-permute-start.23) | collective-permute-done | bytes 65568 | tf_op jit(solution)/shard_map/ppermute | solution.py:30
  167.0 2.6 collective-permute-start.24
  169.6 1.7 collective-permute-start.25
  171.6 2.3 collective-permute-done.24
  173.9 9.6 %collective-permute-done.25 = bf16[32,2048]{1,0:T(8,128)(2,1)S(1)} collective-permute-done((bf16[32,2048]{1,0:T(8,128)(2,1)S(1)}, bf16[32,2048]{1,0:T(8,128)(2,1)S(1)}, u32[]{:S(2)}, u32[]{:S(2)}) %collective-permute-start.25) | collective-permute-done | bytes 131104 | tf_op jit(solution)/shard_map/ppermute | solution.py:36
  183.7 1.3 collective-permute-start.35
  185.2 1.3 collective-permute-start.16
  186.5 10.8 %collective-permute-done.35 = bf16[64,4096]{1,0:T(8,128)(2,1)S(1)} collective-permute-done((bf16[64,4096]{1,0:T(8,128)(2,1)S(1)}, bf16[64,4096]{1,0:T(8,128)(2,1)S(1)}, u32[]{:S(2)}, u32[]{:S(2)}) %collective-permute-start.35) | collective-permute-done | bytes 524320 | tf_op jit(solution)/shard_map/ppermute | solution.py:63
  197.5 4.4 %collective-permute-start.36 = (bf16[64,4096]{1,0:T(8,128)(2,1)S(1)}, bf16[64,4096]{1,0:T(8,128)(2,1)S(1)}, u32[]{:S(2)}, u32[]{:S(2)}) collective-permute-start(bf16[64,4096]{1,0:T(8,128)(2,1)S(1)} %add_convert_fusion.4), channel_id=1, source_target_pairs={{0,1},{1,2},{4,5},{5,6},{8,9},{9,10},{12,13},{13,14},{16,17},{17,1... | collective-permute-start | bytes 1572872 | tf_op jit(solution)/shard_map/ppermute | solution.py:63
  201.9 6.6 %collective-permute-done.16 = bf16[64,4096]{1,0:T(8,128)(2,1)S(1)} collective-permute-done((bf16[64,4096]{1,0:T(8,128)(2,1)S(1)}, bf16[64,4096]{1,0:T(8,128)(2,1)S(1)}, u32[]{:S(2)}, u32[]{:S(2)}) %collective-permute-start.16) | collective-permute-done | bytes 524320 | tf_op jit(solution)/shard_map/ppermute | solution.py:63
  208.7 4.6 %collective-permute-start.17 = (bf16[64,4096]{1,0:T(8,128)(2,1)S(1)}, bf16[64,4096]{1,0:T(8,128)(2,1)S(1)}, u32[]{:S(2)}, u32[]{:S(2)}) collective-permute-start(bf16[64,4096]{1,0:T(8,128)(2,1)S(1)} %add_convert_fusion.9), channel_id=1, source_target_pairs={{0,1},{1,2},{4,5},{5,6},{8,9},{9,10},{12,13},{13,14},{16,17},{17,1... | collective-permute-start | bytes 1572872 | tf_op jit(solution)/shard_map/ppermute | solution.py:63
  213.3 6.4 %collective-permute-done.36 = bf16[64,4096]{1,0:T(8,128)(2,1)S(1)} collective-permute-done((bf16[64,4096]{1,0:T(8,128)(2,1)S(1)}, bf16[64,4096]{1,0:T(8,128)(2,1)S(1)}, u32[]{:S(2)}, u32[]{:S(2)}) %collective-permute-start.36) | collective-permute-done | bytes 524320 | tf_op jit(solution)/shard_map/ppermute | solution.py:63
  220.7 4.4 %collective-permute-start.37 = (bf16[64,4096]{1,0:T(8,128)(2,1)S(1)}, bf16[64,4096]{1,0:T(8,128)(2,1)S(1)}, u32[]{:S(2)}, u32[]{:S(2)}) collective-permute-start(bf16[64,4096]{1,0:T(8,128)(2,1)S(1)} %get-tuple-element.26), channel_id=1, source_target_pairs={{0,1},{1,2},{2,3},{4,5},{5,6},{6,7},{8,9},{9,10},{10,11},{12,13},{... | collective-permute-start | bytes 1572872 | tf_op jit(solution)/shard_map/ppermute | solution.py:63
  225.1 5.9 %collective-permute-done.17 = bf16[64,4096]{1,0:T(8,128)(2,1)S(1)} collective-permute-done((bf16[64,4096]{1,0:T(8,128)(2,1)S(1)}, bf16[64,4096]{1,0:T(8,128)(2,1)S(1)}, u32[]{:S(2)}, u32[]{:S(2)}) %collective-permute-start.17) | collective-permute-done | bytes 524320 | tf_op jit(solution)/shard_map/ppermute | solution.py:63
  231.9 4.4 %collective-permute-start.18 = (bf16[64,4096]{1,0:T(8,128)(2,1)S(1)}, bf16[64,4096]{1,0:T(8,128)(2,1)S(1)}, u32[]{:S(2)}, u32[]{:S(2)}) collective-permute-start(bf16[64,4096]{1,0:T(8,128)(2,1)S(1)} %get-tuple-element.24), channel_id=1, source_target_pairs={{0,1},{1,2},{2,3},{4,5},{5,6},{6,7},{8,9},{9,10},{10,11},{12,13},{... | collective-permute-start | bytes 1572872 | tf_op jit(solution)/shard_map/ppermute | solution.py:63
  238.6 1.3 collective-permute-start.40
  240.1 1.3 collective-permute-start.21
  243.3 9.0 %collective-permute-done.18 = bf16[64,4096]{1,0:T(8,128)(2,1)S(1)} collective-permute-done((bf16[64,4096]{1,0:T(8,128)(2,1)S(1)}, bf16[64,4096]{1,0:T(8,128)(2,1)S(1)}, u32[]{:S(2)}, u32[]{:S(2)}) %collective-permute-start.18) | collective-permute-done | bytes 524320 | tf_op jit(solution)/shard_map/ppermute | solution.py:63
  252.3 11.6 %collective-permute-done.40 = bf16[64,4096]{1,0:T(8,128)(2,1)S(1)} collective-permute-done((bf16[64,4096]{1,0:T(8,128)(2,1)S(1)}, bf16[64,4096]{1,0:T(8,128)(2,1)S(1)}, u32[]{:S(2)}, u32[]{:S(2)}) %collective-permute-start.40) | collective-permute-done | bytes 524320 | tf_op jit(solution)/shard_map/ppermute | solution.py:64
  263.9 9.9 %collective-permute-done.21 = bf16[64,4096]{1,0:T(8,128)(2,1)S(1)} collective-permute-done((bf16[64,4096]{1,0:T(8,128)(2,1)S(1)}, bf16[64,4096]{1,0:T(8,128)(2,1)S(1)}, u32[]{:S(2)}, u32[]{:S(2)}) %collective-permute-start.21) | collective-permute-done | bytes 524320 | tf_op jit(solution)/shard_map/ppermute | solution.py:64
  273.8 1.3 fusion.12
  275.5 11.9 %collective-permute-start.43 = (bf16[64,4096]{1,0:T(8,128)(2,1)S(1)}, bf16[64,4096]{1,0:T(8,128)(2,1)S(1)}, u32[]{:S(2)}, u32[]{:S(2)}) collective-permute-start(bf16[64,4096]{1,0:T(8,128)(2,1)S(1)} %get-tuple-element.51), channel_id=1, source_target_pairs={{0,1},{1,2},{2,3},{4,5},{5,6},{6,7},{8,9},{9,10},{10,11},{12,13},{... | collective-permute-start | bytes 1572872 | tf_op jit(solution)/shard_map/ppermute | solution.py:44
  287.4 1.3 collective-permute-start.42
  288.8 4.7 %collective-permute-start.50 = (bf16[64,4096]{1,0:T(8,128)(2,1)S(1)}, bf16[64,4096]{1,0:T(8,128)(2,1)S(1)}, u32[]{:S(2)}, u32[]{:S(2)}) collective-permute-start(bf16[64,4096]{1,0:T(8,128)(2,1)S(1)} %get-tuple-element.52), channel_id=1, source_target_pairs={{0,1},{1,2},{2,3},{4,5},{5,6},{6,7},{8,9},{9,10},{10,11},{12,13},{... | collective-permute-start | bytes 1572872 | tf_op jit(solution)/shard_map/ppermute | solution.py:44
  293.5 1.3 collective-permute-start.49
  294.8 5.0 %collective-permute-done.43 = bf16[64,4096]{1,0:T(8,128)(2,1)S(1)} collective-permute-done((bf16[64,4096]{1,0:T(8,128)(2,1)S(1)}, bf16[64,4096]{1,0:T(8,128)(2,1)S(1)}, u32[]{:S(2)}, u32[]{:S(2)}) %collective-permute-start.43) | collective-permute-done | bytes 524320 | tf_op jit(solution)/shard_map/ppermute | solution.py:44
  300.5 3.7 collective-permute-done.42
  305.5 1.4 collective-permute-done.50
  309.1 6.3 %collective-permute-done.49 = bf16[64,4096]{1,0:T(8,128)(2,1)S(1)} collective-permute-done((bf16[64,4096]{1,0:T(8,128)(2,1)S(1)}, bf16[64,4096]{1,0:T(8,128)(2,1)S(1)}, u32[]{:S(2)}, u32[]{:S(2)}) %collective-permute-start.49) | collective-permute-done | bytes 524320 | tf_op jit(solution)/shard_map/ppermute | solution.py:45
  317.4 6.8 %collective-permute-done.46 = bf16[64,4096]{1,0:T(8,128)(2,1)S(1)} collective-permute-done((bf16[64,4096]{1,0:T(8,128)(2,1)S(1)}, bf16[64,4096]{1,0:T(8,128)(2,1)S(1)}, u32[]{:S(2)}, u32[]{:S(2)}) %collective-permute-start.46) | collective-permute-done | bytes 524320 | tf_op jit(solution)/shard_map/ppermute | solution.py:45
  326.3 9.2 %collective-permute-done.53 = bf16[64,4096]{1,0:T(8,128)(2,1)S(1)} collective-permute-done((bf16[64,4096]{1,0:T(8,128)(2,1)S(1)}, bf16[64,4096]{1,0:T(8,128)(2,1)S(1)}, u32[]{:S(2)}, u32[]{:S(2)}) %collective-permute-start.53) | collective-permute-done | bytes 524320 | tf_op jit(solution)/shard_map/ppermute | solution.py:45
  335.5 1.3 collective-permute-start.54
  336.9 9.8 %collective-permute-done.47 = bf16[64,4096]{1,0:T(8,128)(2,1)S(1)} collective-permute-done((bf16[64,4096]{1,0:T(8,128)(2,1)S(1)}, bf16[64,4096]{1,0:T(8,128)(2,1)S(1)}, u32[]{:S(2)}, u32[]{:S(2)}) %collective-permute-start.47) | collective-permute-done | bytes 524320 | tf_op jit(solution)/shard_map/ppermute | solution.py:45
  348.3 7.7 %collective-permute-done.54 = bf16[64,4096]{1,0:T(8,128)(2,1)S(1)} collective-permute-done((bf16[64,4096]{1,0:T(8,128)(2,1)S(1)}, bf16[64,4096]{1,0:T(8,128)(2,1)S(1)}, u32[]{:S(2)}, u32[]{:S(2)}) %collective-permute-start.54) | collective-permute-done | bytes 524320 | tf_op jit(solution)/shard_map/ppermute | solution.py:45
  358.5 1.5 collective-permute-done.55
  360.6 3.7 collective-permute-start.58
  364.5 4.2 %collective-permute-done.56 = bf16[32,2048]{1,0:T(8,128)(2,1)S(1)} collective-permute-done((bf16[32,2048]{1,0:T(8,128)(2,1)S(1)}, bf16[32,2048]{1,0:T(8,128)(2,1)S(1)}, u32[]{:S(2)}, u32[]{:S(2)}) %collective-permute-start.56) | collective-permute-done | bytes 131104 | tf_op jit(solution)/shard_map/ppermute | solution.py:75
  368.8 4.7 %collective-permute-done.57 = bf16[32,2048]{1,0:T(8,128)(2,1)S(1)} collective-permute-done((bf16[32,2048]{1,0:T(8,128)(2,1)S(1)}, bf16[32,2048]{1,0:T(8,128)(2,1)S(1)}, u32[]{:S(2)}, u32[]{:S(2)}) %collective-permute-start.57) | collective-permute-done | bytes 131104 | tf_op jit(solution)/shard_map/ppermute | solution.py:75
  (186 shorter events, 43.7 us)
Async XLA Ops:
  0.6 56.5 %copy-start = (bf16[256,2048]{1,0:T(8,128)(2,1)S(1)}, bf16[256,2048]{1,0:T(8,128)(2,1)}, u32[]{:S(2)}) copy-start(bf16[256,2048]{1,0:T(8,128)(2,1)} %param.26) | copy-start | bytes 3145732
  2.9 9.8 %collective-permute-start = (bf16[16,2048]{1,0:T(8,128)(2,1)S(1)}, bf16[16,2048]{1,0:T(8,128)(2,1)S(1)}, u32[]{:S(2)}, u32[]{:S(2)}) collective-permute-start(bf16[16,2048]{1,0:T(8,128)(2,1)S(1)} %get-tuple-element.50), channel_id=1, source_target_pairs={{0,4},{4,0},{1,5},{5,1},{2,6},{6,2},{3,7},{7,3},{8,12},{12,8},{9,1... | collective-permute-start | bytes 196616 | tf_op jit(solution)/shard_map/ppermute | solution.py:30
  6.1 37.1 %copy-start.4 = (bf16[64,4096]{1,0:T(8,128)(2,1)}, bf16[64,4096]{1,0:T(8,128)(2,1)S(1)}, u32[]{:S(2)}) copy-start(bf16[64,4096]{1,0:T(8,128)(2,1)S(1)} %get-tuple-element.30) | copy-start | bytes 1572868
  6.1 39.4 %collective-permute-start.9 = (bf16[64,4096]{1,0:T(8,128)(2,1)S(1)}, bf16[64,4096]{1,0:T(8,128)(2,1)}, u32[]{:S(2)}, u32[]{:S(2)}) collective-permute-start(bf16[64,4096]{1,0:T(8,128)(2,1)S(1)} %get-tuple-element.30), channel_id=1, source_target_pairs={{0,1},{1,2},{2,3},{4,5},{5,6},{6,7},{8,9},{9,10},{10,11},{12,13},{... | collective-permute-start | bytes 1572872 | tf_op jit(solution)/shard_map/ppermute | solution.py:44
  11.4 35.6 %collective-permute-start.8 = (bf16[64,4096]{1,0:T(8,128)(2,1)S(1)}, bf16[64,4096]{1,0:T(8,128)(2,1)}, u32[]{:S(2)}, u32[]{:S(2)}) collective-permute-start(bf16[64,4096]{1,0:T(8,128)(2,1)S(1)} %get-tuple-element.30), channel_id=1, source_target_pairs={{1,0},{2,1},{3,2},{5,4},{6,5},{7,6},{9,8},{10,9},{11,10},{13,12},{... | collective-permute-start | bytes 1572872 | tf_op jit(solution)/shard_map/ppermute | solution.py:45
  12.8 29.1 %copy-start.11 = (bf16[32,2048]{1,0:T(8,128)(2,1)}, bf16[32,2048]{1,0:T(8,128)(2,1)S(1)}, u32[]{:S(2)}) copy-start(bf16[32,2048]{1,0:T(8,128)(2,1)S(1)} %maximum_select_fusion.3) | copy-start | bytes 393220
  12.8 17.9 %collective-permute-start.1 = (bf16[32,2048]{1,0:T(8,128)(2,1)S(1)}, bf16[32,2048]{1,0:T(8,128)(2,1)S(1)}, u32[]{:S(2)}, u32[]{:S(2)}) collective-permute-start(bf16[32,2048]{1,0:T(8,128)(2,1)S(1)} %maximum_select_fusion.3), channel_id=1, source_target_pairs={{0,3},{1,0},{2,1},{3,2},{4,7},{5,4},{6,5},{7,6},{8,11},{9,8},{10,9... | collective-permute-start | bytes 393224 | tf_op jit(solution)/shard_map/ppermute | solution.py:36
  17.5 21.3 %collective-permute-start.2 = (bf16[32,2048]{1,0:T(8,128)(2,1)S(1)}, bf16[32,2048]{1,0:T(8,128)(2,1)S(1)}, u32[]{:S(2)}, u32[]{:S(2)}) collective-permute-start(bf16[32,2048]{1,0:T(8,128)(2,1)S(1)} %maximum_select_fusion.3), channel_id=1, source_target_pairs={{0,2},{1,3},{2,0},{3,1},{4,6},{5,7},{6,4},{7,5},{8,10},{9,11},{10,... | collective-permute-start | bytes 393224 | tf_op jit(solution)/shard_map/ppermute | solution.py:36
  17.5 22.6 %collective-permute-start.3 = (bf16[32,2048]{1,0:T(8,128)(2,1)S(1)}, bf16[32,2048]{1,0:T(8,128)(2,1)}, u32[]{:S(2)}, u32[]{:S(2)}) collective-permute-start(bf16[32,2048]{1,0:T(8,128)(2,1)S(1)} %maximum_select_fusion.3), channel_id=1, source_target_pairs={{0,1},{1,2},{2,3},{3,0},{4,5},{5,6},{6,7},{7,4},{8,9},{9,10},{10,1... | collective-permute-start | bytes 393224 | tf_op jit(solution)/shard_map/ppermute | solution.py:36
  30.6 17.7 %collective-permute-start.28 = (bf16[64,4096]{1,0:T(8,128)(2,1)S(1)}, bf16[64,4096]{1,0:T(8,128)(2,1)}, u32[]{:S(2)}, u32[]{:S(2)}) collective-permute-start(bf16[64,4096]{1,0:T(8,128)(2,1)S(1)} %get-tuple-element.31), channel_id=1, source_target_pairs={{0,1},{1,2},{2,3},{4,5},{5,6},{6,7},{8,9},{9,10},{10,11},{12,13},{... | collective-permute-start | bytes 1572872 | tf_op jit(solution)/shard_map/ppermute | solution.py:44
  38.8 15.3 %collective-permute-start.27 = (bf16[64,4096]{1,0:T(8,128)(2,1)S(1)}, bf16[64,4096]{1,0:T(8,128)(2,1)}, u32[]{:S(2)}, u32[]{:S(2)}) collective-permute-start(bf16[64,4096]{1,0:T(8,128)(2,1)S(1)} %get-tuple-element.31), channel_id=1, source_target_pairs={{1,0},{2,1},{3,2},{5,4},{6,5},{7,6},{9,8},{10,9},{11,10},{13,12},{... | collective-permute-start | bytes 1572872 | tf_op jit(solution)/shard_map/ppermute | solution.py:45
  45.3 10.1 %collective-permute-start.4 = (f32[3,128,256]{2,1,0:T(8,128)}, f32[3,128,256]{2,1,0:T(8,128)}, u32[]{:S(2)}, u32[]{:S(2)}) collective-permute-start(f32[3,128,256]{2,1,0:T(8,128)} %pad_maximum_fusion.7), channel_id=1, source_target_pairs={{0,4},{4,0},{1,5},{5,1},{2,6},{6,2},{3,7},{7,3},{8,12},{12,8},{9,1... | collective-permute-start | bytes 1179656 | tf_op jit(solution)/shard_map/ppermute | solution.py:30
  45.5 12.9 %collective-permute-start.10 = (bf16[64,4096]{1,0:T(8,128)(2,1)}, bf16[64,4096]{1,0:T(8,128)(2,1)}, u32[]{:S(2)}, u32[]{:S(2)}) collective-permute-start(bf16[64,4096]{1,0:T(8,128)(2,1)} %collective-permute-done.9), channel_id=1, source_target_pairs={{1,2},{2,3},{5,6},{6,7},{9,10},{10,11},{13,14},{14,15},{17,18},{18... | collective-permute-start | bytes 1572872 | tf_op jit(solution)/shard_map/ppermute | solution.py:44
  47.0 18.3 %collective-permute-start.12 = (bf16[64,4096]{1,0:T(8,128)(2,1)}, bf16[64,4096]{1,0:T(8,128)(2,1)}, u32[]{:S(2)}, u32[]{:S(2)}) collective-permute-start(bf16[64,4096]{1,0:T(8,128)(2,1)} %collective-permute-done.8), channel_id=1, source_target_pairs={{1,0},{2,1},{5,4},{6,5},{9,8},{10,9},{13,12},{14,13},{17,16},{18,1... | collective-permute-start | bytes 1572872 | tf_op jit(solution)/shard_map/ppermute | solution.py:45
  48.3 18.3 %collective-permute-start.29 = (bf16[64,4096]{1,0:T(8,128)(2,1)}, bf16[64,4096]{1,0:T(8,128)(2,1)}, u32[]{:S(2)}, u32[]{:S(2)}) collective-permute-start(bf16[64,4096]{1,0:T(8,128)(2,1)} %collective-permute-done.28), channel_id=1, source_target_pairs={{1,2},{2,3},{5,6},{6,7},{9,10},{10,11},{13,14},{14,15},{17,18},{18... | collective-permute-start | bytes 1572872 | tf_op jit(solution)/shard_map/ppermute | solution.py:44
  54.1 22.5 %collective-permute-start.31 = (bf16[64,4096]{1,0:T(8,128)(2,1)}, bf16[64,4096]{1,0:T(8,128)(2,1)}, u32[]{:S(2)}, u32[]{:S(2)}) collective-permute-start(bf16[64,4096]{1,0:T(8,128)(2,1)} %collective-permute-done.27), channel_id=1, source_target_pairs={{1,0},{2,1},{5,4},{6,5},{9,8},{10,9},{13,12},{14,13},{17,16},{18,1... | collective-permute-start | bytes 1572872 | tf_op jit(solution)/shard_map/ppermute | solution.py:45
  58.5 20.5 %collective-permute-start.11 = (bf16[64,4096]{1,0:T(8,128)(2,1)}, bf16[64,4096]{1,0:T(8,128)(2,1)S(1)}, u32[]{:S(2)}, u32[]{:S(2)}) collective-permute-start(bf16[64,4096]{1,0:T(8,128)(2,1)} %collective-permute-done.10), channel_id=1, source_target_pairs={{2,3},{6,7},{10,11},{14,15},{18,19},{22,23},{26,27},{30,31}} | collective-permute-start | bytes 1572872 | tf_op jit(solution)/shard_map/ppermute | solution.py:44
  65.3 22.4 %collective-permute-start.13 = (bf16[64,4096]{1,0:T(8,128)(2,1)}, bf16[64,4096]{1,0:T(8,128)(2,1)S(1)}, u32[]{:S(2)}, u32[]{:S(2)}) collective-permute-start(bf16[64,4096]{1,0:T(8,128)(2,1)} %collective-permute-done.12), channel_id=1, source_target_pairs={{1,0},{5,4},{9,8},{13,12},{17,16},{21,20},{25,24},{29,28}} | collective-permute-start | bytes 1572872 | tf_op jit(solution)/shard_map/ppermute | solution.py:45
  66.6 22.7 %collective-permute-start.30 = (bf16[64,4096]{1,0:T(8,128)(2,1)}, bf16[64,4096]{1,0:T(8,128)(2,1)S(1)}, u32[]{:S(2)}, u32[]{:S(2)}) collective-permute-start(bf16[64,4096]{1,0:T(8,128)(2,1)} %collective-permute-done.29), channel_id=1, source_target_pairs={{2,3},{6,7},{10,11},{14,15},{18,19},{22,23},{26,27},{30,31}} | collective-permute-start | bytes 1572872 | tf_op jit(solution)/shard_map/ppermute | solution.py:44
  76.6 22.3 %collective-permute-start.32 = (bf16[64,4096]{1,0:T(8,128)(2,1)}, bf16[64,4096]{1,0:T(8,128)(2,1)S(1)}, u32[]{:S(2)}, u32[]{:S(2)}) collective-permute-start(bf16[64,4096]{1,0:T(8,128)(2,1)} %collective-permute-done.31), channel_id=1, source_target_pairs={{1,0},{5,4},{9,8},{13,12},{17,16},{21,20},{25,24},{29,28}} | collective-permute-start | bytes 1572872 | tf_op jit(solution)/shard_map/ppermute | solution.py:45
  89.3 24.8 %collective-permute-start.14 = (bf16[256,4096]{1,0:T(8,128)(2,1)}, bf16[256,4096]{1,0:T(8,128)(2,1)}, u32[]{:S(2)}, u32[]{:S(2)}) collective-permute-start(bf16[256,4096]{1,0:T(8,128)(2,1)} %pad_maximum_fusion.xa_ref), channel_id=1, source_target_pairs={{0,4},{4,0},{1,5},{5,1},{2,6},{6,2},{3,7},{7,3},{8,12},{12,8},{9,1... | collective-permute-start | bytes 6291464 | tf_op jit(solution)/shard_map/ppermute | solution.py:30
  100.5 36.3 %collective-permute-start.33 = (bf16[256,4096]{1,0:T(8,128)(2,1)}, bf16[256,4096]{1,0:T(8,128)(2,1)}, u32[]{:S(2)}, u32[]{:S(2)}) collective-permute-start(bf16[256,4096]{1,0:T(8,128)(2,1)} %pad_maximum_fusion.1.xa_ref), channel_id=1, source_target_pairs={{0,4},{4,0},{1,5},{5,1},{2,6},{6,2},{3,7},{7,3},{8,12},{12,8},{9,1... | collective-permute-start | bytes 6291464 | tf_op jit(solution)/shard_map/ppermute | solution.py:30
  100.5 8.3 %collective-permute-start.5 = (bf16[32,2048]{1,0:T(8,128)(2,1)S(1)}, bf16[32,2048]{1,0:T(8,128)(2,1)S(1)}, u32[]{:S(2)}, u32[]{:S(2)}) collective-permute-start(bf16[32,2048]{1,0:T(8,128)(2,1)S(1)} %get-tuple-element.37), channel_id=1, source_target_pairs={{0,1},{1,2},{2,3},{3,0},{4,5},{5,6},{6,7},{7,4},{8,9},{9,10},{10,1... | collective-permute-start | bytes 393224 | tf_op jit(solution)/shard_map/ppermute | solution.py:75
  101.3 12.7 %collective-permute-start.6 = (bf16[32,2048]{1,0:T(8,128)(2,1)S(1)}, bf16[32,2048]{1,0:T(8,128)(2,1)S(1)}, u32[]{:S(2)}, u32[]{:S(2)}) collective-permute-start(bf16[32,2048]{1,0:T(8,128)(2,1)S(1)} %get-tuple-element.39), channel_id=1, source_target_pairs={{0,2},{1,3},{2,0},{3,1},{4,6},{5,7},{6,4},{7,5},{8,10},{9,11},{10,... | collective-permute-start | bytes 393224 | tf_op jit(solution)/shard_map/ppermute | solution.py:75
  101.5 12.5 %collective-permute-start.7 = (bf16[32,2048]{1,0:T(8,128)(2,1)S(1)}, bf16[32,2048]{1,0:T(8,128)(2,1)S(1)}, u32[]{:S(2)}, u32[]{:S(2)}) collective-permute-start(bf16[32,2048]{1,0:T(8,128)(2,1)S(1)} %get-tuple-element.38), channel_id=1, source_target_pairs={{0,3},{1,0},{2,1},{3,2},{4,7},{5,4},{6,5},{7,6},{8,11},{9,8},{10,9... | collective-permute-start | bytes 393224 | tf_op jit(solution)/shard_map/ppermute | solution.py:75
  136.7 23.4 %collective-permute-start.22 = (f32[16,2048]{1,0:T(8,128)S(1)}, f32[16,2048]{1,0:T(8,128)S(1)}, u32[]{:S(2)}, u32[]{:S(2)}) collective-permute-start(f32[16,2048]{1,0:T(8,128)S(1)} %get-tuple-element.45), channel_id=1, source_target_pairs={{0,4},{4,0},{1,5},{5,1},{2,6},{6,2},{3,7},{7,3},{8,12},{12,8},{9,1... | collective-permute-start | bytes 393224 | tf_op jit(solution)/shard_map/ppermute | solution.py:30
  136.8 34.5 %copy-start.3 = (bf16[2048,2,256]{2,1,0:T(2,128)(2,1)S(1)}, bf16[2048,2,256]{2,1,0:T(2,128)(2,1)}, u32[]{:S(2)}) copy-start(bf16[2048,2,256]{2,1,0:T(2,128)(2,1)} %param.29) | copy-start | bytes 6291460
  159.6 24.0 %collective-permute-start.34 = (bf16[256,4096]{1,0:T(8,128)(2,1)S(1)}, bf16[256,4096]{1,0:T(8,128)(2,1)S(1)}, u32[]{:S(2)}, u32[]{:S(2)}) collective-permute-start(bf16[256,4096]{1,0:T(8,128)(2,1)S(1)} %get-tuple-element.16), channel_id=1, source_target_pairs={{0,4},{4,0},{1,5},{5,1},{2,6},{6,2},{3,7},{7,3},{8,12},{12,8},{9,1... | collective-permute-start | bytes 6291464 | tf_op jit(solution)/shard_map/ppermute | solution.py:30
  160.1 24.9 %collective-permute-start.15 = (bf16[256,4096]{1,0:T(8,128)(2,1)S(1)}, bf16[256,4096]{1,0:T(8,128)(2,1)S(1)}, u32[]{:S(2)}, u32[]{:S(2)}) collective-permute-start(bf16[256,4096]{1,0:T(8,128)(2,1)S(1)} %get-tuple-element.12), channel_id=1, source_target_pairs={{0,4},{4,0},{1,5},{5,1},{2,6},{6,2},{3,7},{7,3},{8,12},{12,8},{9,1... | collective-permute-start | bytes 6291464 | tf_op jit(solution)/shard_map/ppermute | solution.py:30
  160.5 6.5 %collective-permute-start.23 = (bf16[16,2048]{1,0:T(8,128)(2,1)S(1)}, bf16[16,2048]{1,0:T(8,128)(2,1)S(1)}, u32[]{:S(2)}, u32[]{:S(2)}) collective-permute-start(bf16[16,2048]{1,0:T(8,128)(2,1)S(1)} %get-tuple-element.48), channel_id=1, source_target_pairs={{0,4},{4,0},{1,5},{5,1},{2,6},{6,2},{3,7},{7,3},{8,12},{12,8},{9,1... | collective-permute-start | bytes 196616 | tf_op jit(solution)/shard_map/ppermute | solution.py:30
  167.0 6.9 %collective-permute-start.24 = (bf16[32,2048]{1,0:T(8,128)(2,1)S(1)}, bf16[32,2048]{1,0:T(8,128)(2,1)S(1)}, u32[]{:S(2)}, u32[]{:S(2)}) collective-permute-start(bf16[32,2048]{1,0:T(8,128)(2,1)S(1)} %maximum_select_fusion.4), channel_id=1, source_target_pairs={{0,3},{1,0},{2,1},{3,2},{4,7},{5,4},{6,5},{7,6},{8,11},{9,8},{10,9... | collective-permute-start | bytes 393224 | tf_op jit(solution)/shard_map/ppermute | solution.py:36
  169.6 13.9 %collective-permute-start.25 = (bf16[32,2048]{1,0:T(8,128)(2,1)S(1)}, bf16[32,2048]{1,0:T(8,128)(2,1)S(1)}, u32[]{:S(2)}, u32[]{:S(2)}) collective-permute-start(bf16[32,2048]{1,0:T(8,128)(2,1)S(1)} %maximum_select_fusion.4), channel_id=1, source_target_pairs={{0,2},{1,3},{2,0},{3,1},{4,6},{5,7},{6,4},{7,5},{8,10},{9,11},{10,... | collective-permute-start | bytes 393224 | tf_op jit(solution)/shard_map/ppermute | solution.py:36
  171.3 12.2 %collective-permute-start.26 = (bf16[32,2048]{1,0:T(8,128)(2,1)S(1)}, bf16[32,2048]{1,0:T(8,128)(2,1)S(1)}, u32[]{:S(2)}, u32[]{:S(2)}) collective-permute-start(bf16[32,2048]{1,0:T(8,128)(2,1)S(1)} %maximum_select_fusion.4), channel_id=1, source_target_pairs={{0,1},{1,2},{2,3},{3,0},{4,5},{5,6},{6,7},{7,4},{8,9},{9,10},{10,1... | collective-permute-start | bytes 393224 | tf_op jit(solution)/shard_map/ppermute | solution.py:36
  173.9 133.7 %collective-permute-start.48 = (bf16[2,2048,256]{2,1,0:T(8,128)(2,1)S(1)}, bf16[2,2048,256]{2,1,0:T(8,128)(2,1)S(1)}, u32[]{:S(2)}, u32[]{:S(2)}) collective-permute-start(bf16[2,2048,256]{2,1,0:T(8,128)(2,1)S(1)} %bitcast.87), channel_id=1, source_target_pairs={{0,4},{4,0},{1,5},{5,1},{2,6},{6,2},{3,7},{7,3},{8,12},{12,8},{9,1... | collective-permute-start | bytes 6291464 | tf_op jit(solution)/shard_map/ppermute | solution.py:30
  183.7 13.6 %collective-permute-start.35 = (bf16[64,4096]{1,0:T(8,128)(2,1)S(1)}, bf16[64,4096]{1,0:T(8,128)(2,1)S(1)}, u32[]{:S(2)}, u32[]{:S(2)}) collective-permute-start(bf16[64,4096]{1,0:T(8,128)(2,1)S(1)} %fusion.21), channel_id=1, source_target_pairs={{0,1},{4,5},{8,9},{12,13},{16,17},{20,21},{24,25},{28,29}} | collective-permute-start | bytes 1572872 | tf_op jit(solution)/shard_map/ppermute | solution.py:63
  185.2 23.4 %collective-permute-start.16 = (bf16[64,4096]{1,0:T(8,128)(2,1)S(1)}, bf16[64,4096]{1,0:T(8,128)(2,1)S(1)}, u32[]{:S(2)}, u32[]{:S(2)}) collective-permute-start(bf16[64,4096]{1,0:T(8,128)(2,1)S(1)} %fusion.19), channel_id=1, source_target_pairs={{0,1},{4,5},{8,9},{12,13},{16,17},{20,21},{24,25},{28,29}} | collective-permute-start | bytes 1572872 | tf_op jit(solution)/shard_map/ppermute | solution.py:63
  197.5 22.3 %collective-permute-start.36 = (bf16[64,4096]{1,0:T(8,128)(2,1)S(1)}, bf16[64,4096]{1,0:T(8,128)(2,1)S(1)}, u32[]{:S(2)}, u32[]{:S(2)}) collective-permute-start(bf16[64,4096]{1,0:T(8,128)(2,1)S(1)} %add_convert_fusion.4), channel_id=1, source_target_pairs={{0,1},{1,2},{4,5},{5,6},{8,9},{9,10},{12,13},{13,14},{16,17},{17,1... | collective-permute-start | bytes 1572872 | tf_op jit(solution)/shard_map/ppermute | solution.py:63
  208.7 22.3 %collective-permute-start.17 = (bf16[64,4096]{1,0:T(8,128)(2,1)S(1)}, bf16[64,4096]{1,0:T(8,128)(2,1)S(1)}, u32[]{:S(2)}, u32[]{:S(2)}) collective-permute-start(bf16[64,4096]{1,0:T(8,128)(2,1)S(1)} %add_convert_fusion.9), channel_id=1, source_target_pairs={{0,1},{1,2},{4,5},{5,6},{8,9},{9,10},{12,13},{13,14},{16,17},{17,1... | collective-permute-start | bytes 1572872 | tf_op jit(solution)/shard_map/ppermute | solution.py:63
  220.0 16.4 %collective-permute-start.38 = (bf16[64,4096]{1,0:T(8,128)(2,1)S(1)}, bf16[64,4096]{1,0:T(8,128)(2,1)S(1)}, u32[]{:S(2)}, u32[]{:S(2)}) collective-permute-start(bf16[64,4096]{1,0:T(8,128)(2,1)S(1)} %get-tuple-element.27), channel_id=1, source_target_pairs={{3,2},{7,6},{11,10},{15,14},{19,18},{23,22},{27,26},{31,30}} | collective-permute-start | bytes 1572872 | tf_op jit(solution)/shard_map/ppermute | solution.py:64
  220.7 22.6 %collective-permute-start.37 = (bf16[64,4096]{1,0:T(8,128)(2,1)S(1)}, bf16[64,4096]{1,0:T(8,128)(2,1)S(1)}, u32[]{:S(2)}, u32[]{:S(2)}) collective-permute-start(bf16[64,4096]{1,0:T(8,128)(2,1)S(1)} %get-tuple-element.26), channel_id=1, source_target_pairs={{0,1},{1,2},{2,3},{4,5},{5,6},{6,7},{8,9},{9,10},{10,11},{12,13},{... | collective-permute-start | bytes 1572872 | tf_op jit(solution)/shard_map/ppermute | solution.py:63
  231.2 6.0 %collective-permute-start.19 = (bf16[64,4096]{1,0:T(8,128)(2,1)S(1)}, bf16[64,4096]{1,0:T(8,128)(2,1)S(1)}, u32[]{:S(2)}, u32[]{:S(2)}) collective-permute-start(bf16[64,4096]{1,0:T(8,128)(2,1)S(1)} %get-tuple-element.25), channel_id=1, source_target_pairs={{3,2},{7,6},{11,10},{15,14},{19,18},{23,22},{27,26},{31,30}} | collective-permute-start | bytes 1572872 | tf_op jit(solution)/shard_map/ppermute | solution.py:64
  231.9 20.4 %collective-permute-start.18 = (bf16[64,4096]{1,0:T(8,128)(2,1)S(1)}, bf16[64,4096]{1,0:T(8,128)(2,1)S(1)}, u32[]{:S(2)}, u32[]{:S(2)}) collective-permute-start(bf16[64,4096]{1,0:T(8,128)(2,1)S(1)} %get-tuple-element.24), channel_id=1, source_target_pairs={{0,1},{1,2},{2,3},{4,5},{5,6},{6,7},{8,9},{9,10},{10,11},{12,13},{... | collective-permute-start | bytes 1572872 | tf_op jit(solution)/shard_map/ppermute | solution.py:63
  236.6 1.8 collective-permute-start.39
  237.5 2.3 collective-permute-start.20
  238.6 25.3 %collective-permute-start.40 = (bf16[64,4096]{1,0:T(8,128)(2,1)S(1)}, bf16[64,4096]{1,0:T(8,128)(2,1)S(1)}, u32[]{:S(2)}, u32[]{:S(2)}) collective-permute-start(bf16[64,4096]{1,0:T(8,128)(2,1)S(1)} %add_convert_fusion.1), channel_id=1, source_target_pairs={{1,0},{2,1},{3,2},{5,4},{6,5},{7,6},{9,8},{10,9},{11,10},{13,12},{... | collective-permute-start | bytes 1572872 | tf_op jit(solution)/shard_map/ppermute | solution.py:64
  240.1 33.8 %collective-permute-start.21 = (bf16[64,4096]{1,0:T(8,128)(2,1)S(1)}, bf16[64,4096]{1,0:T(8,128)(2,1)S(1)}, u32[]{:S(2)}, u32[]{:S(2)}) collective-permute-start(bf16[64,4096]{1,0:T(8,128)(2,1)S(1)} %add_convert_fusion.6), channel_id=1, source_target_pairs={{1,0},{2,1},{3,2},{5,4},{6,5},{7,6},{9,8},{10,9},{11,10},{13,12},{... | collective-permute-start | bytes 1572872 | tf_op jit(solution)/shard_map/ppermute | solution.py:64
  275.5 24.3 %collective-permute-start.43 = (bf16[64,4096]{1,0:T(8,128)(2,1)S(1)}, bf16[64,4096]{1,0:T(8,128)(2,1)S(1)}, u32[]{:S(2)}, u32[]{:S(2)}) collective-permute-start(bf16[64,4096]{1,0:T(8,128)(2,1)S(1)} %get-tuple-element.51), channel_id=1, source_target_pairs={{0,1},{1,2},{2,3},{4,5},{5,6},{6,7},{8,9},{9,10},{10,11},{12,13},{... | collective-permute-start | bytes 1572872 | tf_op jit(solution)/shard_map/ppermute | solution.py:44
  287.4 16.8 %collective-permute-start.42 = (bf16[64,4096]{1,0:T(8,128)(2,1)S(1)}, bf16[64,4096]{1,0:T(8,128)(2,1)S(1)}, u32[]{:S(2)}, u32[]{:S(2)}) collective-permute-start(bf16[64,4096]{1,0:T(8,128)(2,1)S(1)} %get-tuple-element.51), channel_id=1, source_target_pairs={{1,0},{2,1},{3,2},{5,4},{6,5},{7,6},{9,8},{10,9},{11,10},{13,12},{... | collective-permute-start | bytes 1572872 | tf_op jit(solution)/shard_map/ppermute | solution.py:45
  288.8 18.1 %collective-permute-start.50 = (bf16[64,4096]{1,0:T(8,128)(2,1)S(1)}, bf16[64,4096]{1,0:T(8,128)(2,1)S(1)}, u32[]{:S(2)}, u32[]{:S(2)}) collective-permute-start(bf16[64,4096]{1,0:T(8,128)(2,1)S(1)} %get-tuple-element.52), channel_id=1, source_target_pairs={{0,1},{1,2},{2,3},{4,5},{5,6},{6,7},{8,9},{9,10},{10,11},{12,13},{... | collective-permute-start | bytes 1572872 | tf_op jit(solution)/shard_map/ppermute | solution.py:44
  293.5 22.0 %collective-permute-start.49 = (bf16[64,4096]{1,0:T(8,128)(2,1)S(1)}, bf16[64,4096]{1,0:T(8,128)(2,1)S(1)}, u32[]{:S(2)}, u32[]{:S(2)}) collective-permute-start(bf16[64,4096]{1,0:T(8,128)(2,1)S(1)} %get-tuple-element.52), channel_id=1, source_target_pairs={{1,0},{2,1},{3,2},{5,4},{6,5},{7,6},{9,8},{10,9},{11,10},{13,12},{... | collective-permute-start | bytes 1572872 | tf_op jit(solution)/shard_map/ppermute | solution.py:45
  299.8 17.0 %collective-permute-start.44 = (bf16[64,4096]{1,0:T(8,128)(2,1)S(1)}, bf16[64,4096]{1,0:T(8,128)(2,1)S(1)}, u32[]{:S(2)}, u32[]{:S(2)}) collective-permute-start(bf16[64,4096]{1,0:T(8,128)(2,1)S(1)} %collective-permute-done.43), channel_id=1, source_target_pairs={{1,2},{2,3},{5,6},{6,7},{9,10},{10,11},{13,14},{14,15},{17,18},{18... | collective-permute-start | bytes 1572872 | tf_op jit(solution)/shard_map/ppermute | solution.py:44
  304.2 20.0 %collective-permute-start.46 = (bf16[64,4096]{1,0:T(8,128)(2,1)S(1)}, bf16[64,4096]{1,0:T(8,128)(2,1)S(1)}, u32[]{:S(2)}, u32[]{:S(2)}) collective-permute-start(bf16[64,4096]{1,0:T(8,128)(2,1)S(1)} %collective-permute-done.42), channel_id=1, source_target_pairs={{1,0},{2,1},{5,4},{6,5},{9,8},{10,9},{13,12},{14,13},{17,16},{18,1... | collective-permute-start | bytes 1572872 | tf_op jit(solution)/shard_map/ppermute | solution.py:45
  306.9 18.6 %collective-permute-start.51 = (bf16[64,4096]{1,0:T(8,128)(2,1)S(1)}, bf16[64,4096]{1,0:T(8,128)(2,1)S(1)}, u32[]{:S(2)}, u32[]{:S(2)}) collective-permute-start(bf16[64,4096]{1,0:T(8,128)(2,1)S(1)} %collective-permute-done.50), channel_id=1, source_target_pairs={{1,2},{2,3},{5,6},{6,7},{9,10},{10,11},{13,14},{14,15},{17,18},{18... | collective-permute-start | bytes 1572872 | tf_op jit(solution)/shard_map/ppermute | solution.py:44
  309.0 48.5 %collective-permute-start.41 = (f32[128,256]{1,0:T(8,128)S(1)}, f32[128,256]{1,0:T(8,128)S(1)}, u32[]{:S(2)}, u32[]{:S(2)}) collective-permute-start(f32[128,256]{1,0:T(8,128)S(1)} %fusion.74), channel_id=1, source_target_pairs={{0,4},{4,0},{1,5},{5,1},{2,6},{6,2},{3,7},{7,3},{8,12},{12,8},{9,1... | collective-permute-start | bytes 393224 | tf_op jit(solution)/shard_map/ppermute | solution.py:30
  315.4 20.0 %collective-permute-start.53 = (bf16[64,4096]{1,0:T(8,128)(2,1)S(1)}, bf16[64,4096]{1,0:T(8,128)(2,1)S(1)}, u32[]{:S(2)}, u32[]{:S(2)}) collective-permute-start(bf16[64,4096]{1,0:T(8,128)(2,1)S(1)} %collective-permute-done.49), channel_id=1, source_target_pairs={{1,0},{2,1},{5,4},{6,5},{9,8},{10,9},{13,12},{14,13},{17,16},{18,1... | collective-permute-start | bytes 1572872 | tf_op jit(solution)/shard_map/ppermute | solution.py:45
  316.7 20.1 %collective-permute-start.45 = (bf16[64,4096]{1,0:T(8,128)(2,1)S(1)}, bf16[64,4096]{1,0:T(8,128)(2,1)S(1)}, u32[]{:S(2)}, u32[]{:S(2)}) collective-permute-start(bf16[64,4096]{1,0:T(8,128)(2,1)S(1)} %collective-permute-done.44), channel_id=1, source_target_pairs={{2,3},{6,7},{10,11},{14,15},{18,19},{22,23},{26,27},{30,31}} | collective-permute-start | bytes 1572872 | tf_op jit(solution)/shard_map/ppermute | solution.py:44
  324.2 22.5 %collective-permute-start.47 = (bf16[64,4096]{1,0:T(8,128)(2,1)S(1)}, bf16[64,4096]{1,0:T(8,128)(2,1)S(1)}, u32[]{:S(2)}, u32[]{:S(2)}) collective-permute-start(bf16[64,4096]{1,0:T(8,128)(2,1)S(1)} %collective-permute-done.46), channel_id=1, source_target_pairs={{1,0},{5,4},{9,8},{13,12},{17,16},{21,20},{25,24},{29,28}} | collective-permute-start | bytes 1572872 | tf_op jit(solution)/shard_map/ppermute | solution.py:45
  325.5 21.2 %collective-permute-start.52 = (bf16[64,4096]{1,0:T(8,128)(2,1)S(1)}, bf16[64,4096]{1,0:T(8,128)(2,1)S(1)}, u32[]{:S(2)}, u32[]{:S(2)}) collective-permute-start(bf16[64,4096]{1,0:T(8,128)(2,1)S(1)} %collective-permute-done.51), channel_id=1, source_target_pairs={{2,3},{6,7},{10,11},{14,15},{18,19},{22,23},{26,27},{30,31}} | collective-permute-start | bytes 1572872 | tf_op jit(solution)/shard_map/ppermute | solution.py:44
  335.5 20.5 %collective-permute-start.54 = (bf16[64,4096]{1,0:T(8,128)(2,1)S(1)}, bf16[64,4096]{1,0:T(8,128)(2,1)S(1)}, u32[]{:S(2)}, u32[]{:S(2)}) collective-permute-start(bf16[64,4096]{1,0:T(8,128)(2,1)S(1)} %collective-permute-done.53), channel_id=1, source_target_pairs={{1,0},{5,4},{9,8},{13,12},{17,16},{21,20},{25,24},{29,28}} | collective-permute-start | bytes 1572872 | tf_op jit(solution)/shard_map/ppermute | solution.py:45
  358.4 1.6 collective-permute-start.55
  360.4 8.3 %collective-permute-start.56 = (bf16[32,2048]{1,0:T(8,128)(2,1)S(1)}, bf16[32,2048]{1,0:T(8,128)(2,1)S(1)}, u32[]{:S(2)}, u32[]{:S(2)}) collective-permute-start(bf16[32,2048]{1,0:T(8,128)(2,1)S(1)} %get-tuple-element.32), channel_id=1, source_target_pairs={{0,1},{1,2},{2,3},{3,0},{4,5},{5,6},{6,7},{7,4},{8,9},{9,10},{10,1... | collective-permute-start | bytes 393224 | tf_op jit(solution)/shard_map/ppermute | solution.py:75
  360.5 13.0 %collective-permute-start.57 = (bf16[32,2048]{1,0:T(8,128)(2,1)S(1)}, bf16[32,2048]{1,0:T(8,128)(2,1)S(1)}, u32[]{:S(2)}, u32[]{:S(2)}) collective-permute-start(bf16[32,2048]{1,0:T(8,128)(2,1)S(1)} %get-tuple-element.34), channel_id=1, source_target_pairs={{0,2},{1,3},{2,0},{3,1},{4,6},{5,7},{6,4},{7,5},{8,10},{9,11},{10,... | collective-permute-start | bytes 393224 | tf_op jit(solution)/shard_map/ppermute | solution.py:75
  360.6 12.9 %collective-permute-start.58 = (bf16[32,2048]{1,0:T(8,128)(2,1)S(1)}, bf16[32,2048]{1,0:T(8,128)(2,1)S(1)}, u32[]{:S(2)}, u32[]{:S(2)}) collective-permute-start(bf16[32,2048]{1,0:T(8,128)(2,1)S(1)} %get-tuple-element.33), channel_id=1, source_target_pairs={{0,3},{1,0},{2,1},{3,2},{4,7},{5,4},{6,5},{7,6},{8,11},{9,8},{10,9... | collective-permute-start | bytes 393224 | tf_op jit(solution)/shard_map/ppermute | solution.py:75
  373.5 1.4 collective-permute-start.59
  (16 other events, 154.5 us)

commit v4 on v2

--- a/solution.py
+++ b/solution.py
@@ -10,7 +10,6 @@
 HD = 256
 F32 = jnp.float32
 BF16 = jnp.bfloat16
-CHUNKS = 2
 STATS = 5
 
 
@@ -31,43 +30,84 @@
     return lax.ppermute(value, axis, [(i, i ^ distance) for i in range(lax.axis_size(axis))])
 
 
-def near_bits(axis):
-    bits, bit = [], 1
-    while bit < lax.axis_size(axis):
-        bits.append(bit)
-        bit *= 2
-    return bits
-
-
-def slot_order(bits):
-    order = [0]
-    for bit in bits:
-        order = order + [m ^ bit for m in order]
-    return order
-
-
-def gather_swaps(value, axis, bits):
-    for bit in bits:
-        value = jnp.concatenate([value, swap(value, axis, bit)], 0)
-    return value
-
-
-def sum_swaps(value, axis, bits, sent):
-    for bit in bits[::-1]:
-        half = value.shape[0] // 2
-        value = value[:half] + swap(value[half:].astype(sent), axis, bit).astype(F32)
-    return value
+def from_slots(value):
+    count = lax.axis_size("tensor")
+    return [value] + [
+        lax.ppermute(value, "tensor", [(i, (i - o) % count) for i in range(count)]) for o in range(1, count)
+    ]
+
+
+def gated(value, *others):
+    return lax.optimization_barrier((value,) + others)[0]
+
+
+def line_step(above, below, step):
+    count = lax.axis_size("tensor")
+    return (
+        lax.ppermute(above, "tensor", [(i, i + 1) for i in range(step - 1, count - 1)]),
+        lax.ppermute(below, "tensor", [(i, i - 1) for i in range(1, count - step + 1)]),
+    )
+
+
+def line_rows(above, below):
+    count, tensor = lax.axis_size("tensor"), lax.axis_index("tensor")
+    return jnp.concatenate(
+        [above[0]] + [jnp.where(tensor + o < count, below[o], above[count - o]) for o in range(1, count)], 0
+    )
+
+
+def slot_sum(mine, got, slot):
+    block = mine.shape[0] // lax.axis_size("tensor")
+    at = slice(slot * block, (slot + 1) * block)
+    return mine[at].astype(F32) + got[at].astype(F32)
+
+
+def sum_sends(mine, got, came, step):
+    up, down = slot_sum(mine, got, lax.axis_size("tensor") - step), slot_sum(mine, got, step)
+    if came is not None:
+        up, down = up + came[0].astype(F32), down + came[1].astype(F32)
+    return up.astype(BF16), down.astype(BF16)
+
+
+def sum_step(sends, step):
+    count = lax.axis_size("tensor")
+    above = lax.ppermute(sends[0], "tensor", [(i, i + 1) for i in range(step)])
+    below = lax.ppermute(sends[1], "tensor", [(i, i - 1) for i in range(count - step, count)])
+    return lax.optimization_barrier((above, below))
+
+
+def slots_sum(product):
+    count = lax.axis_size("tensor")
+    product = product.reshape(count, product.shape[0] // count, product.shape[1])
+    total = product[0].astype(F32)
+    for o in range(1, count):
+        total = total + lax.ppermute(
+            product[o], "tensor", [(i, (i + o) % count) for i in range(count)]
+        ).astype(F32)
+    return total
 
 
 def half_columns(value, index):
     return lax.dynamic_slice_in_dim(value, index * (value.shape[1] // 2), value.shape[1] // 2, 1)
 
 
-def gather_half(rows, section, bits):
+def in_order(own, other, section, axis):
+    return jnp.where(
+        section == 0, jnp.concatenate([own, other], axis), jnp.concatenate([other, own], axis)
+    )
+
+
+def gather_half(rows, section):
     own = half_columns(rows, section)
     other = swap(half_columns(rows, 1 - section), "section", 1)
-    pair = jnp.where(section == 0, jnp.concatenate([own, other], 0), jnp.concatenate([other, own], 0))
-    return gather_swaps(pair, "tensor", bits)
+    return jnp.concatenate(from_slots(in_order(own, other, section, 0)), 0)
+
+
+def whole_rows(total, section):
+    rows = total.shape[0] // 2
+    own = lax.dynamic_slice_in_dim(total, section * rows, rows, 0)
+    other = swap(lax.dynamic_slice_in_dim(total, (1 - section) * rows, rows, 0), "section", 1)
+    return in_order(own, other, section, 1)
 
 
 def both_halves(partial):
@@ -78,17 +118,21 @@
     return 0.5 * x * (1.0 + jnp.tanh(0.7978845608028654 * (x + 0.044715 * x * x * x)))
 
 
-def ffn_kernel(hidden_steps, xa_ref, xb_ref, gate_ref, up_ref, down_ref, ya_ref, yb_ref, hidden):
+def ffn_kernel(hidden_steps, xa_ref, xb_ref, gate_ref, up_ref, down_ref, ya_ref, yb_ref, x, hidden):
     step = pl.program_id(0)
     rows = xa_ref.shape[0]
     width = gate_ref.shape[1]
 
+    @pl.when(step == 0)
+    def _():
+        x[:rows, :] = xa_ref[...]
+        x[rows:, :] = xb_ref[...]
+
     @pl.when(step < hidden_steps)
     def _():
-        for i, x_ref in enumerate((xa_ref, xb_ref)):
-            gate = jnp.dot(x_ref[...], gate_ref[...], preferred_element_type=F32)
-            up = jnp.dot(x_ref[...], up_ref[...], preferred_element_type=F32)
-            hidden[step, i * rows : (i + 1) * rows, :] = (gelu(gate) * up).astype(BF16)
+        gate = jnp.dot(x[...], gate_ref[...], preferred_element_type=F32)
+        up = jnp.dot(x[...], up_ref[...], preferred_element_type=F32)
+        hidden[step] = (gelu(gate) * up).astype(BF16)
 
     @pl.when(step >= hidden_steps)
     def _():
@@ -119,7 +163,10 @@
         ],
         out_specs=[pl.BlockSpec((rows, tile), lambda i: (0, jnp.maximum(i - first, 0)))] * 2,
         out_shape=[jax.ShapeDtypeStruct((rows, features), BF16)] * 2,
-        scratch_shapes=[pltpu.VMEM((first, 2 * rows, width), BF16)],
+        scratch_shapes=[
+            pltpu.VMEM((2 * rows, features), BF16),
+            pltpu.VMEM((first, 2 * rows, width), BF16),
+        ],
         compiler_params=pltpu.CompilerParams(vmem_limit_bytes=48 * 2**20),
         cost_estimate=pl.CostEstimate(
             flops=12 * rows * features * units, bytes_accessed=6 * features * units, transcendentals=0
@@ -135,12 +182,12 @@
     head = ids[slot]
     groups, depth = a0_ref.shape[0], a0_ref.shape[3]
 
-    def attend(own_ref, other_ref, row):
+    def attend(own_ref, other_ref):
         keys = jnp.zeros((mem_ref.shape[0], HD), F32)
         values = jnp.zeros((mem_ref.shape[0], HD), F32)
         for place, ref in enumerate((own_ref, other_ref)):
             for i in range(groups):
-                at = pl.multiple_of(table[row + place, i] * depth, depth)
+                at = pl.multiple_of(table[place, i] * depth, depth)
                 x = mem_ref[:, pl.ds(at, depth)]
                 keys += jnp.dot(x, ref[i, 0, 0], preferred_element_type=F32)
                 values += jnp.dot(x, ref[i, 0, 1], preferred_element_type=F32)
@@ -167,11 +214,11 @@
 
     @pl.when(slot < heads // 2)
     def _():
-        attend(a0_ref, a1_ref, 0)
+        attend(a0_ref, a1_ref)
 
     @pl.when(slot >= heads // 2)
     def _():
-        attend(b0_ref, b1_ref, 2)
+        attend(b0_ref, b1_ref)
 
 
 def attend_own_keys(memory, weights, queries, table, ids):
@@ -259,28 +306,11 @@
     rows, features = mid.shape
     per_word = words.shape[1] // depth
     block = (1, half, 1, depth, width)
-    bits = []
-    while 1 << len(bits) < groups:
-        bits.append(len(bits))
-    top = len(bits) - 1
-
-    def reverse(i):
-        out = 0
-        for b in bits:
-            out = out + ((i >> b) & 1) * (1 << (top - b))
-        return out
-
-    def a_own(p, i, t, n):
+    def own_block(p, i, t, n):
         return (jnp.where(p == 0, i, groups - 1), 0, 2, 0, 0)
 
-    def a_other(p, i, t, n):
+    def other_block(p, i, t, n):
         return (jnp.where(p == 0, 0, i), 0, 2, 0, 0)
-
-    def b_own(p, i, t, n):
-        return (reverse(jnp.where(p == 0, i, groups - 1)), 0, 2, 0, 0)
-
-    def b_other(p, i, t, n):
-        return (reverse(jnp.where(p == 0, 0, i)), 0, 2, 0, 0)
 
     return pl.pallas_call(
         functools.partial(finish_kernel, heads, words.shape[1]),
@@ -289,10 +319,10 @@
             grid=(2, groups),
             in_specs=[
                 pl.BlockSpec(parts.shape, lambda p, i, t, n: (0, 0, 0)),
-                pl.BlockSpec(block, a_own),
-                pl.BlockSpec(block, a_other),
-                pl.BlockSpec(block, b_own),
-                pl.BlockSpec(block, b_other),
+                pl.BlockSpec(block, own_block),
+                pl.BlockSpec(block, other_block),
+                pl.BlockSpec(block, own_block),
+                pl.BlockSpec(block, other_block),
                 pl.BlockSpec((rows, depth), lambda p, i, t, n: (0, t[p, i])),
                 pl.BlockSpec((rows, depth), lambda p, i, t, n: (0, lax.rem(t[p, i], per_word))),
             ],
@@ -328,25 +358,58 @@
     cross_out,
     dec_keep,
 ):
-    count, groups = lax.axis_size("tensor"), lax.axis_size("dp")
-    section, tensor, group = lax.axis_index("section"), lax.axis_index("tensor"), lax.axis_index("dp")
+    section, group = lax.axis_index("section"), lax.axis_index("dp")
+    count, tensor = lax.axis_size("tensor"), lax.axis_index("tensor")
+    groups = lax.axis_size("dp")
+    rows = target.shape[0]
     devices = 2 * count
-    bits = near_bits("tensor")[::-1]
-    order = slot_order(bits)
-    rows = target.shape[0]
-    after = lax.optimization_barrier
 
     normed = norm_rows(source, enc_gain).astype(BF16)
-    block = normed.shape[0] // CHUNKS
-    near = [gather_swaps(normed[c * block : (c + 1) * block], "tensor", bits) for c in range(CHUNKS)]
-    far = [swap(x, "section", 1) for x in near]
-
-    selfin = norm_rows(target, self_gain).astype(BF16)
-    x = gather_half(selfin, section, bits)
+    block = normed.shape[0] // 2
+    above, below = [[normed[:block]], [normed[block:]]], [[normed[:block]], [normed[block:]]]
+
+    def pass_on(c):
+        one, two = line_step(above[c][-1], below[c][-1], len(above[c]))
+        above[c].append(one)
+        below[c].append(two)
+
+    for step in range(1, count):
+        pass_on(0)
+        if step == count - 2:
+            second = gated(normed[block:], above[0][-1], below[0][-1])
+            above[1], below[1] = [second], [second]
+            pass_on(1)
+    near = line_rows(above[0], below[0])
+    far = swap(near, "section", 1)
+    near = gated(near, above[1][-1], below[1][-1])
+    if count > 2:
+        pass_on(1)
+
+    selfin = gather_half(gated(norm_rows(target, self_gain).astype(BF16), above[0][-2], below[0][-2]), section)
+
+    mine, theirs = ffn(near, far, w_gate, w_up, w_down)
+    while len(above[1]) < count:
+        pass_on(1)
+    near = line_rows(above[1], below[1])
+    far = swap(near, "section", 1)
+
+    depth = cross_kv.shape[0] // groups
+    kv_share = lax.dynamic_slice_in_dim(jnp.transpose(cross_kv, (1, 0, 2)), group * depth, depth, 1)
+    out_share = lax.dynamic_slice_in_dim(cross_out, group * depth, depth, 1)
+    out_share = jnp.transpose(out_share.reshape(HD, depth // HD, HD), (1, 0, 2)).reshape(1, depth, HD)
+    share = gated(jnp.concatenate([kv_share, out_share], 0), above[1][-2], below[1][-2])
+    slots = from_slots(share)
+    weights = []
+    for pieces in (slots[: count // 2], slots[count // 2 :]):
+        own = lax.all_gather(jnp.stack(pieces), "dp", axis=0, tiled=False)
+        weights += [own, swap(own, "section", 1)]
+    table = jnp.stack([section * groups, (1 - section) * groups])[:, None] + jnp.arange(groups, dtype=jnp.int32)
+    slot_chip = lax.rem(tensor + jnp.arange(count, dtype=jnp.int32), count)
+
+    selfin = gated(selfin, mine)
     qkv_w = jnp.transpose(self_qkv, (1, 0, 2))
-    q, k, v = [jnp.dot(x, qkv_w[i], preferred_element_type=F32) for i in range(3)]
+    q, k, v = [jnp.dot(selfin, qkv_w[i], preferred_element_type=F32) for i in range(3)]
     q, k, v = [y.astype(BF16) for y in both_halves(jnp.stack([q, k, v]))]
-    slot_chip = jnp.stack([tensor ^ m for m in order])
     positions = (
         (jnp.arange(2, dtype=jnp.int32)[None, :] * count + slot_chip[:, None])[:, :, None] * rows
         + jnp.arange(rows, dtype=jnp.int32)
@@ -356,59 +419,42 @@
     expo = jnp.exp(scores - jnp.max(scores, axis=-1, keepdims=True))
     probs = (expo / jnp.sum(expo, axis=-1, keepdims=True)).astype(BF16)
     context = jnp.dot(probs, v, preferred_element_type=F32).astype(BF16)
-    product = jnp.dot(context, self_out, preferred_element_type=F32).astype(BF16).astype(F32)
-    total = sum_swaps(product, "tensor", bits, BF16)
-    own = lax.dynamic_slice_in_dim(total, section * rows, rows, 0)
-    other = swap(lax.dynamic_slice_in_dim(total, (1 - section) * rows, rows, 0), "section", 1)
-    selfsum = jnp.where(section == 0, jnp.concatenate([own, other], 1), jnp.concatenate([other, own], 1))
-    mid = (target.astype(F32) + selfsum).astype(BF16)
-
-    shares = [ffn(near[0], far[0], w_gate, w_up, w_down)]
-
-    depth = cross_kv.shape[0] // groups
-    kv_share = lax.dynamic_slice_in_dim(jnp.transpose(cross_kv, (1, 0, 2)), group * depth, depth, 1)
-    out_share = lax.dynamic_slice_in_dim(cross_out, group * depth, depth, 1)
-    out_share = jnp.transpose(out_share.reshape(HD, depth // HD, HD), (1, 0, 2)).reshape(1, depth, HD)
-    share = jnp.concatenate([kv_share, out_share], 0)[None]
-    share, near[0] = after((share, near[0]))
-    share = gather_swaps(share, "tensor", bits)
-    dp_bits = near_bits("dp")
-    weights, table = [], []
-    for piece, way in ((share[: count // 2], dp_bits), (share[count // 2 :], dp_bits[::-1])):
-        own = gather_swaps(piece[None], "dp", way)
-        weights += [own, swap(own, "section", 1)]
-        at = jnp.stack([group ^ m for m in slot_order(way)])
-        table += [section * groups + at, (1 - section) * groups + at]
-    table = jnp.stack(table).astype(jnp.int32)
-    ids = slot_chip.astype(jnp.int32)
-
-    mid, first = after((mid, shares[0][0]))
-    shares[0] = (first, shares[0][1])
-    crossin = norm_rows(mid, cross_gain).astype(BF16)
-    x = gather_half(crossin, section, bits)
-    cq = both_halves(jnp.dot(x, cross_q, preferred_element_type=F32)).astype(BF16)
-    cq = cq.reshape(count, 2, rows, HD)
-    place = [order.index(m) for m in range(count)]
-    back = jnp.asarray(place, jnp.int32)
-    cq = jnp.stack(
-        [lax.dynamic_index_in_dim(cq, back[tensor ^ c], 0, keepdims=False) for c in range(count)]
-    )
+    product = jnp.dot(context, self_out, preferred_element_type=F32).astype(BF16)
+    total = slots_sum(product)
+
+    got = swap(theirs, "section", 1)
+    came = sum_step(sum_sends(mine, got, None, 1), 1)
+    sends = sum_sends(mine, got, came, 2)
+    near = gated(near, *sends)
+    came = sum_step(sends, 2)
+    mine_b, theirs_b = ffn(near, far, w_gate, w_up, w_down)
+    for step in range(3, count):
+        came = sum_step(sum_sends(mine, got, came, step), step)
+    ffn_a = slot_sum(mine, got, 0) + came[0].astype(F32) + came[1].astype(F32)
+
+    total = gated(total, mine_b)
+    mid = (target.astype(F32) + whole_rows(total, section)).astype(BF16)
+    crossin = gather_half(norm_rows(mid, cross_gain).astype(BF16), section)
+
+    got_b = swap(theirs_b, "section", 1)
+    came_b = sum_step(sum_sends(mine_b, got_b, None, 1), 1)
+    crossin = gated(crossin, *came_b)
+    for step in range(2, count):
+        came_b = sum_step(sum_sends(mine_b, got_b, came_b, step), step)
+    cq = both_halves(jnp.dot(crossin, cross_q, preferred_element_type=F32)).astype(BF16)
+    cq = jnp.roll(cq.reshape(count, 2, rows, HD), tensor, axis=0)
     cq = jnp.transpose(cq, (1, 0, 2, 3)).reshape(devices * rows, HD)
-    queries = gather_swaps(cq[None], "tensor", bits)
-
-    for c in range(1, CHUNKS):
-        shares.append(ffn(near[c], far[c], w_gate, w_up, w_down))
-    total = [
-        sum_swaps(ya.astype(F32) + swap(yb, "section", 1).astype(F32), "tensor", bits, BF16)
-        for ya, yb in shares
-    ]
-    enc_out = (source.astype(F32) + keep_factor(enc_keep) * jnp.concatenate(total, 0)).astype(BF16)
+    queries = jnp.stack(from_slots(cq))
+    ffn_b = slot_sum(mine_b, got_b, 0) + came_b[0].astype(F32) + came_b[1].astype(F32)
+
+    total = jnp.concatenate([ffn_a, ffn_b], 0)
+    enc_out = (source.astype(F32) + keep_factor(enc_keep) * total).astype(BF16)
     memory = norm_rows(enc_out, final_gain).astype(BF16)
 
-    parts = attend_own_keys(memory, weights, queries, table, ids)
+    parts = attend_own_keys(memory, weights, queries, table, slot_chip)
     parts = parts.reshape(devices, rows, parts.shape[1])
     parts = lax.all_to_all(parts, ("section", "tensor"), split_axis=0, concat_axis=0, tiled=True)
-    dec_out = finish(parts, weights, mid, dec_keep, table, ids)
+    dec_out = finish(parts, weights, mid, dec_keep, table, slot_chip)
     return (enc_out, dec_out)
 
 

time: 439 us -> 390 us (0.89)
  waiting for transfers between devices: 255 us -> 144 us
  starting transfers between devices: 35.3 us -> 97.5 us
  local copies, waits for them, and re-layouts: 20.3 us -> 11.2 us
  between operations: 9.11 us -> 15 us
    ppermute x33 -> x11, waiting for transfers between devices: 255 us -> 3.42 us  [swap(): lax.ppermute(value, axis, [(i, i ^ distance) for i in range(lax.axis_size...]
    ppermute x0 -> x39, waiting for transfers between devices: none -> 141 us  [the longest x6 60.5 us: line_step(): lax.ppermute(below, 'tensor', [(i, i - 1) for i in range(1, count - step...]
    ppermute x0 -> x39, starting transfers between devices: none -> 95.3 us  [the longest x12 32.9 us: from_slots(): lax.ppermute(value, 'tensor', [(i, (i - o) % count) for i in range(count)])]
    ppermute x33 -> x11, starting transfers between devices: 35.3 us -> 2.16 us  [swap(): lax.ppermute(value, axis, [(i, i ^ distance) for i in range(lax.axis_size...]
    concatenate x12 -> x6, other arithmetic: 18.2 us -> 3.88 us  [the longest x2 1.76 us: line_rows(): jnp.concatenate([above[0]] + [jnp.where(tensor + o < count, below[o], abo...]
    convert_element_type x4 -> x9, other arithmetic: 1.16 us -> 14.3 us  [the longest x6 13.4 us: sum_sends(): return (up.astype(BF16), down.astype(BF16))]
    unnamed x67 -> x72, local copies, waits for them, and re-layouts: 13.9 us -> 7.52 us
  transfers between devices with their start and end apart: 33 -> 52, of which waited for: 13 -> 20; matrix products, arithmetic and copies ran while one was open for 11% -> 11% of each run, Pallas kernels for 10% -> 12%
where the time goes in v4:
time: 390 us; the launch traced here: 388 us
  waiting for transfers between devices  144 us (37%)
  starting transfers between devices  97.5 us (25%)
  Pallas kernels  64.8 us (17%)
  other arithmetic  35.2 us (9%)
  blocking collectives  15.5 us (4%)
  between operations  15 us (4%)
  local copies, waits for them, and re-layouts  11.2 us (3%)
  matrix products  4.34 us (1%)
    ppermute x6, waiting for transfers between devices, line_step(): lax.ppermute(below, 'tensor', [(i, i - 1) for i in range(1, count - step...  60.5 us
    ppermute x12, waiting for transfers between devices, from_slots(): lax.ppermute(value, 'tensor', [(i, (i - o) % count) for i in range(count)])  49.2 us
    pallas_call x2, Pallas kernels, ffn(): pl.pallas_call(functools.partial(ffn_kernel, first), grid=(first + last,)...  47.3 us
    ppermute x12, starting transfers between devices, from_slots(): lax.ppermute(value, 'tensor', [(i, (i - o) % count) for i in range(count)])  32.9 us
    ppermute x6, starting transfers between devices, sum_step(): above = lax.ppermute(sends[0], 'tensor', [(i, i + 1) for i in range(step)])  29.1 us
    all_to_all x1, blocking collectives, per_device(): lax.all_to_all(parts, ('section', 'tensor'), split_axis=0, concat_axis=0,...  15.5 us
    ppermute x6, starting transfers between devices, line_step(): lax.ppermute(above, 'tensor', [(i, i + 1) for i in range(step - 1, count...  14.8 us
    convert_element_type x6, other arithmetic, sum_sends(): return (up.astype(BF16), down.astype(BF16))  13.4 us
  transfers between devices with their start and end apart: 52, of which 20 were waited for; matrix products, arithmetic and copies ran while one was open for 11% of the time, Pallas kernels for 12%

profile of v4, /device:TPU:0, one launch (start us, length us, event | category | flops | bytes accessed | tf_op | source)
XLA Modules:
  0.0 387.8 jit_solution(13941464521640811513)
XLA Ops:
  7.2 1.7 fusion.3
  8.9 1.6 fusion.5
  10.6 5.1 %collective-permute-start.1 = (bf16[64,4096]{1,0:T(8,128)(2,1)S(1)}, bf16[64,4096]{1,0:T(8,128)(2,1)S(1)}, u32[]{:S(2)}, u32[]{:S(2)}) collective-permute-start(bf16[64,4096]{1,0:T(8,128)(2,1)S(1)} %get-tuple-element.66), channel_id=1, source_target_pairs={{0,1},{1,2},{2,3},{4,5},{5,6},{6,7},{8,9},{9,10},{10,11},{12,13},{... | collective-permute-start | bytes 1572872 | tf_op jit(solution)/shard_map/ppermute | solution.py:47
  15.7 1.3 collective-permute-start
  17.0 9.8 %collective-permute-done.1 = bf16[64,4096]{1,0:T(8,128)(2,1)S(1)} collective-permute-done((bf16[64,4096]{1,0:T(8,128)(2,1)S(1)}, bf16[64,4096]{1,0:T(8,128)(2,1)S(1)}, u32[]{:S(2)}, u32[]{:S(2)}) %collective-permute-start.1) | collective-permute-done | bytes 524320 | tf_op jit(solution)/shard_map/ppermute | solution.py:47
  26.8 1.5 collective-permute-start.2
  28.2 2.8 collective-permute-done
  32.4 14.3 %collective-permute-done.4 = bf16[64,4096]{1,0:T(8,128)(2,1)} collective-permute-done((bf16[64,4096]{1,0:T(8,128)(2,1)}, bf16[64,4096]{1,0:T(8,128)(2,1)}, u32[]{:S(2)}, u32[]{:S(2)}) %collective-permute-start.4) | collective-permute-done | bytes 524320 | tf_op jit(solution)/shard_map/ppermute | solution.py:48
  47.9 5.4 %collective-permute-start.6 = (bf16[64,4096]{1,0:T(8,128)(2,1)S(1)}, bf16[64,4096]{1,0:T(8,128)(2,1)}, u32[]{:S(2)}, u32[]{:S(2)}) collective-permute-start(bf16[64,4096]{1,0:T(8,128)(2,1)S(1)} %get-tuple-element.26), channel_id=1, source_target_pairs={{0,1},{1,2},{2,3},{4,5},{5,6},{6,7},{8,9},{9,10},{10,11},{12,13},{... | collective-permute-start | bytes 1572872 | tf_op jit(solution)/shard_map/ppermute | solution.py:47
  56.9 3.7 collective-permute-done.7
  61.9 1.5 collective-permute-start.16
  63.5 10.5 %collective-permute-done.18 = bf16[64,4096]{1,0:T(8,128)(2,1)S(1)} collective-permute-done((bf16[64,4096]{1,0:T(8,128)(2,1)}, bf16[64,4096]{1,0:T(8,128)(2,1)S(1)}, u32[]{:S(2)}, u32[]{:S(2)}) %collective-permute-start.18) | collective-permute-done | bytes 524320 | tf_op jit(solution)/shard_map/ppermute | solution.py:48
  74.8 3.1 collective-permute-start.28
  78.7 24.4 %collective-permute-done.28 = bf16[3,512,256]{2,1,0:T(8,128)(2,1)S(1)} collective-permute-done((bf16[3,512,256]{2,1,0:T(8,128)(2,1)S(1)}, bf16[3,512,256]{2,1,0:T(8,128)(2,1)S(1)}, u32[]{:S(2)}, u32[]{:S(2)}) %collective-permute-start.28) | collective-permute-done | bytes 786464 | tf_op jit(solution)/shard_map/ppermute | solution.py:36
  103.1 1.3 pad_maximum_fusion.2
  105.4 1.3 collective-permute-start.5
  106.8 2.7 collective-permute-start.36
  109.5 1.5 collective-permute-start.35
  111.0 2.8 collective-permute-start.34
  115.1 5.3 %collective-permute-done.35 = bf16[32,2048]{1,0:T(8,128)(2,1)S(1)} collective-permute-done((bf16[32,2048]{1,0:T(8,128)(2,1)S(1)}, bf16[32,2048]{1,0:T(8,128)(2,1)S(1)}, u32[]{:S(2)}, u32[]{:S(2)}) %collective-permute-start.35) | collective-permute-done | bytes 131104 | tf_op jit(solution)/shard_map/ppermute | solution.py:36
  120.3 10.0 %collective-permute-done.34 = bf16[32,2048]{1,0:T(8,128)(2,1)S(1)} collective-permute-done((bf16[32,2048]{1,0:T(8,128)(2,1)S(1)}, bf16[32,2048]{1,0:T(8,128)(2,1)S(1)}, u32[]{:S(2)}, u32[]{:S(2)}) %collective-permute-start.34) | collective-permute-done | bytes 131104 | tf_op jit(solution)/shard_map/ppermute | solution.py:36
  132.0 1.7 collective-permute-start.30
  135.8 29.2 %collective-permute-done.19 = bf16[64,4096]{1,0:T(8,128)(2,1)S(1)} collective-permute-done((bf16[64,4096]{1,0:T(8,128)(2,1)S(1)}, bf16[64,4096]{1,0:T(8,128)(2,1)S(1)}, u32[]{:S(2)}, u32[]{:S(2)}) %collective-permute-start.19) | collective-permute-done | bytes 524320 | tf_op jit(solution)/shard_map/ppermute | solution.py:48
  166.3 23.7 %ffn.2 = (bf16[256,4096]{1,0:T(8,128)(2,1)S(1)}, bf16[256,4096]{1,0:T(8,128)(2,1)}) custom-call(bf16[256,4096]{1,0:T(8,128)(2,1)} %copy-done.10, bf16[256,4096]{1,0:T(8,128)(2,1)} %collective-permute-done.8.xb_ref, bf16[4096,1024]{1,0:T(8,128)(2,1)} %gate_ref.3, bf16[4096,1024]{1,0:T(8,128)(2,1)} %up_ref.3, bf16[1024,4096]{1,0:T(8,128)(2,1)} %down_ref.3), custom_call_target="tpu_custom_call" | custom-call | flops 12884901888 | bytes 25165824 | tf_op jit(solution)/shard_map/ffn/pallas_call | solution.py:154
  192.3 1.6 pad_maximum_fusion.1.xa_ref
  194.0 1.4 pad_maximum_fusion.3
  196.7 1.7 convolution_convert_fusion
  199.6 3.4 collective-permute-start.40
  202.9 2.6 fusion.8
  207.2 2.3 collective-permute-start.10
  209.5 4.1 %collective-permute-done.39 = bf16[32,2048]{1,0:T(8,128)(2,1)} collective-permute-done((bf16[32,2048]{1,0:T(8,128)(2,1)S(1)}, bf16[32,2048]{1,0:T(8,128)(2,1)}, u32[]{:S(2)}, u32[]{:S(2)}) %collective-permute-start.39) | collective-permute-done | bytes 131104 | tf_op jit(solution)/shard_map/ppermute | solution.py:84
  215.4 4.9 %collective-permute-done.10 = bf16[64,4096]{1,0:T(8,128)(2,1)} collective-permute-done((bf16[64,4096]{1,0:T(8,128)(2,1)}, bf16[64,4096]{1,0:T(8,128)(2,1)}, u32[]{:S(2)}, u32[]{:S(2)}) %collective-permute-start.10) | collective-permute-done | bytes 524320 | tf_op jit(solution)/shard_map/ppermute | solution.py:74
  220.3 2.4 add_convert_fusion.6
  222.8 23.6 %ffn.3 = (bf16[256,4096]{1,0:T(8,128)(2,1)S(1)}, bf16[256,4096]{1,0:T(8,128)(2,1)}) custom-call(bf16[256,4096]{1,0:T(8,128)(2,1)} %pad_maximum_fusion.1.xa_ref, bf16[256,4096]{1,0:T(8,128)(2,1)} %collective-permute-done.20.xb_ref, bf16[4096,1024]{1,0:T(8,128)(2,1)} %gate_ref.3, bf16[4096,1024]{1,0:T(8,128)(2,1)} %up_ref.3, bf16[1024,4096]{1,0:T(8,128)(2,1)} %down_ref.3), custom_call_target="tpu_custom_call" | custom-call | flops 12884901888 | bytes 25165824 | tf_op jit(solution)/shard_map/ffn/pallas_call | solution.py:154
  246.4 1.3 copy-done.4
  249.7 2.6 collective-permute-done.42
  252.3 2.5 collective-permute-start.45
  254.8 1.5 collective-permute-start.13
  256.3 6.2 %collective-permute-start.12 = (bf16[64,4096]{1,0:T(8,128)(2,1)S(1)}, bf16[64,4096]{1,0:T(8,128)(2,1)}, u32[]{:S(2)}, u32[]{:S(2)}) collective-permute-start(bf16[64,4096]{1,0:T(8,128)(2,1)S(1)} %get-tuple-element.63), channel_id=1, source_target_pairs={{0,1},{1,2},{4,5},{5,6},{8,9},{9,10},{12,13},{13,14},{16,17},{17,1... | collective-permute-start | bytes 1572872 | tf_op jit(solution)/shard_map/ppermute | solution.py:74
  263.3 3.5 collective-permute-start.43
  268.1 3.0 copy.38
  271.1 9.5 %collective-permute-done.44 = bf16[32,2048]{1,0:T(8,128)(2,1)} collective-permute-done((bf16[32,2048]{1,0:T(8,128)(2,1)S(1)}, bf16[32,2048]{1,0:T(8,128)(2,1)}, u32[]{:S(2)}, u32[]{:S(2)}) %collective-permute-start.44) | collective-permute-done | bytes 131104 | tf_op jit(solution)/shard_map/ppermute | solution.py:36
  281.6 1.8 fusion.10
  283.4 1.5 collective-permute-start.23
  284.9 6.0 %collective-permute-start.22 = (bf16[64,4096]{1,0:T(8,128)(2,1)S(1)}, bf16[64,4096]{1,0:T(8,128)(2,1)}, u32[]{:S(2)}, u32[]{:S(2)}) collective-permute-start(bf16[64,4096]{1,0:T(8,128)(2,1)S(1)} %get-tuple-element.61), channel_id=1, source_target_pairs={{0,1},{4,5},{8,9},{12,13},{16,17},{20,21},{24,25},{28,29}} | collective-permute-start | bytes 1572872 | tf_op jit(solution)/shard_map/ppermute | solution.py:74
  290.9 3.0 add_convert_fusion.4
  295.2 5.3 %collective-permute-start.14 = (bf16[64,4096]{1,0:T(8,128)(2,1)}, bf16[64,4096]{1,0:T(8,128)(2,1)}, u32[]{:S(2)}, u32[]{:S(2)}) collective-permute-start(bf16[64,4096]{1,0:T(8,128)(2,1)} %get-tuple-element.55), channel_id=1, source_target_pairs={{0,1},{1,2},{2,3},{4,5},{5,6},{6,7},{8,9},{9,10},{10,11},{12,13},{... | collective-permute-start | bytes 1572872 | tf_op jit(solution)/shard_map/ppermute | solution.py:74
  300.6 1.7 collective-permute-done.22
  302.7 1.5 fusion.31
  304.4 1.9 add_convert_fusion.2
  306.3 2.1 collective-permute-done.15
  309.1 2.5 collective-permute-done.14
  311.7 4.4 %collective-permute-start.24 = (bf16[64,4096]{1,0:T(8,128)(2,1)S(1)}, bf16[64,4096]{1,0:T(8,128)(2,1)S(1)}, u32[]{:S(2)}, u32[]{:S(2)}) collective-permute-start(bf16[64,4096]{1,0:T(8,128)(2,1)S(1)} %get-tuple-element.59), channel_id=1, source_target_pairs={{0,1},{1,2},{4,5},{5,6},{8,9},{9,10},{12,13},{13,14},{16,17},{17,1... | collective-permute-start | bytes 1572872 | tf_op jit(solution)/shard_map/ppermute | solution.py:74
  316.2 2.1 collective-permute-start.49
  318.3 10.7 %collective-permute-start.48 = (bf16[128,256]{1,0:T(8,128)(2,1)S(1)}, bf16[128,256]{1,0:T(8,128)(2,1)S(1)}, u32[]{:S(2)}, u32[]{:S(2)}) collective-permute-start(bf16[128,256]{1,0:T(8,128)(2,1)S(1)} %bitcast.90), channel_id=1, source_target_pairs={{0,2},{1,3},{2,0},{3,1},{4,6},{5,7},{6,4},{7,5},{8,10},{9,11},{10,... | collective-permute-start | bytes 196616 | tf_op jit(solution)/shard_map/ppermute | solution.py:36
  330.3 1.7 add_convert_fusion
  332.0 1.3 collective-permute-start.27
  333.3 4.8 %collective-permute-start.26 = (bf16[64,4096]{1,0:T(8,128)(2,1)S(1)}, bf16[64,4096]{1,0:T(8,128)(2,1)S(1)}, u32[]{:S(2)}, u32[]{:S(2)}) collective-permute-start(bf16[64,4096]{1,0:T(8,128)(2,1)S(1)} %get-tuple-element.57), channel_id=1, source_target_pairs={{0,1},{1,2},{2,3},{4,5},{5,6},{6,7},{8,9},{9,10},{10,11},{12,13},{... | collective-permute-start | bytes 1572872 | tf_op jit(solution)/shard_map/ppermute | solution.py:74
  338.1 1.4 convert_add_fusion.5
  339.7 4.5 %collective-permute-done.27 = bf16[64,4096]{1,0:T(8,128)(2,1)S(1)} collective-permute-done((bf16[64,4096]{1,0:T(8,128)(2,1)S(1)}, bf16[64,4096]{1,0:T(8,128)(2,1)S(1)}, u32[]{:S(2)}, u32[]{:S(2)}) %collective-permute-start.27) | collective-permute-done | bytes 524320 | tf_op jit(solution)/shard_map/ppermute | solution.py:75
  344.7 1.4 convert_add_fusion.1
  348.0 9.7 %attend_own_keys.1 = bf16[128,1152]{1,0:T(8,128)(2,1)S(1)} custom-call(s32[2,4]{1,0:T(2,128)S(1)} %iota_add_fusion.1.table, s32[4]{0:T(128)S(1)} %compare_select_fusion.ids, bf16[128,4096]{1,0:T(8,128)(2,1)S(1)} %fusion.2.mem_ref, bf16[4,2,3,512,256]{4,3,2,1,0:T(8,128)(2,1)S(1)} %bitcast.71, bf16[4,2,3,512,256]{4,3,2,1,0:T(8,128)(2,1)} %collective-permute-done.29.a1_ref, ...), custom_call_target="tpu_custom_call" | custom-call | flops 2147483648 | bytes 16777216 | tf_op jit(solution)/shard_map/attend_own_keys/pallas_call | solution.py:231
  357.7 15.5 %all_to_all.5.parts_ref = bf16[8,16,1152]{2,1,0:T(8,128)(2,1)S(1)} all-to-all(bf16[8,16,1152]{2,1,0:T(8,128)(2,1)S(1)} %bitcast.78), channel_id=1, replica_groups=mesh['dp'=4,'section'=2,'tensor'=4] {'section','tensor'}, dimensions={0} | all-to-all | bytes 589824 | tf_op jit(solution)/shard_map/all_to_all | solution.py:456
  373.2 7.7 %finish.1 = bf16[16,4096]{1,0:T(8,128)(2,1)} custom-call(s32[2,4]{1,0:T(2,128)S(1)} %iota_add_fusion.1.table, s32[4]{0:T(128)S(1)} %compare_select_fusion.ids, bf16[8,16,1152]{2,1,0:T(8,128)(2,1)S(1)} %all_to_all.5.parts_ref, bf16[4,2,3,512,256]{4,3,2,1,0:T(8,128)(2,1)S(1)} %bitcast.72, bf16[4,2,3,512,256]{4,3,2,1,0:T(8,128)(2,1)} %collective-permute-done.29.a1_ref, ...), custom_call_target="tpu_custom_call" | custom-call | flops 134217728 | bytes 8388608 | tf_op jit(solution)/shard_map/finish/pallas_call | solution.py:315
  (186 shorter events, 35.9 us)
Async XLA Ops:
  7.2 48.1 %copy-start = (bf16[2048,2,256]{2,1,0:T(2,128)(2,1)S(1)}, bf16[2048,2,256]{2,1,0:T(2,128)(2,1)}, u32[]{:S(2)}) copy-start(bf16[2048,2,256]{2,1,0:T(2,128)(2,1)} %param.29) | copy-start | bytes 6291460
  7.2 295.0 %all-gather.5.cloned.1.call-start = ((), (), s32[]{:S(2)}) async-start(), calls=%async_computation.1 | async-start | bytes 7864320 | tf_op jit(solution)/shard_map/all_gather | solution.py:404
  10.5 45.2 %copy-start.13 = (bf16[16,4096]{1,0:T(8,128)(2,1)S(1)}, bf16[16,4096]{1,0:T(8,128)(2,1)}, u32[]{:S(2)}) copy-start(bf16[16,4096]{1,0:T(8,128)(2,1)} %param.23) | copy-start | bytes 393220
  10.6 16.2 %collective-permute-start.1 = (bf16[64,4096]{1,0:T(8,128)(2,1)S(1)}, bf16[64,4096]{1,0:T(8,128)(2,1)S(1)}, u32[]{:S(2)}, u32[]{:S(2)}) collective-permute-start(bf16[64,4096]{1,0:T(8,128)(2,1)S(1)} %get-tuple-element.66), channel_id=1, source_target_pairs={{0,1},{1,2},{2,3},{4,5},{5,6},{6,7},{8,9},{9,10},{10,11},{12,13},{... | collective-permute-start | bytes 1572872 | tf_op jit(solution)/shard_map/ppermute | solution.py:47
  15.7 15.4 %collective-permute-start = (bf16[64,4096]{1,0:T(8,128)(2,1)S(1)}, bf16[64,4096]{1,0:T(8,128)(2,1)}, u32[]{:S(2)}, u32[]{:S(2)}) collective-permute-start(bf16[64,4096]{1,0:T(8,128)(2,1)S(1)} %get-tuple-element.66), channel_id=1, source_target_pairs={{1,0},{2,1},{3,2},{5,4},{6,5},{7,6},{9,8},{10,9},{11,10},{13,12},{... | collective-permute-start | bytes 1572872 | tf_op jit(solution)/shard_map/ppermute | solution.py:48
  26.8 5.6 %collective-permute-start.2 = (bf16[64,4096]{1,0:T(8,128)(2,1)S(1)}, bf16[64,4096]{1,0:T(8,128)(2,1)}, u32[]{:S(2)}, u32[]{:S(2)}) collective-permute-start(bf16[64,4096]{1,0:T(8,128)(2,1)S(1)} %collective-permute-done.1), channel_id=1, source_target_pairs={{1,2},{2,3},{5,6},{6,7},{9,10},{10,11},{13,14},{14,15},{17,18},{18... | collective-permute-start | bytes 1572872 | tf_op jit(solution)/shard_map/ppermute | solution.py:47
  31.0 15.6 %collective-permute-start.4 = (bf16[64,4096]{1,0:T(8,128)(2,1)}, bf16[64,4096]{1,0:T(8,128)(2,1)}, u32[]{:S(2)}, u32[]{:S(2)}) collective-permute-start(bf16[64,4096]{1,0:T(8,128)(2,1)} %collective-permute-done), channel_id=1, source_target_pairs={{1,0},{2,1},{5,4},{6,5},{9,8},{10,9},{13,12},{14,13},{17,16},{18,1... | collective-permute-start | bytes 1572872 | tf_op jit(solution)/shard_map/ppermute | solution.py:48
  46.6 14.0 %collective-permute-start.7 = (bf16[64,4096]{1,0:T(8,128)(2,1)S(1)}, bf16[64,4096]{1,0:T(8,128)(2,1)}, u32[]{:S(2)}, u32[]{:S(2)}) collective-permute-start(bf16[64,4096]{1,0:T(8,128)(2,1)S(1)} %get-tuple-element.26), channel_id=1, source_target_pairs={{1,0},{2,1},{3,2},{5,4},{6,5},{7,6},{9,8},{10,9},{11,10},{13,12},{... | collective-permute-start | bytes 1572872 | tf_op jit(solution)/shard_map/ppermute | solution.py:48
  47.9 14.0 %collective-permute-start.6 = (bf16[64,4096]{1,0:T(8,128)(2,1)S(1)}, bf16[64,4096]{1,0:T(8,128)(2,1)}, u32[]{:S(2)}, u32[]{:S(2)}) collective-permute-start(bf16[64,4096]{1,0:T(8,128)(2,1)S(1)} %get-tuple-element.26), channel_id=1, source_target_pairs={{0,1},{1,2},{2,3},{4,5},{5,6},{6,7},{8,9},{9,10},{10,11},{12,13},{... | collective-permute-start | bytes 1572872 | tf_op jit(solution)/shard_map/ppermute | solution.py:47
  60.6 13.4 %collective-permute-start.18 = (bf16[64,4096]{1,0:T(8,128)(2,1)}, bf16[64,4096]{1,0:T(8,128)(2,1)S(1)}, u32[]{:S(2)}, u32[]{:S(2)}) collective-permute-start(bf16[64,4096]{1,0:T(8,128)(2,1)} %collective-permute-done.7), channel_id=1, source_target_pairs={{1,0},{2,1},{5,4},{6,5},{9,8},{10,9},{13,12},{14,13},{17,16},{18,1... | collective-permute-start | bytes 1572872 | tf_op jit(solution)/shard_map/ppermute | solution.py:48
  61.9 12.9 %collective-permute-start.16 = (bf16[64,4096]{1,0:T(8,128)(2,1)}, bf16[64,4096]{1,0:T(8,128)(2,1)}, u32[]{:S(2)}, u32[]{:S(2)}) collective-permute-start(bf16[64,4096]{1,0:T(8,128)(2,1)} %collective-permute-done.6), channel_id=1, source_target_pairs={{1,2},{2,3},{5,6},{6,7},{9,10},{10,11},{13,14},{14,15},{17,18},{18... | collective-permute-start | bytes 1572872 | tf_op jit(solution)/shard_map/ppermute | solution.py:47
  74.8 28.3 %collective-permute-start.28 = (bf16[3,512,256]{2,1,0:T(8,128)(2,1)S(1)}, bf16[3,512,256]{2,1,0:T(8,128)(2,1)S(1)}, u32[]{:S(2)}, u32[]{:S(2)}) collective-permute-start(bf16[3,512,256]{2,1,0:T(8,128)(2,1)S(1)} %pad_maximum_fusion.4), channel_id=1, source_target_pairs={{0,3},{1,0},{2,1},{3,2},{4,7},{5,4},{6,5},{7,6},{8,11},{9,8},{10,9... | collective-permute-start | bytes 2359304 | tf_op jit(solution)/shard_map/ppermute | solution.py:36
  104.4 197.8 %all-gather.7.cloned.1.call-start = ((), (), s32[]{:S(2)}) async-start(), calls=%async_computation.2 | async-start | bytes 7864320 | tf_op jit(solution)/shard_map/all_gather | solution.py:404
  104.5 2.2 collective-permute-start.33
  104.7 25.7 %collective-permute-start.3 = (bf16[64,4096]{1,0:T(8,128)(2,1)}, bf16[64,4096]{1,0:T(8,128)(2,1)S(1)}, u32[]{:S(2)}, u32[]{:S(2)}) collective-permute-start(bf16[64,4096]{1,0:T(8,128)(2,1)} %collective-permute-done.2), channel_id=1, source_target_pairs={{2,3},{6,7},{10,11},{14,15},{18,19},{22,23},{26,27},{30,31}} | collective-permute-start | bytes 1572872 | tf_op jit(solution)/shard_map/ppermute | solution.py:47
  105.4 26.1 %collective-permute-start.5 = (bf16[64,4096]{1,0:T(8,128)(2,1)}, bf16[64,4096]{1,0:T(8,128)(2,1)S(1)}, u32[]{:S(2)}, u32[]{:S(2)}) collective-permute-start(bf16[64,4096]{1,0:T(8,128)(2,1)} %collective-permute-done.4), channel_id=1, source_target_pairs={{1,0},{5,4},{9,8},{13,12},{17,16},{21,20},{25,24},{29,28}} | collective-permute-start | bytes 1572872 | tf_op jit(solution)/shard_map/ppermute | solution.py:48
  106.8 24.8 %copy-start.17 = (bf16[64,4096]{1,0:T(8,128)(2,1)S(1)}, bf16[64,4096]{1,0:T(8,128)(2,1)}, u32[]{:S(2)}) copy-start(bf16[64,4096]{1,0:T(8,128)(2,1)} %copy-done.16) | copy-start | bytes 1572868
  106.8 8.3 %collective-permute-start.36 = (bf16[32,2048]{1,0:T(8,128)(2,1)S(1)}, bf16[32,2048]{1,0:T(8,128)(2,1)S(1)}, u32[]{:S(2)}, u32[]{:S(2)}) collective-permute-start(bf16[32,2048]{1,0:T(8,128)(2,1)S(1)} %maximum_select_fusion.1), channel_id=1, source_target_pairs={{0,1},{1,2},{2,3},{3,0},{4,5},{5,6},{6,7},{7,4},{8,9},{9,10},{10,1... | collective-permute-start | bytes 393224 | tf_op jit(solution)/shard_map/ppermute | solution.py:36
  109.5 10.8 %collective-permute-start.35 = (bf16[32,2048]{1,0:T(8,128)(2,1)S(1)}, bf16[32,2048]{1,0:T(8,128)(2,1)S(1)}, u32[]{:S(2)}, u32[]{:S(2)}) collective-permute-start(bf16[32,2048]{1,0:T(8,128)(2,1)S(1)} %maximum_select_fusion.1), channel_id=1, source_target_pairs={{0,2},{1,3},{2,0},{3,1},{4,6},{5,7},{6,4},{7,5},{8,10},{9,11},{10,... | collective-permute-start | bytes 393224 | tf_op jit(solution)/shard_map/ppermute | solution.py:36
  111.0 19.4 %collective-permute-start.34 = (bf16[32,2048]{1,0:T(8,128)(2,1)S(1)}, bf16[32,2048]{1,0:T(8,128)(2,1)S(1)}, u32[]{:S(2)}, u32[]{:S(2)}) collective-permute-start(bf16[32,2048]{1,0:T(8,128)(2,1)S(1)} %maximum_select_fusion.1), channel_id=1, source_target_pairs={{0,3},{1,0},{2,1},{3,2},{4,7},{5,4},{6,5},{7,6},{8,11},{9,8},{10,9... | collective-permute-start | bytes 393224 | tf_op jit(solution)/shard_map/ppermute | solution.py:36
  131.9 34.4 %copy-start.10 = (bf16[256,4096]{1,0:T(8,128)(2,1)}, bf16[256,4096]{1,0:T(8,128)(2,1)S(1)}, u32[]{:S(2)}) copy-start(bf16[256,4096]{1,0:T(8,128)(2,1)S(1)} %pad_maximum_fusion.xa_ref) | copy-start | bytes 6291460
  131.9 34.4 %collective-permute-start.8 = (bf16[256,4096]{1,0:T(8,128)(2,1)S(1)}, bf16[256,4096]{1,0:T(8,128)(2,1)}, u32[]{:S(2)}, u32[]{:S(2)}) collective-permute-start(bf16[256,4096]{1,0:T(8,128)(2,1)S(1)} %pad_maximum_fusion.xa_ref), channel_id=1, source_target_pairs={{0,4},{4,0},{1,5},{5,1},{2,6},{6,2},{3,7},{7,3},{8,12},{12,8},{9,1... | collective-permute-start | bytes 6291464 | tf_op jit(solution)/shard_map/ppermute | solution.py:30
  132.0 62.0 %collective-permute-start.31 = (bf16[3,512,256]{2,1,0:T(8,128)(2,1)S(1)}, bf16[3,512,256]{2,1,0:T(8,128)(2,1)S(1)}, u32[]{:S(2)}, u32[]{:S(2)}) collective-permute-start(bf16[3,512,256]{2,1,0:T(8,128)(2,1)S(1)} %pad_maximum_fusion.4), channel_id=1, source_target_pairs={{0,1},{1,2},{2,3},{3,0},{4,5},{5,6},{6,7},{7,4},{8,9},{9,10},{10,1... | collective-permute-start | bytes 2359304 | tf_op jit(solution)/shard_map/ppermute | solution.py:36
  132.0 61.9 %collective-permute-start.30 = (bf16[3,512,256]{2,1,0:T(8,128)(2,1)S(1)}, bf16[3,512,256]{2,1,0:T(8,128)(2,1)S(1)}, u32[]{:S(2)}, u32[]{:S(2)}) collective-permute-start(bf16[3,512,256]{2,1,0:T(8,128)(2,1)S(1)} %pad_maximum_fusion.4), channel_id=1, source_target_pairs={{0,2},{1,3},{2,0},{3,1},{4,6},{5,7},{6,4},{7,5},{8,10},{9,11},{10,... | collective-permute-start | bytes 2359304 | tf_op jit(solution)/shard_map/ppermute | solution.py:36
  133.8 31.3 %collective-permute-start.19 = (bf16[64,4096]{1,0:T(8,128)(2,1)S(1)}, bf16[64,4096]{1,0:T(8,128)(2,1)S(1)}, u32[]{:S(2)}, u32[]{:S(2)}) collective-permute-start(bf16[64,4096]{1,0:T(8,128)(2,1)S(1)} %copy-done.19), channel_id=1, source_target_pairs={{1,0},{5,4},{9,8},{13,12},{17,16},{21,20},{25,24},{29,28}} | collective-permute-start | bytes 1572872 | tf_op jit(solution)/shard_map/ppermute | solution.py:48
  135.1 30.0 %collective-permute-start.17 = (bf16[64,4096]{1,0:T(8,128)(2,1)}, bf16[64,4096]{1,0:T(8,128)(2,1)S(1)}, u32[]{:S(2)}, u32[]{:S(2)}) collective-permute-start(bf16[64,4096]{1,0:T(8,128)(2,1)} %collective-permute-done.16), channel_id=1, source_target_pairs={{2,3},{6,7},{10,11},{14,15},{18,19},{22,23},{26,27},{30,31}} | collective-permute-start | bytes 1572872 | tf_op jit(solution)/shard_map/ppermute | solution.py:47
  166.2 23.9 %copy-start.28 = (bf16[2048,3,256]{2,0,1:T(8,128)(2,1)S(1)}, bf16[2048,3,256]{2,0,1:T(8,128)(2,1)}, u32[]{:S(2)}) copy-start(bf16[2048,3,256]{2,0,1:T(8,128)(2,1)} %param.25) | copy-start | bytes 9437188
  190.0 30.3 %copy-start.2 = (bf16[256,4096]{1,0:T(8,128)(2,1)}, bf16[256,4096]{1,0:T(8,128)(2,1)S(1)}, u32[]{:S(2)}) copy-start(bf16[256,4096]{1,0:T(8,128)(2,1)S(1)} %get-tuple-element.28) | copy-start | bytes 6291460
  190.0 12.9 %collective-permute-start.9 = (bf16[256,4096]{1,0:T(8,128)(2,1)}, bf16[256,4096]{1,0:T(8,128)(2,1)}, u32[]{:S(2)}, u32[]{:S(2)}) collective-permute-start(bf16[256,4096]{1,0:T(8,128)(2,1)} %get-tuple-element.29), channel_id=1, source_target_pairs={{0,4},{4,0},{1,5},{5,1},{2,6},{6,2},{3,7},{7,3},{8,12},{12,8},{9,1... | collective-permute-start | bytes 6291464 | tf_op jit(solution)/shard_map/ppermute | solution.py:30
  191.9 3.5 collective-permute-start.37
  193.8 28.9 %collective-permute-start.20 = (bf16[256,4096]{1,0:T(8,128)(2,1)}, bf16[256,4096]{1,0:T(8,128)(2,1)}, u32[]{:S(2)}, u32[]{:S(2)}) collective-permute-start(bf16[256,4096]{1,0:T(8,128)(2,1)} %pad_maximum_fusion.1.xa_ref), channel_id=1, source_target_pairs={{0,4},{4,0},{1,5},{5,1},{2,6},{6,2},{3,7},{7,3},{8,12},{12,8},{9,1... | collective-permute-start | bytes 6291464 | tf_op jit(solution)/shard_map/ppermute | solution.py:30
  199.1 8.2 %collective-permute-start.38 = (bf16[32,2048]{1,0:T(8,128)(2,1)S(1)}, bf16[32,2048]{1,0:T(8,128)(2,1)S(1)}, u32[]{:S(2)}, u32[]{:S(2)}) collective-permute-start(bf16[32,2048]{1,0:T(8,128)(2,1)S(1)} %get-tuple-element.68), channel_id=1, source_target_pairs={{0,1},{1,2},{2,3},{3,0},{4,5},{5,6},{6,7},{7,4},{8,9},{9,10},{10,1... | collective-permute-start | bytes 393224 | tf_op jit(solution)/shard_map/ppermute | solution.py:84
  199.6 10.0 %collective-permute-start.40 = (bf16[32,2048]{1,0:T(8,128)(2,1)}, bf16[32,2048]{1,0:T(8,128)(2,1)S(1)}, u32[]{:S(2)}, u32[]{:S(2)}) collective-permute-start(bf16[32,2048]{1,0:T(8,128)(2,1)} %get-tuple-element.69), channel_id=1, source_target_pairs={{0,3},{1,0},{2,1},{3,2},{4,7},{5,4},{6,5},{7,6},{8,11},{9,8},{10,9... | collective-permute-start | bytes 393224 | tf_op jit(solution)/shard_map/ppermute | solution.py:84
  202.9 10.7 %collective-permute-start.39 = (bf16[32,2048]{1,0:T(8,128)(2,1)S(1)}, bf16[32,2048]{1,0:T(8,128)(2,1)}, u32[]{:S(2)}, u32[]{:S(2)}) collective-permute-start(bf16[32,2048]{1,0:T(8,128)(2,1)S(1)} %get-tuple-element.70), channel_id=1, source_target_pairs={{0,2},{1,3},{2,0},{3,1},{4,6},{5,7},{6,4},{7,5},{8,10},{9,11},{10,... | collective-permute-start | bytes 393224 | tf_op jit(solution)/shard_map/ppermute | solution.py:84
  205.5 9.1 %collective-permute-start.11 = (bf16[64,4096]{1,0:T(8,128)(2,1)}, bf16[64,4096]{1,0:T(8,128)(2,1)S(1)}, u32[]{:S(2)}, u32[]{:S(2)}) collective-permute-start(bf16[64,4096]{1,0:T(8,128)(2,1)} %get-tuple-element.64), channel_id=1, source_target_pairs={{3,2},{7,6},{11,10},{15,14},{19,18},{23,22},{27,26},{31,30}} | collective-permute-start | bytes 1572872 | tf_op jit(solution)/shard_map/ppermute | solution.py:75
  207.2 13.1 %collective-permute-start.10 = (bf16[64,4096]{1,0:T(8,128)(2,1)}, bf16[64,4096]{1,0:T(8,128)(2,1)}, u32[]{:S(2)}, u32[]{:S(2)}) collective-permute-start(bf16[64,4096]{1,0:T(8,128)(2,1)} %get-tuple-element.65), channel_id=1, source_target_pairs={{0,1},{4,5},{8,9},{12,13},{16,17},{20,21},{24,25},{28,29}} | collective-permute-start | bytes 1572872 | tf_op jit(solution)/shard_map/ppermute | solution.py:74
  222.7 26.4 %copy-start.14 = (bf16[16,4096]{1,0:T(8,128)(2,1)S(1)}, bf16[16,4096]{1,0:T(8,128)(2,1)}, u32[]{:S(2)}) copy-start(bf16[16,4096]{1,0:T(8,128)(2,1)} %param.23) | copy-start | bytes 393220
  222.7 26.6 %copy-start.27 = (f32[4096]{0:T(1024)S(1)}, f32[4096]{0:T(1024)}, u32[]{:S(2)}) copy-start(f32[4096]{0:T(1024)} %param.27) | copy-start | bytes 49156
  247.7 1.4 collective-permute-start.41
  247.8 33.8 %collective-permute-start.21 = (bf16[256,4096]{1,0:T(8,128)(2,1)}, bf16[256,4096]{1,0:T(8,128)(2,1)}, u32[]{:S(2)}, u32[]{:S(2)}) collective-permute-start(bf16[256,4096]{1,0:T(8,128)(2,1)} %get-tuple-element.38), channel_id=1, source_target_pairs={{0,4},{4,0},{1,5},{5,1},{2,6},{6,2},{3,7},{7,3},{8,12},{12,8},{9,1... | collective-permute-start | bytes 6291464 | tf_op jit(solution)/shard_map/ppermute | solution.py:30
  249.5 2.8 collective-permute-start.42
  252.3 11.0 %collective-permute-start.45 = (bf16[32,2048]{1,0:T(8,128)(2,1)S(1)}, bf16[32,2048]{1,0:T(8,128)(2,1)S(1)}, u32[]{:S(2)}, u32[]{:S(2)}) collective-permute-start(bf16[32,2048]{1,0:T(8,128)(2,1)S(1)} %maximum_select_fusion.2), channel_id=1, source_target_pairs={{0,1},{1,2},{2,3},{3,0},{4,5},{5,6},{6,7},{7,4},{8,9},{9,10},{10,1... | collective-permute-start | bytes 393224 | tf_op jit(solution)/shard_map/ppermute | solution.py:36
  254.8 26.8 %collective-permute-start.13 = (bf16[64,4096]{1,0:T(8,128)(2,1)}, bf16[64,4096]{1,0:T(8,128)(2,1)}, u32[]{:S(2)}, u32[]{:S(2)}) collective-permute-start(bf16[64,4096]{1,0:T(8,128)(2,1)} %get-tuple-element.62), channel_id=1, source_target_pairs={{2,1},{3,2},{6,5},{7,6},{10,9},{11,10},{14,13},{15,14},{18,17},{19... | collective-permute-start | bytes 1572872 | tf_op jit(solution)/shard_map/ppermute | solution.py:75
  256.3 25.3 %collective-permute-start.12 = (bf16[64,4096]{1,0:T(8,128)(2,1)S(1)}, bf16[64,4096]{1,0:T(8,128)(2,1)}, u32[]{:S(2)}, u32[]{:S(2)}) collective-permute-start(bf16[64,4096]{1,0:T(8,128)(2,1)S(1)} %get-tuple-element.63), channel_id=1, source_target_pairs={{0,1},{1,2},{4,5},{5,6},{8,9},{9,10},{12,13},{13,14},{16,17},{17,1... | collective-permute-start | bytes 1572872 | tf_op jit(solution)/shard_map/ppermute | solution.py:74
  262.5 18.0 %collective-permute-start.44 = (bf16[32,2048]{1,0:T(8,128)(2,1)S(1)}, bf16[32,2048]{1,0:T(8,128)(2,1)}, u32[]{:S(2)}, u32[]{:S(2)}) collective-permute-start(bf16[32,2048]{1,0:T(8,128)(2,1)S(1)} %maximum_select_fusion.2), channel_id=1, source_target_pairs={{0,2},{1,3},{2,0},{3,1},{4,6},{5,7},{6,4},{7,5},{8,10},{9,11},{10,... | collective-permute-start | bytes 393224 | tf_op jit(solution)/shard_map/ppermute | solution.py:36
  263.3 17.3 %collective-permute-start.43 = (bf16[32,2048]{1,0:T(8,128)(2,1)S(1)}, bf16[32,2048]{1,0:T(8,128)(2,1)}, u32[]{:S(2)}, u32[]{:S(2)}) collective-permute-start(bf16[32,2048]{1,0:T(8,128)(2,1)S(1)} %maximum_select_fusion.2), channel_id=1, source_target_pairs={{0,3},{1,0},{2,1},{3,2},{4,7},{5,4},{6,5},{7,6},{8,11},{9,8},{10,9... | collective-permute-start | bytes 393224 | tf_op jit(solution)/shard_map/ppermute | solution.py:36
  283.4 17.2 %collective-permute-start.23 = (bf16[64,4096]{1,0:T(8,128)(2,1)S(1)}, bf16[64,4096]{1,0:T(8,128)(2,1)}, u32[]{:S(2)}, u32[]{:S(2)}) collective-permute-start(bf16[64,4096]{1,0:T(8,128)(2,1)S(1)} %get-tuple-element.60), channel_id=1, source_target_pairs={{3,2},{7,6},{11,10},{15,14},{19,18},{23,22},{27,26},{31,30}} | collective-permute-start | bytes 1572872 | tf_op jit(solution)/shard_map/ppermute | solution.py:75
  284.9 17.3 %collective-permute-start.22 = (bf16[64,4096]{1,0:T(8,128)(2,1)S(1)}, bf16[64,4096]{1,0:T(8,128)(2,1)}, u32[]{:S(2)}, u32[]{:S(2)}) collective-permute-start(bf16[64,4096]{1,0:T(8,128)(2,1)S(1)} %get-tuple-element.61), channel_id=1, source_target_pairs={{0,1},{4,5},{8,9},{12,13},{16,17},{20,21},{24,25},{28,29}} | collective-permute-start | bytes 1572872 | tf_op jit(solution)/shard_map/ppermute | solution.py:74
  293.9 14.5 %collective-permute-start.15 = (bf16[64,4096]{1,0:T(8,128)(2,1)}, bf16[64,4096]{1,0:T(8,128)(2,1)S(1)}, u32[]{:S(2)}, u32[]{:S(2)}) collective-permute-start(bf16[64,4096]{1,0:T(8,128)(2,1)} %get-tuple-element.54), channel_id=1, source_target_pairs={{1,0},{2,1},{3,2},{5,4},{6,5},{7,6},{9,8},{10,9},{11,10},{13,12},{... | collective-permute-start | bytes 1572872 | tf_op jit(solution)/shard_map/ppermute | solution.py:75
  295.2 16.5 %collective-permute-start.14 = (bf16[64,4096]{1,0:T(8,128)(2,1)}, bf16[64,4096]{1,0:T(8,128)(2,1)}, u32[]{:S(2)}, u32[]{:S(2)}) collective-permute-start(bf16[64,4096]{1,0:T(8,128)(2,1)} %get-tuple-element.55), channel_id=1, source_target_pairs={{0,1},{1,2},{2,3},{4,5},{5,6},{6,7},{8,9},{9,10},{10,11},{12,13},{... | collective-permute-start | bytes 1572872 | tf_op jit(solution)/shard_map/ppermute | solution.py:74
  302.2 45.1 %collective-permute-start.29 = (bf16[4,2,3,512,256]{4,3,2,1,0:T(8,128)(2,1)}, bf16[4,2,3,512,256]{4,3,2,1,0:T(8,128)(2,1)}, u32[]{:S(2)}, u32[]{:S(2)}) collective-permute-start(bf16[4,2,3,512,256]{4,3,2,1,0:T(8,128)(2,1)} %bitcast.68), channel_id=1, source_target_pairs={{0,4},{4,0},{1,5},{5,1},{2,6},{6,2},{3,7},{7,3},{8,12},{12,8},{9,1... | collective-permute-start | bytes 18874376 | tf_op jit(solution)/shard_map/ppermute | solution.py:30
  302.2 45.1 %collective-permute-start.32 = (bf16[4,2,3,512,256]{4,3,2,1,0:T(8,128)(2,1)}, bf16[4,2,3,512,256]{4,3,2,1,0:T(8,128)(2,1)}, u32[]{:S(2)}, u32[]{:S(2)}) collective-permute-start(bf16[4,2,3,512,256]{4,3,2,1,0:T(8,128)(2,1)} %bitcast.73), channel_id=1, source_target_pairs={{0,4},{4,0},{1,5},{5,1},{2,6},{6,2},{3,7},{7,3},{8,12},{12,8},{9,1... | collective-permute-start | bytes 18874376 | tf_op jit(solution)/shard_map/ppermute | solution.py:30
  304.3 26.1 %copy-start.5 = (bf16[256,4096]{1,0:T(8,128)(2,1)S(1)}, bf16[256,4096]{1,0:T(8,128)(2,1)}, u32[]{:S(2)}) copy-start(bf16[256,4096]{1,0:T(8,128)(2,1)} %copy-done.4) | copy-start | bytes 6291460
  304.3 11.9 %collective-permute-start.46 = (f32[128,256]{1,0:T(8,128)S(1)}, f32[128,256]{1,0:T(8,128)S(1)}, u32[]{:S(2)}, u32[]{:S(2)}) collective-permute-start(f32[128,256]{1,0:T(8,128)S(1)} %fusion.31), channel_id=1, source_target_pairs={{0,4},{4,0},{1,5},{5,1},{2,6},{6,2},{3,7},{7,3},{8,12},{12,8},{9,1... | collective-permute-start | bytes 393224 | tf_op jit(solution)/shard_map/ppermute | solution.py:30
  308.4 9.9 %collective-permute-start.25 = (bf16[64,4096]{1,0:T(8,128)(2,1)S(1)}, bf16[64,4096]{1,0:T(8,128)(2,1)S(1)}, u32[]{:S(2)}, u32[]{:S(2)}) collective-permute-start(bf16[64,4096]{1,0:T(8,128)(2,1)S(1)} %get-tuple-element.58), channel_id=1, source_target_pairs={{2,1},{3,2},{6,5},{7,6},{10,9},{11,10},{14,13},{15,14},{18,17},{19... | collective-permute-start | bytes 1572872 | tf_op jit(solution)/shard_map/ppermute | solution.py:75
  311.7 17.4 %collective-permute-start.24 = (bf16[64,4096]{1,0:T(8,128)(2,1)S(1)}, bf16[64,4096]{1,0:T(8,128)(2,1)S(1)}, u32[]{:S(2)}, u32[]{:S(2)}) collective-permute-start(bf16[64,4096]{1,0:T(8,128)(2,1)S(1)} %get-tuple-element.59), channel_id=1, source_target_pairs={{0,1},{1,2},{4,5},{5,6},{8,9},{9,10},{12,13},{13,14},{16,17},{17,1... | collective-permute-start | bytes 1572872 | tf_op jit(solution)/shard_map/ppermute | solution.py:74
  316.2 15.8 %collective-permute-start.49 = (bf16[128,256]{1,0:T(8,128)(2,1)S(1)}, bf16[128,256]{1,0:T(8,128)(2,1)S(1)}, u32[]{:S(2)}, u32[]{:S(2)}) collective-permute-start(bf16[128,256]{1,0:T(8,128)(2,1)S(1)} %bitcast.89), channel_id=1, source_target_pairs={{0,1},{1,2},{2,3},{3,0},{4,5},{5,6},{6,7},{7,4},{8,9},{9,10},{10,1... | collective-permute-start | bytes 196616 | tf_op jit(solution)/shard_map/ppermute | solution.py:36
  318.3 15.0 %collective-permute-start.48 = (bf16[128,256]{1,0:T(8,128)(2,1)S(1)}, bf16[128,256]{1,0:T(8,128)(2,1)S(1)}, u32[]{:S(2)}, u32[]{:S(2)}) collective-permute-start(bf16[128,256]{1,0:T(8,128)(2,1)S(1)} %bitcast.90), channel_id=1, source_target_pairs={{0,2},{1,3},{2,0},{3,1},{4,6},{5,7},{6,4},{7,5},{8,10},{9,11},{10,... | collective-permute-start | bytes 196616 | tf_op jit(solution)/shard_map/ppermute | solution.py:36
  329.0 10.6 %collective-permute-start.47 = (bf16[128,256]{1,0:T(8,128)(2,1)S(1)}, bf16[128,256]{1,0:T(8,128)(2,1)S(1)}, u32[]{:S(2)}, u32[]{:S(2)}) collective-permute-start(bf16[128,256]{1,0:T(8,128)(2,1)S(1)} %bitcast.91), channel_id=1, source_target_pairs={{0,3},{1,0},{2,1},{3,2},{4,7},{5,4},{6,5},{7,6},{8,11},{9,8},{10,9... | collective-permute-start | bytes 196616 | tf_op jit(solution)/shard_map/ppermute | solution.py:36
  332.0 12.2 %collective-permute-start.27 = (bf16[64,4096]{1,0:T(8,128)(2,1)S(1)}, bf16[64,4096]{1,0:T(8,128)(2,1)S(1)}, u32[]{:S(2)}, u32[]{:S(2)}) collective-permute-start(bf16[64,4096]{1,0:T(8,128)(2,1)S(1)} %get-tuple-element.56), channel_id=1, source_target_pairs={{1,0},{2,1},{3,2},{5,4},{6,5},{7,6},{9,8},{10,9},{11,10},{13,12},{... | collective-permute-start | bytes 1572872 | tf_op jit(solution)/shard_map/ppermute | solution.py:75
  333.3 11.3 %collective-permute-start.26 = (bf16[64,4096]{1,0:T(8,128)(2,1)S(1)}, bf16[64,4096]{1,0:T(8,128)(2,1)S(1)}, u32[]{:S(2)}, u32[]{:S(2)}) collective-permute-start(bf16[64,4096]{1,0:T(8,128)(2,1)S(1)} %get-tuple-element.57), channel_id=1, source_target_pairs={{0,1},{1,2},{2,3},{4,5},{5,6},{6,7},{8,9},{9,10},{10,11},{12,13},{... | collective-permute-start | bytes 1572872 | tf_op jit(solution)/shard_map/ppermute | solution.py:74
  347.0 26.2 %slice-start.2 = ((s8[6291456]{0:T(1024)(128)(4,1)}), s8[4194304]{0:T(1024)(128)(4,1)S(1)}, s32[]{:S(2)}) async-start(s8[6291456]{0:T(1024)(128)(4,1)} %bitcast.75), calls=%async_computation.5 | async-start | bytes 8388608
  347.3 25.9 %slice-start.3 = ((s8[6291456]{0:T(1024)(128)(4,1)}), s8[2097152]{0:T(1024)(128)(4,1)S(1)}, s32[]{:S(2)}) async-start(s8[6291456]{0:T(1024)(128)(4,1)} %bitcast.75), calls=%async_computation.6 | async-start | bytes 4194304
  347.3 25.9 %copy-start.6 = (s32[16,1024]{1,0:T(8,128)S(1)}, s32[16,1024]{1,0:T(8,128)}, u32[]{:S(2)}) copy-start(s32[16,1024]{1,0:T(8,128)} %words_ref.1) | copy-start | bytes 196612
  (21 other events, 139.5 us)
Sparse Core Ops, SparseCore 0:
  104.5 71.7 all-gather.4
  195.5 68.4 all-gather.6

commit v5 on v3

--- a/solution.py
+++ b/solution.py
@@ -10,7 +10,6 @@
 HD = 256
 F32 = jnp.float32
 BF16 = jnp.bfloat16
-CHUNKS = 2
 
 
 def norm_rows(x, gain):
@@ -37,34 +36,28 @@
     ]
 
 
-def line_slots(value):
-    count, tensor = lax.axis_size("tensor"), lax.axis_index("tensor")
-    above, below = [value], [value]
-    for step in range(1, count):
-        above.append(lax.ppermute(above[-1], "tensor", [(i, i + 1) for i in range(step - 1, count - 1)]))
-        below.append(lax.ppermute(below[-1], "tensor", [(i, i - 1) for i in range(1, count - step + 1)]))
-    return [value] + [jnp.where(tensor + o < count, below[o], above[count - o]) for o in range(1, count)]
-
-
-def line_sum(mine, got):
+def gated(value, *others):
+    return lax.optimization_barrier((value,) + others)[0]
+
+
+def slot_sum(mine, got, slot):
+    block = mine.shape[0] // lax.axis_size("tensor")
+    at = slice(slot * block, (slot + 1) * block)
+    return mine[at].astype(F32) + got[at].astype(F32)
+
+
+def sum_sends(mine, got, came, step):
+    up, down = slot_sum(mine, got, lax.axis_size("tensor") - step), slot_sum(mine, got, step)
+    if came is not None:
+        up, down = up + came[0].astype(F32), down + came[1].astype(F32)
+    return up.astype(BF16), down.astype(BF16)
+
+
+def sum_step(sends, step):
     count = lax.axis_size("tensor")
-    block = mine.shape[0] // count
-
-    def part(slot):
-        at = slice(slot * block, (slot + 1) * block)
-        return mine[at].astype(F32) + got[at].astype(F32)
-
-    above, below = None, None
-    for step in range(1, count):
-        send_up, send_down = part(count - step), part(step)
-        if step > 1:
-            send_up = send_up + above.astype(F32)
-            send_down = send_down + below.astype(F32)
-        above = lax.ppermute(send_up.astype(BF16), "tensor", [(i, i + 1) for i in range(step)])
-        below = lax.ppermute(
-            send_down.astype(BF16), "tensor", [(i, i - 1) for i in range(count - step, count)]
-        )
-    return part(0) + above.astype(F32) + below.astype(F32)
+    above = lax.ppermute(sends[0], "tensor", [(i, i + 1) for i in range(step)])
+    below = lax.ppermute(sends[1], "tensor", [(i, i - 1) for i in range(count - step, count)])
+    return lax.optimization_barrier((above, below))
 
 
 def slots_sum(product):
@@ -109,15 +102,18 @@
     return 0.5 * x * (1.0 + jnp.tanh(0.7978845608028654 * (x + 0.044715 * x * x * x)))
 
 
-def ffn_kernel(hidden_steps, xa_ref, xb_ref, gate_ref, up_ref, down_ref, ya_ref, yb_ref, x, hidden):
+def ffn_kernel(hidden_steps, order, x_ref, gate_ref, up_ref, down_ref, ya_ref, yb_ref, x, hidden):
     step = pl.program_id(0)
-    rows = xa_ref.shape[0]
+    rows = ya_ref.shape[0]
     width = gate_ref.shape[1]
+    blocks = order.shape[0]
+    block = 2 * rows // blocks
 
     @pl.when(step == 0)
     def _():
-        x[:rows, :] = xa_ref[...]
-        x[rows:, :] = xb_ref[...]
+        for slot in range(blocks):
+            at = pl.multiple_of(order[slot] * block, block)
+            x[slot * block : (slot + 1) * block, :] = x_ref[pl.ds(at, block), :]
 
     @pl.when(step < hidden_steps)
     def _():
@@ -136,34 +132,36 @@
         yb_ref[...] = total[rows:].astype(BF16)
 
 
-def ffn(xa, xb, w_gate, w_up, w_down):
-    rows, features = xa.shape
+def ffn(x, order, w_gate, w_up, w_down):
+    rows, features = x.shape
     units = w_gate.shape[1]
     width = min(256, units)
     tile = 512
     first, last = units // width, features // tile
     return pl.pallas_call(
         functools.partial(ffn_kernel, first),
-        grid=(first + last,),
-        in_specs=[
-            pl.BlockSpec((rows, features), lambda i: (0, 0)),
-            pl.BlockSpec((rows, features), lambda i: (0, 0)),
-            pl.BlockSpec((features, width), lambda i: (0, jnp.minimum(i, first - 1))),
-            pl.BlockSpec((features, width), lambda i: (0, jnp.minimum(i, first - 1))),
-            pl.BlockSpec((units, tile), lambda i: (0, jnp.maximum(i - first, 0))),
-        ],
-        out_specs=[pl.BlockSpec((rows, tile), lambda i: (0, jnp.maximum(i - first, 0)))] * 2,
-        out_shape=[jax.ShapeDtypeStruct((rows, features), BF16)] * 2,
-        scratch_shapes=[
-            pltpu.VMEM((2 * rows, features), BF16),
-            pltpu.VMEM((first, 2 * rows, width), BF16),
-        ],
+        grid_spec=pltpu.PrefetchScalarGridSpec(
+            num_scalar_prefetch=1,
+            grid=(first + last,),
+            in_specs=[
+                pl.BlockSpec((rows, features), lambda i, t: (0, 0), pipeline_mode=pl.Buffered(1)),
+                pl.BlockSpec((features, width), lambda i, t: (0, jnp.minimum(i, first - 1))),
+                pl.BlockSpec((features, width), lambda i, t: (0, jnp.minimum(i, first - 1))),
+                pl.BlockSpec((units, tile), lambda i, t: (0, jnp.maximum(i - first, 0))),
+            ],
+            out_specs=[pl.BlockSpec((rows // 2, tile), lambda i, t: (0, jnp.maximum(i - first, 0)))] * 2,
+            scratch_shapes=[
+                pltpu.VMEM((rows, features), BF16),
+                pltpu.VMEM((first, rows, width), BF16),
+            ],
+        ),
+        out_shape=[jax.ShapeDtypeStruct((rows // 2, features), BF16)] * 2,
         compiler_params=pltpu.CompilerParams(vmem_limit_bytes=48 * 2**20),
         cost_estimate=pl.CostEstimate(
-            flops=12 * rows * features * units, bytes_accessed=6 * features * units, transcendentals=0
+            flops=6 * rows * features * units, bytes_accessed=6 * features * units, transcendentals=0
         ),
         name="ffn",
-    )(xa, xb, w_gate, w_up, w_down)
+    )(order, x, w_gate, w_up, w_down)
 
 
 def per_device(
@@ -187,24 +185,23 @@
     section = lax.axis_index("section")
     count, tensor = lax.axis_size("tensor"), lax.axis_index("tensor")
     rows = target.shape[0]
-    after = lax.optimization_barrier
-
-    selfin = norm_rows(target, self_gain).astype(BF16)
-    selfin = gather_half(selfin, section)
+    slot_chip = lax.rem(tensor + jnp.arange(count, dtype=jnp.int32), count)
+    order = jnp.concatenate([section * count + slot_chip, (1 - section) * count + slot_chip])
+
+    selfin = gather_half(norm_rows(target, self_gain).astype(BF16), section)
 
     normed = norm_rows(source, enc_gain).astype(BF16)
-    block = normed.shape[0] // CHUNKS
+    block = normed.shape[0] // 2
     near = [
-        jnp.concatenate(line_slots(normed[c * block : (c + 1) * block]), 0) for c in range(CHUNKS)
+        lax.all_gather(normed[c * block : (c + 1) * block], ("section", "tensor"), axis=0, tiled=True)
+        for c in range(2)
     ]
-    far = [swap(x, "section", 1) for x in near]
     kv = jnp.transpose(cross_kv, (1, 0, 2))
     kv = in_order(kv, swap(kv, "section", 1), section, 1)
 
     qkv_w = jnp.transpose(self_qkv, (1, 0, 2))
     q, k, v = [jnp.dot(selfin, qkv_w[i], preferred_element_type=F32) for i in range(3)]
     q, k, v = [y.astype(BF16) for y in both_halves(jnp.stack([q, k, v]))]
-    slot_chip = lax.rem(tensor + jnp.arange(count, dtype=jnp.int32), count)
     positions = (
         (jnp.arange(2, dtype=jnp.int32)[None, :] * count + slot_chip[:, None])[:, :, None] * rows
         + jnp.arange(rows, dtype=jnp.int32)
@@ -217,29 +214,47 @@
     product = jnp.dot(context, self_out, preferred_element_type=F32).astype(BF16)
     total = slots_sum(product)
 
-    shares = [ffn(near[0], far[0], w_gate, w_up, w_down)]
-    total, first = after((total, shares[0][0]))
-    shares[0] = (first, shares[0][1])
+    mine, theirs = ffn(near[0], order, w_gate, w_up, w_down)
+    got = swap(theirs, "section", 1)
+    came = sum_step(sum_sends(mine, got, None, 1), 1)
+    total = gated(total, *came)
     mid = (target.astype(F32) + whole_rows(total, section)).astype(BF16)
     crossin = gather_half(norm_rows(mid, cross_gain).astype(BF16), section)
-    for c in range(1, CHUNKS):
-        shares.append(ffn(near[c], far[c], w_gate, w_up, w_down))
-    crossin, last = after((crossin, shares[-1][0]))
-    shares[-1] = (last, shares[-1][1])
+    for step in range(2, count - 1):
+        came = sum_step(sum_sends(mine, got, came, step), step)
+    sends = sum_sends(mine, got, came, count - 1)
+    came = sum_step(sends, count - 1)
+    mine_b, theirs_b = ffn(gated(near[1], *sends), order, w_gate, w_up, w_down)
+
+    def finish_rows(c, mine, got, came):
+        at = slice(c * block, (c + 1) * block)
+        total = slot_sum(mine, got, 0) + came[0].astype(F32) + came[1].astype(F32)
+        out = (source[at].astype(F32) + keep_factor(enc_keep[at]) * total).astype(BF16)
+        memory = norm_rows(out, final_gain).astype(BF16)
+        return out, memory
+
+    def to_heads(memory):
+        return lax.all_gather(memory, "tensor", axis=0, tiled=True)
+
+    def keys_values(memory):
+        return [jnp.dot(memory, kv[i], preferred_element_type=F32).astype(BF16) for i in range(2)]
+
+    out_a, memory_a = finish_rows(0, mine, got, came)
+    memory_a, mine_b = lax.optimization_barrier((memory_a, mine_b))
+    memory_a = to_heads(memory_a)
+    got = swap(theirs_b, "section", 1)
+    came = sum_step(sum_sends(mine_b, got, None, 1), 1)
+    crossin = gated(crossin, *came)
     cq = both_halves(jnp.dot(crossin, cross_q, preferred_element_type=F32)).astype(BF16)
-
-    outs, keys, values = [], [], []
-    for c, (ya, yb) in enumerate(shares):
-        at = slice(c * block, (c + 1) * block)
-        total = line_sum(ya, swap(yb, "section", 1))
-        out = (source[at].astype(F32) + keep_factor(enc_keep[at]) * total).astype(BF16)
-        outs.append(out)
-        memory = norm_rows(out, final_gain).astype(BF16)
-        memory = jnp.concatenate(line_slots(memory), 0)
-        keys.append(jnp.dot(memory, kv[0], preferred_element_type=F32).astype(BF16))
-        values.append(jnp.dot(memory, kv[1], preferred_element_type=F32).astype(BF16))
-    enc_out = jnp.concatenate(outs, 0)
-    keys, values = jnp.concatenate(keys, 0), jnp.concatenate(values, 0)
+    for step in range(2, count):
+        came = sum_step(sum_sends(mine_b, got, came, step), step)
+    out_b, memory_b = finish_rows(1, mine_b, got, came)
+    memory_b = to_heads(memory_b)
+    memory_a = gated(memory_a, out_b)
+    keys_a, values_a = keys_values(memory_a)
+    keys_b, values_b = keys_values(memory_b)
+    enc_out = jnp.concatenate([out_a, out_b], 0)
+    keys, values = jnp.concatenate([keys_a, keys_b], 0), jnp.concatenate([values_a, values_b], 0)
 
     scores = lax.dot_general(cq, keys, (((1,), (1,)), ((), ())), preferred_element_type=F32) * (1.0 / 16.0)
     top = jnp.max(scores, axis=-1, keepdims=True)

time: 377 us -> 364 us (0.966)
  starting transfers between devices: 93.9 us -> 43.8 us
  between operations: 1.8 us -> 14.5 us
  other arithmetic: 22 us -> 34.6 us
  local copies, waits for them, and re-layouts: 3.31 us -> 14.3 us
  waiting for transfers between devices: 199 us -> 193 us
  Pallas kernels: 45.3 us -> 49.3 us
    ppermute x36 -> x12, waiting for transfers between devices: 145 us -> 68.6 us  [the longest x6 48.5 us: sum_step(): above = lax.ppermute(sends[0], 'tensor', [(i, i + 1) for i in range(step)])]
    all_gather x0 -> x4, waiting for transfers between devices: none -> 64 us  [the longest x2 48.9 us: per_device(): lax.all_gather(normed[c * block:(c + 1) * block], ('section', 'tensor'),...]
    ppermute x36 -> x12, starting transfers between devices: 74.6 us -> 28.8 us  [the longest x6 21.8 us: sum_step(): above = lax.ppermute(sends[0], 'tensor', [(i, i + 1) for i in range(step)])]
    ppermute x6, waiting for transfers between devices: 28.4 us -> 47.3 us  [from_slots(): lax.ppermute(value, 'tensor', [(i, (i - o) % count) for i in range(count)])]
    convert_element_type x12 -> x9, other arithmetic: 3.21 us -> 14.6 us  [the longest x6 12.6 us: sum_sends(): return (up.astype(BF16), down.astype(BF16))]
    ppermute x6, waiting for transfers between devices: 18.5 us -> 8.92 us  [slots_sum(): lax.ppermute(product[o], 'tensor', [(i, (i + o) % count) for i in range(c...]
    dot_general x4, matrix products: 2.86 us -> 9.19 us  [keys_values(): jnp.dot(memory, kv[i], preferred_element_type=F32).astype(BF16)]
    unnamed x46 -> x64, local copies, waits for them, and re-layouts: 2.32 us -> 8.49 us
  transfers between devices with their start and end apart: 60 -> 38, of which waited for: 31 -> 19; matrix products, arithmetic and copies ran while one was open for 8% -> 14% of each run, Pallas kernels for 12% -> 14%
where the time goes in v5:
time: 364 us; the launch traced here: 363 us
  waiting for transfers between devices  193 us (53%)
  Pallas kernels  49.3 us (14%)
  starting transfers between devices  43.8 us (12%)
  other arithmetic  34.6 us (10%)
  between operations  14.5 us (4%)
  local copies, waits for them, and re-layouts  14.3 us (4%)
  matrix products  13.7 us (4%)
    pallas_call x2, Pallas kernels, ffn(): pl.pallas_call(functools.partial(ffn_kernel, first), grid_spec=pltpu.Pref...  49.3 us
    all_gather x2, waiting for transfers between devices, per_device(): lax.all_gather(normed[c * block:(c + 1) * block], ('section', 'tensor'),...  48.9 us
    ppermute x6, waiting for transfers between devices, sum_step(): above = lax.ppermute(sends[0], 'tensor', [(i, i + 1) for i in range(step)])  48.5 us
    ppermute x6, waiting for transfers between devices, from_slots(): lax.ppermute(value, 'tensor', [(i, (i - o) % count) for i in range(count)])  47.3 us
    ppermute x6, starting transfers between devices, sum_step(): above = lax.ppermute(sends[0], 'tensor', [(i, i + 1) for i in range(step)])  21.8 us
    ppermute x6, waiting for transfers between devices, sum_step(): lax.ppermute(sends[1], 'tensor', [(i, i - 1) for i in range(count - step,...  20.2 us
    all_gather x2, waiting for transfers between devices, to_heads(): return lax.all_gather(memory, 'tensor', axis=0, tiled=True)  15 us
    convert_element_type x6, other arithmetic, sum_sends(): return (up.astype(BF16), down.astype(BF16))  12.6 us
  transfers between devices with their start and end apart: 38, of which 19 were waited for; matrix products, arithmetic and copies ran while one was open for 14% of the time, Pallas kernels for 14%

profile of v5, /device:TPU:0, one launch (start us, length us, event | category | flops | bytes accessed | tf_op | source)
XLA Modules:
  0.0 363.0 jit_solution(6313965030926168261)
XLA Ops:
  7.2 1.6 fusion
  8.8 1.6 fusion.2
  10.4 1.0 fusion.64
  12.6 48.9 %all-gather.5.cloned.1.call-done.x_ref = bf16[512,4096]{1,0:T(8,128)(2,1)} async-done(((bf16[64,4096]{1,0:T(8,128)(2,1)}), bf16[512,4096]{1,0:T(8,128)(2,1)}) %all-gather.5.cloned.1.call-update) | async-done | bytes 4194320 | tf_op jit(solution)/shard_map/all_gather | solution.py:196
  61.5 24.7 %ffn.2 = (bf16[256,4096]{1,0:T(8,128)(2,1)S(1)}, bf16[256,4096]{1,0:T(8,128)(2,1)}) custom-call(s32[8]{0:T(128)S(1)} %pad_add_fusion.order, bf16[512,4096]{1,0:T(8,128)(2,1)} %all-gather.5.cloned.1.call-done.x_ref, bf16[4096,1024]{1,0:T(8,128)(2,1)} %gate_ref.3, bf16[4096,1024]{1,0:T(8,128)(2,1)} %up_ref.3, bf16[1024,4096]{1,0:T(8,128)(2,1)} %down_ref.3), custom_call_target="tpu_custom_call" | custom-call | flops 12884901888 | bytes 25165824 | tf_op jit(solution)/shard_map/ffn/pallas_call | solution.py:141
  86.6 0.9 constant_dynamic-slice_fusion.7
  88.5 1.9 fusion.67
  90.7 1.4 fusion.18
  92.1 2.0 collective-permute-start.1
  94.8 0.9 maximum_select_fusion.3
  95.8 2.5 collective-permute-start.15
  99.0 19.4 %collective-permute-done.15 = bf16[32,2048]{1,0:T(8,128)(2,1)S(1)} collective-permute-done((bf16[32,2048]{1,0:T(8,128)(2,1)S(1)}, bf16[32,2048]{1,0:T(8,128)(2,1)S(1)}, u32[]{:S(2)}, u32[]{:S(2)}) %collective-permute-start.15) | collective-permute-done | bytes 131104 | tf_op jit(solution)/shard_map/ppermute | solution.py:35
  118.4 2.8 collective-permute-done.16
  121.2 6.3 %collective-permute-done.17 = bf16[32,2048]{1,0:T(8,128)(2,1)S(1)} collective-permute-done((bf16[32,2048]{1,0:T(8,128)(2,1)S(1)}, bf16[32,2048]{1,0:T(8,128)(2,1)S(1)}, u32[]{:S(2)}, u32[]{:S(2)}) %collective-permute-start.17) | collective-permute-done | bytes 131104 | tf_op jit(solution)/shard_map/ppermute | solution.py:35
  127.8 1.4 add_convert_fusion.8
  129.2 1.3 collective-permute-start.3
  131.9 0.8 pad_maximum_fusion.3
  132.7 9.3 %collective-permute-done.3 = bf16[64,4096]{1,0:T(8,128)(2,1)S(1)} collective-permute-done((bf16[64,4096]{1,0:T(8,128)(2,1)S(1)}, bf16[64,4096]{1,0:T(8,128)(2,1)S(1)}, u32[]{:S(2)}, u32[]{:S(2)}) %collective-permute-start.3) | collective-permute-done | bytes 524320 | tf_op jit(solution)/shard_map/ppermute | solution.py:58
  142.0 2.7 add_convert_fusion.6
  144.7 24.7 %ffn.3 = (bf16[256,4096]{1,0:T(8,128)(2,1)S(1)}, bf16[256,4096]{1,0:T(8,128)(2,1)}) custom-call(s32[8]{0:T(128)S(1)} %pad_add_fusion.order, bf16[512,4096]{1,0:T(8,128)(2,1)} %all-gather.7.cloned.1.call-done.x_ref, bf16[4096,1024]{1,0:T(8,128)(2,1)} %gate_ref.3, bf16[4096,1024]{1,0:T(8,128)(2,1)} %up_ref.3, bf16[1024,4096]{1,0:T(8,128)(2,1)} %down_ref.3), custom_call_target="tpu_custom_call" | custom-call | flops 12884901888 | bytes 25165824 | tf_op jit(solution)/shard_map/ffn/pallas_call | solution.py:141
  169.4 1.3 copy.36
  171.1 1.6 copy.29
  172.7 5.4 %collective-permute-start.5 = (bf16[64,4096]{1,0:T(8,128)(2,1)}, bf16[64,4096]{1,0:T(8,128)(2,1)S(1)}, u32[]{:S(2)}, u32[]{:S(2)}) collective-permute-start(bf16[64,4096]{1,0:T(8,128)(2,1)} %get-tuple-element.59), channel_id=1, source_target_pairs={{0,1},{1,2},{2,3},{4,5},{5,6},{6,7},{8,9},{9,10},{10,11},{12,13},{... | collective-permute-start | bytes 1572872 | tf_op jit(solution)/shard_map/ppermute | solution.py:58
  178.1 1.3 collective-permute-start.6
  179.5 1.1 add_convert_fusion.10
  180.8 9.5 %collective-permute-done.5 = bf16[64,4096]{1,0:T(8,128)(2,1)S(1)} collective-permute-done((bf16[64,4096]{1,0:T(8,128)(2,1)}, bf16[64,4096]{1,0:T(8,128)(2,1)S(1)}, u32[]{:S(2)}, u32[]{:S(2)}) %collective-permute-start.5) | collective-permute-done | bytes 524320 | tf_op jit(solution)/shard_map/ppermute | solution.py:58
  190.3 4.0 %collective-permute-done.6 = bf16[64,4096]{1,0:T(8,128)(2,1)S(1)} collective-permute-done((bf16[64,4096]{1,0:T(8,128)(2,1)}, bf16[64,4096]{1,0:T(8,128)(2,1)S(1)}, u32[]{:S(2)}, u32[]{:S(2)}) %collective-permute-start.6) | collective-permute-done | bytes 524320 | tf_op jit(solution)/shard_map/ppermute | solution.py:59
  194.3 2.4 fusion.12
  197.5 1.0 fusion.14
  198.5 2.4 fusion.20
  200.9 3.0 collective-permute-start.8
  203.8 1.5 collective-permute-start.9
  205.3 2.1 convolution_convert_fusion.1
  207.4 1.1 fusion.66
  208.5 1.1 collective-permute-start.20
  209.6 2.7 collective-permute-start.21
  212.3 3.3 collective-permute-done.8
  215.7 2.6 add_convert_fusion.3
  218.3 5.2 %collective-permute-start.10 = (bf16[64,4096]{1,0:T(8,128)(2,1)}, bf16[64,4096]{1,0:T(8,128)(2,1)}, u32[]{:S(2)}, u32[]{:S(2)}) collective-permute-start(bf16[64,4096]{1,0:T(8,128)(2,1)} %get-tuple-element.55), channel_id=1, source_target_pairs={{0,1},{1,2},{4,5},{5,6},{8,9},{9,10},{12,13},{13,14},{16,17},{17,1... | collective-permute-start | bytes 1572872 | tf_op jit(solution)/shard_map/ppermute | solution.py:58
  223.5 1.5 collective-permute-start.11
  225.0 1.0 convert_add_fusion.9
  226.1 7.9 %collective-permute-done.10 = bf16[64,4096]{1,0:T(8,128)(2,1)} collective-permute-done((bf16[64,4096]{1,0:T(8,128)(2,1)}, bf16[64,4096]{1,0:T(8,128)(2,1)}, u32[]{:S(2)}, u32[]{:S(2)}) %collective-permute-start.10) | collective-permute-done | bytes 524320 | tf_op jit(solution)/shard_map/ppermute | solution.py:58
  234.1 2.0 add_convert_fusion.1
  236.1 5.0 %collective-permute-start.12 = (bf16[64,4096]{1,0:T(8,128)(2,1)S(1)}, bf16[64,4096]{1,0:T(8,128)(2,1)S(1)}, u32[]{:S(2)}, u32[]{:S(2)}) collective-permute-start(bf16[64,4096]{1,0:T(8,128)(2,1)S(1)} %get-tuple-element.53), channel_id=1, source_target_pairs={{0,1},{1,2},{2,3},{4,5},{5,6},{6,7},{8,9},{9,10},{10,11},{12,13},{... | collective-permute-start | bytes 1572872 | tf_op jit(solution)/shard_map/ppermute | solution.py:58
  241.1 1.4 collective-permute-start.13
  242.5 1.6 copy.35
  245.3 18.4 %collective-permute-done.12 = bf16[64,4096]{1,0:T(8,128)(2,1)S(1)} collective-permute-done((bf16[64,4096]{1,0:T(8,128)(2,1)S(1)}, bf16[64,4096]{1,0:T(8,128)(2,1)S(1)}, u32[]{:S(2)}, u32[]{:S(2)}) %collective-permute-start.12) | collective-permute-done | bytes 524320 | tf_op jit(solution)/shard_map/ppermute | solution.py:58
  263.7 16.1 %collective-permute-done.13 = bf16[64,4096]{1,0:T(8,128)(2,1)S(1)} collective-permute-done((bf16[64,4096]{1,0:T(8,128)(2,1)S(1)}, bf16[64,4096]{1,0:T(8,128)(2,1)S(1)}, u32[]{:S(2)}, u32[]{:S(2)}) %collective-permute-start.13) | collective-permute-done | bytes 524320 | tf_op jit(solution)/shard_map/ppermute | solution.py:59
  279.8 1.7 fusion.15
  282.4 1.0 fusion.17
  283.6 1.2 collective-permute-done.23
  284.9 2.8 collective-permute-start.25
  287.7 6.0 %maximum_select_fusion = bf16[2,4096,256]{2,1,0:T(8,128)(2,1)} fusion(bf16[2,2048,256]{2,1,0:T(8,128)(2,1)} %collective-permute-done.28, bf16[2,2048,256]{2,1,0:T(8,128)(2,1)} %bitcast.89, pred[]{:T(512)S(6)} %eq.21), kind=kLoop, calls=%fused_computation | loop fusion | flops 18874368 | bytes 8388609 | tf_op jit(solution)/shard_map/jit(_where)/select_n | solution.py:79
  293.8 18.9 %collective-permute-done.25 = bf16[32,2048]{1,0:T(8,128)(2,1)S(1)} collective-permute-done((bf16[32,2048]{1,0:T(8,128)(2,1)S(1)}, bf16[32,2048]{1,0:T(8,128)(2,1)S(1)}, u32[]{:S(2)}, u32[]{:S(2)}) %collective-permute-start.25) | collective-permute-done | bytes 131104 | tf_op jit(solution)/shard_map/ppermute | solution.py:35
  313.2 3.1 fusion.7
  316.6 2.3 fusion.9
  318.9 15.0 %all-gather.11.cloned.1.call-done = bf16[256,4096]{1,0:T(8,128)(2,1)} async-done(((bf16[64,4096]{1,0:T(8,128)(2,1)}), bf16[256,4096]{1,0:T(8,128)(2,1)}) %all-gather.11.cloned.1.call-update) | async-done | bytes 2097168 | tf_op jit(solution)/shard_map/all_gather | solution.py:237
  334.0 3.1 fusion.10
  339.3 1.5 collective-permute-done.29
  341.3 1.8 collective-permute-start.31
  343.1 2.0 collective-permute-start.32
  345.3 4.2 %collective-permute-done.30 = bf16[32,2048]{1,0:T(8,128)(2,1)S(1)} collective-permute-done((bf16[32,2048]{1,0:T(8,128)(2,1)S(1)}, bf16[32,2048]{1,0:T(8,128)(2,1)S(1)}, u32[]{:S(2)}, u32[]{:S(2)}) %collective-permute-start.30) | collective-permute-done | bytes 131104 | tf_op jit(solution)/shard_map/ppermute | solution.py:68
  349.6 4.7 %collective-permute-done.31 = bf16[32,2048]{1,0:T(8,128)(2,1)S(1)} collective-permute-done((bf16[32,2048]{1,0:T(8,128)(2,1)S(1)}, bf16[32,2048]{1,0:T(8,128)(2,1)S(1)}, u32[]{:S(2)}, u32[]{:S(2)}) %collective-permute-start.31) | collective-permute-done | bytes 131104 | tf_op jit(solution)/shard_map/ppermute | solution.py:68
  354.4 1.1 pad_maximum_fusion
  (152 shorter events, 14.5 us)
Async XLA Ops:
  7.2 198.1 %copy-start = (bf16[256,2048]{1,0:T(8,128)(2,1)S(1)}, bf16[256,2048]{1,0:T(8,128)(2,1)}, u32[]{:S(2)}) copy-start(bf16[256,2048]{1,0:T(8,128)(2,1)} %param.26) | copy-start | bytes 3145732
  7.2 54.3 %all-gather.5.cloned.1.call-start = ((), (), s32[]{:S(2)}) async-start(), calls=%async_computation | async-start | bytes 4718592 | tf_op jit(solution)/shard_map/all_gather | solution.py:196
  10.4 1.9 copy-start.10
  11.5 133.2 %all-gather.7.cloned.1.call-start = ((), (), s32[]{:S(2)}) async-start(), calls=%async_computation.1 | async-start | bytes 4718592 | tf_op jit(solution)/shard_map/all_gather | solution.py:196
  12.2 300.9 %all-gather.9.cloned.1.call-start = ((), (), s32[]{:S(2)}) async-start(), calls=%async_computation.2 | async-start | bytes 2621440 | tf_op jit(solution)/shard_map/all_gather | solution.py:237
  12.5 73.9 %copy-start.25 = (f32[4096]{0:T(1024)S(1)}, f32[4096]{0:T(1024)}, u32[]{:S(2)}) copy-start(f32[4096]{0:T(1024)} %param.24) | copy-start | bytes 49156
  86.2 55.8 %copy-start.1 = (bf16[256,4096]{1,0:T(8,128)(2,1)}, bf16[256,4096]{1,0:T(8,128)(2,1)S(1)}, u32[]{:S(2)}) copy-start(bf16[256,4096]{1,0:T(8,128)(2,1)S(1)} %get-tuple-element.24) | copy-start | bytes 6291460
  86.2 4.5 %collective-permute-start = (bf16[256,4096]{1,0:T(8,128)(2,1)}, bf16[256,4096]{1,0:T(8,128)(2,1)}, u32[]{:S(2)}, u32[]{:S(2)}) collective-permute-start(bf16[256,4096]{1,0:T(8,128)(2,1)} %get-tuple-element.25), channel_id=1, source_target_pairs={{0,4},{4,0},{1,5},{5,1},{2,6},{6,2},{3,7},{7,3},{8,12},{12,8},{9,1... | collective-permute-start | bytes 6291464 | tf_op jit(solution)/shard_map/ppermute | solution.py:29
  87.5 7.3 %collective-permute-start.14 = (bf16[16,2048]{1,0:T(8,128)(2,1)}, bf16[16,2048]{1,0:T(8,128)(2,1)}, u32[]{:S(2)}, u32[]{:S(2)}) collective-permute-start(bf16[16,2048]{1,0:T(8,128)(2,1)} %get-tuple-element.84), channel_id=1, source_target_pairs={{0,4},{4,0},{1,5},{5,1},{2,6},{6,2},{3,7},{7,3},{8,12},{12,8},{9,1... | collective-permute-start | bytes 196616 | tf_op jit(solution)/shard_map/ppermute | solution.py:29
  88.5 6.3 %copy-start.21 = (bf16[16,2048]{1,0:T(8,128)(2,1)S(1)}, bf16[16,2048]{1,0:T(8,128)(2,1)}, u32[]{:S(2)}) copy-start(bf16[16,2048]{1,0:T(8,128)(2,1)} %get-tuple-element.83) | copy-start | bytes 196612
  88.5 39.0 %copy-start.27 = (bf16[2048,3,256]{2,0,1:T(8,128)(2,1)S(1)}, bf16[2048,3,256]{2,0,1:T(8,128)(2,1)}, u32[]{:S(2)}) copy-start(bf16[2048,3,256]{2,0,1:T(8,128)(2,1)} %param.25) | copy-start | bytes 9437188
  92.1 35.7 %collective-permute-start.1 = (bf16[64,4096]{1,0:T(8,128)(2,1)S(1)}, bf16[64,4096]{1,0:T(8,128)(2,1)S(1)}, u32[]{:S(2)}, u32[]{:S(2)}) collective-permute-start(bf16[64,4096]{1,0:T(8,128)(2,1)S(1)} %get-tuple-element.63), channel_id=1, source_target_pairs={{0,1},{4,5},{8,9},{12,13},{16,17},{20,21},{24,25},{28,29}} | collective-permute-start | bytes 1572872 | tf_op jit(solution)/shard_map/ppermute | solution.py:58
  94.1 33.7 %collective-permute-start.2 = (bf16[64,4096]{1,0:T(8,128)(2,1)S(1)}, bf16[64,4096]{1,0:T(8,128)(2,1)S(1)}, u32[]{:S(2)}, u32[]{:S(2)}) collective-permute-start(bf16[64,4096]{1,0:T(8,128)(2,1)S(1)} %get-tuple-element.62), channel_id=1, source_target_pairs={{3,2},{7,6},{11,10},{15,14},{19,18},{23,22},{27,26},{31,30}} | collective-permute-start | bytes 1572872 | tf_op jit(solution)/shard_map/ppermute | solution.py:59
  95.8 22.6 %collective-permute-start.15 = (bf16[32,2048]{1,0:T(8,128)(2,1)S(1)}, bf16[32,2048]{1,0:T(8,128)(2,1)S(1)}, u32[]{:S(2)}, u32[]{:S(2)}) collective-permute-start(bf16[32,2048]{1,0:T(8,128)(2,1)S(1)} %maximum_select_fusion.3), channel_id=1, source_target_pairs={{0,3},{1,0},{2,1},{3,2},{4,7},{5,4},{6,5},{7,6},{8,11},{9,8},{10,9... | collective-permute-start | bytes 393224 | tf_op jit(solution)/shard_map/ppermute | solution.py:35
  98.3 22.9 %collective-permute-start.16 = (bf16[32,2048]{1,0:T(8,128)(2,1)S(1)}, bf16[32,2048]{1,0:T(8,128)(2,1)S(1)}, u32[]{:S(2)}, u32[]{:S(2)}) collective-permute-start(bf16[32,2048]{1,0:T(8,128)(2,1)S(1)} %maximum_select_fusion.3), channel_id=1, source_target_pairs={{0,2},{1,3},{2,0},{3,1},{4,6},{5,7},{6,4},{7,5},{8,10},{9,11},{10,... | collective-permute-start | bytes 393224 | tf_op jit(solution)/shard_map/ppermute | solution.py:35
  98.3 29.2 %collective-permute-start.17 = (bf16[32,2048]{1,0:T(8,128)(2,1)S(1)}, bf16[32,2048]{1,0:T(8,128)(2,1)S(1)}, u32[]{:S(2)}, u32[]{:S(2)}) collective-permute-start(bf16[32,2048]{1,0:T(8,128)(2,1)S(1)} %maximum_select_fusion.3), channel_id=1, source_target_pairs={{0,1},{1,2},{2,3},{3,0},{4,5},{5,6},{6,7},{7,4},{8,9},{9,10},{10,1... | collective-permute-start | bytes 393224 | tf_op jit(solution)/shard_map/ppermute | solution.py:35
  127.8 4.1 %copy-start.14 = (f32[1,128,256]{2,1,0:T(8,128)}, f32[1,128,256]{2,1,0:T(8,128)S(1)}, u32[]{:S(2)}) copy-start(f32[1,128,256]{2,1,0:T(8,128)S(1)} %convolution_bitcast_fusion) | copy-start | bytes 393220
  129.2 12.8 %collective-permute-start.3 = (bf16[64,4096]{1,0:T(8,128)(2,1)S(1)}, bf16[64,4096]{1,0:T(8,128)(2,1)S(1)}, u32[]{:S(2)}, u32[]{:S(2)}) collective-permute-start(bf16[64,4096]{1,0:T(8,128)(2,1)S(1)} %get-tuple-element.61), channel_id=1, source_target_pairs={{0,1},{1,2},{4,5},{5,6},{8,9},{9,10},{12,13},{13,14},{16,17},{17,1... | collective-permute-start | bytes 1572872 | tf_op jit(solution)/shard_map/ppermute | solution.py:58
  130.5 11.5 %collective-permute-start.4 = (bf16[64,4096]{1,0:T(8,128)(2,1)S(1)}, bf16[64,4096]{1,0:T(8,128)(2,1)S(1)}, u32[]{:S(2)}, u32[]{:S(2)}) collective-permute-start(bf16[64,4096]{1,0:T(8,128)(2,1)S(1)} %get-tuple-element.60), channel_id=1, source_target_pairs={{2,1},{3,2},{6,5},{7,6},{10,9},{11,10},{14,13},{15,14},{18,17},{19... | collective-permute-start | bytes 1572872 | tf_op jit(solution)/shard_map/ppermute | solution.py:59
  131.6 1.1 copy-start.16
  132.7 46.7 %collective-permute-start.18 = (f32[3,128,256]{2,1,0:T(8,128)}, f32[3,128,256]{2,1,0:T(8,128)}, u32[]{:S(2)}, u32[]{:S(2)}) collective-permute-start(f32[3,128,256]{2,1,0:T(8,128)} %pad_maximum_fusion.3), channel_id=1, source_target_pairs={{0,4},{4,0},{1,5},{5,1},{2,6},{6,2},{3,7},{7,3},{8,12},{12,8},{9,1... | collective-permute-start | bytes 1179656 | tf_op jit(solution)/shard_map/ppermute | solution.py:29
  169.3 29.1 %collective-permute-start.7 = (bf16[256,4096]{1,0:T(8,128)(2,1)}, bf16[256,4096]{1,0:T(8,128)(2,1)}, u32[]{:S(2)}, u32[]{:S(2)}) collective-permute-start(bf16[256,4096]{1,0:T(8,128)(2,1)} %get-tuple-element.35), channel_id=1, source_target_pairs={{0,4},{4,0},{1,5},{5,1},{2,6},{6,2},{3,7},{7,3},{8,12},{12,8},{9,1... | collective-permute-start | bytes 6291464 | tf_op jit(solution)/shard_map/ppermute | solution.py:29
  171.0 8.4 %copy-start.15 = (f32[1,128,256]{2,1,0:T(8,128)S(1)}, f32[1,128,256]{2,1,0:T(8,128)}, u32[]{:S(2)}) copy-start(f32[1,128,256]{2,1,0:T(8,128)} %copy-done.14) | copy-start | bytes 393220
  171.0 8.4 %copy-start.17 = (f32[1,128,256]{2,1,0:T(8,128)S(1)}, f32[1,128,256]{2,1,0:T(8,128)}, u32[]{:S(2)}) copy-start(f32[1,128,256]{2,1,0:T(8,128)} %copy-done.16) | copy-start | bytes 393220
  172.7 17.5 %collective-permute-start.5 = (bf16[64,4096]{1,0:T(8,128)(2,1)}, bf16[64,4096]{1,0:T(8,128)(2,1)S(1)}, u32[]{:S(2)}, u32[]{:S(2)}) collective-permute-start(bf16[64,4096]{1,0:T(8,128)(2,1)} %get-tuple-element.59), channel_id=1, source_target_pairs={{0,1},{1,2},{2,3},{4,5},{5,6},{6,7},{8,9},{9,10},{10,11},{12,13},{... | collective-permute-start | bytes 1572872 | tf_op jit(solution)/shard_map/ppermute | solution.py:58
  178.1 16.2 %collective-permute-start.6 = (bf16[64,4096]{1,0:T(8,128)(2,1)}, bf16[64,4096]{1,0:T(8,128)(2,1)S(1)}, u32[]{:S(2)}, u32[]{:S(2)}) collective-permute-start(bf16[64,4096]{1,0:T(8,128)(2,1)} %get-tuple-element.58), channel_id=1, source_target_pairs={{1,0},{2,1},{3,2},{5,4},{6,5},{7,6},{9,8},{10,9},{11,10},{13,12},{... | collective-permute-start | bytes 1572872 | tf_op jit(solution)/shard_map/ppermute | solution.py:59
  180.6 13.8 %copy-start.19 = (bf16[3,128,256]{2,1,0:T(8,128)(2,1)}, bf16[3,128,256]{2,1,0:T(8,128)(2,1)S(1)}, u32[]{:S(2)}) copy-start(bf16[3,128,256]{2,1,0:T(8,128)(2,1)S(1)} %add_convert_fusion.10) | copy-start | bytes 589828
  194.3 3.2 copy-start.22
  200.9 14.8 %collective-permute-start.8 = (bf16[64,4096]{1,0:T(8,128)(2,1)}, bf16[64,4096]{1,0:T(8,128)(2,1)}, u32[]{:S(2)}, u32[]{:S(2)}) collective-permute-start(bf16[64,4096]{1,0:T(8,128)(2,1)} %get-tuple-element.57), channel_id=1, source_target_pairs={{0,1},{4,5},{8,9},{12,13},{16,17},{20,21},{24,25},{28,29}} | collective-permute-start | bytes 1572872 | tf_op jit(solution)/shard_map/ppermute | solution.py:58
  203.8 11.8 %collective-permute-start.9 = (bf16[64,4096]{1,0:T(8,128)(2,1)}, bf16[64,4096]{1,0:T(8,128)(2,1)}, u32[]{:S(2)}, u32[]{:S(2)}) collective-permute-start(bf16[64,4096]{1,0:T(8,128)(2,1)} %get-tuple-element.56), channel_id=1, source_target_pairs={{3,2},{7,6},{11,10},{15,14},{19,18},{23,22},{27,26},{31,30}} | collective-permute-start | bytes 1572872 | tf_op jit(solution)/shard_map/ppermute | solution.py:59
  208.5 16.5 %collective-permute-start.19 = (bf16[32,2048]{1,0:T(8,128)(2,1)S(1)}, bf16[32,2048]{1,0:T(8,128)(2,1)S(1)}, u32[]{:S(2)}, u32[]{:S(2)}) collective-permute-start(bf16[32,2048]{1,0:T(8,128)(2,1)S(1)} %get-tuple-element.69), channel_id=1, source_target_pairs={{0,1},{1,2},{2,3},{3,0},{4,5},{5,6},{6,7},{7,4},{8,9},{9,10},{10,1... | collective-permute-start | bytes 393224 | tf_op jit(solution)/shard_map/ppermute | solution.py:68
  208.5 16.4 %collective-permute-start.20 = (bf16[32,2048]{1,0:T(8,128)(2,1)S(1)}, bf16[32,2048]{1,0:T(8,128)(2,1)S(1)}, u32[]{:S(2)}, u32[]{:S(2)}) collective-permute-start(bf16[32,2048]{1,0:T(8,128)(2,1)S(1)} %get-tuple-element.71), channel_id=1, source_target_pairs={{0,2},{1,3},{2,0},{3,1},{4,6},{5,7},{6,4},{7,5},{8,10},{9,11},{10,... | collective-permute-start | bytes 393224 | tf_op jit(solution)/shard_map/ppermute | solution.py:68
  209.6 15.3 %collective-permute-start.21 = (bf16[32,2048]{1,0:T(8,128)(2,1)S(1)}, bf16[32,2048]{1,0:T(8,128)(2,1)S(1)}, u32[]{:S(2)}, u32[]{:S(2)}) collective-permute-start(bf16[32,2048]{1,0:T(8,128)(2,1)S(1)} %get-tuple-element.70), channel_id=1, source_target_pairs={{0,3},{1,0},{2,1},{3,2},{4,7},{5,4},{6,5},{7,6},{8,11},{9,8},{10,9... | collective-permute-start | bytes 393224 | tf_op jit(solution)/shard_map/ppermute | solution.py:68
  218.3 15.8 %collective-permute-start.10 = (bf16[64,4096]{1,0:T(8,128)(2,1)}, bf16[64,4096]{1,0:T(8,128)(2,1)}, u32[]{:S(2)}, u32[]{:S(2)}) collective-permute-start(bf16[64,4096]{1,0:T(8,128)(2,1)} %get-tuple-element.55), channel_id=1, source_target_pairs={{0,1},{1,2},{4,5},{5,6},{8,9},{9,10},{12,13},{13,14},{16,17},{17,1... | collective-permute-start | bytes 1572872 | tf_op jit(solution)/shard_map/ppermute | solution.py:58
  223.5 10.6 %collective-permute-start.11 = (bf16[64,4096]{1,0:T(8,128)(2,1)}, bf16[64,4096]{1,0:T(8,128)(2,1)}, u32[]{:S(2)}, u32[]{:S(2)}) collective-permute-start(bf16[64,4096]{1,0:T(8,128)(2,1)} %get-tuple-element.54), channel_id=1, source_target_pairs={{2,1},{3,2},{6,5},{7,6},{10,9},{11,10},{14,13},{15,14},{18,17},{19... | collective-permute-start | bytes 1572872 | tf_op jit(solution)/shard_map/ppermute | solution.py:59
  225.9 108.0 %all-gather.11.cloned.1.call-start = ((), (), s32[]{:S(2)}) async-start(), calls=%async_computation.3 | async-start | bytes 2621440 | tf_op jit(solution)/shard_map/all_gather | solution.py:237
  226.0 16.5 %copy-start.9 = (bf16[2048,2,256]{2,1,0:T(2,128)(2,1)S(1)}, bf16[2048,2,256]{2,1,0:T(2,128)(2,1)}, u32[]{:S(2)}) copy-start(bf16[2048,2,256]{2,1,0:T(2,128)(2,1)} %param.29) | copy-start | bytes 6291460
  226.0 19.0 %collective-permute-start.22 = (f32[16,2048]{1,0:T(8,128)S(1)}, f32[16,2048]{1,0:T(8,128)S(1)}, u32[]{:S(2)}, u32[]{:S(2)}) collective-permute-start(f32[16,2048]{1,0:T(8,128)S(1)} %get-tuple-element.79), channel_id=1, source_target_pairs={{0,4},{4,0},{1,5},{5,1},{2,6},{6,2},{3,7},{7,3},{8,12},{12,8},{9,1... | collective-permute-start | bytes 393224 | tf_op jit(solution)/shard_map/ppermute | solution.py:29
  236.1 27.6 %collective-permute-start.12 = (bf16[64,4096]{1,0:T(8,128)(2,1)S(1)}, bf16[64,4096]{1,0:T(8,128)(2,1)S(1)}, u32[]{:S(2)}, u32[]{:S(2)}) collective-permute-start(bf16[64,4096]{1,0:T(8,128)(2,1)S(1)} %get-tuple-element.53), channel_id=1, source_target_pairs={{0,1},{1,2},{2,3},{4,5},{5,6},{6,7},{8,9},{9,10},{10,11},{12,13},{... | collective-permute-start | bytes 1572872 | tf_op jit(solution)/shard_map/ppermute | solution.py:58
  241.1 3.1 copy-start.12
  241.1 38.7 %collective-permute-start.13 = (bf16[64,4096]{1,0:T(8,128)(2,1)S(1)}, bf16[64,4096]{1,0:T(8,128)(2,1)S(1)}, u32[]{:S(2)}, u32[]{:S(2)}) collective-permute-start(bf16[64,4096]{1,0:T(8,128)(2,1)S(1)} %get-tuple-element.52), channel_id=1, source_target_pairs={{1,0},{2,1},{3,2},{5,4},{6,5},{7,6},{9,8},{10,9},{11,10},{13,12},{... | collective-permute-start | bytes 1572872 | tf_op jit(solution)/shard_map/ppermute | solution.py:59
  244.1 35.7 %copy-start.2 = (bf16[128,4096]{1,0:T(8,128)(2,1)S(1)}, bf16[128,4096]{1,0:T(8,128)(2,1)}, u32[]{:S(2)}) copy-start(bf16[128,4096]{1,0:T(8,128)(2,1)} %param.16) | copy-start | bytes 3145732
  244.1 35.7 %copy-start.20 = (s32[1,8,4,128]{3,1,2,0:T(8,128)S(1)}, s32[1,8,4,128]{3,1,2,0:T(8,128)}, u32[]{:S(2)}) copy-start(s32[1,8,4,128]{3,1,2,0:T(8,128)} %copy.36) | copy-start | bytes 49156
  244.1 43.6 %collective-permute-start.28 = (bf16[2,2048,256]{2,1,0:T(8,128)(2,1)}, bf16[2,2048,256]{2,1,0:T(8,128)(2,1)}, u32[]{:S(2)}, u32[]{:S(2)}) collective-permute-start(bf16[2,2048,256]{2,1,0:T(8,128)(2,1)} %bitcast.89), channel_id=1, source_target_pairs={{0,4},{4,0},{1,5},{5,1},{2,6},{6,2},{3,7},{7,3},{8,12},{12,8},{9,1... | collective-permute-start | bytes 6291464 | tf_op jit(solution)/shard_map/ppermute | solution.py:29
  279.8 2.6 copy-start.23
  279.8 3.6 copy-start.26
  283.5 1.3 collective-permute-start.23
  284.9 27.9 %copy-start.13 = (bf16[2048,256]{1,0:T(8,128)(2,1)S(1)}, bf16[2048,256]{1,0:T(8,128)(2,1)}, u32[]{:S(2)}) copy-start(bf16[2048,256]{1,0:T(8,128)(2,1)} %param.28) | copy-start | bytes 3145732
  284.9 8.9 %collective-permute-start.24 = (bf16[32,2048]{1,0:T(8,128)(2,1)S(1)}, bf16[32,2048]{1,0:T(8,128)(2,1)S(1)}, u32[]{:S(2)}, u32[]{:S(2)}) collective-permute-start(bf16[32,2048]{1,0:T(8,128)(2,1)S(1)} %maximum_select_fusion.4), channel_id=1, source_target_pairs={{0,3},{1,0},{2,1},{3,2},{4,7},{5,4},{6,5},{7,6},{8,11},{9,8},{10,9... | collective-permute-start | bytes 393224 | tf_op jit(solution)/shard_map/ppermute | solution.py:35
  284.9 27.7 %collective-permute-start.25 = (bf16[32,2048]{1,0:T(8,128)(2,1)S(1)}, bf16[32,2048]{1,0:T(8,128)(2,1)S(1)}, u32[]{:S(2)}, u32[]{:S(2)}) collective-permute-start(bf16[32,2048]{1,0:T(8,128)(2,1)S(1)} %maximum_select_fusion.4), channel_id=1, source_target_pairs={{0,2},{1,3},{2,0},{3,1},{4,6},{5,7},{6,4},{7,5},{8,10},{9,11},{10,... | collective-permute-start | bytes 393224 | tf_op jit(solution)/shard_map/ppermute | solution.py:35
  287.7 24.9 %collective-permute-start.26 = (bf16[32,2048]{1,0:T(8,128)(2,1)S(1)}, bf16[32,2048]{1,0:T(8,128)(2,1)S(1)}, u32[]{:S(2)}, u32[]{:S(2)}) collective-permute-start(bf16[32,2048]{1,0:T(8,128)(2,1)S(1)} %maximum_select_fusion.4), channel_id=1, source_target_pairs={{0,1},{1,2},{2,3},{3,0},{4,5},{5,6},{6,7},{7,4},{8,9},{9,10},{10,1... | collective-permute-start | bytes 393224 | tf_op jit(solution)/shard_map/ppermute | solution.py:35
  313.1 24.0 %collective-permute-start.27 = (f32[128,256]{1,0:T(8,128)S(1)}, f32[128,256]{1,0:T(8,128)S(1)}, u32[]{:S(2)}, u32[]{:S(2)}) collective-permute-start(f32[128,256]{1,0:T(8,128)S(1)} %fusion.70), channel_id=1, source_target_pairs={{0,4},{4,0},{1,5},{5,1},{2,6},{6,2},{3,7},{7,3},{8,12},{12,8},{9,1... | collective-permute-start | bytes 393224 | tf_op jit(solution)/shard_map/ppermute | solution.py:29
  313.2 3.5 copy-start.7
  334.0 3.6 copy-start.8
  334.0 4.1 %copy-start.28 = (bf16[256,4096]{1,0:T(8,128)(2,1)S(1)}, bf16[256,4096]{1,0:T(8,128)(2,1)}, u32[]{:S(2)}) copy-start(bf16[256,4096]{1,0:T(8,128)(2,1)} %all-gather.11.cloned.1.call-done) | copy-start | bytes 6291460
  338.1 2.7 copy-start.11
  338.8 6.3 %copy-start.24 = (s32[16,1024]{1,0:T(8,128)S(1)}, s32[16,1024]{1,0:T(8,128)}, u32[]{:S(2)}) copy-start(s32[16,1024]{1,0:T(8,128)} %param.31) | copy-start | bytes 196612
  339.2 1.6 collective-permute-start.29
  340.8 13.6 %copy-start.4 = (bf16[64,4096]{1,0:T(8,128)(2,1)S(1)}, bf16[64,4096]{1,0:T(8,128)(2,1)}, u32[]{:S(2)}) copy-start(bf16[64,4096]{1,0:T(8,128)(2,1)} %copy-done.3) | copy-start | bytes 1572868
  340.8 13.6 %copy-start.6 = (bf16[64,4096]{1,0:T(8,128)(2,1)S(1)}, bf16[64,4096]{1,0:T(8,128)(2,1)}, u32[]{:S(2)}) copy-start(bf16[64,4096]{1,0:T(8,128)(2,1)} %copy-done.5) | copy-start | bytes 1572868
  341.2 8.3 %collective-permute-start.30 = (bf16[32,2048]{1,0:T(8,128)(2,1)S(1)}, bf16[32,2048]{1,0:T(8,128)(2,1)S(1)}, u32[]{:S(2)}, u32[]{:S(2)}) collective-permute-start(bf16[32,2048]{1,0:T(8,128)(2,1)S(1)} %get-tuple-element.66), channel_id=1, source_target_pairs={{0,1},{1,2},{2,3},{3,0},{4,5},{5,6},{6,7},{7,4},{8,9},{9,10},{10,1... | collective-permute-start | bytes 393224 | tf_op jit(solution)/shard_map/ppermute | solution.py:68
  341.3 13.0 %collective-permute-start.31 = (bf16[32,2048]{1,0:T(8,128)(2,1)S(1)}, bf16[32,2048]{1,0:T(8,128)(2,1)S(1)}, u32[]{:S(2)}, u32[]{:S(2)}) collective-permute-start(bf16[32,2048]{1,0:T(8,128)(2,1)S(1)} %get-tuple-element.68), channel_id=1, source_target_pairs={{0,2},{1,3},{2,0},{3,1},{4,6},{5,7},{6,4},{7,5},{8,10},{9,11},{10,... | collective-permute-start | bytes 393224 | tf_op jit(solution)/shard_map/ppermute | solution.py:68
  343.1 11.1 %collective-permute-start.32 = (bf16[32,2048]{1,0:T(8,128)(2,1)S(1)}, bf16[32,2048]{1,0:T(8,128)(2,1)S(1)}, u32[]{:S(2)}, u32[]{:S(2)}) collective-permute-start(bf16[32,2048]{1,0:T(8,128)(2,1)S(1)} %get-tuple-element.67), channel_id=1, source_target_pairs={{0,3},{1,0},{2,1},{3,2},{4,7},{5,4},{6,5},{7,6},{8,11},{9,8},{10,9... | collective-permute-start | bytes 393224 | tf_op jit(solution)/shard_map/ppermute | solution.py:68
  354.4 1.4 collective-permute-start.33
  (3 other events, 2.4 us)
Sparse Core Ops, SparseCore 0:
  11.6 49.8 all-gather.4
  63.1 50.7 all-gather.6
  226.1 57.7 all-gather.8
  285.3 48.5 all-gather.10

commit v6 on v5

--- a/solution.py
+++ b/solution.py
@@ -102,66 +102,80 @@
     return 0.5 * x * (1.0 + jnp.tanh(0.7978845608028654 * (x + 0.044715 * x * x * x)))
 
 
-def ffn_kernel(hidden_steps, order, x_ref, gate_ref, up_ref, down_ref, ya_ref, yb_ref, x, hidden):
+def ffn_kernel(ins, order, x_ref, gate_ref, up_ref, down_ref, ya_ref, yb_ref, x, gate, up, hidden):
     step = pl.program_id(0)
-    rows = ya_ref.shape[0]
-    width = gate_ref.shape[1]
-    blocks = order.shape[0]
-    block = 2 * rows // blocks
+    blocks, block, _ = x_ref.shape
+    depth = gate_ref.shape[0]
 
     @pl.when(step == 0)
     def _():
         for slot in range(blocks):
-            at = pl.multiple_of(order[slot] * block, block)
-            x[slot * block : (slot + 1) * block, :] = x_ref[pl.ds(at, block), :]
-
-    @pl.when(step < hidden_steps)
+            rows = x_ref[order[slot]]
+            for k in range(ins):
+                x[k, slot * block : (slot + 1) * block, :] = rows[:, k * depth : (k + 1) * depth]
+
+    @pl.when(step < ins)
     def _():
-        gate = jnp.dot(x[...], gate_ref[...], preferred_element_type=F32)
-        up = jnp.dot(x[...], up_ref[...], preferred_element_type=F32)
-        hidden[step] = (gelu(gate) * up).astype(BF16)
-
-    @pl.when(step >= hidden_steps)
+        part = x[step]
+        one = jnp.dot(part, gate_ref[...], preferred_element_type=F32)
+        two = jnp.dot(part, up_ref[...], preferred_element_type=F32)
+
+        @pl.when(step == 0)
+        def _():
+            gate[...] = one
+            up[...] = two
+
+        @pl.when(step > 0)
+        def _():
+            gate[...] += one
+            up[...] += two
+
+    @pl.when(step == ins)
     def _():
-        total = jnp.zeros((2 * rows, ya_ref.shape[1]), F32)
-        for k in range(hidden.shape[0]):
-            total += jnp.dot(
-                hidden[k], down_ref[k * width : (k + 1) * width, :], preferred_element_type=F32
-            )
-        ya_ref[...] = total[:rows].astype(BF16)
-        yb_ref[...] = total[rows:].astype(BF16)
-
-
-def ffn(x, order, w_gate, w_up, w_down):
+        hidden[...] = (gelu(gate[...]) * up[...]).astype(BF16)
+
+    @pl.when(step >= ins)
+    def _():
+        total = jnp.dot(hidden[...], down_ref[...], preferred_element_type=F32).astype(BF16)
+        half = total.shape[0] // 2
+        ya_ref[...] = total[:half]
+        yb_ref[...] = total[half:]
+
+
+def ffn(x, order, piece, pieces, w_gate, w_up, w_down):
     rows, features = x.shape
     units = w_gate.shape[1]
-    width = min(256, units)
-    tile = 512
-    first, last = units // width, features // tile
+    depth, tile = 512, 1024
+    ins, outs = features // depth, features // tile
+    blocks = order.shape[0]
+    block = rows // blocks // pieces
+    rows = rows // pieces
     return pl.pallas_call(
-        functools.partial(ffn_kernel, first),
+        functools.partial(ffn_kernel, ins),
         grid_spec=pltpu.PrefetchScalarGridSpec(
             num_scalar_prefetch=1,
-            grid=(first + last,),
+            grid=(ins + outs,),
             in_specs=[
-                pl.BlockSpec((rows, features), lambda i, t: (0, 0), pipeline_mode=pl.Buffered(1)),
-                pl.BlockSpec((features, width), lambda i, t: (0, jnp.minimum(i, first - 1))),
-                pl.BlockSpec((features, width), lambda i, t: (0, jnp.minimum(i, first - 1))),
-                pl.BlockSpec((units, tile), lambda i, t: (0, jnp.maximum(i - first, 0))),
+                pl.BlockSpec((blocks, block, features), lambda i, t: (0, piece, 0), pipeline_mode=pl.Buffered(1)),
+                pl.BlockSpec((depth, units), lambda i, t: (jnp.minimum(i, ins - 1), 0)),
+                pl.BlockSpec((depth, units), lambda i, t: (jnp.minimum(i, ins - 1), 0)),
+                pl.BlockSpec((units, tile), lambda i, t: (0, jnp.maximum(i - ins, 0))),
             ],
-            out_specs=[pl.BlockSpec((rows // 2, tile), lambda i, t: (0, jnp.maximum(i - first, 0)))] * 2,
+            out_specs=[pl.BlockSpec((rows // 2, tile), lambda i, t: (0, jnp.maximum(i - ins, 0)))] * 2,
             scratch_shapes=[
-                pltpu.VMEM((rows, features), BF16),
-                pltpu.VMEM((first, rows, width), BF16),
+                pltpu.VMEM((ins, rows, depth), BF16),
+                pltpu.VMEM((rows, units), F32),
+                pltpu.VMEM((rows, units), F32),
+                pltpu.VMEM((rows, units), BF16),
             ],
         ),
         out_shape=[jax.ShapeDtypeStruct((rows // 2, features), BF16)] * 2,
-        compiler_params=pltpu.CompilerParams(vmem_limit_bytes=48 * 2**20),
+        compiler_params=pltpu.CompilerParams(vmem_limit_bytes=40 * 2**20),
         cost_estimate=pl.CostEstimate(
             flops=6 * rows * features * units, bytes_accessed=6 * features * units, transcendentals=0
         ),
         name="ffn",
-    )(order, x, w_gate, w_up, w_down)
+    )(order, x.reshape(blocks, -1, features), w_gate, w_up, w_down)
 
 
 def per_device(
@@ -214,24 +228,18 @@
     product = jnp.dot(context, self_out, preferred_element_type=F32).astype(BF16)
     total = slots_sum(product)
 
-    mine, theirs = ffn(near[0], order, w_gate, w_up, w_down)
-    got = swap(theirs, "section", 1)
-    came = sum_step(sum_sends(mine, got, None, 1), 1)
-    total = gated(total, *came)
-    mid = (target.astype(F32) + whole_rows(total, section)).astype(BF16)
-    crossin = gather_half(norm_rows(mid, cross_gain).astype(BF16), section)
-    for step in range(2, count - 1):
-        came = sum_step(sum_sends(mine, got, came, step), step)
-    sends = sum_sends(mine, got, came, count - 1)
-    came = sum_step(sends, count - 1)
-    mine_b, theirs_b = ffn(gated(near[1], *sends), order, w_gate, w_up, w_down)
-
-    def finish_rows(c, mine, got, came):
-        at = slice(c * block, (c + 1) * block)
-        total = slot_sum(mine, got, 0) + came[0].astype(F32) + came[1].astype(F32)
+    def begin(rows, mine, theirs):
+        got = swap(theirs, "section", 1)
+        return dict(rows=rows, mine=mine, got=got, came=None)
+
+    def sends(state, step):
+        return sum_sends(state["mine"], state["got"], state["came"], step)
+
+    def finish_rows(state):
+        at, came = state["rows"], state["came"]
+        total = slot_sum(state["mine"], state["got"], 0) + came[0].astype(F32) + came[1].astype(F32)
         out = (source[at].astype(F32) + keep_factor(enc_keep[at]) * total).astype(BF16)
-        memory = norm_rows(out, final_gain).astype(BF16)
-        return out, memory
+        return out, norm_rows(out, final_gain).astype(BF16)
 
     def to_heads(memory):
         return lax.all_gather(memory, "tensor", axis=0, tiled=True)
@@ -239,22 +247,45 @@
     def keys_values(memory):
         return [jnp.dot(memory, kv[i], preferred_element_type=F32).astype(BF16) for i in range(2)]
 
-    out_a, memory_a = finish_rows(0, mine, got, came)
-    memory_a, mine_b = lax.optimization_barrier((memory_a, mine_b))
+    weights = (w_gate, w_up, w_down)
+    quarter = block // 2
+    a = begin(slice(0, block), *ffn(gated(near[0], product), order, 0, 1, *weights))
+    for step in range(1, count - 1):
+        a["came"] = sum_step(sends(a, step), step)
+        if step == 1:
+            total = gated(total, *a["came"])
+            mid = (target.astype(F32) + whole_rows(total, section)).astype(BF16)
+            crossin = gather_half(norm_rows(mid, cross_gain).astype(BF16), section)
+    last = sends(a, count - 1)
+    x = gated(near[1], *last)
+    b = begin(slice(block, block + quarter), *ffn(x, order, 0, 2, *weights))
+    a["came"] = sum_step(last, count - 1)
+    out_a, memory_a = finish_rows(a)
+
+    first = sends(b, 1)
+    x, memory_a = lax.optimization_barrier((x, memory_a) + first)[:2]
     memory_a = to_heads(memory_a)
-    got = swap(theirs_b, "section", 1)
-    came = sum_step(sum_sends(mine_b, got, None, 1), 1)
-    crossin = gated(crossin, *came)
-    cq = both_halves(jnp.dot(crossin, cross_q, preferred_element_type=F32)).astype(BF16)
+    b["came"] = sum_step(first, 1)
+    c = begin(slice(block + quarter, 2 * block), *ffn(x, order, 1, 2, *weights))
     for step in range(2, count):
-        came = sum_step(sum_sends(mine_b, got, came, step), step)
-    out_b, memory_b = finish_rows(1, mine_b, got, came)
-    memory_b = to_heads(memory_b)
-    memory_a = gated(memory_a, out_b)
-    keys_a, values_a = keys_values(memory_a)
-    keys_b, values_b = keys_values(memory_b)
-    enc_out = jnp.concatenate([out_a, out_b], 0)
-    keys, values = jnp.concatenate([keys_a, keys_b], 0), jnp.concatenate([values_a, values_b], 0)
+        b["came"] = sum_step(sends(b, step), step)
+        if step == 2:
+            first = lax.optimization_barrier(sends(c, 1) + b["came"])[:2]
+            c["came"] = sum_step(first, 1)
+            crossin = gated(crossin, *c["came"])
+            cq = both_halves(jnp.dot(crossin, cross_q, preferred_element_type=F32)).astype(BF16)
+    out_b, memory_b = finish_rows(b)
+    second = lax.optimization_barrier(sends(c, 2) + (memory_b,))
+    memory_b = to_heads(second[2])
+    c["came"] = sum_step(second[:2], 2)
+    for step in range(3, count):
+        c["came"] = sum_step(sends(c, step), step)
+    out_c, memory_c = finish_rows(c)
+    memory_a, memory_c = lax.optimization_barrier((memory_a, memory_c))
+    memory_c = to_heads(memory_c)
+    memories = [keys_values(m) for m in (memory_a, memory_b, memory_c)]
+    enc_out = jnp.concatenate([out_a, out_b, out_c], 0)
+    keys, values = [jnp.concatenate([m[i] for m in memories], 0) for i in range(2)]
 
     scores = lax.dot_general(cq, keys, (((1,), (1,)), ((), ())), preferred_element_type=F32) * (1.0 / 16.0)
     top = jnp.max(scores, axis=-1, keepdims=True)

time: 364 us -> 385 us (1.058)
  starting transfers between devices: 43.8 us -> 76.2 us
  waiting for transfers between devices: 193 us -> 163 us
  Pallas kernels: 49.3 us -> 58.9 us
  other arithmetic: 34.6 us -> 38.9 us
    ppermute x6, waiting for transfers between devices: 47.3 us -> 12.2 us  [from_slots(): lax.ppermute(value, 'tensor', [(i, (i - o) % count) for i in range(count)])]
    all_gather x2 -> x3, waiting for transfers between devices: 15 us -> 45.5 us  [to_heads(): return lax.all_gather(memory, 'tensor', axis=0, tiled=True)]
    ppermute x6 -> x9, starting transfers between devices: 21.8 us -> 46.9 us  [sum_step(): above = lax.ppermute(sends[0], 'tensor', [(i, i + 1) for i in range(step)])]
    all_gather x2, waiting for transfers between devices: 48.9 us -> 28.8 us  [per_device(): lax.all_gather(normed[c * block:(c + 1) * block], ('section', 'tensor'),...]
    ppermute x6 -> x9, waiting for transfers between devices: 20.2 us -> 5.05 us  [sum_step(): lax.ppermute(sends[1], 'tensor', [(i, i - 1) for i in range(count - step,...]
    pallas_call x2 -> x3, Pallas kernels: 49.3 us -> 58.9 us  [ffn(): pl.pallas_call(functools.partial(ffn_kernel, ins), grid_spec=pltpu.Prefet...]
    ppermute x6, waiting for transfers between devices: 8.92 us -> 16.3 us  [slots_sum(): lax.ppermute(product[o], 'tensor', [(i, (i + o) % count) for i in range(c...]
    ppermute x6, starting transfers between devices: 6.03 us -> 10.7 us  [from_slots(): lax.ppermute(value, 'tensor', [(i, (i - o) % count) for i in range(count)])]
  transfers between devices with their start and end apart: 38 -> 46, of which waited for: 19 -> 20; matrix products, arithmetic and copies ran while one was open for 14% -> 14% of each run, Pallas kernels for 14% -> 15%
where the time goes in v6:
time: 385 us; the launch traced here: 383 us
  waiting for transfers between devices  163 us (42%)
  starting transfers between devices  76.2 us (20%)
  Pallas kernels  58.9 us (15%)
  other arithmetic  38.9 us (10%)
  matrix products  16 us (4%)
  local copies, waits for them, and re-layouts  15.4 us (4%)
  between operations  14.7 us (4%)
    pallas_call x3, Pallas kernels, ffn(): pl.pallas_call(functools.partial(ffn_kernel, ins), grid_spec=pltpu.Prefet...  58.9 us
    ppermute x9, waiting for transfers between devices, sum_step(): above = lax.ppermute(sends[0], 'tensor', [(i, i + 1) for i in range(step)])  48.9 us
    ppermute x9, starting transfers between devices, sum_step(): above = lax.ppermute(sends[0], 'tensor', [(i, i + 1) for i in range(step)])  46.9 us
    all_gather x3, waiting for transfers between devices, to_heads(): return lax.all_gather(memory, 'tensor', axis=0, tiled=True)  45.5 us
    all_gather x2, waiting for transfers between devices, per_device(): lax.all_gather(normed[c * block:(c + 1) * block], ('section', 'tensor'),...  28.8 us
    ppermute x6, waiting for transfers between devices, slots_sum(): lax.ppermute(product[o], 'tensor', [(i, (i + o) % count) for i in range(c...  16.3 us
    convert_element_type x9, other arithmetic, sum_sends(): return (up.astype(BF16), down.astype(BF16))  14.1 us
    ppermute x6, waiting for transfers between devices, from_slots(): lax.ppermute(value, 'tensor', [(i, (i - o) % count) for i in range(count)])  12.2 us
  transfers between devices with their start and end apart: 46, of which 20 were waited for; matrix products, arithmetic and copies ran while one was open for 14% of the time, Pallas kernels for 15%

profile of v6, /device:TPU:0, one launch (start us, length us, event | category | flops | bytes accessed | tf_op | source)
XLA Modules:
  0.0 382.7 jit_solution(14593994026751156351)
XLA Ops:
  7.2 1.6 fusion
  8.9 1.6 fusion.2
  13.3 3.0 collective-permute-start.3
  16.3 2.6 collective-permute-start.2
  18.9 1.3 collective-permute-start.1
  20.3 2.4 collective-permute-done.3
  22.7 9.8 %collective-permute-done.2 = bf16[32,2048]{1,0:T(8,128)(2,1)S(1)} collective-permute-done((bf16[32,2048]{1,0:T(8,128)(2,1)S(1)}, bf16[32,2048]{1,0:T(8,128)(2,1)S(1)}, u32[]{:S(2)}, u32[]{:S(2)}) %collective-permute-start.2) | collective-permute-done | bytes 131104 | tf_op jit(solution)/shard_map/ppermute | solution.py:35
  32.5 1.6 convolution_bitcast_fusion
  35.1 1.5 collective-permute-done.4
  37.3 28.8 %all-gather.6.cloned.1.call-done = bf16[512,4096]{1,0:T(8,128)(2,1)} async-done(((bf16[64,4096]{1,0:T(8,128)(2,1)}), bf16[512,4096]{1,0:T(8,128)(2,1)}) %all-gather.6.cloned.1.call-update) | async-done | bytes 4194320 | tf_op jit(solution)/shard_map/all_gather | solution.py:210
  66.1 2.2 copy-done.4
  68.3 23.9 %ffn.3 = (bf16[256,4096]{1,0:T(8,128)(2,1)S(1)}, bf16[256,4096]{1,0:T(8,128)(2,1)}) custom-call(s32[8]{0:T(128)S(1)} %pad_add_fusion.order, bf16[8,64,4096]{2,1,0:T(8,128)(2,1)S(1)} %bitcast.106, bf16[4096,1024]{1,0:T(8,128)(2,1)} %gate_ref.5, bf16[4096,1024]{1,0:T(8,128)(2,1)} %up_ref.5, bf16[1024,4096]{1,0:T(8,128)(2,1)} %down_ref.5), custom_call_target="tpu_custom_call" | custom-call | flops 12884901888 | bytes 25165824 | tf_op jit(solution)/shard_map/ffn/pallas_call | solution.py:153
  92.4 1.6 copy.36
  95.1 1.7 collective-permute-done.5
  96.7 1.5 fusion.19
  98.2 1.3 collective-permute-start.6
  100.3 1.9 collective-permute-start.28
  102.2 18.7 %collective-permute-done.6 = bf16[64,4096]{1,0:T(8,128)(2,1)S(1)} collective-permute-done((bf16[64,4096]{1,0:T(8,128)(2,1)S(1)}, bf16[64,4096]{1,0:T(8,128)(2,1)S(1)}, u32[]{:S(2)}, u32[]{:S(2)}) %collective-permute-start.6) | collective-permute-done | bytes 524320 | tf_op jit(solution)/shard_map/ppermute | solution.py:58
  120.9 2.5 collective-permute-start.26
  123.4 1.3 add_convert_fusion.3
  124.7 1.9 collective-permute-start.8
  127.4 5.7 %collective-permute-done.26 = bf16[32,2048]{1,0:T(8,128)(2,1)S(1)} collective-permute-done((bf16[32,2048]{1,0:T(8,128)(2,1)S(1)}, bf16[32,2048]{1,0:T(8,128)(2,1)S(1)}, u32[]{:S(2)}, u32[]{:S(2)}) %collective-permute-start.26) | collective-permute-done | bytes 131104 | tf_op jit(solution)/shard_map/ppermute | solution.py:68
  133.9 6.6 %collective-permute-done.8 = bf16[64,4096]{1,0:T(8,128)(2,1)S(1)} collective-permute-done((bf16[64,4096]{1,0:T(8,128)(2,1)S(1)}, bf16[64,4096]{1,0:T(8,128)(2,1)S(1)}, u32[]{:S(2)}, u32[]{:S(2)}) %collective-permute-start.8) | collective-permute-done | bytes 524320 | tf_op jit(solution)/shard_map/ppermute | solution.py:58
  140.4 2.7 add_convert_fusion.1
  143.1 6.9 %collective-permute-start.10 = (bf16[64,4096]{1,0:T(8,128)(2,1)}, bf16[64,4096]{1,0:T(8,128)(2,1)}, u32[]{:S(2)}, u32[]{:S(2)}) collective-permute-start(bf16[64,4096]{1,0:T(8,128)(2,1)} %get-tuple-element.85), channel_id=1, source_target_pairs={{0,1},{1,2},{2,3},{4,5},{5,6},{6,7},{8,9},{9,10},{10,11},{12,13},{... | collective-permute-start | bytes 1572872 | tf_op jit(solution)/shard_map/ppermute | solution.py:58
  150.0 1.5 collective-permute-start.11
  151.5 2.2 copy-done.2
  153.7 17.5 %ffn.4 = (bf16[128,4096]{1,0:T(8,128)(2,1)S(1)}, bf16[128,4096]{1,0:T(8,128)(2,1)S(1)}) custom-call(s32[8]{0:T(128)S(1)} %pad_add_fusion.order, bf16[8,64,4096]{2,1,0:T(8,128)(2,1)S(1)} %bitcast.104, bf16[4096,1024]{1,0:T(8,128)(2,1)} %gate_ref.5, bf16[4096,1024]{1,0:T(8,128)(2,1)} %up_ref.5, bf16[1024,4096]{1,0:T(8,128)(2,1)} %down_ref.5), custom_call_target="tpu_custom_call" | custom-call | flops 6442450944 | bytes 25165824 | tf_op jit(solution)/shard_map/ffn/pallas_call | solution.py:153
  174.7 2.1 fusion.16
  176.9 1.3 fusion.27
  178.2 4.6 %collective-permute-start.13 = (bf16[32,4096]{1,0:T(8,128)(2,1)S(1)}, bf16[32,4096]{1,0:T(8,128)(2,1)S(1)}, u32[]{:S(2)}, u32[]{:S(2)}) collective-permute-start(bf16[32,4096]{1,0:T(8,128)(2,1)S(1)} %get-tuple-element.101), channel_id=1, source_target_pairs={{0,1},{4,5},{8,9},{12,13},{16,17},{20,21},{24,25},{28,29}} | collective-permute-start | bytes 786440 | tf_op jit(solution)/shard_map/ppermute | solution.py:58
  184.4 4.5 %collective-permute-done.13 = bf16[32,4096]{1,0:T(8,128)(2,1)S(1)} collective-permute-done((bf16[32,4096]{1,0:T(8,128)(2,1)S(1)}, bf16[32,4096]{1,0:T(8,128)(2,1)S(1)}, u32[]{:S(2)}, u32[]{:S(2)}) %collective-permute-start.13) | collective-permute-done | bytes 262176 | tf_op jit(solution)/shard_map/ppermute | solution.py:58
  190.0 4.4 %collective-permute-start.15 = (bf16[32,4096]{1,0:T(8,128)(2,1)S(1)}, bf16[32,4096]{1,0:T(8,128)(2,1)S(1)}, u32[]{:S(2)}, u32[]{:S(2)}) collective-permute-start(bf16[32,4096]{1,0:T(8,128)(2,1)S(1)} %get-tuple-element.97), channel_id=1, source_target_pairs={{0,1},{1,2},{4,5},{5,6},{8,9},{9,10},{12,13},{13,14},{16,17},{17,1... | collective-permute-start | bytes 786440 | tf_op jit(solution)/shard_map/ppermute | solution.py:58
  195.2 2.2 copy-done.3
  197.3 17.5 %ffn.5 = (bf16[128,4096]{1,0:T(8,128)(2,1)S(1)}, bf16[128,4096]{1,0:T(8,128)(2,1)S(1)}) custom-call(s32[8]{0:T(128)S(1)} %pad_add_fusion.order, bf16[8,64,4096]{2,1,0:T(8,128)(2,1)S(1)} %bitcast.105, bf16[4096,1024]{1,0:T(8,128)(2,1)} %gate_ref.5, bf16[4096,1024]{1,0:T(8,128)(2,1)} %up_ref.5, bf16[1024,4096]{1,0:T(8,128)(2,1)} %down_ref.5), custom_call_target="tpu_custom_call" | custom-call | flops 6442450944 | bytes 25165824 | tf_op jit(solution)/shard_map/ffn/pallas_call | solution.py:153
  214.9 2.0 add_convert_fusion.11
  217.0 3.7 collective-permute-start.17
  223.0 3.5 collective-permute-done.17
  226.4 5.0 %collective-permute-done.18 = bf16[32,4096]{1,0:T(8,128)(2,1)} collective-permute-done((bf16[32,4096]{1,0:T(8,128)(2,1)}, bf16[32,4096]{1,0:T(8,128)(2,1)}, u32[]{:S(2)}, u32[]{:S(2)}) %collective-permute-start.18) | collective-permute-done | bytes 262176 | tf_op jit(solution)/shard_map/ppermute | solution.py:59
  231.5 1.9 fusion.21
  234.6 3.8 collective-permute-start.20
  239.1 1.6 fusion.23
  240.7 9.4 %collective-permute-done.20 = bf16[32,4096]{1,0:T(8,128)(2,1)S(1)} collective-permute-done((bf16[32,4096]{1,0:T(8,128)(2,1)S(1)}, bf16[32,4096]{1,0:T(8,128)(2,1)S(1)}, u32[]{:S(2)}, u32[]{:S(2)}) %collective-permute-start.20) | collective-permute-done | bytes 262176 | tf_op jit(solution)/shard_map/ppermute | solution.py:58
  251.2 4.4 %collective-permute-start.22 = (bf16[32,4096]{1,0:T(8,128)(2,1)S(1)}, bf16[32,4096]{1,0:T(8,128)(2,1)S(1)}, u32[]{:S(2)}, u32[]{:S(2)}) collective-permute-start(bf16[32,4096]{1,0:T(8,128)(2,1)S(1)} %get-tuple-element.64), channel_id=1, source_target_pairs={{0,1},{1,2},{4,5},{5,6},{8,9},{9,10},{12,13},{13,14},{16,17},{17,1... | collective-permute-start | bytes 786440 | tf_op jit(solution)/shard_map/ppermute | solution.py:58
  257.7 1.7 collective-permute-start.33
  259.4 2.2 collective-permute-start.32
  261.6 6.3 %collective-permute-done.22 = bf16[32,4096]{1,0:T(8,128)(2,1)S(1)} collective-permute-done((bf16[32,4096]{1,0:T(8,128)(2,1)S(1)}, bf16[32,4096]{1,0:T(8,128)(2,1)S(1)}, u32[]{:S(2)}, u32[]{:S(2)}) %collective-permute-start.22) | collective-permute-done | bytes 262176 | tf_op jit(solution)/shard_map/ppermute | solution.py:58
  267.8 1.9 add_convert_fusion.6
  269.8 15.8 %collective-permute-start.24 = (bf16[32,4096]{1,0:T(8,128)(2,1)}, bf16[32,4096]{1,0:T(8,128)(2,1)S(1)}, u32[]{:S(2)}, u32[]{:S(2)}) collective-permute-start(bf16[32,4096]{1,0:T(8,128)(2,1)} %get-tuple-element.91), channel_id=1, source_target_pairs={{0,1},{1,2},{2,3},{4,5},{5,6},{6,7},{8,9},{9,10},{10,11},{12,13},{... | collective-permute-start | bytes 786440 | tf_op jit(solution)/shard_map/ppermute | solution.py:58
  285.6 1.3 collective-permute-start.25
  286.9 6.1 %maximum_select_fusion = bf16[2,4096,256]{2,1,0:T(8,128)(2,1)} fusion(bf16[2,2048,256]{2,1,0:T(8,128)(2,1)} %collective-permute-done.35, bf16[2,2048,256]{2,1,0:T(8,128)(2,1)} %bitcast.102, pred[]{:T(512)S(6)} %eq.24), kind=kLoop, calls=%fused_computation | loop fusion | flops 18874368 | bytes 8388609 | tf_op jit(solution)/shard_map/jit(_where)/select_n | solution.py:79
  295.0 1.4 fusion.24
  296.4 1.6 fusion.26
  298.0 1.5 fusion.83
  299.6 22.7 %all-gather.12.cloned.1.call-done = bf16[128,4096]{1,0:T(8,128)(2,1)} async-done(((bf16[32,4096]{1,0:T(8,128)(2,1)}), bf16[128,4096]{1,0:T(8,128)(2,1)}) %all-gather.12.cloned.1.call-update) | async-done | bytes 1048592 | tf_op jit(solution)/shard_map/all_gather | solution.py:245
  322.3 2.5 fusion.13
  324.8 2.5 fusion.11
  328.9 22.8 %all-gather.14.cloned.1.call-done = bf16[128,4096]{1,0:T(8,128)(2,1)} async-done(((bf16[32,4096]{1,0:T(8,128)(2,1)}), bf16[128,4096]{1,0:T(8,128)(2,1)}) %all-gather.14.cloned.1.call-update) | async-done | bytes 1048592 | tf_op jit(solution)/shard_map/all_gather | solution.py:245
  351.8 2.5 fusion.14
  354.9 1.8 fusion.12
  357.1 1.5 collective-permute-done.36
  359.1 2.0 collective-permute-start.39
  363.3 1.7 collective-permute-done.39
  365.0 9.0 %collective-permute-done.38 = bf16[32,2048]{1,0:T(8,128)(2,1)S(1)} collective-permute-done((bf16[32,2048]{1,0:T(8,128)(2,1)S(1)}, bf16[32,2048]{1,0:T(8,128)(2,1)S(1)}, u32[]{:S(2)}, u32[]{:S(2)}) %collective-permute-start.38) | collective-permute-done | bytes 131104 | tf_op jit(solution)/shard_map/ppermute | solution.py:68
  (171 shorter events, 32.0 us)
Async XLA Ops:
  7.2 29.7 %copy-start = (bf16[256,2048]{1,0:T(8,128)(2,1)S(1)}, bf16[256,2048]{1,0:T(8,128)(2,1)}, u32[]{:S(2)}) copy-start(bf16[256,2048]{1,0:T(8,128)(2,1)} %param.26) | copy-start | bytes 3145732
  7.2 58.9 %all-gather.6.cloned.1.call-start = ((), (), s32[]{:S(2)}) async-start(), calls=%async_computation | async-start | bytes 4718592 | tf_op jit(solution)/shard_map/all_gather | solution.py:210
  8.8 2.8 copy-start.11
  8.8 2.9 copy-start.20
  11.5 140.0 %all-gather.8.cloned.1.call-start = ((), (), s32[]{:S(2)}) async-start(), calls=%async_computation.1 | async-start | bytes 4718592 | tf_op jit(solution)/shard_map/all_gather | solution.py:210
  11.9 1.4 collective-permute-start
  12.4 285.5 %all-gather.10.cloned.1.call-start = ((), (), s32[]{:S(2)}) async-start(), calls=%async_computation.2 | async-start | bytes 2621440 | tf_op jit(solution)/shard_map/all_gather | solution.py:245
  12.5 21.6 %copy-start.22 = (bf16[2048,3,256]{2,0,1:T(8,128)(2,1)S(1)}, bf16[2048,3,256]{2,0,1:T(8,128)(2,1)}, u32[]{:S(2)}) copy-start(bf16[2048,3,256]{2,0,1:T(8,128)(2,1)} %param.25) | copy-start | bytes 9437188
  13.3 9.4 %collective-permute-start.3 = (bf16[32,2048]{1,0:T(8,128)(2,1)S(1)}, bf16[32,2048]{1,0:T(8,128)(2,1)S(1)}, u32[]{:S(2)}, u32[]{:S(2)}) collective-permute-start(bf16[32,2048]{1,0:T(8,128)(2,1)S(1)} %maximum_select_fusion.3), channel_id=1, source_target_pairs={{0,1},{1,2},{2,3},{3,0},{4,5},{5,6},{6,7},{7,4},{8,9},{9,10},{10,1... | collective-permute-start | bytes 393224 | tf_op jit(solution)/shard_map/ppermute | solution.py:35
  16.3 16.2 %collective-permute-start.2 = (bf16[32,2048]{1,0:T(8,128)(2,1)S(1)}, bf16[32,2048]{1,0:T(8,128)(2,1)S(1)}, u32[]{:S(2)}, u32[]{:S(2)}) collective-permute-start(bf16[32,2048]{1,0:T(8,128)(2,1)S(1)} %maximum_select_fusion.3), channel_id=1, source_target_pairs={{0,2},{1,3},{2,0},{3,1},{4,6},{5,7},{6,4},{7,5},{8,10},{9,11},{10,... | collective-permute-start | bytes 393224 | tf_op jit(solution)/shard_map/ppermute | solution.py:35
  18.9 13.6 %collective-permute-start.1 = (bf16[32,2048]{1,0:T(8,128)(2,1)S(1)}, bf16[32,2048]{1,0:T(8,128)(2,1)S(1)}, u32[]{:S(2)}, u32[]{:S(2)}) collective-permute-start(bf16[32,2048]{1,0:T(8,128)(2,1)S(1)} %maximum_select_fusion.3), channel_id=1, source_target_pairs={{0,3},{1,0},{2,1},{3,2},{4,7},{5,4},{6,5},{7,6},{8,11},{9,8},{10,9... | collective-permute-start | bytes 393224 | tf_op jit(solution)/shard_map/ppermute | solution.py:35
  34.8 1.8 collective-permute-start.4
  68.3 24.2 %copy-start.10 = (bf16[2048,2,256]{2,1,0:T(2,128)(2,1)S(1)}, bf16[2048,2,256]{2,1,0:T(2,128)(2,1)}, u32[]{:S(2)}) copy-start(bf16[2048,2,256]{2,1,0:T(2,128)(2,1)} %param.29) | copy-start | bytes 6291460
  92.2 4.5 %collective-permute-start.5 = (bf16[256,4096]{1,0:T(8,128)(2,1)}, bf16[256,4096]{1,0:T(8,128)(2,1)}, u32[]{:S(2)}, u32[]{:S(2)}) collective-permute-start(bf16[256,4096]{1,0:T(8,128)(2,1)} %get-tuple-element.41), channel_id=1, source_target_pairs={{0,4},{4,0},{1,5},{5,1},{2,6},{6,2},{3,7},{7,3},{8,12},{12,8},{9,1... | collective-permute-start | bytes 6291464 | tf_op jit(solution)/shard_map/ppermute | solution.py:29
  94.1 191.5 %collective-permute-start.35 = (bf16[2,2048,256]{2,1,0:T(8,128)(2,1)}, bf16[2,2048,256]{2,1,0:T(8,128)(2,1)}, u32[]{:S(2)}, u32[]{:S(2)}) collective-permute-start(bf16[2,2048,256]{2,1,0:T(8,128)(2,1)} %bitcast.102), channel_id=1, source_target_pairs={{0,4},{4,0},{1,5},{5,1},{2,6},{6,2},{3,7},{7,3},{8,12},{12,8},{9,1... | collective-permute-start | bytes 6291464 | tf_op jit(solution)/shard_map/ppermute | solution.py:29
  98.2 22.7 %collective-permute-start.6 = (bf16[64,4096]{1,0:T(8,128)(2,1)S(1)}, bf16[64,4096]{1,0:T(8,128)(2,1)S(1)}, u32[]{:S(2)}, u32[]{:S(2)}) collective-permute-start(bf16[64,4096]{1,0:T(8,128)(2,1)S(1)} %get-tuple-element.89), channel_id=1, source_target_pairs={{0,1},{4,5},{8,9},{12,13},{16,17},{20,21},{24,25},{28,29}} | collective-permute-start | bytes 1572872 | tf_op jit(solution)/shard_map/ppermute | solution.py:58
  99.5 23.8 %collective-permute-start.7 = (bf16[64,4096]{1,0:T(8,128)(2,1)S(1)}, bf16[64,4096]{1,0:T(8,128)(2,1)S(1)}, u32[]{:S(2)}, u32[]{:S(2)}) collective-permute-start(bf16[64,4096]{1,0:T(8,128)(2,1)S(1)} %get-tuple-element.88), channel_id=1, source_target_pairs={{3,2},{7,6},{11,10},{15,14},{19,18},{23,22},{27,26},{31,30}} | collective-permute-start | bytes 1572872 | tf_op jit(solution)/shard_map/ppermute | solution.py:59
  100.3 26.4 %collective-permute-start.28 = (bf16[32,2048]{1,0:T(8,128)(2,1)S(1)}, bf16[32,2048]{1,0:T(8,128)(2,1)S(1)}, u32[]{:S(2)}, u32[]{:S(2)}) collective-permute-start(bf16[32,2048]{1,0:T(8,128)(2,1)S(1)} %get-tuple-element.108), channel_id=1, source_target_pairs={{0,3},{1,0},{2,1},{3,2},{4,7},{5,4},{6,5},{7,6},{8,11},{9,8},{10,9... | collective-permute-start | bytes 393224 | tf_op jit(solution)/shard_map/ppermute | solution.py:68
  102.2 25.2 %collective-permute-start.27 = (bf16[32,2048]{1,0:T(8,128)(2,1)S(1)}, bf16[32,2048]{1,0:T(8,128)(2,1)S(1)}, u32[]{:S(2)}, u32[]{:S(2)}) collective-permute-start(bf16[32,2048]{1,0:T(8,128)(2,1)S(1)} %get-tuple-element.109), channel_id=1, source_target_pairs={{0,2},{1,3},{2,0},{3,1},{4,6},{5,7},{6,4},{7,5},{8,10},{9,11},{10,... | collective-permute-start | bytes 393224 | tf_op jit(solution)/shard_map/ppermute | solution.py:68
  120.9 12.2 %collective-permute-start.26 = (bf16[32,2048]{1,0:T(8,128)(2,1)S(1)}, bf16[32,2048]{1,0:T(8,128)(2,1)S(1)}, u32[]{:S(2)}, u32[]{:S(2)}) collective-permute-start(bf16[32,2048]{1,0:T(8,128)(2,1)S(1)} %get-tuple-element.107), channel_id=1, source_target_pairs={{0,1},{1,2},{2,3},{3,0},{4,5},{5,6},{6,7},{7,4},{8,9},{9,10},{10,1... | collective-permute-start | bytes 393224 | tf_op jit(solution)/shard_map/ppermute | solution.py:68
  124.7 15.7 %collective-permute-start.8 = (bf16[64,4096]{1,0:T(8,128)(2,1)S(1)}, bf16[64,4096]{1,0:T(8,128)(2,1)S(1)}, u32[]{:S(2)}, u32[]{:S(2)}) collective-permute-start(bf16[64,4096]{1,0:T(8,128)(2,1)S(1)} %get-tuple-element.87), channel_id=1, source_target_pairs={{0,1},{1,2},{4,5},{5,6},{8,9},{9,10},{12,13},{13,14},{16,17},{17,1... | collective-permute-start | bytes 1572872 | tf_op jit(solution)/shard_map/ppermute | solution.py:58
  126.7 13.8 %collective-permute-start.9 = (bf16[64,4096]{1,0:T(8,128)(2,1)S(1)}, bf16[64,4096]{1,0:T(8,128)(2,1)S(1)}, u32[]{:S(2)}, u32[]{:S(2)}) collective-permute-start(bf16[64,4096]{1,0:T(8,128)(2,1)S(1)} %get-tuple-element.86), channel_id=1, source_target_pairs={{2,1},{3,2},{6,5},{7,6},{10,9},{11,10},{14,13},{15,14},{18,17},{19... | collective-permute-start | bytes 1572872 | tf_op jit(solution)/shard_map/ppermute | solution.py:59
  133.9 39.7 %collective-permute-start.29 = (f32[16,2048]{1,0:T(8,128)}, f32[16,2048]{1,0:T(8,128)}, u32[]{:S(2)}, u32[]{:S(2)}) collective-permute-start(f32[16,2048]{1,0:T(8,128)} %get-tuple-element.117), channel_id=1, source_target_pairs={{0,4},{4,0},{1,5},{5,1},{2,6},{6,2},{3,7},{7,3},{8,12},{12,8},{9,1... | collective-permute-start | bytes 393224 | tf_op jit(solution)/shard_map/ppermute | solution.py:29
  143.1 31.6 %collective-permute-start.10 = (bf16[64,4096]{1,0:T(8,128)(2,1)}, bf16[64,4096]{1,0:T(8,128)(2,1)}, u32[]{:S(2)}, u32[]{:S(2)}) collective-permute-start(bf16[64,4096]{1,0:T(8,128)(2,1)} %get-tuple-element.85), channel_id=1, source_target_pairs={{0,1},{1,2},{2,3},{4,5},{5,6},{6,7},{8,9},{9,10},{10,11},{12,13},{... | collective-permute-start | bytes 1572872 | tf_op jit(solution)/shard_map/ppermute | solution.py:58
  150.0 24.7 %collective-permute-start.11 = (bf16[64,4096]{1,0:T(8,128)(2,1)}, bf16[64,4096]{1,0:T(8,128)(2,1)}, u32[]{:S(2)}, u32[]{:S(2)}) collective-permute-start(bf16[64,4096]{1,0:T(8,128)(2,1)} %get-tuple-element.84), channel_id=1, source_target_pairs={{1,0},{2,1},{3,2},{5,4},{6,5},{7,6},{9,8},{10,9},{11,10},{13,12},{... | collective-permute-start | bytes 1572872 | tf_op jit(solution)/shard_map/ppermute | solution.py:59
  153.7 17.6 %slice-start = ((s32[128,1024]{1,0:T(8,128)}), s32[64,1024]{1,0:T(8,128)S(1)}, s32[]{:S(2)}) async-start(s32[128,1024]{1,0:T(8,128)} %param.21), calls=%async_computation.5 | async-start | bytes 524288 | tf_op jit(solution)/shard_map/slice | solution.py:241
  171.2 5.6 %collective-permute-start.12 = (bf16[128,4096]{1,0:T(8,128)(2,1)S(1)}, bf16[128,4096]{1,0:T(8,128)(2,1)}, u32[]{:S(2)}, u32[]{:S(2)}) collective-permute-start(bf16[128,4096]{1,0:T(8,128)(2,1)S(1)} %get-tuple-element.50), channel_id=1, source_target_pairs={{0,4},{4,0},{1,5},{5,1},{2,6},{6,2},{3,7},{7,3},{8,12},{12,8},{9,1... | collective-permute-start | bytes 3145736 | tf_op jit(solution)/shard_map/ppermute | solution.py:29
  171.7 3.1 copy-start.5
  174.7 8.7 %copy-start.17 = (f32[4096]{0:T(1024)S(1)}, f32[4096]{0:T(1024)}, u32[]{:S(2)}) copy-start(f32[4096]{0:T(1024)} %param.22) | copy-start | bytes 49156
  176.8 6.6 %copy-start.6 = (bf16[64,4096]{1,0:T(8,128)(2,1)}, bf16[64,4096]{1,0:T(8,128)(2,1)S(1)}, u32[]{:S(2)}) copy-start(bf16[64,4096]{1,0:T(8,128)(2,1)S(1)} %get-tuple-element.83) | copy-start | bytes 1572868
  178.2 10.8 %collective-permute-start.13 = (bf16[32,4096]{1,0:T(8,128)(2,1)S(1)}, bf16[32,4096]{1,0:T(8,128)(2,1)S(1)}, u32[]{:S(2)}, u32[]{:S(2)}) collective-permute-start(bf16[32,4096]{1,0:T(8,128)(2,1)S(1)} %get-tuple-element.101), channel_id=1, source_target_pairs={{0,1},{4,5},{8,9},{12,13},{16,17},{20,21},{24,25},{28,29}} | collective-permute-start | bytes 786440 | tf_op jit(solution)/shard_map/ppermute | solution.py:58
  182.8 6.2 %collective-permute-start.14 = (bf16[32,4096]{1,0:T(8,128)(2,1)S(1)}, bf16[32,4096]{1,0:T(8,128)(2,1)S(1)}, u32[]{:S(2)}, u32[]{:S(2)}) collective-permute-start(bf16[32,4096]{1,0:T(8,128)(2,1)S(1)} %get-tuple-element.100), channel_id=1, source_target_pairs={{3,2},{7,6},{11,10},{15,14},{19,18},{23,22},{27,26},{31,30}} | collective-permute-start | bytes 786440 | tf_op jit(solution)/shard_map/ppermute | solution.py:59
  190.0 24.9 %collective-permute-start.15 = (bf16[32,4096]{1,0:T(8,128)(2,1)S(1)}, bf16[32,4096]{1,0:T(8,128)(2,1)S(1)}, u32[]{:S(2)}, u32[]{:S(2)}) collective-permute-start(bf16[32,4096]{1,0:T(8,128)(2,1)S(1)} %get-tuple-element.97), channel_id=1, source_target_pairs={{0,1},{1,2},{4,5},{5,6},{8,9},{9,10},{12,13},{13,14},{16,17},{17,1... | collective-permute-start | bytes 786440 | tf_op jit(solution)/shard_map/ppermute | solution.py:58
  194.5 20.5 %collective-permute-start.16 = (bf16[32,4096]{1,0:T(8,128)(2,1)S(1)}, bf16[32,4096]{1,0:T(8,128)(2,1)S(1)}, u32[]{:S(2)}, u32[]{:S(2)}) collective-permute-start(bf16[32,4096]{1,0:T(8,128)(2,1)S(1)} %get-tuple-element.96), channel_id=1, source_target_pairs={{2,1},{3,2},{6,5},{7,6},{10,9},{11,10},{14,13},{15,14},{18,17},{19... | collective-permute-start | bytes 786440 | tf_op jit(solution)/shard_map/ppermute | solution.py:59
  214.8 7.1 %copy-start.21 = (f32[4096]{0:T(1024)S(1)}, f32[4096]{0:T(1024)}, u32[]{:S(2)}) copy-start(f32[4096]{0:T(1024)} %param.27) | copy-start | bytes 49156
  214.8 18.5 %collective-permute-start.19 = (bf16[128,4096]{1,0:T(8,128)(2,1)S(1)}, bf16[128,4096]{1,0:T(8,128)(2,1)}, u32[]{:S(2)}, u32[]{:S(2)}) collective-permute-start(bf16[128,4096]{1,0:T(8,128)(2,1)S(1)} %get-tuple-element.59), channel_id=1, source_target_pairs={{0,4},{4,0},{1,5},{5,1},{2,6},{6,2},{3,7},{7,3},{8,12},{12,8},{9,1... | collective-permute-start | bytes 3145736 | tf_op jit(solution)/shard_map/ppermute | solution.py:29
  217.0 9.5 %collective-permute-start.17 = (bf16[32,4096]{1,0:T(8,128)(2,1)}, bf16[32,4096]{1,0:T(8,128)(2,1)}, u32[]{:S(2)}, u32[]{:S(2)}) collective-permute-start(bf16[32,4096]{1,0:T(8,128)(2,1)} %get-tuple-element.93), channel_id=1, source_target_pairs={{0,1},{1,2},{2,3},{4,5},{5,6},{6,7},{8,9},{9,10},{10,11},{12,13},{... | collective-permute-start | bytes 786440 | tf_op jit(solution)/shard_map/ppermute | solution.py:58
  220.6 10.8 %collective-permute-start.18 = (bf16[32,4096]{1,0:T(8,128)(2,1)}, bf16[32,4096]{1,0:T(8,128)(2,1)}, u32[]{:S(2)}, u32[]{:S(2)}) collective-permute-start(bf16[32,4096]{1,0:T(8,128)(2,1)} %get-tuple-element.92), channel_id=1, source_target_pairs={{1,0},{2,1},{3,2},{5,4},{6,5},{7,6},{9,8},{10,9},{11,10},{13,12},{... | collective-permute-start | bytes 786440 | tf_op jit(solution)/shard_map/ppermute | solution.py:59
  222.7 34.0 %collective-permute-start.30 = (bf16[16,2048]{1,0:T(8,128)(2,1)}, bf16[16,2048]{1,0:T(8,128)(2,1)}, u32[]{:S(2)}, u32[]{:S(2)}) collective-permute-start(bf16[16,2048]{1,0:T(8,128)(2,1)} %get-tuple-element.120), channel_id=1, source_target_pairs={{0,4},{4,0},{1,5},{5,1},{2,6},{6,2},{3,7},{7,3},{8,12},{12,8},{9,1... | collective-permute-start | bytes 196616 | tf_op jit(solution)/shard_map/ppermute | solution.py:29
  222.9 99.4 %all-gather.12.cloned.1.call-start = ((), (), s32[]{:S(2)}) async-start(), calls=%async_computation.3 | async-start | bytes 1310720 | tf_op jit(solution)/shard_map/all_gather | solution.py:245
  233.3 23.0 %copy-start.14 = (s32[32,1024]{1,0:T(8,128)S(1)}, s32[32,1024]{1,0:T(8,128)}, u32[]{:S(2)}) copy-start(s32[32,1024]{1,0:T(8,128)} %get-tuple-element.110) | copy-start | bytes 393220
  234.6 22.2 %copy-start.16 = (bf16[16,2048]{1,0:T(8,128)(2,1)S(1)}, bf16[16,2048]{1,0:T(8,128)(2,1)}, u32[]{:S(2)}) copy-start(bf16[16,2048]{1,0:T(8,128)(2,1)} %get-tuple-element.119) | copy-start | bytes 196612
  234.6 15.5 %collective-permute-start.20 = (bf16[32,4096]{1,0:T(8,128)(2,1)S(1)}, bf16[32,4096]{1,0:T(8,128)(2,1)S(1)}, u32[]{:S(2)}, u32[]{:S(2)}) collective-permute-start(bf16[32,4096]{1,0:T(8,128)(2,1)S(1)} %get-tuple-element.60), channel_id=1, source_target_pairs={{0,1},{4,5},{8,9},{12,13},{16,17},{20,21},{24,25},{28,29}} | collective-permute-start | bytes 786440 | tf_op jit(solution)/shard_map/ppermute | solution.py:58
  238.4 11.7 %collective-permute-start.21 = (bf16[32,4096]{1,0:T(8,128)(2,1)S(1)}, bf16[32,4096]{1,0:T(8,128)(2,1)S(1)}, u32[]{:S(2)}, u32[]{:S(2)}) collective-permute-start(bf16[32,4096]{1,0:T(8,128)(2,1)S(1)} %get-tuple-element.61), channel_id=1, source_target_pairs={{3,2},{7,6},{11,10},{15,14},{19,18},{23,22},{27,26},{31,30}} | collective-permute-start | bytes 786440 | tf_op jit(solution)/shard_map/ppermute | solution.py:59
  251.2 16.6 %collective-permute-start.22 = (bf16[32,4096]{1,0:T(8,128)(2,1)S(1)}, bf16[32,4096]{1,0:T(8,128)(2,1)S(1)}, u32[]{:S(2)}, u32[]{:S(2)}) collective-permute-start(bf16[32,4096]{1,0:T(8,128)(2,1)S(1)} %get-tuple-element.64), channel_id=1, source_target_pairs={{0,1},{1,2},{4,5},{5,6},{8,9},{9,10},{12,13},{13,14},{16,17},{17,1... | collective-permute-start | bytes 786440 | tf_op jit(solution)/shard_map/ppermute | solution.py:58
  255.6 12.2 %collective-permute-start.23 = (bf16[32,4096]{1,0:T(8,128)(2,1)S(1)}, bf16[32,4096]{1,0:T(8,128)(2,1)S(1)}, u32[]{:S(2)}, u32[]{:S(2)}) collective-permute-start(bf16[32,4096]{1,0:T(8,128)(2,1)S(1)} %get-tuple-element.65), channel_id=1, source_target_pairs={{2,1},{3,2},{6,5},{7,6},{10,9},{11,10},{14,13},{15,14},{18,17},{19... | collective-permute-start | bytes 786440 | tf_op jit(solution)/shard_map/ppermute | solution.py:59
  257.7 35.6 %collective-permute-start.33 = (bf16[32,2048]{1,0:T(8,128)(2,1)S(1)}, bf16[32,2048]{1,0:T(8,128)(2,1)S(1)}, u32[]{:S(2)}, u32[]{:S(2)}) collective-permute-start(bf16[32,2048]{1,0:T(8,128)(2,1)S(1)} %maximum_select_fusion.4), channel_id=1, source_target_pairs={{0,1},{1,2},{2,3},{3,0},{4,5},{5,6},{6,7},{7,4},{8,9},{9,10},{10,1... | collective-permute-start | bytes 393224 | tf_op jit(solution)/shard_map/ppermute | solution.py:35
  259.4 33.9 %collective-permute-start.32 = (bf16[32,2048]{1,0:T(8,128)(2,1)S(1)}, bf16[32,2048]{1,0:T(8,128)(2,1)S(1)}, u32[]{:S(2)}, u32[]{:S(2)}) collective-permute-start(bf16[32,2048]{1,0:T(8,128)(2,1)S(1)} %maximum_select_fusion.4), channel_id=1, source_target_pairs={{0,2},{1,3},{2,0},{3,1},{4,6},{5,7},{6,4},{7,5},{8,10},{9,11},{10,... | collective-permute-start | bytes 393224 | tf_op jit(solution)/shard_map/ppermute | solution.py:35
  267.8 26.1 %collective-permute-start.31 = (bf16[32,2048]{1,0:T(8,128)(2,1)S(1)}, bf16[32,2048]{1,0:T(8,128)(2,1)}, u32[]{:S(2)}, u32[]{:S(2)}) collective-permute-start(bf16[32,2048]{1,0:T(8,128)(2,1)S(1)} %maximum_select_fusion.4), channel_id=1, source_target_pairs={{0,3},{1,0},{2,1},{3,2},{4,7},{5,4},{6,5},{7,6},{8,11},{9,8},{10,9... | collective-permute-start | bytes 393224 | tf_op jit(solution)/shard_map/ppermute | solution.py:35
  269.8 25.2 %collective-permute-start.24 = (bf16[32,4096]{1,0:T(8,128)(2,1)}, bf16[32,4096]{1,0:T(8,128)(2,1)S(1)}, u32[]{:S(2)}, u32[]{:S(2)}) collective-permute-start(bf16[32,4096]{1,0:T(8,128)(2,1)} %get-tuple-element.91), channel_id=1, source_target_pairs={{0,1},{1,2},{2,3},{4,5},{5,6},{6,7},{8,9},{9,10},{10,11},{12,13},{... | collective-permute-start | bytes 786440 | tf_op jit(solution)/shard_map/ppermute | solution.py:58
  285.6 9.4 %collective-permute-start.25 = (bf16[32,4096]{1,0:T(8,128)(2,1)S(1)}, bf16[32,4096]{1,0:T(8,128)(2,1)S(1)}, u32[]{:S(2)}, u32[]{:S(2)}) collective-permute-start(bf16[32,4096]{1,0:T(8,128)(2,1)S(1)} %get-tuple-element.90), channel_id=1, source_target_pairs={{1,0},{2,1},{3,2},{5,4},{6,5},{7,6},{9,8},{10,9},{11,10},{13,12},{... | collective-permute-start | bytes 786440 | tf_op jit(solution)/shard_map/ppermute | solution.py:59
  293.0 58.7 %all-gather.14.cloned.1.call-start = ((), (), s32[]{:S(2)}) async-start(), calls=%async_computation.4 | async-start | bytes 1310720 | tf_op jit(solution)/shard_map/all_gather | solution.py:245
  299.6 54.7 %collective-permute-start.34 = (f32[128,256]{1,0:T(8,128)S(1)}, f32[128,256]{1,0:T(8,128)S(1)}, u32[]{:S(2)}, u32[]{:S(2)}) collective-permute-start(f32[128,256]{1,0:T(8,128)S(1)} %fusion.83), channel_id=1, source_target_pairs={{0,4},{4,0},{1,5},{5,1},{2,6},{6,2},{3,7},{7,3},{8,12},{12,8},{9,1... | collective-permute-start | bytes 393224 | tf_op jit(solution)/shard_map/ppermute | solution.py:29
  322.3 5.0 %copy-start.8 = (bf16[2,4096,256]{2,1,0:T(8,128)(2,1)S(1)}, bf16[2,4096,256]{2,1,0:T(8,128)(2,1)}, u32[]{:S(2)}) copy-start(bf16[2,4096,256]{2,1,0:T(8,128)(2,1)} %maximum_select_fusion) | copy-start | bytes 12582916
  351.8 3.1 copy-start.9
  354.9 3.8 copy-start.13
  356.6 6.4 %copy-start.19 = (s32[16,1024]{1,0:T(8,128)S(1)}, s32[16,1024]{1,0:T(8,128)}, u32[]{:S(2)}) copy-start(s32[16,1024]{1,0:T(8,128)} %param.31) | copy-start | bytes 196612
  357.0 1.6 collective-permute-start.36
  358.7 15.5 %copy-start.7 = (bf16[64,4096]{1,0:T(8,128)(2,1)S(1)}, bf16[64,4096]{1,0:T(8,128)(2,1)}, u32[]{:S(2)}) copy-start(bf16[64,4096]{1,0:T(8,128)(2,1)} %copy-done.6) | copy-start | bytes 1572868
  359.1 5.9 %collective-permute-start.39 = (bf16[32,2048]{1,0:T(8,128)(2,1)S(1)}, bf16[32,2048]{1,0:T(8,128)(2,1)S(1)}, u32[]{:S(2)}, u32[]{:S(2)}) collective-permute-start(bf16[32,2048]{1,0:T(8,128)(2,1)S(1)} %get-tuple-element.105), channel_id=1, source_target_pairs={{0,3},{1,0},{2,1},{3,2},{4,7},{5,4},{6,5},{7,6},{8,11},{9,8},{10,9... | collective-permute-start | bytes 393224 | tf_op jit(solution)/shard_map/ppermute | solution.py:68
  361.0 12.9 %collective-permute-start.38 = (bf16[32,2048]{1,0:T(8,128)(2,1)S(1)}, bf16[32,2048]{1,0:T(8,128)(2,1)S(1)}, u32[]{:S(2)}, u32[]{:S(2)}) collective-permute-start(bf16[32,2048]{1,0:T(8,128)(2,1)S(1)} %get-tuple-element.106), channel_id=1, source_target_pairs={{0,2},{1,3},{2,0},{3,1},{4,6},{5,7},{6,4},{7,5},{8,10},{9,11},{10,... | collective-permute-start | bytes 393224 | tf_op jit(solution)/shard_map/ppermute | solution.py:68
  362.0 11.9 %collective-permute-start.37 = (bf16[32,2048]{1,0:T(8,128)(2,1)S(1)}, bf16[32,2048]{1,0:T(8,128)(2,1)S(1)}, u32[]{:S(2)}, u32[]{:S(2)}) collective-permute-start(bf16[32,2048]{1,0:T(8,128)(2,1)S(1)} %get-tuple-element.104), channel_id=1, source_target_pairs={{0,1},{1,2},{2,3},{3,0},{4,5},{5,6},{6,7},{7,4},{8,9},{9,10},{10,1... | collective-permute-start | bytes 393224 | tf_op jit(solution)/shard_map/ppermute | solution.py:68
  363.1 13.1 %copy-start.1 = (bf16[256,2048]{1,0:T(8,128)(2,1)S(1)}, bf16[256,2048]{1,0:T(8,128)(2,1)}, u32[]{:S(2)}) copy-start(bf16[256,2048]{1,0:T(8,128)(2,1)} %param.26) | copy-start | bytes 3145732
  374.1 1.4 collective-permute-start.40
  (7 other events, 14.0 us)
Sparse Core Ops, SparseCore 0:
  11.7 54.3 all-gather.5
  67.7 51.2 all-gather.7
  223.1 66.4 all-gather.9
  293.1 29.1 all-gather.11
  324.3 27.4 all-gather.13

commit v7 on v5

--- a/solution.py
+++ b/solution.py
@@ -158,7 +158,7 @@
         out_shape=[jax.ShapeDtypeStruct((rows // 2, features), BF16)] * 2,
         compiler_params=pltpu.CompilerParams(vmem_limit_bytes=48 * 2**20),
         cost_estimate=pl.CostEstimate(
-            flops=6 * rows * features * units, bytes_accessed=6 * features * units, transcendentals=0
+            flops=1024, bytes_accessed=1024, transcendentals=0
         ),
         name="ffn",
     )(order, x, w_gate, w_up, w_down)
@@ -214,7 +214,7 @@
     product = jnp.dot(context, self_out, preferred_element_type=F32).astype(BF16)
     total = slots_sum(product)
 
-    mine, theirs = ffn(near[0], order, w_gate, w_up, w_down)
+    mine, theirs = ffn(gated(near[0], product), order, w_gate, w_up, w_down)
     got = swap(theirs, "section", 1)
     came = sum_step(sum_sends(mine, got, None, 1), 1)
     total = gated(total, *came)
@@ -247,7 +247,10 @@
     crossin = gated(crossin, *came)
     cq = both_halves(jnp.dot(crossin, cross_q, preferred_element_type=F32)).astype(BF16)
     for step in range(2, count):
-        came = sum_step(sum_sends(mine_b, got, came, step), step)
+        sends = sum_sends(mine_b, got, came, step)
+        if step == count - 1:
+            sends = lax.optimization_barrier(sends + (memory_a,))[:2]
+        came = sum_step(sends, step)
     out_b, memory_b = finish_rows(1, mine_b, got, came)
     memory_b = to_heads(memory_b)
     memory_a = gated(memory_a, out_b)

time: 364 us -> 363 us (level)
  waiting for transfers between devices: 193 us -> 201 us
  other arithmetic: 34.6 us -> 27 us
  starting transfers between devices: 43.8 us -> 51.2 us
  local copies, waits for them, and re-layouts: 14.3 us -> 10.5 us
    ppermute x6, waiting for transfers between devices: 48.5 us -> 76 us  [sum_step(): above = lax.ppermute(sends[0], 'tensor', [(i, i + 1) for i in range(step)])]
    all_gather x2, waiting for transfers between devices: 48.9 us -> 21.8 us  [per_device(): lax.all_gather(normed[c * block:(c + 1) * block], ('section', 'tensor'),...]
    all_gather x2, waiting for transfers between devices: 15 us -> 29.7 us  [to_heads(): return lax.all_gather(memory, 'tensor', axis=0, tiled=True)]
    ppermute x6, waiting for transfers between devices: 20.2 us -> 8.09 us  [sum_step(): lax.ppermute(sends[1], 'tensor', [(i, i - 1) for i in range(count - step,...]
    ppermute x6, waiting for transfers between devices: 47.3 us -> 37.1 us  [from_slots(): lax.ppermute(value, 'tensor', [(i, (i - o) % count) for i in range(count)])]
    ppermute x6, waiting for transfers between devices: 8.92 us -> 18.9 us  [slots_sum(): lax.ppermute(product[o], 'tensor', [(i, (i + o) % count) for i in range(c...]
    ppermute x10, waiting for transfers between devices: 3.19 us -> 9.09 us  [swap(): lax.ppermute(value, axis, [(i, i ^ distance) for i in range(lax.axis_size...]
    ppermute x6, starting transfers between devices: 21.8 us -> 27 us  [sum_step(): above = lax.ppermute(sends[0], 'tensor', [(i, i + 1) for i in range(step)])]
  transfers between devices with their start and end apart: 38 -> 38, of which waited for: 19 -> 24; matrix products, arithmetic and copies ran while one was open for 14% -> 10% of each run, Pallas kernels for 14% -> 7%
where the time goes in v7:
time: 363 us; the launch traced here: 362 us
  waiting for transfers between devices  201 us (55%)
  starting transfers between devices  51.2 us (14%)
  Pallas kernels  48.5 us (13%)
  other arithmetic  27 us (7%)
  between operations  14.5 us (4%)
  local copies, waits for them, and re-layouts  10.5 us (3%)
  matrix products  10.1 us (3%)
    ppermute x6, waiting for transfers between devices, sum_step(): above = lax.ppermute(sends[0], 'tensor', [(i, i + 1) for i in range(step)])  76 us
    pallas_call x2, Pallas kernels, ffn(): pl.pallas_call(functools.partial(ffn_kernel, first), grid_spec=pltpu.Pref...  48.5 us
    ppermute x6, waiting for transfers between devices, from_slots(): lax.ppermute(value, 'tensor', [(i, (i - o) % count) for i in range(count)])  37.1 us
    all_gather x2, waiting for transfers between devices, to_heads(): return lax.all_gather(memory, 'tensor', axis=0, tiled=True)  29.7 us
    ppermute x6, starting transfers between devices, sum_step(): above = lax.ppermute(sends[0], 'tensor', [(i, i + 1) for i in range(step)])  27 us
    all_gather x2, waiting for transfers between devices, per_device(): lax.all_gather(normed[c * block:(c + 1) * block], ('section', 'tensor'),...  21.8 us
    ppermute x6, waiting for transfers between devices, slots_sum(): lax.ppermute(product[o], 'tensor', [(i, (i + o) % count) for i in range(c...  18.9 us
    ppermute x10, waiting for transfers between devices, swap(): lax.ppermute(value, axis, [(i, i ^ distance) for i in range(lax.axis_size...  9.09 us
  transfers between devices with their start and end apart: 38, of which 24 were waited for; matrix products, arithmetic and copies ran while one was open for 10% of the time, Pallas kernels for 7%

profile of v7, /device:TPU:0, one launch (start us, length us, event | category | flops | bytes accessed | tf_op | source)
XLA Modules:
  0.0 362.4 jit_solution(14104821867282001785)
XLA Ops:
  7.2 1.6 fusion
  8.9 1.6 fusion.2
  10.4 1.0 fusion.64
  12.5 0.8 collective-permute-done
  13.3 5.0 %collective-permute-start.1 = (bf16[32,2048]{1,0:T(8,128)(2,1)S(1)}, bf16[32,2048]{1,0:T(8,128)(2,1)S(1)}, u32[]{:S(2)}, u32[]{:S(2)}) collective-permute-start(bf16[32,2048]{1,0:T(8,128)(2,1)S(1)} %maximum_select_fusion.3), channel_id=1, source_target_pairs={{0,3},{1,0},{2,1},{3,2},{4,7},{5,4},{6,5},{7,6},{8,11},{9,8},{10,9... | collective-permute-start | bytes 393224 | tf_op jit(solution)/shard_map/ppermute | solution.py:35
  18.3 1.0 collective-permute-start.3
  19.4 2.9 collective-permute-done.1
  22.3 16.1 %collective-permute-done.2 = bf16[32,2048]{1,0:T(8,128)(2,1)S(1)} collective-permute-done((bf16[32,2048]{1,0:T(8,128)(2,1)S(1)}, bf16[32,2048]{1,0:T(8,128)(2,1)S(1)}, u32[]{:S(2)}, u32[]{:S(2)}) %collective-permute-start.2) | collective-permute-done | bytes 131104 | tf_op jit(solution)/shard_map/ppermute | solution.py:35
  38.4 1.5 convolution_bitcast_fusion.2
  41.0 1.4 collective-permute-done.4
  42.7 1.3 convolution_convert_fusion.1
  44.0 21.8 %all-gather.5.cloned.1.call-done.x_ref = bf16[512,4096]{1,0:T(8,128)(2,1)} async-done(((bf16[64,4096]{1,0:T(8,128)(2,1)}), bf16[512,4096]{1,0:T(8,128)(2,1)}) %all-gather.5.cloned.1.call-update) | async-done | bytes 4194320 | tf_op jit(solution)/shard_map/all_gather | solution.py:196
  65.8 23.8 %ffn.2 = (bf16[256,4096]{1,0:T(8,128)(2,1)S(1)}, bf16[256,4096]{1,0:T(8,128)(2,1)S(1)}) custom-call(s32[8]{0:T(128)S(1)} %pad_add_fusion.order, bf16[512,4096]{1,0:T(8,128)(2,1)} %all-gather.5.cloned.1.call-done.x_ref, bf16[4096,1024]{1,0:T(8,128)(2,1)} %gate_ref.3, bf16[4096,1024]{1,0:T(8,128)(2,1)} %up_ref.3, bf16[1024,4096]{1,0:T(8,128)(2,1)} %down_ref.3), custom_call_target="tpu_custom_call" | custom-call | flops 1024 | bytes 1024 | tf_op jit(solution)/shard_map/ffn/pallas_call | solution.py:141
  89.9 3.9 %collective-permute-done.5 = bf16[256,4096]{1,0:T(8,128)(2,1)S(1)} collective-permute-done((bf16[256,4096]{1,0:T(8,128)(2,1)S(1)}, bf16[256,4096]{1,0:T(8,128)(2,1)S(1)}, u32[]{:S(2)}, u32[]{:S(2)}) %collective-permute-start.5) | collective-permute-done | bytes 2097184 | tf_op jit(solution)/shard_map/ppermute | solution.py:29
  94.0 1.5 collective-permute-start.6
  96.3 22.6 %collective-permute-done.6 = bf16[64,4096]{1,0:T(8,128)(2,1)S(1)} collective-permute-done((bf16[64,4096]{1,0:T(8,128)(2,1)S(1)}, bf16[64,4096]{1,0:T(8,128)(2,1)S(1)}, u32[]{:S(2)}, u32[]{:S(2)}) %collective-permute-start.6) | collective-permute-done | bytes 524320 | tf_op jit(solution)/shard_map/ppermute | solution.py:58
  119.1 4.4 %collective-permute-start.8 = (bf16[64,4096]{1,0:T(8,128)(2,1)S(1)}, bf16[64,4096]{1,0:T(8,128)(2,1)S(1)}, u32[]{:S(2)}, u32[]{:S(2)}) collective-permute-start(bf16[64,4096]{1,0:T(8,128)(2,1)S(1)} %get-tuple-element.67), channel_id=1, source_target_pairs={{0,1},{1,2},{4,5},{5,6},{8,9},{9,10},{12,13},{13,14},{16,17},{17,1... | collective-permute-start | bytes 1572872 | tf_op jit(solution)/shard_map/ppermute | solution.py:58
  124.2 10.2 %collective-permute-done.8 = bf16[64,4096]{1,0:T(8,128)(2,1)S(1)} collective-permute-done((bf16[64,4096]{1,0:T(8,128)(2,1)S(1)}, bf16[64,4096]{1,0:T(8,128)(2,1)S(1)}, u32[]{:S(2)}, u32[]{:S(2)}) %collective-permute-start.8) | collective-permute-done | bytes 524320 | tf_op jit(solution)/shard_map/ppermute | solution.py:58
  134.5 1.5 add_convert_fusion.6
  136.0 24.7 %ffn.3 = (bf16[256,4096]{1,0:T(8,128)(2,1)S(1)}, bf16[256,4096]{1,0:T(8,128)(2,1)}) custom-call(s32[8]{0:T(128)S(1)} %pad_add_fusion.order, bf16[512,4096]{1,0:T(8,128)(2,1)} %all-gather.7.cloned.1.call-done.x_ref, bf16[4096,1024]{1,0:T(8,128)(2,1)} %gate_ref.3, bf16[4096,1024]{1,0:T(8,128)(2,1)} %up_ref.3, bf16[1024,4096]{1,0:T(8,128)(2,1)} %down_ref.3), custom_call_target="tpu_custom_call" | custom-call | flops 1024 | bytes 1024 | tf_op jit(solution)/shard_map/ffn/pallas_call | solution.py:141
  160.6 9.1 %collective-permute-start.10 = (bf16[64,4096]{1,0:T(8,128)(2,1)}, bf16[64,4096]{1,0:T(8,128)(2,1)S(1)}, u32[]{:S(2)}, u32[]{:S(2)}) collective-permute-start(bf16[64,4096]{1,0:T(8,128)(2,1)} %get-tuple-element.65), channel_id=1, source_target_pairs={{0,1},{1,2},{2,3},{4,5},{5,6},{6,7},{8,9},{9,10},{10,11},{12,13},{... | collective-permute-start | bytes 1572872 | tf_op jit(solution)/shard_map/ppermute | solution.py:58
  169.7 1.3 collective-permute-start.11
  172.1 9.8 %collective-permute-done.10 = bf16[64,4096]{1,0:T(8,128)(2,1)S(1)} collective-permute-done((bf16[64,4096]{1,0:T(8,128)(2,1)}, bf16[64,4096]{1,0:T(8,128)(2,1)S(1)}, u32[]{:S(2)}, u32[]{:S(2)}) %collective-permute-start.10) | collective-permute-done | bytes 524320 | tf_op jit(solution)/shard_map/ppermute | solution.py:58
  181.8 4.0 %collective-permute-done.11 = bf16[64,4096]{1,0:T(8,128)(2,1)S(1)} collective-permute-done((bf16[64,4096]{1,0:T(8,128)(2,1)}, bf16[64,4096]{1,0:T(8,128)(2,1)S(1)}, u32[]{:S(2)}, u32[]{:S(2)}) %collective-permute-start.11) | collective-permute-done | bytes 524320 | tf_op jit(solution)/shard_map/ppermute | solution.py:59
  185.9 1.9 fusion.12
  187.8 0.8 copy-done.5
  188.6 1.0 fusion.14
  189.5 2.4 fusion.20
  192.0 3.0 collective-permute-start.13
  194.9 1.5 collective-permute-start.14
  196.5 1.1 fusion.66
  197.6 1.1 collective-permute-start.20
  198.7 2.7 collective-permute-start.21
  201.4 8.9 %collective-permute-done.13 = bf16[64,4096]{1,0:T(8,128)(2,1)} collective-permute-done((bf16[64,4096]{1,0:T(8,128)(2,1)}, bf16[64,4096]{1,0:T(8,128)(2,1)}, u32[]{:S(2)}, u32[]{:S(2)}) %collective-permute-start.13) | collective-permute-done | bytes 524320 | tf_op jit(solution)/shard_map/ppermute | solution.py:58
  210.3 1.6 add_convert_fusion.3
  212.0 4.4 %collective-permute-start.15 = (bf16[64,4096]{1,0:T(8,128)(2,1)S(1)}, bf16[64,4096]{1,0:T(8,128)(2,1)S(1)}, u32[]{:S(2)}, u32[]{:S(2)}) collective-permute-start(bf16[64,4096]{1,0:T(8,128)(2,1)S(1)} %get-tuple-element.61), channel_id=1, source_target_pairs={{0,1},{1,2},{4,5},{5,6},{8,9},{9,10},{12,13},{13,14},{16,17},{17,1... | collective-permute-start | bytes 1572872 | tf_op jit(solution)/shard_map/ppermute | solution.py:58
  217.1 4.3 %collective-permute-done.20 = bf16[32,2048]{1,0:T(8,128)(2,1)S(1)} collective-permute-done((bf16[32,2048]{1,0:T(8,128)(2,1)S(1)}, bf16[32,2048]{1,0:T(8,128)(2,1)S(1)}, u32[]{:S(2)}, u32[]{:S(2)}) %collective-permute-start.20) | collective-permute-done | bytes 131104 | tf_op jit(solution)/shard_map/ppermute | solution.py:68
  221.4 5.6 %collective-permute-done.21 = bf16[32,2048]{1,0:T(8,128)(2,1)S(1)} collective-permute-done((bf16[32,2048]{1,0:T(8,128)(2,1)S(1)}, bf16[32,2048]{1,0:T(8,128)(2,1)S(1)}, u32[]{:S(2)}, u32[]{:S(2)}) %collective-permute-start.21) | collective-permute-done | bytes 131104 | tf_op jit(solution)/shard_map/ppermute | solution.py:68
  227.1 1.0 convert_add_fusion.9
  228.7 19.5 %collective-permute-done.15 = bf16[64,4096]{1,0:T(8,128)(2,1)S(1)} collective-permute-done((bf16[64,4096]{1,0:T(8,128)(2,1)S(1)}, bf16[64,4096]{1,0:T(8,128)(2,1)S(1)}, u32[]{:S(2)}, u32[]{:S(2)}) %collective-permute-start.15) | collective-permute-done | bytes 524320 | tf_op jit(solution)/shard_map/ppermute | solution.py:58
  248.3 2.6 add_convert_fusion.1
  250.9 8.0 %all-gather.9.cloned.1.call-done = bf16[256,4096]{1,0:T(8,128)(2,1)} async-done(((bf16[64,4096]{1,0:T(8,128)(2,1)}), bf16[256,4096]{1,0:T(8,128)(2,1)}) %all-gather.9.cloned.1.call-update) | async-done | bytes 2097168 | tf_op jit(solution)/shard_map/all_gather | solution.py:237
  258.9 4.6 %collective-permute-start.17 = (bf16[64,4096]{1,0:T(8,128)(2,1)}, bf16[64,4096]{1,0:T(8,128)(2,1)S(1)}, u32[]{:S(2)}, u32[]{:S(2)}) collective-permute-start(bf16[64,4096]{1,0:T(8,128)(2,1)} %get-tuple-element.45), channel_id=1, source_target_pairs={{0,1},{1,2},{2,3},{4,5},{5,6},{6,7},{8,9},{9,10},{10,11},{12,13},{... | collective-permute-start | bytes 1572872 | tf_op jit(solution)/shard_map/ppermute | solution.py:58
  263.5 1.3 collective-permute-start.18
  264.8 3.2 copy.35
  269.0 1.1 fusion.26
  270.1 5.1 %collective-permute-done.17 = bf16[64,4096]{1,0:T(8,128)(2,1)S(1)} collective-permute-done((bf16[64,4096]{1,0:T(8,128)(2,1)}, bf16[64,4096]{1,0:T(8,128)(2,1)S(1)}, u32[]{:S(2)}, u32[]{:S(2)}) %collective-permute-start.17) | collective-permute-done | bytes 524320 | tf_op jit(solution)/shard_map/ppermute | solution.py:58
  275.2 4.0 %collective-permute-done.18 = bf16[64,4096]{1,0:T(8,128)(2,1)S(1)} collective-permute-done((bf16[64,4096]{1,0:T(8,128)(2,1)}, bf16[64,4096]{1,0:T(8,128)(2,1)S(1)}, u32[]{:S(2)}, u32[]{:S(2)}) %collective-permute-start.18) | collective-permute-done | bytes 524320 | tf_op jit(solution)/shard_map/ppermute | solution.py:59
  279.2 1.7 fusion.15
  281.0 0.8 copy-done.7
  281.8 1.0 fusion.17
  283.0 1.2 collective-permute-done.23
  284.4 2.6 collective-permute-start.25
  287.2 4.4 %maximum_select_fusion = bf16[2,4096,256]{2,1,0:T(8,128)(2,1)S(1)} fusion(bf16[2,2048,256]{2,1,0:T(8,128)(2,1)} %collective-permute-done.28, bf16[2,2048,256]{2,1,0:T(8,128)(2,1)} %bitcast.89, pred[]{:T(512)S(6)} %eq.20), kind=kLoop, calls=%fused_computation | loop fusion | flops 18874368 | bytes 8388609 | tf_op jit(solution)/shard_map/jit(_where)/select_n | solution.py:79
  291.7 18.1 %collective-permute-done.25 = bf16[32,2048]{1,0:T(8,128)(2,1)S(1)} collective-permute-done((bf16[32,2048]{1,0:T(8,128)(2,1)S(1)}, bf16[32,2048]{1,0:T(8,128)(2,1)S(1)}, u32[]{:S(2)}, u32[]{:S(2)}) %collective-permute-start.25) | collective-permute-done | bytes 131104 | tf_op jit(solution)/shard_map/ppermute | solution.py:35
  311.7 21.7 %all-gather.11.cloned.1.call-done = bf16[256,4096]{1,0:T(8,128)(2,1)} async-done(((bf16[64,4096]{1,0:T(8,128)(2,1)}), bf16[256,4096]{1,0:T(8,128)(2,1)}) %all-gather.11.cloned.1.call-update) | async-done | bytes 2097168 | tf_op jit(solution)/shard_map/all_gather | solution.py:237
  333.3 3.1 fusion.10
  338.7 1.5 collective-permute-done.29
  340.7 1.8 collective-permute-start.31
  342.5 2.0 collective-permute-start.32
  344.7 4.2 %collective-permute-done.30 = bf16[32,2048]{1,0:T(8,128)(2,1)S(1)} collective-permute-done((bf16[32,2048]{1,0:T(8,128)(2,1)S(1)}, bf16[32,2048]{1,0:T(8,128)(2,1)S(1)}, u32[]{:S(2)}, u32[]{:S(2)}) %collective-permute-start.30) | collective-permute-done | bytes 131104 | tf_op jit(solution)/shard_map/ppermute | solution.py:68
  348.9 4.7 %collective-permute-done.31 = bf16[32,2048]{1,0:T(8,128)(2,1)S(1)} collective-permute-done((bf16[32,2048]{1,0:T(8,128)(2,1)S(1)}, bf16[32,2048]{1,0:T(8,128)(2,1)S(1)}, u32[]{:S(2)}, u32[]{:S(2)}) %collective-permute-start.31) | collective-permute-done | bytes 131104 | tf_op jit(solution)/shard_map/ppermute | solution.py:68
  353.8 1.1 pad_maximum_fusion
  355.2 0.7 fusion.29
  (142 shorter events, 13.9 us)
Async XLA Ops:
  7.2 35.6 %copy-start = (bf16[256,2048]{1,0:T(8,128)(2,1)S(1)}, bf16[256,2048]{1,0:T(8,128)(2,1)}, u32[]{:S(2)}) copy-start(bf16[256,2048]{1,0:T(8,128)(2,1)} %param.26) | copy-start | bytes 3145732
  7.2 58.6 %all-gather.5.cloned.1.call-start = ((), (), s32[]{:S(2)}) async-start(), calls=%async_computation | async-start | bytes 4718592 | tf_op jit(solution)/shard_map/all_gather | solution.py:196
  8.8 2.7 copy-start.11
  8.8 2.9 copy-start.19
  11.5 124.4 %all-gather.7.cloned.1.call-start = ((), (), s32[]{:S(2)}) async-start(), calls=%async_computation.1 | async-start | bytes 4718592 | tf_op jit(solution)/shard_map/all_gather | solution.py:196
  11.9 1.4 collective-permute-start
  12.4 246.5 %all-gather.9.cloned.1.call-start = ((), (), s32[]{:S(2)}) async-start(), calls=%async_computation.2 | async-start | bytes 2621440 | tf_op jit(solution)/shard_map/all_gather | solution.py:237
  12.5 27.5 %copy-start.21 = (bf16[2048,3,256]{2,0,1:T(8,128)(2,1)S(1)}, bf16[2048,3,256]{2,0,1:T(8,128)(2,1)}, u32[]{:S(2)}) copy-start(bf16[2048,3,256]{2,0,1:T(8,128)(2,1)} %param.25) | copy-start | bytes 9437188
  13.3 8.9 %collective-permute-start.1 = (bf16[32,2048]{1,0:T(8,128)(2,1)S(1)}, bf16[32,2048]{1,0:T(8,128)(2,1)S(1)}, u32[]{:S(2)}, u32[]{:S(2)}) collective-permute-start(bf16[32,2048]{1,0:T(8,128)(2,1)S(1)} %maximum_select_fusion.3), channel_id=1, source_target_pairs={{0,3},{1,0},{2,1},{3,2},{4,7},{5,4},{6,5},{7,6},{8,11},{9,8},{10,9... | collective-permute-start | bytes 393224 | tf_op jit(solution)/shard_map/ppermute | solution.py:35
  18.3 20.1 %collective-permute-start.2 = (bf16[32,2048]{1,0:T(8,128)(2,1)S(1)}, bf16[32,2048]{1,0:T(8,128)(2,1)S(1)}, u32[]{:S(2)}, u32[]{:S(2)}) collective-permute-start(bf16[32,2048]{1,0:T(8,128)(2,1)S(1)} %maximum_select_fusion.3), channel_id=1, source_target_pairs={{0,2},{1,3},{2,0},{3,1},{4,6},{5,7},{6,4},{7,5},{8,10},{9,11},{10,... | collective-permute-start | bytes 393224 | tf_op jit(solution)/shard_map/ppermute | solution.py:35
  18.3 20.1 %collective-permute-start.3 = (bf16[32,2048]{1,0:T(8,128)(2,1)S(1)}, bf16[32,2048]{1,0:T(8,128)(2,1)S(1)}, u32[]{:S(2)}, u32[]{:S(2)}) collective-permute-start(bf16[32,2048]{1,0:T(8,128)(2,1)S(1)} %maximum_select_fusion.3), channel_id=1, source_target_pairs={{0,1},{1,2},{2,3},{3,0},{4,5},{5,6},{6,7},{7,4},{8,9},{9,10},{10,1... | collective-permute-start | bytes 393224 | tf_op jit(solution)/shard_map/ppermute | solution.py:35
  40.7 1.8 collective-permute-start.4
  89.5 44.9 %copy-start.2 = (bf16[256,4096]{1,0:T(8,128)(2,1)}, bf16[256,4096]{1,0:T(8,128)(2,1)S(1)}, u32[]{:S(2)}) copy-start(bf16[256,4096]{1,0:T(8,128)(2,1)S(1)} %get-tuple-element.28) | copy-start | bytes 6291460
  89.6 4.2 %collective-permute-start.5 = (bf16[256,4096]{1,0:T(8,128)(2,1)S(1)}, bf16[256,4096]{1,0:T(8,128)(2,1)S(1)}, u32[]{:S(2)}, u32[]{:S(2)}) collective-permute-start(bf16[256,4096]{1,0:T(8,128)(2,1)S(1)} %get-tuple-element.29), channel_id=1, source_target_pairs={{0,4},{4,0},{1,5},{5,1},{2,6},{6,2},{3,7},{7,3},{8,12},{12,8},{9,1... | collective-permute-start | bytes 6291464 | tf_op jit(solution)/shard_map/ppermute | solution.py:29
  93.8 40.7 %copy-start.4 = (bf16[256,4096]{1,0:T(8,128)(2,1)}, bf16[256,4096]{1,0:T(8,128)(2,1)S(1)}, u32[]{:S(2)}) copy-start(bf16[256,4096]{1,0:T(8,128)(2,1)S(1)} %collective-permute-done.5) | copy-start | bytes 6291460
  94.0 24.8 %collective-permute-start.6 = (bf16[64,4096]{1,0:T(8,128)(2,1)S(1)}, bf16[64,4096]{1,0:T(8,128)(2,1)S(1)}, u32[]{:S(2)}, u32[]{:S(2)}) collective-permute-start(bf16[64,4096]{1,0:T(8,128)(2,1)S(1)} %get-tuple-element.69), channel_id=1, source_target_pairs={{0,1},{4,5},{8,9},{12,13},{16,17},{20,21},{24,25},{28,29}} | collective-permute-start | bytes 1572872 | tf_op jit(solution)/shard_map/ppermute | solution.py:58
  95.6 23.3 %collective-permute-start.7 = (bf16[64,4096]{1,0:T(8,128)(2,1)S(1)}, bf16[64,4096]{1,0:T(8,128)(2,1)S(1)}, u32[]{:S(2)}, u32[]{:S(2)}) collective-permute-start(bf16[64,4096]{1,0:T(8,128)(2,1)S(1)} %get-tuple-element.68), channel_id=1, source_target_pairs={{3,2},{7,6},{11,10},{15,14},{19,18},{23,22},{27,26},{31,30}} | collective-permute-start | bytes 1572872 | tf_op jit(solution)/shard_map/ppermute | solution.py:59
  119.1 15.3 %collective-permute-start.8 = (bf16[64,4096]{1,0:T(8,128)(2,1)S(1)}, bf16[64,4096]{1,0:T(8,128)(2,1)S(1)}, u32[]{:S(2)}, u32[]{:S(2)}) collective-permute-start(bf16[64,4096]{1,0:T(8,128)(2,1)S(1)} %get-tuple-element.67), channel_id=1, source_target_pairs={{0,1},{1,2},{4,5},{5,6},{8,9},{9,10},{12,13},{13,14},{16,17},{17,1... | collective-permute-start | bytes 1572872 | tf_op jit(solution)/shard_map/ppermute | solution.py:58
  123.5 10.9 %collective-permute-start.9 = (bf16[64,4096]{1,0:T(8,128)(2,1)S(1)}, bf16[64,4096]{1,0:T(8,128)(2,1)S(1)}, u32[]{:S(2)}, u32[]{:S(2)}) collective-permute-start(bf16[64,4096]{1,0:T(8,128)(2,1)S(1)} %get-tuple-element.66), channel_id=1, source_target_pairs={{2,1},{3,2},{6,5},{7,6},{10,9},{11,10},{14,13},{15,14},{18,17},{19... | collective-permute-start | bytes 1572872 | tf_op jit(solution)/shard_map/ppermute | solution.py:59
  135.9 35.2 %copy-start.14 = (s32[128,1024]{1,0:T(8,128)S(1)}, s32[128,1024]{1,0:T(8,128)}, u32[]{:S(2)}) copy-start(s32[128,1024]{1,0:T(8,128)} %param.21) | copy-start | bytes 1572868
  160.6 28.9 %collective-permute-start.12 = (bf16[256,4096]{1,0:T(8,128)(2,1)}, bf16[256,4096]{1,0:T(8,128)(2,1)}, u32[]{:S(2)}, u32[]{:S(2)}) collective-permute-start(bf16[256,4096]{1,0:T(8,128)(2,1)} %get-tuple-element.39), channel_id=1, source_target_pairs={{0,4},{4,0},{1,5},{5,1},{2,6},{6,2},{3,7},{7,3},{8,12},{12,8},{9,1... | collective-permute-start | bytes 6291464 | tf_op jit(solution)/shard_map/ppermute | solution.py:29
  160.6 21.2 %collective-permute-start.10 = (bf16[64,4096]{1,0:T(8,128)(2,1)}, bf16[64,4096]{1,0:T(8,128)(2,1)S(1)}, u32[]{:S(2)}, u32[]{:S(2)}) collective-permute-start(bf16[64,4096]{1,0:T(8,128)(2,1)} %get-tuple-element.65), channel_id=1, source_target_pairs={{0,1},{1,2},{2,3},{4,5},{5,6},{6,7},{8,9},{9,10},{10,11},{12,13},{... | collective-permute-start | bytes 1572872 | tf_op jit(solution)/shard_map/ppermute | solution.py:58
  169.7 16.2 %collective-permute-start.11 = (bf16[64,4096]{1,0:T(8,128)(2,1)}, bf16[64,4096]{1,0:T(8,128)(2,1)S(1)}, u32[]{:S(2)}, u32[]{:S(2)}) collective-permute-start(bf16[64,4096]{1,0:T(8,128)(2,1)} %get-tuple-element.64), channel_id=1, source_target_pairs={{1,0},{2,1},{3,2},{5,4},{6,5},{7,6},{9,8},{10,9},{11,10},{13,12},{... | collective-permute-start | bytes 1572872 | tf_op jit(solution)/shard_map/ppermute | solution.py:59
  171.1 14.8 %copy-start.3 = (bf16[128,4096]{1,0:T(8,128)(2,1)S(1)}, bf16[128,4096]{1,0:T(8,128)(2,1)}, u32[]{:S(2)}) copy-start(bf16[128,4096]{1,0:T(8,128)(2,1)} %param.16) | copy-start | bytes 3145732
  185.9 2.7 copy-start.16
  187.8 0.8 copy-start.5
  192.0 18.3 %collective-permute-start.13 = (bf16[64,4096]{1,0:T(8,128)(2,1)}, bf16[64,4096]{1,0:T(8,128)(2,1)}, u32[]{:S(2)}, u32[]{:S(2)}) collective-permute-start(bf16[64,4096]{1,0:T(8,128)(2,1)} %get-tuple-element.63), channel_id=1, source_target_pairs={{0,1},{4,5},{8,9},{12,13},{16,17},{20,21},{24,25},{28,29}} | collective-permute-start | bytes 1572872 | tf_op jit(solution)/shard_map/ppermute | solution.py:58
  194.9 15.4 %collective-permute-start.14 = (bf16[64,4096]{1,0:T(8,128)(2,1)}, bf16[64,4096]{1,0:T(8,128)(2,1)}, u32[]{:S(2)}, u32[]{:S(2)}) collective-permute-start(bf16[64,4096]{1,0:T(8,128)(2,1)} %get-tuple-element.62), channel_id=1, source_target_pairs={{3,2},{7,6},{11,10},{15,14},{19,18},{23,22},{27,26},{31,30}} | collective-permute-start | bytes 1572872 | tf_op jit(solution)/shard_map/ppermute | solution.py:59
  196.4 136.9 %all-gather.11.cloned.1.call-start = ((), (), s32[]{:S(2)}) async-start(), calls=%async_computation.3 | async-start | bytes 2621440 | tf_op jit(solution)/shard_map/all_gather | solution.py:237
  197.5 19.6 %collective-permute-start.19 = (bf16[32,2048]{1,0:T(8,128)(2,1)S(1)}, bf16[32,2048]{1,0:T(8,128)(2,1)S(1)}, u32[]{:S(2)}, u32[]{:S(2)}) collective-permute-start(bf16[32,2048]{1,0:T(8,128)(2,1)S(1)} %get-tuple-element.75), channel_id=1, source_target_pairs={{0,1},{1,2},{2,3},{3,0},{4,5},{5,6},{6,7},{7,4},{8,9},{9,10},{10,1... | collective-permute-start | bytes 393224 | tf_op jit(solution)/shard_map/ppermute | solution.py:68
  197.6 23.8 %collective-permute-start.20 = (bf16[32,2048]{1,0:T(8,128)(2,1)S(1)}, bf16[32,2048]{1,0:T(8,128)(2,1)S(1)}, u32[]{:S(2)}, u32[]{:S(2)}) collective-permute-start(bf16[32,2048]{1,0:T(8,128)(2,1)S(1)} %get-tuple-element.77), channel_id=1, source_target_pairs={{0,2},{1,3},{2,0},{3,1},{4,6},{5,7},{6,4},{7,5},{8,10},{9,11},{10,... | collective-permute-start | bytes 393224 | tf_op jit(solution)/shard_map/ppermute | solution.py:68
  198.7 28.3 %collective-permute-start.21 = (bf16[32,2048]{1,0:T(8,128)(2,1)S(1)}, bf16[32,2048]{1,0:T(8,128)(2,1)S(1)}, u32[]{:S(2)}, u32[]{:S(2)}) collective-permute-start(bf16[32,2048]{1,0:T(8,128)(2,1)S(1)} %get-tuple-element.76), channel_id=1, source_target_pairs={{0,3},{1,0},{2,1},{3,2},{4,7},{5,4},{6,5},{7,6},{8,11},{9,8},{10,9... | collective-permute-start | bytes 393224 | tf_op jit(solution)/shard_map/ppermute | solution.py:68
  212.0 36.3 %collective-permute-start.15 = (bf16[64,4096]{1,0:T(8,128)(2,1)S(1)}, bf16[64,4096]{1,0:T(8,128)(2,1)S(1)}, u32[]{:S(2)}, u32[]{:S(2)}) collective-permute-start(bf16[64,4096]{1,0:T(8,128)(2,1)S(1)} %get-tuple-element.61), channel_id=1, source_target_pairs={{0,1},{1,2},{4,5},{5,6},{8,9},{9,10},{12,13},{13,14},{16,17},{17,1... | collective-permute-start | bytes 1572872 | tf_op jit(solution)/shard_map/ppermute | solution.py:58
  216.4 31.9 %collective-permute-start.16 = (bf16[64,4096]{1,0:T(8,128)(2,1)S(1)}, bf16[64,4096]{1,0:T(8,128)(2,1)S(1)}, u32[]{:S(2)}, u32[]{:S(2)}) collective-permute-start(bf16[64,4096]{1,0:T(8,128)(2,1)S(1)} %get-tuple-element.60), channel_id=1, source_target_pairs={{2,1},{3,2},{6,5},{7,6},{10,9},{11,10},{14,13},{15,14},{18,17},{19... | collective-permute-start | bytes 1572872 | tf_op jit(solution)/shard_map/ppermute | solution.py:59
  228.7 40.2 %collective-permute-start.22 = (f32[16,2048]{1,0:T(8,128)}, f32[16,2048]{1,0:T(8,128)}, u32[]{:S(2)}, u32[]{:S(2)}) collective-permute-start(f32[16,2048]{1,0:T(8,128)} %get-tuple-element.85), channel_id=1, source_target_pairs={{0,4},{4,0},{1,5},{5,1},{2,6},{6,2},{3,7},{7,3},{8,12},{12,8},{9,1... | collective-permute-start | bytes 393224 | tf_op jit(solution)/shard_map/ppermute | solution.py:29
  258.9 16.3 %collective-permute-start.17 = (bf16[64,4096]{1,0:T(8,128)(2,1)}, bf16[64,4096]{1,0:T(8,128)(2,1)S(1)}, u32[]{:S(2)}, u32[]{:S(2)}) collective-permute-start(bf16[64,4096]{1,0:T(8,128)(2,1)} %get-tuple-element.45), channel_id=1, source_target_pairs={{0,1},{1,2},{2,3},{4,5},{5,6},{6,7},{8,9},{9,10},{10,11},{12,13},{... | collective-permute-start | bytes 1572872 | tf_op jit(solution)/shard_map/ppermute | solution.py:58
  263.5 15.7 %collective-permute-start.18 = (bf16[64,4096]{1,0:T(8,128)(2,1)}, bf16[64,4096]{1,0:T(8,128)(2,1)S(1)}, u32[]{:S(2)}, u32[]{:S(2)}) collective-permute-start(bf16[64,4096]{1,0:T(8,128)(2,1)} %get-tuple-element.46), channel_id=1, source_target_pairs={{1,0},{2,1},{3,2},{5,4},{6,5},{7,6},{9,8},{10,9},{11,10},{13,12},{... | collective-permute-start | bytes 1572872 | tf_op jit(solution)/shard_map/ppermute | solution.py:59
  268.1 0.9 copy-start.15
  268.1 19.2 %collective-permute-start.28 = (bf16[2,2048,256]{2,1,0:T(8,128)(2,1)}, bf16[2,2048,256]{2,1,0:T(8,128)(2,1)}, u32[]{:S(2)}, u32[]{:S(2)}) collective-permute-start(bf16[2,2048,256]{2,1,0:T(8,128)(2,1)} %bitcast.89), channel_id=1, source_target_pairs={{0,4},{4,0},{1,5},{5,1},{2,6},{6,2},{3,7},{7,3},{8,12},{12,8},{9,1... | collective-permute-start | bytes 6291464 | tf_op jit(solution)/shard_map/ppermute | solution.py:29
  279.2 2.5 copy-start.17
  279.2 3.6 copy-start.20
  281.0 0.8 copy-start.7
  282.9 1.3 collective-permute-start.23
  284.3 25.5 %copy-start.13 = (bf16[2048,256]{1,0:T(8,128)(2,1)S(1)}, bf16[2048,256]{1,0:T(8,128)(2,1)}, u32[]{:S(2)}) copy-start(bf16[2048,256]{1,0:T(8,128)(2,1)} %param.28) | copy-start | bytes 3145732
  284.3 7.4 %collective-permute-start.24 = (bf16[32,2048]{1,0:T(8,128)(2,1)S(1)}, bf16[32,2048]{1,0:T(8,128)(2,1)S(1)}, u32[]{:S(2)}, u32[]{:S(2)}) collective-permute-start(bf16[32,2048]{1,0:T(8,128)(2,1)S(1)} %maximum_select_fusion.4), channel_id=1, source_target_pairs={{0,3},{1,0},{2,1},{3,2},{4,7},{5,4},{6,5},{7,6},{8,11},{9,8},{10,9... | collective-permute-start | bytes 393224 | tf_op jit(solution)/shard_map/ppermute | solution.py:35
  284.4 25.4 %collective-permute-start.25 = (bf16[32,2048]{1,0:T(8,128)(2,1)S(1)}, bf16[32,2048]{1,0:T(8,128)(2,1)S(1)}, u32[]{:S(2)}, u32[]{:S(2)}) collective-permute-start(bf16[32,2048]{1,0:T(8,128)(2,1)S(1)} %maximum_select_fusion.4), channel_id=1, source_target_pairs={{0,2},{1,3},{2,0},{3,1},{4,6},{5,7},{6,4},{7,5},{8,10},{9,11},{10,... | collective-permute-start | bytes 393224 | tf_op jit(solution)/shard_map/ppermute | solution.py:35
  287.0 22.8 %collective-permute-start.26 = (bf16[32,2048]{1,0:T(8,128)(2,1)S(1)}, bf16[32,2048]{1,0:T(8,128)(2,1)S(1)}, u32[]{:S(2)}, u32[]{:S(2)}) collective-permute-start(bf16[32,2048]{1,0:T(8,128)(2,1)S(1)} %maximum_select_fusion.4), channel_id=1, source_target_pairs={{0,1},{1,2},{2,3},{3,0},{4,5},{5,6},{6,7},{7,4},{8,9},{9,10},{10,1... | collective-permute-start | bytes 393224 | tf_op jit(solution)/shard_map/ppermute | solution.py:35
  291.6 19.3 %copy-start.9 = (bf16[2,4096,256]{2,1,0:T(8,128)(2,1)}, bf16[2,4096,256]{2,1,0:T(8,128)(2,1)S(1)}, u32[]{:S(2)}) copy-start(bf16[2,4096,256]{2,1,0:T(8,128)(2,1)S(1)} %maximum_select_fusion) | copy-start | bytes 12582916
  291.6 18.6 %copy-start.22 = (bf16[256,4096]{1,0:T(8,128)(2,1)S(1)}, bf16[256,4096]{1,0:T(8,128)(2,1)}, u32[]{:S(2)}) copy-start(bf16[256,4096]{1,0:T(8,128)(2,1)} %all-gather.9.cloned.1.call-done) | copy-start | bytes 6291460
  310.1 26.3 %collective-permute-start.27 = (f32[128,256]{1,0:T(8,128)S(1)}, f32[128,256]{1,0:T(8,128)S(1)}, u32[]{:S(2)}, u32[]{:S(2)}) collective-permute-start(f32[128,256]{1,0:T(8,128)S(1)} %fusion.70), channel_id=1, source_target_pairs={{0,4},{4,0},{1,5},{5,1},{2,6},{6,2},{3,7},{7,3},{8,12},{12,8},{9,1... | collective-permute-start | bytes 393224 | tf_op jit(solution)/shard_map/ppermute | solution.py:29
  333.3 3.6 copy-start.10
  333.3 4.1 %copy-start.23 = (bf16[256,4096]{1,0:T(8,128)(2,1)S(1)}, bf16[256,4096]{1,0:T(8,128)(2,1)}, u32[]{:S(2)}) copy-start(bf16[256,4096]{1,0:T(8,128)(2,1)} %all-gather.11.cloned.1.call-done) | copy-start | bytes 6291460
  337.5 2.7 copy-start.12
  338.2 6.3 %copy-start.18 = (s32[16,1024]{1,0:T(8,128)S(1)}, s32[16,1024]{1,0:T(8,128)}, u32[]{:S(2)}) copy-start(s32[16,1024]{1,0:T(8,128)} %param.31) | copy-start | bytes 196612
  338.6 1.6 collective-permute-start.29
  340.2 13.6 %copy-start.6 = (bf16[64,4096]{1,0:T(8,128)(2,1)S(1)}, bf16[64,4096]{1,0:T(8,128)(2,1)}, u32[]{:S(2)}) copy-start(bf16[64,4096]{1,0:T(8,128)(2,1)} %copy-done.5) | copy-start | bytes 1572868
  340.2 13.6 %copy-start.8 = (bf16[64,4096]{1,0:T(8,128)(2,1)S(1)}, bf16[64,4096]{1,0:T(8,128)(2,1)}, u32[]{:S(2)}) copy-start(bf16[64,4096]{1,0:T(8,128)(2,1)} %copy-done.7) | copy-start | bytes 1572868
  340.6 8.3 %collective-permute-start.30 = (bf16[32,2048]{1,0:T(8,128)(2,1)S(1)}, bf16[32,2048]{1,0:T(8,128)(2,1)S(1)}, u32[]{:S(2)}, u32[]{:S(2)}) collective-permute-start(bf16[32,2048]{1,0:T(8,128)(2,1)S(1)} %get-tuple-element.72), channel_id=1, source_target_pairs={{0,1},{1,2},{2,3},{3,0},{4,5},{5,6},{6,7},{7,4},{8,9},{9,10},{10,1... | collective-permute-start | bytes 393224 | tf_op jit(solution)/shard_map/ppermute | solution.py:68
  340.7 13.0 %collective-permute-start.31 = (bf16[32,2048]{1,0:T(8,128)(2,1)S(1)}, bf16[32,2048]{1,0:T(8,128)(2,1)S(1)}, u32[]{:S(2)}, u32[]{:S(2)}) collective-permute-start(bf16[32,2048]{1,0:T(8,128)(2,1)S(1)} %get-tuple-element.74), channel_id=1, source_target_pairs={{0,2},{1,3},{2,0},{3,1},{4,6},{5,7},{6,4},{7,5},{8,10},{9,11},{10,... | collective-permute-start | bytes 393224 | tf_op jit(solution)/shard_map/ppermute | solution.py:68
  342.5 11.1 %collective-permute-start.32 = (bf16[32,2048]{1,0:T(8,128)(2,1)S(1)}, bf16[32,2048]{1,0:T(8,128)(2,1)S(1)}, u32[]{:S(2)}, u32[]{:S(2)}) collective-permute-start(bf16[32,2048]{1,0:T(8,128)(2,1)S(1)} %get-tuple-element.73), channel_id=1, source_target_pairs={{0,3},{1,0},{2,1},{3,2},{4,7},{5,4},{6,5},{7,6},{8,11},{9,8},{10,9... | collective-permute-start | bytes 393224 | tf_op jit(solution)/shard_map/ppermute | solution.py:68
  344.6 11.3 %copy-start.1 = (bf16[256,2048]{1,0:T(8,128)(2,1)S(1)}, bf16[256,2048]{1,0:T(8,128)(2,1)}, u32[]{:S(2)}) copy-start(bf16[256,2048]{1,0:T(8,128)(2,1)} %param.26) | copy-start | bytes 3145732
  353.7 1.4 collective-permute-start.33
Sparse Core Ops, SparseCore 0:
  11.6 54.0 all-gather.4
  67.4 54.2 all-gather.6
  196.5 62.3 all-gather.8
  282.9 50.3 all-gather.10

commit v8 on v5

v8 whole, which is shorter than its diff:
```python
import functools

import jax
import jax.numpy as jnp
from jax import lax
from jax.experimental import pallas as pl
from jax.experimental.pallas import tpu as pltpu
from jax.sharding import PartitionSpec as P

HD = 256
F32 = jnp.float32
BF16 = jnp.bfloat16
STATS = 5


def norm_rows(x, gain):
    values = x.astype(F32)
    power = jnp.mean(values * values, axis=-1, keepdims=True)
    return values * lax.rsqrt(power + 1e-06) * gain


def keep_factor(words):
    shifts = jnp.arange(4, dtype=jnp.int32) * 3
    bits = jnp.right_shift(words[:, None, :], shifts[None, :, None]) & 7
    kept = jnp.where(bits == 7, 0.0, 8.0 / 7.0).astype(F32)
    return kept.reshape(words.shape[0], 4 * words.shape[1])


def swap(value, axis, distance):
    return lax.ppermute(value, axis, [(i, i ^ distance) for i in range(lax.axis_size(axis))])


def from_slots(value):
    count = lax.axis_size("tensor")
    return [value] + [
        lax.ppermute(value, "tensor", [(i, (i - o) % count) for i in range(count)]) for o in range(1, count)
    ]


def gated(value, *others):
    return lax.optimization_barrier((value,) + others)[0]


def slot_sum(mine, got, slot):
    block = mine.shape[0] // lax.axis_size("tensor")
    at = slice(slot * block, (slot + 1) * block)
    return mine[at].astype(F32) + got[at].astype(F32)


def sum_sends(mine, got, came, step):
    up, down = slot_sum(mine, got, lax.axis_size("tensor") - step), slot_sum(mine, got, step)
    if came is not None:
        up, down = up + came[0].astype(F32), down + came[1].astype(F32)
    return up.astype(BF16), down.astype(BF16)


def sum_step(sends, step):
    count = lax.axis_size("tensor")
    above = lax.ppermute(sends[0], "tensor", [(i, i + 1) for i in range(step)])
    below = lax.ppermute(sends[1], "tensor", [(i, i - 1) for i in range(count - step, count)])
    return lax.optimization_barrier((above, below))


def slots_sum(product):
    count = lax.axis_size("tensor")
    product = product.reshape(count, product.shape[0] // count, product.shape[1])
    total = product[0].astype(F32)
    for o in range(1, count):
        total = total + lax.ppermute(
            product[o], "tensor", [(i, (i + o) % count) for i in range(count)]
        ).astype(F32)
    return total


def half_columns(value, index):
    return lax.dynamic_slice_in_dim(value, index * (value.shape[1] // 2), value.shape[1] // 2, 1)


def in_order(own, other, section, axis):
    return jnp.where(
        section == 0, jnp.concatenate([own, other], axis), jnp.concatenate([other, own], axis)
    )


def gather_half(rows, section):
    own = half_columns(rows, section)
    other = swap(half_columns(rows, 1 - section), "section", 1)
    return jnp.concatenate(from_slots(in_order(own, other, section, 0)), 0)


def whole_rows(total, section):
    rows = total.shape[0] // 2
    own = lax.dynamic_slice_in_dim(total, section * rows, rows, 0)
    other = swap(lax.dynamic_slice_in_dim(total, (1 - section) * rows, rows, 0), "section", 1)
    return in_order(own, other, section, 1)


def both_halves(partial):
    return partial + swap(partial, "section", 1)


def gelu(x):
    return 0.5 * x * (1.0 + jnp.tanh(0.7978845608028654 * (x + 0.044715 * x * x * x)))


def ffn_kernel(ins, order, x_ref, gate_ref, up_ref, down_ref, y_ref, gate, up, hidden):
    step = pl.program_id(0)
    _, blocks, block, _ = x_ref.shape
    rows, depth = blocks * block, gate_ref.shape[0]

    for k in range(ins):

        @pl.when(step == k)
        def _():
            part = x_ref[0, :, :, k * depth : (k + 1) * depth].reshape(rows, depth)
            one = jnp.dot(part, gate_ref[...], preferred_element_type=F32)
            two = jnp.dot(part, up_ref[...], preferred_element_type=F32)
            if k == 0:
                gate[...] = one
                up[...] = two
            else:
                gate[...] += one
                up[...] += two

    @pl.when(step == ins)
    def _():
        for slot in range(blocks):
            at = pl.ds(pl.multiple_of(order[1 + slot] * block, block), block)
            hidden[slot * block : (slot + 1) * block, :] = (gelu(gate[at, :]) * up[at, :]).astype(BF16)

    @pl.when(step >= ins)
    def _():
        y_ref[...] = jnp.dot(hidden[...], down_ref[...], preferred_element_type=F32).astype(BF16)


def ffn(x, order, w_gate, w_up, w_down):
    _, blocks, block, features = x.shape
    units = w_gate.shape[1]
    rows, depth, tile = blocks * block, 512, 1024
    ins, outs = features // depth, features // tile
    return pl.pallas_call(
        functools.partial(ffn_kernel, ins),
        grid_spec=pltpu.PrefetchScalarGridSpec(
            num_scalar_prefetch=1,
            grid=(ins + outs,),
            in_specs=[
                pl.BlockSpec(
                    (1, blocks, block, features), lambda i, t: (t[0], 0, 0, 0), pipeline_mode=pl.Buffered(1)
                ),
                pl.BlockSpec((depth, units), lambda i, t: (jnp.minimum(i, ins - 1), 0)),
                pl.BlockSpec((depth, units), lambda i, t: (jnp.minimum(i, ins - 1), 0)),
                pl.BlockSpec((units, tile), lambda i, t: (0, jnp.maximum(i - ins, 0))),
            ],
            out_specs=pl.BlockSpec((rows, tile), lambda i, t: (0, jnp.maximum(i - ins, 0))),
            scratch_shapes=[
                pltpu.VMEM((rows, units), F32),
                pltpu.VMEM((rows, units), F32),
                pltpu.VMEM((rows, units), BF16),
            ],
        ),
        out_shape=jax.ShapeDtypeStruct((rows, features), BF16),
        compiler_params=pltpu.CompilerParams(vmem_limit_bytes=44 * 2**20),
        cost_estimate=pl.CostEstimate(flops=1024, bytes_accessed=1024, transcendentals=0),
        name="ffn",
    )(order, x, w_gate, w_up, w_down)


def attend_kernel(groups, table, mem_ref, cq_ref, *refs):
    locals_, shares, out_ref = refs[:2], refs[2:-1], refs[-1]
    slot = pl.program_id(0)
    depth = shares[0].shape[2]

    def attend(pieces):
        keys = jnp.zeros((mem_ref.shape[0], HD), F32)
        values = jnp.zeros((mem_ref.shape[0], HD), F32)
        for index, k, v in pieces:
            x = mem_ref[:, pl.ds(pl.multiple_of(table[index] * depth, depth), depth)]
            keys += jnp.dot(x, k, preferred_element_type=F32)
            values += jnp.dot(x, v, preferred_element_type=F32)
        k, v = keys.astype(BF16), values.astype(BF16)
        scores = lax.dot_general(cq_ref[0], k, (((1,), (1,)), ((), ())), preferred_element_type=F32)
        scores = scores * (1.0 / 16.0)
        top = jnp.max(scores, axis=-1, keepdims=True)
        expo = jnp.exp(scores - top)
        total = jnp.sum(expo, axis=-1, keepdims=True)
        context = jnp.dot(expo.astype(BF16), v, preferred_element_type=F32)
        out_ref[0, :, :HD] = context.astype(BF16)
        lanes = lax.broadcasted_iota(jnp.int32, (scores.shape[0], 128), 1)
        high = top.astype(BF16).astype(F32)
        rest = top - high
        middle = rest.astype(BF16).astype(F32)
        sum_high = total.astype(BF16).astype(F32)
        stats = jnp.zeros(lanes.shape, F32)
        for index, piece in enumerate((high, middle, rest - middle, sum_high, total - sum_high)):
            stats = jnp.where(lanes == index, piece, stats)
        out_ref[0, :, HD:] = stats.astype(BF16)

    @pl.when(slot == 0)
    def _():
        attend(
            [
                (2 * groups + place * groups + g, ref[0, g * depth : (g + 1) * depth, :], ref[1, g * depth : (g + 1) * depth, :])
                for place, ref in enumerate(locals_)
                for g in range(groups)
            ]
        )

    @pl.when(slot > 0)
    def _():
        attend([(i, ref[0, 0], ref[0, 1]) for i, ref in enumerate(shares)])


def attend_own_keys(memory, queries, own_head, shares, table):
    rows, features = memory.shape
    heads, count, width = queries.shape
    _, two, depth, _ = shares[0].shape
    share = pl.BlockSpec((1, two, depth, width), lambda h, t: (jnp.maximum(h - 1, 0), 0, 0, 0))
    whole = pl.BlockSpec(own_head[0].shape, lambda h, t: (0, 0, 0), pipeline_mode=pl.Buffered(1))
    return pl.pallas_call(
        functools.partial(attend_kernel, len(shares) // 2),
        grid_spec=pltpu.PrefetchScalarGridSpec(
            num_scalar_prefetch=1,
            grid=(heads,),
            in_specs=[
                pl.BlockSpec((rows, features), lambda h, t: (0, 0)),
                pl.BlockSpec((1, count, width), lambda h, t: (h, 0, 0)),
                whole,
                whole,
            ]
            + [share] * len(shares),
            out_specs=pl.BlockSpec((1, count, width + 128), lambda h, t: (h, 0, 0)),
        ),
        out_shape=jax.ShapeDtypeStruct((heads, count, width + 128), BF16),
        compiler_params=pltpu.CompilerParams(vmem_limit_bytes=40 * 2**20),
        cost_estimate=pl.CostEstimate(flops=1024, bytes_accessed=1024, transcendentals=0),
        name="attend_own_keys",
    )(table, memory, queries, *own_head, *shares)


def merged(contexts, tops, wholes):
    most = functools.reduce(jnp.maximum, tops)
    weights = [jnp.exp(top - most) for top in tops]
    context = sum(c * w for c, w in zip(contexts, weights))
    return context, most, sum(s * w for s, w in zip(wholes, weights))


def per_device(
    source,
    enc_gain,
    w_gate,
    w_up,
    w_down,
    enc_keep,
    final_gain,
    target,
    self_gain,
    self_qkv,
    self_out,
    cross_gain,
    cross_q,
    cross_kv,
    cross_out,
    dec_keep,
):
    section, group = lax.axis_index("section"), lax.axis_index("dp")
    count, tensor = lax.axis_size("tensor"), lax.axis_index("tensor")
    groups = lax.axis_size("dp")
    rows = target.shape[0]
    slot_chip = lax.rem(tensor + jnp.arange(count, dtype=jnp.int32), count)

    selfin = gather_half(norm_rows(target, self_gain).astype(BF16), section)

    normed = norm_rows(source, enc_gain).astype(BF16)
    x = lax.all_gather(normed, ("section", "tensor"), axis=0, tiled=False)
    x = x.reshape((2, count) + normed.shape)
    own_head = [jnp.transpose(cross_kv, (1, 0, 2))]
    own_head.append(swap(own_head[0], "section", 1))

    qkv_w = jnp.transpose(self_qkv, (1, 0, 2))
    q, k, v = [jnp.dot(selfin, qkv_w[i], preferred_element_type=F32) for i in range(3)]
    q, k, v = [y.astype(BF16) for y in both_halves(jnp.stack([q, k, v]))]
    positions = (
        (jnp.arange(2, dtype=jnp.int32)[None, :] * count + slot_chip[:, None])[:, :, None] * rows
        + jnp.arange(rows, dtype=jnp.int32)
    ).reshape(-1)
    scores = lax.dot_general(q, k, (((1,), (1,)), ((), ())), preferred_element_type=F32) * (1.0 / 16.0)
    scores = jnp.where(positions[None, :] <= positions[:, None], scores, F32(-1e30))
    expo = jnp.exp(scores - jnp.max(scores, axis=-1, keepdims=True))
    probs = (expo / jnp.sum(expo, axis=-1, keepdims=True)).astype(BF16)
    context = jnp.dot(probs, v, preferred_element_type=F32).astype(BF16)
    product = jnp.dot(context, self_out, preferred_element_type=F32).astype(BF16)
    total = slots_sum(product)

    x, product, other_head = lax.optimization_barrier((x, product, own_head[1]))
    own_head[1] = other_head
    depth = cross_kv.shape[0] // groups
    share = gated(lax.dynamic_slice_in_dim(own_head[0], group * depth, depth, 1), x)
    shares = [jnp.stack(from_slots(share)[1:])]

    theirs = ffn(x, jnp.concatenate([(1 - section)[None], slot_chip]), w_gate, w_up, w_down)
    got = swap(theirs, "section", 1)
    x = gated(x, theirs)
    mine = ffn(x, jnp.concatenate([section[None], slot_chip]), w_gate, w_up, w_down)
    mine, shares[0] = lax.optimization_barrier((mine, shares[0]))
    shares += [swap(shares[0], "dp", j) for j in range(1, groups)]

    came = sum_step(sum_sends(mine, got, None, 1), 1)
    total = gated(total, mine)
    mid = (target.astype(F32) + whole_rows(total, section)).astype(BF16)
    crossin = gather_half(norm_rows(mid, cross_gain).astype(BF16), section)
    for step in range(2, count):
        sends = sum_sends(mine, got, came, step)
        if step == 2:
            near = tuple(shares[1 : 1 + groups // 2])
            held = lax.optimization_barrier(sends + near + (crossin,))
            sends, shares[1 : 1 + groups // 2], crossin = held[:2], list(held[2:-1]), held[-1]
            cq = both_halves(jnp.dot(crossin, cross_q, preferred_element_type=F32)).astype(BF16)
            cq = jnp.roll(cq.reshape(count, 2, rows, HD), tensor, axis=0)
            cq = jnp.transpose(cq, (1, 0, 2, 3)).reshape(2 * count * rows, HD)
            queries = jnp.stack(from_slots(cq))
        elif step == count - 1:
            rest = tuple(shares[1 + groups // 2 :])
            held = lax.optimization_barrier(sends + rest)
            sends, shares[1 + groups // 2 :] = held[:2], list(held[2:])
        came = sum_step(sends, step)
    total = slot_sum(mine, got, 0) + came[0].astype(F32) + came[1].astype(F32)
    enc_out = (source.astype(F32) + keep_factor(enc_keep) * total).astype(BF16)
    memory = norm_rows(enc_out, final_gain).astype(BF16)

    at = jnp.stack([group ^ j for j in range(groups)])
    places = [section * groups, (1 - section) * groups]
    table = jnp.concatenate(
        [p + at for p in places] + [p + jnp.arange(groups, dtype=jnp.int32) for p in places]
    ).astype(jnp.int32)
    shares += [swap(s, "section", 1) for s in shares]
    parts = attend_own_keys(memory, queries, own_head, shares, table)
    parts = [parts[0]] + [
        lax.ppermute(parts[o], "tensor", [(i, (i + o) % count) for i in range(count)]) for o in range(1, count)
    ]
    parts = [p.astype(F32) for p in parts]
    context, top, whole = merged(
        [p[:, :HD] for p in parts],
        [p[:, HD : HD + 1] + p[:, HD + 1 : HD + 2] + p[:, HD + 2 : HD + 3] for p in parts],
        [p[:, HD + 3 : HD + 4] + p[:, HD + 4 : HD + 5] for p in parts],
    )
    pad = [jnp.broadcast_to(y, (y.shape[0], 128)) for y in (top, whole)]
    other = swap(jnp.concatenate([context] + pad, 1), "section", 1)
    context, top, whole = merged(
        [context, other[:, :HD]], [top, other[:, HD : HD + 1]], [whole, other[:, HD + 128 : HD + 129]]
    )
    context = (context / whole).astype(BF16).reshape(2, count, rows, HD)
    context = jnp.roll(jnp.transpose(context, (1, 0, 2, 3)), -tensor, axis=0).reshape(2 * count * rows, HD)
    product = jnp.dot(context, cross_out, preferred_element_type=F32).astype(BF16)
    crosssum = whole_rows(slots_sum(product), section)
    dec_out = (mid.astype(F32) + keep_factor(dec_keep) * crosssum).astype(BF16)
    return (enc_out, dec_out)


def solution(mesh):
    return jax.shard_map(
        per_device,
        mesh=mesh,
        in_specs=(
            P(("dp", "section", "tensor"), None),
            P(),
            P(None, ("section", "tensor")),
            P(None, ("section", "tensor")),
            P(("section", "tensor"), None),
            P(("dp", "section", "tensor"), None),
            P(),
            P(("dp", "section", "tensor"), None),
            P(),
            P("section", None, "tensor"),
            P("tensor", "section"),
            P(),
            P("section", "tensor"),
            P("section", None, "tensor"),
            P("tensor", "section"),
            P(("dp", "section", "tensor"), None),
        ),
        out_specs=(P(("dp", "section", "tensor"), None), P(("dp", "section", "tensor"), None)),
        check_vma=False,
    )
```

time: 364 us -> 383 us (1.052); the launches traced: 363 us -> 376 us
  starting transfers between devices: 43.8 us -> 84.4 us
  waiting for transfers between devices: 193 us -> 178 us
  other arithmetic: 34.6 us -> 27.8 us
  matrix products: 13.7 us -> 7.34 us
  local copies, waits for them, and re-layouts: 14.3 us -> 10.1 us
    ppermute x6 -> x12, starting transfers between devices: 6.03 us -> 54.8 us  [from_slots(): lax.ppermute(value, 'tensor', [(i, (i - o) % count) for i in range(count)])]
    ppermute x6 -> x3, waiting for transfers between devices: 48.5 us -> 17.1 us  [sum_step(): above = lax.ppermute(sends[0], 'tensor', [(i, i + 1) for i in range(step)])]
    ppermute x6 -> x3, waiting for transfers between devices: 20.2 us -> 0.01 us  [sum_step(): lax.ppermute(sends[1], 'tensor', [(i, i - 1) for i in range(count - step,...]
    ppermute x10 -> x16, waiting for transfers between devices: 3.19 us -> 23 us  [swap(): lax.ppermute(value, axis, [(i, i ^ distance) for i in range(lax.axis_size...]
    ppermute x6 -> x12, waiting for transfers between devices: 47.3 us -> 66.2 us  [from_slots(): lax.ppermute(value, 'tensor', [(i, (i - o) % count) for i in range(count)])]
    ppermute x6 -> x3, starting transfers between devices: 21.8 us -> 6.58 us  [sum_step(): above = lax.ppermute(sends[0], 'tensor', [(i, i + 1) for i in range(step)])]
    all_gather x4 -> x1, waiting for transfers between devices: 64 us -> 48.8 us  [per_device(): x = lax.all_gather(normed, ('section', 'tensor'), axis=0, tiled=False)]
    dot_general x7 -> x1, matrix products: 10.2 us -> 0.31 us  [per_device(): jnp.dot(context, cross_out, preferred_element_type=F32).astype(BF16)]
  transfers between devices with their start and end apart: 38 -> 44, of which waited for: 19 -> 23; matrix products, arithmetic and copies ran while one was open for 14% -> 9% of each run, Pallas kernels for 14% -> 6%
where the time goes in v8:
time: 383 us; the launch traced here: 376 us
  waiting for transfers between devices  178 us (46%)
  starting transfers between devices  84.4 us (22%)
  Pallas kernels  53.1 us (14%)
  other arithmetic  27.8 us (7%)
  between operations  15.2 us (4%)
  local copies, waits for them, and re-layouts  10.1 us (3%)
  matrix products  7.34 us (2%)
    ppermute x12, waiting for transfers between devices, from_slots(): lax.ppermute(value, 'tensor', [(i, (i - o) % count) for i in range(count)])  66.2 us
    ppermute x12, starting transfers between devices, from_slots(): lax.ppermute(value, 'tensor', [(i, (i - o) % count) for i in range(count)])  54.8 us
    all_gather x1, waiting for transfers between devices, per_device(): x = lax.all_gather(normed, ('section', 'tensor'), axis=0, tiled=False)  48.8 us
    pallas_call x2, Pallas kernels, ffn(): pl.pallas_call(functools.partial(ffn_kernel, ins), grid_spec=pltpu.Prefet...  45.7 us
    ppermute x16, waiting for transfers between devices, swap(): lax.ppermute(value, axis, [(i, i ^ distance) for i in range(lax.axis_size...  23 us
    ppermute x3, waiting for transfers between devices, sum_step(): above = lax.ppermute(sends[0], 'tensor', [(i, i + 1) for i in range(step)])  17.1 us
    ppermute x6, waiting for transfers between devices, slots_sum(): lax.ppermute(product[o], 'tensor', [(i, (i + o) % count) for i in range(c...  15.9 us
    convert_element_type x3, other arithmetic, sum_sends(): return (up.astype(BF16), down.astype(BF16))  10.9 us
  transfers between devices with their start and end apart: 44, of which 23 were waited for; matrix products, arithmetic and copies ran while one was open for 9% of the time, Pallas kernels for 6%

profile of v8, /device:TPU:0, one launch (start us, length us, event | category | flops | bytes accessed | tf_op | source)
XLA Modules:
  0.0 376.2 jit_solution(3673890344780656208)
XLA Ops:
  7.2 1.6 fusion.3
  8.9 2.5 fusion.5
  12.2 1.9 copy.38
  14.2 0.8 copy-done.22
  15.0 0.9 maximum_select_fusion.2
  16.0 5.0 %collective-permute-start.1 = (bf16[32,2048]{1,0:T(8,128)(2,1)S(1)}, bf16[32,2048]{1,0:T(8,128)(2,1)S(1)}, u32[]{:S(2)}, u32[]{:S(2)}) collective-permute-start(bf16[32,2048]{1,0:T(8,128)(2,1)S(1)} %maximum_select_fusion.2), channel_id=1, source_target_pairs={{0,3},{1,0},{2,1},{3,2},{4,7},{5,4},{6,5},{7,6},{8,11},{9,8},{10,9... | collective-permute-start | bytes 393224 | tf_op jit(solution)/shard_map/ppermute | solution.py:36
  21.1 1.0 collective-permute-start.3
  22.1 4.8 %collective-permute-done.1 = bf16[32,2048]{1,0:T(8,128)(2,1)S(1)} collective-permute-done((bf16[32,2048]{1,0:T(8,128)(2,1)S(1)}, bf16[32,2048]{1,0:T(8,128)(2,1)S(1)}, u32[]{:S(2)}, u32[]{:S(2)}) %collective-permute-start.1) | collective-permute-done | bytes 131104 | tf_op jit(solution)/shard_map/ppermute | solution.py:36
  26.9 14.1 %collective-permute-done.2 = bf16[32,2048]{1,0:T(8,128)(2,1)} collective-permute-done((bf16[32,2048]{1,0:T(8,128)(2,1)S(1)}, bf16[32,2048]{1,0:T(8,128)(2,1)}, u32[]{:S(2)}, u32[]{:S(2)}) %collective-permute-start.2) | collective-permute-done | bytes 131104 | tf_op jit(solution)/shard_map/ppermute | solution.py:36
  41.0 1.8 convolution_bitcast_fusion.2
  42.8 1.4 convolution_bitcast_fusion.1
  44.2 1.3 convolution_bitcast_fusion
  47.2 1.9 collective-permute-done.4
  49.1 1.1 add_convert_fusion.4
  51.1 2.1 convolution_convert_fusion.1
  53.2 48.8 %all-gather.3.cloned.1.call-done = bf16[1024,4096]{1,0:T(8,128)(2,1)} async-done(((bf16[128,4096]{1,0:T(8,128)(2,1)}), bf16[1024,4096]{1,0:T(8,128)(2,1)}) %all-gather.3.cloned.1.call-update) | async-done | bytes 8388624 | tf_op jit(solution)/shard_map/all_gather | solution.py:274
  102.1 23.5 %ffn.2 = bf16[512,4096]{1,0:T(8,128)(2,1)} custom-call(s32[5]{0:T(128)S(1)} %get-tuple-element.93.order, bf16[2,4,128,4096]{3,2,1,0:T(8,128)(2,1)} %bitcast.83, bf16[4096,1024]{1,0:T(8,128)(2,1)} %gate_ref.3, bf16[4096,1024]{1,0:T(8,128)(2,1)} %up_ref.3, bf16[1024,4096]{1,0:T(8,128)(2,1)} %down_ref.3), custom_call_target="tpu_custom_call" | custom-call | flops 1024 | bytes 1024 | tf_op jit(solution)/shard_map/ffn/pallas_call | solution.py:141
  125.9 3.8 %collective-permute-start.15 = (bf16[32,2048]{1,0:T(8,128)(2,1)S(1)}, bf16[32,2048]{1,0:T(8,128)(2,1)S(1)}, u32[]{:S(2)}, u32[]{:S(2)}) collective-permute-start(bf16[32,2048]{1,0:T(8,128)(2,1)S(1)} %get-tuple-element.79), channel_id=1, source_target_pairs={{0,2},{1,3},{2,0},{3,1},{4,6},{5,7},{6,4},{7,5},{8,10},{9,11},{10,... | collective-permute-start | bytes 393224 | tf_op jit(solution)/shard_map/ppermute | solution.py:69
  129.8 0.8 dynamic-slice_bitcast_fusion
  130.6 1.5 collective-permute-start.6
  132.1 2.1 collective-permute-done.14
  134.1 5.0 %collective-permute-done.15 = bf16[32,2048]{1,0:T(8,128)(2,1)S(1)} collective-permute-done((bf16[32,2048]{1,0:T(8,128)(2,1)S(1)}, bf16[32,2048]{1,0:T(8,128)(2,1)S(1)}, u32[]{:S(2)}, u32[]{:S(2)}) %collective-permute-start.15) | collective-permute-done | bytes 131104 | tf_op jit(solution)/shard_map/ppermute | solution.py:69
  139.1 31.3 %collective-permute-start.8 = (bf16[2,512,256]{2,1,0:T(8,128)(2,1)}, bf16[2,512,256]{2,1,0:T(8,128)(2,1)S(1)}, u32[]{:S(2)}, u32[]{:S(2)}) collective-permute-start(bf16[2,512,256]{2,1,0:T(8,128)(2,1)} %dynamic-slice_bitcast_fusion), channel_id=1, source_target_pairs={{0,1},{1,2},{2,3},{3,0},{4,5},{5,6},{6,7},{7,4},{8,9},{9,10},{10,1... | collective-permute-start | bytes 1572872 | tf_op jit(solution)/shard_map/ppermute | solution.py:36
  170.5 22.2 %ffn.3 = bf16[512,4096]{1,0:T(8,128)(2,1)S(1)} custom-call(s32[5]{0:T(128)S(1)} %get-tuple-element.92.order, bf16[2,4,128,4096]{3,2,1,0:T(8,128)(2,1)} %bitcast.84, bf16[4096,1024]{1,0:T(8,128)(2,1)} %gate_ref.3, bf16[4096,1024]{1,0:T(8,128)(2,1)} %up_ref.3, bf16[1024,4096]{1,0:T(8,128)(2,1)} %down_ref.3), custom_call_target="tpu_custom_call" | custom-call | flops 1024 | bytes 1024 | tf_op jit(solution)/shard_map/ffn/pallas_call | solution.py:141
  192.7 0.8 copy-done.16
  193.7 2.1 pad_maximum_fusion.refs_2_
  195.9 1.3 collective-permute-done.17
  197.6 2.3 fusion.7
  199.9 2.0 collective-permute-start.10
  202.8 1.2 collective-permute-done.18
  204.0 4.9 %collective-permute-start.19 = (bf16[32,2048]{1,0:T(8,128)(2,1)S(1)}, bf16[32,2048]{1,0:T(8,128)(2,1)S(1)}, u32[]{:S(2)}, u32[]{:S(2)}) collective-permute-start(bf16[32,2048]{1,0:T(8,128)(2,1)S(1)} %maximum_select_fusion.3), channel_id=1, source_target_pairs={{0,3},{1,0},{2,1},{3,2},{4,7},{5,4},{6,5},{7,6},{8,11},{9,8},{10,9... | collective-permute-start | bytes 393224 | tf_op jit(solution)/shard_map/ppermute | solution.py:36
  208.9 1.5 collective-permute-start.12
  210.4 1.5 collective-permute-start.13
  211.9 15.5 %collective-permute-done.19 = bf16[32,2048]{1,0:T(8,128)(2,1)S(1)} collective-permute-done((bf16[32,2048]{1,0:T(8,128)(2,1)S(1)}, bf16[32,2048]{1,0:T(8,128)(2,1)S(1)}, u32[]{:S(2)}, u32[]{:S(2)}) %collective-permute-start.19) | collective-permute-done | bytes 131104 | tf_op jit(solution)/shard_map/ppermute | solution.py:36
  227.4 6.8 %collective-permute-start.20 = (bf16[32,2048]{1,0:T(8,128)(2,1)S(1)}, bf16[32,2048]{1,0:T(8,128)(2,1)S(1)}, u32[]{:S(2)}, u32[]{:S(2)}) collective-permute-start(bf16[32,2048]{1,0:T(8,128)(2,1)S(1)} %maximum_select_fusion.3), channel_id=1, source_target_pairs={{0,2},{1,3},{2,0},{3,1},{4,6},{5,7},{6,4},{7,5},{8,10},{9,11},{10,... | collective-permute-start | bytes 393224 | tf_op jit(solution)/shard_map/ppermute | solution.py:36
  234.2 4.8 %collective-permute-done.20 = bf16[32,2048]{1,0:T(8,128)(2,1)S(1)} collective-permute-done((bf16[32,2048]{1,0:T(8,128)(2,1)S(1)}, bf16[32,2048]{1,0:T(8,128)(2,1)S(1)}, u32[]{:S(2)}, u32[]{:S(2)}) %collective-permute-start.20) | collective-permute-done | bytes 131104 | tf_op jit(solution)/shard_map/ppermute | solution.py:36
  239.0 7.2 %collective-permute-done.21 = bf16[32,2048]{1,0:T(8,128)(2,1)S(1)} collective-permute-done((bf16[32,2048]{1,0:T(8,128)(2,1)S(1)}, bf16[32,2048]{1,0:T(8,128)(2,1)S(1)}, u32[]{:S(2)}, u32[]{:S(2)}) %collective-permute-start.21) | collective-permute-done | bytes 131104 | tf_op jit(solution)/shard_map/ppermute | solution.py:36
  246.3 3.3 add_convert_fusion.2
  249.7 2.3 collective-permute-start.22
  251.9 1.6 collective-permute-start.23
  253.6 2.5 collective-permute-start.24
  256.2 17.1 %collective-permute-done.22 = bf16[128,4096]{1,0:T(8,128)(2,1)} collective-permute-done((bf16[128,4096]{1,0:T(8,128)(2,1)}, bf16[128,4096]{1,0:T(8,128)(2,1)}, u32[]{:S(2)}, u32[]{:S(2)}) %collective-permute-start.22) | collective-permute-done | bytes 1048608 | tf_op jit(solution)/shard_map/ppermute | solution.py:59
  273.3 5.3 %add_convert_fusion = (bf16[128,4096]{1,0:T(8,128)(2,1)}, bf16[128,4096]{1,0:T(8,128)(2,1)}) fusion(bf16[128,4096]{1,0:T(8,128)(2,1)} %collective-permute-done.23, bf16[512,4096]{1,0:T(8,128)(2,1)} %collective-permute-done.9, bf16[512,4096]{1,0:T(8,128)(2,1)} %copy-done.2, bf16[128,4096]{1,0:T(8,128)(2,1)} %collective-permute-done.22), kind=kLoop, calls=%fused_computation.14 | loop fusion | flops 6291456 | bytes 8388608 | tf_op jit(solution)/shard_map/convert_element_type | solution.py:54
  278.6 11.5 %collective-permute-done.24.refs_5_ = bf16[3,2,512,256]{3,2,1,0:T(8,128)(2,1)} collective-permute-done((bf16[3,2,512,256]{3,2,1,0:T(8,128)(2,1)S(1)}, bf16[3,2,512,256]{3,2,1,0:T(8,128)(2,1)}, u32[]{:S(2)}, u32[]{:S(2)}) %collective-permute-start.24) | collective-permute-done | bytes 1572896 | tf_op jit(solution)/shard_map/ppermute | solution.py:30
  290.1 2.3 collective-permute-start.25
  292.4 1.3 collective-permute-start.26
  294.7 2.9 copy.29
  297.7 3.2 collective-permute-start.28
  300.9 1.0 collective-permute-start.29
  302.2 19.1 %collective-permute-done.28 = bf16[128,256]{1,0:T(8,128)(2,1)S(1)} collective-permute-done((bf16[128,256]{1,0:T(8,128)(2,1)S(1)}, bf16[128,256]{1,0:T(8,128)(2,1)S(1)}, u32[]{:S(2)}, u32[]{:S(2)}) %collective-permute-start.28) | collective-permute-done | bytes 65568 | tf_op jit(solution)/shard_map/ppermute | solution.py:36
  322.7 4.2 %fusion = (f32[128]{0:T(128)S(1)}, bf16[128,4096]{1,0:T(8,128)(2,1)S(1)}) fusion(bf16[128,4096]{1,0:T(8,128)(2,1)} %collective-permute-done.26, bf16[128,4096]{1,0:T(8,128)(2,1)} %collective-permute-done.25, bf16[512,4096]{1,0:T(8,128)(2,1)} %collective-permute-done.9, bf16[512,4096]{1,0:T(8,128)(2,1)} %copy-done.2, s32[128,4096]{1,0:T(8,128)} %bitcast.88, ...), kind=kLoop, calls=%fused_computation.7 | loop fusion | flops 9437056 | bytes 8405504 | tf_op jit(solution)/shard_map/reduce_sum | solution.py:18
  327.2 2.2 collective-permute-done.33.refs_8_
  329.4 2.2 collective-permute-done.34.refs_9_
  331.7 7.4 %attend_own_keys.1 = bf16[4,128,384]{2,1,0:T(8,128)(2,1)S(1)} custom-call(s32[16]{0:T(128)S(1)} %pad_add_fusion.3.table, bf16[128,4096]{1,0:T(8,128)(2,1)S(1)} %fusion.2.mem_ref, bf16[4,128,256]{2,1,0:T(8,128)(2,1)S(1)} %pad_maximum_fusion.4.cq_ref, bf16[2,2048,256]{2,1,0:T(8,128)(2,1)} %bitcast.86, bf16[2,2048,256]{2,1,0:T(8,128)(2,1)} %collective-permute-done.5.refs_1_, ...), custom_call_target="tpu_custom_call" | custom-call | flops 1024 | bytes 1024 | tf_op jit(solution)/shard_map/attend_own_keys/pallas_call | solution.py:219
  339.7 3.4 collective-permute-start.37
  343.0 3.7 collective-permute-done.35
  346.8 3.4 collective-permute-done.36
  351.4 1.5 collective-permute-done.38
  353.6 1.9 collective-permute-start.39
  355.4 0.9 collective-permute-start.40
  356.3 1.6 collective-permute-start.41
  357.9 4.0 %collective-permute-done.39 = bf16[32,2048]{1,0:T(8,128)(2,1)S(1)} collective-permute-done((bf16[32,2048]{1,0:T(8,128)(2,1)S(1)}, bf16[32,2048]{1,0:T(8,128)(2,1)S(1)}, u32[]{:S(2)}, u32[]{:S(2)}) %collective-permute-start.39) | collective-permute-done | bytes 131104 | tf_op jit(solution)/shard_map/ppermute | solution.py:69
  361.9 4.8 %collective-permute-done.40 = bf16[32,2048]{1,0:T(8,128)(2,1)S(1)} collective-permute-done((bf16[32,2048]{1,0:T(8,128)(2,1)S(1)}, bf16[32,2048]{1,0:T(8,128)(2,1)S(1)}, u32[]{:S(2)}, u32[]{:S(2)}) %collective-permute-start.40) | collective-permute-done | bytes 131104 | tf_op jit(solution)/shard_map/ppermute | solution.py:69
  367.2 1.1 collective-permute-done.42
  (161 shorter events, 12.2 us)
Async XLA Ops:
  7.2 44.0 %copy-start = (bf16[256,2048]{1,0:T(8,128)(2,1)S(1)}, bf16[256,2048]{1,0:T(8,128)(2,1)}, u32[]{:S(2)}) copy-start(bf16[256,2048]{1,0:T(8,128)(2,1)} %param.28) | copy-start | bytes 3145732
  7.2 4.2 %copy-start.11 = (bf16[16,4096]{1,0:T(8,128)(2,1)S(1)}, bf16[16,4096]{1,0:T(8,128)(2,1)}, u32[]{:S(2)}) copy-start(bf16[16,4096]{1,0:T(8,128)(2,1)} %param.25) | copy-start | bytes 393220
  7.2 4.4 %copy-start.24 = (f32[4096]{0:T(1024)S(1)}, f32[4096]{0:T(1024)}, u32[]{:S(2)}) copy-start(f32[4096]{0:T(1024)} %param.26) | copy-start | bytes 49156
  7.2 94.9 %all-gather.3.cloned.1.call-start = ((), (), s32[]{:S(2)}) async-start(), calls=%async_computation | async-start | bytes 9437184 | tf_op jit(solution)/shard_map/all_gather | solution.py:274
  11.7 2.5 collective-permute-start
  14.1 115.7 %copy-start.7 = (bf16[2048,2,256]{2,0,1:T(8,128)(2,1)}, bf16[2048,2,256]{2,0,1:T(8,128)(2,1)S(1)}, u32[]{:S(2)}) copy-start(bf16[2048,2,256]{2,0,1:T(8,128)(2,1)S(1)} %copy.38) | copy-start | bytes 6291460
  14.1 39.1 %collective-permute-start.5 = (bf16[2,2048,256]{2,1,0:T(8,128)(2,1)S(1)}, bf16[2,2048,256]{2,1,0:T(8,128)(2,1)}, u32[]{:S(2)}, u32[]{:S(2)}) collective-permute-start(bf16[2,2048,256]{2,1,0:T(8,128)(2,1)S(1)} %bitcast.85), channel_id=1, source_target_pairs={{0,4},{4,0},{1,5},{5,1},{2,6},{6,2},{3,7},{7,3},{8,12},{12,8},{9,1... | collective-permute-start | bytes 6291464 | tf_op jit(solution)/shard_map/ppermute | solution.py:30
  16.0 25.0 %copy-start.19 = (bf16[32,2048]{1,0:T(8,128)(2,1)}, bf16[32,2048]{1,0:T(8,128)(2,1)S(1)}, u32[]{:S(2)}) copy-start(bf16[32,2048]{1,0:T(8,128)(2,1)S(1)} %maximum_select_fusion.2) | copy-start | bytes 393220
  16.0 10.9 %collective-permute-start.1 = (bf16[32,2048]{1,0:T(8,128)(2,1)S(1)}, bf16[32,2048]{1,0:T(8,128)(2,1)S(1)}, u32[]{:S(2)}, u32[]{:S(2)}) collective-permute-start(bf16[32,2048]{1,0:T(8,128)(2,1)S(1)} %maximum_select_fusion.2), channel_id=1, source_target_pairs={{0,3},{1,0},{2,1},{3,2},{4,7},{5,4},{6,5},{7,6},{8,11},{9,8},{10,9... | collective-permute-start | bytes 393224 | tf_op jit(solution)/shard_map/ppermute | solution.py:36
  21.1 19.9 %collective-permute-start.2 = (bf16[32,2048]{1,0:T(8,128)(2,1)S(1)}, bf16[32,2048]{1,0:T(8,128)(2,1)}, u32[]{:S(2)}, u32[]{:S(2)}) collective-permute-start(bf16[32,2048]{1,0:T(8,128)(2,1)S(1)} %maximum_select_fusion.2), channel_id=1, source_target_pairs={{0,2},{1,3},{2,0},{3,1},{4,6},{5,7},{6,4},{7,5},{8,10},{9,11},{10,... | collective-permute-start | bytes 393224 | tf_op jit(solution)/shard_map/ppermute | solution.py:36
  21.1 19.9 %collective-permute-start.3 = (bf16[32,2048]{1,0:T(8,128)(2,1)S(1)}, bf16[32,2048]{1,0:T(8,128)(2,1)}, u32[]{:S(2)}, u32[]{:S(2)}) collective-permute-start(bf16[32,2048]{1,0:T(8,128)(2,1)S(1)} %maximum_select_fusion.2), channel_id=1, source_target_pairs={{0,1},{1,2},{2,3},{3,0},{4,5},{5,6},{6,7},{7,4},{8,9},{9,10},{10,1... | collective-permute-start | bytes 393224 | tf_op jit(solution)/shard_map/ppermute | solution.py:36
  22.1 20.7 %copy-start.26 = (bf16[2048,3,256]{2,0,1:T(8,128)(2,1)S(1)}, bf16[2048,3,256]{2,0,1:T(8,128)(2,1)}, u32[]{:S(2)}) copy-start(bf16[2048,3,256]{2,0,1:T(8,128)(2,1)} %param.27) | copy-start | bytes 9437188
  26.9 14.1 %copy-start.27 = (bf16[32,2048]{1,0:T(8,128)(2,1)}, bf16[32,2048]{1,0:T(8,128)(2,1)S(1)}, u32[]{:S(2)}) copy-start(bf16[32,2048]{1,0:T(8,128)(2,1)S(1)} %collective-permute-done.1) | copy-start | bytes 393220
  46.9 2.2 collective-permute-start.4
  102.1 23.7 %copy-start.10 = (bf16[128,2048]{1,0:T(8,128)(2,1)S(1)}, bf16[128,2048]{1,0:T(8,128)(2,1)}, u32[]{:S(2)}) copy-start(bf16[128,2048]{1,0:T(8,128)(2,1)} %convolution_convert_fusion.1) | copy-start | bytes 1572868
  125.6 72.0 %collective-permute-start.9 = (bf16[512,4096]{1,0:T(8,128)(2,1)}, bf16[512,4096]{1,0:T(8,128)(2,1)}, u32[]{:S(2)}, u32[]{:S(2)}) collective-permute-start(bf16[512,4096]{1,0:T(8,128)(2,1)} %ffn.2), channel_id=1, source_target_pairs={{0,4},{4,0},{1,5},{5,1},{2,6},{6,2},{3,7},{7,3},{8,12},{12,8},{9,1... | collective-permute-start | bytes 12582920 | tf_op jit(solution)/shard_map/ppermute | solution.py:30
  125.9 8.3 %collective-permute-start.14 = (bf16[32,2048]{1,0:T(8,128)(2,1)S(1)}, bf16[32,2048]{1,0:T(8,128)(2,1)S(1)}, u32[]{:S(2)}, u32[]{:S(2)}) collective-permute-start(bf16[32,2048]{1,0:T(8,128)(2,1)S(1)} %get-tuple-element.77), channel_id=1, source_target_pairs={{0,1},{1,2},{2,3},{3,0},{4,5},{5,6},{6,7},{7,4},{8,9},{9,10},{10,1... | collective-permute-start | bytes 393224 | tf_op jit(solution)/shard_map/ppermute | solution.py:69
  125.9 13.2 %collective-permute-start.15 = (bf16[32,2048]{1,0:T(8,128)(2,1)S(1)}, bf16[32,2048]{1,0:T(8,128)(2,1)S(1)}, u32[]{:S(2)}, u32[]{:S(2)}) collective-permute-start(bf16[32,2048]{1,0:T(8,128)(2,1)S(1)} %get-tuple-element.79), channel_id=1, source_target_pairs={{0,2},{1,3},{2,0},{3,1},{4,6},{5,7},{6,4},{7,5},{8,10},{9,11},{10,... | collective-permute-start | bytes 393224 | tf_op jit(solution)/shard_map/ppermute | solution.py:69
  129.8 40.6 %collective-permute-start.16 = (bf16[32,2048]{1,0:T(8,128)(2,1)S(1)}, bf16[32,2048]{1,0:T(8,128)(2,1)S(1)}, u32[]{:S(2)}, u32[]{:S(2)}) collective-permute-start(bf16[32,2048]{1,0:T(8,128)(2,1)S(1)} %get-tuple-element.78), channel_id=1, source_target_pairs={{0,3},{1,0},{2,1},{3,2},{4,7},{5,4},{6,5},{7,6},{8,11},{9,8},{10,9... | collective-permute-start | bytes 393224 | tf_op jit(solution)/shard_map/ppermute | solution.py:69
  130.6 62.1 %collective-permute-start.6 = (bf16[2,512,256]{2,1,0:T(8,128)(2,1)}, bf16[2,512,256]{2,1,0:T(8,128)(2,1)S(1)}, u32[]{:S(2)}, u32[]{:S(2)}) collective-permute-start(bf16[2,512,256]{2,1,0:T(8,128)(2,1)} %dynamic-slice_bitcast_fusion), channel_id=1, source_target_pairs={{0,3},{1,0},{2,1},{3,2},{4,7},{5,4},{6,5},{7,6},{8,11},{9,8},{10,9... | collective-permute-start | bytes 1572872 | tf_op jit(solution)/shard_map/ppermute | solution.py:36
  134.1 58.5 %collective-permute-start.7 = (bf16[2,512,256]{2,1,0:T(8,128)(2,1)}, bf16[2,512,256]{2,1,0:T(8,128)(2,1)S(1)}, u32[]{:S(2)}, u32[]{:S(2)}) collective-permute-start(bf16[2,512,256]{2,1,0:T(8,128)(2,1)} %dynamic-slice_bitcast_fusion), channel_id=1, source_target_pairs={{0,2},{1,3},{2,0},{3,1},{4,6},{5,7},{6,4},{7,5},{8,10},{9,11},{10,... | collective-permute-start | bytes 1572872 | tf_op jit(solution)/shard_map/ppermute | solution.py:36
  139.1 53.6 %collective-permute-start.8 = (bf16[2,512,256]{2,1,0:T(8,128)(2,1)}, bf16[2,512,256]{2,1,0:T(8,128)(2,1)S(1)}, u32[]{:S(2)}, u32[]{:S(2)}) collective-permute-start(bf16[2,512,256]{2,1,0:T(8,128)(2,1)} %dynamic-slice_bitcast_fusion), channel_id=1, source_target_pairs={{0,1},{1,2},{2,3},{3,0},{4,5},{5,6},{6,7},{7,4},{8,9},{9,10},{10,1... | collective-permute-start | bytes 1572872 | tf_op jit(solution)/shard_map/ppermute | solution.py:36
  192.7 53.6 %copy-start.2 = (bf16[512,4096]{1,0:T(8,128)(2,1)}, bf16[512,4096]{1,0:T(8,128)(2,1)S(1)}, u32[]{:S(2)}) copy-start(bf16[512,4096]{1,0:T(8,128)(2,1)S(1)} %ffn.3) | copy-start | bytes 12582916
  193.7 3.8 %copy-start.25 = (f32[4096]{0:T(1024)S(1)}, f32[4096]{0:T(1024)}, u32[]{:S(2)}) copy-start(f32[4096]{0:T(1024)} %param.29) | copy-start | bytes 49156
  195.9 1.4 collective-permute-start.17
  199.9 46.4 %collective-permute-start.10 = (bf16[128,4096]{1,0:T(8,128)(2,1)S(1)}, bf16[128,4096]{1,0:T(8,128)(2,1)S(1)}, u32[]{:S(2)}, u32[]{:S(2)}) collective-permute-start(bf16[128,4096]{1,0:T(8,128)(2,1)S(1)} %get-tuple-element.71), channel_id=1, source_target_pairs={{0,1},{4,5},{8,9},{12,13},{16,17},{20,21},{24,25},{28,29}} | collective-permute-start | bytes 3145736 | tf_op jit(solution)/shard_map/ppermute | solution.py:59
  201.9 44.4 %collective-permute-start.11 = (bf16[128,4096]{1,0:T(8,128)(2,1)S(1)}, bf16[128,4096]{1,0:T(8,128)(2,1)S(1)}, u32[]{:S(2)}, u32[]{:S(2)}) collective-permute-start(bf16[128,4096]{1,0:T(8,128)(2,1)S(1)} %get-tuple-element.70), channel_id=1, source_target_pairs={{3,2},{7,6},{11,10},{15,14},{19,18},{23,22},{27,26},{31,30}} | collective-permute-start | bytes 3145736 | tf_op jit(solution)/shard_map/ppermute | solution.py:60
  202.7 1.3 collective-permute-start.18
  204.0 23.3 %collective-permute-start.19 = (bf16[32,2048]{1,0:T(8,128)(2,1)S(1)}, bf16[32,2048]{1,0:T(8,128)(2,1)S(1)}, u32[]{:S(2)}, u32[]{:S(2)}) collective-permute-start(bf16[32,2048]{1,0:T(8,128)(2,1)S(1)} %maximum_select_fusion.3), channel_id=1, source_target_pairs={{0,3},{1,0},{2,1},{3,2},{4,7},{5,4},{6,5},{7,6},{8,11},{9,8},{10,9... | collective-permute-start | bytes 393224 | tf_op jit(solution)/shard_map/ppermute | solution.py:36
  208.9 40.7 %collective-permute-start.12 = (bf16[3,2,512,256]{3,2,1,0:T(8,128)(2,1)S(1)}, bf16[3,2,512,256]{3,2,1,0:T(8,128)(2,1)S(1)}, u32[]{:S(2)}, u32[]{:S(2)}) collective-permute-start(bf16[3,2,512,256]{3,2,1,0:T(8,128)(2,1)S(1)} %pad_maximum_fusion.refs_2_), channel_id=1, source_target_pairs={{0,8},{8,0},{16,24},{24,16},{1,9},{9,1},{17,25},{25,17},{2,10},{10... | collective-permute-start | bytes 4718600 | tf_op jit(solution)/shard_map/ppermute | solution.py:30
  210.4 39.2 %collective-permute-start.13 = (bf16[3,2,512,256]{3,2,1,0:T(8,128)(2,1)S(1)}, bf16[3,2,512,256]{3,2,1,0:T(8,128)(2,1)S(1)}, u32[]{:S(2)}, u32[]{:S(2)}) collective-permute-start(bf16[3,2,512,256]{3,2,1,0:T(8,128)(2,1)S(1)} %pad_maximum_fusion.refs_2_), channel_id=1, source_target_pairs={{0,16},{8,24},{16,0},{24,8},{1,17},{9,25},{17,1},{25,9},{2,18},{10... | collective-permute-start | bytes 4718600 | tf_op jit(solution)/shard_map/ppermute | solution.py:30
  227.4 11.6 %collective-permute-start.20 = (bf16[32,2048]{1,0:T(8,128)(2,1)S(1)}, bf16[32,2048]{1,0:T(8,128)(2,1)S(1)}, u32[]{:S(2)}, u32[]{:S(2)}) collective-permute-start(bf16[32,2048]{1,0:T(8,128)(2,1)S(1)} %maximum_select_fusion.3), channel_id=1, source_target_pairs={{0,2},{1,3},{2,0},{3,1},{4,6},{5,7},{6,4},{7,5},{8,10},{9,11},{10,... | collective-permute-start | bytes 393224 | tf_op jit(solution)/shard_map/ppermute | solution.py:36
  239.0 7.2 %collective-permute-start.21 = (bf16[32,2048]{1,0:T(8,128)(2,1)S(1)}, bf16[32,2048]{1,0:T(8,128)(2,1)S(1)}, u32[]{:S(2)}, u32[]{:S(2)}) collective-permute-start(bf16[32,2048]{1,0:T(8,128)(2,1)S(1)} %maximum_select_fusion.3), channel_id=1, source_target_pairs={{0,1},{1,2},{2,3},{3,0},{4,5},{5,6},{6,7},{7,4},{8,9},{9,10},{10,1... | collective-permute-start | bytes 393224 | tf_op jit(solution)/shard_map/ppermute | solution.py:36
  249.6 3.9 %copy-start.5 = (bf16[3,2,512,256]{3,2,1,0:T(8,128)(2,1)}, bf16[3,2,512,256]{3,2,1,0:T(8,128)(2,1)S(1)}, u32[]{:S(2)}) copy-start(bf16[3,2,512,256]{3,2,1,0:T(8,128)(2,1)S(1)} %collective-permute-done.13.refs_4_) | copy-start | bytes 4718596
  249.7 23.6 %collective-permute-start.22 = (bf16[128,4096]{1,0:T(8,128)(2,1)}, bf16[128,4096]{1,0:T(8,128)(2,1)}, u32[]{:S(2)}, u32[]{:S(2)}) collective-permute-start(bf16[128,4096]{1,0:T(8,128)(2,1)} %get-tuple-element.32), channel_id=1, source_target_pairs={{0,1},{1,2},{4,5},{5,6},{8,9},{9,10},{12,13},{13,14},{16,17},{17,1... | collective-permute-start | bytes 3145736 | tf_op jit(solution)/shard_map/ppermute | solution.py:59
  251.9 21.3 %collective-permute-start.23 = (bf16[128,4096]{1,0:T(8,128)(2,1)}, bf16[128,4096]{1,0:T(8,128)(2,1)}, u32[]{:S(2)}, u32[]{:S(2)}) collective-permute-start(bf16[128,4096]{1,0:T(8,128)(2,1)} %get-tuple-element.33), channel_id=1, source_target_pairs={{2,1},{3,2},{6,5},{7,6},{10,9},{11,10},{14,13},{15,14},{18,17},{19... | collective-permute-start | bytes 3145736 | tf_op jit(solution)/shard_map/ppermute | solution.py:60
  253.6 36.5 %collective-permute-start.24 = (bf16[3,2,512,256]{3,2,1,0:T(8,128)(2,1)S(1)}, bf16[3,2,512,256]{3,2,1,0:T(8,128)(2,1)}, u32[]{:S(2)}, u32[]{:S(2)}) collective-permute-start(bf16[3,2,512,256]{3,2,1,0:T(8,128)(2,1)S(1)} %pad_maximum_fusion.refs_2_), channel_id=1, source_target_pairs={{0,24},{8,16},{16,8},{24,0},{1,25},{9,17},{17,9},{25,1},{2,26},{10... | collective-permute-start | bytes 4718600 | tf_op jit(solution)/shard_map/ppermute | solution.py:30
  256.2 37.5 %copy-start.13 = (bf16[2048,256]{1,0:T(8,128)(2,1)S(1)}, bf16[2048,256]{1,0:T(8,128)(2,1)}, u32[]{:S(2)}) copy-start(bf16[2048,256]{1,0:T(8,128)(2,1)} %param.30) | copy-start | bytes 3145732
  278.6 15.5 %copy-start.14 = (s32[128,1024]{1,0:T(8,128)S(1)}, s32[128,1024]{1,0:T(8,128)}, u32[]{:S(2)}) copy-start(s32[128,1024]{1,0:T(8,128)} %param.23) | copy-start | bytes 1572868
  290.1 32.5 %collective-permute-start.25 = (bf16[128,4096]{1,0:T(8,128)(2,1)}, bf16[128,4096]{1,0:T(8,128)(2,1)}, u32[]{:S(2)}, u32[]{:S(2)}) collective-permute-start(bf16[128,4096]{1,0:T(8,128)(2,1)} %get-tuple-element.36), channel_id=1, source_target_pairs={{0,1},{1,2},{2,3},{4,5},{5,6},{6,7},{8,9},{9,10},{10,11},{12,13},{... | collective-permute-start | bytes 3145736 | tf_op jit(solution)/shard_map/ppermute | solution.py:59
  292.4 30.3 %collective-permute-start.26 = (bf16[128,4096]{1,0:T(8,128)(2,1)}, bf16[128,4096]{1,0:T(8,128)(2,1)}, u32[]{:S(2)}, u32[]{:S(2)}) collective-permute-start(bf16[128,4096]{1,0:T(8,128)(2,1)} %get-tuple-element.37), channel_id=1, source_target_pairs={{1,0},{2,1},{3,2},{5,4},{6,5},{7,6},{9,8},{10,9},{11,10},{13,12},{... | collective-permute-start | bytes 3145736 | tf_op jit(solution)/shard_map/ppermute | solution.py:60
  294.0 3.7 collective-permute-start.27
  294.7 27.9 %copy-start.8 = (bf16[128,4096]{1,0:T(8,128)(2,1)S(1)}, bf16[128,4096]{1,0:T(8,128)(2,1)}, u32[]{:S(2)}) copy-start(bf16[128,4096]{1,0:T(8,128)(2,1)} %param.18) | copy-start | bytes 3145732
  297.7 23.5 %collective-permute-start.28 = (bf16[128,256]{1,0:T(8,128)(2,1)S(1)}, bf16[128,256]{1,0:T(8,128)(2,1)S(1)}, u32[]{:S(2)}, u32[]{:S(2)}) collective-permute-start(bf16[128,256]{1,0:T(8,128)(2,1)S(1)} %bitcast.98), channel_id=1, source_target_pairs={{0,3},{1,0},{2,1},{3,2},{4,7},{5,4},{6,5},{7,6},{8,11},{9,8},{10,9... | collective-permute-start | bytes 196616 | tf_op jit(solution)/shard_map/ppermute | solution.py:36
  300.9 21.1 %collective-permute-start.29 = (bf16[128,256]{1,0:T(8,128)(2,1)S(1)}, bf16[128,256]{1,0:T(8,128)(2,1)S(1)}, u32[]{:S(2)}, u32[]{:S(2)}) collective-permute-start(bf16[128,256]{1,0:T(8,128)(2,1)S(1)} %bitcast.99), channel_id=1, source_target_pairs={{0,2},{1,3},{2,0},{3,1},{4,6},{5,7},{6,4},{7,5},{8,10},{9,11},{10,... | collective-permute-start | bytes 196616 | tf_op jit(solution)/shard_map/ppermute | solution.py:36
  301.9 20.1 %collective-permute-start.30 = (bf16[128,256]{1,0:T(8,128)(2,1)S(1)}, bf16[128,256]{1,0:T(8,128)(2,1)S(1)}, u32[]{:S(2)}, u32[]{:S(2)}) collective-permute-start(bf16[128,256]{1,0:T(8,128)(2,1)S(1)} %bitcast.100), channel_id=1, source_target_pairs={{0,1},{1,2},{2,3},{3,0},{4,5},{5,6},{6,7},{7,4},{8,9},{9,10},{10,1... | collective-permute-start | bytes 196616 | tf_op jit(solution)/shard_map/ppermute | solution.py:36
  321.3 5.9 %collective-permute-start.31 = (bf16[3,2,512,256]{3,2,1,0:T(8,128)(2,1)S(1)}, bf16[3,2,512,256]{3,2,1,0:T(8,128)(2,1)S(1)}, u32[]{:S(2)}, u32[]{:S(2)}) collective-permute-start(bf16[3,2,512,256]{3,2,1,0:T(8,128)(2,1)S(1)} %pad_maximum_fusion.refs_2_), channel_id=1, source_target_pairs={{0,4},{4,0},{1,5},{5,1},{2,6},{6,2},{3,7},{7,3},{8,12},{12,8},{9,1... | collective-permute-start | bytes 4718600 | tf_op jit(solution)/shard_map/ppermute | solution.py:30
  322.0 5.2 %collective-permute-start.32 = (bf16[3,2,512,256]{3,2,1,0:T(8,128)(2,1)}, bf16[3,2,512,256]{3,2,1,0:T(8,128)(2,1)S(1)}, u32[]{:S(2)}, u32[]{:S(2)}) collective-permute-start(bf16[3,2,512,256]{3,2,1,0:T(8,128)(2,1)} %copy-done.3), channel_id=1, source_target_pairs={{0,4},{4,0},{1,5},{5,1},{2,6},{6,2},{3,7},{7,3},{8,12},{12,8},{9,1... | collective-permute-start | bytes 4718600 | tf_op jit(solution)/shard_map/ppermute | solution.py:30
  322.0 7.4 %collective-permute-start.33 = (bf16[3,2,512,256]{3,2,1,0:T(8,128)(2,1)}, bf16[3,2,512,256]{3,2,1,0:T(8,128)(2,1)S(1)}, u32[]{:S(2)}, u32[]{:S(2)}) collective-permute-start(bf16[3,2,512,256]{3,2,1,0:T(8,128)(2,1)} %copy-done.5), channel_id=1, source_target_pairs={{0,4},{4,0},{1,5},{5,1},{2,6},{6,2},{3,7},{7,3},{8,12},{12,8},{9,1... | collective-permute-start | bytes 4718600 | tf_op jit(solution)/shard_map/ppermute | solution.py:30
  322.5 9.1 %collective-permute-start.34 = (bf16[3,2,512,256]{3,2,1,0:T(8,128)(2,1)}, bf16[3,2,512,256]{3,2,1,0:T(8,128)(2,1)S(1)}, u32[]{:S(2)}, u32[]{:S(2)}) collective-permute-start(bf16[3,2,512,256]{3,2,1,0:T(8,128)(2,1)} %collective-permute-done.24.refs_5_), channel_id=1, source_target_pairs={{0,4},{4,0},{1,5},{5,1},{2,6},{6,2},{3,7},{7,3},{8,12},{12,8},{9,1... | collective-permute-start | bytes 4718600 | tf_op jit(solution)/shard_map/ppermute | solution.py:30
  322.6 4.2 %copy-start.23 = (f32[4096]{0:T(1024)S(1)}, f32[4096]{0:T(1024)}, u32[]{:S(2)}) copy-start(f32[4096]{0:T(1024)} %param.24) | copy-start | bytes 49156
  322.6 9.0 %copy-start.6 = (bf16[3,2,512,256]{3,2,1,0:T(8,128)(2,1)S(1)}, bf16[3,2,512,256]{3,2,1,0:T(8,128)(2,1)}, u32[]{:S(2)}) copy-start(bf16[3,2,512,256]{3,2,1,0:T(8,128)(2,1)} %copy-done.5) | copy-start | bytes 4718596
  326.8 4.8 %copy-start.4 = (bf16[3,2,512,256]{3,2,1,0:T(8,128)(2,1)S(1)}, bf16[3,2,512,256]{3,2,1,0:T(8,128)(2,1)}, u32[]{:S(2)}) copy-start(bf16[3,2,512,256]{3,2,1,0:T(8,128)(2,1)} %copy-done.3) | copy-start | bytes 4718596
  339.2 7.6 %collective-permute-start.35 = (bf16[128,384]{1,0:T(8,128)(2,1)S(1)}, bf16[128,384]{1,0:T(8,128)(2,1)S(1)}, u32[]{:S(2)}, u32[]{:S(2)}) collective-permute-start(bf16[128,384]{1,0:T(8,128)(2,1)S(1)} %get-tuple-element.83), channel_id=1, source_target_pairs={{0,1},{1,2},{2,3},{3,0},{4,5},{5,6},{6,7},{7,4},{8,9},{9,10},{10,1... | collective-permute-start | bytes 294920 | tf_op jit(solution)/shard_map/ppermute | solution.py:338
  339.7 10.5 %collective-permute-start.36 = (bf16[128,384]{1,0:T(8,128)(2,1)S(1)}, bf16[128,384]{1,0:T(8,128)(2,1)S(1)}, u32[]{:S(2)}, u32[]{:S(2)}) collective-permute-start(bf16[128,384]{1,0:T(8,128)(2,1)S(1)} %get-tuple-element.82), channel_id=1, source_target_pairs={{0,2},{1,3},{2,0},{3,1},{4,6},{5,7},{6,4},{7,5},{8,10},{9,11},{10,... | collective-permute-start | bytes 294920 | tf_op jit(solution)/shard_map/ppermute | solution.py:338
  339.7 10.5 %collective-permute-start.37 = (bf16[128,384]{1,0:T(8,128)(2,1)S(1)}, bf16[128,384]{1,0:T(8,128)(2,1)S(1)}, u32[]{:S(2)}, u32[]{:S(2)}) collective-permute-start(bf16[128,384]{1,0:T(8,128)(2,1)S(1)} %get-tuple-element.81), channel_id=1, source_target_pairs={{0,3},{1,0},{2,1},{3,2},{4,7},{5,4},{6,5},{7,6},{8,11},{9,8},{10,9... | collective-permute-start | bytes 294920 | tf_op jit(solution)/shard_map/ppermute | solution.py:338
  350.2 3.0 copy-start.12
  351.2 1.6 collective-permute-start.38
  353.0 13.9 %copy-start.21 = (s32[16,1024]{1,0:T(8,128)S(1)}, s32[16,1024]{1,0:T(8,128)}, u32[]{:S(2)}) copy-start(s32[16,1024]{1,0:T(8,128)} %param.33) | copy-start | bytes 196612
  353.2 15.8 %copy-start.1 = (bf16[256,2048]{1,0:T(8,128)(2,1)S(1)}, bf16[256,2048]{1,0:T(8,128)(2,1)}, u32[]{:S(2)}) copy-start(bf16[256,2048]{1,0:T(8,128)(2,1)} %param.28) | copy-start | bytes 3145732
  353.6 8.3 %collective-permute-start.39 = (bf16[32,2048]{1,0:T(8,128)(2,1)S(1)}, bf16[32,2048]{1,0:T(8,128)(2,1)S(1)}, u32[]{:S(2)}, u32[]{:S(2)}) collective-permute-start(bf16[32,2048]{1,0:T(8,128)(2,1)S(1)} %get-tuple-element.74), channel_id=1, source_target_pairs={{0,1},{1,2},{2,3},{3,0},{4,5},{5,6},{6,7},{7,4},{8,9},{9,10},{10,1... | collective-permute-start | bytes 393224 | tf_op jit(solution)/shard_map/ppermute | solution.py:69
  355.4 11.3 %collective-permute-start.40 = (bf16[32,2048]{1,0:T(8,128)(2,1)S(1)}, bf16[32,2048]{1,0:T(8,128)(2,1)S(1)}, u32[]{:S(2)}, u32[]{:S(2)}) collective-permute-start(bf16[32,2048]{1,0:T(8,128)(2,1)S(1)} %get-tuple-element.76), channel_id=1, source_target_pairs={{0,2},{1,3},{2,0},{3,1},{4,6},{5,7},{6,4},{7,5},{8,10},{9,11},{10,... | collective-permute-start | bytes 393224 | tf_op jit(solution)/shard_map/ppermute | solution.py:69
  356.3 10.4 %collective-permute-start.41 = (bf16[32,2048]{1,0:T(8,128)(2,1)S(1)}, bf16[32,2048]{1,0:T(8,128)(2,1)S(1)}, u32[]{:S(2)}, u32[]{:S(2)}) collective-permute-start(bf16[32,2048]{1,0:T(8,128)(2,1)S(1)} %get-tuple-element.75), channel_id=1, source_target_pairs={{0,3},{1,0},{2,1},{3,2},{4,7},{5,4},{6,5},{7,6},{8,11},{9,8},{10,9... | collective-permute-start | bytes 393224 | tf_op jit(solution)/shard_map/ppermute | solution.py:69
  366.8 1.4 collective-permute-start.42
  (9 other events, 12.1 us)
Sparse Core Ops, SparseCore 0:
  11.5 90.5 all-gather.2

commit v9 on v8

--- a/solution.py
+++ b/solution.py
@@ -291,33 +291,36 @@
     product = jnp.dot(context, self_out, preferred_element_type=F32).astype(BF16)
     total = slots_sum(product)
 
-    x, product, other_head = lax.optimization_barrier((x, product, own_head[1]))
+    mid = (target.astype(F32) + whole_rows(total, section)).astype(BF16)
+    crossin = norm_rows(mid, cross_gain).astype(BF16)
+    x, crossin, other_head = lax.optimization_barrier((x, crossin, own_head[1]))
     own_head[1] = other_head
+    crossin = gather_half(crossin, section)
+
     depth = cross_kv.shape[0] // groups
     share = gated(lax.dynamic_slice_in_dim(own_head[0], group * depth, depth, 1), x)
-    shares = [jnp.stack(from_slots(share)[1:])]
+    share = lax.all_gather(share, "tensor", axis=0, tiled=False)
+    shares = [jnp.roll(share, -tensor, axis=0)[1:]]
 
     theirs = ffn(x, jnp.concatenate([(1 - section)[None], slot_chip]), w_gate, w_up, w_down)
+    theirs, crossin = lax.optimization_barrier((theirs, crossin))
     got = swap(theirs, "section", 1)
-    x = gated(x, theirs)
+    cq = both_halves(jnp.dot(crossin, cross_q, preferred_element_type=F32)).astype(BF16)
+    cq = jnp.roll(cq.reshape(count, 2, rows, HD), tensor, axis=0)
+    cq = jnp.transpose(cq, (1, 0, 2, 3)).reshape(2 * count * rows, HD)
+    x, cq, shares[0] = lax.optimization_barrier((x, cq, shares[0]))
+    queries = jnp.stack(from_slots(cq))
     mine = ffn(x, jnp.concatenate([section[None], slot_chip]), w_gate, w_up, w_down)
-    mine, shares[0] = lax.optimization_barrier((mine, shares[0]))
     shares += [swap(shares[0], "dp", j) for j in range(1, groups)]
 
+    mine, queries = lax.optimization_barrier((mine, queries))
     came = sum_step(sum_sends(mine, got, None, 1), 1)
-    total = gated(total, mine)
-    mid = (target.astype(F32) + whole_rows(total, section)).astype(BF16)
-    crossin = gather_half(norm_rows(mid, cross_gain).astype(BF16), section)
     for step in range(2, count):
         sends = sum_sends(mine, got, came, step)
         if step == 2:
             near = tuple(shares[1 : 1 + groups // 2])
-            held = lax.optimization_barrier(sends + near + (crossin,))
-            sends, shares[1 : 1 + groups // 2], crossin = held[:2], list(held[2:-1]), held[-1]
-            cq = both_halves(jnp.dot(crossin, cross_q, preferred_element_type=F32)).astype(BF16)
-            cq = jnp.roll(cq.reshape(count, 2, rows, HD), tensor, axis=0)
-            cq = jnp.transpose(cq, (1, 0, 2, 3)).reshape(2 * count * rows, HD)
-            queries = jnp.stack(from_slots(cq))
+            held = lax.optimization_barrier(sends + near)
+            sends, shares[1 : 1 + groups // 2] = held[:2], list(held[2:])
         elif step == count - 1:
             rest = tuple(shares[1 + groups // 2 :])
             held = lax.optimization_barrier(sends + rest)

time: 383 us -> 381 us (level)
  waiting for transfers between devices: 178 us -> 213 us
  starting transfers between devices: 84.4 us -> 55 us
    ppermute x12 -> x9, waiting for transfers between devices: 66.2 us -> 11.3 us  [from_slots(): lax.ppermute(value, 'tensor', [(i, (i - o) % count) for i in range(count)])]
    ppermute x12 -> x9, starting transfers between devices: 54.8 us -> 15.1 us  [from_slots(): lax.ppermute(value, 'tensor', [(i, (i - o) % count) for i in range(count)])]
    all_gather x0 -> x1, waiting for transfers between devices: none -> 39.4 us  [per_device(): share = lax.all_gather(share, 'tensor', axis=0, tiled=False)]
    ppermute x3, waiting for transfers between devices: 17.1 us -> 47.7 us  [sum_step(): above = lax.ppermute(sends[0], 'tensor', [(i, i + 1) for i in range(step)])]
    ppermute x6, waiting for transfers between devices: 15.9 us -> 38.3 us  [slots_sum(): lax.ppermute(product[o], 'tensor', [(i, (i + o) % count) for i in range(c...]
    all_gather x1, waiting for transfers between devices: 48.8 us -> 29.6 us  [per_device(): x = lax.all_gather(normed, ('section', 'tensor'), axis=0, tiled=False)]
    ppermute x16, waiting for transfers between devices: 23 us -> 36.6 us  [swap(): lax.ppermute(value, axis, [(i, i ^ distance) for i in range(lax.axis_size...]
    ppermute x6, starting transfers between devices: 8.2 us -> 17.1 us  [slots_sum(): lax.ppermute(product[o], 'tensor', [(i, (i + o) % count) for i in range(c...]
  transfers between devices with their start and end apart: 44 -> 42, of which waited for: 23 -> 24; matrix products, arithmetic and copies ran while one was open for 9% -> 7% of each run, Pallas kernels for 6% -> 12%
where the time goes in v9:
time: 381 us; the launch traced here: 376 us
  waiting for transfers between devices  213 us (56%)
  starting transfers between devices  55 us (14%)
  Pallas kernels  53 us (14%)
  other arithmetic  24.7 us (6%)
  between operations  15.2 us (4%)
  local copies, waits for them, and re-layouts  10.7 us (3%)
  matrix products  4.67 us (1%)
    ppermute x3, waiting for transfers between devices, sum_step(): above = lax.ppermute(sends[0], 'tensor', [(i, i + 1) for i in range(step)])  47.7 us
    pallas_call x2, Pallas kernels, ffn(): pl.pallas_call(functools.partial(ffn_kernel, ins), grid_spec=pltpu.Prefet...  45.7 us
    all_gather x1, waiting for transfers between devices, per_device(): share = lax.all_gather(share, 'tensor', axis=0, tiled=False)  39.4 us
    ppermute x6, waiting for transfers between devices, slots_sum(): lax.ppermute(product[o], 'tensor', [(i, (i + o) % count) for i in range(c...  38.3 us
    ppermute x16, waiting for transfers between devices, swap(): lax.ppermute(value, axis, [(i, i ^ distance) for i in range(lax.axis_size...  36.6 us
    all_gather x1, waiting for transfers between devices, per_device(): x = lax.all_gather(normed, ('section', 'tensor'), axis=0, tiled=False)  29.6 us
    ppermute x6, starting transfers between devices, slots_sum(): lax.ppermute(product[o], 'tensor', [(i, (i + o) % count) for i in range(c...  17.1 us
    ppermute x9, starting transfers between devices, from_slots(): lax.ppermute(value, 'tensor', [(i, (i - o) % count) for i in range(count)])  15.1 us
  transfers between devices with their start and end apart: 42, of which 24 were waited for; matrix products, arithmetic and copies ran while one was open for 7% of the time, Pallas kernels for 12%

profile of v9, /device:TPU:0, one launch (start us, length us, event | category | flops | bytes accessed | tf_op | source)
XLA Modules:
  0.0 376.0 jit_solution(11209324246102331453)
XLA Ops:
  7.2 1.6 fusion.3
  8.9 2.5 fusion.5
  12.3 0.9 collective-permute-done
  13.2 3.0 collective-permute-start.3
  16.2 2.6 collective-permute-start.2
  18.8 1.3 collective-permute-start.1
  20.2 2.5 collective-permute-done.3
  22.6 8.8 %collective-permute-done.2 = bf16[32,2048]{1,0:T(8,128)(2,1)S(1)} collective-permute-done((bf16[32,2048]{1,0:T(8,128)(2,1)S(1)}, bf16[32,2048]{1,0:T(8,128)(2,1)S(1)}, u32[]{:S(2)}, u32[]{:S(2)}) %collective-permute-start.2) | collective-permute-done | bytes 131104 | tf_op jit(solution)/shard_map/ppermute | solution.py:36
  31.5 1.5 convolution_bitcast_fusion
  34.0 1.5 collective-permute-done.4
  36.3 12.9 %collective-permute-start.7 = (bf16[32,2048]{1,0:T(8,128)(2,1)S(1)}, bf16[32,2048]{1,0:T(8,128)(2,1)S(1)}, u32[]{:S(2)}, u32[]{:S(2)}) collective-permute-start(bf16[32,2048]{1,0:T(8,128)(2,1)S(1)} %get-tuple-element.84), channel_id=1, source_target_pairs={{0,3},{1,0},{2,1},{3,2},{4,7},{5,4},{6,5},{7,6},{8,11},{9,8},{10,9... | collective-permute-start | bytes 393224 | tf_op jit(solution)/shard_map/ppermute | solution.py:69
  49.8 1.9 copy.43
  51.8 6.0 %collective-permute-done.7 = bf16[32,2048]{1,0:T(8,128)(2,1)S(1)} collective-permute-done((bf16[32,2048]{1,0:T(8,128)(2,1)S(1)}, bf16[32,2048]{1,0:T(8,128)(2,1)S(1)}, u32[]{:S(2)}, u32[]{:S(2)}) %collective-permute-start.7) | collective-permute-done | bytes 131104 | tf_op jit(solution)/shard_map/ppermute | solution.py:69
  57.8 20.9 %collective-permute-done.6 = bf16[32,2048]{1,0:T(8,128)(2,1)S(1)} collective-permute-done((bf16[32,2048]{1,0:T(8,128)(2,1)S(1)}, bf16[32,2048]{1,0:T(8,128)(2,1)S(1)}, u32[]{:S(2)}, u32[]{:S(2)}) %collective-permute-start.6) | collective-permute-done | bytes 131104 | tf_op jit(solution)/shard_map/ppermute | solution.py:69
  78.7 1.0 convert_add_fusion.7
  79.8 1.3 collective-permute-done.8
  81.4 29.6 %all-gather.5.cloned.1.call-done = bf16[1024,4096]{1,0:T(8,128)(2,1)} async-done(((bf16[128,4096]{1,0:T(8,128)(2,1)}), bf16[1024,4096]{1,0:T(8,128)(2,1)}) %all-gather.5.cloned.1.call-update) | async-done | bytes 8388624 | tf_op jit(solution)/shard_map/all_gather | solution.py:274
  111.3 1.0 collective-permute-done.10
  112.4 2.2 collective-permute-start.12
  114.7 1.7 collective-permute-start.11
  116.5 23.6 %ffn.2 = bf16[512,4096]{1,0:T(8,128)(2,1)} custom-call(s32[5]{0:T(128)S(1)} %get-tuple-element.99.order, bf16[2,4,128,4096]{3,2,1,0:T(8,128)(2,1)} %bitcast.80, bf16[4096,1024]{1,0:T(8,128)(2,1)} %gate_ref.3, bf16[4096,1024]{1,0:T(8,128)(2,1)} %up_ref.3, bf16[1024,4096]{1,0:T(8,128)(2,1)} %down_ref.3), custom_call_target="tpu_custom_call" | custom-call | flops 1024 | bytes 1024 | tf_op jit(solution)/shard_map/ffn/pallas_call | solution.py:141
  140.2 0.8 dynamic-slice_bitcast_fusion
  141.0 1.5 fusion.60
  143.1 4.4 %collective-permute-done.14 = f32[128,256]{1,0:T(8,128)S(1)} collective-permute-done((f32[128,256]{1,0:T(8,128)S(1)}, f32[128,256]{1,0:T(8,128)S(1)}, u32[]{:S(2)}, u32[]{:S(2)}) %collective-permute-start.14) | collective-permute-done | bytes 131104 | tf_op jit(solution)/shard_map/ppermute | solution.py:30
  147.6 39.4 %all-gather.7.cloned.1.call-done = bf16[8,512,256]{2,1,0:T(8,128)(2,1)} async-done(((bf16[2,512,256]{2,1,0:T(8,128)(2,1)}), bf16[8,512,256]{2,1,0:T(8,128)(2,1)}) %all-gather.7.cloned.1.call-update) | async-done | bytes 2097168 | tf_op jit(solution)/shard_map/all_gather | solution.py:302
  186.9 2.0 fusion.9.refs_2_
  189.0 1.7 collective-permute-start.16
  190.7 2.4 collective-permute-start.15
  193.1 22.2 %ffn.3 = bf16[512,4096]{1,0:T(8,128)(2,1)S(1)} custom-call(s32[5]{0:T(128)S(1)} %get-tuple-element.98.order, bf16[2,4,128,4096]{3,2,1,0:T(8,128)(2,1)} %bitcast.81, bf16[4096,1024]{1,0:T(8,128)(2,1)} %gate_ref.3, bf16[4096,1024]{1,0:T(8,128)(2,1)} %up_ref.3, bf16[1024,4096]{1,0:T(8,128)(2,1)} %down_ref.3), custom_call_target="tpu_custom_call" | custom-call | flops 1024 | bytes 1024 | tf_op jit(solution)/shard_map/ffn/pallas_call | solution.py:141
  215.4 3.7 fusion.7
  219.2 2.4 collective-permute-start.19
  221.6 0.7 collective-permute-start.20
  222.3 1.5 collective-permute-start.21
  223.9 1.5 collective-permute-start.22
  225.3 18.0 %collective-permute-done.19 = bf16[128,4096]{1,0:T(8,128)(2,1)S(1)} collective-permute-done((bf16[128,4096]{1,0:T(8,128)(2,1)S(1)}, bf16[128,4096]{1,0:T(8,128)(2,1)S(1)}, u32[]{:S(2)}, u32[]{:S(2)}) %collective-permute-start.19) | collective-permute-done | bytes 1048608 | tf_op jit(solution)/shard_map/ppermute | solution.py:59
  243.4 2.0 add_convert_fusion.2
  245.4 12.3 %collective-permute-done.21.refs_3_ = bf16[3,2,512,256]{3,2,1,0:T(8,128)(2,1)S(1)} collective-permute-done((bf16[3,2,512,256]{3,2,1,0:T(8,128)(2,1)S(1)}, bf16[3,2,512,256]{3,2,1,0:T(8,128)(2,1)S(1)}, u32[]{:S(2)}, u32[]{:S(2)}) %collective-permute-start.21) | collective-permute-done | bytes 1572896 | tf_op jit(solution)/shard_map/ppermute | solution.py:30
  257.7 1.2 collective-permute-done.22.refs_4_
  258.9 1.6 collective-permute-start.23
  260.5 1.0 collective-permute-start.24
  261.4 1.5 collective-permute-start.25
  263.0 18.0 %collective-permute-done.23 = bf16[128,4096]{1,0:T(8,128)(2,1)S(1)} collective-permute-done((bf16[128,4096]{1,0:T(8,128)(2,1)S(1)}, bf16[128,4096]{1,0:T(8,128)(2,1)S(1)}, u32[]{:S(2)}, u32[]{:S(2)}) %collective-permute-start.23) | collective-permute-done | bytes 1048608 | tf_op jit(solution)/shard_map/ppermute | solution.py:59
  281.0 4.0 %add_convert_fusion = (bf16[128,4096]{1,0:T(8,128)(2,1)}, bf16[128,4096]{1,0:T(8,128)(2,1)}) fusion(bf16[128,4096]{1,0:T(8,128)(2,1)S(1)} %collective-permute-done.24, bf16[512,4096]{1,0:T(8,128)(2,1)} %collective-permute-done.18, bf16[512,4096]{1,0:T(8,128)(2,1)S(1)} %ffn.3, bf16[128,4096]{1,0:T(8,128)(2,1)S(1)} %collective-permute-done.23), kind=kLoop, calls=%fused_computation.16 | loop fusion | flops 6291456 | bytes 8388608 | tf_op jit(solution)/shard_map/convert_element_type | solution.py:54
  285.1 11.4 %collective-permute-done.25.refs_5_ = bf16[3,2,512,256]{3,2,1,0:T(8,128)(2,1)S(1)} collective-permute-done((bf16[3,2,512,256]{3,2,1,0:T(8,128)(2,1)S(1)}, bf16[3,2,512,256]{3,2,1,0:T(8,128)(2,1)S(1)}, u32[]{:S(2)}, u32[]{:S(2)}) %collective-permute-start.25) | collective-permute-done | bytes 1572896 | tf_op jit(solution)/shard_map/ppermute | solution.py:30
  296.5 1.2 copy-done.7
  297.7 4.9 %collective-permute-start.26 = (bf16[128,4096]{1,0:T(8,128)(2,1)}, bf16[128,4096]{1,0:T(8,128)(2,1)}, u32[]{:S(2)}, u32[]{:S(2)}) collective-permute-start(bf16[128,4096]{1,0:T(8,128)(2,1)} %get-tuple-element.42), channel_id=1, source_target_pairs={{0,1},{1,2},{2,3},{4,5},{5,6},{6,7},{8,9},{9,10},{10,11},{12,13},{... | collective-permute-start | bytes 3145736 | tf_op jit(solution)/shard_map/ppermute | solution.py:59
  302.5 1.3 collective-permute-start.27
  303.8 1.6 shift_right_arithmetic.40
  305.5 3.0 copy.34
  309.4 11.6 %collective-permute-done.26 = bf16[128,4096]{1,0:T(8,128)(2,1)} collective-permute-done((bf16[128,4096]{1,0:T(8,128)(2,1)}, bf16[128,4096]{1,0:T(8,128)(2,1)}, u32[]{:S(2)}, u32[]{:S(2)}) %collective-permute-start.26) | collective-permute-done | bytes 1048608 | tf_op jit(solution)/shard_map/ppermute | solution.py:59
  321.0 5.1 %collective-permute-done.27 = bf16[128,4096]{1,0:T(8,128)(2,1)} collective-permute-done((bf16[128,4096]{1,0:T(8,128)(2,1)}, bf16[128,4096]{1,0:T(8,128)(2,1)}, u32[]{:S(2)}, u32[]{:S(2)}) %collective-permute-start.27) | collective-permute-done | bytes 1048608 | tf_op jit(solution)/shard_map/ppermute | solution.py:60
  326.1 4.2 %fusion = (f32[128]{0:T(128)S(1)}, bf16[128,4096]{1,0:T(8,128)(2,1)S(1)}) fusion(bf16[128,4096]{1,0:T(8,128)(2,1)} %collective-permute-done.27, bf16[128,4096]{1,0:T(8,128)(2,1)} %collective-permute-done.26, bf16[512,4096]{1,0:T(8,128)(2,1)} %collective-permute-done.18, bf16[512,4096]{1,0:T(8,128)(2,1)} %copy-done.2, s32[128,4096]{1,0:T(8,128)} %bitcast.85, ...), kind=kLoop, calls=%fused_computation.9 | loop fusion | flops 9437056 | bytes 8405504 | tf_op jit(solution)/shard_map/reduce_sum | solution.py:18
  330.8 1.4 copy-done.4
  332.1 7.2 %attend_own_keys.1 = bf16[4,128,384]{2,1,0:T(8,128)(2,1)S(1)} custom-call(s32[16]{0:T(128)S(1)} %pad_add_fusion.3.table, bf16[128,4096]{1,0:T(8,128)(2,1)S(1)} %fusion.2.mem_ref, bf16[4,128,256]{2,1,0:T(8,128)(2,1)S(1)} %pad_maximum_fusion.3.cq_ref, bf16[2,2048,256]{2,1,0:T(8,128)(2,1)} %bitcast.83, bf16[2,2048,256]{2,1,0:T(8,128)(2,1)} %collective-permute-done.9.refs_1_, ...), custom_call_target="tpu_custom_call" | custom-call | flops 1024 | bytes 1024 | tf_op jit(solution)/shard_map/attend_own_keys/pallas_call | solution.py:219
  339.4 1.1 collective-permute-start.32
  340.6 2.7 collective-permute-start.34
  343.3 2.7 collective-permute-done.32
  346.1 1.9 collective-permute-done.33
  349.2 1.5 collective-permute-done.35
  351.4 3.0 collective-permute-start.38
  355.0 3.3 collective-permute-done.38
  358.3 8.1 %collective-permute-done.37 = bf16[32,2048]{1,0:T(8,128)(2,1)S(1)} collective-permute-done((bf16[32,2048]{1,0:T(8,128)(2,1)S(1)}, bf16[32,2048]{1,0:T(8,128)(2,1)S(1)}, u32[]{:S(2)}, u32[]{:S(2)}) %collective-permute-start.37) | collective-permute-done | bytes 131104 | tf_op jit(solution)/shard_map/ppermute | solution.py:69
  366.9 1.1 collective-permute-done.39
  368.0 0.7 fusion.18
  (140 shorter events, 9.2 us)
Async XLA Ops:
  7.2 28.6 %copy-start = (bf16[256,2048]{1,0:T(8,128)(2,1)S(1)}, bf16[256,2048]{1,0:T(8,128)(2,1)}, u32[]{:S(2)}) copy-start(bf16[256,2048]{1,0:T(8,128)(2,1)} %param.28) | copy-start | bytes 3145732
  7.2 4.3 %copy-start.13 = (bf16[16,4096]{1,0:T(8,128)(2,1)S(1)}, bf16[16,4096]{1,0:T(8,128)(2,1)}, u32[]{:S(2)}) copy-start(bf16[16,4096]{1,0:T(8,128)(2,1)} %param.25) | copy-start | bytes 393220
  7.2 4.4 %copy-start.17 = (f32[4096]{0:T(1024)S(1)}, f32[4096]{0:T(1024)}, u32[]{:S(2)}) copy-start(f32[4096]{0:T(1024)} %param.26) | copy-start | bytes 49156
  7.2 103.8 %all-gather.5.cloned.1.call-start = ((), (), s32[]{:S(2)}) async-start(), calls=%async_computation | async-start | bytes 9437184 | tf_op jit(solution)/shard_map/all_gather | solution.py:274
  11.4 175.5 %all-gather.7.cloned.1.call-start = ((), (), s32[]{:S(2)}) async-start(), calls=%async_computation.1 | async-start | bytes 2621440 | tf_op jit(solution)/shard_map/all_gather | solution.py:302
  11.8 1.4 collective-permute-start
  13.2 9.4 %collective-permute-start.3 = (bf16[32,2048]{1,0:T(8,128)(2,1)S(1)}, bf16[32,2048]{1,0:T(8,128)(2,1)S(1)}, u32[]{:S(2)}, u32[]{:S(2)}) collective-permute-start(bf16[32,2048]{1,0:T(8,128)(2,1)S(1)} %maximum_select_fusion.2), channel_id=1, source_target_pairs={{0,1},{1,2},{2,3},{3,0},{4,5},{5,6},{6,7},{7,4},{8,9},{9,10},{10,1... | collective-permute-start | bytes 393224 | tf_op jit(solution)/shard_map/ppermute | solution.py:36
  16.2 15.3 %collective-permute-start.2 = (bf16[32,2048]{1,0:T(8,128)(2,1)S(1)}, bf16[32,2048]{1,0:T(8,128)(2,1)S(1)}, u32[]{:S(2)}, u32[]{:S(2)}) collective-permute-start(bf16[32,2048]{1,0:T(8,128)(2,1)S(1)} %maximum_select_fusion.2), channel_id=1, source_target_pairs={{0,2},{1,3},{2,0},{3,1},{4,6},{5,7},{6,4},{7,5},{8,10},{9,11},{10,... | collective-permute-start | bytes 393224 | tf_op jit(solution)/shard_map/ppermute | solution.py:36
  18.8 12.7 %collective-permute-start.1 = (bf16[32,2048]{1,0:T(8,128)(2,1)S(1)}, bf16[32,2048]{1,0:T(8,128)(2,1)S(1)}, u32[]{:S(2)}, u32[]{:S(2)}) collective-permute-start(bf16[32,2048]{1,0:T(8,128)(2,1)S(1)} %maximum_select_fusion.2), channel_id=1, source_target_pairs={{0,3},{1,0},{2,1},{3,2},{4,7},{5,4},{6,5},{7,6},{8,11},{9,8},{10,9... | collective-permute-start | bytes 393224 | tf_op jit(solution)/shard_map/ppermute | solution.py:36
  20.1 12.9 %copy-start.19 = (bf16[2048,3,256]{2,0,1:T(8,128)(2,1)S(1)}, bf16[2048,3,256]{2,0,1:T(8,128)(2,1)}, u32[]{:S(2)}) copy-start(bf16[2048,3,256]{2,0,1:T(8,128)(2,1)} %param.27) | copy-start | bytes 9437188
  33.7 1.8 collective-permute-start.4
  36.2 13.2 %copy-start.12 = (bf16[128,2048]{1,0:T(8,128)(2,1)}, bf16[128,2048]{1,0:T(8,128)(2,1)S(1)}, u32[]{:S(2)}) copy-start(bf16[128,2048]{1,0:T(8,128)(2,1)S(1)} %convolution_convert_fusion.1) | copy-start | bytes 1572868
  36.3 21.5 %collective-permute-start.7 = (bf16[32,2048]{1,0:T(8,128)(2,1)S(1)}, bf16[32,2048]{1,0:T(8,128)(2,1)S(1)}, u32[]{:S(2)}, u32[]{:S(2)}) collective-permute-start(bf16[32,2048]{1,0:T(8,128)(2,1)S(1)} %get-tuple-element.84), channel_id=1, source_target_pairs={{0,3},{1,0},{2,1},{3,2},{4,7},{5,4},{6,5},{7,6},{8,11},{9,8},{10,9... | collective-permute-start | bytes 393224 | tf_op jit(solution)/shard_map/ppermute | solution.py:69
  49.2 29.5 %collective-permute-start.6 = (bf16[32,2048]{1,0:T(8,128)(2,1)S(1)}, bf16[32,2048]{1,0:T(8,128)(2,1)S(1)}, u32[]{:S(2)}, u32[]{:S(2)}) collective-permute-start(bf16[32,2048]{1,0:T(8,128)(2,1)S(1)} %get-tuple-element.85), channel_id=1, source_target_pairs={{0,2},{1,3},{2,0},{3,1},{4,6},{5,7},{6,4},{7,5},{8,10},{9,11},{10,... | collective-permute-start | bytes 393224 | tf_op jit(solution)/shard_map/ppermute | solution.py:69
  49.5 31.8 %copy-start.18 = (f32[4096]{0:T(1024)S(1)}, f32[4096]{0:T(1024)}, u32[]{:S(2)}) copy-start(f32[4096]{0:T(1024)} %param.29) | copy-start | bytes 49156
  49.5 29.2 %collective-permute-start.5 = (bf16[32,2048]{1,0:T(8,128)(2,1)S(1)}, bf16[32,2048]{1,0:T(8,128)(2,1)S(1)}, u32[]{:S(2)}, u32[]{:S(2)}) collective-permute-start(bf16[32,2048]{1,0:T(8,128)(2,1)S(1)} %get-tuple-element.83), channel_id=1, source_target_pairs={{0,1},{1,2},{2,3},{3,0},{4,5},{5,6},{6,7},{7,4},{8,9},{9,10},{10,1... | collective-permute-start | bytes 393224 | tf_op jit(solution)/shard_map/ppermute | solution.py:69
  51.7 88.5 %copy-start.9 = (bf16[2048,2,256]{2,0,1:T(8,128)(2,1)}, bf16[2048,2,256]{2,0,1:T(8,128)(2,1)S(1)}, u32[]{:S(2)}) copy-start(bf16[2048,2,256]{2,0,1:T(8,128)(2,1)S(1)} %copy.43) | copy-start | bytes 6291460
  51.7 29.7 %collective-permute-start.9 = (bf16[2,2048,256]{2,1,0:T(8,128)(2,1)S(1)}, bf16[2,2048,256]{2,1,0:T(8,128)(2,1)}, u32[]{:S(2)}, u32[]{:S(2)}) collective-permute-start(bf16[2,2048,256]{2,1,0:T(8,128)(2,1)S(1)} %bitcast.82), channel_id=1, source_target_pairs={{0,4},{4,0},{1,5},{5,1},{2,6},{6,2},{3,7},{7,3},{8,12},{12,8},{9,1... | collective-permute-start | bytes 6291464 | tf_op jit(solution)/shard_map/ppermute | solution.py:30
  79.7 1.4 collective-permute-start.8
  111.0 1.3 collective-permute-start.10
  112.4 27.7 %collective-permute-start.13 = (bf16[32,2048]{1,0:T(8,128)(2,1)S(1)}, bf16[32,2048]{1,0:T(8,128)(2,1)S(1)}, u32[]{:S(2)}, u32[]{:S(2)}) collective-permute-start(bf16[32,2048]{1,0:T(8,128)(2,1)S(1)} %maximum_select_fusion.3), channel_id=1, source_target_pairs={{0,1},{1,2},{2,3},{3,0},{4,5},{5,6},{6,7},{7,4},{8,9},{9,10},{10,1... | collective-permute-start | bytes 393224 | tf_op jit(solution)/shard_map/ppermute | solution.py:36
  112.4 27.6 %collective-permute-start.12 = (bf16[32,2048]{1,0:T(8,128)(2,1)S(1)}, bf16[32,2048]{1,0:T(8,128)(2,1)S(1)}, u32[]{:S(2)}, u32[]{:S(2)}) collective-permute-start(bf16[32,2048]{1,0:T(8,128)(2,1)S(1)} %maximum_select_fusion.3), channel_id=1, source_target_pairs={{0,2},{1,3},{2,0},{3,1},{4,6},{5,7},{6,4},{7,5},{8,10},{9,11},{10,... | collective-permute-start | bytes 393224 | tf_op jit(solution)/shard_map/ppermute | solution.py:36
  114.7 25.4 %collective-permute-start.11 = (bf16[32,2048]{1,0:T(8,128)(2,1)S(1)}, bf16[32,2048]{1,0:T(8,128)(2,1)S(1)}, u32[]{:S(2)}, u32[]{:S(2)}) collective-permute-start(bf16[32,2048]{1,0:T(8,128)(2,1)S(1)} %maximum_select_fusion.3), channel_id=1, source_target_pairs={{0,3},{1,0},{2,1},{3,2},{4,7},{5,4},{6,5},{7,6},{8,11},{9,8},{10,9... | collective-permute-start | bytes 393224 | tf_op jit(solution)/shard_map/ppermute | solution.py:36
  140.1 75.3 %collective-permute-start.18 = (bf16[512,4096]{1,0:T(8,128)(2,1)}, bf16[512,4096]{1,0:T(8,128)(2,1)}, u32[]{:S(2)}, u32[]{:S(2)}) collective-permute-start(bf16[512,4096]{1,0:T(8,128)(2,1)} %ffn.2), channel_id=1, source_target_pairs={{0,4},{4,0},{1,5},{5,1},{2,6},{6,2},{3,7},{7,3},{8,12},{12,8},{9,1... | collective-permute-start | bytes 12582920 | tf_op jit(solution)/shard_map/ppermute | solution.py:30
  142.6 4.9 %collective-permute-start.14 = (f32[128,256]{1,0:T(8,128)S(1)}, f32[128,256]{1,0:T(8,128)S(1)}, u32[]{:S(2)}, u32[]{:S(2)}) collective-permute-start(f32[128,256]{1,0:T(8,128)S(1)} %fusion.60), channel_id=1, source_target_pairs={{0,4},{4,0},{1,5},{5,1},{2,6},{6,2},{3,7},{7,3},{8,12},{12,8},{9,1... | collective-permute-start | bytes 393224 | tf_op jit(solution)/shard_map/ppermute | solution.py:30
  188.9 26.4 %collective-permute-start.17 = (bf16[128,256]{1,0:T(8,128)(2,1)S(1)}, bf16[128,256]{1,0:T(8,128)(2,1)S(1)}, u32[]{:S(2)}, u32[]{:S(2)}) collective-permute-start(bf16[128,256]{1,0:T(8,128)(2,1)S(1)} %bitcast.93), channel_id=1, source_target_pairs={{0,1},{1,2},{2,3},{3,0},{4,5},{5,6},{6,7},{7,4},{8,9},{9,10},{10,1... | collective-permute-start | bytes 196616 | tf_op jit(solution)/shard_map/ppermute | solution.py:36
  189.0 26.4 %collective-permute-start.16 = (bf16[128,256]{1,0:T(8,128)(2,1)S(1)}, bf16[128,256]{1,0:T(8,128)(2,1)S(1)}, u32[]{:S(2)}, u32[]{:S(2)}) collective-permute-start(bf16[128,256]{1,0:T(8,128)(2,1)S(1)} %bitcast.94), channel_id=1, source_target_pairs={{0,2},{1,3},{2,0},{3,1},{4,6},{5,7},{6,4},{7,5},{8,10},{9,11},{10,... | collective-permute-start | bytes 196616 | tf_op jit(solution)/shard_map/ppermute | solution.py:36
  190.7 24.7 %collective-permute-start.15 = (bf16[128,256]{1,0:T(8,128)(2,1)S(1)}, bf16[128,256]{1,0:T(8,128)(2,1)S(1)}, u32[]{:S(2)}, u32[]{:S(2)}) collective-permute-start(bf16[128,256]{1,0:T(8,128)(2,1)S(1)} %bitcast.95), channel_id=1, source_target_pairs={{0,3},{1,0},{2,1},{3,2},{4,7},{5,4},{6,5},{7,6},{8,11},{9,8},{10,9... | collective-permute-start | bytes 196616 | tf_op jit(solution)/shard_map/ppermute | solution.py:36
  215.3 65.7 %copy-start.2 = (bf16[512,4096]{1,0:T(8,128)(2,1)}, bf16[512,4096]{1,0:T(8,128)(2,1)S(1)}, u32[]{:S(2)}) copy-start(bf16[512,4096]{1,0:T(8,128)(2,1)S(1)} %ffn.3) | copy-start | bytes 12582916
  219.2 24.2 %collective-permute-start.19 = (bf16[128,4096]{1,0:T(8,128)(2,1)S(1)}, bf16[128,4096]{1,0:T(8,128)(2,1)S(1)}, u32[]{:S(2)}, u32[]{:S(2)}) collective-permute-start(bf16[128,4096]{1,0:T(8,128)(2,1)S(1)} %get-tuple-element.77), channel_id=1, source_target_pairs={{0,1},{4,5},{8,9},{12,13},{16,17},{20,21},{24,25},{28,29}} | collective-permute-start | bytes 3145736 | tf_op jit(solution)/shard_map/ppermute | solution.py:59
  221.6 21.8 %collective-permute-start.20 = (bf16[128,4096]{1,0:T(8,128)(2,1)S(1)}, bf16[128,4096]{1,0:T(8,128)(2,1)S(1)}, u32[]{:S(2)}, u32[]{:S(2)}) collective-permute-start(bf16[128,4096]{1,0:T(8,128)(2,1)S(1)} %get-tuple-element.76), channel_id=1, source_target_pairs={{3,2},{7,6},{11,10},{15,14},{19,18},{23,22},{27,26},{31,30}} | collective-permute-start | bytes 3145736 | tf_op jit(solution)/shard_map/ppermute | solution.py:60
  222.3 35.4 %collective-permute-start.21 = (bf16[3,2,512,256]{3,2,1,0:T(8,128)(2,1)S(1)}, bf16[3,2,512,256]{3,2,1,0:T(8,128)(2,1)S(1)}, u32[]{:S(2)}, u32[]{:S(2)}) collective-permute-start(bf16[3,2,512,256]{3,2,1,0:T(8,128)(2,1)S(1)} %fusion.9.refs_2_), channel_id=1, source_target_pairs={{0,8},{8,0},{16,24},{24,16},{1,9},{9,1},{17,25},{25,17},{2,10},{10... | collective-permute-start | bytes 4718600 | tf_op jit(solution)/shard_map/ppermute | solution.py:30
  223.9 35.0 %collective-permute-start.22 = (bf16[3,2,512,256]{3,2,1,0:T(8,128)(2,1)S(1)}, bf16[3,2,512,256]{3,2,1,0:T(8,128)(2,1)S(1)}, u32[]{:S(2)}, u32[]{:S(2)}) collective-permute-start(bf16[3,2,512,256]{3,2,1,0:T(8,128)(2,1)S(1)} %fusion.9.refs_2_), channel_id=1, source_target_pairs={{0,16},{8,24},{16,0},{24,8},{1,17},{9,25},{17,1},{25,9},{2,18},{10... | collective-permute-start | bytes 4718600 | tf_op jit(solution)/shard_map/ppermute | solution.py:30
  257.7 27.4 %copy-start.3 = (bf16[3,2,512,256]{3,2,1,0:T(8,128)(2,1)}, bf16[3,2,512,256]{3,2,1,0:T(8,128)(2,1)S(1)}, u32[]{:S(2)}) copy-start(bf16[3,2,512,256]{3,2,1,0:T(8,128)(2,1)S(1)} %collective-permute-done.21.refs_3_) | copy-start | bytes 4718596
  258.9 26.2 %copy-start.5 = (bf16[3,2,512,256]{3,2,1,0:T(8,128)(2,1)}, bf16[3,2,512,256]{3,2,1,0:T(8,128)(2,1)S(1)}, u32[]{:S(2)}) copy-start(bf16[3,2,512,256]{3,2,1,0:T(8,128)(2,1)S(1)} %collective-permute-done.22.refs_4_) | copy-start | bytes 4718596
  258.9 22.1 %collective-permute-start.23 = (bf16[128,4096]{1,0:T(8,128)(2,1)S(1)}, bf16[128,4096]{1,0:T(8,128)(2,1)S(1)}, u32[]{:S(2)}, u32[]{:S(2)}) collective-permute-start(bf16[128,4096]{1,0:T(8,128)(2,1)S(1)} %get-tuple-element.38), channel_id=1, source_target_pairs={{0,1},{1,2},{4,5},{5,6},{8,9},{9,10},{12,13},{13,14},{16,17},{17,1... | collective-permute-start | bytes 3145736 | tf_op jit(solution)/shard_map/ppermute | solution.py:59
  260.5 20.6 %collective-permute-start.24 = (bf16[128,4096]{1,0:T(8,128)(2,1)S(1)}, bf16[128,4096]{1,0:T(8,128)(2,1)S(1)}, u32[]{:S(2)}, u32[]{:S(2)}) collective-permute-start(bf16[128,4096]{1,0:T(8,128)(2,1)S(1)} %get-tuple-element.39), channel_id=1, source_target_pairs={{2,1},{3,2},{6,5},{7,6},{10,9},{11,10},{14,13},{15,14},{18,17},{19... | collective-permute-start | bytes 3145736 | tf_op jit(solution)/shard_map/ppermute | solution.py:60
  261.4 35.1 %collective-permute-start.25 = (bf16[3,2,512,256]{3,2,1,0:T(8,128)(2,1)S(1)}, bf16[3,2,512,256]{3,2,1,0:T(8,128)(2,1)S(1)}, u32[]{:S(2)}, u32[]{:S(2)}) collective-permute-start(bf16[3,2,512,256]{3,2,1,0:T(8,128)(2,1)S(1)} %fusion.9.refs_2_), channel_id=1, source_target_pairs={{0,24},{8,16},{16,8},{24,0},{1,25},{9,17},{17,9},{25,1},{2,26},{10... | collective-permute-start | bytes 4718600 | tf_op jit(solution)/shard_map/ppermute | solution.py:30
  296.5 1.2 copy-start.7
  297.7 23.3 %collective-permute-start.26 = (bf16[128,4096]{1,0:T(8,128)(2,1)}, bf16[128,4096]{1,0:T(8,128)(2,1)}, u32[]{:S(2)}, u32[]{:S(2)}) collective-permute-start(bf16[128,4096]{1,0:T(8,128)(2,1)} %get-tuple-element.42), channel_id=1, source_target_pairs={{0,1},{1,2},{2,3},{4,5},{5,6},{6,7},{8,9},{9,10},{10,11},{12,13},{... | collective-permute-start | bytes 3145736 | tf_op jit(solution)/shard_map/ppermute | solution.py:59
  302.5 23.6 %collective-permute-start.27 = (bf16[128,4096]{1,0:T(8,128)(2,1)}, bf16[128,4096]{1,0:T(8,128)(2,1)}, u32[]{:S(2)}, u32[]{:S(2)}) collective-permute-start(bf16[128,4096]{1,0:T(8,128)(2,1)} %get-tuple-element.43), channel_id=1, source_target_pairs={{1,0},{2,1},{3,2},{5,4},{6,5},{7,6},{9,8},{10,9},{11,10},{13,12},{... | collective-permute-start | bytes 3145736 | tf_op jit(solution)/shard_map/ppermute | solution.py:60
  305.5 20.6 %copy-start.10 = (bf16[128,4096]{1,0:T(8,128)(2,1)S(1)}, bf16[128,4096]{1,0:T(8,128)(2,1)}, u32[]{:S(2)}) copy-start(bf16[128,4096]{1,0:T(8,128)(2,1)} %param.18) | copy-start | bytes 3145732
  308.8 21.9 %collective-permute-start.28 = (bf16[3,2,512,256]{3,2,1,0:T(8,128)(2,1)S(1)}, bf16[3,2,512,256]{3,2,1,0:T(8,128)(2,1)S(1)}, u32[]{:S(2)}, u32[]{:S(2)}) collective-permute-start(bf16[3,2,512,256]{3,2,1,0:T(8,128)(2,1)S(1)} %fusion.9.refs_2_), channel_id=1, source_target_pairs={{0,4},{4,0},{1,5},{5,1},{2,6},{6,2},{3,7},{7,3},{8,12},{12,8},{9,1... | collective-permute-start | bytes 4718600 | tf_op jit(solution)/shard_map/ppermute | solution.py:30
  308.8 21.9 %collective-permute-start.29 = (bf16[3,2,512,256]{3,2,1,0:T(8,128)(2,1)}, bf16[3,2,512,256]{3,2,1,0:T(8,128)(2,1)S(1)}, u32[]{:S(2)}, u32[]{:S(2)}) collective-permute-start(bf16[3,2,512,256]{3,2,1,0:T(8,128)(2,1)} %copy-done.3), channel_id=1, source_target_pairs={{0,4},{4,0},{1,5},{5,1},{2,6},{6,2},{3,7},{7,3},{8,12},{12,8},{9,1... | collective-permute-start | bytes 4718600 | tf_op jit(solution)/shard_map/ppermute | solution.py:30
  309.3 21.5 %collective-permute-start.30 = (bf16[3,2,512,256]{3,2,1,0:T(8,128)(2,1)}, bf16[3,2,512,256]{3,2,1,0:T(8,128)(2,1)S(1)}, u32[]{:S(2)}, u32[]{:S(2)}) collective-permute-start(bf16[3,2,512,256]{3,2,1,0:T(8,128)(2,1)} %copy-done.5), channel_id=1, source_target_pairs={{0,4},{4,0},{1,5},{5,1},{2,6},{6,2},{3,7},{7,3},{8,12},{12,8},{9,1... | collective-permute-start | bytes 4718600 | tf_op jit(solution)/shard_map/ppermute | solution.py:30
  321.0 9.8 %collective-permute-start.31 = (bf16[3,2,512,256]{3,2,1,0:T(8,128)(2,1)}, bf16[3,2,512,256]{3,2,1,0:T(8,128)(2,1)S(1)}, u32[]{:S(2)}, u32[]{:S(2)}) collective-permute-start(bf16[3,2,512,256]{3,2,1,0:T(8,128)(2,1)} %copy-done.7), channel_id=1, source_target_pairs={{0,4},{4,0},{1,5},{5,1},{2,6},{6,2},{3,7},{7,3},{8,12},{12,8},{9,1... | collective-permute-start | bytes 4718600 | tf_op jit(solution)/shard_map/ppermute | solution.py:30
  326.1 4.3 %copy-start.16 = (f32[4096]{0:T(1024)S(1)}, f32[4096]{0:T(1024)}, u32[]{:S(2)}) copy-start(f32[4096]{0:T(1024)} %param.24) | copy-start | bytes 49156
  326.1 4.6 %copy-start.6 = (bf16[3,2,512,256]{3,2,1,0:T(8,128)(2,1)S(1)}, bf16[3,2,512,256]{3,2,1,0:T(8,128)(2,1)}, u32[]{:S(2)}) copy-start(bf16[3,2,512,256]{3,2,1,0:T(8,128)(2,1)} %copy-done.5) | copy-start | bytes 4718596
  326.1 4.6 %copy-start.8 = (bf16[3,2,512,256]{3,2,1,0:T(8,128)(2,1)S(1)}, bf16[3,2,512,256]{3,2,1,0:T(8,128)(2,1)}, u32[]{:S(2)}) copy-start(bf16[3,2,512,256]{3,2,1,0:T(8,128)(2,1)} %copy-done.7) | copy-start | bytes 4718596
  330.3 9.0 %copy-start.11 = (bf16[128,4096]{1,0:T(8,128)(2,1)}, bf16[128,4096]{1,0:T(8,128)(2,1)S(1)}, u32[]{:S(2)}) copy-start(bf16[128,4096]{1,0:T(8,128)(2,1)S(1)} %get-tuple-element.67) | copy-start | bytes 3145732
  330.3 1.8 copy-start.4
  339.4 6.6 %collective-permute-start.32 = (bf16[128,384]{1,0:T(8,128)(2,1)S(1)}, bf16[128,384]{1,0:T(8,128)(2,1)S(1)}, u32[]{:S(2)}, u32[]{:S(2)}) collective-permute-start(bf16[128,384]{1,0:T(8,128)(2,1)S(1)} %get-tuple-element.89), channel_id=1, source_target_pairs={{0,1},{1,2},{2,3},{3,0},{4,5},{5,6},{6,7},{7,4},{8,9},{9,10},{10,1... | collective-permute-start | bytes 294920 | tf_op jit(solution)/shard_map/ppermute | solution.py:341
  340.6 7.4 %collective-permute-start.33 = (bf16[128,384]{1,0:T(8,128)(2,1)S(1)}, bf16[128,384]{1,0:T(8,128)(2,1)S(1)}, u32[]{:S(2)}, u32[]{:S(2)}) collective-permute-start(bf16[128,384]{1,0:T(8,128)(2,1)S(1)} %get-tuple-element.88), channel_id=1, source_target_pairs={{0,2},{1,3},{2,0},{3,1},{4,6},{5,7},{6,4},{7,5},{8,10},{9,11},{10,... | collective-permute-start | bytes 294920 | tf_op jit(solution)/shard_map/ppermute | solution.py:341
  340.6 7.5 %collective-permute-start.34 = (bf16[128,384]{1,0:T(8,128)(2,1)S(1)}, bf16[128,384]{1,0:T(8,128)(2,1)S(1)}, u32[]{:S(2)}, u32[]{:S(2)}) collective-permute-start(bf16[128,384]{1,0:T(8,128)(2,1)S(1)} %get-tuple-element.87), channel_id=1, source_target_pairs={{0,3},{1,0},{2,1},{3,2},{4,7},{5,4},{6,5},{7,6},{8,11},{9,8},{10,9... | collective-permute-start | bytes 294920 | tf_op jit(solution)/shard_map/ppermute | solution.py:341
  348.1 3.0 copy-start.14
  349.1 1.6 collective-permute-start.35
  350.8 15.8 %copy-start.15 = (s32[16,1024]{1,0:T(8,128)S(1)}, s32[16,1024]{1,0:T(8,128)}, u32[]{:S(2)}) copy-start(s32[16,1024]{1,0:T(8,128)} %param.33) | copy-start | bytes 196612
  351.0 17.7 %copy-start.1 = (bf16[256,2048]{1,0:T(8,128)(2,1)S(1)}, bf16[256,2048]{1,0:T(8,128)(2,1)}, u32[]{:S(2)}) copy-start(bf16[256,2048]{1,0:T(8,128)(2,1)} %param.28) | copy-start | bytes 3145732
  351.4 6.9 %collective-permute-start.38 = (bf16[32,2048]{1,0:T(8,128)(2,1)S(1)}, bf16[32,2048]{1,0:T(8,128)(2,1)S(1)}, u32[]{:S(2)}, u32[]{:S(2)}) collective-permute-start(bf16[32,2048]{1,0:T(8,128)(2,1)S(1)} %get-tuple-element.81), channel_id=1, source_target_pairs={{0,3},{1,0},{2,1},{3,2},{4,7},{5,4},{6,5},{7,6},{8,11},{9,8},{10,9... | collective-permute-start | bytes 393224 | tf_op jit(solution)/shard_map/ppermute | solution.py:69
  354.4 12.1 %collective-permute-start.37 = (bf16[32,2048]{1,0:T(8,128)(2,1)S(1)}, bf16[32,2048]{1,0:T(8,128)(2,1)S(1)}, u32[]{:S(2)}, u32[]{:S(2)}) collective-permute-start(bf16[32,2048]{1,0:T(8,128)(2,1)S(1)} %get-tuple-element.82), channel_id=1, source_target_pairs={{0,2},{1,3},{2,0},{3,1},{4,6},{5,7},{6,4},{7,5},{8,10},{9,11},{10,... | collective-permute-start | bytes 393224 | tf_op jit(solution)/shard_map/ppermute | solution.py:69
  354.5 11.9 %collective-permute-start.36 = (bf16[32,2048]{1,0:T(8,128)(2,1)S(1)}, bf16[32,2048]{1,0:T(8,128)(2,1)S(1)}, u32[]{:S(2)}, u32[]{:S(2)}) collective-permute-start(bf16[32,2048]{1,0:T(8,128)(2,1)S(1)} %get-tuple-element.80), channel_id=1, source_target_pairs={{0,1},{1,2},{2,3},{3,0},{4,5},{5,6},{6,7},{7,4},{8,9},{9,10},{10,1... | collective-permute-start | bytes 393224 | tf_op jit(solution)/shard_map/ppermute | solution.py:69
  366.6 1.4 collective-permute-start.39
Sparse Core Ops, SparseCore 0:
  11.5 99.4 all-gather.4
  141.2 45.7 all-gather.6

commit v10 on v9

--- a/solution.py
+++ b/solution.py
@@ -70,6 +70,14 @@
             product[o], "tensor", [(i, (i + o) % count) for i in range(count)]
         ).astype(F32)
     return total
+
+
+def near_bits(axis):
+    bits, bit = [], 1
+    while bit < lax.axis_size(axis):
+        bits.append(bit)
+        bit *= 2
+    return bits
 
 
 def half_columns(value, index):
@@ -159,16 +167,16 @@
             ],
         ),
         out_shape=jax.ShapeDtypeStruct((rows, features), BF16),
-        compiler_params=pltpu.CompilerParams(vmem_limit_bytes=44 * 2**20),
+        compiler_params=pltpu.CompilerParams(vmem_limit_bytes=28 * 2**20),
         cost_estimate=pl.CostEstimate(flops=1024, bytes_accessed=1024, transcendentals=0),
         name="ffn",
     )(order, x, w_gate, w_up, w_down)
 
 
-def attend_kernel(groups, table, mem_ref, cq_ref, *refs):
+def attend_kernel(plan, depth, table, mem_ref, cq_ref, *refs):
     locals_, shares, out_ref = refs[:2], refs[2:-1], refs[-1]
     slot = pl.program_id(0)
-    depth = shares[0].shape[2]
+    groups = len(plan) // 2
 
     def attend(pieces):
         keys = jnp.zeros((mem_ref.shape[0], HD), F32)
@@ -207,17 +215,16 @@
 
     @pl.when(slot > 0)
     def _():
-        attend([(i, ref[0, 0], ref[0, 1]) for i, ref in enumerate(shares)])
-
-
-def attend_own_keys(memory, queries, own_head, shares, table):
+        attend([(i, shares[k][0, a], shares[v][0, b]) for i, (k, a, v, b) in enumerate(plan)])
+
+
+def attend_own_keys(memory, queries, own_head, shares, plan, table):
     rows, features = memory.shape
     heads, count, width = queries.shape
-    _, two, depth, _ = shares[0].shape
-    share = pl.BlockSpec((1, two, depth, width), lambda h, t: (jnp.maximum(h - 1, 0), 0, 0, 0))
+    depth = shares[0].shape[2]
     whole = pl.BlockSpec(own_head[0].shape, lambda h, t: (0, 0, 0), pipeline_mode=pl.Buffered(1))
     return pl.pallas_call(
-        functools.partial(attend_kernel, len(shares) // 2),
+        functools.partial(attend_kernel, plan, depth),
         grid_spec=pltpu.PrefetchScalarGridSpec(
             num_scalar_prefetch=1,
             grid=(heads,),
@@ -227,11 +234,14 @@
                 whole,
                 whole,
             ]
-            + [share] * len(shares),
+            + [
+                pl.BlockSpec((1,) + share.shape[1:], lambda h, t: (jnp.maximum(h - 1, 0), 0, 0, 0))
+                for share in shares
+            ],
             out_specs=pl.BlockSpec((1, count, width + 128), lambda h, t: (h, 0, 0)),
         ),
         out_shape=jax.ShapeDtypeStruct((heads, count, width + 128), BF16),
-        compiler_params=pltpu.CompilerParams(vmem_limit_bytes=40 * 2**20),
+        compiler_params=pltpu.CompilerParams(vmem_limit_bytes=30 * 2**20),
         cost_estimate=pl.CostEstimate(flops=1024, bytes_accessed=1024, transcendentals=0),
         name="attend_own_keys",
     )(table, memory, queries, *own_head, *shares)
@@ -293,39 +303,49 @@
 
     mid = (target.astype(F32) + whole_rows(total, section)).astype(BF16)
     crossin = norm_rows(mid, cross_gain).astype(BF16)
-    x, crossin, other_head = lax.optimization_barrier((x, crossin, own_head[1]))
-    own_head[1] = other_head
     crossin = gather_half(crossin, section)
 
-    depth = cross_kv.shape[0] // groups
-    share = gated(lax.dynamic_slice_in_dim(own_head[0], group * depth, depth, 1), x)
-    share = lax.all_gather(share, "tensor", axis=0, tiled=False)
-    shares = [jnp.roll(share, -tensor, axis=0)[1:]]
-
-    theirs = ffn(x, jnp.concatenate([(1 - section)[None], slot_chip]), w_gate, w_up, w_down)
-    theirs, crossin = lax.optimization_barrier((theirs, crossin))
-    got = swap(theirs, "section", 1)
     cq = both_halves(jnp.dot(crossin, cross_q, preferred_element_type=F32)).astype(BF16)
     cq = jnp.roll(cq.reshape(count, 2, rows, HD), tensor, axis=0)
     cq = jnp.transpose(cq, (1, 0, 2, 3)).reshape(2 * count * rows, HD)
-    x, cq, shares[0] = lax.optimization_barrier((x, cq, shares[0]))
-    queries = jnp.stack(from_slots(cq))
+    x, cq, other_head = lax.optimization_barrier((x, cq, own_head[1]))
+    own_head[1] = other_head
+    heads = [0]
+    for bit in near_bits("tensor")[::-1]:
+        heads += [m ^ bit for m in heads]
+    queries = jnp.stack([cq] + [swap(cq, "tensor", m) for m in heads[1:]])
+
+    depth = cross_kv.shape[0] // groups
+    share = lax.dynamic_slice_in_dim(own_head[0], group * depth, depth, 1)[None]
+    share, x = lax.optimization_barrier((share, x))
+    bits = near_bits("tensor")[::-1]
+    for bit in bits[:-1]:
+        share = jnp.concatenate([share, swap(share, "tensor", bit)], 0)
+
+    theirs = ffn(x, jnp.concatenate([(1 - section)[None], slot_chip]), w_gate, w_up, w_down)
+    theirs, queries, share = lax.optimization_barrier((theirs, queries, share))
+    got = swap(theirs, "section", 1)
+    x = gated(x, share)
+    last = swap(share, "tensor", bits[-1])
     mine = ffn(x, jnp.concatenate([section[None], slot_chip]), w_gate, w_up, w_down)
-    shares += [swap(shares[0], "dp", j) for j in range(1, groups)]
-
-    mine, queries = lax.optimization_barrier((mine, queries))
+    mine, last = lax.optimization_barrier((mine, last))
+    shares = [jnp.concatenate([share[1:], last], 0)]
+
+    far = [j for j in range(1, groups) if groups != 4 or j < 3]
+    shares += [swap(shares[0], "dp", j) for j in far]
+    plan = [(j, 0, j, 1) for j in range(len(shares))]
     came = sum_step(sum_sends(mine, got, None, 1), 1)
     for step in range(2, count):
         sends = sum_sends(mine, got, came, step)
-        if step == 2:
-            near = tuple(shares[1 : 1 + groups // 2])
-            held = lax.optimization_barrier(sends + near)
-            sends, shares[1 : 1 + groups // 2] = held[:2], list(held[2:])
-        elif step == count - 1:
-            rest = tuple(shares[1 + groups // 2 :])
-            held = lax.optimization_barrier(sends + rest)
-            sends, shares[1 + groups // 2 :] = held[:2], list(held[2:])
+        if step == count - 1:
+            held = lax.optimization_barrier(sends + tuple(shares[1:]))
+            sends, shares[1:] = held[:2], list(held[2:])
         came = sum_step(sends, step)
+    if groups == 4:
+        passed = [swap(shares[2][:, :1], "dp", 1), swap(shares[1][:, 1:], "dp", 2)]
+        held = lax.optimization_barrier(came + tuple(passed))
+        came, shares = held[:2], shares + list(held[2:])
+        plan.append((3, 0, 4, 0))
     total = slot_sum(mine, got, 0) + came[0].astype(F32) + came[1].astype(F32)
     enc_out = (source.astype(F32) + keep_factor(enc_keep) * total).astype(BF16)
     memory = norm_rows(enc_out, final_gain).astype(BF16)
@@ -335,10 +355,11 @@
     table = jnp.concatenate(
         [p + at for p in places] + [p + jnp.arange(groups, dtype=jnp.int32) for p in places]
     ).astype(jnp.int32)
+    plan += [(k + len(shares), a, v + len(shares), b) for k, a, v, b in plan]
     shares += [swap(s, "section", 1) for s in shares]
-    parts = attend_own_keys(memory, queries, own_head, shares, table)
+    parts = attend_own_keys(memory, queries, own_head, shares, tuple(plan), table)
     parts = [parts[0]] + [
-        lax.ppermute(parts[o], "tensor", [(i, (i + o) % count) for i in range(count)]) for o in range(1, count)
+        swap(parts[o], "tensor", heads[o]) for o in range(1, count)
     ]
     parts = [p.astype(F32) for p in parts]
     context, top, whole = merged(

time: 381 us -> 335 us (0.88)
  waiting for transfers between devices: 213 us -> 167 us
  local copies, waits for them, and re-layouts: 10.7 us -> 19.8 us
  other arithmetic: 24.7 us -> 17.3 us
  starting transfers between devices: 55 us -> 61.7 us
  Pallas kernels: 53 us -> 46.5 us
    all_gather x1 -> x0, waiting for transfers between devices: 39.4 us -> none  [per_device(): share = lax.all_gather(share, 'tensor', axis=0, tiled=False)]
    ppermute x9 -> x6, waiting for transfers between devices: 11.3 us -> 25.9 us  [from_slots(): lax.ppermute(value, 'tensor', [(i, (i - o) % count) for i in range(count)])]
    all_gather x1, waiting for transfers between devices: 29.6 us -> 16.5 us  [per_device(): x = lax.all_gather(normed, ('section', 'tensor'), axis=0, tiled=False)]
    ppermute x16 -> x26, starting transfers between devices: 6.9 us -> 17.6 us  [swap(): lax.ppermute(value, axis, [(i, i ^ distance) for i in range(lax.axis_size...]
    unnamed x46 -> x58, local copies, waits for them, and re-layouts: 7.76 us -> 16.8 us
    pallas_call x2, Pallas kernels: 45.7 us -> 39.7 us  [ffn(): pl.pallas_call(functools.partial(ffn_kernel, ins), grid_spec=pltpu.Prefet...]
    ppermute x16 -> x26, waiting for transfers between devices: 36.6 us -> 30.7 us  [swap(): lax.ppermute(value, axis, [(i, i ^ distance) for i in range(lax.axis_size...]
    convert_element_type x3, other arithmetic: 9.79 us -> 4.07 us  [sum_sends(): return (up.astype(BF16), down.astype(BF16))]
  transfers between devices with their start and end apart: 42 -> 45, of which waited for: 24 -> 25; matrix products, arithmetic and copies ran while one was open for 7% -> 6% of each run, Pallas kernels for 12% -> 12%
where the time goes in v10:
time: 335 us; the launch traced here: 331 us
  waiting for transfers between devices  167 us (50%)
  starting transfers between devices  61.7 us (18%)
  Pallas kernels  46.5 us (14%)
  local copies, waits for them, and re-layouts  19.8 us (6%)
  other arithmetic  17.3 us (5%)
  between operations  15.2 us (5%)
  matrix products  3.45 us (1%)
    ppermute x3, waiting for transfers between devices, sum_step(): above = lax.ppermute(sends[0], 'tensor', [(i, i + 1) for i in range(step)])  48.4 us
    ppermute x6, waiting for transfers between devices, slots_sum(): lax.ppermute(product[o], 'tensor', [(i, (i + o) % count) for i in range(c...  40.8 us
    pallas_call x2, Pallas kernels, ffn(): pl.pallas_call(functools.partial(ffn_kernel, ins), grid_spec=pltpu.Prefet...  39.7 us
    ppermute x26, waiting for transfers between devices, swap(): lax.ppermute(value, axis, [(i, i ^ distance) for i in range(lax.axis_size...  30.7 us
    ppermute x6, waiting for transfers between devices, from_slots(): lax.ppermute(value, 'tensor', [(i, (i - o) % count) for i in range(count)])  25.9 us
    ppermute x26, starting transfers between devices, swap(): lax.ppermute(value, axis, [(i, i ^ distance) for i in range(lax.axis_size...  17.6 us
    ppermute x6, starting transfers between devices, slots_sum(): lax.ppermute(product[o], 'tensor', [(i, (i + o) % count) for i in range(c...  17 us
    unnamed x58, local copies, waits for them, and re-layouts  16.8 us
  transfers between devices with their start and end apart: 45, of which 25 were waited for; matrix products, arithmetic and copies ran while one was open for 6% of the time, Pallas kernels for 12%

profile of v10, /device:TPU:0, one launch (start us, length us, event | category | flops | bytes accessed | tf_op | source)
XLA Modules:
  0.0 331.5 jit_solution(14769142543542769057)
XLA Ops:
  7.2 1.6 fusion.3
  8.9 2.5 fusion.5
  12.2 0.9 collective-permute-done
  13.2 3.0 collective-permute-start.3
  16.1 2.6 collective-permute-start.2
  18.7 1.3 collective-permute-start.1
  20.1 2.5 collective-permute-done.3
  22.6 8.8 %collective-permute-done.2 = bf16[32,2048]{1,0:T(8,128)(2,1)S(1)} collective-permute-done((bf16[32,2048]{1,0:T(8,128)(2,1)S(1)}, bf16[32,2048]{1,0:T(8,128)(2,1)S(1)}, u32[]{:S(2)}, u32[]{:S(2)}) %collective-permute-start.2) | collective-permute-done | bytes 131104 | tf_op jit(solution)/shard_map/ppermute | solution.py:36
  31.4 1.5 convolution_bitcast_fusion
  33.9 1.5 collective-permute-done.4
  36.2 12.9 %collective-permute-start.7 = (bf16[32,2048]{1,0:T(8,128)(2,1)S(1)}, bf16[32,2048]{1,0:T(8,128)(2,1)S(1)}, u32[]{:S(2)}, u32[]{:S(2)}) collective-permute-start(bf16[32,2048]{1,0:T(8,128)(2,1)S(1)} %get-tuple-element.86), channel_id=1, source_target_pairs={{0,3},{1,0},{2,1},{3,2},{4,7},{5,4},{6,5},{7,6},{8,11},{9,8},{10,9... | collective-permute-start | bytes 393224 | tf_op jit(solution)/shard_map/ppermute | solution.py:69
  49.8 8.0 %collective-permute-done.7 = bf16[32,2048]{1,0:T(8,128)(2,1)S(1)} collective-permute-done((bf16[32,2048]{1,0:T(8,128)(2,1)S(1)}, bf16[32,2048]{1,0:T(8,128)(2,1)S(1)}, u32[]{:S(2)}, u32[]{:S(2)}) %collective-permute-start.7) | collective-permute-done | bytes 131104 | tf_op jit(solution)/shard_map/ppermute | solution.py:69
  57.8 20.9 %collective-permute-done.6 = bf16[32,2048]{1,0:T(8,128)(2,1)S(1)} collective-permute-done((bf16[32,2048]{1,0:T(8,128)(2,1)S(1)}, bf16[32,2048]{1,0:T(8,128)(2,1)S(1)}, u32[]{:S(2)}, u32[]{:S(2)}) %collective-permute-start.6) | collective-permute-done | bytes 131104 | tf_op jit(solution)/shard_map/ppermute | solution.py:69
  78.8 1.9 copy.38
  81.7 3.5 %collective-permute-done.9 = bf16[16,2048]{1,0:T(8,128)(2,1)S(1)} collective-permute-done((bf16[16,2048]{1,0:T(8,128)(2,1)S(1)}, bf16[16,2048]{1,0:T(8,128)(2,1)S(1)}, u32[]{:S(2)}, u32[]{:S(2)}) %collective-permute-start.9) | collective-permute-done | bytes 65568 | tf_op jit(solution)/shard_map/ppermute | solution.py:30
  85.4 3.9 %collective-permute-start.10 = (bf16[32,2048]{1,0:T(8,128)(2,1)S(1)}, bf16[32,2048]{1,0:T(8,128)(2,1)S(1)}, u32[]{:S(2)}, u32[]{:S(2)}) collective-permute-start(bf16[32,2048]{1,0:T(8,128)(2,1)S(1)} %maximum_select_fusion.3), channel_id=1, source_target_pairs={{0,3},{1,0},{2,1},{3,2},{4,7},{5,4},{6,5},{7,6},{8,11},{9,8},{10,9... | collective-permute-start | bytes 393224 | tf_op jit(solution)/shard_map/ppermute | solution.py:36
  89.3 7.0 %collective-permute-done.12 = bf16[32,2048]{1,0:T(8,128)(2,1)S(1)} collective-permute-done((bf16[32,2048]{1,0:T(8,128)(2,1)S(1)}, bf16[32,2048]{1,0:T(8,128)(2,1)S(1)}, u32[]{:S(2)}, u32[]{:S(2)}) %collective-permute-start.12) | collective-permute-done | bytes 131104 | tf_op jit(solution)/shard_map/ppermute | solution.py:36
  96.3 7.6 %collective-permute-done.11 = bf16[32,2048]{1,0:T(8,128)(2,1)S(1)} collective-permute-done((bf16[32,2048]{1,0:T(8,128)(2,1)S(1)}, bf16[32,2048]{1,0:T(8,128)(2,1)S(1)}, u32[]{:S(2)}, u32[]{:S(2)}) %collective-permute-start.11) | collective-permute-done | bytes 131104 | tf_op jit(solution)/shard_map/ppermute | solution.py:36
  104.5 1.2 collective-permute-done.13
  105.8 16.5 %all-gather.3.cloned.1.call-done = bf16[1024,4096]{1,0:T(8,128)(2,1)} async-done(((bf16[128,4096]{1,0:T(8,128)(2,1)}), bf16[1024,4096]{1,0:T(8,128)(2,1)}) %all-gather.3.cloned.1.call-update) | async-done | bytes 8388624 | tf_op jit(solution)/shard_map/all_gather | solution.py:284
  122.2 1.6 collective-permute-start.17
  123.8 1.9 collective-permute-start.16
  125.7 0.9 collective-permute-start.15
  126.7 3.4 %copy-done.2 = bf16[4096,1024]{1,0:T(8,128)(2,1)S(1)} copy-done((bf16[4096,1024]{1,0:T(8,128)(2,1)S(1)}, bf16[4096,1024]{1,0:T(8,128)(2,1)}, u32[]{:S(2)}) %copy-start.2) | copy-done | bytes 8388632
  130.1 3.4 %copy-done.4 = bf16[1024,4096]{1,0:T(8,128)(2,1)S(1)} copy-done((bf16[1024,4096]{1,0:T(8,128)(2,1)S(1)}, bf16[1024,4096]{1,0:T(8,128)(2,1)}, u32[]{:S(2)}) %copy-start.4) | copy-done | bytes 8388632
  133.5 19.9 %ffn.2 = bf16[512,4096]{1,0:T(8,128)(2,1)S(1)} custom-call(s32[5]{0:T(128)S(1)} %get-tuple-element.101.order, bf16[2,4,128,4096]{3,2,1,0:T(8,128)(2,1)S(1)} %bitcast.81, bf16[4096,1024]{1,0:T(8,128)(2,1)S(1)} %copy-done.2, bf16[4096,1024]{1,0:T(8,128)(2,1)} %up_ref.3, bf16[1024,4096]{1,0:T(8,128)(2,1)} %down_ref.3), custom_call_target="tpu_custom_call" | custom-call | flops 1024 | bytes 1024 | tf_op jit(solution)/shard_map/ffn/pallas_call | solution.py:149
  153.4 1.1 pad_maximum_fusion.1
  154.6 1.3 collective-permute-start.19
  156.0 3.4 %copy-done.3 = bf16[4096,1024]{1,0:T(8,128)(2,1)S(1)} copy-done((bf16[4096,1024]{1,0:T(8,128)(2,1)S(1)}, bf16[4096,1024]{1,0:T(8,128)(2,1)}, u32[]{:S(2)}) %copy-start.3) | copy-done | bytes 8388632
  159.3 19.8 %ffn.3 = bf16[512,4096]{1,0:T(8,128)(2,1)S(1)} custom-call(s32[5]{0:T(128)S(1)} %get-tuple-element.100.order, bf16[2,4,128,4096]{3,2,1,0:T(8,128)(2,1)S(1)} %bitcast.82, bf16[4096,1024]{1,0:T(8,128)(2,1)S(1)} %copy-done.3, bf16[4096,1024]{1,0:T(8,128)(2,1)} %up_ref.3, bf16[1024,4096]{1,0:T(8,128)(2,1)} %down_ref.3), custom_call_target="tpu_custom_call" | custom-call | flops 1024 | bytes 1024 | tf_op jit(solution)/shard_map/ffn/pallas_call | solution.py:149
  179.2 1.0 collective-permute-done.19
  180.2 0.8 fusion.7
  181.0 3.2 collective-permute-start.21
  185.0 21.4 %collective-permute-done.21 = bf16[128,4096]{1,0:T(8,128)(2,1)S(1)} collective-permute-done((bf16[128,4096]{1,0:T(8,128)(2,1)S(1)}, bf16[128,4096]{1,0:T(8,128)(2,1)S(1)}, u32[]{:S(2)}, u32[]{:S(2)}) %collective-permute-start.21) | collective-permute-done | bytes 1048608 | tf_op jit(solution)/shard_map/ppermute | solution.py:59
  206.4 0.8 add_convert_fusion.2
  207.2 4.5 %collective-permute-start.23 = (bf16[128,4096]{1,0:T(8,128)(2,1)S(1)}, bf16[128,4096]{1,0:T(8,128)(2,1)S(1)}, u32[]{:S(2)}, u32[]{:S(2)}) collective-permute-start(bf16[128,4096]{1,0:T(8,128)(2,1)S(1)} %get-tuple-element.77), channel_id=1, source_target_pairs={{0,1},{1,2},{4,5},{5,6},{8,9},{9,10},{12,13},{13,14},{16,17},{17,1... | collective-permute-start | bytes 3145736 | tf_op jit(solution)/shard_map/ppermute | solution.py:59
  211.6 1.0 collective-permute-start.24
  212.8 1.6 collective-permute-start.25
  214.4 1.5 collective-permute-start.26
  215.9 17.0 %collective-permute-done.23 = bf16[128,4096]{1,0:T(8,128)(2,1)S(1)} collective-permute-done((bf16[128,4096]{1,0:T(8,128)(2,1)S(1)}, bf16[128,4096]{1,0:T(8,128)(2,1)S(1)}, u32[]{:S(2)}, u32[]{:S(2)}) %collective-permute-start.23) | collective-permute-done | bytes 1048608 | tf_op jit(solution)/shard_map/ppermute | solution.py:59
  232.9 2.5 add_convert_fusion
  235.4 12.2 %collective-permute-done.25.refs_3_ = bf16[3,2,512,256]{3,2,1,0:T(8,128)(2,1)S(1)} collective-permute-done((bf16[3,2,512,256]{3,2,1,0:T(8,128)(2,1)S(1)}, bf16[3,2,512,256]{3,2,1,0:T(8,128)(2,1)S(1)}, u32[]{:S(2)}, u32[]{:S(2)}) %collective-permute-start.25) | collective-permute-done | bytes 1572896 | tf_op jit(solution)/shard_map/ppermute | solution.py:30
  247.7 1.2 collective-permute-done.26.refs_4_
  248.9 5.5 %collective-permute-start.27 = (bf16[128,4096]{1,0:T(8,128)(2,1)}, bf16[128,4096]{1,0:T(8,128)(2,1)}, u32[]{:S(2)}, u32[]{:S(2)}) collective-permute-start(bf16[128,4096]{1,0:T(8,128)(2,1)} %get-tuple-element.41), channel_id=1, source_target_pairs={{0,1},{1,2},{2,3},{4,5},{5,6},{6,7},{8,9},{9,10},{10,11},{12,13},{... | collective-permute-start | bytes 3145736 | tf_op jit(solution)/shard_map/ppermute | solution.py:59
  254.3 1.3 collective-permute-start.28
  255.6 1.0 slice.189
  257.1 0.9 slice.190
  258.1 1.5 collective-permute-start.30
  260.2 3.0 copy.29
  263.5 10.0 %collective-permute-done.27 = bf16[128,4096]{1,0:T(8,128)(2,1)} collective-permute-done((bf16[128,4096]{1,0:T(8,128)(2,1)}, bf16[128,4096]{1,0:T(8,128)(2,1)}, u32[]{:S(2)}, u32[]{:S(2)}) %collective-permute-start.27) | collective-permute-done | bytes 1048608 | tf_op jit(solution)/shard_map/ppermute | solution.py:59
  273.5 5.1 %collective-permute-done.28 = bf16[128,4096]{1,0:T(8,128)(2,1)} collective-permute-done((bf16[128,4096]{1,0:T(8,128)(2,1)}, bf16[128,4096]{1,0:T(8,128)(2,1)}, u32[]{:S(2)}, u32[]{:S(2)}) %collective-permute-start.28) | collective-permute-done | bytes 1048608 | tf_op jit(solution)/shard_map/ppermute | solution.py:60
  279.2 4.2 %fusion = (f32[128]{0:T(128)S(1)}, bf16[128,4096]{1,0:T(8,128)(2,1)S(1)}) fusion(bf16[128,4096]{1,0:T(8,128)(2,1)} %collective-permute-done.28, bf16[128,4096]{1,0:T(8,128)(2,1)} %collective-permute-done.27, bf16[512,4096]{1,0:T(8,128)(2,1)} %copy-done.14, bf16[512,4096]{1,0:T(8,128)(2,1)} %copy-done.6, s32[128,4096]{1,0:T(8,128)} %bitcast.86, ...), kind=kLoop, calls=%fused_computation.7 | loop fusion | flops 9437056 | bytes 8405504 | tf_op jit(solution)/shard_map/reduce_sum | solution.py:18
  285.2 6.8 %attend_own_keys.1 = bf16[4,128,384]{2,1,0:T(8,128)(2,1)S(1)} custom-call(s32[16]{0:T(128)S(1)} %pad_add_fusion.3.table, bf16[128,4096]{1,0:T(8,128)(2,1)S(1)} %fusion.2.mem_ref, bf16[4,128,256]{2,1,0:T(8,128)(2,1)S(1)} %pad_maximum_fusion.4.cq_ref, bf16[2,2048,256]{2,1,0:T(8,128)(2,1)S(1)} %bitcast.84, ...), custom_call_target="tpu_custom_call" | custom-call | flops 1024 | bytes 1024 | tf_op jit(solution)/shard_map/attend_own_keys/pallas_call | solution.py:226
  292.1 0.9 collective-permute-start.36
  293.4 3.2 collective-permute-start.38
  296.6 4.5 %collective-permute-done.36 = bf16[128,384]{1,0:T(8,128)(2,1)S(1)} collective-permute-done((bf16[128,384]{1,0:T(8,128)(2,1)S(1)}, bf16[128,384]{1,0:T(8,128)(2,1)S(1)}, u32[]{:S(2)}, u32[]{:S(2)}) %collective-permute-start.36) | collective-permute-done | bytes 98336 | tf_op jit(solution)/shard_map/ppermute | solution.py:30
  301.1 2.0 collective-permute-done.38
  304.3 1.5 collective-permute-done.39
  306.5 1.2 collective-permute-start.42
  307.8 2.2 collective-permute-start.41
  310.0 2.3 collective-permute-done.42
  312.3 9.6 %collective-permute-done.41 = bf16[32,2048]{1,0:T(8,128)(2,1)S(1)} collective-permute-done((bf16[32,2048]{1,0:T(8,128)(2,1)S(1)}, bf16[32,2048]{1,0:T(8,128)(2,1)S(1)}, u32[]{:S(2)}, u32[]{:S(2)}) %collective-permute-start.41) | collective-permute-done | bytes 131104 | tf_op jit(solution)/shard_map/ppermute | solution.py:69
  322.4 1.1 collective-permute-done.43
  323.5 0.7 fusion.25
  (160 shorter events, 12.6 us)
Async XLA Ops:
  7.2 28.5 %copy-start = (bf16[256,2048]{1,0:T(8,128)(2,1)S(1)}, bf16[256,2048]{1,0:T(8,128)(2,1)}, u32[]{:S(2)}) copy-start(bf16[256,2048]{1,0:T(8,128)(2,1)} %param.28) | copy-start | bytes 3145732
  7.2 4.2 %copy-start.17 = (bf16[16,4096]{1,0:T(8,128)(2,1)S(1)}, bf16[16,4096]{1,0:T(8,128)(2,1)}, u32[]{:S(2)}) copy-start(bf16[16,4096]{1,0:T(8,128)(2,1)} %param.25) | copy-start | bytes 393220
  7.2 4.4 %copy-start.22 = (f32[4096]{0:T(1024)S(1)}, f32[4096]{0:T(1024)}, u32[]{:S(2)}) copy-start(f32[4096]{0:T(1024)} %param.26) | copy-start | bytes 49156
  7.2 115.0 %all-gather.3.cloned.1.call-start = ((), (), s32[]{:S(2)}) async-start(), calls=%async_computation | async-start | bytes 9437184 | tf_op jit(solution)/shard_map/all_gather | solution.py:284
  11.7 1.4 collective-permute-start
  13.2 9.4 %collective-permute-start.3 = (bf16[32,2048]{1,0:T(8,128)(2,1)S(1)}, bf16[32,2048]{1,0:T(8,128)(2,1)S(1)}, u32[]{:S(2)}, u32[]{:S(2)}) collective-permute-start(bf16[32,2048]{1,0:T(8,128)(2,1)S(1)} %maximum_select_fusion.2), channel_id=1, source_target_pairs={{0,1},{1,2},{2,3},{3,0},{4,5},{5,6},{6,7},{7,4},{8,9},{9,10},{10,1... | collective-permute-start | bytes 393224 | tf_op jit(solution)/shard_map/ppermute | solution.py:36
  16.1 15.2 %collective-permute-start.2 = (bf16[32,2048]{1,0:T(8,128)(2,1)S(1)}, bf16[32,2048]{1,0:T(8,128)(2,1)S(1)}, u32[]{:S(2)}, u32[]{:S(2)}) collective-permute-start(bf16[32,2048]{1,0:T(8,128)(2,1)S(1)} %maximum_select_fusion.2), channel_id=1, source_target_pairs={{0,2},{1,3},{2,0},{3,1},{4,6},{5,7},{6,4},{7,5},{8,10},{9,11},{10,... | collective-permute-start | bytes 393224 | tf_op jit(solution)/shard_map/ppermute | solution.py:36
  18.7 12.6 %collective-permute-start.1 = (bf16[32,2048]{1,0:T(8,128)(2,1)S(1)}, bf16[32,2048]{1,0:T(8,128)(2,1)S(1)}, u32[]{:S(2)}, u32[]{:S(2)}) collective-permute-start(bf16[32,2048]{1,0:T(8,128)(2,1)S(1)} %maximum_select_fusion.2), channel_id=1, source_target_pairs={{0,3},{1,0},{2,1},{3,2},{4,7},{5,4},{6,5},{7,6},{8,11},{9,8},{10,9... | collective-permute-start | bytes 393224 | tf_op jit(solution)/shard_map/ppermute | solution.py:36
  20.1 12.8 %copy-start.24 = (bf16[2048,3,256]{2,0,1:T(8,128)(2,1)S(1)}, bf16[2048,3,256]{2,0,1:T(8,128)(2,1)}, u32[]{:S(2)}) copy-start(bf16[2048,3,256]{2,0,1:T(8,128)(2,1)} %param.27) | copy-start | bytes 9437188
  33.6 1.8 collective-permute-start.4
  36.2 21.6 %collective-permute-start.7 = (bf16[32,2048]{1,0:T(8,128)(2,1)S(1)}, bf16[32,2048]{1,0:T(8,128)(2,1)S(1)}, u32[]{:S(2)}, u32[]{:S(2)}) collective-permute-start(bf16[32,2048]{1,0:T(8,128)(2,1)S(1)} %get-tuple-element.86), channel_id=1, source_target_pairs={{0,3},{1,0},{2,1},{3,2},{4,7},{5,4},{6,5},{7,6},{8,11},{9,8},{10,9... | collective-permute-start | bytes 393224 | tf_op jit(solution)/shard_map/ppermute | solution.py:69
  49.1 29.5 %collective-permute-start.6 = (bf16[32,2048]{1,0:T(8,128)(2,1)S(1)}, bf16[32,2048]{1,0:T(8,128)(2,1)S(1)}, u32[]{:S(2)}, u32[]{:S(2)}) collective-permute-start(bf16[32,2048]{1,0:T(8,128)(2,1)S(1)} %get-tuple-element.87), channel_id=1, source_target_pairs={{0,2},{1,3},{2,0},{3,1},{4,6},{5,7},{6,4},{7,5},{8,10},{9,11},{10,... | collective-permute-start | bytes 393224 | tf_op jit(solution)/shard_map/ppermute | solution.py:69
  49.4 29.2 %collective-permute-start.5 = (bf16[32,2048]{1,0:T(8,128)(2,1)S(1)}, bf16[32,2048]{1,0:T(8,128)(2,1)S(1)}, u32[]{:S(2)}, u32[]{:S(2)}) collective-permute-start(bf16[32,2048]{1,0:T(8,128)(2,1)S(1)} %get-tuple-element.85), channel_id=1, source_target_pairs={{0,1},{1,2},{2,3},{3,0},{4,5},{5,6},{6,7},{7,4},{8,9},{9,10},{10,1... | collective-permute-start | bytes 393224 | tf_op jit(solution)/shard_map/ppermute | solution.py:69
  78.7 25.2 %copy-start.25 = (bf16[2048,256]{1,0:T(8,128)(2,1)S(1)}, bf16[2048,256]{1,0:T(8,128)(2,1)}, u32[]{:S(2)}) copy-start(bf16[2048,256]{1,0:T(8,128)(2,1)} %param.30) | copy-start | bytes 3145732
  78.8 2.5 collective-permute-start.8
  80.8 25.0 %collective-permute-start.14 = (bf16[2,2048,256]{2,1,0:T(8,128)(2,1)S(1)}, bf16[2,2048,256]{2,1,0:T(8,128)(2,1)}, u32[]{:S(2)}, u32[]{:S(2)}) collective-permute-start(bf16[2,2048,256]{2,1,0:T(8,128)(2,1)S(1)} %bitcast.83), channel_id=1, source_target_pairs={{0,4},{4,0},{1,5},{5,1},{2,6},{6,2},{3,7},{7,3},{8,12},{12,8},{9,1... | collective-permute-start | bytes 6291464 | tf_op jit(solution)/shard_map/ppermute | solution.py:30
  81.6 3.7 %collective-permute-start.9 = (bf16[16,2048]{1,0:T(8,128)(2,1)S(1)}, bf16[16,2048]{1,0:T(8,128)(2,1)S(1)}, u32[]{:S(2)}, u32[]{:S(2)}) collective-permute-start(bf16[16,2048]{1,0:T(8,128)(2,1)S(1)} %get-tuple-element.97), channel_id=1, source_target_pairs={{0,4},{4,0},{1,5},{5,1},{2,6},{6,2},{3,7},{7,3},{8,12},{12,8},{9,1... | collective-permute-start | bytes 196616 | tf_op jit(solution)/shard_map/ppermute | solution.py:30
  85.3 11.0 %collective-permute-start.12 = (bf16[32,2048]{1,0:T(8,128)(2,1)S(1)}, bf16[32,2048]{1,0:T(8,128)(2,1)S(1)}, u32[]{:S(2)}, u32[]{:S(2)}) collective-permute-start(bf16[32,2048]{1,0:T(8,128)(2,1)S(1)} %maximum_select_fusion.3), channel_id=1, source_target_pairs={{0,1},{1,2},{2,3},{3,0},{4,5},{5,6},{6,7},{7,4},{8,9},{9,10},{10,1... | collective-permute-start | bytes 393224 | tf_op jit(solution)/shard_map/ppermute | solution.py:36
  85.3 18.6 %collective-permute-start.11 = (bf16[32,2048]{1,0:T(8,128)(2,1)S(1)}, bf16[32,2048]{1,0:T(8,128)(2,1)S(1)}, u32[]{:S(2)}, u32[]{:S(2)}) collective-permute-start(bf16[32,2048]{1,0:T(8,128)(2,1)S(1)} %maximum_select_fusion.3), channel_id=1, source_target_pairs={{0,2},{1,3},{2,0},{3,1},{4,6},{5,7},{6,4},{7,5},{8,10},{9,11},{10,... | collective-permute-start | bytes 393224 | tf_op jit(solution)/shard_map/ppermute | solution.py:36
  85.4 18.5 %collective-permute-start.10 = (bf16[32,2048]{1,0:T(8,128)(2,1)S(1)}, bf16[32,2048]{1,0:T(8,128)(2,1)S(1)}, u32[]{:S(2)}, u32[]{:S(2)}) collective-permute-start(bf16[32,2048]{1,0:T(8,128)(2,1)S(1)} %maximum_select_fusion.3), channel_id=1, source_target_pairs={{0,3},{1,0},{2,1},{3,2},{4,7},{5,4},{6,5},{7,6},{8,11},{9,8},{10,9... | collective-permute-start | bytes 393224 | tf_op jit(solution)/shard_map/ppermute | solution.py:36
  104.3 1.4 collective-permute-start.13
  104.5 48.8 %copy-start.16 = (bf16[1,2,512,256]{3,2,1,0:T(8,128)(2,1)}, bf16[1,2,512,256]{3,2,1,0:T(8,128)(2,1)S(1)}, u32[]{:S(2)}) copy-start(bf16[1,2,512,256]{3,2,1,0:T(8,128)(2,1)S(1)} %dynamic-slice_bitcast_fusion) | copy-start | bytes 1572868
  122.2 31.2 %collective-permute-start.18 = (bf16[1,2,512,256]{3,2,1,0:T(8,128)(2,1)S(1)}, bf16[1,2,512,256]{3,2,1,0:T(8,128)(2,1)S(1)}, u32[]{:S(2)}, u32[]{:S(2)}) collective-permute-start(bf16[1,2,512,256]{3,2,1,0:T(8,128)(2,1)S(1)} %dynamic-slice_bitcast_fusion), channel_id=1, source_target_pairs={{0,2},{1,3},{2,0},{3,1},{4,6},{5,7},{6,4},{7,5},{8,10},{9,11},{10,... | collective-permute-start | bytes 1572872 | tf_op jit(solution)/shard_map/ppermute | solution.py:30
  122.2 31.1 %collective-permute-start.17 = (bf16[128,256]{1,0:T(8,128)(2,1)S(1)}, bf16[128,256]{1,0:T(8,128)(2,1)S(1)}, u32[]{:S(2)}, u32[]{:S(2)}) collective-permute-start(bf16[128,256]{1,0:T(8,128)(2,1)S(1)} %bitcast.93), channel_id=1, source_target_pairs={{0,3},{1,2},{2,1},{3,0},{4,7},{5,6},{6,5},{7,4},{8,11},{9,10},{10,... | collective-permute-start | bytes 196616 | tf_op jit(solution)/shard_map/ppermute | solution.py:30
  123.8 29.5 %collective-permute-start.16 = (bf16[128,256]{1,0:T(8,128)(2,1)S(1)}, bf16[128,256]{1,0:T(8,128)(2,1)S(1)}, u32[]{:S(2)}, u32[]{:S(2)}) collective-permute-start(bf16[128,256]{1,0:T(8,128)(2,1)S(1)} %bitcast.94), channel_id=1, source_target_pairs={{0,1},{1,0},{2,3},{3,2},{4,5},{5,4},{6,7},{7,6},{8,9},{9,8},{10,11... | collective-permute-start | bytes 196616 | tf_op jit(solution)/shard_map/ppermute | solution.py:30
  125.7 27.6 %collective-permute-start.15 = (bf16[128,256]{1,0:T(8,128)(2,1)S(1)}, bf16[128,256]{1,0:T(8,128)(2,1)S(1)}, u32[]{:S(2)}, u32[]{:S(2)}) collective-permute-start(bf16[128,256]{1,0:T(8,128)(2,1)S(1)} %bitcast.95), channel_id=1, source_target_pairs={{0,2},{1,3},{2,0},{3,1},{4,6},{5,7},{6,4},{7,5},{8,10},{9,11},{10,... | collective-permute-start | bytes 196616 | tf_op jit(solution)/shard_map/ppermute | solution.py:30
  133.5 22.5 %copy-start.5 = (bf16[1024,4096]{1,0:T(8,128)(2,1)S(1)}, bf16[1024,4096]{1,0:T(8,128)(2,1)}, u32[]{:S(2)}) copy-start(bf16[1024,4096]{1,0:T(8,128)(2,1)} %all-gather.3.cloned.1.call-done) | copy-start | bytes 25165828
  154.6 25.7 %collective-permute-start.20 = (bf16[512,4096]{1,0:T(8,128)(2,1)S(1)}, bf16[512,4096]{1,0:T(8,128)(2,1)S(1)}, u32[]{:S(2)}, u32[]{:S(2)}) collective-permute-start(bf16[512,4096]{1,0:T(8,128)(2,1)S(1)} %ffn.2), channel_id=1, source_target_pairs={{0,4},{4,0},{1,5},{5,1},{2,6},{6,2},{3,7},{7,3},{8,12},{12,8},{9,1... | collective-permute-start | bytes 12582920 | tf_op jit(solution)/shard_map/ppermute | solution.py:30
  154.6 25.6 %collective-permute-start.19 = (bf16[2,2,512,256]{3,2,1,0:T(8,128)(2,1)S(1)}, bf16[2,2,512,256]{3,2,1,0:T(8,128)(2,1)S(1)}, u32[]{:S(2)}, u32[]{:S(2)}) collective-permute-start(bf16[2,2,512,256]{3,2,1,0:T(8,128)(2,1)S(1)} %pad_maximum_fusion.1), channel_id=1, source_target_pairs={{0,1},{1,0},{2,3},{3,2},{4,5},{5,4},{6,7},{7,6},{8,9},{9,8},{10,11... | collective-permute-start | bytes 3145736 | tf_op jit(solution)/shard_map/ppermute | solution.py:30
  179.2 53.7 %copy-start.6 = (bf16[512,4096]{1,0:T(8,128)(2,1)}, bf16[512,4096]{1,0:T(8,128)(2,1)S(1)}, u32[]{:S(2)}) copy-start(bf16[512,4096]{1,0:T(8,128)(2,1)S(1)} %ffn.3) | copy-start | bytes 12582916
  180.2 52.7 %copy-start.14 = (bf16[512,4096]{1,0:T(8,128)(2,1)}, bf16[512,4096]{1,0:T(8,128)(2,1)S(1)}, u32[]{:S(2)}) copy-start(bf16[512,4096]{1,0:T(8,128)(2,1)S(1)} %collective-permute-done.20) | copy-start | bytes 12582916
  181.0 25.4 %collective-permute-start.21 = (bf16[128,4096]{1,0:T(8,128)(2,1)S(1)}, bf16[128,4096]{1,0:T(8,128)(2,1)S(1)}, u32[]{:S(2)}, u32[]{:S(2)}) collective-permute-start(bf16[128,4096]{1,0:T(8,128)(2,1)S(1)} %get-tuple-element.79), channel_id=1, source_target_pairs={{0,1},{4,5},{8,9},{12,13},{16,17},{20,21},{24,25},{28,29}} | collective-permute-start | bytes 3145736 | tf_op jit(solution)/shard_map/ppermute | solution.py:59
  184.2 22.2 %collective-permute-start.22 = (bf16[128,4096]{1,0:T(8,128)(2,1)S(1)}, bf16[128,4096]{1,0:T(8,128)(2,1)S(1)}, u32[]{:S(2)}, u32[]{:S(2)}) collective-permute-start(bf16[128,4096]{1,0:T(8,128)(2,1)S(1)} %get-tuple-element.78), channel_id=1, source_target_pairs={{3,2},{7,6},{11,10},{15,14},{19,18},{23,22},{27,26},{31,30}} | collective-permute-start | bytes 3145736 | tf_op jit(solution)/shard_map/ppermute | solution.py:60
  207.2 25.7 %collective-permute-start.23 = (bf16[128,4096]{1,0:T(8,128)(2,1)S(1)}, bf16[128,4096]{1,0:T(8,128)(2,1)S(1)}, u32[]{:S(2)}, u32[]{:S(2)}) collective-permute-start(bf16[128,4096]{1,0:T(8,128)(2,1)S(1)} %get-tuple-element.77), channel_id=1, source_target_pairs={{0,1},{1,2},{4,5},{5,6},{8,9},{9,10},{12,13},{13,14},{16,17},{17,1... | collective-permute-start | bytes 3145736 | tf_op jit(solution)/shard_map/ppermute | solution.py:59
  211.6 21.3 %collective-permute-start.24 = (bf16[128,4096]{1,0:T(8,128)(2,1)S(1)}, bf16[128,4096]{1,0:T(8,128)(2,1)S(1)}, u32[]{:S(2)}, u32[]{:S(2)}) collective-permute-start(bf16[128,4096]{1,0:T(8,128)(2,1)S(1)} %get-tuple-element.76), channel_id=1, source_target_pairs={{2,1},{3,2},{6,5},{7,6},{10,9},{11,10},{14,13},{15,14},{18,17},{19... | collective-permute-start | bytes 3145736 | tf_op jit(solution)/shard_map/ppermute | solution.py:60
  212.8 22.6 %copy-start.7 = (bf16[3,2,512,256]{3,2,1,0:T(8,128)(2,1)}, bf16[3,2,512,256]{3,2,1,0:T(8,128)(2,1)S(1)}, u32[]{:S(2)}) copy-start(bf16[3,2,512,256]{3,2,1,0:T(8,128)(2,1)S(1)} %pad_maximum_fusion.refs_2_) | copy-start | bytes 4718596
  212.8 34.9 %collective-permute-start.25 = (bf16[3,2,512,256]{3,2,1,0:T(8,128)(2,1)S(1)}, bf16[3,2,512,256]{3,2,1,0:T(8,128)(2,1)S(1)}, u32[]{:S(2)}, u32[]{:S(2)}) collective-permute-start(bf16[3,2,512,256]{3,2,1,0:T(8,128)(2,1)S(1)} %pad_maximum_fusion.refs_2_), channel_id=1, source_target_pairs={{0,8},{8,0},{16,24},{24,16},{1,9},{9,1},{17,25},{25,17},{2,10},{10... | collective-permute-start | bytes 4718600 | tf_op jit(solution)/shard_map/ppermute | solution.py:30
  214.4 34.5 %collective-permute-start.26 = (bf16[3,2,512,256]{3,2,1,0:T(8,128)(2,1)S(1)}, bf16[3,2,512,256]{3,2,1,0:T(8,128)(2,1)S(1)}, u32[]{:S(2)}, u32[]{:S(2)}) collective-permute-start(bf16[3,2,512,256]{3,2,1,0:T(8,128)(2,1)S(1)} %pad_maximum_fusion.refs_2_), channel_id=1, source_target_pairs={{0,16},{8,24},{16,0},{24,8},{1,17},{9,25},{17,1},{25,9},{2,18},{10... | collective-permute-start | bytes 4718600 | tf_op jit(solution)/shard_map/ppermute | solution.py:30
  235.4 24.2 %copy-start.19 = (s32[128,1024]{1,0:T(8,128)S(1)}, s32[128,1024]{1,0:T(8,128)}, u32[]{:S(2)}) copy-start(s32[128,1024]{1,0:T(8,128)} %param.23) | copy-start | bytes 1572868
  247.7 9.4 %copy-start.9 = (bf16[3,2,512,256]{3,2,1,0:T(8,128)(2,1)}, bf16[3,2,512,256]{3,2,1,0:T(8,128)(2,1)S(1)}, u32[]{:S(2)}) copy-start(bf16[3,2,512,256]{3,2,1,0:T(8,128)(2,1)S(1)} %collective-permute-done.25.refs_3_) | copy-start | bytes 4718596
  248.9 9.2 %copy-start.11 = (bf16[3,2,512,256]{3,2,1,0:T(8,128)(2,1)}, bf16[3,2,512,256]{3,2,1,0:T(8,128)(2,1)S(1)}, u32[]{:S(2)}) copy-start(bf16[3,2,512,256]{3,2,1,0:T(8,128)(2,1)S(1)} %collective-permute-done.26.refs_4_) | copy-start | bytes 4718596
  248.9 24.6 %collective-permute-start.27 = (bf16[128,4096]{1,0:T(8,128)(2,1)}, bf16[128,4096]{1,0:T(8,128)(2,1)}, u32[]{:S(2)}, u32[]{:S(2)}) collective-permute-start(bf16[128,4096]{1,0:T(8,128)(2,1)} %get-tuple-element.41), channel_id=1, source_target_pairs={{0,1},{1,2},{2,3},{4,5},{5,6},{6,7},{8,9},{9,10},{10,11},{12,13},{... | collective-permute-start | bytes 3145736 | tf_op jit(solution)/shard_map/ppermute | solution.py:59
  254.3 24.3 %collective-permute-start.28 = (bf16[128,4096]{1,0:T(8,128)(2,1)}, bf16[128,4096]{1,0:T(8,128)(2,1)}, u32[]{:S(2)}, u32[]{:S(2)}) collective-permute-start(bf16[128,4096]{1,0:T(8,128)(2,1)} %get-tuple-element.42), channel_id=1, source_target_pairs={{1,0},{2,1},{3,2},{5,4},{6,5},{7,6},{9,8},{10,9},{11,10},{13,12},{... | collective-permute-start | bytes 3145736 | tf_op jit(solution)/shard_map/ppermute | solution.py:60
  256.6 22.0 %collective-permute-start.29 = (bf16[3,1,512,256]{3,2,1,0:T(8,128)(2,1)}, bf16[3,1,512,256]{3,2,1,0:T(8,128)(2,1)}, u32[]{:S(2)}, u32[]{:S(2)}) collective-permute-start(bf16[3,1,512,256]{3,2,1,0:T(8,128)(2,1)} %slice.189), channel_id=1, source_target_pairs={{0,8},{8,0},{16,24},{24,16},{1,9},{9,1},{17,25},{25,17},{2,10},{10... | collective-permute-start | bytes 2359304 | tf_op jit(solution)/shard_map/ppermute | solution.py:30
  258.1 20.5 %collective-permute-start.30 = (bf16[3,1,512,256]{3,2,1,0:T(8,128)(2,1)}, bf16[3,1,512,256]{3,2,1,0:T(8,128)(2,1)}, u32[]{:S(2)}, u32[]{:S(2)}) collective-permute-start(bf16[3,1,512,256]{3,2,1,0:T(8,128)(2,1)} %slice.190), channel_id=1, source_target_pairs={{0,16},{8,24},{16,0},{24,8},{1,17},{9,25},{17,1},{25,9},{2,18},{10... | collective-permute-start | bytes 2359304 | tf_op jit(solution)/shard_map/ppermute | solution.py:30
  260.2 19.0 %copy-start.13 = (bf16[128,4096]{1,0:T(8,128)(2,1)S(1)}, bf16[128,4096]{1,0:T(8,128)(2,1)}, u32[]{:S(2)}) copy-start(bf16[128,4096]{1,0:T(8,128)(2,1)} %param.18) | copy-start | bytes 3145732
  263.5 20.3 %collective-permute-start.31 = (bf16[3,2,512,256]{3,2,1,0:T(8,128)(2,1)}, bf16[3,2,512,256]{3,2,1,0:T(8,128)(2,1)S(1)}, u32[]{:S(2)}, u32[]{:S(2)}) collective-permute-start(bf16[3,2,512,256]{3,2,1,0:T(8,128)(2,1)} %copy-done.7), channel_id=1, source_target_pairs={{0,4},{4,0},{1,5},{5,1},{2,6},{6,2},{3,7},{7,3},{8,12},{12,8},{9,1... | collective-permute-start | bytes 4718600 | tf_op jit(solution)/shard_map/ppermute | solution.py:30
  273.5 10.3 %collective-permute-start.32 = (bf16[3,2,512,256]{3,2,1,0:T(8,128)(2,1)}, bf16[3,2,512,256]{3,2,1,0:T(8,128)(2,1)S(1)}, u32[]{:S(2)}, u32[]{:S(2)}) collective-permute-start(bf16[3,2,512,256]{3,2,1,0:T(8,128)(2,1)} %copy-done.9), channel_id=1, source_target_pairs={{0,4},{4,0},{1,5},{5,1},{2,6},{6,2},{3,7},{7,3},{8,12},{12,8},{9,1... | collective-permute-start | bytes 4718600 | tf_op jit(solution)/shard_map/ppermute | solution.py:30
  278.6 5.2 %collective-permute-start.33 = (bf16[3,2,512,256]{3,2,1,0:T(8,128)(2,1)}, bf16[3,2,512,256]{3,2,1,0:T(8,128)(2,1)S(1)}, u32[]{:S(2)}, u32[]{:S(2)}) collective-permute-start(bf16[3,2,512,256]{3,2,1,0:T(8,128)(2,1)} %copy-done.11), channel_id=1, source_target_pairs={{0,4},{4,0},{1,5},{5,1},{2,6},{6,2},{3,7},{7,3},{8,12},{12,8},{9,1... | collective-permute-start | bytes 4718600 | tf_op jit(solution)/shard_map/ppermute | solution.py:30
  278.6 5.2 %collective-permute-start.34 = (bf16[3,1,512,256]{3,2,1,0:T(8,128)(2,1)}, bf16[3,1,512,256]{3,2,1,0:T(8,128)(2,1)S(1)}, u32[]{:S(2)}, u32[]{:S(2)}) collective-permute-start(bf16[3,1,512,256]{3,2,1,0:T(8,128)(2,1)} %collective-permute-done.29.refs_5_), channel_id=1, source_target_pairs={{0,4},{4,0},{1,5},{5,1},{2,6},{6,2},{3,7},{7,3},{8,12},{12,8},{9,1... | collective-permute-start | bytes 2359304 | tf_op jit(solution)/shard_map/ppermute | solution.py:30
  279.1 5.4 %collective-permute-start.35 = (bf16[3,1,512,256]{3,2,1,0:T(8,128)(2,1)}, bf16[3,1,512,256]{3,2,1,0:T(8,128)(2,1)S(1)}, u32[]{:S(2)}, u32[]{:S(2)}) collective-permute-start(bf16[3,1,512,256]{3,2,1,0:T(8,128)(2,1)} %collective-permute-done.30.refs_6_), channel_id=1, source_target_pairs={{0,4},{4,0},{1,5},{5,1},{2,6},{6,2},{3,7},{7,3},{8,12},{12,8},{9,1... | collective-permute-start | bytes 2359304 | tf_op jit(solution)/shard_map/ppermute | solution.py:30
  279.2 4.3 %copy-start.21 = (f32[4096]{0:T(1024)S(1)}, f32[4096]{0:T(1024)}, u32[]{:S(2)}) copy-start(f32[4096]{0:T(1024)} %param.24) | copy-start | bytes 49156
  279.2 5.3 %copy-start.10 = (bf16[3,2,512,256]{3,2,1,0:T(8,128)(2,1)S(1)}, bf16[3,2,512,256]{3,2,1,0:T(8,128)(2,1)}, u32[]{:S(2)}) copy-start(bf16[3,2,512,256]{3,2,1,0:T(8,128)(2,1)} %copy-done.9) | copy-start | bytes 4718596
  279.2 5.3 %copy-start.12 = (bf16[3,2,512,256]{3,2,1,0:T(8,128)(2,1)S(1)}, bf16[3,2,512,256]{3,2,1,0:T(8,128)(2,1)}, u32[]{:S(2)}) copy-start(bf16[3,2,512,256]{3,2,1,0:T(8,128)(2,1)} %copy-done.11) | copy-start | bytes 4718596
  292.1 9.0 %collective-permute-start.36 = (bf16[128,384]{1,0:T(8,128)(2,1)S(1)}, bf16[128,384]{1,0:T(8,128)(2,1)S(1)}, u32[]{:S(2)}, u32[]{:S(2)}) collective-permute-start(bf16[128,384]{1,0:T(8,128)(2,1)S(1)} %get-tuple-element.91), channel_id=1, source_target_pairs={{0,2},{1,3},{2,0},{3,1},{4,6},{5,7},{6,4},{7,5},{8,10},{9,11},{10,... | collective-permute-start | bytes 294920 | tf_op jit(solution)/shard_map/ppermute | solution.py:30
  293.0 8.0 %collective-permute-start.37 = (bf16[128,384]{1,0:T(8,128)(2,1)S(1)}, bf16[128,384]{1,0:T(8,128)(2,1)S(1)}, u32[]{:S(2)}, u32[]{:S(2)}) collective-permute-start(bf16[128,384]{1,0:T(8,128)(2,1)S(1)} %get-tuple-element.90), channel_id=1, source_target_pairs={{0,1},{1,0},{2,3},{3,2},{4,5},{5,4},{6,7},{7,6},{8,9},{9,8},{10,11... | collective-permute-start | bytes 294920 | tf_op jit(solution)/shard_map/ppermute | solution.py:30
  293.4 9.8 %collective-permute-start.38 = (bf16[128,384]{1,0:T(8,128)(2,1)S(1)}, bf16[128,384]{1,0:T(8,128)(2,1)S(1)}, u32[]{:S(2)}, u32[]{:S(2)}) collective-permute-start(bf16[128,384]{1,0:T(8,128)(2,1)S(1)} %get-tuple-element.89), channel_id=1, source_target_pairs={{0,3},{1,2},{2,1},{3,0},{4,7},{5,6},{6,5},{7,4},{8,11},{9,10},{10,... | collective-permute-start | bytes 294920 | tf_op jit(solution)/shard_map/ppermute | solution.py:30
  304.2 1.6 collective-permute-start.39
  305.9 16.2 %copy-start.20 = (s32[16,1024]{1,0:T(8,128)S(1)}, s32[16,1024]{1,0:T(8,128)}, u32[]{:S(2)}) copy-start(s32[16,1024]{1,0:T(8,128)} %param.33) | copy-start | bytes 196612
  306.2 18.0 %copy-start.1 = (bf16[256,2048]{1,0:T(8,128)(2,1)S(1)}, bf16[256,2048]{1,0:T(8,128)(2,1)}, u32[]{:S(2)}) copy-start(bf16[256,2048]{1,0:T(8,128)(2,1)} %param.28) | copy-start | bytes 3145732
  306.5 5.8 %collective-permute-start.42 = (bf16[32,2048]{1,0:T(8,128)(2,1)S(1)}, bf16[32,2048]{1,0:T(8,128)(2,1)S(1)}, u32[]{:S(2)}, u32[]{:S(2)}) collective-permute-start(bf16[32,2048]{1,0:T(8,128)(2,1)S(1)} %get-tuple-element.83), channel_id=1, source_target_pairs={{0,3},{1,0},{2,1},{3,2},{4,7},{5,4},{6,5},{7,6},{8,11},{9,8},{10,9... | collective-permute-start | bytes 393224 | tf_op jit(solution)/shard_map/ppermute | solution.py:69
  307.8 14.2 %collective-permute-start.41 = (bf16[32,2048]{1,0:T(8,128)(2,1)S(1)}, bf16[32,2048]{1,0:T(8,128)(2,1)S(1)}, u32[]{:S(2)}, u32[]{:S(2)}) collective-permute-start(bf16[32,2048]{1,0:T(8,128)(2,1)S(1)} %get-tuple-element.84), channel_id=1, source_target_pairs={{0,2},{1,3},{2,0},{3,1},{4,6},{5,7},{6,4},{7,5},{8,10},{9,11},{10,... | collective-permute-start | bytes 393224 | tf_op jit(solution)/shard_map/ppermute | solution.py:69
  310.0 11.9 %collective-permute-start.40 = (bf16[32,2048]{1,0:T(8,128)(2,1)S(1)}, bf16[32,2048]{1,0:T(8,128)(2,1)S(1)}, u32[]{:S(2)}, u32[]{:S(2)}) collective-permute-start(bf16[32,2048]{1,0:T(8,128)(2,1)S(1)} %get-tuple-element.82), channel_id=1, source_target_pairs={{0,1},{1,2},{2,3},{3,0},{4,5},{5,6},{6,7},{7,4},{8,9},{9,10},{10,1... | collective-permute-start | bytes 393224 | tf_op jit(solution)/shard_map/ppermute | solution.py:69
  322.0 1.4 collective-permute-start.43
  (7 other events, 18.6 us)
Sparse Core Ops, SparseCore 0:
  11.5 110.6 all-gather.2

commit v11 on v10

--- a/solution.py
+++ b/solution.py
@@ -155,9 +155,15 @@
                 pl.BlockSpec(
                     (1, blocks, block, features), lambda i, t: (t[0], 0, 0, 0), pipeline_mode=pl.Buffered(1)
                 ),
-                pl.BlockSpec((depth, units), lambda i, t: (jnp.minimum(i, ins - 1), 0)),
-                pl.BlockSpec((depth, units), lambda i, t: (jnp.minimum(i, ins - 1), 0)),
-                pl.BlockSpec((units, tile), lambda i, t: (0, jnp.maximum(i - ins, 0))),
+                pl.BlockSpec(
+                    (depth, units), lambda i, t: (jnp.minimum(i, ins - 1), 0)
+                ),
+                pl.BlockSpec(
+                    (depth, units), lambda i, t: (jnp.minimum(i, ins - 1), 0)
+                ),
+                pl.BlockSpec(
+                    (units, tile), lambda i, t: (0, jnp.maximum(i - ins, 0))
+                ),
             ],
             out_specs=pl.BlockSpec((rows, tile), lambda i, t: (0, jnp.maximum(i - ins, 0))),
             scratch_shapes=[
@@ -167,7 +173,7 @@
             ],
         ),
         out_shape=jax.ShapeDtypeStruct((rows, features), BF16),
-        compiler_params=pltpu.CompilerParams(vmem_limit_bytes=28 * 2**20),
+        compiler_params=pltpu.CompilerParams(vmem_limit_bytes=48 * 2**20),
         cost_estimate=pl.CostEstimate(flops=1024, bytes_accessed=1024, transcendentals=0),
         name="ffn",
     )(order, x, w_gate, w_up, w_down)
@@ -337,15 +343,16 @@
     came = sum_step(sum_sends(mine, got, None, 1), 1)
     for step in range(2, count):
         sends = sum_sends(mine, got, came, step)
-        if step == count - 1:
+        if step == 2:
             held = lax.optimization_barrier(sends + tuple(shares[1:]))
             sends, shares[1:] = held[:2], list(held[2:])
+            if groups == 4:
+                passed = [swap(shares[2][:, :1], "dp", 1), swap(shares[1][:, 1:], "dp", 2)]
+                plan.append((3, 0, 4, 0))
+        if step == count - 1 and groups == 4:
+            held = lax.optimization_barrier(sends + tuple(passed))
+            sends, shares = held[:2], shares + list(held[2:])
         came = sum_step(sends, step)
-    if groups == 4:
-        passed = [swap(shares[2][:, :1], "dp", 1), swap(shares[1][:, 1:], "dp", 2)]
-        held = lax.optimization_barrier(came + tuple(passed))
-        came, shares = held[:2], shares + list(held[2:])
-        plan.append((3, 0, 4, 0))
     total = slot_sum(mine, got, 0) + came[0].astype(F32) + came[1].astype(F32)
     enc_out = (source.astype(F32) + keep_factor(enc_keep) * total).astype(BF16)
     memory = norm_rows(enc_out, final_gain).astype(BF16)

time: 335 us -> 337 us (level)
  local copies, waits for them, and re-layouts: 19.8 us -> 9.98 us
  waiting for transfers between devices: 167 us -> 174 us
  Pallas kernels: 46.5 us -> 51.4 us
    unnamed x58 -> x46, local copies, waits for them, and re-layouts: 16.8 us -> 6.67 us
    ppermute x26, waiting for transfers between devices: 30.7 us -> 39.5 us  [swap(): lax.ppermute(value, axis, [(i, i ^ distance) for i in range(lax.axis_size...]
    pallas_call x2, Pallas kernels: 39.7 us -> 44.6 us  [ffn(): pl.pallas_call(functools.partial(ffn_kernel, ins), grid_spec=pltpu.Prefet...]
  transfers between devices with their start and end apart: 45 -> 45, of which waited for: 25 -> 26; matrix products, arithmetic and copies ran while one was open for 6% -> 7% of each run, Pallas kernels for 12% -> 13%
where the time goes in v11:
time: 337 us; the launch traced here: 333 us
  waiting for transfers between devices  174 us (52%)
  starting transfers between devices  60.1 us (18%)
  Pallas kernels  51.4 us (15%)
  other arithmetic  18.6 us (6%)
  between operations  15.2 us (5%)
  local copies, waits for them, and re-layouts  9.98 us (3%)
  matrix products  3.45 us (1%)
    ppermute x3, waiting for transfers between devices, sum_step(): above = lax.ppermute(sends[0], 'tensor', [(i, i + 1) for i in range(step)])  46.6 us
    pallas_call x2, Pallas kernels, ffn(): pl.pallas_call(functools.partial(ffn_kernel, ins), grid_spec=pltpu.Prefet...  44.6 us
    ppermute x6, waiting for transfers between devices, slots_sum(): lax.ppermute(product[o], 'tensor', [(i, (i + o) % count) for i in range(c...  40.8 us
    ppermute x26, waiting for transfers between devices, swap(): lax.ppermute(value, axis, [(i, i ^ distance) for i in range(lax.axis_size...  39.5 us
    ppermute x6, waiting for transfers between devices, from_slots(): lax.ppermute(value, 'tensor', [(i, (i - o) % count) for i in range(count)])  25.9 us
    ppermute x6, starting transfers between devices, slots_sum(): lax.ppermute(product[o], 'tensor', [(i, (i + o) % count) for i in range(c...  17.6 us
    all_gather x1, waiting for transfers between devices, per_device(): x = lax.all_gather(normed, ('section', 'tensor'), axis=0, tiled=False)  16.5 us
    ppermute x26, starting transfers between devices, swap(): lax.ppermute(value, axis, [(i, i ^ distance) for i in range(lax.axis_size...  16.4 us
  transfers between devices with their start and end apart: 45, of which 26 were waited for; matrix products, arithmetic and copies ran while one was open for 7% of the time, Pallas kernels for 13%

profile of v11, /device:TPU:0, one launch (start us, length us, event | category | flops | bytes accessed | tf_op | source)
XLA Modules:
  0.0 333.1 jit_solution(1788233661807175270)
XLA Ops:
  7.2 1.6 fusion.3
  8.9 2.5 fusion.5
  12.2 0.9 collective-permute-done
  13.2 3.0 collective-permute-start.3
  16.1 2.6 collective-permute-start.2
  18.7 1.3 collective-permute-start.1
  20.1 2.5 collective-permute-done.3
  22.6 8.8 %collective-permute-done.2 = bf16[32,2048]{1,0:T(8,128)(2,1)S(1)} collective-permute-done((bf16[32,2048]{1,0:T(8,128)(2,1)S(1)}, bf16[32,2048]{1,0:T(8,128)(2,1)S(1)}, u32[]{:S(2)}, u32[]{:S(2)}) %collective-permute-start.2) | collective-permute-done | bytes 131104 | tf_op jit(solution)/shard_map/ppermute | solution.py:36
  31.4 1.5 convolution_bitcast_fusion
  33.9 1.5 collective-permute-done.4
  36.2 12.9 %collective-permute-start.7 = (bf16[32,2048]{1,0:T(8,128)(2,1)S(1)}, bf16[32,2048]{1,0:T(8,128)(2,1)S(1)}, u32[]{:S(2)}, u32[]{:S(2)}) collective-permute-start(bf16[32,2048]{1,0:T(8,128)(2,1)S(1)} %get-tuple-element.86), channel_id=1, source_target_pairs={{0,3},{1,0},{2,1},{3,2},{4,7},{5,4},{6,5},{7,6},{8,11},{9,8},{10,9... | collective-permute-start | bytes 393224 | tf_op jit(solution)/shard_map/ppermute | solution.py:69
  49.8 8.0 %collective-permute-done.7 = bf16[32,2048]{1,0:T(8,128)(2,1)S(1)} collective-permute-done((bf16[32,2048]{1,0:T(8,128)(2,1)S(1)}, bf16[32,2048]{1,0:T(8,128)(2,1)S(1)}, u32[]{:S(2)}, u32[]{:S(2)}) %collective-permute-start.7) | collective-permute-done | bytes 131104 | tf_op jit(solution)/shard_map/ppermute | solution.py:69
  57.8 20.9 %collective-permute-done.6 = bf16[32,2048]{1,0:T(8,128)(2,1)S(1)} collective-permute-done((bf16[32,2048]{1,0:T(8,128)(2,1)S(1)}, bf16[32,2048]{1,0:T(8,128)(2,1)S(1)}, u32[]{:S(2)}, u32[]{:S(2)}) %collective-permute-start.6) | collective-permute-done | bytes 131104 | tf_op jit(solution)/shard_map/ppermute | solution.py:69
  78.8 1.9 copy.38
  81.7 3.5 %collective-permute-done.9 = bf16[16,2048]{1,0:T(8,128)(2,1)S(1)} collective-permute-done((bf16[16,2048]{1,0:T(8,128)(2,1)S(1)}, bf16[16,2048]{1,0:T(8,128)(2,1)S(1)}, u32[]{:S(2)}, u32[]{:S(2)}) %collective-permute-start.9) | collective-permute-done | bytes 65568 | tf_op jit(solution)/shard_map/ppermute | solution.py:30
  85.4 3.9 %collective-permute-start.10 = (bf16[32,2048]{1,0:T(8,128)(2,1)S(1)}, bf16[32,2048]{1,0:T(8,128)(2,1)S(1)}, u32[]{:S(2)}, u32[]{:S(2)}) collective-permute-start(bf16[32,2048]{1,0:T(8,128)(2,1)S(1)} %maximum_select_fusion.3), channel_id=1, source_target_pairs={{0,3},{1,0},{2,1},{3,2},{4,7},{5,4},{6,5},{7,6},{8,11},{9,8},{10,9... | collective-permute-start | bytes 393224 | tf_op jit(solution)/shard_map/ppermute | solution.py:36
  89.3 7.0 %collective-permute-done.12 = bf16[32,2048]{1,0:T(8,128)(2,1)S(1)} collective-permute-done((bf16[32,2048]{1,0:T(8,128)(2,1)S(1)}, bf16[32,2048]{1,0:T(8,128)(2,1)S(1)}, u32[]{:S(2)}, u32[]{:S(2)}) %collective-permute-start.12) | collective-permute-done | bytes 131104 | tf_op jit(solution)/shard_map/ppermute | solution.py:36
  96.3 7.6 %collective-permute-done.11 = bf16[32,2048]{1,0:T(8,128)(2,1)S(1)} collective-permute-done((bf16[32,2048]{1,0:T(8,128)(2,1)S(1)}, bf16[32,2048]{1,0:T(8,128)(2,1)S(1)}, u32[]{:S(2)}, u32[]{:S(2)}) %collective-permute-start.11) | collective-permute-done | bytes 131104 | tf_op jit(solution)/shard_map/ppermute | solution.py:36
  104.5 1.2 collective-permute-done.13
  105.8 16.5 %all-gather.3.cloned.1.call-done = bf16[1024,4096]{1,0:T(8,128)(2,1)} async-done(((bf16[128,4096]{1,0:T(8,128)(2,1)}), bf16[1024,4096]{1,0:T(8,128)(2,1)}) %all-gather.3.cloned.1.call-update) | async-done | bytes 8388624 | tf_op jit(solution)/shard_map/all_gather | solution.py:290
  122.2 1.6 collective-permute-start.17
  123.8 1.9 collective-permute-start.16
  125.7 0.9 collective-permute-start.15
  126.7 22.2 %ffn.2 = bf16[512,4096]{1,0:T(8,128)(2,1)S(1)} custom-call(s32[5]{0:T(128)S(1)} %get-tuple-element.101.order, bf16[2,4,128,4096]{3,2,1,0:T(8,128)(2,1)} %bitcast.83, bf16[4096,1024]{1,0:T(8,128)(2,1)} %gate_ref.3, bf16[4096,1024]{1,0:T(8,128)(2,1)} %up_ref.3, bf16[1024,4096]{1,0:T(8,128)(2,1)} %down_ref.3), custom_call_target="tpu_custom_call" | custom-call | flops 1024 | bytes 1024 | tf_op jit(solution)/shard_map/ffn/pallas_call | solution.py:149
  148.9 4.1 %collective-permute-done.15 = bf16[128,256]{1,0:T(8,128)(2,1)S(1)} collective-permute-done((bf16[128,256]{1,0:T(8,128)(2,1)S(1)}, bf16[128,256]{1,0:T(8,128)(2,1)S(1)}, u32[]{:S(2)}, u32[]{:S(2)}) %collective-permute-start.15) | collective-permute-done | bytes 65568 | tf_op jit(solution)/shard_map/ppermute | solution.py:30
  153.1 1.1 pad_maximum_fusion.1
  154.2 22.4 %ffn.3 = bf16[512,4096]{1,0:T(8,128)(2,1)S(1)} custom-call(s32[5]{0:T(128)S(1)} %get-tuple-element.100.order, bf16[2,4,128,4096]{3,2,1,0:T(8,128)(2,1)} %bitcast.84, bf16[4096,1024]{1,0:T(8,128)(2,1)} %gate_ref.3, bf16[4096,1024]{1,0:T(8,128)(2,1)} %up_ref.3, bf16[1024,4096]{1,0:T(8,128)(2,1)} %down_ref.3), custom_call_target="tpu_custom_call" | custom-call | flops 1024 | bytes 1024 | tf_op jit(solution)/shard_map/ffn/pallas_call | solution.py:149
  176.6 3.4 %collective-permute-done.19 = bf16[2,2,512,256]{3,2,1,0:T(8,128)(2,1)} collective-permute-done((bf16[2,2,512,256]{3,2,1,0:T(8,128)(2,1)}, bf16[2,2,512,256]{3,2,1,0:T(8,128)(2,1)}, u32[]{:S(2)}, u32[]{:S(2)}) %collective-permute-start.19) | collective-permute-done | bytes 1048608 | tf_op jit(solution)/shard_map/ppermute | solution.py:30
  180.0 0.9 fusion.7
  180.9 2.3 collective-permute-start.21
  183.2 0.7 collective-permute-start.22
  183.9 1.1 slice.188
  185.0 1.4 pad_maximum_fusion.refs_2_
  186.4 1.6 collective-permute-start.23
  188.0 1.5 collective-permute-start.24
  189.5 16.1 %collective-permute-done.21 = bf16[128,4096]{1,0:T(8,128)(2,1)S(1)} collective-permute-done((bf16[128,4096]{1,0:T(8,128)(2,1)S(1)}, bf16[128,4096]{1,0:T(8,128)(2,1)S(1)}, u32[]{:S(2)}, u32[]{:S(2)}) %collective-permute-start.21) | collective-permute-done | bytes 1048608 | tf_op jit(solution)/shard_map/ppermute | solution.py:59
  205.6 0.7 add_convert_fusion.2
  206.3 16.0 %collective-permute-done.23.refs_3_ = bf16[3,2,512,256]{3,2,1,0:T(8,128)(2,1)S(1)} collective-permute-done((bf16[3,2,512,256]{3,2,1,0:T(8,128)(2,1)S(1)}, bf16[3,2,512,256]{3,2,1,0:T(8,128)(2,1)S(1)}, u32[]{:S(2)}, u32[]{:S(2)}) %collective-permute-start.23) | collective-permute-done | bytes 1572896 | tf_op jit(solution)/shard_map/ppermute | solution.py:30
  222.4 1.2 collective-permute-done.24.refs_4_
  223.6 1.6 collective-permute-start.25
  225.2 1.0 collective-permute-start.26
  226.2 0.6 collective-permute-start.27
  226.9 1.6 collective-permute-start.28
  228.5 17.9 %collective-permute-done.25 = bf16[128,4096]{1,0:T(8,128)(2,1)S(1)} collective-permute-done((bf16[128,4096]{1,0:T(8,128)(2,1)S(1)}, bf16[128,4096]{1,0:T(8,128)(2,1)S(1)}, u32[]{:S(2)}, u32[]{:S(2)}) %collective-permute-start.25) | collective-permute-done | bytes 1048608 | tf_op jit(solution)/shard_map/ppermute | solution.py:59
  246.4 2.5 add_convert_fusion
  248.9 8.4 %collective-permute-start.29 = (bf16[128,4096]{1,0:T(8,128)(2,1)}, bf16[128,4096]{1,0:T(8,128)(2,1)}, u32[]{:S(2)}, u32[]{:S(2)}) collective-permute-start(bf16[128,4096]{1,0:T(8,128)(2,1)} %get-tuple-element.45), channel_id=1, source_target_pairs={{0,1},{1,2},{2,3},{4,5},{5,6},{6,7},{8,9},{9,10},{10,11},{12,13},{... | collective-permute-start | bytes 3145736 | tf_op jit(solution)/shard_map/ppermute | solution.py:59
  257.3 1.3 collective-permute-start.30
  258.5 1.6 shift_right_arithmetic.40
  260.2 3.0 copy.29
  264.1 12.6 %collective-permute-done.29 = bf16[128,4096]{1,0:T(8,128)(2,1)} collective-permute-done((bf16[128,4096]{1,0:T(8,128)(2,1)}, bf16[128,4096]{1,0:T(8,128)(2,1)}, u32[]{:S(2)}, u32[]{:S(2)}) %collective-permute-start.29) | collective-permute-done | bytes 1048608 | tf_op jit(solution)/shard_map/ppermute | solution.py:59
  276.7 5.1 %collective-permute-done.30 = bf16[128,4096]{1,0:T(8,128)(2,1)} collective-permute-done((bf16[128,4096]{1,0:T(8,128)(2,1)}, bf16[128,4096]{1,0:T(8,128)(2,1)}, u32[]{:S(2)}, u32[]{:S(2)}) %collective-permute-start.30) | collective-permute-done | bytes 1048608 | tf_op jit(solution)/shard_map/ppermute | solution.py:60
  281.8 4.2 %fusion = (f32[128]{0:T(128)S(1)}, bf16[128,4096]{1,0:T(8,128)(2,1)S(1)}) fusion(bf16[128,4096]{1,0:T(8,128)(2,1)} %collective-permute-done.30, bf16[128,4096]{1,0:T(8,128)(2,1)} %collective-permute-done.29, bf16[512,4096]{1,0:T(8,128)(2,1)} %copy-done.10, bf16[512,4096]{1,0:T(8,128)(2,1)} %copy-done.2, s32[128,4096]{1,0:T(8,128)} %bitcast.86, ...), kind=kLoop, calls=%fused_computation.7 | loop fusion | flops 9437056 | bytes 8405504 | tf_op jit(solution)/shard_map/reduce_sum | solution.py:18
  287.0 0.8 copy-done.4
  287.8 6.8 %attend_own_keys.1 = bf16[4,128,384]{2,1,0:T(8,128)(2,1)S(1)} custom-call(s32[16]{0:T(128)S(1)} %pad_add_fusion.3.table, bf16[128,4096]{1,0:T(8,128)(2,1)S(1)} %fusion.2.mem_ref, bf16[4,128,256]{2,1,0:T(8,128)(2,1)S(1)} %pad_maximum_fusion.4.cq_ref, bf16[2,2048,256]{2,1,0:T(8,128)(2,1)S(1)} %bitcast.82, ...), custom_call_target="tpu_custom_call" | custom-call | flops 1024 | bytes 1024 | tf_op jit(solution)/shard_map/attend_own_keys/pallas_call | solution.py:232
  294.8 4.3 %collective-permute-start.38 = (bf16[128,384]{1,0:T(8,128)(2,1)S(1)}, bf16[128,384]{1,0:T(8,128)(2,1)S(1)}, u32[]{:S(2)}, u32[]{:S(2)}) collective-permute-start(bf16[128,384]{1,0:T(8,128)(2,1)S(1)} %get-tuple-element.89), channel_id=1, source_target_pairs={{0,3},{1,2},{2,1},{3,0},{4,7},{5,6},{6,5},{7,4},{8,11},{9,10},{10,... | collective-permute-start | bytes 294920 | tf_op jit(solution)/shard_map/ppermute | solution.py:30
  299.1 3.6 %collective-permute-done.36 = bf16[128,384]{1,0:T(8,128)(2,1)S(1)} collective-permute-done((bf16[128,384]{1,0:T(8,128)(2,1)S(1)}, bf16[128,384]{1,0:T(8,128)(2,1)S(1)}, u32[]{:S(2)}, u32[]{:S(2)}) %collective-permute-start.36) | collective-permute-done | bytes 98336 | tf_op jit(solution)/shard_map/ppermute | solution.py:30
  302.9 1.4 collective-permute-done.38
  305.4 1.5 collective-permute-done.39
  307.6 2.2 collective-permute-start.42
  309.8 1.8 collective-permute-start.41
  311.6 2.3 collective-permute-done.42
  314.0 9.6 %collective-permute-done.41 = bf16[32,2048]{1,0:T(8,128)(2,1)S(1)} collective-permute-done((bf16[32,2048]{1,0:T(8,128)(2,1)S(1)}, bf16[32,2048]{1,0:T(8,128)(2,1)S(1)}, u32[]{:S(2)}, u32[]{:S(2)}) %collective-permute-start.41) | collective-permute-done | bytes 131104 | tf_op jit(solution)/shard_map/ppermute | solution.py:69
  324.0 1.1 collective-permute-done.43
  325.1 0.7 fusion.25
  (148 shorter events, 9.7 us)
Async XLA Ops:
  7.2 28.5 %copy-start = (bf16[256,2048]{1,0:T(8,128)(2,1)S(1)}, bf16[256,2048]{1,0:T(8,128)(2,1)}, u32[]{:S(2)}) copy-start(bf16[256,2048]{1,0:T(8,128)(2,1)} %param.28) | copy-start | bytes 3145732
  7.2 4.2 %copy-start.12 = (bf16[16,4096]{1,0:T(8,128)(2,1)S(1)}, bf16[16,4096]{1,0:T(8,128)(2,1)}, u32[]{:S(2)}) copy-start(bf16[16,4096]{1,0:T(8,128)(2,1)} %param.25) | copy-start | bytes 393220
  7.2 4.4 %copy-start.16 = (f32[4096]{0:T(1024)S(1)}, f32[4096]{0:T(1024)}, u32[]{:S(2)}) copy-start(f32[4096]{0:T(1024)} %param.26) | copy-start | bytes 49156
  7.2 115.0 %all-gather.3.cloned.1.call-start = ((), (), s32[]{:S(2)}) async-start(), calls=%async_computation | async-start | bytes 9437184 | tf_op jit(solution)/shard_map/all_gather | solution.py:290
  11.7 1.4 collective-permute-start
  13.2 9.4 %collective-permute-start.3 = (bf16[32,2048]{1,0:T(8,128)(2,1)S(1)}, bf16[32,2048]{1,0:T(8,128)(2,1)S(1)}, u32[]{:S(2)}, u32[]{:S(2)}) collective-permute-start(bf16[32,2048]{1,0:T(8,128)(2,1)S(1)} %maximum_select_fusion.2), channel_id=1, source_target_pairs={{0,1},{1,2},{2,3},{3,0},{4,5},{5,6},{6,7},{7,4},{8,9},{9,10},{10,1... | collective-permute-start | bytes 393224 | tf_op jit(solution)/shard_map/ppermute | solution.py:36
  16.1 15.2 %collective-permute-start.2 = (bf16[32,2048]{1,0:T(8,128)(2,1)S(1)}, bf16[32,2048]{1,0:T(8,128)(2,1)S(1)}, u32[]{:S(2)}, u32[]{:S(2)}) collective-permute-start(bf16[32,2048]{1,0:T(8,128)(2,1)S(1)} %maximum_select_fusion.2), channel_id=1, source_target_pairs={{0,2},{1,3},{2,0},{3,1},{4,6},{5,7},{6,4},{7,5},{8,10},{9,11},{10,... | collective-permute-start | bytes 393224 | tf_op jit(solution)/shard_map/ppermute | solution.py:36
  18.7 12.6 %collective-permute-start.1 = (bf16[32,2048]{1,0:T(8,128)(2,1)S(1)}, bf16[32,2048]{1,0:T(8,128)(2,1)S(1)}, u32[]{:S(2)}, u32[]{:S(2)}) collective-permute-start(bf16[32,2048]{1,0:T(8,128)(2,1)S(1)} %maximum_select_fusion.2), channel_id=1, source_target_pairs={{0,3},{1,0},{2,1},{3,2},{4,7},{5,4},{6,5},{7,6},{8,11},{9,8},{10,9... | collective-permute-start | bytes 393224 | tf_op jit(solution)/shard_map/ppermute | solution.py:36
  20.1 12.8 %copy-start.18 = (bf16[2048,3,256]{2,0,1:T(8,128)(2,1)S(1)}, bf16[2048,3,256]{2,0,1:T(8,128)(2,1)}, u32[]{:S(2)}) copy-start(bf16[2048,3,256]{2,0,1:T(8,128)(2,1)} %param.27) | copy-start | bytes 9437188
  33.6 1.8 collective-permute-start.4
  36.2 21.6 %collective-permute-start.7 = (bf16[32,2048]{1,0:T(8,128)(2,1)S(1)}, bf16[32,2048]{1,0:T(8,128)(2,1)S(1)}, u32[]{:S(2)}, u32[]{:S(2)}) collective-permute-start(bf16[32,2048]{1,0:T(8,128)(2,1)S(1)} %get-tuple-element.86), channel_id=1, source_target_pairs={{0,3},{1,0},{2,1},{3,2},{4,7},{5,4},{6,5},{7,6},{8,11},{9,8},{10,9... | collective-permute-start | bytes 393224 | tf_op jit(solution)/shard_map/ppermute | solution.py:69
  49.1 29.5 %collective-permute-start.6 = (bf16[32,2048]{1,0:T(8,128)(2,1)S(1)}, bf16[32,2048]{1,0:T(8,128)(2,1)S(1)}, u32[]{:S(2)}, u32[]{:S(2)}) collective-permute-start(bf16[32,2048]{1,0:T(8,128)(2,1)S(1)} %get-tuple-element.87), channel_id=1, source_target_pairs={{0,2},{1,3},{2,0},{3,1},{4,6},{5,7},{6,4},{7,5},{8,10},{9,11},{10,... | collective-permute-start | bytes 393224 | tf_op jit(solution)/shard_map/ppermute | solution.py:69
  49.4 29.2 %collective-permute-start.5 = (bf16[32,2048]{1,0:T(8,128)(2,1)S(1)}, bf16[32,2048]{1,0:T(8,128)(2,1)S(1)}, u32[]{:S(2)}, u32[]{:S(2)}) collective-permute-start(bf16[32,2048]{1,0:T(8,128)(2,1)S(1)} %get-tuple-element.85), channel_id=1, source_target_pairs={{0,1},{1,2},{2,3},{3,0},{4,5},{5,6},{6,7},{7,4},{8,9},{9,10},{10,1... | collective-permute-start | bytes 393224 | tf_op jit(solution)/shard_map/ppermute | solution.py:69
  78.7 2.7 copy-start.17
  78.7 25.2 %copy-start.19 = (bf16[2048,256]{1,0:T(8,128)(2,1)S(1)}, bf16[2048,256]{1,0:T(8,128)(2,1)}, u32[]{:S(2)}) copy-start(bf16[2048,256]{1,0:T(8,128)(2,1)} %param.30) | copy-start | bytes 3145732
  78.8 2.5 collective-permute-start.8
  80.8 25.0 %collective-permute-start.14 = (bf16[2,2048,256]{2,1,0:T(8,128)(2,1)S(1)}, bf16[2,2048,256]{2,1,0:T(8,128)(2,1)}, u32[]{:S(2)}, u32[]{:S(2)}) collective-permute-start(bf16[2,2048,256]{2,1,0:T(8,128)(2,1)S(1)} %bitcast.81), channel_id=1, source_target_pairs={{0,4},{4,0},{1,5},{5,1},{2,6},{6,2},{3,7},{7,3},{8,12},{12,8},{9,1... | collective-permute-start | bytes 6291464 | tf_op jit(solution)/shard_map/ppermute | solution.py:30
  81.6 3.7 %collective-permute-start.9 = (bf16[16,2048]{1,0:T(8,128)(2,1)S(1)}, bf16[16,2048]{1,0:T(8,128)(2,1)S(1)}, u32[]{:S(2)}, u32[]{:S(2)}) collective-permute-start(bf16[16,2048]{1,0:T(8,128)(2,1)S(1)} %get-tuple-element.97), channel_id=1, source_target_pairs={{0,4},{4,0},{1,5},{5,1},{2,6},{6,2},{3,7},{7,3},{8,12},{12,8},{9,1... | collective-permute-start | bytes 196616 | tf_op jit(solution)/shard_map/ppermute | solution.py:30
  85.3 11.0 %collective-permute-start.12 = (bf16[32,2048]{1,0:T(8,128)(2,1)S(1)}, bf16[32,2048]{1,0:T(8,128)(2,1)S(1)}, u32[]{:S(2)}, u32[]{:S(2)}) collective-permute-start(bf16[32,2048]{1,0:T(8,128)(2,1)S(1)} %maximum_select_fusion.3), channel_id=1, source_target_pairs={{0,1},{1,2},{2,3},{3,0},{4,5},{5,6},{6,7},{7,4},{8,9},{9,10},{10,1... | collective-permute-start | bytes 393224 | tf_op jit(solution)/shard_map/ppermute | solution.py:36
  85.3 18.6 %collective-permute-start.11 = (bf16[32,2048]{1,0:T(8,128)(2,1)S(1)}, bf16[32,2048]{1,0:T(8,128)(2,1)S(1)}, u32[]{:S(2)}, u32[]{:S(2)}) collective-permute-start(bf16[32,2048]{1,0:T(8,128)(2,1)S(1)} %maximum_select_fusion.3), channel_id=1, source_target_pairs={{0,2},{1,3},{2,0},{3,1},{4,6},{5,7},{6,4},{7,5},{8,10},{9,11},{10,... | collective-permute-start | bytes 393224 | tf_op jit(solution)/shard_map/ppermute | solution.py:36
  85.4 18.5 %collective-permute-start.10 = (bf16[32,2048]{1,0:T(8,128)(2,1)S(1)}, bf16[32,2048]{1,0:T(8,128)(2,1)S(1)}, u32[]{:S(2)}, u32[]{:S(2)}) collective-permute-start(bf16[32,2048]{1,0:T(8,128)(2,1)S(1)} %maximum_select_fusion.3), channel_id=1, source_target_pairs={{0,3},{1,0},{2,1},{3,2},{4,7},{5,4},{6,5},{7,6},{8,11},{9,8},{10,9... | collective-permute-start | bytes 393224 | tf_op jit(solution)/shard_map/ppermute | solution.py:36
  104.3 1.4 collective-permute-start.13
  122.2 30.8 %collective-permute-start.18 = (bf16[1,2,512,256]{3,2,1,0:T(8,128)(2,1)S(1)}, bf16[1,2,512,256]{3,2,1,0:T(8,128)(2,1)S(1)}, u32[]{:S(2)}, u32[]{:S(2)}) collective-permute-start(bf16[1,2,512,256]{3,2,1,0:T(8,128)(2,1)S(1)} %dynamic-slice_bitcast_fusion), channel_id=1, source_target_pairs={{0,2},{1,3},{2,0},{3,1},{4,6},{5,7},{6,4},{7,5},{8,10},{9,11},{10,... | collective-permute-start | bytes 1572872 | tf_op jit(solution)/shard_map/ppermute | solution.py:30
  122.2 26.7 %collective-permute-start.17 = (bf16[128,256]{1,0:T(8,128)(2,1)S(1)}, bf16[128,256]{1,0:T(8,128)(2,1)S(1)}, u32[]{:S(2)}, u32[]{:S(2)}) collective-permute-start(bf16[128,256]{1,0:T(8,128)(2,1)S(1)} %bitcast.93), channel_id=1, source_target_pairs={{0,3},{1,2},{2,1},{3,0},{4,7},{5,6},{6,5},{7,4},{8,11},{9,10},{10,... | collective-permute-start | bytes 196616 | tf_op jit(solution)/shard_map/ppermute | solution.py:30
  123.8 25.1 %collective-permute-start.16 = (bf16[128,256]{1,0:T(8,128)(2,1)S(1)}, bf16[128,256]{1,0:T(8,128)(2,1)S(1)}, u32[]{:S(2)}, u32[]{:S(2)}) collective-permute-start(bf16[128,256]{1,0:T(8,128)(2,1)S(1)} %bitcast.94), channel_id=1, source_target_pairs={{0,1},{1,0},{2,3},{3,2},{4,5},{5,4},{6,7},{7,6},{8,9},{9,8},{10,11... | collective-permute-start | bytes 196616 | tf_op jit(solution)/shard_map/ppermute | solution.py:30
  125.7 27.3 %collective-permute-start.15 = (bf16[128,256]{1,0:T(8,128)(2,1)S(1)}, bf16[128,256]{1,0:T(8,128)(2,1)S(1)}, u32[]{:S(2)}, u32[]{:S(2)}) collective-permute-start(bf16[128,256]{1,0:T(8,128)(2,1)S(1)} %bitcast.95), channel_id=1, source_target_pairs={{0,2},{1,3},{2,0},{3,1},{4,6},{5,7},{6,4},{7,5},{8,10},{9,11},{10,... | collective-permute-start | bytes 196616 | tf_op jit(solution)/shard_map/ppermute | solution.py:30
  154.1 25.9 %collective-permute-start.20 = (bf16[512,4096]{1,0:T(8,128)(2,1)S(1)}, bf16[512,4096]{1,0:T(8,128)(2,1)S(1)}, u32[]{:S(2)}, u32[]{:S(2)}) collective-permute-start(bf16[512,4096]{1,0:T(8,128)(2,1)S(1)} %ffn.2), channel_id=1, source_target_pairs={{0,4},{4,0},{1,5},{5,1},{2,6},{6,2},{3,7},{7,3},{8,12},{12,8},{9,1... | collective-permute-start | bytes 12582920 | tf_op jit(solution)/shard_map/ppermute | solution.py:30
  154.2 25.8 %collective-permute-start.19 = (bf16[2,2,512,256]{3,2,1,0:T(8,128)(2,1)}, bf16[2,2,512,256]{3,2,1,0:T(8,128)(2,1)}, u32[]{:S(2)}, u32[]{:S(2)}) collective-permute-start(bf16[2,2,512,256]{3,2,1,0:T(8,128)(2,1)} %pad_maximum_fusion.1), channel_id=1, source_target_pairs={{0,1},{1,0},{2,3},{3,2},{4,5},{5,4},{6,7},{7,6},{8,9},{9,8},{10,11... | collective-permute-start | bytes 3145736 | tf_op jit(solution)/shard_map/ppermute | solution.py:30
  176.6 69.8 %copy-start.2 = (bf16[512,4096]{1,0:T(8,128)(2,1)}, bf16[512,4096]{1,0:T(8,128)(2,1)S(1)}, u32[]{:S(2)}) copy-start(bf16[512,4096]{1,0:T(8,128)(2,1)S(1)} %ffn.3) | copy-start | bytes 12582916
  180.0 66.4 %copy-start.10 = (bf16[512,4096]{1,0:T(8,128)(2,1)}, bf16[512,4096]{1,0:T(8,128)(2,1)S(1)}, u32[]{:S(2)}) copy-start(bf16[512,4096]{1,0:T(8,128)(2,1)S(1)} %collective-permute-done.20) | copy-start | bytes 12582916
  180.9 24.6 %collective-permute-start.21 = (bf16[128,4096]{1,0:T(8,128)(2,1)S(1)}, bf16[128,4096]{1,0:T(8,128)(2,1)S(1)}, u32[]{:S(2)}, u32[]{:S(2)}) collective-permute-start(bf16[128,4096]{1,0:T(8,128)(2,1)S(1)} %get-tuple-element.79), channel_id=1, source_target_pairs={{0,1},{4,5},{8,9},{12,13},{16,17},{20,21},{24,25},{28,29}} | collective-permute-start | bytes 3145736 | tf_op jit(solution)/shard_map/ppermute | solution.py:59
  183.2 22.4 %collective-permute-start.22 = (bf16[128,4096]{1,0:T(8,128)(2,1)S(1)}, bf16[128,4096]{1,0:T(8,128)(2,1)S(1)}, u32[]{:S(2)}, u32[]{:S(2)}) collective-permute-start(bf16[128,4096]{1,0:T(8,128)(2,1)S(1)} %get-tuple-element.78), channel_id=1, source_target_pairs={{3,2},{7,6},{11,10},{15,14},{19,18},{23,22},{27,26},{31,30}} | collective-permute-start | bytes 3145736 | tf_op jit(solution)/shard_map/ppermute | solution.py:60
  186.4 19.9 %copy-start.3 = (bf16[3,2,512,256]{3,2,1,0:T(8,128)(2,1)}, bf16[3,2,512,256]{3,2,1,0:T(8,128)(2,1)S(1)}, u32[]{:S(2)}) copy-start(bf16[3,2,512,256]{3,2,1,0:T(8,128)(2,1)S(1)} %pad_maximum_fusion.refs_2_) | copy-start | bytes 4718596
  186.4 36.0 %collective-permute-start.23 = (bf16[3,2,512,256]{3,2,1,0:T(8,128)(2,1)S(1)}, bf16[3,2,512,256]{3,2,1,0:T(8,128)(2,1)S(1)}, u32[]{:S(2)}, u32[]{:S(2)}) collective-permute-start(bf16[3,2,512,256]{3,2,1,0:T(8,128)(2,1)S(1)} %pad_maximum_fusion.refs_2_), channel_id=1, source_target_pairs={{0,8},{8,0},{16,24},{24,16},{1,9},{9,1},{17,25},{25,17},{2,10},{10... | collective-permute-start | bytes 4718600 | tf_op jit(solution)/shard_map/ppermute | solution.py:30
  188.0 35.6 %collective-permute-start.24 = (bf16[3,2,512,256]{3,2,1,0:T(8,128)(2,1)S(1)}, bf16[3,2,512,256]{3,2,1,0:T(8,128)(2,1)S(1)}, u32[]{:S(2)}, u32[]{:S(2)}) collective-permute-start(bf16[3,2,512,256]{3,2,1,0:T(8,128)(2,1)S(1)} %pad_maximum_fusion.refs_2_), channel_id=1, source_target_pairs={{0,16},{8,24},{16,0},{24,8},{1,17},{9,25},{17,1},{25,9},{2,18},{10... | collective-permute-start | bytes 4718600 | tf_op jit(solution)/shard_map/ppermute | solution.py:30
  222.4 26.5 %copy-start.5 = (bf16[3,2,512,256]{3,2,1,0:T(8,128)(2,1)}, bf16[3,2,512,256]{3,2,1,0:T(8,128)(2,1)S(1)}, u32[]{:S(2)}) copy-start(bf16[3,2,512,256]{3,2,1,0:T(8,128)(2,1)S(1)} %collective-permute-done.23.refs_3_) | copy-start | bytes 4718596
  223.6 25.3 %copy-start.7 = (bf16[3,2,512,256]{3,2,1,0:T(8,128)(2,1)}, bf16[3,2,512,256]{3,2,1,0:T(8,128)(2,1)S(1)}, u32[]{:S(2)}) copy-start(bf16[3,2,512,256]{3,2,1,0:T(8,128)(2,1)S(1)} %collective-permute-done.24.refs_4_) | copy-start | bytes 4718596
  223.6 22.8 %collective-permute-start.25 = (bf16[128,4096]{1,0:T(8,128)(2,1)S(1)}, bf16[128,4096]{1,0:T(8,128)(2,1)S(1)}, u32[]{:S(2)}, u32[]{:S(2)}) collective-permute-start(bf16[128,4096]{1,0:T(8,128)(2,1)S(1)} %get-tuple-element.39), channel_id=1, source_target_pairs={{0,1},{1,2},{4,5},{5,6},{8,9},{9,10},{12,13},{13,14},{16,17},{17,1... | collective-permute-start | bytes 3145736 | tf_op jit(solution)/shard_map/ppermute | solution.py:59
  225.2 21.2 %collective-permute-start.26 = (bf16[128,4096]{1,0:T(8,128)(2,1)S(1)}, bf16[128,4096]{1,0:T(8,128)(2,1)S(1)}, u32[]{:S(2)}, u32[]{:S(2)}) collective-permute-start(bf16[128,4096]{1,0:T(8,128)(2,1)S(1)} %get-tuple-element.40), channel_id=1, source_target_pairs={{2,1},{3,2},{6,5},{7,6},{10,9},{11,10},{14,13},{15,14},{18,17},{19... | collective-permute-start | bytes 3145736 | tf_op jit(solution)/shard_map/ppermute | solution.py:60
  226.2 22.7 %collective-permute-start.27 = (bf16[3,1,512,256]{3,2,1,0:T(8,128)(2,1)S(1)}, bf16[3,1,512,256]{3,2,1,0:T(8,128)(2,1)}, u32[]{:S(2)}, u32[]{:S(2)}) collective-permute-start(bf16[3,1,512,256]{3,2,1,0:T(8,128)(2,1)S(1)} %slice.189), channel_id=1, source_target_pairs={{0,8},{8,0},{16,24},{24,16},{1,9},{9,1},{17,25},{25,17},{2,10},{10... | collective-permute-start | bytes 2359304 | tf_op jit(solution)/shard_map/ppermute | solution.py:30
  226.9 22.0 %collective-permute-start.28 = (bf16[3,1,512,256]{3,2,1,0:T(8,128)(2,1)S(1)}, bf16[3,1,512,256]{3,2,1,0:T(8,128)(2,1)}, u32[]{:S(2)}, u32[]{:S(2)}) collective-permute-start(bf16[3,1,512,256]{3,2,1,0:T(8,128)(2,1)S(1)} %slice.190), channel_id=1, source_target_pairs={{0,16},{8,24},{16,0},{24,8},{1,17},{9,25},{17,1},{25,9},{2,18},{10... | collective-permute-start | bytes 2359304 | tf_op jit(solution)/shard_map/ppermute | solution.py:30
  248.9 27.8 %collective-permute-start.29 = (bf16[128,4096]{1,0:T(8,128)(2,1)}, bf16[128,4096]{1,0:T(8,128)(2,1)}, u32[]{:S(2)}, u32[]{:S(2)}) collective-permute-start(bf16[128,4096]{1,0:T(8,128)(2,1)} %get-tuple-element.45), channel_id=1, source_target_pairs={{0,1},{1,2},{2,3},{4,5},{5,6},{6,7},{8,9},{9,10},{10,11},{12,13},{... | collective-permute-start | bytes 3145736 | tf_op jit(solution)/shard_map/ppermute | solution.py:59
  257.3 24.5 %collective-permute-start.30 = (bf16[128,4096]{1,0:T(8,128)(2,1)}, bf16[128,4096]{1,0:T(8,128)(2,1)}, u32[]{:S(2)}, u32[]{:S(2)}) collective-permute-start(bf16[128,4096]{1,0:T(8,128)(2,1)} %get-tuple-element.46), channel_id=1, source_target_pairs={{1,0},{2,1},{3,2},{5,4},{6,5},{7,6},{9,8},{10,9},{11,10},{13,12},{... | collective-permute-start | bytes 3145736 | tf_op jit(solution)/shard_map/ppermute | solution.py:60
  260.2 21.6 %copy-start.9 = (bf16[128,4096]{1,0:T(8,128)(2,1)S(1)}, bf16[128,4096]{1,0:T(8,128)(2,1)}, u32[]{:S(2)}) copy-start(bf16[128,4096]{1,0:T(8,128)(2,1)} %param.18) | copy-start | bytes 3145732
  263.5 22.9 %collective-permute-start.31 = (bf16[3,2,512,256]{3,2,1,0:T(8,128)(2,1)}, bf16[3,2,512,256]{3,2,1,0:T(8,128)(2,1)S(1)}, u32[]{:S(2)}, u32[]{:S(2)}) collective-permute-start(bf16[3,2,512,256]{3,2,1,0:T(8,128)(2,1)} %copy-done.3), channel_id=1, source_target_pairs={{0,4},{4,0},{1,5},{5,1},{2,6},{6,2},{3,7},{7,3},{8,12},{12,8},{9,1... | collective-permute-start | bytes 4718600 | tf_op jit(solution)/shard_map/ppermute | solution.py:30
  263.5 22.9 %collective-permute-start.32 = (bf16[3,2,512,256]{3,2,1,0:T(8,128)(2,1)}, bf16[3,2,512,256]{3,2,1,0:T(8,128)(2,1)S(1)}, u32[]{:S(2)}, u32[]{:S(2)}) collective-permute-start(bf16[3,2,512,256]{3,2,1,0:T(8,128)(2,1)} %copy-done.5), channel_id=1, source_target_pairs={{0,4},{4,0},{1,5},{5,1},{2,6},{6,2},{3,7},{7,3},{8,12},{12,8},{9,1... | collective-permute-start | bytes 4718600 | tf_op jit(solution)/shard_map/ppermute | solution.py:30
  264.0 22.4 %collective-permute-start.33 = (bf16[3,2,512,256]{3,2,1,0:T(8,128)(2,1)}, bf16[3,2,512,256]{3,2,1,0:T(8,128)(2,1)S(1)}, u32[]{:S(2)}, u32[]{:S(2)}) collective-permute-start(bf16[3,2,512,256]{3,2,1,0:T(8,128)(2,1)} %copy-done.7), channel_id=1, source_target_pairs={{0,4},{4,0},{1,5},{5,1},{2,6},{6,2},{3,7},{7,3},{8,12},{12,8},{9,1... | collective-permute-start | bytes 4718600 | tf_op jit(solution)/shard_map/ppermute | solution.py:30
  276.7 9.7 %collective-permute-start.34 = (bf16[3,1,512,256]{3,2,1,0:T(8,128)(2,1)}, bf16[3,1,512,256]{3,2,1,0:T(8,128)(2,1)S(1)}, u32[]{:S(2)}, u32[]{:S(2)}) collective-permute-start(bf16[3,1,512,256]{3,2,1,0:T(8,128)(2,1)} %collective-permute-done.27.refs_5_), channel_id=1, source_target_pairs={{0,4},{4,0},{1,5},{5,1},{2,6},{6,2},{3,7},{7,3},{8,12},{12,8},{9,1... | collective-permute-start | bytes 2359304 | tf_op jit(solution)/shard_map/ppermute | solution.py:30
  281.7 5.2 %collective-permute-start.35 = (bf16[3,1,512,256]{3,2,1,0:T(8,128)(2,1)}, bf16[3,1,512,256]{3,2,1,0:T(8,128)(2,1)S(1)}, u32[]{:S(2)}, u32[]{:S(2)}) collective-permute-start(bf16[3,1,512,256]{3,2,1,0:T(8,128)(2,1)} %collective-permute-done.28.refs_6_), channel_id=1, source_target_pairs={{0,4},{4,0},{1,5},{5,1},{2,6},{6,2},{3,7},{7,3},{8,12},{12,8},{9,1... | collective-permute-start | bytes 2359304 | tf_op jit(solution)/shard_map/ppermute | solution.py:30
  281.7 4.3 %copy-start.15 = (f32[4096]{0:T(1024)S(1)}, f32[4096]{0:T(1024)}, u32[]{:S(2)}) copy-start(f32[4096]{0:T(1024)} %param.24) | copy-start | bytes 49156
  281.8 5.2 %copy-start.6 = (bf16[3,2,512,256]{3,2,1,0:T(8,128)(2,1)S(1)}, bf16[3,2,512,256]{3,2,1,0:T(8,128)(2,1)}, u32[]{:S(2)}) copy-start(bf16[3,2,512,256]{3,2,1,0:T(8,128)(2,1)} %copy-done.5) | copy-start | bytes 4718596
  281.8 5.2 %copy-start.8 = (bf16[3,2,512,256]{3,2,1,0:T(8,128)(2,1)S(1)}, bf16[3,2,512,256]{3,2,1,0:T(8,128)(2,1)}, u32[]{:S(2)}) copy-start(bf16[3,2,512,256]{3,2,1,0:T(8,128)(2,1)} %copy-done.7) | copy-start | bytes 4718596
  286.0 1.8 copy-start.4
  294.7 8.1 %collective-permute-start.36 = (bf16[128,384]{1,0:T(8,128)(2,1)S(1)}, bf16[128,384]{1,0:T(8,128)(2,1)S(1)}, u32[]{:S(2)}, u32[]{:S(2)}) collective-permute-start(bf16[128,384]{1,0:T(8,128)(2,1)S(1)} %get-tuple-element.91), channel_id=1, source_target_pairs={{0,2},{1,3},{2,0},{3,1},{4,6},{5,7},{6,4},{7,5},{8,10},{9,11},{10,... | collective-permute-start | bytes 294920 | tf_op jit(solution)/shard_map/ppermute | solution.py:30
  294.7 8.1 %collective-permute-start.37 = (bf16[128,384]{1,0:T(8,128)(2,1)S(1)}, bf16[128,384]{1,0:T(8,128)(2,1)S(1)}, u32[]{:S(2)}, u32[]{:S(2)}) collective-permute-start(bf16[128,384]{1,0:T(8,128)(2,1)S(1)} %get-tuple-element.90), channel_id=1, source_target_pairs={{0,1},{1,0},{2,3},{3,2},{4,5},{5,4},{6,7},{7,6},{8,9},{9,8},{10,11... | collective-permute-start | bytes 294920 | tf_op jit(solution)/shard_map/ppermute | solution.py:30
  294.8 9.4 %collective-permute-start.38 = (bf16[128,384]{1,0:T(8,128)(2,1)S(1)}, bf16[128,384]{1,0:T(8,128)(2,1)S(1)}, u32[]{:S(2)}, u32[]{:S(2)}) collective-permute-start(bf16[128,384]{1,0:T(8,128)(2,1)S(1)} %get-tuple-element.89), channel_id=1, source_target_pairs={{0,3},{1,2},{2,1},{3,0},{4,7},{5,6},{6,5},{7,4},{8,11},{9,10},{10,... | collective-permute-start | bytes 294920 | tf_op jit(solution)/shard_map/ppermute | solution.py:30
  304.2 3.0 copy-start.13
  305.3 1.6 collective-permute-start.39
  307.0 16.7 %copy-start.14 = (s32[16,1024]{1,0:T(8,128)S(1)}, s32[16,1024]{1,0:T(8,128)}, u32[]{:S(2)}) copy-start(s32[16,1024]{1,0:T(8,128)} %param.33) | copy-start | bytes 196612
  307.2 18.6 %copy-start.1 = (bf16[256,2048]{1,0:T(8,128)(2,1)S(1)}, bf16[256,2048]{1,0:T(8,128)(2,1)}, u32[]{:S(2)}) copy-start(bf16[256,2048]{1,0:T(8,128)(2,1)} %param.28) | copy-start | bytes 3145732
  307.6 6.4 %collective-permute-start.42 = (bf16[32,2048]{1,0:T(8,128)(2,1)S(1)}, bf16[32,2048]{1,0:T(8,128)(2,1)S(1)}, u32[]{:S(2)}, u32[]{:S(2)}) collective-permute-start(bf16[32,2048]{1,0:T(8,128)(2,1)S(1)} %get-tuple-element.83), channel_id=1, source_target_pairs={{0,3},{1,0},{2,1},{3,2},{4,7},{5,4},{6,5},{7,6},{8,11},{9,8},{10,9... | collective-permute-start | bytes 393224 | tf_op jit(solution)/shard_map/ppermute | solution.py:69
  309.8 13.8 %collective-permute-start.41 = (bf16[32,2048]{1,0:T(8,128)(2,1)S(1)}, bf16[32,2048]{1,0:T(8,128)(2,1)S(1)}, u32[]{:S(2)}, u32[]{:S(2)}) collective-permute-start(bf16[32,2048]{1,0:T(8,128)(2,1)S(1)} %get-tuple-element.84), channel_id=1, source_target_pairs={{0,2},{1,3},{2,0},{3,1},{4,6},{5,7},{6,4},{7,5},{8,10},{9,11},{10,... | collective-permute-start | bytes 393224 | tf_op jit(solution)/shard_map/ppermute | solution.py:69
  311.6 11.9 %collective-permute-start.40 = (bf16[32,2048]{1,0:T(8,128)(2,1)S(1)}, bf16[32,2048]{1,0:T(8,128)(2,1)S(1)}, u32[]{:S(2)}, u32[]{:S(2)}) collective-permute-start(bf16[32,2048]{1,0:T(8,128)(2,1)S(1)} %get-tuple-element.82), channel_id=1, source_target_pairs={{0,1},{1,2},{2,3},{3,0},{4,5},{5,6},{6,7},{7,4},{8,9},{9,10},{10,1... | collective-permute-start | bytes 393224 | tf_op jit(solution)/shard_map/ppermute | solution.py:69
  323.7 1.4 collective-permute-start.43
  (1 other events, 1.0 us)
Sparse Core Ops, SparseCore 0:
  11.5 110.6 all-gather.2

commit v12 on v11

--- a/solution.py
+++ b/solution.py
@@ -337,22 +337,36 @@
     mine, last = lax.optimization_barrier((mine, last))
     shares = [jnp.concatenate([share[1:], last], 0)]
 
-    far = [j for j in range(1, groups) if groups != 4 or j < 3]
-    shares += [swap(shares[0], "dp", j) for j in far]
-    plan = [(j, 0, j, 1) for j in range(len(shares))]
     came = sum_step(sum_sends(mine, got, None, 1), 1)
+    if groups == 4:
+        k, v = shares[0][:, :1], shares[0][:, 1:]
+        near = [swap(k, "dp", 1), swap(k, "dp", 2)]
+        plan = [(0, 0, 0, 1), (1, 0, 3, 0), (2, 0, 4, 0), (5, 0, 6, 0)]
+        swapped = []
+    else:
+        near = [swap(shares[0], "dp", j) for j in range(1, groups)]
+        plan = [(j, 0, j, 1) for j in range(groups)]
     for step in range(2, count):
         sends = sum_sends(mine, got, came, step)
         if step == 2:
-            held = lax.optimization_barrier(sends + tuple(shares[1:]))
-            sends, shares[1:] = held[:2], list(held[2:])
+            held = lax.optimization_barrier(sends + tuple(near))
+            sends, shares = held[:2], shares + list(held[2:])
             if groups == 4:
-                passed = [swap(shares[2][:, :1], "dp", 1), swap(shares[1][:, 1:], "dp", 2)]
-                plan.append((3, 0, 4, 0))
+                near = [swap(v, "dp", 1), swap(v, "dp", 2)]
+                swapped = [swap(y, "section", 1) for y in shares]
         if step == count - 1 and groups == 4:
-            held = lax.optimization_barrier(sends + tuple(passed))
-            sends, shares = held[:2], shares + list(held[2:])
+            held = lax.optimization_barrier(sends + tuple(near) + tuple(swapped))
+            sends, near, swapped = held[:2], list(held[2:4]), list(held[4:])
+            shares = shares + near
+            passed = [swap(shares[2], "dp", 1), swap(near[0], "dp", 2)]
+            swapped += [swap(y, "section", 1) for y in near]
         came = sum_step(sends, step)
+    if groups == 4:
+        held = lax.optimization_barrier(came + tuple(passed))
+        came, shares = held[:2], shares + list(held[2:])
+        swapped += [swap(y, "section", 1) for y in held[2:]]
+    else:
+        swapped = [swap(y, "section", 1) for y in shares]
     total = slot_sum(mine, got, 0) + came[0].astype(F32) + came[1].astype(F32)
     enc_out = (source.astype(F32) + keep_factor(enc_keep) * total).astype(BF16)
     memory = norm_rows(enc_out, final_gain).astype(BF16)
@@ -363,7 +377,7 @@
         [p + at for p in places] + [p + jnp.arange(groups, dtype=jnp.int32) for p in places]
     ).astype(jnp.int32)
     plan += [(k + len(shares), a, v + len(shares), b) for k, a, v, b in plan]
-    shares += [swap(s, "section", 1) for s in shares]
+    shares = shares + swapped
     parts = attend_own_keys(memory, queries, own_head, shares, tuple(plan), table)
     parts = [parts[0]] + [
         swap(parts[o], "tensor", heads[o]) for o in range(1, count)

time: 337 us -> 332 us (0.985)
  waiting for transfers between devices: 174 us -> 159 us
  starting transfers between devices: 60.1 us -> 67.3 us
    ppermute x26 -> x30, waiting for transfers between devices: 39.5 us -> 25.1 us  [swap(): lax.ppermute(value, axis, [(i, i ^ distance) for i in range(lax.axis_size...]
    ppermute x26 -> x30, starting transfers between devices: 16.4 us -> 20.9 us  [swap(): lax.ppermute(value, axis, [(i, i ^ distance) for i in range(lax.axis_size...]
    unnamed x46 -> x54, local copies, waits for them, and re-layouts: 6.67 us -> 8.35 us
  transfers between devices with their start and end apart: 45 -> 49, of which waited for: 26 -> 25; matrix products, arithmetic and copies ran while one was open for 7% -> 7% of each run, Pallas kernels for 13% -> 14%
where the time goes in v12:
time: 332 us; the launch traced here: 328 us
  waiting for transfers between devices  159 us (48%)
  starting transfers between devices  67.3 us (20%)
  Pallas kernels  51.8 us (16%)
  other arithmetic  19.8 us (6%)
  between operations  15.3 us (5%)
  local copies, waits for them, and re-layouts  11.6 us (3%)
  matrix products  3.45 us (1%)
    ppermute x3, waiting for transfers between devices, sum_step(): above = lax.ppermute(sends[0], 'tensor', [(i, i + 1) for i in range(step)])  45.2 us
    pallas_call x2, Pallas kernels, ffn(): pl.pallas_call(functools.partial(ffn_kernel, ins), grid_spec=pltpu.Prefet...  44.6 us
    ppermute x6, waiting for transfers between devices, slots_sum(): lax.ppermute(product[o], 'tensor', [(i, (i + o) % count) for i in range(c...  40.8 us
    ppermute x6, waiting for transfers between devices, from_slots(): lax.ppermute(value, 'tensor', [(i, (i - o) % count) for i in range(count)])  25.9 us
    ppermute x30, waiting for transfers between devices, swap(): lax.ppermute(value, axis, [(i, i ^ distance) for i in range(lax.axis_size...  25.1 us
    ppermute x30, starting transfers between devices, swap(): lax.ppermute(value, axis, [(i, i ^ distance) for i in range(lax.axis_size...  20.9 us
    ppermute x6, starting transfers between devices, slots_sum(): lax.ppermute(product[o], 'tensor', [(i, (i + o) % count) for i in range(c...  17.6 us
    all_gather x1, waiting for transfers between devices, per_device(): x = lax.all_gather(normed, ('section', 'tensor'), axis=0, tiled=False)  16.5 us
  transfers between devices with their start and end apart: 49, of which 25 were waited for; matrix products, arithmetic and copies ran while one was open for 7% of the time, Pallas kernels for 14%

profile of v12, /device:TPU:0, one launch (start us, length us, event | category | flops | bytes accessed | tf_op | source)
XLA Modules:
  0.0 327.8 jit_solution(15222349419892707668)
XLA Ops:
  7.2 1.6 fusion.3
  8.9 2.5 fusion.5
  12.2 0.9 collective-permute-done
  13.2 3.0 collective-permute-start.3
  16.1 2.6 collective-permute-start.2
  18.7 1.3 collective-permute-start.1
  20.1 2.5 collective-permute-done.3
  22.6 8.8 %collective-permute-done.2 = bf16[32,2048]{1,0:T(8,128)(2,1)S(1)} collective-permute-done((bf16[32,2048]{1,0:T(8,128)(2,1)S(1)}, bf16[32,2048]{1,0:T(8,128)(2,1)S(1)}, u32[]{:S(2)}, u32[]{:S(2)}) %collective-permute-start.2) | collective-permute-done | bytes 131104 | tf_op jit(solution)/shard_map/ppermute | solution.py:36
  31.4 1.5 convolution_bitcast_fusion
  33.9 1.5 collective-permute-done.4
  36.2 12.9 %collective-permute-start.7 = (bf16[32,2048]{1,0:T(8,128)(2,1)S(1)}, bf16[32,2048]{1,0:T(8,128)(2,1)S(1)}, u32[]{:S(2)}, u32[]{:S(2)}) collective-permute-start(bf16[32,2048]{1,0:T(8,128)(2,1)S(1)} %get-tuple-element.102), channel_id=1, source_target_pairs={{0,3},{1,0},{2,1},{3,2},{4,7},{5,4},{6,5},{7,6},{8,11},{9,8},{10,9... | collective-permute-start | bytes 393224 | tf_op jit(solution)/shard_map/ppermute | solution.py:69
  49.8 8.0 %collective-permute-done.7 = bf16[32,2048]{1,0:T(8,128)(2,1)S(1)} collective-permute-done((bf16[32,2048]{1,0:T(8,128)(2,1)S(1)}, bf16[32,2048]{1,0:T(8,128)(2,1)S(1)}, u32[]{:S(2)}, u32[]{:S(2)}) %collective-permute-start.7) | collective-permute-done | bytes 131104 | tf_op jit(solution)/shard_map/ppermute | solution.py:69
  57.8 20.9 %collective-permute-done.6 = bf16[32,2048]{1,0:T(8,128)(2,1)S(1)} collective-permute-done((bf16[32,2048]{1,0:T(8,128)(2,1)S(1)}, bf16[32,2048]{1,0:T(8,128)(2,1)S(1)}, u32[]{:S(2)}, u32[]{:S(2)}) %collective-permute-start.6) | collective-permute-done | bytes 131104 | tf_op jit(solution)/shard_map/ppermute | solution.py:69
  78.8 1.9 copy.38
  81.7 3.5 %collective-permute-done.9 = bf16[16,2048]{1,0:T(8,128)(2,1)S(1)} collective-permute-done((bf16[16,2048]{1,0:T(8,128)(2,1)S(1)}, bf16[16,2048]{1,0:T(8,128)(2,1)S(1)}, u32[]{:S(2)}, u32[]{:S(2)}) %collective-permute-start.9) | collective-permute-done | bytes 65568 | tf_op jit(solution)/shard_map/ppermute | solution.py:30
  85.4 3.9 %collective-permute-start.10 = (bf16[32,2048]{1,0:T(8,128)(2,1)S(1)}, bf16[32,2048]{1,0:T(8,128)(2,1)S(1)}, u32[]{:S(2)}, u32[]{:S(2)}) collective-permute-start(bf16[32,2048]{1,0:T(8,128)(2,1)S(1)} %maximum_select_fusion.3), channel_id=1, source_target_pairs={{0,3},{1,0},{2,1},{3,2},{4,7},{5,4},{6,5},{7,6},{8,11},{9,8},{10,9... | collective-permute-start | bytes 393224 | tf_op jit(solution)/shard_map/ppermute | solution.py:36
  89.3 7.0 %collective-permute-done.12 = bf16[32,2048]{1,0:T(8,128)(2,1)S(1)} collective-permute-done((bf16[32,2048]{1,0:T(8,128)(2,1)S(1)}, bf16[32,2048]{1,0:T(8,128)(2,1)S(1)}, u32[]{:S(2)}, u32[]{:S(2)}) %collective-permute-start.12) | collective-permute-done | bytes 131104 | tf_op jit(solution)/shard_map/ppermute | solution.py:36
  96.3 7.6 %collective-permute-done.11 = bf16[32,2048]{1,0:T(8,128)(2,1)S(1)} collective-permute-done((bf16[32,2048]{1,0:T(8,128)(2,1)S(1)}, bf16[32,2048]{1,0:T(8,128)(2,1)S(1)}, u32[]{:S(2)}, u32[]{:S(2)}) %collective-permute-start.11) | collective-permute-done | bytes 131104 | tf_op jit(solution)/shard_map/ppermute | solution.py:36
  104.5 1.2 collective-permute-done.13
  105.8 16.5 %all-gather.3.cloned.1.call-done = bf16[1024,4096]{1,0:T(8,128)(2,1)} async-done(((bf16[128,4096]{1,0:T(8,128)(2,1)}), bf16[1024,4096]{1,0:T(8,128)(2,1)}) %all-gather.3.cloned.1.call-update) | async-done | bytes 8388624 | tf_op jit(solution)/shard_map/all_gather | solution.py:290
  122.2 1.6 collective-permute-start.17
  123.8 1.9 collective-permute-start.16
  125.7 0.9 collective-permute-start.15
  126.7 22.2 %ffn.2 = bf16[512,4096]{1,0:T(8,128)(2,1)S(1)} custom-call(s32[5]{0:T(128)S(1)} %get-tuple-element.117.order, bf16[2,4,128,4096]{3,2,1,0:T(8,128)(2,1)} %bitcast.83, bf16[4096,1024]{1,0:T(8,128)(2,1)} %gate_ref.3, bf16[4096,1024]{1,0:T(8,128)(2,1)} %up_ref.3, bf16[1024,4096]{1,0:T(8,128)(2,1)} %down_ref.3), custom_call_target="tpu_custom_call" | custom-call | flops 1024 | bytes 1024 | tf_op jit(solution)/shard_map/ffn/pallas_call | solution.py:149
  148.9 4.1 %collective-permute-done.15 = bf16[128,256]{1,0:T(8,128)(2,1)S(1)} collective-permute-done((bf16[128,256]{1,0:T(8,128)(2,1)S(1)}, bf16[128,256]{1,0:T(8,128)(2,1)S(1)}, u32[]{:S(2)}, u32[]{:S(2)}) %collective-permute-start.15) | collective-permute-done | bytes 65568 | tf_op jit(solution)/shard_map/ppermute | solution.py:30
  153.1 1.1 pad_maximum_fusion.1
  154.2 22.4 %ffn.3 = bf16[512,4096]{1,0:T(8,128)(2,1)S(1)} custom-call(s32[5]{0:T(128)S(1)} %get-tuple-element.116.order, bf16[2,4,128,4096]{3,2,1,0:T(8,128)(2,1)} %bitcast.84, bf16[4096,1024]{1,0:T(8,128)(2,1)} %gate_ref.3, bf16[4096,1024]{1,0:T(8,128)(2,1)} %up_ref.3, bf16[1024,4096]{1,0:T(8,128)(2,1)} %down_ref.3), custom_call_target="tpu_custom_call" | custom-call | flops 1024 | bytes 1024 | tf_op jit(solution)/shard_map/ffn/pallas_call | solution.py:149
  176.6 3.4 %collective-permute-done.19 = bf16[2,2,512,256]{3,2,1,0:T(8,128)(2,1)} collective-permute-done((bf16[2,2,512,256]{3,2,1,0:T(8,128)(2,1)}, bf16[2,2,512,256]{3,2,1,0:T(8,128)(2,1)}, u32[]{:S(2)}, u32[]{:S(2)}) %collective-permute-start.19) | collective-permute-done | bytes 1048608 | tf_op jit(solution)/shard_map/ppermute | solution.py:30
  180.8 2.3 collective-permute-start.21
  183.8 1.1 slice.188
  184.9 1.3 fusion.11
  186.2 1.6 collective-permute-start.23
  187.8 1.5 collective-permute-start.24
  189.3 16.1 %collective-permute-done.21 = bf16[128,4096]{1,0:T(8,128)(2,1)S(1)} collective-permute-done((bf16[128,4096]{1,0:T(8,128)(2,1)S(1)}, bf16[128,4096]{1,0:T(8,128)(2,1)S(1)}, u32[]{:S(2)}, u32[]{:S(2)}) %collective-permute-start.21) | collective-permute-done | bytes 1048608 | tf_op jit(solution)/shard_map/ppermute | solution.py:59
  206.7 4.0 %collective-permute-start.25 = (bf16[128,4096]{1,0:T(8,128)(2,1)S(1)}, bf16[128,4096]{1,0:T(8,128)(2,1)S(1)}, u32[]{:S(2)}, u32[]{:S(2)}) collective-permute-start(bf16[128,4096]{1,0:T(8,128)(2,1)S(1)} %get-tuple-element.46), channel_id=1, source_target_pairs={{0,1},{1,2},{4,5},{5,6},{8,9},{9,10},{12,13},{13,14},{16,17},{17,1... | collective-permute-start | bytes 3145736 | tf_op jit(solution)/shard_map/ppermute | solution.py:59
  210.7 1.0 collective-permute-start.26
  211.7 1.4 pad_maximum_fusion.refs_2_
  213.1 1.6 collective-permute-start.27
  214.7 1.5 collective-permute-start.28
  216.2 16.0 %collective-permute-done.25 = bf16[128,4096]{1,0:T(8,128)(2,1)S(1)} collective-permute-done((bf16[128,4096]{1,0:T(8,128)(2,1)S(1)}, bf16[128,4096]{1,0:T(8,128)(2,1)S(1)}, u32[]{:S(2)}, u32[]{:S(2)}) %collective-permute-start.25) | collective-permute-done | bytes 1048608 | tf_op jit(solution)/shard_map/ppermute | solution.py:59
  232.7 2.5 add_convert_fusion
  235.3 1.2 copy-done.5
  236.4 0.9 copy-done.9
  237.3 0.9 copy-done.11
  238.3 8.6 %collective-permute-start.32 = (bf16[128,4096]{1,0:T(8,128)(2,1)}, bf16[128,4096]{1,0:T(8,128)(2,1)}, u32[]{:S(2)}, u32[]{:S(2)}) collective-permute-start(bf16[128,4096]{1,0:T(8,128)(2,1)} %get-tuple-element.52), channel_id=1, source_target_pairs={{0,1},{1,2},{2,3},{4,5},{5,6},{6,7},{8,9},{9,10},{10,11},{12,13},{... | collective-permute-start | bytes 3145736 | tf_op jit(solution)/shard_map/ppermute | solution.py:59
  246.9 1.3 collective-permute-start.33
  248.1 1.6 collective-permute-start.34
  249.7 1.5 collective-permute-start.35
  251.2 1.6 shift_right_arithmetic.40
  252.9 3.1 copy.29
  256.2 13.1 %collective-permute-done.32 = bf16[128,4096]{1,0:T(8,128)(2,1)} collective-permute-done((bf16[128,4096]{1,0:T(8,128)(2,1)}, bf16[128,4096]{1,0:T(8,128)(2,1)}, u32[]{:S(2)}, u32[]{:S(2)}) %collective-permute-start.32) | collective-permute-done | bytes 1048608 | tf_op jit(solution)/shard_map/ppermute | solution.py:59
  269.2 5.1 %collective-permute-done.33 = bf16[128,4096]{1,0:T(8,128)(2,1)} collective-permute-done((bf16[128,4096]{1,0:T(8,128)(2,1)}, bf16[128,4096]{1,0:T(8,128)(2,1)}, u32[]{:S(2)}, u32[]{:S(2)}) %collective-permute-start.33) | collective-permute-done | bytes 1048608 | tf_op jit(solution)/shard_map/ppermute | solution.py:60
  274.4 4.2 %fusion = (f32[128]{0:T(128)S(1)}, bf16[128,4096]{1,0:T(8,128)(2,1)S(1)}) fusion(bf16[128,4096]{1,0:T(8,128)(2,1)} %collective-permute-done.33, bf16[128,4096]{1,0:T(8,128)(2,1)} %collective-permute-done.32, bf16[512,4096]{1,0:T(8,128)(2,1)} %copy-done.14, bf16[512,4096]{1,0:T(8,128)(2,1)} %copy-done.2, s32[128,4096]{1,0:T(8,128)} %bitcast.86, ...), kind=kLoop, calls=%fused_computation.10 | loop fusion | flops 9437056 | bytes 8405504 | tf_op jit(solution)/shard_map/reduce_sum | solution.py:18
  279.6 1.6 collective-permute-done.38.refs_14_
  281.2 1.1 collective-permute-done.39.refs_15_
  282.4 7.2 %attend_own_keys.1 = bf16[4,128,384]{2,1,0:T(8,128)(2,1)S(1)} custom-call(s32[16]{0:T(128)S(1)} %pad_add_fusion.3.table, bf16[128,4096]{1,0:T(8,128)(2,1)S(1)} %fusion.2.mem_ref, bf16[4,128,256]{2,1,0:T(8,128)(2,1)S(1)} %pad_maximum_fusion.4.cq_ref, bf16[2,2048,256]{2,1,0:T(8,128)(2,1)S(1)} %bitcast.82, ...), custom_call_target="tpu_custom_call" | custom-call | flops 1024 | bytes 1024 | tf_op jit(solution)/shard_map/attend_own_keys/pallas_call | solution.py:232
  289.8 4.3 %collective-permute-start.42 = (bf16[128,384]{1,0:T(8,128)(2,1)S(1)}, bf16[128,384]{1,0:T(8,128)(2,1)S(1)}, u32[]{:S(2)}, u32[]{:S(2)}) collective-permute-start(bf16[128,384]{1,0:T(8,128)(2,1)S(1)} %get-tuple-element.105), channel_id=1, source_target_pairs={{0,3},{1,2},{2,1},{3,0},{4,7},{5,6},{6,5},{7,4},{8,11},{9,10},{10,... | collective-permute-start | bytes 294920 | tf_op jit(solution)/shard_map/ppermute | solution.py:30
  294.1 4.7 %collective-permute-done.40 = bf16[128,384]{1,0:T(8,128)(2,1)S(1)} collective-permute-done((bf16[128,384]{1,0:T(8,128)(2,1)S(1)}, bf16[128,384]{1,0:T(8,128)(2,1)S(1)}, u32[]{:S(2)}, u32[]{:S(2)}) %collective-permute-start.40) | collective-permute-done | bytes 98336 | tf_op jit(solution)/shard_map/ppermute | solution.py:30
  300.0 1.5 collective-permute-done.43
  302.3 2.2 collective-permute-start.46
  304.4 1.8 collective-permute-start.45
  306.3 2.3 collective-permute-done.46
  308.6 9.6 %collective-permute-done.45 = bf16[32,2048]{1,0:T(8,128)(2,1)S(1)} collective-permute-done((bf16[32,2048]{1,0:T(8,128)(2,1)S(1)}, bf16[32,2048]{1,0:T(8,128)(2,1)S(1)}, u32[]{:S(2)}, u32[]{:S(2)}) %collective-permute-start.45) | collective-permute-done | bytes 131104 | tf_op jit(solution)/shard_map/ppermute | solution.py:69
  318.6 1.1 collective-permute-done.47
  (163 shorter events, 13.0 us)
Async XLA Ops:
  7.2 28.5 %copy-start = (bf16[256,2048]{1,0:T(8,128)(2,1)S(1)}, bf16[256,2048]{1,0:T(8,128)(2,1)}, u32[]{:S(2)}) copy-start(bf16[256,2048]{1,0:T(8,128)(2,1)} %param.28) | copy-start | bytes 3145732
  7.2 115.0 %all-gather.3.cloned.1.call-start = ((), (), s32[]{:S(2)}) async-start(), calls=%async_computation | async-start | bytes 9437184 | tf_op jit(solution)/shard_map/all_gather | solution.py:290
  11.7 1.4 collective-permute-start
  13.2 9.4 %collective-permute-start.3 = (bf16[32,2048]{1,0:T(8,128)(2,1)S(1)}, bf16[32,2048]{1,0:T(8,128)(2,1)S(1)}, u32[]{:S(2)}, u32[]{:S(2)}) collective-permute-start(bf16[32,2048]{1,0:T(8,128)(2,1)S(1)} %maximum_select_fusion.2), channel_id=1, source_target_pairs={{0,1},{1,2},{2,3},{3,0},{4,5},{5,6},{6,7},{7,4},{8,9},{9,10},{10,1... | collective-permute-start | bytes 393224 | tf_op jit(solution)/shard_map/ppermute | solution.py:36
  16.1 15.2 %collective-permute-start.2 = (bf16[32,2048]{1,0:T(8,128)(2,1)S(1)}, bf16[32,2048]{1,0:T(8,128)(2,1)S(1)}, u32[]{:S(2)}, u32[]{:S(2)}) collective-permute-start(bf16[32,2048]{1,0:T(8,128)(2,1)S(1)} %maximum_select_fusion.2), channel_id=1, source_target_pairs={{0,2},{1,3},{2,0},{3,1},{4,6},{5,7},{6,4},{7,5},{8,10},{9,11},{10,... | collective-permute-start | bytes 393224 | tf_op jit(solution)/shard_map/ppermute | solution.py:36
  18.7 12.6 %collective-permute-start.1 = (bf16[32,2048]{1,0:T(8,128)(2,1)S(1)}, bf16[32,2048]{1,0:T(8,128)(2,1)S(1)}, u32[]{:S(2)}, u32[]{:S(2)}) collective-permute-start(bf16[32,2048]{1,0:T(8,128)(2,1)S(1)} %maximum_select_fusion.2), channel_id=1, source_target_pairs={{0,3},{1,0},{2,1},{3,2},{4,7},{5,4},{6,5},{7,6},{8,11},{9,8},{10,9... | collective-permute-start | bytes 393224 | tf_op jit(solution)/shard_map/ppermute | solution.py:36
  20.1 12.8 %copy-start.22 = (bf16[2048,3,256]{2,0,1:T(8,128)(2,1)S(1)}, bf16[2048,3,256]{2,0,1:T(8,128)(2,1)}, u32[]{:S(2)}) copy-start(bf16[2048,3,256]{2,0,1:T(8,128)(2,1)} %param.27) | copy-start | bytes 9437188
  33.6 1.8 collective-permute-start.4
  36.2 21.6 %collective-permute-start.7 = (bf16[32,2048]{1,0:T(8,128)(2,1)S(1)}, bf16[32,2048]{1,0:T(8,128)(2,1)S(1)}, u32[]{:S(2)}, u32[]{:S(2)}) collective-permute-start(bf16[32,2048]{1,0:T(8,128)(2,1)S(1)} %get-tuple-element.102), channel_id=1, source_target_pairs={{0,3},{1,0},{2,1},{3,2},{4,7},{5,4},{6,5},{7,6},{8,11},{9,8},{10,9... | collective-permute-start | bytes 393224 | tf_op jit(solution)/shard_map/ppermute | solution.py:69
  49.1 29.5 %collective-permute-start.6 = (bf16[32,2048]{1,0:T(8,128)(2,1)S(1)}, bf16[32,2048]{1,0:T(8,128)(2,1)S(1)}, u32[]{:S(2)}, u32[]{:S(2)}) collective-permute-start(bf16[32,2048]{1,0:T(8,128)(2,1)S(1)} %get-tuple-element.103), channel_id=1, source_target_pairs={{0,2},{1,3},{2,0},{3,1},{4,6},{5,7},{6,4},{7,5},{8,10},{9,11},{10,... | collective-permute-start | bytes 393224 | tf_op jit(solution)/shard_map/ppermute | solution.py:69
  49.4 29.2 %collective-permute-start.5 = (bf16[32,2048]{1,0:T(8,128)(2,1)S(1)}, bf16[32,2048]{1,0:T(8,128)(2,1)S(1)}, u32[]{:S(2)}, u32[]{:S(2)}) collective-permute-start(bf16[32,2048]{1,0:T(8,128)(2,1)S(1)} %get-tuple-element.101), channel_id=1, source_target_pairs={{0,1},{1,2},{2,3},{3,0},{4,5},{5,6},{6,7},{7,4},{8,9},{9,10},{10,1... | collective-permute-start | bytes 393224 | tf_op jit(solution)/shard_map/ppermute | solution.py:69
  78.7 25.2 %copy-start.23 = (bf16[2048,256]{1,0:T(8,128)(2,1)S(1)}, bf16[2048,256]{1,0:T(8,128)(2,1)}, u32[]{:S(2)}) copy-start(bf16[2048,256]{1,0:T(8,128)(2,1)} %param.30) | copy-start | bytes 3145732
  78.8 2.5 collective-permute-start.8
  80.8 25.0 %collective-permute-start.14 = (bf16[2,2048,256]{2,1,0:T(8,128)(2,1)S(1)}, bf16[2,2048,256]{2,1,0:T(8,128)(2,1)}, u32[]{:S(2)}, u32[]{:S(2)}) collective-permute-start(bf16[2,2048,256]{2,1,0:T(8,128)(2,1)S(1)} %bitcast.81), channel_id=1, source_target_pairs={{0,4},{4,0},{1,5},{5,1},{2,6},{6,2},{3,7},{7,3},{8,12},{12,8},{9,1... | collective-permute-start | bytes 6291464 | tf_op jit(solution)/shard_map/ppermute | solution.py:30
  81.6 3.7 %collective-permute-start.9 = (bf16[16,2048]{1,0:T(8,128)(2,1)S(1)}, bf16[16,2048]{1,0:T(8,128)(2,1)S(1)}, u32[]{:S(2)}, u32[]{:S(2)}) collective-permute-start(bf16[16,2048]{1,0:T(8,128)(2,1)S(1)} %get-tuple-element.113), channel_id=1, source_target_pairs={{0,4},{4,0},{1,5},{5,1},{2,6},{6,2},{3,7},{7,3},{8,12},{12,8},{9,1... | collective-permute-start | bytes 196616 | tf_op jit(solution)/shard_map/ppermute | solution.py:30
  85.3 11.0 %collective-permute-start.12 = (bf16[32,2048]{1,0:T(8,128)(2,1)S(1)}, bf16[32,2048]{1,0:T(8,128)(2,1)S(1)}, u32[]{:S(2)}, u32[]{:S(2)}) collective-permute-start(bf16[32,2048]{1,0:T(8,128)(2,1)S(1)} %maximum_select_fusion.3), channel_id=1, source_target_pairs={{0,1},{1,2},{2,3},{3,0},{4,5},{5,6},{6,7},{7,4},{8,9},{9,10},{10,1... | collective-permute-start | bytes 393224 | tf_op jit(solution)/shard_map/ppermute | solution.py:36
  85.3 18.6 %collective-permute-start.11 = (bf16[32,2048]{1,0:T(8,128)(2,1)S(1)}, bf16[32,2048]{1,0:T(8,128)(2,1)S(1)}, u32[]{:S(2)}, u32[]{:S(2)}) collective-permute-start(bf16[32,2048]{1,0:T(8,128)(2,1)S(1)} %maximum_select_fusion.3), channel_id=1, source_target_pairs={{0,2},{1,3},{2,0},{3,1},{4,6},{5,7},{6,4},{7,5},{8,10},{9,11},{10,... | collective-permute-start | bytes 393224 | tf_op jit(solution)/shard_map/ppermute | solution.py:36
  85.4 18.5 %collective-permute-start.10 = (bf16[32,2048]{1,0:T(8,128)(2,1)S(1)}, bf16[32,2048]{1,0:T(8,128)(2,1)S(1)}, u32[]{:S(2)}, u32[]{:S(2)}) collective-permute-start(bf16[32,2048]{1,0:T(8,128)(2,1)S(1)} %maximum_select_fusion.3), channel_id=1, source_target_pairs={{0,3},{1,0},{2,1},{3,2},{4,7},{5,4},{6,5},{7,6},{8,11},{9,8},{10,9... | collective-permute-start | bytes 393224 | tf_op jit(solution)/shard_map/ppermute | solution.py:36
  104.3 1.4 collective-permute-start.13
  122.2 30.8 %collective-permute-start.18 = (bf16[1,2,512,256]{3,2,1,0:T(8,128)(2,1)S(1)}, bf16[1,2,512,256]{3,2,1,0:T(8,128)(2,1)S(1)}, u32[]{:S(2)}, u32[]{:S(2)}) collective-permute-start(bf16[1,2,512,256]{3,2,1,0:T(8,128)(2,1)S(1)} %dynamic-slice_bitcast_fusion), channel_id=1, source_target_pairs={{0,2},{1,3},{2,0},{3,1},{4,6},{5,7},{6,4},{7,5},{8,10},{9,11},{10,... | collective-permute-start | bytes 1572872 | tf_op jit(solution)/shard_map/ppermute | solution.py:30
  122.2 26.7 %collective-permute-start.17 = (bf16[128,256]{1,0:T(8,128)(2,1)S(1)}, bf16[128,256]{1,0:T(8,128)(2,1)S(1)}, u32[]{:S(2)}, u32[]{:S(2)}) collective-permute-start(bf16[128,256]{1,0:T(8,128)(2,1)S(1)} %bitcast.93), channel_id=1, source_target_pairs={{0,3},{1,2},{2,1},{3,0},{4,7},{5,6},{6,5},{7,4},{8,11},{9,10},{10,... | collective-permute-start | bytes 196616 | tf_op jit(solution)/shard_map/ppermute | solution.py:30
  123.8 25.1 %collective-permute-start.16 = (bf16[128,256]{1,0:T(8,128)(2,1)S(1)}, bf16[128,256]{1,0:T(8,128)(2,1)S(1)}, u32[]{:S(2)}, u32[]{:S(2)}) collective-permute-start(bf16[128,256]{1,0:T(8,128)(2,1)S(1)} %bitcast.94), channel_id=1, source_target_pairs={{0,1},{1,0},{2,3},{3,2},{4,5},{5,4},{6,7},{7,6},{8,9},{9,8},{10,11... | collective-permute-start | bytes 196616 | tf_op jit(solution)/shard_map/ppermute | solution.py:30
  125.7 27.3 %collective-permute-start.15 = (bf16[128,256]{1,0:T(8,128)(2,1)S(1)}, bf16[128,256]{1,0:T(8,128)(2,1)S(1)}, u32[]{:S(2)}, u32[]{:S(2)}) collective-permute-start(bf16[128,256]{1,0:T(8,128)(2,1)S(1)} %bitcast.95), channel_id=1, source_target_pairs={{0,2},{1,3},{2,0},{3,1},{4,6},{5,7},{6,4},{7,5},{8,10},{9,11},{10,... | collective-permute-start | bytes 196616 | tf_op jit(solution)/shard_map/ppermute | solution.py:30
  154.1 25.9 %collective-permute-start.20 = (bf16[512,4096]{1,0:T(8,128)(2,1)S(1)}, bf16[512,4096]{1,0:T(8,128)(2,1)S(1)}, u32[]{:S(2)}, u32[]{:S(2)}) collective-permute-start(bf16[512,4096]{1,0:T(8,128)(2,1)S(1)} %ffn.2), channel_id=1, source_target_pairs={{0,4},{4,0},{1,5},{5,1},{2,6},{6,2},{3,7},{7,3},{8,12},{12,8},{9,1... | collective-permute-start | bytes 12582920 | tf_op jit(solution)/shard_map/ppermute | solution.py:30
  154.2 25.8 %collective-permute-start.19 = (bf16[2,2,512,256]{3,2,1,0:T(8,128)(2,1)}, bf16[2,2,512,256]{3,2,1,0:T(8,128)(2,1)}, u32[]{:S(2)}, u32[]{:S(2)}) collective-permute-start(bf16[2,2,512,256]{3,2,1,0:T(8,128)(2,1)} %pad_maximum_fusion.1), channel_id=1, source_target_pairs={{0,1},{1,0},{2,3},{3,2},{4,5},{5,4},{6,7},{7,6},{8,9},{9,8},{10,11... | collective-permute-start | bytes 3145736 | tf_op jit(solution)/shard_map/ppermute | solution.py:30
  176.6 56.2 %copy-start.2 = (bf16[512,4096]{1,0:T(8,128)(2,1)}, bf16[512,4096]{1,0:T(8,128)(2,1)S(1)}, u32[]{:S(2)}) copy-start(bf16[512,4096]{1,0:T(8,128)(2,1)S(1)} %ffn.3) | copy-start | bytes 12582916
  180.0 52.7 %copy-start.14 = (bf16[512,4096]{1,0:T(8,128)(2,1)}, bf16[512,4096]{1,0:T(8,128)(2,1)S(1)}, u32[]{:S(2)}) copy-start(bf16[512,4096]{1,0:T(8,128)(2,1)S(1)} %collective-permute-done.20) | copy-start | bytes 12582916
  180.8 24.6 %collective-permute-start.21 = (bf16[128,4096]{1,0:T(8,128)(2,1)S(1)}, bf16[128,4096]{1,0:T(8,128)(2,1)S(1)}, u32[]{:S(2)}, u32[]{:S(2)}) collective-permute-start(bf16[128,4096]{1,0:T(8,128)(2,1)S(1)} %get-tuple-element.93), channel_id=1, source_target_pairs={{0,1},{4,5},{8,9},{12,13},{16,17},{20,21},{24,25},{28,29}} | collective-permute-start | bytes 3145736 | tf_op jit(solution)/shard_map/ppermute | solution.py:59
  183.1 22.4 %collective-permute-start.22 = (bf16[128,4096]{1,0:T(8,128)(2,1)S(1)}, bf16[128,4096]{1,0:T(8,128)(2,1)S(1)}, u32[]{:S(2)}, u32[]{:S(2)}) collective-permute-start(bf16[128,4096]{1,0:T(8,128)(2,1)S(1)} %get-tuple-element.92), channel_id=1, source_target_pairs={{3,2},{7,6},{11,10},{15,14},{19,18},{23,22},{27,26},{31,30}} | collective-permute-start | bytes 3145736 | tf_op jit(solution)/shard_map/ppermute | solution.py:60
  186.2 20.0 %collective-permute-start.23 = (bf16[3,1,512,256]{3,2,1,0:T(8,128)(2,1)S(1)}, bf16[3,1,512,256]{3,2,1,0:T(8,128)(2,1)S(1)}, u32[]{:S(2)}, u32[]{:S(2)}) collective-permute-start(bf16[3,1,512,256]{3,2,1,0:T(8,128)(2,1)S(1)} %get-tuple-element.97), channel_id=1, source_target_pairs={{0,8},{8,0},{16,24},{24,16},{1,9},{9,1},{17,25},{25,17},{2,10},{10... | collective-permute-start | bytes 2359304 | tf_op jit(solution)/shard_map/ppermute | solution.py:30
  187.8 18.9 %collective-permute-start.24 = (bf16[3,1,512,256]{3,2,1,0:T(8,128)(2,1)S(1)}, bf16[3,1,512,256]{3,2,1,0:T(8,128)(2,1)}, u32[]{:S(2)}, u32[]{:S(2)}) collective-permute-start(bf16[3,1,512,256]{3,2,1,0:T(8,128)(2,1)S(1)} %get-tuple-element.97), channel_id=1, source_target_pairs={{0,16},{8,24},{16,0},{24,8},{1,17},{9,25},{17,1},{25,9},{2,18},{10... | collective-permute-start | bytes 2359304 | tf_op jit(solution)/shard_map/ppermute | solution.py:30
  206.2 29.0 %copy-start.7 = (bf16[3,1,512,256]{3,2,1,0:T(8,128)(2,1)}, bf16[3,1,512,256]{3,2,1,0:T(8,128)(2,1)S(1)}, u32[]{:S(2)}) copy-start(bf16[3,1,512,256]{3,2,1,0:T(8,128)(2,1)S(1)} %collective-permute-done.23.refs_3_) | copy-start | bytes 2359300
  206.7 25.5 %collective-permute-start.25 = (bf16[128,4096]{1,0:T(8,128)(2,1)S(1)}, bf16[128,4096]{1,0:T(8,128)(2,1)S(1)}, u32[]{:S(2)}, u32[]{:S(2)}) collective-permute-start(bf16[128,4096]{1,0:T(8,128)(2,1)S(1)} %get-tuple-element.46), channel_id=1, source_target_pairs={{0,1},{1,2},{4,5},{5,6},{8,9},{9,10},{12,13},{13,14},{16,17},{17,1... | collective-permute-start | bytes 3145736 | tf_op jit(solution)/shard_map/ppermute | solution.py:59
  210.7 21.5 %collective-permute-start.26 = (bf16[128,4096]{1,0:T(8,128)(2,1)S(1)}, bf16[128,4096]{1,0:T(8,128)(2,1)S(1)}, u32[]{:S(2)}, u32[]{:S(2)}) collective-permute-start(bf16[128,4096]{1,0:T(8,128)(2,1)S(1)} %get-tuple-element.47), channel_id=1, source_target_pairs={{2,1},{3,2},{6,5},{7,6},{10,9},{11,10},{14,13},{15,14},{18,17},{19... | collective-permute-start | bytes 3145736 | tf_op jit(solution)/shard_map/ppermute | solution.py:60
  213.0 22.2 %copy-start.3 = (bf16[3,2,512,256]{3,2,1,0:T(8,128)(2,1)}, bf16[3,2,512,256]{3,2,1,0:T(8,128)(2,1)S(1)}, u32[]{:S(2)}) copy-start(bf16[3,2,512,256]{3,2,1,0:T(8,128)(2,1)S(1)} %pad_maximum_fusion.refs_2_) | copy-start | bytes 4718596
  213.1 22.2 %collective-permute-start.29 = (bf16[3,2,512,256]{3,2,1,0:T(8,128)(2,1)S(1)}, bf16[3,2,512,256]{3,2,1,0:T(8,128)(2,1)S(1)}, u32[]{:S(2)}, u32[]{:S(2)}) collective-permute-start(bf16[3,2,512,256]{3,2,1,0:T(8,128)(2,1)S(1)} %pad_maximum_fusion.refs_2_), channel_id=1, source_target_pairs={{0,4},{4,0},{1,5},{5,1},{2,6},{6,2},{3,7},{7,3},{8,12},{12,8},{9,1... | collective-permute-start | bytes 4718600 | tf_op jit(solution)/shard_map/ppermute | solution.py:30
  213.1 22.1 %collective-permute-start.27 = (bf16[3,1,512,256]{3,2,1,0:T(8,128)(2,1)S(1)}, bf16[3,1,512,256]{3,2,1,0:T(8,128)(2,1)}, u32[]{:S(2)}, u32[]{:S(2)}) collective-permute-start(bf16[3,1,512,256]{3,2,1,0:T(8,128)(2,1)S(1)} %get-tuple-element.96), channel_id=1, source_target_pairs={{0,8},{8,0},{16,24},{24,16},{1,9},{9,1},{17,25},{25,17},{2,10},{10... | collective-permute-start | bytes 2359304 | tf_op jit(solution)/shard_map/ppermute | solution.py:30
  214.7 20.5 %collective-permute-start.28 = (bf16[3,1,512,256]{3,2,1,0:T(8,128)(2,1)S(1)}, bf16[3,1,512,256]{3,2,1,0:T(8,128)(2,1)}, u32[]{:S(2)}, u32[]{:S(2)}) collective-permute-start(bf16[3,1,512,256]{3,2,1,0:T(8,128)(2,1)S(1)} %get-tuple-element.96), channel_id=1, source_target_pairs={{0,16},{8,24},{16,0},{24,8},{1,17},{9,25},{17,1},{25,9},{2,18},{10... | collective-permute-start | bytes 2359304 | tf_op jit(solution)/shard_map/ppermute | solution.py:30
  232.2 4.2 %collective-permute-start.30 = (bf16[3,1,512,256]{3,2,1,0:T(8,128)(2,1)S(1)}, bf16[3,1,512,256]{3,2,1,0:T(8,128)(2,1)S(1)}, u32[]{:S(2)}, u32[]{:S(2)}) collective-permute-start(bf16[3,1,512,256]{3,2,1,0:T(8,128)(2,1)S(1)} %collective-permute-done.23.refs_3_), channel_id=1, source_target_pairs={{0,4},{4,0},{1,5},{5,1},{2,6},{6,2},{3,7},{7,3},{8,12},{12,8},{9,1... | collective-permute-start | bytes 2359304 | tf_op jit(solution)/shard_map/ppermute | solution.py:30
  232.2 5.1 %collective-permute-start.31 = (bf16[3,1,512,256]{3,2,1,0:T(8,128)(2,1)}, bf16[3,1,512,256]{3,2,1,0:T(8,128)(2,1)S(1)}, u32[]{:S(2)}, u32[]{:S(2)}) collective-permute-start(bf16[3,1,512,256]{3,2,1,0:T(8,128)(2,1)} %collective-permute-done.24.refs_4_), channel_id=1, source_target_pairs={{0,4},{4,0},{1,5},{5,1},{2,6},{6,2},{3,7},{7,3},{8,12},{12,8},{9,1... | collective-permute-start | bytes 2359304 | tf_op jit(solution)/shard_map/ppermute | solution.py:30
  238.3 31.0 %collective-permute-start.32 = (bf16[128,4096]{1,0:T(8,128)(2,1)}, bf16[128,4096]{1,0:T(8,128)(2,1)}, u32[]{:S(2)}, u32[]{:S(2)}) collective-permute-start(bf16[128,4096]{1,0:T(8,128)(2,1)} %get-tuple-element.52), channel_id=1, source_target_pairs={{0,1},{1,2},{2,3},{4,5},{5,6},{6,7},{8,9},{9,10},{10,11},{12,13},{... | collective-permute-start | bytes 3145736 | tf_op jit(solution)/shard_map/ppermute | solution.py:59
  246.9 27.5 %collective-permute-start.33 = (bf16[128,4096]{1,0:T(8,128)(2,1)}, bf16[128,4096]{1,0:T(8,128)(2,1)}, u32[]{:S(2)}, u32[]{:S(2)}) collective-permute-start(bf16[128,4096]{1,0:T(8,128)(2,1)} %get-tuple-element.53), channel_id=1, source_target_pairs={{1,0},{2,1},{3,2},{5,4},{6,5},{7,6},{9,8},{10,9},{11,10},{13,12},{... | collective-permute-start | bytes 3145736 | tf_op jit(solution)/shard_map/ppermute | solution.py:60
  248.1 26.2 %collective-permute-start.34 = (bf16[3,1,512,256]{3,2,1,0:T(8,128)(2,1)}, bf16[3,1,512,256]{3,2,1,0:T(8,128)(2,1)}, u32[]{:S(2)}, u32[]{:S(2)}) collective-permute-start(bf16[3,1,512,256]{3,2,1,0:T(8,128)(2,1)} %collective-permute-done.24.refs_4_), channel_id=1, source_target_pairs={{0,8},{8,0},{16,24},{24,16},{1,9},{9,1},{17,25},{25,17},{2,10},{10... | collective-permute-start | bytes 2359304 | tf_op jit(solution)/shard_map/ppermute | solution.py:30
  249.7 24.6 %collective-permute-start.35 = (bf16[3,1,512,256]{3,2,1,0:T(8,128)(2,1)}, bf16[3,1,512,256]{3,2,1,0:T(8,128)(2,1)}, u32[]{:S(2)}, u32[]{:S(2)}) collective-permute-start(bf16[3,1,512,256]{3,2,1,0:T(8,128)(2,1)} %collective-permute-done.27.refs_5_), channel_id=1, source_target_pairs={{0,16},{8,24},{16,0},{24,8},{1,17},{9,25},{17,1},{25,9},{2,18},{10... | collective-permute-start | bytes 2359304 | tf_op jit(solution)/shard_map/ppermute | solution.py:30
  252.9 21.5 %copy-start.13 = (bf16[128,4096]{1,0:T(8,128)(2,1)S(1)}, bf16[128,4096]{1,0:T(8,128)(2,1)}, u32[]{:S(2)}) copy-start(bf16[128,4096]{1,0:T(8,128)(2,1)} %param.18) | copy-start | bytes 3145732
  256.2 23.4 %collective-permute-start.36 = (bf16[3,1,512,256]{3,2,1,0:T(8,128)(2,1)}, bf16[3,1,512,256]{3,2,1,0:T(8,128)(2,1)S(1)}, u32[]{:S(2)}, u32[]{:S(2)}) collective-permute-start(bf16[3,1,512,256]{3,2,1,0:T(8,128)(2,1)} %collective-permute-done.27.refs_5_), channel_id=1, source_target_pairs={{0,4},{4,0},{1,5},{5,1},{2,6},{6,2},{3,7},{7,3},{8,12},{12,8},{9,1... | collective-permute-start | bytes 2359304 | tf_op jit(solution)/shard_map/ppermute | solution.py:30
  269.2 10.3 %collective-permute-start.37 = (bf16[3,1,512,256]{3,2,1,0:T(8,128)(2,1)}, bf16[3,1,512,256]{3,2,1,0:T(8,128)(2,1)S(1)}, u32[]{:S(2)}, u32[]{:S(2)}) collective-permute-start(bf16[3,1,512,256]{3,2,1,0:T(8,128)(2,1)} %collective-permute-done.28.refs_6_), channel_id=1, source_target_pairs={{0,4},{4,0},{1,5},{5,1},{2,6},{6,2},{3,7},{7,3},{8,12},{12,8},{9,1... | collective-permute-start | bytes 2359304 | tf_op jit(solution)/shard_map/ppermute | solution.py:30
  274.4 4.9 %copy-start.19 = (f32[4096]{0:T(1024)S(1)}, f32[4096]{0:T(1024)}, u32[]{:S(2)}) copy-start(f32[4096]{0:T(1024)} %param.24) | copy-start | bytes 49156
  274.4 8.0 %copy-start.6 = (bf16[3,2,512,256]{3,2,1,0:T(8,128)(2,1)S(1)}, bf16[3,2,512,256]{3,2,1,0:T(8,128)(2,1)}, u32[]{:S(2)}) copy-start(bf16[3,2,512,256]{3,2,1,0:T(8,128)(2,1)} %copy-done.5) | copy-start | bytes 4718596
  274.4 8.0 %copy-start.8 = (bf16[3,1,512,256]{3,2,1,0:T(8,128)(2,1)S(1)}, bf16[3,1,512,256]{3,2,1,0:T(8,128)(2,1)}, u32[]{:S(2)}) copy-start(bf16[3,1,512,256]{3,2,1,0:T(8,128)(2,1)} %copy-done.7) | copy-start | bytes 2359300
  274.4 8.0 %copy-start.10 = (bf16[3,1,512,256]{3,2,1,0:T(8,128)(2,1)S(1)}, bf16[3,1,512,256]{3,2,1,0:T(8,128)(2,1)}, u32[]{:S(2)}) copy-start(bf16[3,1,512,256]{3,2,1,0:T(8,128)(2,1)} %copy-done.9) | copy-start | bytes 2359300
  274.4 8.0 %copy-start.12 = (bf16[3,1,512,256]{3,2,1,0:T(8,128)(2,1)S(1)}, bf16[3,1,512,256]{3,2,1,0:T(8,128)(2,1)}, u32[]{:S(2)}) copy-start(bf16[3,1,512,256]{3,2,1,0:T(8,128)(2,1)} %copy-done.11) | copy-start | bytes 2359300
  278.6 2.6 collective-permute-start.38
  278.7 3.6 %collective-permute-start.39 = (bf16[3,1,512,256]{3,2,1,0:T(8,128)(2,1)}, bf16[3,1,512,256]{3,2,1,0:T(8,128)(2,1)S(1)}, u32[]{:S(2)}, u32[]{:S(2)}) collective-permute-start(bf16[3,1,512,256]{3,2,1,0:T(8,128)(2,1)} %collective-permute-done.35.refs_8_), channel_id=1, source_target_pairs={{0,4},{4,0},{1,5},{5,1},{2,6},{6,2},{3,7},{7,3},{8,12},{12,8},{9,1... | collective-permute-start | bytes 2359304 | tf_op jit(solution)/shard_map/ppermute | solution.py:30
  289.7 9.2 %collective-permute-start.40 = (bf16[128,384]{1,0:T(8,128)(2,1)S(1)}, bf16[128,384]{1,0:T(8,128)(2,1)S(1)}, u32[]{:S(2)}, u32[]{:S(2)}) collective-permute-start(bf16[128,384]{1,0:T(8,128)(2,1)S(1)} %get-tuple-element.107), channel_id=1, source_target_pairs={{0,2},{1,3},{2,0},{3,1},{4,6},{5,7},{6,4},{7,5},{8,10},{9,11},{10,... | collective-permute-start | bytes 294920 | tf_op jit(solution)/shard_map/ppermute | solution.py:30
  289.7 9.1 %collective-permute-start.41 = (bf16[128,384]{1,0:T(8,128)(2,1)S(1)}, bf16[128,384]{1,0:T(8,128)(2,1)S(1)}, u32[]{:S(2)}, u32[]{:S(2)}) collective-permute-start(bf16[128,384]{1,0:T(8,128)(2,1)S(1)} %get-tuple-element.106), channel_id=1, source_target_pairs={{0,1},{1,0},{2,3},{3,2},{4,5},{5,4},{6,7},{7,6},{8,9},{9,8},{10,11... | collective-permute-start | bytes 294920 | tf_op jit(solution)/shard_map/ppermute | solution.py:30
  289.8 9.1 %collective-permute-start.42 = (bf16[128,384]{1,0:T(8,128)(2,1)S(1)}, bf16[128,384]{1,0:T(8,128)(2,1)S(1)}, u32[]{:S(2)}, u32[]{:S(2)}) collective-permute-start(bf16[128,384]{1,0:T(8,128)(2,1)S(1)} %get-tuple-element.105), channel_id=1, source_target_pairs={{0,3},{1,2},{2,1},{3,0},{4,7},{5,6},{6,5},{7,4},{8,11},{9,10},{10,... | collective-permute-start | bytes 294920 | tf_op jit(solution)/shard_map/ppermute | solution.py:30
  299.9 1.6 collective-permute-start.43
  301.7 16.7 %copy-start.18 = (s32[16,1024]{1,0:T(8,128)S(1)}, s32[16,1024]{1,0:T(8,128)}, u32[]{:S(2)}) copy-start(s32[16,1024]{1,0:T(8,128)} %param.33) | copy-start | bytes 196612
  301.9 18.6 %copy-start.1 = (bf16[256,2048]{1,0:T(8,128)(2,1)S(1)}, bf16[256,2048]{1,0:T(8,128)(2,1)}, u32[]{:S(2)}) copy-start(bf16[256,2048]{1,0:T(8,128)(2,1)} %param.28) | copy-start | bytes 3145732
  302.3 6.3 %collective-permute-start.46 = (bf16[32,2048]{1,0:T(8,128)(2,1)S(1)}, bf16[32,2048]{1,0:T(8,128)(2,1)S(1)}, u32[]{:S(2)}, u32[]{:S(2)}) collective-permute-start(bf16[32,2048]{1,0:T(8,128)(2,1)S(1)} %get-tuple-element.99), channel_id=1, source_target_pairs={{0,3},{1,0},{2,1},{3,2},{4,7},{5,4},{6,5},{7,6},{8,11},{9,8},{10,9... | collective-permute-start | bytes 393224 | tf_op jit(solution)/shard_map/ppermute | solution.py:69
  304.4 13.8 %collective-permute-start.45 = (bf16[32,2048]{1,0:T(8,128)(2,1)S(1)}, bf16[32,2048]{1,0:T(8,128)(2,1)S(1)}, u32[]{:S(2)}, u32[]{:S(2)}) collective-permute-start(bf16[32,2048]{1,0:T(8,128)(2,1)S(1)} %get-tuple-element.100), channel_id=1, source_target_pairs={{0,2},{1,3},{2,0},{3,1},{4,6},{5,7},{6,4},{7,5},{8,10},{9,11},{10,... | collective-permute-start | bytes 393224 | tf_op jit(solution)/shard_map/ppermute | solution.py:69
  306.3 11.9 %collective-permute-start.44 = (bf16[32,2048]{1,0:T(8,128)(2,1)S(1)}, bf16[32,2048]{1,0:T(8,128)(2,1)S(1)}, u32[]{:S(2)}, u32[]{:S(2)}) collective-permute-start(bf16[32,2048]{1,0:T(8,128)(2,1)S(1)} %get-tuple-element.98), channel_id=1, source_target_pairs={{0,1},{1,2},{2,3},{3,0},{4,5},{5,6},{6,7},{7,4},{8,9},{9,10},{10,1... | collective-permute-start | bytes 393224 | tf_op jit(solution)/shard_map/ppermute | solution.py:69
  318.3 1.4 collective-permute-start.47
  (9 other events, 23.7 us)
Sparse Core Ops, SparseCore 0:
  11.5 110.6 all-gather.2

commit v13 on v12

--- a/solution.py
+++ b/solution.py
@@ -116,19 +116,21 @@
     _, blocks, block, _ = x_ref.shape
     rows, depth = blocks * block, gate_ref.shape[0]
 
-    for k in range(ins):
-
-        @pl.when(step == k)
+    @pl.when(step < ins)
+    def _():
+        part = x_ref[0].reshape(rows, depth)
+        one = jnp.dot(part, gate_ref[...], preferred_element_type=F32)
+        two = jnp.dot(part, up_ref[...], preferred_element_type=F32)
+
+        @pl.when(step == 0)
         def _():
-            part = x_ref[0, :, :, k * depth : (k + 1) * depth].reshape(rows, depth)
-            one = jnp.dot(part, gate_ref[...], preferred_element_type=F32)
-            two = jnp.dot(part, up_ref[...], preferred_element_type=F32)
-            if k == 0:
-                gate[...] = one
-                up[...] = two
-            else:
-                gate[...] += one
-                up[...] += two
+            gate[...] = one
+            up[...] = two
+
+        @pl.when(step > 0)
+        def _():
+            gate[...] += one
+            up[...] += two
 
     @pl.when(step == ins)
     def _():
@@ -153,7 +155,7 @@
             grid=(ins + outs,),
             in_specs=[
                 pl.BlockSpec(
-                    (1, blocks, block, features), lambda i, t: (t[0], 0, 0, 0), pipeline_mode=pl.Buffered(1)
+                    (1, blocks, block, depth), lambda i, t: (t[0], 0, 0, jnp.minimum(i, ins - 1))
                 ),
                 pl.BlockSpec(
                     (depth, units), lambda i, t: (jnp.minimum(i, ins - 1), 0)
@@ -314,12 +316,12 @@
     cq = both_halves(jnp.dot(crossin, cross_q, preferred_element_type=F32)).astype(BF16)
     cq = jnp.roll(cq.reshape(count, 2, rows, HD), tensor, axis=0)
     cq = jnp.transpose(cq, (1, 0, 2, 3)).reshape(2 * count * rows, HD)
-    x, cq, other_head = lax.optimization_barrier((x, cq, own_head[1]))
-    own_head[1] = other_head
     heads = [0]
     for bit in near_bits("tensor")[::-1]:
         heads += [m ^ bit for m in heads]
     queries = jnp.stack([cq] + [swap(cq, "tensor", m) for m in heads[1:]])
+    x, queries, other_head = lax.optimization_barrier((x, queries, own_head[1]))
+    own_head[1] = other_head
 
     depth = cross_kv.shape[0] // groups
     share = lax.dynamic_slice_in_dim(own_head[0], group * depth, depth, 1)[None]
@@ -329,7 +331,7 @@
         share = jnp.concatenate([share, swap(share, "tensor", bit)], 0)
 
     theirs = ffn(x, jnp.concatenate([(1 - section)[None], slot_chip]), w_gate, w_up, w_down)
-    theirs, queries, share = lax.optimization_barrier((theirs, queries, share))
+    theirs, share = lax.optimization_barrier((theirs, share))
     got = swap(theirs, "section", 1)
     x = gated(x, share)
     last = swap(share, "tensor", bits[-1])

time: 332 us -> 328 us (0.988); the launches traced: 328 us -> 327 us
  waiting for transfers between devices: 159 us -> 152 us
  starting transfers between devices: 67.3 us -> 73.2 us
    all_gather x1, waiting for transfers between devices: 16.5 us -> 3.32 us  [per_device(): x = lax.all_gather(normed, ('section', 'tensor'), axis=0, tiled=False)]
    ppermute x30, starting transfers between devices: 20.9 us -> 27.1 us  [swap(): lax.ppermute(value, axis, [(i, i ^ distance) for i in range(lax.axis_size...]
    ppermute x30, waiting for transfers between devices: 25.1 us -> 31.2 us  [swap(): lax.ppermute(value, axis, [(i, i ^ distance) for i in range(lax.axis_size...]
  transfers between devices with their start and end apart: 49 -> 49, of which waited for: 25 -> 28; matrix products, arithmetic and copies ran while one was open for 7% -> 7% of each run, Pallas kernels for 14% -> 14%
where the time goes in v13:
time: 328 us; the launch traced here: 327 us
  waiting for transfers between devices  152 us (46%)
  starting transfers between devices  73.2 us (22%)
  Pallas kernels  52.8 us (16%)
  other arithmetic  19.8 us (6%)
  between operations  14.8 us (5%)
  local copies, waits for them, and re-layouts  11.6 us (4%)
  matrix products  3.45 us (1%)
    pallas_call x2, Pallas kernels, ffn(): pl.pallas_call(functools.partial(ffn_kernel, ins), grid_spec=pltpu.Prefet...  45.5 us
    ppermute x3, waiting for transfers between devices, sum_step(): above = lax.ppermute(sends[0], 'tensor', [(i, i + 1) for i in range(step)])  45.2 us
    ppermute x6, waiting for transfers between devices, slots_sum(): lax.ppermute(product[o], 'tensor', [(i, (i + o) % count) for i in range(c...  40.8 us
    ppermute x30, waiting for transfers between devices, swap(): lax.ppermute(value, axis, [(i, i ^ distance) for i in range(lax.axis_size...  31.2 us
    ppermute x30, starting transfers between devices, swap(): lax.ppermute(value, axis, [(i, i ^ distance) for i in range(lax.axis_size...  27.1 us
    ppermute x6, waiting for transfers between devices, from_slots(): lax.ppermute(value, 'tensor', [(i, (i - o) % count) for i in range(count)])  26 us
    ppermute x6, starting transfers between devices, slots_sum(): lax.ppermute(product[o], 'tensor', [(i, (i + o) % count) for i in range(c...  17.6 us
    ppermute x3, starting transfers between devices, sum_step(): above = lax.ppermute(sends[0], 'tensor', [(i, i + 1) for i in range(step)])  14.8 us
  transfers between devices with their start and end apart: 49, of which 28 were waited for; matrix products, arithmetic and copies ran while one was open for 7% of the time, Pallas kernels for 14%

profile of v13, /device:TPU:0, one launch (start us, length us, event | category | flops | bytes accessed | tf_op | source)
XLA Modules:
  0.0 327.3 jit_solution(8733728774041428139)
XLA Ops:
  7.2 1.6 fusion.3
  8.9 2.5 fusion.5
  12.2 0.9 collective-permute-done
  13.2 3.0 collective-permute-start.3
  16.1 2.6 collective-permute-start.2
  18.7 1.3 collective-permute-start.1
  20.1 2.5 collective-permute-done.3
  22.6 8.8 %collective-permute-done.2 = bf16[32,2048]{1,0:T(8,128)(2,1)S(1)} collective-permute-done((bf16[32,2048]{1,0:T(8,128)(2,1)S(1)}, bf16[32,2048]{1,0:T(8,128)(2,1)S(1)}, u32[]{:S(2)}, u32[]{:S(2)}) %collective-permute-start.2) | collective-permute-done | bytes 131104 | tf_op jit(solution)/shard_map/ppermute | solution.py:36
  31.4 1.5 convolution_bitcast_fusion
  33.9 1.5 collective-permute-done.4
  36.2 12.9 %collective-permute-start.7 = (bf16[32,2048]{1,0:T(8,128)(2,1)S(1)}, bf16[32,2048]{1,0:T(8,128)(2,1)S(1)}, u32[]{:S(2)}, u32[]{:S(2)}) collective-permute-start(bf16[32,2048]{1,0:T(8,128)(2,1)S(1)} %get-tuple-element.100), channel_id=1, source_target_pairs={{0,3},{1,0},{2,1},{3,2},{4,7},{5,4},{6,5},{7,6},{8,11},{9,8},{10,9... | collective-permute-start | bytes 393224 | tf_op jit(solution)/shard_map/ppermute | solution.py:69
  49.8 8.0 %collective-permute-done.7 = bf16[32,2048]{1,0:T(8,128)(2,1)S(1)} collective-permute-done((bf16[32,2048]{1,0:T(8,128)(2,1)S(1)}, bf16[32,2048]{1,0:T(8,128)(2,1)S(1)}, u32[]{:S(2)}, u32[]{:S(2)}) %collective-permute-start.7) | collective-permute-done | bytes 131104 | tf_op jit(solution)/shard_map/ppermute | solution.py:69
  57.8 20.9 %collective-permute-done.6 = bf16[32,2048]{1,0:T(8,128)(2,1)S(1)} collective-permute-done((bf16[32,2048]{1,0:T(8,128)(2,1)S(1)}, bf16[32,2048]{1,0:T(8,128)(2,1)S(1)}, u32[]{:S(2)}, u32[]{:S(2)}) %collective-permute-start.6) | collective-permute-done | bytes 131104 | tf_op jit(solution)/shard_map/ppermute | solution.py:69
  78.8 1.9 copy.38
  81.7 3.5 %collective-permute-done.9 = bf16[16,2048]{1,0:T(8,128)(2,1)S(1)} collective-permute-done((bf16[16,2048]{1,0:T(8,128)(2,1)S(1)}, bf16[16,2048]{1,0:T(8,128)(2,1)S(1)}, u32[]{:S(2)}, u32[]{:S(2)}) %collective-permute-start.9) | collective-permute-done | bytes 65568 | tf_op jit(solution)/shard_map/ppermute | solution.py:30
  85.4 3.7 %collective-permute-start.10 = (bf16[32,2048]{1,0:T(8,128)(2,1)S(1)}, bf16[32,2048]{1,0:T(8,128)(2,1)S(1)}, u32[]{:S(2)}, u32[]{:S(2)}) collective-permute-start(bf16[32,2048]{1,0:T(8,128)(2,1)S(1)} %maximum_select_fusion.3), channel_id=1, source_target_pairs={{0,3},{1,0},{2,1},{3,2},{4,7},{5,4},{6,5},{7,6},{8,11},{9,8},{10,9... | collective-permute-start | bytes 393224 | tf_op jit(solution)/shard_map/ppermute | solution.py:36
  89.1 7.1 %collective-permute-done.12 = bf16[32,2048]{1,0:T(8,128)(2,1)S(1)} collective-permute-done((bf16[32,2048]{1,0:T(8,128)(2,1)S(1)}, bf16[32,2048]{1,0:T(8,128)(2,1)S(1)}, u32[]{:S(2)}, u32[]{:S(2)}) %collective-permute-start.12) | collective-permute-done | bytes 131104 | tf_op jit(solution)/shard_map/ppermute | solution.py:36
  96.3 7.6 %collective-permute-done.11 = bf16[32,2048]{1,0:T(8,128)(2,1)S(1)} collective-permute-done((bf16[32,2048]{1,0:T(8,128)(2,1)S(1)}, bf16[32,2048]{1,0:T(8,128)(2,1)S(1)}, u32[]{:S(2)}, u32[]{:S(2)}) %collective-permute-start.11) | collective-permute-done | bytes 131104 | tf_op jit(solution)/shard_map/ppermute | solution.py:36
  104.5 1.2 collective-permute-done.13
  105.7 8.7 %collective-permute-start.16 = (bf16[128,256]{1,0:T(8,128)(2,1)S(1)}, bf16[128,256]{1,0:T(8,128)(2,1)S(1)}, u32[]{:S(2)}, u32[]{:S(2)}) collective-permute-start(bf16[128,256]{1,0:T(8,128)(2,1)S(1)} %bitcast.94), channel_id=1, source_target_pairs={{0,3},{1,2},{2,1},{3,0},{4,7},{5,6},{6,5},{7,4},{8,11},{9,10},{10,... | collective-permute-start | bytes 196616 | tf_op jit(solution)/shard_map/ppermute | solution.py:30
  114.9 1.4 collective-permute-start.14
  116.9 2.6 collective-permute-done.15
  119.6 4.9 %collective-permute-done.14 = bf16[128,256]{1,0:T(8,128)(2,1)S(1)} collective-permute-done((bf16[128,256]{1,0:T(8,128)(2,1)S(1)}, bf16[128,256]{1,0:T(8,128)(2,1)S(1)}, u32[]{:S(2)}, u32[]{:S(2)}) %collective-permute-start.14) | collective-permute-done | bytes 65568 | tf_op jit(solution)/shard_map/ppermute | solution.py:30
  124.5 3.3 %all-gather.3.cloned.1.call-done = bf16[1024,4096]{1,0:T(8,128)(2,1)} async-done(((bf16[128,4096]{1,0:T(8,128)(2,1)}), bf16[1024,4096]{1,0:T(8,128)(2,1)}) %all-gather.3.cloned.1.call-update) | async-done | bytes 8388624 | tf_op jit(solution)/shard_map/all_gather | solution.py:292
  127.9 22.8 %ffn.2 = bf16[512,4096]{1,0:T(8,128)(2,1)S(1)} custom-call(s32[5]{0:T(128)S(1)} %get-tuple-element.115.order, bf16[2,4,128,4096]{3,2,1,0:T(8,128)(2,1)} %bitcast.84, bf16[4096,1024]{1,0:T(8,128)(2,1)} %gate_ref.3, bf16[4096,1024]{1,0:T(8,128)(2,1)} %up_ref.3, bf16[1024,4096]{1,0:T(8,128)(2,1)} %down_ref.3), custom_call_target="tpu_custom_call" | custom-call | flops 1024 | bytes 1024 | tf_op jit(solution)/shard_map/ffn/pallas_call | solution.py:151
  150.7 2.3 collective-permute-done.18
  153.0 1.1 pad_maximum_fusion.1
  154.1 22.8 %ffn.3 = bf16[512,4096]{1,0:T(8,128)(2,1)S(1)} custom-call(s32[5]{0:T(128)S(1)} %get-tuple-element.114.order, bf16[2,4,128,4096]{3,2,1,0:T(8,128)(2,1)} %bitcast.85, bf16[4096,1024]{1,0:T(8,128)(2,1)} %gate_ref.3, bf16[4096,1024]{1,0:T(8,128)(2,1)} %up_ref.3, bf16[1024,4096]{1,0:T(8,128)(2,1)} %down_ref.3), custom_call_target="tpu_custom_call" | custom-call | flops 1024 | bytes 1024 | tf_op jit(solution)/shard_map/ffn/pallas_call | solution.py:151
  176.9 3.1 collective-permute-done.19
  180.8 2.3 collective-permute-start.21
  183.8 1.1 slice.188
  184.8 1.3 fusion.11
  186.2 1.6 collective-permute-start.23
  187.8 1.5 collective-permute-start.24
  189.3 16.1 %collective-permute-done.21 = bf16[128,4096]{1,0:T(8,128)(2,1)S(1)} collective-permute-done((bf16[128,4096]{1,0:T(8,128)(2,1)S(1)}, bf16[128,4096]{1,0:T(8,128)(2,1)S(1)}, u32[]{:S(2)}, u32[]{:S(2)}) %collective-permute-start.21) | collective-permute-done | bytes 1048608 | tf_op jit(solution)/shard_map/ppermute | solution.py:59
  206.6 4.0 %collective-permute-start.25 = (bf16[128,4096]{1,0:T(8,128)(2,1)S(1)}, bf16[128,4096]{1,0:T(8,128)(2,1)S(1)}, u32[]{:S(2)}, u32[]{:S(2)}) collective-permute-start(bf16[128,4096]{1,0:T(8,128)(2,1)S(1)} %get-tuple-element.44), channel_id=1, source_target_pairs={{0,1},{1,2},{4,5},{5,6},{8,9},{9,10},{12,13},{13,14},{16,17},{17,1... | collective-permute-start | bytes 3145736 | tf_op jit(solution)/shard_map/ppermute | solution.py:59
  211.4 1.4 pad_maximum_fusion.refs_2_
  212.8 1.6 collective-permute-start.27
  214.4 1.5 collective-permute-start.28
  215.9 16.3 %collective-permute-done.25 = bf16[128,4096]{1,0:T(8,128)(2,1)S(1)} collective-permute-done((bf16[128,4096]{1,0:T(8,128)(2,1)S(1)}, bf16[128,4096]{1,0:T(8,128)(2,1)S(1)}, u32[]{:S(2)}, u32[]{:S(2)}) %collective-permute-start.25) | collective-permute-done | bytes 1048608 | tf_op jit(solution)/shard_map/ppermute | solution.py:59
  232.7 2.5 add_convert_fusion
  235.2 1.2 copy-done.5
  236.4 0.9 copy-done.9
  237.3 0.9 copy-done.11
  238.2 8.6 %collective-permute-start.32 = (bf16[128,4096]{1,0:T(8,128)(2,1)}, bf16[128,4096]{1,0:T(8,128)(2,1)}, u32[]{:S(2)}, u32[]{:S(2)}) collective-permute-start(bf16[128,4096]{1,0:T(8,128)(2,1)} %get-tuple-element.50), channel_id=1, source_target_pairs={{0,1},{1,2},{2,3},{4,5},{5,6},{6,7},{8,9},{9,10},{10,11},{12,13},{... | collective-permute-start | bytes 3145736 | tf_op jit(solution)/shard_map/ppermute | solution.py:59
  246.8 1.5 collective-permute-start.33
  248.3 1.6 collective-permute-start.34
  249.9 1.5 collective-permute-start.35
  251.4 1.6 shift_right_arithmetic.40
  253.0 3.1 copy.29
  256.4 12.8 %collective-permute-done.32 = bf16[128,4096]{1,0:T(8,128)(2,1)} collective-permute-done((bf16[128,4096]{1,0:T(8,128)(2,1)}, bf16[128,4096]{1,0:T(8,128)(2,1)}, u32[]{:S(2)}, u32[]{:S(2)}) %collective-permute-start.32) | collective-permute-done | bytes 1048608 | tf_op jit(solution)/shard_map/ppermute | solution.py:59
  269.2 5.1 %collective-permute-done.33 = bf16[128,4096]{1,0:T(8,128)(2,1)} collective-permute-done((bf16[128,4096]{1,0:T(8,128)(2,1)}, bf16[128,4096]{1,0:T(8,128)(2,1)}, u32[]{:S(2)}, u32[]{:S(2)}) %collective-permute-start.33) | collective-permute-done | bytes 1048608 | tf_op jit(solution)/shard_map/ppermute | solution.py:60
  274.4 4.2 %fusion = (f32[128]{0:T(128)S(1)}, bf16[128,4096]{1,0:T(8,128)(2,1)S(1)}) fusion(bf16[128,4096]{1,0:T(8,128)(2,1)} %collective-permute-done.33, bf16[128,4096]{1,0:T(8,128)(2,1)} %collective-permute-done.32, bf16[512,4096]{1,0:T(8,128)(2,1)} %copy-done.14, bf16[512,4096]{1,0:T(8,128)(2,1)} %copy-done.2, s32[128,4096]{1,0:T(8,128)} %bitcast.87, ...), kind=kLoop, calls=%fused_computation.10 | loop fusion | flops 9437056 | bytes 8405504 | tf_op jit(solution)/shard_map/reduce_sum | solution.py:18
  279.5 1.6 collective-permute-done.38.refs_14_
  281.2 1.1 collective-permute-done.39.refs_15_
  282.3 7.2 %attend_own_keys.1 = bf16[4,128,384]{2,1,0:T(8,128)(2,1)S(1)} custom-call(s32[16]{0:T(128)S(1)} %pad_add_fusion.3.table, bf16[128,4096]{1,0:T(8,128)(2,1)S(1)} %fusion.2.mem_ref, bf16[4,128,256]{2,1,0:T(8,128)(2,1)S(1)} %pad_maximum_fusion.4.cq_ref, bf16[2,2048,256]{2,1,0:T(8,128)(2,1)S(1)} %bitcast.83, ...), custom_call_target="tpu_custom_call" | custom-call | flops 1024 | bytes 1024 | tf_op jit(solution)/shard_map/attend_own_keys/pallas_call | solution.py:234
  289.8 4.3 %collective-permute-start.42 = (bf16[128,384]{1,0:T(8,128)(2,1)S(1)}, bf16[128,384]{1,0:T(8,128)(2,1)S(1)}, u32[]{:S(2)}, u32[]{:S(2)}) collective-permute-start(bf16[128,384]{1,0:T(8,128)(2,1)S(1)} %get-tuple-element.103), channel_id=1, source_target_pairs={{0,3},{1,2},{2,1},{3,0},{4,7},{5,6},{6,5},{7,4},{8,11},{9,10},{10,... | collective-permute-start | bytes 294920 | tf_op jit(solution)/shard_map/ppermute | solution.py:30
  294.1 4.7 %collective-permute-done.40 = bf16[128,384]{1,0:T(8,128)(2,1)S(1)} collective-permute-done((bf16[128,384]{1,0:T(8,128)(2,1)S(1)}, bf16[128,384]{1,0:T(8,128)(2,1)S(1)}, u32[]{:S(2)}, u32[]{:S(2)}) %collective-permute-start.40) | collective-permute-done | bytes 98336 | tf_op jit(solution)/shard_map/ppermute | solution.py:30
  300.0 1.5 collective-permute-done.43
  302.2 2.2 collective-permute-start.46
  304.4 1.8 collective-permute-start.45
  306.2 2.3 collective-permute-done.46
  308.5 9.6 %collective-permute-done.45 = bf16[32,2048]{1,0:T(8,128)(2,1)S(1)} collective-permute-done((bf16[32,2048]{1,0:T(8,128)(2,1)S(1)}, bf16[32,2048]{1,0:T(8,128)(2,1)S(1)}, u32[]{:S(2)}, u32[]{:S(2)}) %collective-permute-start.45) | collective-permute-done | bytes 131104 | tf_op jit(solution)/shard_map/ppermute | solution.py:69
  318.6 1.1 collective-permute-done.47
  (163 shorter events, 14.8 us)
Async XLA Ops:
  7.2 28.5 %copy-start = (bf16[256,2048]{1,0:T(8,128)(2,1)S(1)}, bf16[256,2048]{1,0:T(8,128)(2,1)}, u32[]{:S(2)}) copy-start(bf16[256,2048]{1,0:T(8,128)(2,1)} %param.28) | copy-start | bytes 3145732
  7.2 120.7 %all-gather.3.cloned.1.call-start = ((), (), s32[]{:S(2)}) async-start(), calls=%async_computation | async-start | bytes 9437184 | tf_op jit(solution)/shard_map/all_gather | solution.py:292
  11.7 1.4 collective-permute-start
  13.2 9.4 %collective-permute-start.3 = (bf16[32,2048]{1,0:T(8,128)(2,1)S(1)}, bf16[32,2048]{1,0:T(8,128)(2,1)S(1)}, u32[]{:S(2)}, u32[]{:S(2)}) collective-permute-start(bf16[32,2048]{1,0:T(8,128)(2,1)S(1)} %maximum_select_fusion.2), channel_id=1, source_target_pairs={{0,1},{1,2},{2,3},{3,0},{4,5},{5,6},{6,7},{7,4},{8,9},{9,10},{10,1... | collective-permute-start | bytes 393224 | tf_op jit(solution)/shard_map/ppermute | solution.py:36
  16.1 15.2 %collective-permute-start.2 = (bf16[32,2048]{1,0:T(8,128)(2,1)S(1)}, bf16[32,2048]{1,0:T(8,128)(2,1)S(1)}, u32[]{:S(2)}, u32[]{:S(2)}) collective-permute-start(bf16[32,2048]{1,0:T(8,128)(2,1)S(1)} %maximum_select_fusion.2), channel_id=1, source_target_pairs={{0,2},{1,3},{2,0},{3,1},{4,6},{5,7},{6,4},{7,5},{8,10},{9,11},{10,... | collective-permute-start | bytes 393224 | tf_op jit(solution)/shard_map/ppermute | solution.py:36
  18.7 12.6 %collective-permute-start.1 = (bf16[32,2048]{1,0:T(8,128)(2,1)S(1)}, bf16[32,2048]{1,0:T(8,128)(2,1)S(1)}, u32[]{:S(2)}, u32[]{:S(2)}) collective-permute-start(bf16[32,2048]{1,0:T(8,128)(2,1)S(1)} %maximum_select_fusion.2), channel_id=1, source_target_pairs={{0,3},{1,0},{2,1},{3,2},{4,7},{5,4},{6,5},{7,6},{8,11},{9,8},{10,9... | collective-permute-start | bytes 393224 | tf_op jit(solution)/shard_map/ppermute | solution.py:36
  20.1 12.8 %copy-start.22 = (bf16[2048,3,256]{2,0,1:T(8,128)(2,1)S(1)}, bf16[2048,3,256]{2,0,1:T(8,128)(2,1)}, u32[]{:S(2)}) copy-start(bf16[2048,3,256]{2,0,1:T(8,128)(2,1)} %param.27) | copy-start | bytes 9437188
  33.6 1.8 collective-permute-start.4
  36.2 21.6 %collective-permute-start.7 = (bf16[32,2048]{1,0:T(8,128)(2,1)S(1)}, bf16[32,2048]{1,0:T(8,128)(2,1)S(1)}, u32[]{:S(2)}, u32[]{:S(2)}) collective-permute-start(bf16[32,2048]{1,0:T(8,128)(2,1)S(1)} %get-tuple-element.100), channel_id=1, source_target_pairs={{0,3},{1,0},{2,1},{3,2},{4,7},{5,4},{6,5},{7,6},{8,11},{9,8},{10,9... | collective-permute-start | bytes 393224 | tf_op jit(solution)/shard_map/ppermute | solution.py:69
  49.1 29.5 %collective-permute-start.6 = (bf16[32,2048]{1,0:T(8,128)(2,1)S(1)}, bf16[32,2048]{1,0:T(8,128)(2,1)S(1)}, u32[]{:S(2)}, u32[]{:S(2)}) collective-permute-start(bf16[32,2048]{1,0:T(8,128)(2,1)S(1)} %get-tuple-element.101), channel_id=1, source_target_pairs={{0,2},{1,3},{2,0},{3,1},{4,6},{5,7},{6,4},{7,5},{8,10},{9,11},{10,... | collective-permute-start | bytes 393224 | tf_op jit(solution)/shard_map/ppermute | solution.py:69
  49.4 29.2 %collective-permute-start.5 = (bf16[32,2048]{1,0:T(8,128)(2,1)S(1)}, bf16[32,2048]{1,0:T(8,128)(2,1)S(1)}, u32[]{:S(2)}, u32[]{:S(2)}) collective-permute-start(bf16[32,2048]{1,0:T(8,128)(2,1)S(1)} %get-tuple-element.99), channel_id=1, source_target_pairs={{0,1},{1,2},{2,3},{3,0},{4,5},{5,6},{6,7},{7,4},{8,9},{9,10},{10,1... | collective-permute-start | bytes 393224 | tf_op jit(solution)/shard_map/ppermute | solution.py:69
  78.7 25.2 %copy-start.23 = (bf16[2048,256]{1,0:T(8,128)(2,1)S(1)}, bf16[2048,256]{1,0:T(8,128)(2,1)}, u32[]{:S(2)}) copy-start(bf16[2048,256]{1,0:T(8,128)(2,1)} %param.30) | copy-start | bytes 3145732
  78.7 2.5 collective-permute-start.8
  80.8 43.8 %collective-permute-start.17 = (bf16[2,2048,256]{2,1,0:T(8,128)(2,1)S(1)}, bf16[2,2048,256]{2,1,0:T(8,128)(2,1)}, u32[]{:S(2)}, u32[]{:S(2)}) collective-permute-start(bf16[2,2048,256]{2,1,0:T(8,128)(2,1)S(1)} %bitcast.82), channel_id=1, source_target_pairs={{0,4},{4,0},{1,5},{5,1},{2,6},{6,2},{3,7},{7,3},{8,12},{12,8},{9,1... | collective-permute-start | bytes 6291464 | tf_op jit(solution)/shard_map/ppermute | solution.py:30
  81.6 3.7 %collective-permute-start.9 = (bf16[16,2048]{1,0:T(8,128)(2,1)S(1)}, bf16[16,2048]{1,0:T(8,128)(2,1)S(1)}, u32[]{:S(2)}, u32[]{:S(2)}) collective-permute-start(bf16[16,2048]{1,0:T(8,128)(2,1)S(1)} %get-tuple-element.111), channel_id=1, source_target_pairs={{0,4},{4,0},{1,5},{5,1},{2,6},{6,2},{3,7},{7,3},{8,12},{12,8},{9,1... | collective-permute-start | bytes 196616 | tf_op jit(solution)/shard_map/ppermute | solution.py:30
  85.2 11.0 %collective-permute-start.12 = (bf16[32,2048]{1,0:T(8,128)(2,1)S(1)}, bf16[32,2048]{1,0:T(8,128)(2,1)S(1)}, u32[]{:S(2)}, u32[]{:S(2)}) collective-permute-start(bf16[32,2048]{1,0:T(8,128)(2,1)S(1)} %maximum_select_fusion.3), channel_id=1, source_target_pairs={{0,1},{1,2},{2,3},{3,0},{4,5},{5,6},{6,7},{7,4},{8,9},{9,10},{10,1... | collective-permute-start | bytes 393224 | tf_op jit(solution)/shard_map/ppermute | solution.py:36
  85.3 18.6 %collective-permute-start.11 = (bf16[32,2048]{1,0:T(8,128)(2,1)S(1)}, bf16[32,2048]{1,0:T(8,128)(2,1)S(1)}, u32[]{:S(2)}, u32[]{:S(2)}) collective-permute-start(bf16[32,2048]{1,0:T(8,128)(2,1)S(1)} %maximum_select_fusion.3), channel_id=1, source_target_pairs={{0,2},{1,3},{2,0},{3,1},{4,6},{5,7},{6,4},{7,5},{8,10},{9,11},{10,... | collective-permute-start | bytes 393224 | tf_op jit(solution)/shard_map/ppermute | solution.py:36
  85.4 18.5 %collective-permute-start.10 = (bf16[32,2048]{1,0:T(8,128)(2,1)S(1)}, bf16[32,2048]{1,0:T(8,128)(2,1)S(1)}, u32[]{:S(2)}, u32[]{:S(2)}) collective-permute-start(bf16[32,2048]{1,0:T(8,128)(2,1)S(1)} %maximum_select_fusion.3), channel_id=1, source_target_pairs={{0,3},{1,0},{2,1},{3,2},{4,7},{5,4},{6,5},{7,6},{8,11},{9,8},{10,9... | collective-permute-start | bytes 393224 | tf_op jit(solution)/shard_map/ppermute | solution.py:36
  104.2 1.4 collective-permute-start.13
  105.7 11.2 %collective-permute-start.16 = (bf16[128,256]{1,0:T(8,128)(2,1)S(1)}, bf16[128,256]{1,0:T(8,128)(2,1)S(1)}, u32[]{:S(2)}, u32[]{:S(2)}) collective-permute-start(bf16[128,256]{1,0:T(8,128)(2,1)S(1)} %bitcast.94), channel_id=1, source_target_pairs={{0,3},{1,2},{2,1},{3,0},{4,7},{5,6},{6,5},{7,4},{8,11},{9,10},{10,... | collective-permute-start | bytes 196616 | tf_op jit(solution)/shard_map/ppermute | solution.py:30
  114.4 5.1 %collective-permute-start.15 = (bf16[128,256]{1,0:T(8,128)(2,1)S(1)}, bf16[128,256]{1,0:T(8,128)(2,1)S(1)}, u32[]{:S(2)}, u32[]{:S(2)}) collective-permute-start(bf16[128,256]{1,0:T(8,128)(2,1)S(1)} %bitcast.95), channel_id=1, source_target_pairs={{0,1},{1,0},{2,3},{3,2},{4,5},{5,4},{6,7},{7,6},{8,9},{9,8},{10,11... | collective-permute-start | bytes 196616 | tf_op jit(solution)/shard_map/ppermute | solution.py:30
  114.9 9.6 %collective-permute-start.14 = (bf16[128,256]{1,0:T(8,128)(2,1)S(1)}, bf16[128,256]{1,0:T(8,128)(2,1)S(1)}, u32[]{:S(2)}, u32[]{:S(2)}) collective-permute-start(bf16[128,256]{1,0:T(8,128)(2,1)S(1)} %bitcast.96), channel_id=1, source_target_pairs={{0,2},{1,3},{2,0},{3,1},{4,6},{5,7},{6,4},{7,5},{8,10},{9,11},{10,... | collective-permute-start | bytes 196616 | tf_op jit(solution)/shard_map/ppermute | solution.py:30
  127.9 25.1 %collective-permute-start.18 = (bf16[1,2,512,256]{3,2,1,0:T(8,128)(2,1)S(1)}, bf16[1,2,512,256]{3,2,1,0:T(8,128)(2,1)S(1)}, u32[]{:S(2)}, u32[]{:S(2)}) collective-permute-start(bf16[1,2,512,256]{3,2,1,0:T(8,128)(2,1)S(1)} %dynamic-slice_bitcast_fusion), channel_id=1, source_target_pairs={{0,2},{1,3},{2,0},{3,1},{4,6},{5,7},{6,4},{7,5},{8,10},{9,11},{10,... | collective-permute-start | bytes 1572872 | tf_op jit(solution)/shard_map/ppermute | solution.py:30
  154.1 25.9 %collective-permute-start.20 = (bf16[512,4096]{1,0:T(8,128)(2,1)S(1)}, bf16[512,4096]{1,0:T(8,128)(2,1)S(1)}, u32[]{:S(2)}, u32[]{:S(2)}) collective-permute-start(bf16[512,4096]{1,0:T(8,128)(2,1)S(1)} %ffn.2), channel_id=1, source_target_pairs={{0,4},{4,0},{1,5},{5,1},{2,6},{6,2},{3,7},{7,3},{8,12},{12,8},{9,1... | collective-permute-start | bytes 12582920 | tf_op jit(solution)/shard_map/ppermute | solution.py:30
  154.1 25.8 %collective-permute-start.19 = (bf16[2,2,512,256]{3,2,1,0:T(8,128)(2,1)}, bf16[2,2,512,256]{3,2,1,0:T(8,128)(2,1)}, u32[]{:S(2)}, u32[]{:S(2)}) collective-permute-start(bf16[2,2,512,256]{3,2,1,0:T(8,128)(2,1)} %pad_maximum_fusion.1), channel_id=1, source_target_pairs={{0,1},{1,0},{2,3},{3,2},{4,5},{5,4},{6,7},{7,6},{8,9},{9,8},{10,11... | collective-permute-start | bytes 3145736 | tf_op jit(solution)/shard_map/ppermute | solution.py:30
  176.9 55.8 %copy-start.2 = (bf16[512,4096]{1,0:T(8,128)(2,1)}, bf16[512,4096]{1,0:T(8,128)(2,1)S(1)}, u32[]{:S(2)}) copy-start(bf16[512,4096]{1,0:T(8,128)(2,1)S(1)} %ffn.3) | copy-start | bytes 12582916
  180.0 52.7 %copy-start.14 = (bf16[512,4096]{1,0:T(8,128)(2,1)}, bf16[512,4096]{1,0:T(8,128)(2,1)S(1)}, u32[]{:S(2)}) copy-start(bf16[512,4096]{1,0:T(8,128)(2,1)S(1)} %collective-permute-done.20) | copy-start | bytes 12582916
  180.8 24.6 %collective-permute-start.21 = (bf16[128,4096]{1,0:T(8,128)(2,1)S(1)}, bf16[128,4096]{1,0:T(8,128)(2,1)S(1)}, u32[]{:S(2)}, u32[]{:S(2)}) collective-permute-start(bf16[128,4096]{1,0:T(8,128)(2,1)S(1)} %get-tuple-element.91), channel_id=1, source_target_pairs={{0,1},{4,5},{8,9},{12,13},{16,17},{20,21},{24,25},{28,29}} | collective-permute-start | bytes 3145736 | tf_op jit(solution)/shard_map/ppermute | solution.py:59
  183.0 22.4 %collective-permute-start.22 = (bf16[128,4096]{1,0:T(8,128)(2,1)S(1)}, bf16[128,4096]{1,0:T(8,128)(2,1)S(1)}, u32[]{:S(2)}, u32[]{:S(2)}) collective-permute-start(bf16[128,4096]{1,0:T(8,128)(2,1)S(1)} %get-tuple-element.90), channel_id=1, source_target_pairs={{3,2},{7,6},{11,10},{15,14},{19,18},{23,22},{27,26},{31,30}} | collective-permute-start | bytes 3145736 | tf_op jit(solution)/shard_map/ppermute | solution.py:60
  186.2 20.0 %collective-permute-start.23 = (bf16[3,1,512,256]{3,2,1,0:T(8,128)(2,1)S(1)}, bf16[3,1,512,256]{3,2,1,0:T(8,128)(2,1)S(1)}, u32[]{:S(2)}, u32[]{:S(2)}) collective-permute-start(bf16[3,1,512,256]{3,2,1,0:T(8,128)(2,1)S(1)} %get-tuple-element.95), channel_id=1, source_target_pairs={{0,8},{8,0},{16,24},{24,16},{1,9},{9,1},{17,25},{25,17},{2,10},{10... | collective-permute-start | bytes 2359304 | tf_op jit(solution)/shard_map/ppermute | solution.py:30
  187.8 18.9 %collective-permute-start.24 = (bf16[3,1,512,256]{3,2,1,0:T(8,128)(2,1)S(1)}, bf16[3,1,512,256]{3,2,1,0:T(8,128)(2,1)}, u32[]{:S(2)}, u32[]{:S(2)}) collective-permute-start(bf16[3,1,512,256]{3,2,1,0:T(8,128)(2,1)S(1)} %get-tuple-element.95), channel_id=1, source_target_pairs={{0,16},{8,24},{16,0},{24,8},{1,17},{9,25},{17,1},{25,9},{2,18},{10... | collective-permute-start | bytes 2359304 | tf_op jit(solution)/shard_map/ppermute | solution.py:30
  206.2 29.0 %copy-start.7 = (bf16[3,1,512,256]{3,2,1,0:T(8,128)(2,1)}, bf16[3,1,512,256]{3,2,1,0:T(8,128)(2,1)S(1)}, u32[]{:S(2)}) copy-start(bf16[3,1,512,256]{3,2,1,0:T(8,128)(2,1)S(1)} %collective-permute-done.23.refs_3_) | copy-start | bytes 2359300
  206.6 25.5 %collective-permute-start.25 = (bf16[128,4096]{1,0:T(8,128)(2,1)S(1)}, bf16[128,4096]{1,0:T(8,128)(2,1)S(1)}, u32[]{:S(2)}, u32[]{:S(2)}) collective-permute-start(bf16[128,4096]{1,0:T(8,128)(2,1)S(1)} %get-tuple-element.44), channel_id=1, source_target_pairs={{0,1},{1,2},{4,5},{5,6},{8,9},{9,10},{12,13},{13,14},{16,17},{17,1... | collective-permute-start | bytes 3145736 | tf_op jit(solution)/shard_map/ppermute | solution.py:59
  210.6 21.5 %collective-permute-start.26 = (bf16[128,4096]{1,0:T(8,128)(2,1)S(1)}, bf16[128,4096]{1,0:T(8,128)(2,1)S(1)}, u32[]{:S(2)}, u32[]{:S(2)}) collective-permute-start(bf16[128,4096]{1,0:T(8,128)(2,1)S(1)} %get-tuple-element.45), channel_id=1, source_target_pairs={{2,1},{3,2},{6,5},{7,6},{10,9},{11,10},{14,13},{15,14},{18,17},{19... | collective-permute-start | bytes 3145736 | tf_op jit(solution)/shard_map/ppermute | solution.py:60
  212.7 22.4 %copy-start.3 = (bf16[3,2,512,256]{3,2,1,0:T(8,128)(2,1)}, bf16[3,2,512,256]{3,2,1,0:T(8,128)(2,1)S(1)}, u32[]{:S(2)}) copy-start(bf16[3,2,512,256]{3,2,1,0:T(8,128)(2,1)S(1)} %pad_maximum_fusion.refs_2_) | copy-start | bytes 4718596
  212.7 22.4 %collective-permute-start.29 = (bf16[3,2,512,256]{3,2,1,0:T(8,128)(2,1)S(1)}, bf16[3,2,512,256]{3,2,1,0:T(8,128)(2,1)S(1)}, u32[]{:S(2)}, u32[]{:S(2)}) collective-permute-start(bf16[3,2,512,256]{3,2,1,0:T(8,128)(2,1)S(1)} %pad_maximum_fusion.refs_2_), channel_id=1, source_target_pairs={{0,4},{4,0},{1,5},{5,1},{2,6},{6,2},{3,7},{7,3},{8,12},{12,8},{9,1... | collective-permute-start | bytes 4718600 | tf_op jit(solution)/shard_map/ppermute | solution.py:30
  212.8 22.4 %collective-permute-start.27 = (bf16[3,1,512,256]{3,2,1,0:T(8,128)(2,1)S(1)}, bf16[3,1,512,256]{3,2,1,0:T(8,128)(2,1)}, u32[]{:S(2)}, u32[]{:S(2)}) collective-permute-start(bf16[3,1,512,256]{3,2,1,0:T(8,128)(2,1)S(1)} %get-tuple-element.94), channel_id=1, source_target_pairs={{0,8},{8,0},{16,24},{24,16},{1,9},{9,1},{17,25},{25,17},{2,10},{10... | collective-permute-start | bytes 2359304 | tf_op jit(solution)/shard_map/ppermute | solution.py:30
  214.4 20.8 %collective-permute-start.28 = (bf16[3,1,512,256]{3,2,1,0:T(8,128)(2,1)S(1)}, bf16[3,1,512,256]{3,2,1,0:T(8,128)(2,1)}, u32[]{:S(2)}, u32[]{:S(2)}) collective-permute-start(bf16[3,1,512,256]{3,2,1,0:T(8,128)(2,1)S(1)} %get-tuple-element.94), channel_id=1, source_target_pairs={{0,16},{8,24},{16,0},{24,8},{1,17},{9,25},{17,1},{25,9},{2,18},{10... | collective-permute-start | bytes 2359304 | tf_op jit(solution)/shard_map/ppermute | solution.py:30
  232.2 4.2 %collective-permute-start.30 = (bf16[3,1,512,256]{3,2,1,0:T(8,128)(2,1)S(1)}, bf16[3,1,512,256]{3,2,1,0:T(8,128)(2,1)S(1)}, u32[]{:S(2)}, u32[]{:S(2)}) collective-permute-start(bf16[3,1,512,256]{3,2,1,0:T(8,128)(2,1)S(1)} %collective-permute-done.23.refs_3_), channel_id=1, source_target_pairs={{0,4},{4,0},{1,5},{5,1},{2,6},{6,2},{3,7},{7,3},{8,12},{12,8},{9,1... | collective-permute-start | bytes 2359304 | tf_op jit(solution)/shard_map/ppermute | solution.py:30
  232.2 5.1 %collective-permute-start.31 = (bf16[3,1,512,256]{3,2,1,0:T(8,128)(2,1)}, bf16[3,1,512,256]{3,2,1,0:T(8,128)(2,1)S(1)}, u32[]{:S(2)}, u32[]{:S(2)}) collective-permute-start(bf16[3,1,512,256]{3,2,1,0:T(8,128)(2,1)} %collective-permute-done.24.refs_4_), channel_id=1, source_target_pairs={{0,4},{4,0},{1,5},{5,1},{2,6},{6,2},{3,7},{7,3},{8,12},{12,8},{9,1... | collective-permute-start | bytes 2359304 | tf_op jit(solution)/shard_map/ppermute | solution.py:30
  238.2 31.0 %collective-permute-start.32 = (bf16[128,4096]{1,0:T(8,128)(2,1)}, bf16[128,4096]{1,0:T(8,128)(2,1)}, u32[]{:S(2)}, u32[]{:S(2)}) collective-permute-start(bf16[128,4096]{1,0:T(8,128)(2,1)} %get-tuple-element.50), channel_id=1, source_target_pairs={{0,1},{1,2},{2,3},{4,5},{5,6},{6,7},{8,9},{9,10},{10,11},{12,13},{... | collective-permute-start | bytes 3145736 | tf_op jit(solution)/shard_map/ppermute | solution.py:59
  246.8 27.5 %collective-permute-start.33 = (bf16[128,4096]{1,0:T(8,128)(2,1)}, bf16[128,4096]{1,0:T(8,128)(2,1)}, u32[]{:S(2)}, u32[]{:S(2)}) collective-permute-start(bf16[128,4096]{1,0:T(8,128)(2,1)} %get-tuple-element.51), channel_id=1, source_target_pairs={{1,0},{2,1},{3,2},{5,4},{6,5},{7,6},{9,8},{10,9},{11,10},{13,12},{... | collective-permute-start | bytes 3145736 | tf_op jit(solution)/shard_map/ppermute | solution.py:60
  248.3 26.0 %collective-permute-start.34 = (bf16[3,1,512,256]{3,2,1,0:T(8,128)(2,1)}, bf16[3,1,512,256]{3,2,1,0:T(8,128)(2,1)}, u32[]{:S(2)}, u32[]{:S(2)}) collective-permute-start(bf16[3,1,512,256]{3,2,1,0:T(8,128)(2,1)} %collective-permute-done.24.refs_4_), channel_id=1, source_target_pairs={{0,8},{8,0},{16,24},{24,16},{1,9},{9,1},{17,25},{25,17},{2,10},{10... | collective-permute-start | bytes 2359304 | tf_op jit(solution)/shard_map/ppermute | solution.py:30
  249.9 24.4 %collective-permute-start.35 = (bf16[3,1,512,256]{3,2,1,0:T(8,128)(2,1)}, bf16[3,1,512,256]{3,2,1,0:T(8,128)(2,1)}, u32[]{:S(2)}, u32[]{:S(2)}) collective-permute-start(bf16[3,1,512,256]{3,2,1,0:T(8,128)(2,1)} %collective-permute-done.27.refs_5_), channel_id=1, source_target_pairs={{0,16},{8,24},{16,0},{24,8},{1,17},{9,25},{17,1},{25,9},{2,18},{10... | collective-permute-start | bytes 2359304 | tf_op jit(solution)/shard_map/ppermute | solution.py:30
  253.0 21.3 %copy-start.13 = (bf16[128,4096]{1,0:T(8,128)(2,1)S(1)}, bf16[128,4096]{1,0:T(8,128)(2,1)}, u32[]{:S(2)}) copy-start(bf16[128,4096]{1,0:T(8,128)(2,1)} %param.18) | copy-start | bytes 3145732
  256.3 23.2 %collective-permute-start.36 = (bf16[3,1,512,256]{3,2,1,0:T(8,128)(2,1)}, bf16[3,1,512,256]{3,2,1,0:T(8,128)(2,1)S(1)}, u32[]{:S(2)}, u32[]{:S(2)}) collective-permute-start(bf16[3,1,512,256]{3,2,1,0:T(8,128)(2,1)} %collective-permute-done.27.refs_5_), channel_id=1, source_target_pairs={{0,4},{4,0},{1,5},{5,1},{2,6},{6,2},{3,7},{7,3},{8,12},{12,8},{9,1... | collective-permute-start | bytes 2359304 | tf_op jit(solution)/shard_map/ppermute | solution.py:30
  269.2 10.3 %collective-permute-start.37 = (bf16[3,1,512,256]{3,2,1,0:T(8,128)(2,1)}, bf16[3,1,512,256]{3,2,1,0:T(8,128)(2,1)S(1)}, u32[]{:S(2)}, u32[]{:S(2)}) collective-permute-start(bf16[3,1,512,256]{3,2,1,0:T(8,128)(2,1)} %collective-permute-done.28.refs_6_), channel_id=1, source_target_pairs={{0,4},{4,0},{1,5},{5,1},{2,6},{6,2},{3,7},{7,3},{8,12},{12,8},{9,1... | collective-permute-start | bytes 2359304 | tf_op jit(solution)/shard_map/ppermute | solution.py:30
  274.3 4.9 %copy-start.19 = (f32[4096]{0:T(1024)S(1)}, f32[4096]{0:T(1024)}, u32[]{:S(2)}) copy-start(f32[4096]{0:T(1024)} %param.24) | copy-start | bytes 49156
  274.3 8.0 %copy-start.6 = (bf16[3,2,512,256]{3,2,1,0:T(8,128)(2,1)S(1)}, bf16[3,2,512,256]{3,2,1,0:T(8,128)(2,1)}, u32[]{:S(2)}) copy-start(bf16[3,2,512,256]{3,2,1,0:T(8,128)(2,1)} %copy-done.5) | copy-start | bytes 4718596
  274.3 8.0 %copy-start.8 = (bf16[3,1,512,256]{3,2,1,0:T(8,128)(2,1)S(1)}, bf16[3,1,512,256]{3,2,1,0:T(8,128)(2,1)}, u32[]{:S(2)}) copy-start(bf16[3,1,512,256]{3,2,1,0:T(8,128)(2,1)} %copy-done.7) | copy-start | bytes 2359300
  274.3 8.0 %copy-start.10 = (bf16[3,1,512,256]{3,2,1,0:T(8,128)(2,1)S(1)}, bf16[3,1,512,256]{3,2,1,0:T(8,128)(2,1)}, u32[]{:S(2)}) copy-start(bf16[3,1,512,256]{3,2,1,0:T(8,128)(2,1)} %copy-done.9) | copy-start | bytes 2359300
  274.3 8.0 %copy-start.12 = (bf16[3,1,512,256]{3,2,1,0:T(8,128)(2,1)S(1)}, bf16[3,1,512,256]{3,2,1,0:T(8,128)(2,1)}, u32[]{:S(2)}) copy-start(bf16[3,1,512,256]{3,2,1,0:T(8,128)(2,1)} %copy-done.11) | copy-start | bytes 2359300
  278.6 2.6 collective-permute-start.38
  278.7 3.6 %collective-permute-start.39 = (bf16[3,1,512,256]{3,2,1,0:T(8,128)(2,1)}, bf16[3,1,512,256]{3,2,1,0:T(8,128)(2,1)S(1)}, u32[]{:S(2)}, u32[]{:S(2)}) collective-permute-start(bf16[3,1,512,256]{3,2,1,0:T(8,128)(2,1)} %collective-permute-done.35.refs_8_), channel_id=1, source_target_pairs={{0,4},{4,0},{1,5},{5,1},{2,6},{6,2},{3,7},{7,3},{8,12},{12,8},{9,1... | collective-permute-start | bytes 2359304 | tf_op jit(solution)/shard_map/ppermute | solution.py:30
  289.6 9.1 %collective-permute-start.40 = (bf16[128,384]{1,0:T(8,128)(2,1)S(1)}, bf16[128,384]{1,0:T(8,128)(2,1)S(1)}, u32[]{:S(2)}, u32[]{:S(2)}) collective-permute-start(bf16[128,384]{1,0:T(8,128)(2,1)S(1)} %get-tuple-element.105), channel_id=1, source_target_pairs={{0,2},{1,3},{2,0},{3,1},{4,6},{5,7},{6,4},{7,5},{8,10},{9,11},{10,... | collective-permute-start | bytes 294920 | tf_op jit(solution)/shard_map/ppermute | solution.py:30
  289.7 9.1 %collective-permute-start.41 = (bf16[128,384]{1,0:T(8,128)(2,1)S(1)}, bf16[128,384]{1,0:T(8,128)(2,1)S(1)}, u32[]{:S(2)}, u32[]{:S(2)}) collective-permute-start(bf16[128,384]{1,0:T(8,128)(2,1)S(1)} %get-tuple-element.104), channel_id=1, source_target_pairs={{0,1},{1,0},{2,3},{3,2},{4,5},{5,4},{6,7},{7,6},{8,9},{9,8},{10,11... | collective-permute-start | bytes 294920 | tf_op jit(solution)/shard_map/ppermute | solution.py:30
  289.8 9.0 %collective-permute-start.42 = (bf16[128,384]{1,0:T(8,128)(2,1)S(1)}, bf16[128,384]{1,0:T(8,128)(2,1)S(1)}, u32[]{:S(2)}, u32[]{:S(2)}) collective-permute-start(bf16[128,384]{1,0:T(8,128)(2,1)S(1)} %get-tuple-element.103), channel_id=1, source_target_pairs={{0,3},{1,2},{2,1},{3,0},{4,7},{5,6},{6,5},{7,4},{8,11},{9,10},{10,... | collective-permute-start | bytes 294920 | tf_op jit(solution)/shard_map/ppermute | solution.py:30
  299.9 1.6 collective-permute-start.43
  301.6 16.7 %copy-start.18 = (s32[16,1024]{1,0:T(8,128)S(1)}, s32[16,1024]{1,0:T(8,128)}, u32[]{:S(2)}) copy-start(s32[16,1024]{1,0:T(8,128)} %param.33) | copy-start | bytes 196612
  301.8 18.6 %copy-start.1 = (bf16[256,2048]{1,0:T(8,128)(2,1)S(1)}, bf16[256,2048]{1,0:T(8,128)(2,1)}, u32[]{:S(2)}) copy-start(bf16[256,2048]{1,0:T(8,128)(2,1)} %param.28) | copy-start | bytes 3145732
  302.2 6.3 %collective-permute-start.46 = (bf16[32,2048]{1,0:T(8,128)(2,1)S(1)}, bf16[32,2048]{1,0:T(8,128)(2,1)S(1)}, u32[]{:S(2)}, u32[]{:S(2)}) collective-permute-start(bf16[32,2048]{1,0:T(8,128)(2,1)S(1)} %get-tuple-element.97), channel_id=1, source_target_pairs={{0,3},{1,0},{2,1},{3,2},{4,7},{5,4},{6,5},{7,6},{8,11},{9,8},{10,9... | collective-permute-start | bytes 393224 | tf_op jit(solution)/shard_map/ppermute | solution.py:69
  304.4 13.8 %collective-permute-start.45 = (bf16[32,2048]{1,0:T(8,128)(2,1)S(1)}, bf16[32,2048]{1,0:T(8,128)(2,1)S(1)}, u32[]{:S(2)}, u32[]{:S(2)}) collective-permute-start(bf16[32,2048]{1,0:T(8,128)(2,1)S(1)} %get-tuple-element.98), channel_id=1, source_target_pairs={{0,2},{1,3},{2,0},{3,1},{4,6},{5,7},{6,4},{7,5},{8,10},{9,11},{10,... | collective-permute-start | bytes 393224 | tf_op jit(solution)/shard_map/ppermute | solution.py:69
  306.2 11.9 %collective-permute-start.44 = (bf16[32,2048]{1,0:T(8,128)(2,1)S(1)}, bf16[32,2048]{1,0:T(8,128)(2,1)S(1)}, u32[]{:S(2)}, u32[]{:S(2)}) collective-permute-start(bf16[32,2048]{1,0:T(8,128)(2,1)S(1)} %get-tuple-element.96), channel_id=1, source_target_pairs={{0,1},{1,2},{2,3},{3,0},{4,5},{5,6},{6,7},{7,4},{8,9},{9,10},{10,1... | collective-permute-start | bytes 393224 | tf_op jit(solution)/shard_map/ppermute | solution.py:69
  318.2 1.4 collective-permute-start.47
  (9 other events, 23.7 us)
Sparse Core Ops, SparseCore 0:
  11.5 116.2 all-gather.2

commit v14 on v13

--- a/solution.py
+++ b/solution.py
@@ -146,7 +146,7 @@
 def ffn(x, order, w_gate, w_up, w_down):
     _, blocks, block, features = x.shape
     units = w_gate.shape[1]
-    rows, depth, tile = blocks * block, 512, 1024
+    rows, depth, tile = blocks * block, 1024, 1024
     ins, outs = features // depth, features // tile
     return pl.pallas_call(
         functools.partial(ffn_kernel, ins),
@@ -342,7 +342,7 @@
     came = sum_step(sum_sends(mine, got, None, 1), 1)
     if groups == 4:
         k, v = shares[0][:, :1], shares[0][:, 1:]
-        near = [swap(k, "dp", 1), swap(k, "dp", 2)]
+        near = [swap(k, "dp", 1), swap(k, "dp", 2), swap(shares[0], "section", 1)]
         plan = [(0, 0, 0, 1), (1, 0, 3, 0), (2, 0, 4, 0), (5, 0, 6, 0)]
         swapped = []
     else:
@@ -352,10 +352,12 @@
         sends = sum_sends(mine, got, came, step)
         if step == 2:
             held = lax.optimization_barrier(sends + tuple(near))
-            sends, shares = held[:2], shares + list(held[2:])
             if groups == 4:
+                sends, shares = held[:2], shares + list(held[2:4])
                 near = [swap(v, "dp", 1), swap(v, "dp", 2)]
-                swapped = [swap(y, "section", 1) for y in shares]
+                swapped = [held[4]] + [swap(y, "section", 1) for y in shares[1:]]
+            else:
+                sends, shares = held[:2], shares + list(held[2:])
         if step == count - 1 and groups == 4:
             held = lax.optimization_barrier(sends + tuple(near) + tuple(swapped))
             sends, near, swapped = held[:2], list(held[2:4]), list(held[4:])

time: 328 us -> 325 us (level)
    ppermute x30, waiting for transfers between devices: 31.2 us -> 37 us  [swap(): lax.ppermute(value, axis, [(i, i ^ distance) for i in range(lax.axis_size...]
  transfers between devices with their start and end apart: 49 -> 49, of which waited for: 28 -> 30; matrix products, arithmetic and copies ran while one was open for 7% -> 7% of each run, Pallas kernels for 14% -> 13%
where the time goes in v14:
time: 325 us; the launch traced here: 324 us
  waiting for transfers between devices  155 us (48%)
  starting transfers between devices  70.9 us (22%)
  Pallas kernels  49.6 us (15%)
  other arithmetic  20.3 us (6%)
  between operations  14.8 us (5%)
  local copies, waits for them, and re-layouts  10.4 us (3%)
  matrix products  3.45 us (1%)
    pallas_call x2, Pallas kernels, ffn(): pl.pallas_call(functools.partial(ffn_kernel, ins), grid_spec=pltpu.Prefet...  42.4 us
    ppermute x3, waiting for transfers between devices, sum_step(): above = lax.ppermute(sends[0], 'tensor', [(i, i + 1) for i in range(step)])  42.4 us
    ppermute x6, waiting for transfers between devices, slots_sum(): lax.ppermute(product[o], 'tensor', [(i, (i + o) % count) for i in range(c...  40.8 us
    ppermute x30, waiting for transfers between devices, swap(): lax.ppermute(value, axis, [(i, i ^ distance) for i in range(lax.axis_size...  37 us
    ppermute x30, starting transfers between devices, swap(): lax.ppermute(value, axis, [(i, i ^ distance) for i in range(lax.axis_size...  26.4 us
    ppermute x6, waiting for transfers between devices, from_slots(): lax.ppermute(value, 'tensor', [(i, (i - o) % count) for i in range(count)])  26 us
    ppermute x6, starting transfers between devices, slots_sum(): lax.ppermute(product[o], 'tensor', [(i, (i + o) % count) for i in range(c...  17.7 us
    ppermute x3, starting transfers between devices, sum_step(): above = lax.ppermute(sends[0], 'tensor', [(i, i + 1) for i in range(step)])  13 us
  transfers between devices with their start and end apart: 49, of which 30 were waited for; matrix products, arithmetic and copies ran while one was open for 7% of the time, Pallas kernels for 13%

profile of v14, /device:TPU:0, one launch (start us, length us, event | category | flops | bytes accessed | tf_op | source)
XLA Modules:
  0.0 324.0 jit_solution(13978055757790076822)
XLA Ops:
  7.2 1.6 fusion.3
  8.9 2.5 fusion.5
  13.2 3.0 collective-permute-start.3
  16.1 2.6 collective-permute-start.2
  18.7 1.3 collective-permute-start.1
  20.1 2.5 collective-permute-done.3
  22.6 8.8 %collective-permute-done.2 = bf16[32,2048]{1,0:T(8,128)(2,1)S(1)} collective-permute-done((bf16[32,2048]{1,0:T(8,128)(2,1)S(1)}, bf16[32,2048]{1,0:T(8,128)(2,1)S(1)}, u32[]{:S(2)}, u32[]{:S(2)}) %collective-permute-start.2) | collective-permute-done | bytes 131104 | tf_op jit(solution)/shard_map/ppermute | solution.py:36
  31.4 1.5 convolution_bitcast_fusion
  33.9 1.5 collective-permute-done.4
  36.2 12.9 %collective-permute-start.7 = (bf16[32,2048]{1,0:T(8,128)(2,1)S(1)}, bf16[32,2048]{1,0:T(8,128)(2,1)S(1)}, u32[]{:S(2)}, u32[]{:S(2)}) collective-permute-start(bf16[32,2048]{1,0:T(8,128)(2,1)S(1)} %get-tuple-element.102), channel_id=1, source_target_pairs={{0,3},{1,0},{2,1},{3,2},{4,7},{5,4},{6,5},{7,6},{8,11},{9,8},{10,9... | collective-permute-start | bytes 393224 | tf_op jit(solution)/shard_map/ppermute | solution.py:69
  49.8 8.0 %collective-permute-done.7 = bf16[32,2048]{1,0:T(8,128)(2,1)S(1)} collective-permute-done((bf16[32,2048]{1,0:T(8,128)(2,1)S(1)}, bf16[32,2048]{1,0:T(8,128)(2,1)S(1)}, u32[]{:S(2)}, u32[]{:S(2)}) %collective-permute-start.7) | collective-permute-done | bytes 131104 | tf_op jit(solution)/shard_map/ppermute | solution.py:69
  57.8 20.9 %collective-permute-done.6 = bf16[32,2048]{1,0:T(8,128)(2,1)S(1)} collective-permute-done((bf16[32,2048]{1,0:T(8,128)(2,1)S(1)}, bf16[32,2048]{1,0:T(8,128)(2,1)S(1)}, u32[]{:S(2)}, u32[]{:S(2)}) %collective-permute-start.6) | collective-permute-done | bytes 131104 | tf_op jit(solution)/shard_map/ppermute | solution.py:69
  78.8 1.9 copy.38
  81.7 3.5 %collective-permute-done.9 = bf16[16,2048]{1,0:T(8,128)(2,1)S(1)} collective-permute-done((bf16[16,2048]{1,0:T(8,128)(2,1)S(1)}, bf16[16,2048]{1,0:T(8,128)(2,1)S(1)}, u32[]{:S(2)}, u32[]{:S(2)}) %collective-permute-start.9) | collective-permute-done | bytes 65568 | tf_op jit(solution)/shard_map/ppermute | solution.py:30
  85.4 3.7 %collective-permute-start.10 = (bf16[32,2048]{1,0:T(8,128)(2,1)S(1)}, bf16[32,2048]{1,0:T(8,128)(2,1)S(1)}, u32[]{:S(2)}, u32[]{:S(2)}) collective-permute-start(bf16[32,2048]{1,0:T(8,128)(2,1)S(1)} %maximum_select_fusion.3), channel_id=1, source_target_pairs={{0,3},{1,0},{2,1},{3,2},{4,7},{5,4},{6,5},{7,6},{8,11},{9,8},{10,9... | collective-permute-start | bytes 393224 | tf_op jit(solution)/shard_map/ppermute | solution.py:36
  89.1 7.1 %collective-permute-done.12 = bf16[32,2048]{1,0:T(8,128)(2,1)S(1)} collective-permute-done((bf16[32,2048]{1,0:T(8,128)(2,1)S(1)}, bf16[32,2048]{1,0:T(8,128)(2,1)S(1)}, u32[]{:S(2)}, u32[]{:S(2)}) %collective-permute-start.12) | collective-permute-done | bytes 131104 | tf_op jit(solution)/shard_map/ppermute | solution.py:36
  96.3 7.6 %collective-permute-done.11 = bf16[32,2048]{1,0:T(8,128)(2,1)S(1)} collective-permute-done((bf16[32,2048]{1,0:T(8,128)(2,1)S(1)}, bf16[32,2048]{1,0:T(8,128)(2,1)S(1)}, u32[]{:S(2)}, u32[]{:S(2)}) %collective-permute-start.11) | collective-permute-done | bytes 131104 | tf_op jit(solution)/shard_map/ppermute | solution.py:36
  104.5 1.2 collective-permute-done.13
  105.7 8.7 %collective-permute-start.16 = (bf16[128,256]{1,0:T(8,128)(2,1)S(1)}, bf16[128,256]{1,0:T(8,128)(2,1)S(1)}, u32[]{:S(2)}, u32[]{:S(2)}) collective-permute-start(bf16[128,256]{1,0:T(8,128)(2,1)S(1)} %bitcast.94), channel_id=1, source_target_pairs={{0,3},{1,2},{2,1},{3,0},{4,7},{5,6},{6,5},{7,4},{8,11},{9,10},{10,... | collective-permute-start | bytes 196616 | tf_op jit(solution)/shard_map/ppermute | solution.py:30
  114.9 1.4 collective-permute-start.14
  116.9 2.6 collective-permute-done.15
  119.6 4.9 %collective-permute-done.14 = bf16[128,256]{1,0:T(8,128)(2,1)S(1)} collective-permute-done((bf16[128,256]{1,0:T(8,128)(2,1)S(1)}, bf16[128,256]{1,0:T(8,128)(2,1)S(1)}, u32[]{:S(2)}, u32[]{:S(2)}) %collective-permute-start.14) | collective-permute-done | bytes 65568 | tf_op jit(solution)/shard_map/ppermute | solution.py:30
  124.5 3.3 %all-gather.3.cloned.1.call-done = bf16[1024,4096]{1,0:T(8,128)(2,1)} async-done(((bf16[128,4096]{1,0:T(8,128)(2,1)}), bf16[1024,4096]{1,0:T(8,128)(2,1)}) %all-gather.3.cloned.1.call-update) | async-done | bytes 8388624 | tf_op jit(solution)/shard_map/all_gather | solution.py:292
  127.9 21.2 %ffn.2 = bf16[512,4096]{1,0:T(8,128)(2,1)S(1)} custom-call(s32[5]{0:T(128)S(1)} %get-tuple-element.117.order, bf16[2,4,128,4096]{3,2,1,0:T(8,128)(2,1)} %bitcast.84, bf16[4096,1024]{1,0:T(8,128)(2,1)} %gate_ref.3, bf16[4096,1024]{1,0:T(8,128)(2,1)} %up_ref.3, bf16[1024,4096]{1,0:T(8,128)(2,1)} %down_ref.3), custom_call_target="tpu_custom_call" | custom-call | flops 1024 | bytes 1024 | tf_op jit(solution)/shard_map/ffn/pallas_call | solution.py:151
  149.1 3.9 %collective-permute-done.18 = bf16[1,2,512,256]{3,2,1,0:T(8,128)(2,1)S(1)} collective-permute-done((bf16[1,2,512,256]{3,2,1,0:T(8,128)(2,1)S(1)}, bf16[1,2,512,256]{3,2,1,0:T(8,128)(2,1)S(1)}, u32[]{:S(2)}, u32[]{:S(2)}) %collective-permute-start.18) | collective-permute-done | bytes 524320 | tf_op jit(solution)/shard_map/ppermute | solution.py:30
  153.0 1.1 pad_maximum_fusion.1
  154.1 21.2 %ffn.3 = bf16[512,4096]{1,0:T(8,128)(2,1)S(1)} custom-call(s32[5]{0:T(128)S(1)} %get-tuple-element.116.order, bf16[2,4,128,4096]{3,2,1,0:T(8,128)(2,1)} %bitcast.85, bf16[4096,1024]{1,0:T(8,128)(2,1)} %gate_ref.3, bf16[4096,1024]{1,0:T(8,128)(2,1)} %up_ref.3, bf16[1024,4096]{1,0:T(8,128)(2,1)} %down_ref.3), custom_call_target="tpu_custom_call" | custom-call | flops 1024 | bytes 1024 | tf_op jit(solution)/shard_map/ffn/pallas_call | solution.py:151
  175.3 4.6 %collective-permute-done.19 = bf16[2,2,512,256]{3,2,1,0:T(8,128)(2,1)} collective-permute-done((bf16[2,2,512,256]{3,2,1,0:T(8,128)(2,1)}, bf16[2,2,512,256]{3,2,1,0:T(8,128)(2,1)}, u32[]{:S(2)}, u32[]{:S(2)}) %collective-permute-start.19) | collective-permute-done | bytes 1048608 | tf_op jit(solution)/shard_map/ppermute | solution.py:30
  180.8 2.3 collective-permute-start.21
  183.8 1.1 slice.188
  184.8 1.4 pad_maximum_fusion.refs_2_
  186.3 1.8 fusion.11
  188.1 1.6 collective-permute-start.23
  189.7 1.5 collective-permute-start.24
  191.2 14.2 %collective-permute-done.21 = bf16[128,4096]{1,0:T(8,128)(2,1)S(1)} collective-permute-done((bf16[128,4096]{1,0:T(8,128)(2,1)S(1)}, bf16[128,4096]{1,0:T(8,128)(2,1)S(1)}, u32[]{:S(2)}, u32[]{:S(2)}) %collective-permute-start.21) | collective-permute-done | bytes 1048608 | tf_op jit(solution)/shard_map/ppermute | solution.py:59
  206.2 1.5 collective-permute-done.23.refs_3_
  207.7 1.3 collective-permute-done.24.refs_4_
  209.0 1.7 collective-permute-start.26
  210.7 0.9 collective-permute-start.27
  211.6 1.6 collective-permute-start.28
  213.2 1.5 collective-permute-start.29
  214.7 17.6 %collective-permute-done.26 = bf16[128,4096]{1,0:T(8,128)(2,1)S(1)} collective-permute-done((bf16[128,4096]{1,0:T(8,128)(2,1)S(1)}, bf16[128,4096]{1,0:T(8,128)(2,1)S(1)}, u32[]{:S(2)}, u32[]{:S(2)}) %collective-permute-start.26) | collective-permute-done | bytes 1048608 | tf_op jit(solution)/shard_map/ppermute | solution.py:59
  232.3 2.5 add_convert_fusion
  236.7 9.1 %collective-permute-start.32 = (bf16[128,4096]{1,0:T(8,128)(2,1)}, bf16[128,4096]{1,0:T(8,128)(2,1)}, u32[]{:S(2)}, u32[]{:S(2)}) collective-permute-start(bf16[128,4096]{1,0:T(8,128)(2,1)} %get-tuple-element.52), channel_id=1, source_target_pairs={{0,1},{1,2},{2,3},{4,5},{5,6},{6,7},{8,9},{9,10},{10,11},{12,13},{... | collective-permute-start | bytes 3145736 | tf_op jit(solution)/shard_map/ppermute | solution.py:59
  245.8 1.3 collective-permute-start.33
  247.0 1.5 collective-permute-start.34
  248.5 1.5 collective-permute-start.35
  250.0 1.6 shift_right_arithmetic.40
  251.7 3.1 copy.29
  255.0 10.6 %collective-permute-done.32 = bf16[128,4096]{1,0:T(8,128)(2,1)} collective-permute-done((bf16[128,4096]{1,0:T(8,128)(2,1)}, bf16[128,4096]{1,0:T(8,128)(2,1)}, u32[]{:S(2)}, u32[]{:S(2)}) %collective-permute-start.32) | collective-permute-done | bytes 1048608 | tf_op jit(solution)/shard_map/ppermute | solution.py:59
  265.6 5.1 %collective-permute-done.33 = bf16[128,4096]{1,0:T(8,128)(2,1)} collective-permute-done((bf16[128,4096]{1,0:T(8,128)(2,1)}, bf16[128,4096]{1,0:T(8,128)(2,1)}, u32[]{:S(2)}, u32[]{:S(2)}) %collective-permute-start.33) | collective-permute-done | bytes 1048608 | tf_op jit(solution)/shard_map/ppermute | solution.py:60
  270.7 4.2 %fusion = (f32[128]{0:T(128)S(1)}, bf16[128,4096]{1,0:T(8,128)(2,1)S(1)}) fusion(bf16[128,4096]{1,0:T(8,128)(2,1)} %collective-permute-done.33, bf16[128,4096]{1,0:T(8,128)(2,1)} %collective-permute-done.32, bf16[512,4096]{1,0:T(8,128)(2,1)} %copy-done.14, bf16[512,4096]{1,0:T(8,128)(2,1)} %copy-done.2, s32[128,4096]{1,0:T(8,128)} %bitcast.87, ...), kind=kLoop, calls=%fused_computation.10 | loop fusion | flops 9437056 | bytes 8405504 | tf_op jit(solution)/shard_map/reduce_sum | solution.py:18
  275.9 1.6 collective-permute-done.38.refs_14_
  277.5 1.1 collective-permute-done.39.refs_15_
  278.7 7.2 %attend_own_keys.1 = bf16[4,128,384]{2,1,0:T(8,128)(2,1)S(1)} custom-call(s32[16]{0:T(128)S(1)} %pad_add_fusion.3.table, bf16[128,4096]{1,0:T(8,128)(2,1)S(1)} %fusion.2.mem_ref, bf16[4,128,256]{2,1,0:T(8,128)(2,1)S(1)} %pad_maximum_fusion.4.cq_ref, bf16[2,2048,256]{2,1,0:T(8,128)(2,1)S(1)} %bitcast.83, ...), custom_call_target="tpu_custom_call" | custom-call | flops 1024 | bytes 1024 | tf_op jit(solution)/shard_map/attend_own_keys/pallas_call | solution.py:234
  286.2 4.3 %collective-permute-start.42 = (bf16[128,384]{1,0:T(8,128)(2,1)S(1)}, bf16[128,384]{1,0:T(8,128)(2,1)S(1)}, u32[]{:S(2)}, u32[]{:S(2)}) collective-permute-start(bf16[128,384]{1,0:T(8,128)(2,1)S(1)} %get-tuple-element.105), channel_id=1, source_target_pairs={{0,3},{1,2},{2,1},{3,0},{4,7},{5,6},{6,5},{7,4},{8,11},{9,10},{10,... | collective-permute-start | bytes 294920 | tf_op jit(solution)/shard_map/ppermute | solution.py:30
  290.4 3.7 %collective-permute-done.40 = bf16[128,384]{1,0:T(8,128)(2,1)S(1)} collective-permute-done((bf16[128,384]{1,0:T(8,128)(2,1)S(1)}, bf16[128,384]{1,0:T(8,128)(2,1)S(1)}, u32[]{:S(2)}, u32[]{:S(2)}) %collective-permute-start.40) | collective-permute-done | bytes 98336 | tf_op jit(solution)/shard_map/ppermute | solution.py:30
  294.2 1.3 collective-permute-done.42
  296.7 1.5 collective-permute-done.43
  298.9 1.9 collective-permute-start.46
  300.8 2.2 collective-permute-start.45
  303.0 2.3 collective-permute-done.46
  305.3 9.6 %collective-permute-done.45 = bf16[32,2048]{1,0:T(8,128)(2,1)S(1)} collective-permute-done((bf16[32,2048]{1,0:T(8,128)(2,1)S(1)}, bf16[32,2048]{1,0:T(8,128)(2,1)S(1)}, u32[]{:S(2)}, u32[]{:S(2)}) %collective-permute-start.45) | collective-permute-done | bytes 131104 | tf_op jit(solution)/shard_map/ppermute | solution.py:69
  315.4 1.1 collective-permute-done.47
  (163 shorter events, 15.9 us)
Async XLA Ops:
  7.2 28.5 %copy-start = (bf16[256,2048]{1,0:T(8,128)(2,1)S(1)}, bf16[256,2048]{1,0:T(8,128)(2,1)}, u32[]{:S(2)}) copy-start(bf16[256,2048]{1,0:T(8,128)(2,1)} %param.28) | copy-start | bytes 3145732
  7.2 120.7 %all-gather.3.cloned.1.call-start = ((), (), s32[]{:S(2)}) async-start(), calls=%async_computation | async-start | bytes 9437184 | tf_op jit(solution)/shard_map/all_gather | solution.py:292
  11.7 1.4 collective-permute-start
  13.2 9.4 %collective-permute-start.3 = (bf16[32,2048]{1,0:T(8,128)(2,1)S(1)}, bf16[32,2048]{1,0:T(8,128)(2,1)S(1)}, u32[]{:S(2)}, u32[]{:S(2)}) collective-permute-start(bf16[32,2048]{1,0:T(8,128)(2,1)S(1)} %maximum_select_fusion.2), channel_id=1, source_target_pairs={{0,1},{1,2},{2,3},{3,0},{4,5},{5,6},{6,7},{7,4},{8,9},{9,10},{10,1... | collective-permute-start | bytes 393224 | tf_op jit(solution)/shard_map/ppermute | solution.py:36
  16.1 15.2 %collective-permute-start.2 = (bf16[32,2048]{1,0:T(8,128)(2,1)S(1)}, bf16[32,2048]{1,0:T(8,128)(2,1)S(1)}, u32[]{:S(2)}, u32[]{:S(2)}) collective-permute-start(bf16[32,2048]{1,0:T(8,128)(2,1)S(1)} %maximum_select_fusion.2), channel_id=1, source_target_pairs={{0,2},{1,3},{2,0},{3,1},{4,6},{5,7},{6,4},{7,5},{8,10},{9,11},{10,... | collective-permute-start | bytes 393224 | tf_op jit(solution)/shard_map/ppermute | solution.py:36
  18.7 12.6 %collective-permute-start.1 = (bf16[32,2048]{1,0:T(8,128)(2,1)S(1)}, bf16[32,2048]{1,0:T(8,128)(2,1)S(1)}, u32[]{:S(2)}, u32[]{:S(2)}) collective-permute-start(bf16[32,2048]{1,0:T(8,128)(2,1)S(1)} %maximum_select_fusion.2), channel_id=1, source_target_pairs={{0,3},{1,0},{2,1},{3,2},{4,7},{5,4},{6,5},{7,6},{8,11},{9,8},{10,9... | collective-permute-start | bytes 393224 | tf_op jit(solution)/shard_map/ppermute | solution.py:36
  20.1 12.8 %copy-start.22 = (bf16[2048,3,256]{2,0,1:T(8,128)(2,1)S(1)}, bf16[2048,3,256]{2,0,1:T(8,128)(2,1)}, u32[]{:S(2)}) copy-start(bf16[2048,3,256]{2,0,1:T(8,128)(2,1)} %param.27) | copy-start | bytes 9437188
  33.6 1.8 collective-permute-start.4
  36.2 21.6 %collective-permute-start.7 = (bf16[32,2048]{1,0:T(8,128)(2,1)S(1)}, bf16[32,2048]{1,0:T(8,128)(2,1)S(1)}, u32[]{:S(2)}, u32[]{:S(2)}) collective-permute-start(bf16[32,2048]{1,0:T(8,128)(2,1)S(1)} %get-tuple-element.102), channel_id=1, source_target_pairs={{0,3},{1,0},{2,1},{3,2},{4,7},{5,4},{6,5},{7,6},{8,11},{9,8},{10,9... | collective-permute-start | bytes 393224 | tf_op jit(solution)/shard_map/ppermute | solution.py:69
  49.1 29.5 %collective-permute-start.6 = (bf16[32,2048]{1,0:T(8,128)(2,1)S(1)}, bf16[32,2048]{1,0:T(8,128)(2,1)S(1)}, u32[]{:S(2)}, u32[]{:S(2)}) collective-permute-start(bf16[32,2048]{1,0:T(8,128)(2,1)S(1)} %get-tuple-element.103), channel_id=1, source_target_pairs={{0,2},{1,3},{2,0},{3,1},{4,6},{5,7},{6,4},{7,5},{8,10},{9,11},{10,... | collective-permute-start | bytes 393224 | tf_op jit(solution)/shard_map/ppermute | solution.py:69
  49.4 29.2 %collective-permute-start.5 = (bf16[32,2048]{1,0:T(8,128)(2,1)S(1)}, bf16[32,2048]{1,0:T(8,128)(2,1)S(1)}, u32[]{:S(2)}, u32[]{:S(2)}) collective-permute-start(bf16[32,2048]{1,0:T(8,128)(2,1)S(1)} %get-tuple-element.101), channel_id=1, source_target_pairs={{0,1},{1,2},{2,3},{3,0},{4,5},{5,6},{6,7},{7,4},{8,9},{9,10},{10,1... | collective-permute-start | bytes 393224 | tf_op jit(solution)/shard_map/ppermute | solution.py:69
  78.7 25.2 %copy-start.23 = (bf16[2048,256]{1,0:T(8,128)(2,1)S(1)}, bf16[2048,256]{1,0:T(8,128)(2,1)}, u32[]{:S(2)}) copy-start(bf16[2048,256]{1,0:T(8,128)(2,1)} %param.30) | copy-start | bytes 3145732
  78.7 2.5 collective-permute-start.8
  80.8 43.8 %collective-permute-start.17 = (bf16[2,2048,256]{2,1,0:T(8,128)(2,1)S(1)}, bf16[2,2048,256]{2,1,0:T(8,128)(2,1)}, u32[]{:S(2)}, u32[]{:S(2)}) collective-permute-start(bf16[2,2048,256]{2,1,0:T(8,128)(2,1)S(1)} %bitcast.82), channel_id=1, source_target_pairs={{0,4},{4,0},{1,5},{5,1},{2,6},{6,2},{3,7},{7,3},{8,12},{12,8},{9,1... | collective-permute-start | bytes 6291464 | tf_op jit(solution)/shard_map/ppermute | solution.py:30
  81.6 3.7 %collective-permute-start.9 = (bf16[16,2048]{1,0:T(8,128)(2,1)S(1)}, bf16[16,2048]{1,0:T(8,128)(2,1)S(1)}, u32[]{:S(2)}, u32[]{:S(2)}) collective-permute-start(bf16[16,2048]{1,0:T(8,128)(2,1)S(1)} %get-tuple-element.113), channel_id=1, source_target_pairs={{0,4},{4,0},{1,5},{5,1},{2,6},{6,2},{3,7},{7,3},{8,12},{12,8},{9,1... | collective-permute-start | bytes 196616 | tf_op jit(solution)/shard_map/ppermute | solution.py:30
  85.2 11.0 %collective-permute-start.12 = (bf16[32,2048]{1,0:T(8,128)(2,1)S(1)}, bf16[32,2048]{1,0:T(8,128)(2,1)S(1)}, u32[]{:S(2)}, u32[]{:S(2)}) collective-permute-start(bf16[32,2048]{1,0:T(8,128)(2,1)S(1)} %maximum_select_fusion.3), channel_id=1, source_target_pairs={{0,1},{1,2},{2,3},{3,0},{4,5},{5,6},{6,7},{7,4},{8,9},{9,10},{10,1... | collective-permute-start | bytes 393224 | tf_op jit(solution)/shard_map/ppermute | solution.py:36
  85.3 18.6 %collective-permute-start.11 = (bf16[32,2048]{1,0:T(8,128)(2,1)S(1)}, bf16[32,2048]{1,0:T(8,128)(2,1)S(1)}, u32[]{:S(2)}, u32[]{:S(2)}) collective-permute-start(bf16[32,2048]{1,0:T(8,128)(2,1)S(1)} %maximum_select_fusion.3), channel_id=1, source_target_pairs={{0,2},{1,3},{2,0},{3,1},{4,6},{5,7},{6,4},{7,5},{8,10},{9,11},{10,... | collective-permute-start | bytes 393224 | tf_op jit(solution)/shard_map/ppermute | solution.py:36
  85.4 18.5 %collective-permute-start.10 = (bf16[32,2048]{1,0:T(8,128)(2,1)S(1)}, bf16[32,2048]{1,0:T(8,128)(2,1)S(1)}, u32[]{:S(2)}, u32[]{:S(2)}) collective-permute-start(bf16[32,2048]{1,0:T(8,128)(2,1)S(1)} %maximum_select_fusion.3), channel_id=1, source_target_pairs={{0,3},{1,0},{2,1},{3,2},{4,7},{5,4},{6,5},{7,6},{8,11},{9,8},{10,9... | collective-permute-start | bytes 393224 | tf_op jit(solution)/shard_map/ppermute | solution.py:36
  104.2 1.4 collective-permute-start.13
  105.7 11.2 %collective-permute-start.16 = (bf16[128,256]{1,0:T(8,128)(2,1)S(1)}, bf16[128,256]{1,0:T(8,128)(2,1)S(1)}, u32[]{:S(2)}, u32[]{:S(2)}) collective-permute-start(bf16[128,256]{1,0:T(8,128)(2,1)S(1)} %bitcast.94), channel_id=1, source_target_pairs={{0,3},{1,2},{2,1},{3,0},{4,7},{5,6},{6,5},{7,4},{8,11},{9,10},{10,... | collective-permute-start | bytes 196616 | tf_op jit(solution)/shard_map/ppermute | solution.py:30
  114.4 5.1 %collective-permute-start.15 = (bf16[128,256]{1,0:T(8,128)(2,1)S(1)}, bf16[128,256]{1,0:T(8,128)(2,1)S(1)}, u32[]{:S(2)}, u32[]{:S(2)}) collective-permute-start(bf16[128,256]{1,0:T(8,128)(2,1)S(1)} %bitcast.95), channel_id=1, source_target_pairs={{0,1},{1,0},{2,3},{3,2},{4,5},{5,4},{6,7},{7,6},{8,9},{9,8},{10,11... | collective-permute-start | bytes 196616 | tf_op jit(solution)/shard_map/ppermute | solution.py:30
  114.9 9.6 %collective-permute-start.14 = (bf16[128,256]{1,0:T(8,128)(2,1)S(1)}, bf16[128,256]{1,0:T(8,128)(2,1)S(1)}, u32[]{:S(2)}, u32[]{:S(2)}) collective-permute-start(bf16[128,256]{1,0:T(8,128)(2,1)S(1)} %bitcast.96), channel_id=1, source_target_pairs={{0,2},{1,3},{2,0},{3,1},{4,6},{5,7},{6,4},{7,5},{8,10},{9,11},{10,... | collective-permute-start | bytes 196616 | tf_op jit(solution)/shard_map/ppermute | solution.py:30
  127.9 25.1 %collective-permute-start.18 = (bf16[1,2,512,256]{3,2,1,0:T(8,128)(2,1)S(1)}, bf16[1,2,512,256]{3,2,1,0:T(8,128)(2,1)S(1)}, u32[]{:S(2)}, u32[]{:S(2)}) collective-permute-start(bf16[1,2,512,256]{3,2,1,0:T(8,128)(2,1)S(1)} %dynamic-slice_bitcast_fusion), channel_id=1, source_target_pairs={{0,2},{1,3},{2,0},{3,1},{4,6},{5,7},{6,4},{7,5},{8,10},{9,11},{10,... | collective-permute-start | bytes 1572872 | tf_op jit(solution)/shard_map/ppermute | solution.py:30
  154.1 25.9 %collective-permute-start.20 = (bf16[512,4096]{1,0:T(8,128)(2,1)S(1)}, bf16[512,4096]{1,0:T(8,128)(2,1)S(1)}, u32[]{:S(2)}, u32[]{:S(2)}) collective-permute-start(bf16[512,4096]{1,0:T(8,128)(2,1)S(1)} %ffn.2), channel_id=1, source_target_pairs={{0,4},{4,0},{1,5},{5,1},{2,6},{6,2},{3,7},{7,3},{8,12},{12,8},{9,1... | collective-permute-start | bytes 12582920 | tf_op jit(solution)/shard_map/ppermute | solution.py:30
  154.1 25.8 %collective-permute-start.19 = (bf16[2,2,512,256]{3,2,1,0:T(8,128)(2,1)}, bf16[2,2,512,256]{3,2,1,0:T(8,128)(2,1)}, u32[]{:S(2)}, u32[]{:S(2)}) collective-permute-start(bf16[2,2,512,256]{3,2,1,0:T(8,128)(2,1)} %pad_maximum_fusion.1), channel_id=1, source_target_pairs={{0,1},{1,0},{2,3},{3,2},{4,5},{5,4},{6,7},{7,6},{8,9},{9,8},{10,11... | collective-permute-start | bytes 3145736 | tf_op jit(solution)/shard_map/ppermute | solution.py:30
  175.3 57.0 %copy-start.2 = (bf16[512,4096]{1,0:T(8,128)(2,1)}, bf16[512,4096]{1,0:T(8,128)(2,1)S(1)}, u32[]{:S(2)}) copy-start(bf16[512,4096]{1,0:T(8,128)(2,1)S(1)} %ffn.3) | copy-start | bytes 12582916
  180.0 52.3 %copy-start.14 = (bf16[512,4096]{1,0:T(8,128)(2,1)}, bf16[512,4096]{1,0:T(8,128)(2,1)S(1)}, u32[]{:S(2)}) copy-start(bf16[512,4096]{1,0:T(8,128)(2,1)S(1)} %collective-permute-done.20) | copy-start | bytes 12582916
  180.8 24.6 %collective-permute-start.21 = (bf16[128,4096]{1,0:T(8,128)(2,1)S(1)}, bf16[128,4096]{1,0:T(8,128)(2,1)S(1)}, u32[]{:S(2)}, u32[]{:S(2)}) collective-permute-start(bf16[128,4096]{1,0:T(8,128)(2,1)S(1)} %get-tuple-element.93), channel_id=1, source_target_pairs={{0,1},{4,5},{8,9},{12,13},{16,17},{20,21},{24,25},{28,29}} | collective-permute-start | bytes 3145736 | tf_op jit(solution)/shard_map/ppermute | solution.py:59
  183.0 22.4 %collective-permute-start.22 = (bf16[128,4096]{1,0:T(8,128)(2,1)S(1)}, bf16[128,4096]{1,0:T(8,128)(2,1)S(1)}, u32[]{:S(2)}, u32[]{:S(2)}) collective-permute-start(bf16[128,4096]{1,0:T(8,128)(2,1)S(1)} %get-tuple-element.92), channel_id=1, source_target_pairs={{3,2},{7,6},{11,10},{15,14},{19,18},{23,22},{27,26},{31,30}} | collective-permute-start | bytes 3145736 | tf_op jit(solution)/shard_map/ppermute | solution.py:60
  186.2 19.9 %copy-start.3 = (bf16[3,2,512,256]{3,2,1,0:T(8,128)(2,1)}, bf16[3,2,512,256]{3,2,1,0:T(8,128)(2,1)S(1)}, u32[]{:S(2)}) copy-start(bf16[3,2,512,256]{3,2,1,0:T(8,128)(2,1)S(1)} %pad_maximum_fusion.refs_2_) | copy-start | bytes 4718596
  186.2 22.7 %collective-permute-start.25 = (bf16[3,2,512,256]{3,2,1,0:T(8,128)(2,1)S(1)}, bf16[3,2,512,256]{3,2,1,0:T(8,128)(2,1)S(1)}, u32[]{:S(2)}, u32[]{:S(2)}) collective-permute-start(bf16[3,2,512,256]{3,2,1,0:T(8,128)(2,1)S(1)} %pad_maximum_fusion.refs_2_), channel_id=1, source_target_pairs={{0,4},{4,0},{1,5},{5,1},{2,6},{6,2},{3,7},{7,3},{8,12},{12,8},{9,1... | collective-permute-start | bytes 4718600 | tf_op jit(solution)/shard_map/ppermute | solution.py:30
  188.1 19.5 %collective-permute-start.23 = (bf16[3,1,512,256]{3,2,1,0:T(8,128)(2,1)S(1)}, bf16[3,1,512,256]{3,2,1,0:T(8,128)(2,1)S(1)}, u32[]{:S(2)}, u32[]{:S(2)}) collective-permute-start(bf16[3,1,512,256]{3,2,1,0:T(8,128)(2,1)S(1)} %get-tuple-element.97), channel_id=1, source_target_pairs={{0,8},{8,0},{16,24},{24,16},{1,9},{9,1},{17,25},{25,17},{2,10},{10... | collective-permute-start | bytes 2359304 | tf_op jit(solution)/shard_map/ppermute | solution.py:30
  189.7 19.3 %collective-permute-start.24 = (bf16[3,1,512,256]{3,2,1,0:T(8,128)(2,1)S(1)}, bf16[3,1,512,256]{3,2,1,0:T(8,128)(2,1)}, u32[]{:S(2)}, u32[]{:S(2)}) collective-permute-start(bf16[3,1,512,256]{3,2,1,0:T(8,128)(2,1)S(1)} %get-tuple-element.97), channel_id=1, source_target_pairs={{0,16},{8,24},{16,0},{24,8},{1,17},{9,25},{17,1},{25,9},{2,18},{10... | collective-permute-start | bytes 2359304 | tf_op jit(solution)/shard_map/ppermute | solution.py:30
  207.7 27.2 %copy-start.7 = (bf16[3,1,512,256]{3,2,1,0:T(8,128)(2,1)}, bf16[3,1,512,256]{3,2,1,0:T(8,128)(2,1)S(1)}, u32[]{:S(2)}) copy-start(bf16[3,1,512,256]{3,2,1,0:T(8,128)(2,1)S(1)} %collective-permute-done.23.refs_3_) | copy-start | bytes 2359300
  209.0 25.8 %copy-start.5 = (bf16[3,2,512,256]{3,2,1,0:T(8,128)(2,1)}, bf16[3,2,512,256]{3,2,1,0:T(8,128)(2,1)S(1)}, u32[]{:S(2)}) copy-start(bf16[3,2,512,256]{3,2,1,0:T(8,128)(2,1)S(1)} %collective-permute-done.25.refs_9_) | copy-start | bytes 4718596
  209.0 23.3 %collective-permute-start.26 = (bf16[128,4096]{1,0:T(8,128)(2,1)S(1)}, bf16[128,4096]{1,0:T(8,128)(2,1)S(1)}, u32[]{:S(2)}, u32[]{:S(2)}) collective-permute-start(bf16[128,4096]{1,0:T(8,128)(2,1)S(1)} %get-tuple-element.45), channel_id=1, source_target_pairs={{0,1},{1,2},{4,5},{5,6},{8,9},{9,10},{12,13},{13,14},{16,17},{17,1... | collective-permute-start | bytes 3145736 | tf_op jit(solution)/shard_map/ppermute | solution.py:59
  210.7 21.6 %collective-permute-start.27 = (bf16[128,4096]{1,0:T(8,128)(2,1)S(1)}, bf16[128,4096]{1,0:T(8,128)(2,1)S(1)}, u32[]{:S(2)}, u32[]{:S(2)}) collective-permute-start(bf16[128,4096]{1,0:T(8,128)(2,1)S(1)} %get-tuple-element.46), channel_id=1, source_target_pairs={{2,1},{3,2},{6,5},{7,6},{10,9},{11,10},{14,13},{15,14},{18,17},{19... | collective-permute-start | bytes 3145736 | tf_op jit(solution)/shard_map/ppermute | solution.py:60
  211.6 23.2 %collective-permute-start.28 = (bf16[3,1,512,256]{3,2,1,0:T(8,128)(2,1)S(1)}, bf16[3,1,512,256]{3,2,1,0:T(8,128)(2,1)}, u32[]{:S(2)}, u32[]{:S(2)}) collective-permute-start(bf16[3,1,512,256]{3,2,1,0:T(8,128)(2,1)S(1)} %get-tuple-element.96), channel_id=1, source_target_pairs={{0,8},{8,0},{16,24},{24,16},{1,9},{9,1},{17,25},{25,17},{2,10},{10... | collective-permute-start | bytes 2359304 | tf_op jit(solution)/shard_map/ppermute | solution.py:30
  213.2 21.6 %collective-permute-start.29 = (bf16[3,1,512,256]{3,2,1,0:T(8,128)(2,1)S(1)}, bf16[3,1,512,256]{3,2,1,0:T(8,128)(2,1)}, u32[]{:S(2)}, u32[]{:S(2)}) collective-permute-start(bf16[3,1,512,256]{3,2,1,0:T(8,128)(2,1)S(1)} %get-tuple-element.96), channel_id=1, source_target_pairs={{0,16},{8,24},{16,0},{24,8},{1,17},{9,25},{17,1},{25,9},{2,18},{10... | collective-permute-start | bytes 2359304 | tf_op jit(solution)/shard_map/ppermute | solution.py:30
  214.7 20.1 %collective-permute-start.30 = (bf16[3,1,512,256]{3,2,1,0:T(8,128)(2,1)S(1)}, bf16[3,1,512,256]{3,2,1,0:T(8,128)(2,1)S(1)}, u32[]{:S(2)}, u32[]{:S(2)}) collective-permute-start(bf16[3,1,512,256]{3,2,1,0:T(8,128)(2,1)S(1)} %collective-permute-done.23.refs_3_), channel_id=1, source_target_pairs={{0,4},{4,0},{1,5},{5,1},{2,6},{6,2},{3,7},{7,3},{8,12},{12,8},{9,1... | collective-permute-start | bytes 2359304 | tf_op jit(solution)/shard_map/ppermute | solution.py:30
  232.3 3.5 %collective-permute-start.31 = (bf16[3,1,512,256]{3,2,1,0:T(8,128)(2,1)}, bf16[3,1,512,256]{3,2,1,0:T(8,128)(2,1)S(1)}, u32[]{:S(2)}, u32[]{:S(2)}) collective-permute-start(bf16[3,1,512,256]{3,2,1,0:T(8,128)(2,1)} %collective-permute-done.24.refs_4_), channel_id=1, source_target_pairs={{0,4},{4,0},{1,5},{5,1},{2,6},{6,2},{3,7},{7,3},{8,12},{12,8},{9,1... | collective-permute-start | bytes 2359304 | tf_op jit(solution)/shard_map/ppermute | solution.py:30
  236.7 28.9 %collective-permute-start.32 = (bf16[128,4096]{1,0:T(8,128)(2,1)}, bf16[128,4096]{1,0:T(8,128)(2,1)}, u32[]{:S(2)}, u32[]{:S(2)}) collective-permute-start(bf16[128,4096]{1,0:T(8,128)(2,1)} %get-tuple-element.52), channel_id=1, source_target_pairs={{0,1},{1,2},{2,3},{4,5},{5,6},{6,7},{8,9},{9,10},{10,11},{12,13},{... | collective-permute-start | bytes 3145736 | tf_op jit(solution)/shard_map/ppermute | solution.py:59
  245.8 24.9 %collective-permute-start.33 = (bf16[128,4096]{1,0:T(8,128)(2,1)}, bf16[128,4096]{1,0:T(8,128)(2,1)}, u32[]{:S(2)}, u32[]{:S(2)}) collective-permute-start(bf16[128,4096]{1,0:T(8,128)(2,1)} %get-tuple-element.53), channel_id=1, source_target_pairs={{1,0},{2,1},{3,2},{5,4},{6,5},{7,6},{9,8},{10,9},{11,10},{13,12},{... | collective-permute-start | bytes 3145736 | tf_op jit(solution)/shard_map/ppermute | solution.py:60
  247.0 23.6 %collective-permute-start.34 = (bf16[3,1,512,256]{3,2,1,0:T(8,128)(2,1)}, bf16[3,1,512,256]{3,2,1,0:T(8,128)(2,1)}, u32[]{:S(2)}, u32[]{:S(2)}) collective-permute-start(bf16[3,1,512,256]{3,2,1,0:T(8,128)(2,1)} %collective-permute-done.24.refs_4_), channel_id=1, source_target_pairs={{0,8},{8,0},{16,24},{24,16},{1,9},{9,1},{17,25},{25,17},{2,10},{10... | collective-permute-start | bytes 2359304 | tf_op jit(solution)/shard_map/ppermute | solution.py:30
  248.5 22.2 %collective-permute-start.35 = (bf16[3,1,512,256]{3,2,1,0:T(8,128)(2,1)}, bf16[3,1,512,256]{3,2,1,0:T(8,128)(2,1)}, u32[]{:S(2)}, u32[]{:S(2)}) collective-permute-start(bf16[3,1,512,256]{3,2,1,0:T(8,128)(2,1)} %collective-permute-done.28.refs_5_), channel_id=1, source_target_pairs={{0,16},{8,24},{16,0},{24,8},{1,17},{9,25},{17,1},{25,9},{2,18},{10... | collective-permute-start | bytes 2359304 | tf_op jit(solution)/shard_map/ppermute | solution.py:30
  251.7 19.0 %copy-start.13 = (bf16[128,4096]{1,0:T(8,128)(2,1)S(1)}, bf16[128,4096]{1,0:T(8,128)(2,1)}, u32[]{:S(2)}) copy-start(bf16[128,4096]{1,0:T(8,128)(2,1)} %param.18) | copy-start | bytes 3145732
  255.0 20.9 %collective-permute-start.36 = (bf16[3,1,512,256]{3,2,1,0:T(8,128)(2,1)}, bf16[3,1,512,256]{3,2,1,0:T(8,128)(2,1)S(1)}, u32[]{:S(2)}, u32[]{:S(2)}) collective-permute-start(bf16[3,1,512,256]{3,2,1,0:T(8,128)(2,1)} %collective-permute-done.28.refs_5_), channel_id=1, source_target_pairs={{0,4},{4,0},{1,5},{5,1},{2,6},{6,2},{3,7},{7,3},{8,12},{12,8},{9,1... | collective-permute-start | bytes 2359304 | tf_op jit(solution)/shard_map/ppermute | solution.py:30
  265.6 10.3 %collective-permute-start.37 = (bf16[3,1,512,256]{3,2,1,0:T(8,128)(2,1)}, bf16[3,1,512,256]{3,2,1,0:T(8,128)(2,1)S(1)}, u32[]{:S(2)}, u32[]{:S(2)}) collective-permute-start(bf16[3,1,512,256]{3,2,1,0:T(8,128)(2,1)} %collective-permute-done.29.refs_6_), channel_id=1, source_target_pairs={{0,4},{4,0},{1,5},{5,1},{2,6},{6,2},{3,7},{7,3},{8,12},{12,8},{9,1... | collective-permute-start | bytes 2359304 | tf_op jit(solution)/shard_map/ppermute | solution.py:30
  270.7 8.0 %copy-start.6 = (bf16[3,2,512,256]{3,2,1,0:T(8,128)(2,1)S(1)}, bf16[3,2,512,256]{3,2,1,0:T(8,128)(2,1)}, u32[]{:S(2)}) copy-start(bf16[3,2,512,256]{3,2,1,0:T(8,128)(2,1)} %copy-done.5) | copy-start | bytes 4718596
  270.7 8.0 %copy-start.8 = (bf16[3,1,512,256]{3,2,1,0:T(8,128)(2,1)S(1)}, bf16[3,1,512,256]{3,2,1,0:T(8,128)(2,1)}, u32[]{:S(2)}) copy-start(bf16[3,1,512,256]{3,2,1,0:T(8,128)(2,1)} %copy-done.7) | copy-start | bytes 2359300
  270.7 8.0 %copy-start.10 = (bf16[3,1,512,256]{3,2,1,0:T(8,128)(2,1)S(1)}, bf16[3,1,512,256]{3,2,1,0:T(8,128)(2,1)}, u32[]{:S(2)}) copy-start(bf16[3,1,512,256]{3,2,1,0:T(8,128)(2,1)} %copy-done.9) | copy-start | bytes 2359300
  270.7 8.0 %copy-start.12 = (bf16[3,1,512,256]{3,2,1,0:T(8,128)(2,1)S(1)}, bf16[3,1,512,256]{3,2,1,0:T(8,128)(2,1)}, u32[]{:S(2)}) copy-start(bf16[3,1,512,256]{3,2,1,0:T(8,128)(2,1)} %copy-done.11) | copy-start | bytes 2359300
  275.0 2.6 collective-permute-start.38
  275.1 3.6 %collective-permute-start.39 = (bf16[3,1,512,256]{3,2,1,0:T(8,128)(2,1)}, bf16[3,1,512,256]{3,2,1,0:T(8,128)(2,1)S(1)}, u32[]{:S(2)}, u32[]{:S(2)}) collective-permute-start(bf16[3,1,512,256]{3,2,1,0:T(8,128)(2,1)} %collective-permute-done.35.refs_8_), channel_id=1, source_target_pairs={{0,4},{4,0},{1,5},{5,1},{2,6},{6,2},{3,7},{7,3},{8,12},{12,8},{9,1... | collective-permute-start | bytes 2359304 | tf_op jit(solution)/shard_map/ppermute | solution.py:30
  286.0 8.2 %collective-permute-start.40 = (bf16[128,384]{1,0:T(8,128)(2,1)S(1)}, bf16[128,384]{1,0:T(8,128)(2,1)S(1)}, u32[]{:S(2)}, u32[]{:S(2)}) collective-permute-start(bf16[128,384]{1,0:T(8,128)(2,1)S(1)} %get-tuple-element.107), channel_id=1, source_target_pairs={{0,2},{1,3},{2,0},{3,1},{4,6},{5,7},{6,4},{7,5},{8,10},{9,11},{10,... | collective-permute-start | bytes 294920 | tf_op jit(solution)/shard_map/ppermute | solution.py:30
  286.1 8.1 %collective-permute-start.41 = (bf16[128,384]{1,0:T(8,128)(2,1)S(1)}, bf16[128,384]{1,0:T(8,128)(2,1)S(1)}, u32[]{:S(2)}, u32[]{:S(2)}) collective-permute-start(bf16[128,384]{1,0:T(8,128)(2,1)S(1)} %get-tuple-element.106), channel_id=1, source_target_pairs={{0,1},{1,0},{2,3},{3,2},{4,5},{5,4},{6,7},{7,6},{8,9},{9,8},{10,11... | collective-permute-start | bytes 294920 | tf_op jit(solution)/shard_map/ppermute | solution.py:30
  286.2 9.4 %collective-permute-start.42 = (bf16[128,384]{1,0:T(8,128)(2,1)S(1)}, bf16[128,384]{1,0:T(8,128)(2,1)S(1)}, u32[]{:S(2)}, u32[]{:S(2)}) collective-permute-start(bf16[128,384]{1,0:T(8,128)(2,1)S(1)} %get-tuple-element.105), channel_id=1, source_target_pairs={{0,3},{1,2},{2,1},{3,0},{4,7},{5,6},{6,5},{7,4},{8,11},{9,10},{10,... | collective-permute-start | bytes 294920 | tf_op jit(solution)/shard_map/ppermute | solution.py:30
  296.6 1.6 collective-permute-start.43
  298.3 16.8 %copy-start.18 = (s32[16,1024]{1,0:T(8,128)S(1)}, s32[16,1024]{1,0:T(8,128)}, u32[]{:S(2)}) copy-start(s32[16,1024]{1,0:T(8,128)} %param.33) | copy-start | bytes 196612
  298.5 18.7 %copy-start.1 = (bf16[256,2048]{1,0:T(8,128)(2,1)S(1)}, bf16[256,2048]{1,0:T(8,128)(2,1)}, u32[]{:S(2)}) copy-start(bf16[256,2048]{1,0:T(8,128)(2,1)} %param.28) | copy-start | bytes 3145732
  298.9 6.4 %collective-permute-start.46 = (bf16[32,2048]{1,0:T(8,128)(2,1)S(1)}, bf16[32,2048]{1,0:T(8,128)(2,1)S(1)}, u32[]{:S(2)}, u32[]{:S(2)}) collective-permute-start(bf16[32,2048]{1,0:T(8,128)(2,1)S(1)} %get-tuple-element.99), channel_id=1, source_target_pairs={{0,3},{1,0},{2,1},{3,2},{4,7},{5,4},{6,5},{7,6},{8,11},{9,8},{10,9... | collective-permute-start | bytes 393224 | tf_op jit(solution)/shard_map/ppermute | solution.py:69
  300.8 14.2 %collective-permute-start.45 = (bf16[32,2048]{1,0:T(8,128)(2,1)S(1)}, bf16[32,2048]{1,0:T(8,128)(2,1)S(1)}, u32[]{:S(2)}, u32[]{:S(2)}) collective-permute-start(bf16[32,2048]{1,0:T(8,128)(2,1)S(1)} %get-tuple-element.100), channel_id=1, source_target_pairs={{0,2},{1,3},{2,0},{3,1},{4,6},{5,7},{6,4},{7,5},{8,10},{9,11},{10,... | collective-permute-start | bytes 393224 | tf_op jit(solution)/shard_map/ppermute | solution.py:69
  303.0 11.9 %collective-permute-start.44 = (bf16[32,2048]{1,0:T(8,128)(2,1)S(1)}, bf16[32,2048]{1,0:T(8,128)(2,1)S(1)}, u32[]{:S(2)}, u32[]{:S(2)}) collective-permute-start(bf16[32,2048]{1,0:T(8,128)(2,1)S(1)} %get-tuple-element.98), channel_id=1, source_target_pairs={{0,1},{1,2},{2,3},{3,0},{4,5},{5,6},{6,7},{7,4},{8,9},{9,10},{10,1... | collective-permute-start | bytes 393224 | tf_op jit(solution)/shard_map/ppermute | solution.py:69
  315.0 1.4 collective-permute-start.47
  (9 other events, 27.4 us)
Sparse Core Ops, SparseCore 0:
  11.5 116.2 all-gather.2

commit v15 on v14

--- a/solution.py
+++ b/solution.py
@@ -249,7 +249,7 @@
             out_specs=pl.BlockSpec((1, count, width + 128), lambda h, t: (h, 0, 0)),
         ),
         out_shape=jax.ShapeDtypeStruct((heads, count, width + 128), BF16),
-        compiler_params=pltpu.CompilerParams(vmem_limit_bytes=30 * 2**20),
+        compiler_params=pltpu.CompilerParams(vmem_limit_bytes=56 * 2**20),
         cost_estimate=pl.CostEstimate(flops=1024, bytes_accessed=1024, transcendentals=0),
         name="attend_own_keys",
     )(table, memory, queries, *own_head, *shares)

time: 325 us -> 329 us (1.012)
  Pallas kernels: 49.6 us -> 53.4 us
    ppermute x3, waiting for transfers between devices: 42.4 us -> 46.8 us  [sum_step(): above = lax.ppermute(sends[0], 'tensor', [(i, i + 1) for i in range(step)])]
    ppermute x30, waiting for transfers between devices: 37 us -> 32.6 us  [swap(): lax.ppermute(value, axis, [(i, i ^ distance) for i in range(lax.axis_size...]
    pallas_call x1, Pallas kernels: 7.25 us -> 11 us  [attend_own_keys(): pl.pallas_call(functools.partial(attend_kernel, plan, depth), grid_spec=p...]
    unnamed x54 -> x56, local copies, waits for them, and re-layouts: 7.18 us -> 8.21 us
  transfers between devices with their start and end apart: 49 -> 49, of which waited for: 30 -> 28; matrix products, arithmetic and copies ran while one was open for 7% -> 6% of each run, Pallas kernels for 13% -> 13%
where the time goes in v15:
time: 329 us
  waiting for transfers between devices  154 us (47%)
  starting transfers between devices  73.8 us (22%)
  Pallas kernels  53.4 us (16%)
  other arithmetic  18.8 us (6%)
  between operations  14.8 us (4%)
  local copies, waits for them, and re-layouts  10.4 us (3%)
  matrix products  3.45 us (1%)
    ppermute x3, waiting for transfers between devices, sum_step(): above = lax.ppermute(sends[0], 'tensor', [(i, i + 1) for i in range(step)])  46.8 us
    pallas_call x2, Pallas kernels, ffn(): pl.pallas_call(functools.partial(ffn_kernel, ins), grid_spec=pltpu.Prefet...  42.4 us
    ppermute x6, waiting for transfers between devices, slots_sum(): lax.ppermute(product[o], 'tensor', [(i, (i + o) % count) for i in range(c...  40.8 us
    ppermute x30, waiting for transfers between devices, swap(): lax.ppermute(value, axis, [(i, i ^ distance) for i in range(lax.axis_size...  32.6 us
    ppermute x30, starting transfers between devices, swap(): lax.ppermute(value, axis, [(i, i ^ distance) for i in range(lax.axis_size...  26.6 us
    ppermute x6, waiting for transfers between devices, from_slots(): lax.ppermute(value, 'tensor', [(i, (i - o) % count) for i in range(count)])  26 us
    ppermute x6, starting transfers between devices, slots_sum(): lax.ppermute(product[o], 'tensor', [(i, (i + o) % count) for i in range(c...  17.7 us
    ppermute x3, starting transfers between devices, sum_step(): above = lax.ppermute(sends[0], 'tensor', [(i, i + 1) for i in range(step)])  15.7 us
  transfers between devices with their start and end apart: 49, of which 28 were waited for; matrix products, arithmetic and copies ran while one was open for 6% of the time, Pallas kernels for 13%

profile of v15, /device:TPU:0, one launch (start us, length us, event | category | flops | bytes accessed | tf_op | source)
XLA Modules:
  0.0 328.7 jit_solution(16701867011998016020)
XLA Ops:
  7.2 1.6 fusion.3
  8.9 2.5 fusion.5
  12.2 0.9 collective-permute-done
  13.2 3.0 collective-permute-start.3
  16.1 2.6 collective-permute-start.2
  18.7 1.3 collective-permute-start.1
  20.1 2.5 collective-permute-done.3
  22.6 8.8 %collective-permute-done.2 = bf16[32,2048]{1,0:T(8,128)(2,1)S(1)} collective-permute-done((bf16[32,2048]{1,0:T(8,128)(2,1)S(1)}, bf16[32,2048]{1,0:T(8,128)(2,1)S(1)}, u32[]{:S(2)}, u32[]{:S(2)}) %collective-permute-start.2) | collective-permute-done | bytes 131104 | tf_op jit(solution)/shard_map/ppermute | solution.py:36
  31.4 1.5 convolution_bitcast_fusion
  33.9 1.5 collective-permute-done.4
  36.2 12.9 %collective-permute-start.7 = (bf16[32,2048]{1,0:T(8,128)(2,1)S(1)}, bf16[32,2048]{1,0:T(8,128)(2,1)S(1)}, u32[]{:S(2)}, u32[]{:S(2)}) collective-permute-start(bf16[32,2048]{1,0:T(8,128)(2,1)S(1)} %get-tuple-element.102), channel_id=1, source_target_pairs={{0,3},{1,0},{2,1},{3,2},{4,7},{5,4},{6,5},{7,6},{8,11},{9,8},{10,9... | collective-permute-start | bytes 393224 | tf_op jit(solution)/shard_map/ppermute | solution.py:69
  49.8 8.0 %collective-permute-done.7 = bf16[32,2048]{1,0:T(8,128)(2,1)S(1)} collective-permute-done((bf16[32,2048]{1,0:T(8,128)(2,1)S(1)}, bf16[32,2048]{1,0:T(8,128)(2,1)S(1)}, u32[]{:S(2)}, u32[]{:S(2)}) %collective-permute-start.7) | collective-permute-done | bytes 131104 | tf_op jit(solution)/shard_map/ppermute | solution.py:69
  57.8 20.9 %collective-permute-done.6 = bf16[32,2048]{1,0:T(8,128)(2,1)S(1)} collective-permute-done((bf16[32,2048]{1,0:T(8,128)(2,1)S(1)}, bf16[32,2048]{1,0:T(8,128)(2,1)S(1)}, u32[]{:S(2)}, u32[]{:S(2)}) %collective-permute-start.6) | collective-permute-done | bytes 131104 | tf_op jit(solution)/shard_map/ppermute | solution.py:69
  78.8 1.9 copy.38
  81.7 3.5 %collective-permute-done.9 = bf16[16,2048]{1,0:T(8,128)(2,1)S(1)} collective-permute-done((bf16[16,2048]{1,0:T(8,128)(2,1)S(1)}, bf16[16,2048]{1,0:T(8,128)(2,1)S(1)}, u32[]{:S(2)}, u32[]{:S(2)}) %collective-permute-start.9) | collective-permute-done | bytes 65568 | tf_op jit(solution)/shard_map/ppermute | solution.py:30
  85.4 3.7 %collective-permute-start.10 = (bf16[32,2048]{1,0:T(8,128)(2,1)S(1)}, bf16[32,2048]{1,0:T(8,128)(2,1)S(1)}, u32[]{:S(2)}, u32[]{:S(2)}) collective-permute-start(bf16[32,2048]{1,0:T(8,128)(2,1)S(1)} %maximum_select_fusion.3), channel_id=1, source_target_pairs={{0,3},{1,0},{2,1},{3,2},{4,7},{5,4},{6,5},{7,6},{8,11},{9,8},{10,9... | collective-permute-start | bytes 393224 | tf_op jit(solution)/shard_map/ppermute | solution.py:36
  89.2 7.1 %collective-permute-done.12 = bf16[32,2048]{1,0:T(8,128)(2,1)S(1)} collective-permute-done((bf16[32,2048]{1,0:T(8,128)(2,1)S(1)}, bf16[32,2048]{1,0:T(8,128)(2,1)S(1)}, u32[]{:S(2)}, u32[]{:S(2)}) %collective-permute-start.12) | collective-permute-done | bytes 131104 | tf_op jit(solution)/shard_map/ppermute | solution.py:36
  96.3 7.7 %collective-permute-done.11 = bf16[32,2048]{1,0:T(8,128)(2,1)S(1)} collective-permute-done((bf16[32,2048]{1,0:T(8,128)(2,1)S(1)}, bf16[32,2048]{1,0:T(8,128)(2,1)S(1)}, u32[]{:S(2)}, u32[]{:S(2)}) %collective-permute-start.11) | collective-permute-done | bytes 131104 | tf_op jit(solution)/shard_map/ppermute | solution.py:36
  104.5 1.2 collective-permute-done.13
  105.8 8.7 %collective-permute-start.16 = (bf16[128,256]{1,0:T(8,128)(2,1)S(1)}, bf16[128,256]{1,0:T(8,128)(2,1)S(1)}, u32[]{:S(2)}, u32[]{:S(2)}) collective-permute-start(bf16[128,256]{1,0:T(8,128)(2,1)S(1)} %bitcast.94), channel_id=1, source_target_pairs={{0,3},{1,2},{2,1},{3,0},{4,7},{5,6},{6,5},{7,4},{8,11},{9,10},{10,... | collective-permute-start | bytes 196616 | tf_op jit(solution)/shard_map/ppermute | solution.py:30
  114.9 1.4 collective-permute-start.14
  117.0 2.6 collective-permute-done.15
  119.6 4.9 %collective-permute-done.14 = bf16[128,256]{1,0:T(8,128)(2,1)S(1)} collective-permute-done((bf16[128,256]{1,0:T(8,128)(2,1)S(1)}, bf16[128,256]{1,0:T(8,128)(2,1)S(1)}, u32[]{:S(2)}, u32[]{:S(2)}) %collective-permute-start.14) | collective-permute-done | bytes 65568 | tf_op jit(solution)/shard_map/ppermute | solution.py:30
  125.3 2.6 all-gather.3.cloned.1.call-done
  127.9 21.2 %ffn.2 = bf16[512,4096]{1,0:T(8,128)(2,1)S(1)} custom-call(s32[5]{0:T(128)S(1)} %get-tuple-element.117.order, bf16[2,4,128,4096]{3,2,1,0:T(8,128)(2,1)} %bitcast.82, bf16[4096,1024]{1,0:T(8,128)(2,1)} %gate_ref.3, bf16[4096,1024]{1,0:T(8,128)(2,1)} %up_ref.3, bf16[1024,4096]{1,0:T(8,128)(2,1)} %down_ref.3), custom_call_target="tpu_custom_call" | custom-call | flops 1024 | bytes 1024 | tf_op jit(solution)/shard_map/ffn/pallas_call | solution.py:151
  149.1 3.9 %collective-permute-done.18 = bf16[1,2,512,256]{3,2,1,0:T(8,128)(2,1)S(1)} collective-permute-done((bf16[1,2,512,256]{3,2,1,0:T(8,128)(2,1)S(1)}, bf16[1,2,512,256]{3,2,1,0:T(8,128)(2,1)S(1)}, u32[]{:S(2)}, u32[]{:S(2)}) %collective-permute-start.18) | collective-permute-done | bytes 524320 | tf_op jit(solution)/shard_map/ppermute | solution.py:30
  153.3 21.2 %ffn.3 = bf16[512,4096]{1,0:T(8,128)(2,1)S(1)} custom-call(s32[5]{0:T(128)S(1)} %get-tuple-element.116.order, bf16[2,4,128,4096]{3,2,1,0:T(8,128)(2,1)} %bitcast.83, bf16[4096,1024]{1,0:T(8,128)(2,1)} %gate_ref.3, bf16[4096,1024]{1,0:T(8,128)(2,1)} %up_ref.3, bf16[1024,4096]{1,0:T(8,128)(2,1)} %down_ref.3), custom_call_target="tpu_custom_call" | custom-call | flops 1024 | bytes 1024 | tf_op jit(solution)/shard_map/ffn/pallas_call | solution.py:151
  174.5 4.3 %collective-permute-done.19 = bf16[2,2,512,256]{3,2,1,0:T(8,128)(2,1)S(1)} collective-permute-done((bf16[2,2,512,256]{3,2,1,0:T(8,128)(2,1)S(1)}, bf16[2,2,512,256]{3,2,1,0:T(8,128)(2,1)S(1)}, u32[]{:S(2)}, u32[]{:S(2)}) %collective-permute-start.19) | collective-permute-done | bytes 1048608 | tf_op jit(solution)/shard_map/ppermute | solution.py:30
  179.5 2.2 collective-permute-start.21
  183.0 1.6 collective-permute-start.23
  184.5 1.5 collective-permute-start.24
  186.0 18.1 %collective-permute-done.21 = bf16[128,4096]{1,0:T(8,128)(2,1)S(1)} collective-permute-done((bf16[128,4096]{1,0:T(8,128)(2,1)S(1)}, bf16[128,4096]{1,0:T(8,128)(2,1)S(1)}, u32[]{:S(2)}, u32[]{:S(2)}) %collective-permute-start.21) | collective-permute-done | bytes 1048608 | tf_op jit(solution)/shard_map/ppermute | solution.py:59
  205.0 1.2 copy-done.8
  206.2 4.4 %collective-permute-start.26 = (bf16[128,4096]{1,0:T(8,128)(2,1)S(1)}, bf16[128,4096]{1,0:T(8,128)(2,1)S(1)}, u32[]{:S(2)}, u32[]{:S(2)}) collective-permute-start(bf16[128,4096]{1,0:T(8,128)(2,1)S(1)} %get-tuple-element.45), channel_id=1, source_target_pairs={{0,1},{1,2},{4,5},{5,6},{8,9},{9,10},{12,13},{13,14},{16,17},{17,1... | collective-permute-start | bytes 3145736 | tf_op jit(solution)/shard_map/ppermute | solution.py:59
  210.6 0.9 collective-permute-start.27
  211.6 1.6 collective-permute-start.28
  213.1 1.5 collective-permute-start.29
  214.7 17.4 %collective-permute-done.26 = bf16[128,4096]{1,0:T(8,128)(2,1)S(1)} collective-permute-done((bf16[128,4096]{1,0:T(8,128)(2,1)S(1)}, bf16[128,4096]{1,0:T(8,128)(2,1)S(1)}, u32[]{:S(2)}, u32[]{:S(2)}) %collective-permute-start.26) | collective-permute-done | bytes 1048608 | tf_op jit(solution)/shard_map/ppermute | solution.py:59
  232.1 2.5 add_convert_fusion
  234.7 0.9 copy-done.13
  235.6 0.9 copy-done.14
  236.5 9.1 %collective-permute-start.32 = (bf16[128,4096]{1,0:T(8,128)(2,1)}, bf16[128,4096]{1,0:T(8,128)(2,1)}, u32[]{:S(2)}, u32[]{:S(2)}) collective-permute-start(bf16[128,4096]{1,0:T(8,128)(2,1)} %get-tuple-element.52), channel_id=1, source_target_pairs={{0,1},{1,2},{2,3},{4,5},{5,6},{6,7},{8,9},{9,10},{10,11},{12,13},{... | collective-permute-start | bytes 3145736 | tf_op jit(solution)/shard_map/ppermute | solution.py:59
  245.5 1.3 collective-permute-start.33
  246.8 1.6 collective-permute-start.34
  248.4 1.5 collective-permute-start.35
  249.9 1.6 shift_right_arithmetic.40
  251.6 1.6 copy.29
  254.0 11.2 %collective-permute-done.32 = bf16[128,4096]{1,0:T(8,128)(2,1)} collective-permute-done((bf16[128,4096]{1,0:T(8,128)(2,1)}, bf16[128,4096]{1,0:T(8,128)(2,1)}, u32[]{:S(2)}, u32[]{:S(2)}) %collective-permute-start.32) | collective-permute-done | bytes 1048608 | tf_op jit(solution)/shard_map/ppermute | solution.py:59
  265.2 5.1 %collective-permute-done.33 = bf16[128,4096]{1,0:T(8,128)(2,1)} collective-permute-done((bf16[128,4096]{1,0:T(8,128)(2,1)}, bf16[128,4096]{1,0:T(8,128)(2,1)}, u32[]{:S(2)}, u32[]{:S(2)}) %collective-permute-start.33) | collective-permute-done | bytes 1048608 | tf_op jit(solution)/shard_map/ppermute | solution.py:60
  270.3 3.4 %fusion = (f32[128]{0:T(128)S(1)}, bf16[128,4096]{1,0:T(8,128)(2,1)S(1)}) fusion(bf16[128,4096]{1,0:T(8,128)(2,1)} %collective-permute-done.33, bf16[128,4096]{1,0:T(8,128)(2,1)} %collective-permute-done.32, bf16[512,4096]{1,0:T(8,128)(2,1)} %copy-done.5, bf16[512,4096]{1,0:T(8,128)(2,1)} %copy-done.2, s32[128,4096]{1,0:T(8,128)S(1)} %bitcast.87, ...), kind=kLoop, calls=%fused_computation.10 | loop fusion | flops 9437056 | bytes 8405504 | tf_op jit(solution)/shard_map/reduce_sum | solution.py:18
  274.7 1.3 fusion.2.mem_ref
  276.3 1.1 collective-permute-done.39.refs_15_
  277.4 0.9 copy-done.18
  278.3 11.0 %attend_own_keys.1 = bf16[4,128,384]{2,1,0:T(8,128)(2,1)} custom-call(s32[16]{0:T(128)} %pad_add_fusion.3.table, bf16[128,4096]{1,0:T(8,128)(2,1)} %fusion.2.mem_ref, bf16[4,128,256]{2,1,0:T(8,128)(2,1)} %pad_maximum_fusion.4.cq_ref, bf16[2,2048,256]{2,1,0:T(8,128)(2,1)} %bitcast.85, bf16[2,2048,256]{2,1,0:T(8,128)(2,1)} %collective-permute-done.17.refs_1_, ...), custom_call_target="tpu_custom_call" | custom-call | flops 1024 | bytes 1024 | tf_op jit(solution)/shard_map/attend_own_keys/pallas_call | solution.py:234
  289.4 1.1 fusion.35
  290.7 4.2 %collective-permute-start.42 = (bf16[128,384]{1,0:T(8,128)(2,1)S(1)}, bf16[128,384]{1,0:T(8,128)(2,1)S(1)}, u32[]{:S(2)}, u32[]{:S(2)}) collective-permute-start(bf16[128,384]{1,0:T(8,128)(2,1)S(1)} %get-tuple-element.105), channel_id=1, source_target_pairs={{0,3},{1,2},{2,1},{3,0},{4,7},{5,6},{6,5},{7,4},{8,11},{9,10},{10,... | collective-permute-start | bytes 294920 | tf_op jit(solution)/shard_map/ppermute | solution.py:30
  294.9 3.7 %collective-permute-done.40 = bf16[128,384]{1,0:T(8,128)(2,1)S(1)} collective-permute-done((bf16[128,384]{1,0:T(8,128)(2,1)S(1)}, bf16[128,384]{1,0:T(8,128)(2,1)S(1)}, u32[]{:S(2)}, u32[]{:S(2)}) %collective-permute-start.40) | collective-permute-done | bytes 98336 | tf_op jit(solution)/shard_map/ppermute | solution.py:30
  298.7 1.4 collective-permute-done.42
  301.3 1.5 collective-permute-done.43
  303.5 1.7 collective-permute-start.46
  305.2 2.4 collective-permute-start.45
  307.6 2.3 collective-permute-done.46
  309.9 9.6 %collective-permute-done.45 = bf16[32,2048]{1,0:T(8,128)(2,1)S(1)} collective-permute-done((bf16[32,2048]{1,0:T(8,128)(2,1)S(1)}, bf16[32,2048]{1,0:T(8,128)(2,1)S(1)}, u32[]{:S(2)}, u32[]{:S(2)}) %collective-permute-start.45) | collective-permute-done | bytes 131104 | tf_op jit(solution)/shard_map/ppermute | solution.py:69
  320.0 1.1 collective-permute-done.47
  (165 shorter events, 15.3 us)
Async XLA Ops:
  7.2 28.5 %copy-start = (bf16[256,2048]{1,0:T(8,128)(2,1)S(1)}, bf16[256,2048]{1,0:T(8,128)(2,1)}, u32[]{:S(2)}) copy-start(bf16[256,2048]{1,0:T(8,128)(2,1)} %param.28) | copy-start | bytes 3145732
  7.2 4.2 %copy-start.9 = (bf16[16,4096]{1,0:T(8,128)(2,1)S(1)}, bf16[16,4096]{1,0:T(8,128)(2,1)}, u32[]{:S(2)}) copy-start(bf16[16,4096]{1,0:T(8,128)(2,1)} %param.25) | copy-start | bytes 393220
  7.2 4.4 %copy-start.21 = (f32[4096]{0:T(1024)S(1)}, f32[4096]{0:T(1024)}, u32[]{:S(2)}) copy-start(f32[4096]{0:T(1024)} %param.26) | copy-start | bytes 49156
  7.2 120.7 %all-gather.3.cloned.1.call-start = ((), (), s32[]{:S(2)}) async-start(), calls=%async_computation | async-start | bytes 9437184 | tf_op jit(solution)/shard_map/all_gather | solution.py:292
  11.7 1.4 collective-permute-start
  13.2 9.4 %collective-permute-start.3 = (bf16[32,2048]{1,0:T(8,128)(2,1)S(1)}, bf16[32,2048]{1,0:T(8,128)(2,1)S(1)}, u32[]{:S(2)}, u32[]{:S(2)}) collective-permute-start(bf16[32,2048]{1,0:T(8,128)(2,1)S(1)} %maximum_select_fusion.2), channel_id=1, source_target_pairs={{0,1},{1,2},{2,3},{3,0},{4,5},{5,6},{6,7},{7,4},{8,9},{9,10},{10,1... | collective-permute-start | bytes 393224 | tf_op jit(solution)/shard_map/ppermute | solution.py:36
  16.1 15.2 %collective-permute-start.2 = (bf16[32,2048]{1,0:T(8,128)(2,1)S(1)}, bf16[32,2048]{1,0:T(8,128)(2,1)S(1)}, u32[]{:S(2)}, u32[]{:S(2)}) collective-permute-start(bf16[32,2048]{1,0:T(8,128)(2,1)S(1)} %maximum_select_fusion.2), channel_id=1, source_target_pairs={{0,2},{1,3},{2,0},{3,1},{4,6},{5,7},{6,4},{7,5},{8,10},{9,11},{10,... | collective-permute-start | bytes 393224 | tf_op jit(solution)/shard_map/ppermute | solution.py:36
  18.7 12.6 %collective-permute-start.1 = (bf16[32,2048]{1,0:T(8,128)(2,1)S(1)}, bf16[32,2048]{1,0:T(8,128)(2,1)S(1)}, u32[]{:S(2)}, u32[]{:S(2)}) collective-permute-start(bf16[32,2048]{1,0:T(8,128)(2,1)S(1)} %maximum_select_fusion.2), channel_id=1, source_target_pairs={{0,3},{1,0},{2,1},{3,2},{4,7},{5,4},{6,5},{7,6},{8,11},{9,8},{10,9... | collective-permute-start | bytes 393224 | tf_op jit(solution)/shard_map/ppermute | solution.py:36
  20.1 12.8 %copy-start.23 = (bf16[2048,3,256]{2,0,1:T(8,128)(2,1)S(1)}, bf16[2048,3,256]{2,0,1:T(8,128)(2,1)}, u32[]{:S(2)}) copy-start(bf16[2048,3,256]{2,0,1:T(8,128)(2,1)} %param.27) | copy-start | bytes 9437188
  33.6 1.8 collective-permute-start.4
  36.2 21.6 %collective-permute-start.7 = (bf16[32,2048]{1,0:T(8,128)(2,1)S(1)}, bf16[32,2048]{1,0:T(8,128)(2,1)S(1)}, u32[]{:S(2)}, u32[]{:S(2)}) collective-permute-start(bf16[32,2048]{1,0:T(8,128)(2,1)S(1)} %get-tuple-element.102), channel_id=1, source_target_pairs={{0,3},{1,0},{2,1},{3,2},{4,7},{5,4},{6,5},{7,6},{8,11},{9,8},{10,9... | collective-permute-start | bytes 393224 | tf_op jit(solution)/shard_map/ppermute | solution.py:69
  49.1 29.5 %collective-permute-start.6 = (bf16[32,2048]{1,0:T(8,128)(2,1)S(1)}, bf16[32,2048]{1,0:T(8,128)(2,1)S(1)}, u32[]{:S(2)}, u32[]{:S(2)}) collective-permute-start(bf16[32,2048]{1,0:T(8,128)(2,1)S(1)} %get-tuple-element.103), channel_id=1, source_target_pairs={{0,2},{1,3},{2,0},{3,1},{4,6},{5,7},{6,4},{7,5},{8,10},{9,11},{10,... | collective-permute-start | bytes 393224 | tf_op jit(solution)/shard_map/ppermute | solution.py:69
  49.4 29.2 %collective-permute-start.5 = (bf16[32,2048]{1,0:T(8,128)(2,1)S(1)}, bf16[32,2048]{1,0:T(8,128)(2,1)S(1)}, u32[]{:S(2)}, u32[]{:S(2)}) collective-permute-start(bf16[32,2048]{1,0:T(8,128)(2,1)S(1)} %get-tuple-element.101), channel_id=1, source_target_pairs={{0,1},{1,2},{2,3},{3,0},{4,5},{5,6},{6,7},{7,4},{8,9},{9,10},{10,1... | collective-permute-start | bytes 393224 | tf_op jit(solution)/shard_map/ppermute | solution.py:69
  78.7 25.2 %copy-start.24 = (bf16[2048,256]{1,0:T(8,128)(2,1)S(1)}, bf16[2048,256]{1,0:T(8,128)(2,1)}, u32[]{:S(2)}) copy-start(bf16[2048,256]{1,0:T(8,128)(2,1)} %param.30) | copy-start | bytes 3145732
  78.7 2.5 collective-permute-start.8
  80.8 35.5 %copy-start.3 = (bf16[2048,2,256]{2,0,1:T(8,128)(2,1)}, bf16[2048,2,256]{2,0,1:T(8,128)(2,1)S(1)}, u32[]{:S(2)}) copy-start(bf16[2048,2,256]{2,0,1:T(8,128)(2,1)S(1)} %copy.38) | copy-start | bytes 6291460
  80.8 44.5 %collective-permute-start.17 = (bf16[2,2048,256]{2,1,0:T(8,128)(2,1)S(1)}, bf16[2,2048,256]{2,1,0:T(8,128)(2,1)}, u32[]{:S(2)}, u32[]{:S(2)}) collective-permute-start(bf16[2,2048,256]{2,1,0:T(8,128)(2,1)S(1)} %bitcast.84), channel_id=1, source_target_pairs={{0,4},{4,0},{1,5},{5,1},{2,6},{6,2},{3,7},{7,3},{8,12},{12,8},{9,1... | collective-permute-start | bytes 6291464 | tf_op jit(solution)/shard_map/ppermute | solution.py:30
  81.6 3.7 %collective-permute-start.9 = (bf16[16,2048]{1,0:T(8,128)(2,1)S(1)}, bf16[16,2048]{1,0:T(8,128)(2,1)S(1)}, u32[]{:S(2)}, u32[]{:S(2)}) collective-permute-start(bf16[16,2048]{1,0:T(8,128)(2,1)S(1)} %get-tuple-element.113), channel_id=1, source_target_pairs={{0,4},{4,0},{1,5},{5,1},{2,6},{6,2},{3,7},{7,3},{8,12},{12,8},{9,1... | collective-permute-start | bytes 196616 | tf_op jit(solution)/shard_map/ppermute | solution.py:30
  85.3 11.0 %collective-permute-start.12 = (bf16[32,2048]{1,0:T(8,128)(2,1)S(1)}, bf16[32,2048]{1,0:T(8,128)(2,1)S(1)}, u32[]{:S(2)}, u32[]{:S(2)}) collective-permute-start(bf16[32,2048]{1,0:T(8,128)(2,1)S(1)} %maximum_select_fusion.3), channel_id=1, source_target_pairs={{0,1},{1,2},{2,3},{3,0},{4,5},{5,6},{6,7},{7,4},{8,9},{9,10},{10,1... | collective-permute-start | bytes 393224 | tf_op jit(solution)/shard_map/ppermute | solution.py:36
  85.3 18.6 %collective-permute-start.11 = (bf16[32,2048]{1,0:T(8,128)(2,1)S(1)}, bf16[32,2048]{1,0:T(8,128)(2,1)S(1)}, u32[]{:S(2)}, u32[]{:S(2)}) collective-permute-start(bf16[32,2048]{1,0:T(8,128)(2,1)S(1)} %maximum_select_fusion.3), channel_id=1, source_target_pairs={{0,2},{1,3},{2,0},{3,1},{4,6},{5,7},{6,4},{7,5},{8,10},{9,11},{10,... | collective-permute-start | bytes 393224 | tf_op jit(solution)/shard_map/ppermute | solution.py:36
  85.4 18.5 %collective-permute-start.10 = (bf16[32,2048]{1,0:T(8,128)(2,1)S(1)}, bf16[32,2048]{1,0:T(8,128)(2,1)S(1)}, u32[]{:S(2)}, u32[]{:S(2)}) collective-permute-start(bf16[32,2048]{1,0:T(8,128)(2,1)S(1)} %maximum_select_fusion.3), channel_id=1, source_target_pairs={{0,3},{1,0},{2,1},{3,2},{4,7},{5,4},{6,5},{7,6},{8,11},{9,8},{10,9... | collective-permute-start | bytes 393224 | tf_op jit(solution)/shard_map/ppermute | solution.py:36
  104.2 1.4 collective-permute-start.13
  105.8 11.2 %collective-permute-start.16 = (bf16[128,256]{1,0:T(8,128)(2,1)S(1)}, bf16[128,256]{1,0:T(8,128)(2,1)S(1)}, u32[]{:S(2)}, u32[]{:S(2)}) collective-permute-start(bf16[128,256]{1,0:T(8,128)(2,1)S(1)} %bitcast.94), channel_id=1, source_target_pairs={{0,3},{1,2},{2,1},{3,0},{4,7},{5,6},{6,5},{7,4},{8,11},{9,10},{10,... | collective-permute-start | bytes 196616 | tf_op jit(solution)/shard_map/ppermute | solution.py:30
  114.5 5.1 %collective-permute-start.15 = (bf16[128,256]{1,0:T(8,128)(2,1)S(1)}, bf16[128,256]{1,0:T(8,128)(2,1)S(1)}, u32[]{:S(2)}, u32[]{:S(2)}) collective-permute-start(bf16[128,256]{1,0:T(8,128)(2,1)S(1)} %bitcast.95), channel_id=1, source_target_pairs={{0,1},{1,0},{2,3},{3,2},{4,5},{5,4},{6,7},{7,6},{8,9},{9,8},{10,11... | collective-permute-start | bytes 196616 | tf_op jit(solution)/shard_map/ppermute | solution.py:30
  114.9 9.6 %collective-permute-start.14 = (bf16[128,256]{1,0:T(8,128)(2,1)S(1)}, bf16[128,256]{1,0:T(8,128)(2,1)S(1)}, u32[]{:S(2)}, u32[]{:S(2)}) collective-permute-start(bf16[128,256]{1,0:T(8,128)(2,1)S(1)} %bitcast.96), channel_id=1, source_target_pairs={{0,2},{1,3},{2,0},{3,1},{4,6},{5,7},{6,4},{7,5},{8,10},{9,11},{10,... | collective-permute-start | bytes 196616 | tf_op jit(solution)/shard_map/ppermute | solution.py:30
  127.9 25.1 %collective-permute-start.18 = (bf16[1,2,512,256]{3,2,1,0:T(8,128)(2,1)S(1)}, bf16[1,2,512,256]{3,2,1,0:T(8,128)(2,1)S(1)}, u32[]{:S(2)}, u32[]{:S(2)}) collective-permute-start(bf16[1,2,512,256]{3,2,1,0:T(8,128)(2,1)S(1)} %dynamic-slice_bitcast_fusion), channel_id=1, source_target_pairs={{0,2},{1,3},{2,0},{3,1},{4,6},{5,7},{6,4},{7,5},{8,10},{9,11},{10,... | collective-permute-start | bytes 1572872 | tf_op jit(solution)/shard_map/ppermute | solution.py:30
  153.1 25.7 %collective-permute-start.20 = (bf16[512,4096]{1,0:T(8,128)(2,1)S(1)}, bf16[512,4096]{1,0:T(8,128)(2,1)S(1)}, u32[]{:S(2)}, u32[]{:S(2)}) collective-permute-start(bf16[512,4096]{1,0:T(8,128)(2,1)S(1)} %ffn.2), channel_id=1, source_target_pairs={{0,4},{4,0},{1,5},{5,1},{2,6},{6,2},{3,7},{7,3},{8,12},{12,8},{9,1... | collective-permute-start | bytes 12582920 | tf_op jit(solution)/shard_map/ppermute | solution.py:30
  153.2 25.5 %collective-permute-start.19 = (bf16[2,2,512,256]{3,2,1,0:T(8,128)(2,1)S(1)}, bf16[2,2,512,256]{3,2,1,0:T(8,128)(2,1)S(1)}, u32[]{:S(2)}, u32[]{:S(2)}) collective-permute-start(bf16[2,2,512,256]{3,2,1,0:T(8,128)(2,1)S(1)} %pad_maximum_fusion.1), channel_id=1, source_target_pairs={{0,1},{1,0},{2,3},{3,2},{4,5},{5,4},{6,7},{7,6},{8,9},{9,8},{10,11... | collective-permute-start | bytes 3145736 | tf_op jit(solution)/shard_map/ppermute | solution.py:30
  174.5 57.6 %copy-start.2 = (bf16[512,4096]{1,0:T(8,128)(2,1)}, bf16[512,4096]{1,0:T(8,128)(2,1)S(1)}, u32[]{:S(2)}) copy-start(bf16[512,4096]{1,0:T(8,128)(2,1)S(1)} %ffn.3) | copy-start | bytes 12582916
  178.8 53.4 %copy-start.5 = (bf16[512,4096]{1,0:T(8,128)(2,1)}, bf16[512,4096]{1,0:T(8,128)(2,1)S(1)}, u32[]{:S(2)}) copy-start(bf16[512,4096]{1,0:T(8,128)(2,1)S(1)} %collective-permute-done.20) | copy-start | bytes 12582916
  179.5 24.6 %collective-permute-start.21 = (bf16[128,4096]{1,0:T(8,128)(2,1)S(1)}, bf16[128,4096]{1,0:T(8,128)(2,1)S(1)}, u32[]{:S(2)}, u32[]{:S(2)}) collective-permute-start(bf16[128,4096]{1,0:T(8,128)(2,1)S(1)} %get-tuple-element.93), channel_id=1, source_target_pairs={{0,1},{4,5},{8,9},{12,13},{16,17},{20,21},{24,25},{28,29}} | collective-permute-start | bytes 3145736 | tf_op jit(solution)/shard_map/ppermute | solution.py:59
  181.8 22.4 %collective-permute-start.22 = (bf16[128,4096]{1,0:T(8,128)(2,1)S(1)}, bf16[128,4096]{1,0:T(8,128)(2,1)S(1)}, u32[]{:S(2)}, u32[]{:S(2)}) collective-permute-start(bf16[128,4096]{1,0:T(8,128)(2,1)S(1)} %get-tuple-element.92), channel_id=1, source_target_pairs={{3,2},{7,6},{11,10},{15,14},{19,18},{23,22},{27,26},{31,30}} | collective-permute-start | bytes 3145736 | tf_op jit(solution)/shard_map/ppermute | solution.py:60
  182.7 22.2 %copy-start.6 = (bf16[3,2,512,256]{3,2,1,0:T(8,128)(2,1)}, bf16[3,2,512,256]{3,2,1,0:T(8,128)(2,1)S(1)}, u32[]{:S(2)}) copy-start(bf16[3,2,512,256]{3,2,1,0:T(8,128)(2,1)S(1)} %pad_maximum_fusion.refs_2_) | copy-start | bytes 4718596
  182.7 22.2 %collective-permute-start.25 = (bf16[3,2,512,256]{3,2,1,0:T(8,128)(2,1)S(1)}, bf16[3,2,512,256]{3,2,1,0:T(8,128)(2,1)S(1)}, u32[]{:S(2)}, u32[]{:S(2)}) collective-permute-start(bf16[3,2,512,256]{3,2,1,0:T(8,128)(2,1)S(1)} %pad_maximum_fusion.refs_2_), channel_id=1, source_target_pairs={{0,4},{4,0},{1,5},{5,1},{2,6},{6,2},{3,7},{7,3},{8,12},{12,8},{9,1... | collective-permute-start | bytes 4718600 | tf_op jit(solution)/shard_map/ppermute | solution.py:30
  183.0 22.0 %collective-permute-start.23 = (bf16[3,1,512,256]{3,2,1,0:T(8,128)(2,1)S(1)}, bf16[3,1,512,256]{3,2,1,0:T(8,128)(2,1)S(1)}, u32[]{:S(2)}, u32[]{:S(2)}) collective-permute-start(bf16[3,1,512,256]{3,2,1,0:T(8,128)(2,1)S(1)} %get-tuple-element.97), channel_id=1, source_target_pairs={{0,8},{8,0},{16,24},{24,16},{1,9},{9,1},{17,25},{25,17},{2,10},{10... | collective-permute-start | bytes 2359304 | tf_op jit(solution)/shard_map/ppermute | solution.py:30
  184.5 20.5 %collective-permute-start.24 = (bf16[3,1,512,256]{3,2,1,0:T(8,128)(2,1)S(1)}, bf16[3,1,512,256]{3,2,1,0:T(8,128)(2,1)}, u32[]{:S(2)}, u32[]{:S(2)}) collective-permute-start(bf16[3,1,512,256]{3,2,1,0:T(8,128)(2,1)S(1)} %get-tuple-element.97), channel_id=1, source_target_pairs={{0,16},{8,24},{16,0},{24,8},{1,17},{9,25},{17,1},{25,9},{2,18},{10... | collective-permute-start | bytes 2359304 | tf_op jit(solution)/shard_map/ppermute | solution.py:30
  205.0 29.7 %copy-start.11 = (bf16[3,1,512,256]{3,2,1,0:T(8,128)(2,1)}, bf16[3,1,512,256]{3,2,1,0:T(8,128)(2,1)S(1)}, u32[]{:S(2)}) copy-start(bf16[3,1,512,256]{3,2,1,0:T(8,128)(2,1)S(1)} %collective-permute-done.23.refs_3_) | copy-start | bytes 2359300
  206.2 25.9 %collective-permute-start.26 = (bf16[128,4096]{1,0:T(8,128)(2,1)S(1)}, bf16[128,4096]{1,0:T(8,128)(2,1)S(1)}, u32[]{:S(2)}, u32[]{:S(2)}) collective-permute-start(bf16[128,4096]{1,0:T(8,128)(2,1)S(1)} %get-tuple-element.45), channel_id=1, source_target_pairs={{0,1},{1,2},{4,5},{5,6},{8,9},{9,10},{12,13},{13,14},{16,17},{17,1... | collective-permute-start | bytes 3145736 | tf_op jit(solution)/shard_map/ppermute | solution.py:59
  210.6 21.5 %collective-permute-start.27 = (bf16[128,4096]{1,0:T(8,128)(2,1)S(1)}, bf16[128,4096]{1,0:T(8,128)(2,1)S(1)}, u32[]{:S(2)}, u32[]{:S(2)}) collective-permute-start(bf16[128,4096]{1,0:T(8,128)(2,1)S(1)} %get-tuple-element.46), channel_id=1, source_target_pairs={{2,1},{3,2},{6,5},{7,6},{10,9},{11,10},{14,13},{15,14},{18,17},{19... | collective-permute-start | bytes 3145736 | tf_op jit(solution)/shard_map/ppermute | solution.py:60
  211.6 23.0 %collective-permute-start.28 = (bf16[3,1,512,256]{3,2,1,0:T(8,128)(2,1)S(1)}, bf16[3,1,512,256]{3,2,1,0:T(8,128)(2,1)}, u32[]{:S(2)}, u32[]{:S(2)}) collective-permute-start(bf16[3,1,512,256]{3,2,1,0:T(8,128)(2,1)S(1)} %get-tuple-element.96), channel_id=1, source_target_pairs={{0,8},{8,0},{16,24},{24,16},{1,9},{9,1},{17,25},{25,17},{2,10},{10... | collective-permute-start | bytes 2359304 | tf_op jit(solution)/shard_map/ppermute | solution.py:30
  213.1 21.5 %collective-permute-start.29 = (bf16[3,1,512,256]{3,2,1,0:T(8,128)(2,1)S(1)}, bf16[3,1,512,256]{3,2,1,0:T(8,128)(2,1)S(1)}, u32[]{:S(2)}, u32[]{:S(2)}) collective-permute-start(bf16[3,1,512,256]{3,2,1,0:T(8,128)(2,1)S(1)} %get-tuple-element.96), channel_id=1, source_target_pairs={{0,16},{8,24},{16,0},{24,8},{1,17},{9,25},{17,1},{25,9},{2,18},{10... | collective-permute-start | bytes 2359304 | tf_op jit(solution)/shard_map/ppermute | solution.py:30
  214.7 20.0 %collective-permute-start.30 = (bf16[3,1,512,256]{3,2,1,0:T(8,128)(2,1)S(1)}, bf16[3,1,512,256]{3,2,1,0:T(8,128)(2,1)S(1)}, u32[]{:S(2)}, u32[]{:S(2)}) collective-permute-start(bf16[3,1,512,256]{3,2,1,0:T(8,128)(2,1)S(1)} %collective-permute-done.23.refs_3_), channel_id=1, source_target_pairs={{0,4},{4,0},{1,5},{5,1},{2,6},{6,2},{3,7},{7,3},{8,12},{12,8},{9,1... | collective-permute-start | bytes 2359304 | tf_op jit(solution)/shard_map/ppermute | solution.py:30
  232.1 3.5 %collective-permute-start.31 = (bf16[3,1,512,256]{3,2,1,0:T(8,128)(2,1)}, bf16[3,1,512,256]{3,2,1,0:T(8,128)(2,1)S(1)}, u32[]{:S(2)}, u32[]{:S(2)}) collective-permute-start(bf16[3,1,512,256]{3,2,1,0:T(8,128)(2,1)} %collective-permute-done.24.refs_4_), channel_id=1, source_target_pairs={{0,4},{4,0},{1,5},{5,1},{2,6},{6,2},{3,7},{7,3},{8,12},{12,8},{9,1... | collective-permute-start | bytes 2359304 | tf_op jit(solution)/shard_map/ppermute | solution.py:30
  234.6 16.9 %copy-start.12 = (bf16[3,1,512,256]{3,2,1,0:T(8,128)(2,1)}, bf16[3,1,512,256]{3,2,1,0:T(8,128)(2,1)S(1)}, u32[]{:S(2)}) copy-start(bf16[3,1,512,256]{3,2,1,0:T(8,128)(2,1)S(1)} %collective-permute-done.29.refs_6_) | copy-start | bytes 2359300
  236.5 28.7 %collective-permute-start.32 = (bf16[128,4096]{1,0:T(8,128)(2,1)}, bf16[128,4096]{1,0:T(8,128)(2,1)}, u32[]{:S(2)}, u32[]{:S(2)}) collective-permute-start(bf16[128,4096]{1,0:T(8,128)(2,1)} %get-tuple-element.52), channel_id=1, source_target_pairs={{0,1},{1,2},{2,3},{4,5},{5,6},{6,7},{8,9},{9,10},{10,11},{12,13},{... | collective-permute-start | bytes 3145736 | tf_op jit(solution)/shard_map/ppermute | solution.py:59
  245.5 24.8 %collective-permute-start.33 = (bf16[128,4096]{1,0:T(8,128)(2,1)}, bf16[128,4096]{1,0:T(8,128)(2,1)}, u32[]{:S(2)}, u32[]{:S(2)}) collective-permute-start(bf16[128,4096]{1,0:T(8,128)(2,1)} %get-tuple-element.53), channel_id=1, source_target_pairs={{1,0},{2,1},{3,2},{5,4},{6,5},{7,6},{9,8},{10,9},{11,10},{13,12},{... | collective-permute-start | bytes 3145736 | tf_op jit(solution)/shard_map/ppermute | solution.py:60
  246.8 23.5 %collective-permute-start.34 = (bf16[3,1,512,256]{3,2,1,0:T(8,128)(2,1)}, bf16[3,1,512,256]{3,2,1,0:T(8,128)(2,1)}, u32[]{:S(2)}, u32[]{:S(2)}) collective-permute-start(bf16[3,1,512,256]{3,2,1,0:T(8,128)(2,1)} %collective-permute-done.24.refs_4_), channel_id=1, source_target_pairs={{0,8},{8,0},{16,24},{24,16},{1,9},{9,1},{17,25},{25,17},{2,10},{10... | collective-permute-start | bytes 2359304 | tf_op jit(solution)/shard_map/ppermute | solution.py:30
  248.4 21.9 %collective-permute-start.35 = (bf16[3,1,512,256]{3,2,1,0:T(8,128)(2,1)}, bf16[3,1,512,256]{3,2,1,0:T(8,128)(2,1)}, u32[]{:S(2)}, u32[]{:S(2)}) collective-permute-start(bf16[3,1,512,256]{3,2,1,0:T(8,128)(2,1)} %collective-permute-done.28.refs_5_), channel_id=1, source_target_pairs={{0,16},{8,24},{16,0},{24,8},{1,17},{9,25},{17,1},{25,9},{2,18},{10... | collective-permute-start | bytes 2359304 | tf_op jit(solution)/shard_map/ppermute | solution.py:30
  251.6 18.8 %copy-start.4 = (bf16[128,4096]{1,0:T(8,128)(2,1)S(1)}, bf16[128,4096]{1,0:T(8,128)(2,1)}, u32[]{:S(2)}) copy-start(bf16[128,4096]{1,0:T(8,128)(2,1)} %param.18) | copy-start | bytes 3145732
  254.0 22.0 %collective-permute-start.36 = (bf16[3,1,512,256]{3,2,1,0:T(8,128)(2,1)}, bf16[3,1,512,256]{3,2,1,0:T(8,128)(2,1)S(1)}, u32[]{:S(2)}, u32[]{:S(2)}) collective-permute-start(bf16[3,1,512,256]{3,2,1,0:T(8,128)(2,1)} %collective-permute-done.28.refs_5_), channel_id=1, source_target_pairs={{0,4},{4,0},{1,5},{5,1},{2,6},{6,2},{3,7},{7,3},{8,12},{12,8},{9,1... | collective-permute-start | bytes 2359304 | tf_op jit(solution)/shard_map/ppermute | solution.py:30
  265.2 10.8 %collective-permute-start.37 = (bf16[3,1,512,256]{3,2,1,0:T(8,128)(2,1)}, bf16[3,1,512,256]{3,2,1,0:T(8,128)(2,1)S(1)}, u32[]{:S(2)}, u32[]{:S(2)}) collective-permute-start(bf16[3,1,512,256]{3,2,1,0:T(8,128)(2,1)} %copy-done.12), channel_id=1, source_target_pairs={{0,4},{4,0},{1,5},{5,1},{2,6},{6,2},{3,7},{7,3},{8,12},{12,8},{9,1... | collective-permute-start | bytes 2359304 | tf_op jit(solution)/shard_map/ppermute | solution.py:30
  270.3 4.4 %copy-start.20 = (f32[4096]{0:T(1024)S(1)}, f32[4096]{0:T(1024)}, u32[]{:S(2)}) copy-start(f32[4096]{0:T(1024)} %param.24) | copy-start | bytes 49156
  273.7 2.6 collective-permute-start.38
  273.8 3.6 %collective-permute-start.39 = (bf16[3,1,512,256]{3,2,1,0:T(8,128)(2,1)}, bf16[3,1,512,256]{3,2,1,0:T(8,128)(2,1)S(1)}, u32[]{:S(2)}, u32[]{:S(2)}) collective-permute-start(bf16[3,1,512,256]{3,2,1,0:T(8,128)(2,1)} %collective-permute-done.35.refs_8_), channel_id=1, source_target_pairs={{0,4},{4,0},{1,5},{5,1},{2,6},{6,2},{3,7},{7,3},{8,12},{12,8},{9,1... | collective-permute-start | bytes 2359304 | tf_op jit(solution)/shard_map/ppermute | solution.py:30
  290.5 8.2 %collective-permute-start.40 = (bf16[128,384]{1,0:T(8,128)(2,1)S(1)}, bf16[128,384]{1,0:T(8,128)(2,1)S(1)}, u32[]{:S(2)}, u32[]{:S(2)}) collective-permute-start(bf16[128,384]{1,0:T(8,128)(2,1)S(1)} %get-tuple-element.107), channel_id=1, source_target_pairs={{0,2},{1,3},{2,0},{3,1},{4,6},{5,7},{6,4},{7,5},{8,10},{9,11},{10,... | collective-permute-start | bytes 294920 | tf_op jit(solution)/shard_map/ppermute | solution.py:30
  290.5 8.1 %collective-permute-start.41 = (bf16[128,384]{1,0:T(8,128)(2,1)S(1)}, bf16[128,384]{1,0:T(8,128)(2,1)S(1)}, u32[]{:S(2)}, u32[]{:S(2)}) collective-permute-start(bf16[128,384]{1,0:T(8,128)(2,1)S(1)} %get-tuple-element.106), channel_id=1, source_target_pairs={{0,1},{1,0},{2,3},{3,2},{4,5},{5,4},{6,7},{7,6},{8,9},{9,8},{10,11... | collective-permute-start | bytes 294920 | tf_op jit(solution)/shard_map/ppermute | solution.py:30
  290.7 9.4 %collective-permute-start.42 = (bf16[128,384]{1,0:T(8,128)(2,1)S(1)}, bf16[128,384]{1,0:T(8,128)(2,1)S(1)}, u32[]{:S(2)}, u32[]{:S(2)}) collective-permute-start(bf16[128,384]{1,0:T(8,128)(2,1)S(1)} %get-tuple-element.105), channel_id=1, source_target_pairs={{0,3},{1,2},{2,1},{3,0},{4,7},{5,6},{6,5},{7,4},{8,11},{9,10},{10,... | collective-permute-start | bytes 294920 | tf_op jit(solution)/shard_map/ppermute | solution.py:30
  301.2 1.6 collective-permute-start.43
  302.9 16.8 %copy-start.19 = (s32[16,1024]{1,0:T(8,128)S(1)}, s32[16,1024]{1,0:T(8,128)}, u32[]{:S(2)}) copy-start(s32[16,1024]{1,0:T(8,128)} %param.33) | copy-start | bytes 196612
  303.2 18.7 %copy-start.1 = (bf16[256,2048]{1,0:T(8,128)(2,1)S(1)}, bf16[256,2048]{1,0:T(8,128)(2,1)}, u32[]{:S(2)}) copy-start(bf16[256,2048]{1,0:T(8,128)(2,1)} %param.28) | copy-start | bytes 3145732
  303.5 6.4 %collective-permute-start.46 = (bf16[32,2048]{1,0:T(8,128)(2,1)S(1)}, bf16[32,2048]{1,0:T(8,128)(2,1)S(1)}, u32[]{:S(2)}, u32[]{:S(2)}) collective-permute-start(bf16[32,2048]{1,0:T(8,128)(2,1)S(1)} %get-tuple-element.99), channel_id=1, source_target_pairs={{0,3},{1,0},{2,1},{3,2},{4,7},{5,4},{6,5},{7,6},{8,11},{9,8},{10,9... | collective-permute-start | bytes 393224 | tf_op jit(solution)/shard_map/ppermute | solution.py:69
  305.2 14.3 %collective-permute-start.45 = (bf16[32,2048]{1,0:T(8,128)(2,1)S(1)}, bf16[32,2048]{1,0:T(8,128)(2,1)S(1)}, u32[]{:S(2)}, u32[]{:S(2)}) collective-permute-start(bf16[32,2048]{1,0:T(8,128)(2,1)S(1)} %get-tuple-element.100), channel_id=1, source_target_pairs={{0,2},{1,3},{2,0},{3,1},{4,6},{5,7},{6,4},{7,5},{8,10},{9,11},{10,... | collective-permute-start | bytes 393224 | tf_op jit(solution)/shard_map/ppermute | solution.py:69
  307.6 11.9 %collective-permute-start.44 = (bf16[32,2048]{1,0:T(8,128)(2,1)S(1)}, bf16[32,2048]{1,0:T(8,128)(2,1)S(1)}, u32[]{:S(2)}, u32[]{:S(2)}) collective-permute-start(bf16[32,2048]{1,0:T(8,128)(2,1)S(1)} %get-tuple-element.98), channel_id=1, source_target_pairs={{0,1},{1,2},{2,3},{3,0},{4,5},{5,6},{6,7},{7,4},{8,9},{9,10},{10,1... | collective-permute-start | bytes 393224 | tf_op jit(solution)/shard_map/ppermute | solution.py:69
  319.6 1.4 collective-permute-start.47
  (10 other events, 14.6 us)
Sparse Core Ops, SparseCore 0:
  11.5 116.2 all-gather.2
